TPU v7x, 32 devices: a whole 2x2x4 slice. The times are simulated.
32 devices in a mesh: tm: 8 (over y, x, core), head: 4 (over z).
Axes of the slice: x: 2, y: 2, z: 4, core: 2. Of those that a mesh axis runs over, the one named last changes fastest.
Arguments:
- frames: bfloat16 [16, 512, 5120], P('tm', None, 'head'), may hold values from -8 to 8
- taps: float32 [3, 5120], P(None, 'head'), may hold values from -3 to 3
- w_query: bfloat16 [5120, 2560], P(None, 'head')
- w_key: bfloat16 [5120, 2560], P(None, 'head')
- w_value: bfloat16 [5120, 2560], P(None, 'head'), may hold values from -0.078125 to 0.078125
- q_gain: float32 [2560], P('head'), may hold values from 0.5 to 6
- k_gain: float32 [2560], P('head'), may hold values from 0.5 to 6
Outputs:
- attended: bfloat16 [16, 512, 2560], P('tm', None, 'head')
All inputs are finite; a program needn't handle non-finite values.
Results may differ from a plain program's by a relative error of at most 0.0086.
Values may be sent and summed in bfloat16 or wider, within the bound.
No kernel may reach another device: no remote copies, remote signals or barrier semaphores. Data moves between devices by JAX's collectives and lax.ppermute only.
A program may use at most 192 MiB of HBM per device.

v0:
```python
import jax
import jax.numpy as jnp
from jax import lax
from jax.sharding import PartitionSpec as P

DH = 128


def padded_2(x, sides, width):
    for axis, dim in sides:
        count, length = (lax.axis_size(axis), x.shape[dim])
        up = [(i, (i + 1) % count) for i in range(count - 1)]
        down = [(j, i) for i, j in up]
        last = lax.slice_in_dim(x, length - width, length, axis=dim)
        initial = lax.slice_in_dim(x, 0, width, axis=dim)
        before = lax.ppermute(last, axis, up)
        after = lax.ppermute(initial, axis, down)
        x = jnp.concatenate([before, x, after], axis=dim)
    return x


def shifted(value, axis, steps):
    count = lax.axis_size(axis)
    initial, last = (max(0, -steps), min(count, count - steps))
    return lax.ppermute(value, axis, [(source, source + steps) for source in range(initial, last)])


def broadcast(x, axis, root):
    mine = lax.axis_index(axis) == root
    return lax.psum(jnp.where(mine, x, jnp.zeros_like(x)), axis)


def convolve(padded, taps, first, count):
    centre = padded[first : first + count].astype(jnp.float32)
    before = padded[first - 1 : first - 1 + count].astype(jnp.float32)
    after = padded[first + 1 : first + 1 + count].astype(jnp.float32)
    return (centre + taps[0] * before + taps[1] * centre + taps[2] * after).astype(jnp.bfloat16)


def normalize(projected, gain):
    heads_dev = projected.shape[1] // DH
    split_heads = projected.reshape(projected.shape[0], heads_dev, DH)
    mean_sq = jnp.mean(split_heads * split_heads, axis=-1, keepdims=True)
    scaled = split_heads * lax.rsqrt(mean_sq + 1e-06)
    return scaled.reshape(projected.shape[0], heads_dev * DH) * gain


def per_device(frames, taps, w_query, w_key, w_value, q_gain, k_gain):
    frame_dev = frames.shape[0]
    tok_count = frames.shape[1]
    padded = padded_2(frames, (("tm", 0),), 1)
    mixed = convolve(padded, taps, 1, frame_dev)
    frame_count = mixed.shape[0]
    tok_rows = mixed.reshape(frame_count * tok_count, mixed.shape[2])
    col_count = w_query.shape[1]
    heads_dev = col_count // DH
    piece = lax.all_gather(tok_rows, "head", axis=1, tiled=True)
    q_part = jnp.dot(piece, w_query, preferred_element_type=jnp.float32)
    k_part = jnp.dot(piece, w_key, preferred_element_type=jnp.float32)
    v_part = jnp.dot(piece, w_value, preferred_element_type=jnp.float32)
    query = (
        normalize(q_part, q_gain)
        .astype(jnp.bfloat16)
        .reshape(frame_count, tok_count, heads_dev, DH)
    )
    key_proj = (
        normalize(k_part, k_gain)
        .astype(jnp.bfloat16)
        .reshape(frame_count, tok_count, heads_dev, DH)
    )
    value_proj = v_part.astype(jnp.bfloat16).reshape(frame_count, tok_count, heads_dev, DH)
    stacked = jnp.stack([key_proj, value_proj], axis=1)
    at_start = lax.axis_index("tm") == 0
    received = shifted(stacked[-1], "tm", 1)
    previous = jnp.where(at_start, stacked[0], received)
    anchor = broadcast(stacked[0], "tm", 0)
    predecessors = jnp.concatenate([previous[None], stacked[:-1]], axis=0)
    anchors = jnp.broadcast_to(anchor[None], predecessors.shape)
    context = jnp.concatenate([anchors, predecessors], axis=2)
    scale = 1.0 / DH**0.5
    scores = (
        jnp.einsum("fqhd,fkhd->fhqk", query, context[:, 0], preferred_element_type=jnp.float32)
        * scale
    )
    top = jnp.max(scores, axis=-1, keepdims=True)
    expo = jnp.exp(scores - top)
    probs = (expo / jnp.sum(expo, axis=-1, keepdims=True)).astype(jnp.bfloat16)
    result = jnp.einsum("fhqk,fkhd->fqhd", probs, context[:, 1], preferred_element_type=jnp.float32)
    return result.astype(jnp.bfloat16).reshape(frame_dev, tok_count, heads_dev * DH)


def solution(mesh):
    placed = (
        P("tm", None, "head"),
        P(None, "head"),
        P(None, "head"),
        P(None, "head"),
        P(None, "head"),
        P("head"),
        P("head"),
    )
    return jax.shard_map(
        per_device, mesh=mesh, in_specs=placed, out_specs=P("tm", None, "head"), check_vma=False
    )
```

profile of v0, /device:TPU:10, one launch (start us, length us, event | category | flops | bytes accessed | tf_op | source)
XLA Modules:
  0.0 380.3 jit_solution(7993037469907127204)
XLA Ops:
  6.5 2.0 fusion.26
  8.6 1.9 collective-permute-start
  10.5 3.6 collective-permute-start.1
  14.2 13.3 %collective-permute-done = bf16[1,512,1280]{2,1,0:T(8,128)(2,1)S(1)} collective-permute-done((bf16[1,512,1280]{2,1,0:T(8,128)(2,1)S(1)}, bf16[1,512,1280]{2,1,0:T(8,128)(2,1)S(1)}, u32[]{:S(2)}, u32[]{:S(2)}) %collective-permute-start) | collective-permute-done | bytes 1310752 | tf_op jit(solution)/shard_map/ppermute | solution.py:16
  27.5 13.1 %collective-permute-done.1 = bf16[1,512,1280]{2,1,0:T(8,128)(2,1)S(1)} collective-permute-done((bf16[1,512,1280]{2,1,0:T(8,128)(2,1)S(1)}, bf16[1,512,1280]{2,1,0:T(8,128)(2,1)S(1)}, u32[]{:S(2)}, u32[]{:S(2)}) %collective-permute-start.1) | collective-permute-done | bytes 1310752 | tf_op jit(solution)/shard_map/ppermute | solution.py:17
  40.6 2.8 fusion.10
  43.4 182.9 %all-gather.2.cloned.1.call-done = bf16[1024,5120]{1,0:T(8,128)(2,1)} async-done(((bf16[1024,1280]{1,0:T(8,128)(2,1)}), bf16[1024,5120]{1,0:T(8,128)(2,1)}) %all-gather.2.cloned.1.call-update) | async-done | bytes 10485776 | tf_op jit(solution)/shard_map/all_gather | solution.py:57
  226.3 12.9 %convolution_convert_fusion = bf16[1024,640]{1,0:T(8,128)(2,1)S(1)} fusion(bf16[1024,5120]{1,0:T(8,128)(2,1)} %all-gather.2.cloned.1.call-done, bf16[5120,640]{1,0:T(8,128)(2,1)} %param.11), kind=kOutput, calls=%fused_computation.28 | convolution fusion | flops 6711541760 | bytes 18350080 | tf_op jit(solution)/shard_map/dot_general | solution.py:60
  240.9 13.1 %fusion.27 = (f32[1024,640]{0,1:T(8,128)}, f32[1024,640]{0,1:T(8,128)}) fusion(bf16[1024,5120]{1,0:T(8,128)(2,1)} %all-gather.2.cloned.1.call-done, bf16[5120,640]{1,0:T(8,128)(2,1)} %param.10), kind=kOutput, calls=%fused_computation.45 | convolution fusion | flops 6711541760 | bytes 22282240 | tf_op jit(solution)/shard_map/dot_general | solution.py:59
  254.1 2.0 reduce_sum.27
  256.1 2.0 fusion.14
  258.1 1.8 stack_reshape.6
  259.9 3.5 copy.16
  265.1 2.1 collective-permute-start.2
  267.2 17.1 %collective-permute-done.2 = bf16[2,512,5,128]{3,1,2,0:T(8,128)(2,1)} collective-permute-done((bf16[2,512,5,128]{3,1,2,0:T(8,128)(2,1)}, bf16[2,512,5,128]{3,1,2,0:T(8,128)(2,1)}, u32[]{:S(2)}, u32[]{:S(2)}) %collective-permute-start.2) | collective-permute-done | bytes 1310752 | tf_op jit(solution)/shard_map/ppermute | solution.py:25
  284.4 3.0 bitcast_select_fusion.1
  287.4 12.7 %fusion.28 = (f32[1024,640]{0,1:T(8,128)S(1)}, f32[1024,640]{0,1:T(8,128)}) fusion(bf16[1024,5120]{1,0:T(8,128)(2,1)} %all-gather.2.cloned.1.call-done, bf16[5120,640]{1,0:T(8,128)(2,1)} %param.9), kind=kOutput, calls=%fused_computation.46 | convolution fusion | flops 6711541760 | bytes 22282240 | tf_op jit(solution)/shard_map/dot_general | solution.py:58
  300.8 2.0 fusion.12
  302.9 1.8 reshape.42
  304.7 40.6 %all-reduce.2.cloned.1.call-done = bf16[2,512,5,128]{3,1,2,0:T(8,128)(2,1)} async-done(((bf16[2,512,5,128]{3,1,2,0:T(8,128)(2,1)}), bf16[2,512,5,128]{3,1,2,0:T(8,128)(2,1)}) %all-reduce.2.cloned.1.call-update) | async-done | bytes 1310736 | tf_op jit(solution)/shard_map/psum | solution.py:30
  345.3 1.8 broadcast_in_dim.7
  347.2 2.7 maximum_maximum_fusion
  349.9 12.6 %fusion.29 = (f32[2,5,512]{2,1,0:T(8,128)S(1)}, f32[2,5,512,1024]{3,2,1,0:T(8,128)}) fusion(bf16[2,2,1024,5,128]{4,2,3,0,1:T(8,128)(2,1)} %maximum_maximum_fusion, bf16[2,512,5,128]{1,0,3,2:T(2,128)(2,1)} %reshape.42), kind=kOutput, calls=%fused_computation.47 | convolution fusion | flops 1357906944 | bytes 24924160 | tf_op jit(solution)/shard_map/sub | solution.py:86
  362.4 9.5 %fusion.16 = bf16[2,5,128,512]{3,2,1,0:T(8,128)(2,1)S(1)} fusion(f32[2,5,512,1024]{3,2,1,0:T(8,128)} %get-tuple-element.19, f32[2,5,512]{2,1,0:T(8,128)S(1)} %get-tuple-element.18, bf16[2,2,1024,5,128]{4,2,3,0,1:T(8,128)(2,1)} %maximum_maximum_fusion), kind=kOutput, calls=%fused_computation.27 | convolution fusion | flops 1353318400 | bytes 24924160 | tf_op jit(solution)/shard_map/fhqk,fkhd->fqhd/dot_general | solution.py:88
  (24 shorter events, 5.7 us)
Async XLA Ops:
  6.5 34.0 %copy-start = (bf16[2,512,1280]{2,1,0:T(8,128)(2,1)S(1)}, bf16[2,512,1280]{2,1,0:T(8,128)(2,1)}, u32[]{:S(2)}) copy-start(bf16[2,512,1280]{2,1,0:T(8,128)(2,1)} %param.7) | copy-start | bytes 7864324
  6.5 7.6 %copy-start.3 = (f32[3,1280]{1,0:T(4,128)S(1)}, f32[3,1280]{1,0:T(4,128)}, u32[]{:S(2)}) copy-start(f32[3,1280]{1,0:T(4,128)} %param.8) | copy-start | bytes 46084
  6.5 219.8 %all-gather.2.cloned.1.call-start = ((), (), s32[]{:S(2)}) async-start(), calls=%async_computation | async-start | bytes 13107200 | tf_op jit(solution)/shard_map/all_gather | solution.py:57
  8.6 18.9 %collective-permute-start = (bf16[1,512,1280]{2,1,0:T(8,128)(2,1)S(1)}, bf16[1,512,1280]{2,1,0:T(8,128)(2,1)S(1)}, u32[]{:S(2)}, u32[]{:S(2)}) collective-permute-start(bf16[1,512,1280]{2,1,0:T(8,128)(2,1)S(1)} %get-tuple-element.12), channel_id=1, source_target_pairs={{0,4},{4,8},{8,12},{12,16},{16,20},{20,24},{24,28},{1,5},{5,9},{9,... | collective-permute-start | bytes 3932168 | tf_op jit(solution)/shard_map/ppermute | solution.py:16
  10.5 30.1 %collective-permute-start.1 = (bf16[1,512,1280]{2,1,0:T(8,128)(2,1)S(1)}, bf16[1,512,1280]{2,1,0:T(8,128)(2,1)S(1)}, u32[]{:S(2)}, u32[]{:S(2)}) collective-permute-start(bf16[1,512,1280]{2,1,0:T(8,128)(2,1)S(1)} %get-tuple-element.13), channel_id=1, source_target_pairs={{4,0},{8,4},{12,8},{16,12},{20,16},{24,20},{28,24},{5,1},{9,5},{13... | collective-permute-start | bytes 3932168 | tf_op jit(solution)/shard_map/ppermute | solution.py:17
  43.4 301.9 %all-reduce.2.cloned.1.call-start = ((), (), s32[]{:S(2)}) async-start(), calls=%async_computation.1 | async-start | bytes 2621440 | tf_op jit(solution)/shard_map/psum | solution.py:30
  254.1 2.0 copy-start.4
  265.1 19.2 %collective-permute-start.2 = (bf16[2,512,5,128]{3,1,2,0:T(8,128)(2,1)}, bf16[2,512,5,128]{3,1,2,0:T(8,128)(2,1)}, u32[]{:S(2)}, u32[]{:S(2)}) collective-permute-start(bf16[2,512,5,128]{3,1,2,0:T(8,128)(2,1)} %get-tuple-element.10), channel_id=1, source_target_pairs={{0,4},{4,8},{8,12},{12,16},{16,20},{20,24},{24,28},{1,5},{5,9},{9,... | collective-permute-start | bytes 3932168 | tf_op jit(solution)/shard_map/ppermute | solution.py:25
  300.1 0.7 copy-start.5
  304.7 42.5 %copy-start.1 = (bf16[1,2,512,5,128]{4,2,3,0,1:T(8,128)(2,1)S(1)}, bf16[1,2,512,5,128]{4,2,3,0,1:T(8,128)(2,1)}, u32[]{:S(2)}) copy-start(bf16[1,2,512,5,128]{4,2,3,0,1:T(8,128)(2,1)} %get-tuple-element.11) | copy-start | bytes 3932164
  304.7 42.5 %copy-start.2 = (bf16[1,2,512,5,128]{4,2,3,0,1:T(8,128)(2,1)S(1)}, bf16[1,2,512,5,128]{4,2,3,0,1:T(8,128)(2,1)}, u32[]{:S(2)}) copy-start(bf16[1,2,512,5,128]{4,2,3,0,1:T(8,128)(2,1)} %get-tuple-element.9) | copy-start | bytes 3932164
Sparse Core Ops, SparseCore 0:
  43.5 182.7 all-gather.1
  287.5 57.7 all-reduce.1
where the time goes:
time: 383 us; the launch traced here: 380 us
  waiting for transfers between devices  267 us (70%)
  matrix products  60.9 us (16%)
  other arithmetic  16.5 us (4%)
  local copies, waits for them, and re-layouts  14.7 us (4%)
  between operations  13.6 us (4%)
  starting transfers between devices  7.7 us (2%)
    all_gather x1, waiting for transfers between devices, per_device(): piece = lax.all_gather(tok_rows, 'head', axis=1, tiled=True)  183 us
    psum x1, waiting for transfers between devices, broadcast(): return lax.psum(jnp.where(mine, x, jnp.zeros_like(x)), axis)  40.6 us
    ppermute x1, waiting for transfers between devices, shifted(): lax.ppermute(value, axis, [(source, source + steps) for source in range(i...  17.1 us
    ppermute x1, waiting for transfers between devices, padded_2(): before = lax.ppermute(last, axis, up)  13.3 us
    dot_general x1, matrix products, per_device(): k_part = jnp.dot(piece, w_key, preferred_element_type=jnp.float32)  13.1 us
    ppermute x1, waiting for transfers between devices, padded_2(): after = lax.ppermute(initial, axis, down)  13.1 us
    dot_general x1, matrix products, per_device(): v_part = jnp.dot(piece, w_value, preferred_element_type=jnp.float32)  12.9 us
    dot_general x1, matrix products, per_device(): q_part = jnp.dot(piece, w_query, preferred_element_type=jnp.float32)  12.7 us
  transfers between devices with their start and end apart: 5, of which 5 were waited for; matrix products, arithmetic and copies ran while one was open for 4% of the time, Pallas kernels for 0%

commit v1 on v0

v1 whole, which is shorter than its diff:
```python
import functools

import jax
import jax.numpy as jnp
from jax import lax
from jax.experimental import pallas as pl
from jax.experimental.pallas import tpu as pltpu
from jax.sharding import PartitionSpec as P

DH = 128
BF16 = jnp.bfloat16
F32 = jnp.float32


def whole(shape):
    return pl.BlockSpec(shape, lambda *_: (0,) * len(shape))


def norm_heads(raw, gain, heads):
    cols = []
    for h in range(heads):
        part = raw[:, h * DH : (h + 1) * DH]
        mean_sq = jnp.mean(part * part, axis=-1, keepdims=True)
        scaled = part * lax.rsqrt(mean_sq + 1e-06)
        cols.append((scaled * gain[:, h * DH : (h + 1) * DH]).astype(BF16))
    return jnp.concatenate(cols, axis=1)


def project_body(count, halves, src_ref, *refs):
    xs = refs[:count]
    wq, wk, wv, qg, kg, q_out, kv_out, acc = refs[count:]
    step = pl.program_id(0)
    weight = jnp.concatenate([wq[...], wk[...], wv[...]], axis=1)
    for i in range(count):

        @pl.when(step // halves == i)
        def _(i=i):
            part = jnp.dot(xs[i][...], weight, preferred_element_type=F32)

            if i == 0:

                @pl.when(step == 0)
                def _():
                    acc[...] = part

                @pl.when(step != 0)
                def _():
                    acc[...] += part
            else:
                acc[...] += part

    @pl.when(step == count * halves - 1)
    def _():
        width = q_out.shape[1]
        heads = width // DH
        q_out[...] = norm_heads(acc[:, :width], qg[...], heads)
        kv_out[:, :width] = norm_heads(acc[:, width : 2 * width], kg[...], heads)
        kv_out[:, width:] = acc[:, 2 * width :].astype(BF16)


def project(xs, planes, w_query, w_key, w_value, q_gain, k_gain):
    count, halves = len(xs), 2
    rows, chans = xs[0].shape
    width = w_query.shape[1]
    depth = chans // halves
    x_specs = [
        pl.BlockSpec((rows, depth), lambda k, src, i=i: (0, jnp.clip(k - halves * i, 0, halves - 1)))
        for i in range(count)
    ]
    w_spec = pl.BlockSpec((depth, width), lambda k, src: (src[k // halves] * halves + k % halves, 0))
    g_spec = pl.BlockSpec((1, width), lambda k, src: (0, 0))
    return pl.pallas_call(
        functools.partial(project_body, count, halves),
        grid_spec=pltpu.PrefetchScalarGridSpec(
            num_scalar_prefetch=1,
            grid=(count * halves,),
            in_specs=x_specs + [w_spec] * 3 + [g_spec] * 2,
            out_specs=[
                pl.BlockSpec((rows, width), lambda k, src: (0, 0)),
                pl.BlockSpec((rows, 2 * width), lambda k, src: (0, 0)),
            ],
            scratch_shapes=[pltpu.VMEM((rows, 3 * width), F32)],
        ),
        out_shape=[
            jax.ShapeDtypeStruct((rows, width), BF16),
            jax.ShapeDtypeStruct((rows, 2 * width), BF16),
        ],
        compiler_params=pltpu.CompilerParams(vmem_limit_bytes=48 * 2**20),
        cost_estimate=pl.CostEstimate(
            flops=2 * rows * count * chans * 3 * width,
            bytes_accessed=2 * count * chans * (rows + 3 * width) + 6 * rows * width,
            transcendentals=0,
        ),
        name="project",
    )(jnp.stack(planes).astype(jnp.int32), *xs, w_query, w_key, w_value, q_gain[None], k_gain[None])


def attend_body(row_block, pos_ref, q1, q2, *refs):
    keys, values, out = refs[:5], refs[5:10], refs[10]
    pos = pos_ref[0]
    slot = pl.program_id(1)

    def pick(blocks):
        own1, own2, shift1, shift2 = (blocks[i][...] for i in range(1, 5))
        for_first = jnp.where(pos == 0, own1, own2)
        for_second = jnp.where(pos == 0, own1, jnp.where(pos == 1, shift2, shift1))
        return jnp.where(slot == 0, for_first, for_second)

    factor = 1.4426950408889634 / DH**0.5
    key = jnp.concatenate([keys[0][...], pick(keys)], axis=0)
    value = jnp.concatenate([values[0][...], pick(values)], axis=0)
    rows = q1.shape[0]
    for r in range(rows // row_block):
        span = pl.ds(r * row_block, row_block)
        query = jnp.where(slot == 0, q1[span, :], q2[span, :])
        scores = lax.dot_general(query, key, (((1,), (1,)), ((), ())), preferred_element_type=F32)
        top = jnp.max(scores, axis=-1, keepdims=True)
        expo = jnp.exp2((scores - top) * factor)
        total = jnp.sum(expo, axis=-1, keepdims=True)
        result = jnp.dot(expo.astype(BF16), value, preferred_element_type=F32)
        out[0, span, :] = (result / total).astype(BF16)


def attend(pos, q1, q2, anchor, own1, own2, shift1, shift2):
    rows, width = q1.shape
    heads = width // DH
    q_spec = pl.BlockSpec((rows, DH), lambda h, f, pos: (0, h))
    k_spec = pl.BlockSpec((rows, DH), lambda h, f, pos: (0, h))
    v_spec = pl.BlockSpec((rows, DH), lambda h, f, pos: (0, heads + h))
    kv = (anchor, own1, own2, shift1, shift2)
    return pl.pallas_call(
        functools.partial(attend_body, 256),
        grid_spec=pltpu.PrefetchScalarGridSpec(
            num_scalar_prefetch=1,
            grid=(heads, 2),
            in_specs=[q_spec] * 2 + [k_spec] * 5 + [v_spec] * 5,
            out_specs=pl.BlockSpec(
                (1, rows, DH), lambda h, f, pos: (jnp.where(pos[0] == 0, f, 1 - f), 0, h)
            ),
        ),
        out_shape=jax.ShapeDtypeStruct((2, rows, width), BF16),
        compiler_params=pltpu.CompilerParams(vmem_limit_bytes=48 * 2**20),
        cost_estimate=pl.CostEstimate(
            flops=16 * heads * rows * rows * DH,
            bytes_accessed=2 * rows * width * 14,
            transcendentals=4 * heads * rows * rows,
        ),
        name="attend",
    )(pos[None].astype(jnp.int32), q1, q2, *kv, *kv)


def broadcast_first(x, axis):
    count = lax.axis_size(axis)
    mine = lax.axis_index(axis)
    step = count // 2
    held = x
    while step:
        pairs = [(i, i + step) for i in range(0, count, 2 * step)]
        got = lax.ppermute(held, axis, pairs)
        held = jnp.where(mine % (2 * step) == step, got, held)
        step //= 2
    return held


def gather_line(x, axis):
    count = lax.axis_size(axis)
    z = lax.axis_index(axis)
    ups = [(i, i + 1) for i in range(count - 1)]
    downs = [(j, i) for i, j in ups]
    up, down = [x], [x]
    for _ in range(count - 1):
        up.append(lax.ppermute(up[-1], axis, ups))
        down.append(lax.ppermute(down[-1], axis, downs))
    return [x] + [jnp.where(z + k < count, down[k], up[count - k]) for k in range(1, count)]


def mix(before, centre, after, taps):
    before, centre, after = (v.astype(F32) for v in (before, centre, after))
    return (centre + taps[0] * before + taps[1] * centre + taps[2] * after).astype(BF16)


def per_device(frames, taps, w_query, w_key, w_value, q_gain, k_gain):
    count = lax.axis_size("tm")
    pos = lax.axis_index("tm")
    planes = lax.axis_size("head")
    z = lax.axis_index("head")
    first, last = frames[0], frames[1]
    ups = [(i, i + 1) for i in range(count - 1)]
    following = lax.ppermute(first, "tm", [(j, i) for i, j in ups])
    preceding = lax.ppermute(last, "tm", ups)
    start = pos == 0
    mixed1 = mix(
        jnp.where(start, jnp.zeros_like(first), first),
        jnp.where(start, first, last),
        jnp.where(start, last, following),
        taps,
    )
    mixed2 = mix(
        jnp.where(start, first, preceding),
        jnp.where(start, last, first),
        jnp.where(start, following, last),
        taps,
    )
    order = [(z + k) % planes for k in range(planes)]
    weights = (w_query, w_key, w_value, q_gain, k_gain)
    q1, kv1 = project(gather_line(mixed1, "head"), order, *weights)
    anchor = broadcast_first(kv1, "tm")
    shift1 = lax.ppermute(kv1, "tm", [(i, i + 1) for i in range(1, count - 1)])
    q2, kv2 = project(gather_line(mixed2, "head"), order, *weights)
    shift2 = lax.ppermute(kv2, "tm", [(0, 1)])
    return attend(pos, q1, q2, anchor, kv1, kv2, shift1, shift2)


def solution(mesh):
    placed = (
        P("tm", None, "head"),
        P(None, "head"),
        P(None, "head"),
        P(None, "head"),
        P(None, "head"),
        P("head"),
        P("head"),
    )
    return jax.shard_map(
        per_device, mesh=mesh, in_specs=placed, out_specs=P("tm", None, "head"), check_vma=False
    )
```

time: 383 us -> 271 us (0.71)
  waiting for transfers between devices: 267 us -> 136 us
  matrix products: 60.9 us -> 0 us
  Pallas kernels: 0 us -> 55.6 us
  starting transfers between devices: 7.7 us -> 53.9 us
  between operations: 13.6 us -> 0.42 us
  local copies, waits for them, and re-layouts: 14.7 us -> 4.91 us
    all_gather x1 -> x0, waiting for transfers between devices: 183 us -> none  [per_device(): piece = lax.all_gather(tok_rows, 'head', axis=1, tiled=True)]
    ppermute x3 -> x19, waiting for transfers between devices: 43.5 us -> 136 us  [the longest x6 97.3 us: gather_line(): up.append(lax.ppermute(up[-1], axis, ups))]
    pallas_call x0 -> x3, Pallas kernels: none -> 55.6 us  [the longest x2 41 us: project(): pl.pallas_call(functools.partial(project_body, count, halves), grid_spec=...]
    dot_general x4 -> x0, matrix products: 48.3 us -> none  [the longest x1 13.1 us: per_device(): k_part = jnp.dot(piece, w_key, preferred_element_type=jnp.float32)]
    ppermute x3 -> x19, starting transfers between devices: 7.65 us -> 53.9 us  [the longest x6 20.2 us: gather_line(): up.append(lax.ppermute(up[-1], axis, ups))]
    psum x1 -> x0, waiting for transfers between devices: 40.6 us -> none  [broadcast(): return lax.psum(jnp.where(mine, x, jnp.zeros_like(x)), axis)]
    sub x1 -> x0, matrix products: 12.6 us -> none  [per_device(): expo = jnp.exp(scores - top)]
    select_n x1 -> x9, other arithmetic: 3.01 us -> 12.4 us  [the longest x6 9.54 us: gather_line(): jnp.where(z + k < count, down[k], up[count - k])]
  transfers between devices with their start and end apart: 5 -> 19, of which waited for: 5 -> 14; matrix products, arithmetic and copies ran while one was open for 4% -> 5% of each run, Pallas kernels for 0% -> 15%
where the time goes in v1:
time: 271 us; the launch traced here: 267 us
  waiting for transfers between devices  136 us (50%)
  Pallas kernels  55.6 us (21%)
  starting transfers between devices  53.9 us (20%)
  other arithmetic  16.2 us (6%)
  local copies, waits for them, and re-layouts  4.91 us (2%)
    ppermute x6, waiting for transfers between devices, gather_line(): up.append(lax.ppermute(up[-1], axis, ups))  97.3 us
    pallas_call x2, Pallas kernels, project(): pl.pallas_call(functools.partial(project_body, count, halves), grid_spec=...  41 us
    ppermute x1, waiting for transfers between devices, per_device(): following = lax.ppermute(first, 'tm', [(j, i) for i, j in ups])  23.4 us
    ppermute x6, starting transfers between devices, gather_line(): up.append(lax.ppermute(up[-1], axis, ups))  20.2 us
    ppermute x6, starting transfers between devices, gather_line(): down.append(lax.ppermute(down[-1], axis, downs))  18.2 us
    pallas_call x1, Pallas kernels, attend(): pl.pallas_call(functools.partial(attend_body, 256), grid_spec=pltpu.Prefe...  14.6 us
    ppermute x6, waiting for transfers between devices, gather_line(): down.append(lax.ppermute(down[-1], axis, downs))  10.4 us
    select_n x6, other arithmetic, gather_line(): jnp.where(z + k < count, down[k], up[count - k])  9.54 us
  transfers between devices with their start and end apart: 19, of which 14 were waited for; matrix products, arithmetic and copies ran while one was open for 5% of the time, Pallas kernels for 15%

profile of v1, /device:TPU:10, one launch (start us, length us, event | category | flops | bytes accessed | tf_op | source)
XLA Modules:
  0.0 267.1 jit_solution(6834315957137759451)
XLA Ops:
  0.0 2.9 %slice_bitcast_fusion = (bf16[512,1280]{1,0:T(8,128)(2,1)S(1)}, bf16[512,1280]{1,0:T(8,128)(2,1)}) fusion(bf16[2,512,1280]{2,1,0:T(8,128)(2,1)} %param.7), kind=kLoop, calls=%fused_computation.10 | loop fusion | bytes 5242880 | tf_op jit(solution)/shard_map/squeeze | solution.py:187
  7.4 23.4 %collective-permute-done = bf16[512,1280]{1,0:T(8,128)(2,1)S(1)} collective-permute-done((bf16[512,1280]{1,0:T(8,128)(2,1)}, bf16[512,1280]{1,0:T(8,128)(2,1)S(1)}, u32[]{:S(2)}, u32[]{:S(2)}) %collective-permute-start) | collective-permute-done | bytes 1310752 | tf_op jit(solution)/shard_map/ppermute | solution.py:189
  31.8 3.7 %fusion.5 = (bf16[512,1280]{1,0:T(8,128)(2,1)S(1)}, bf16[512,1280]{1,0:T(8,128)(2,1)S(1)}) fusion(bf16[512,1280]{1,0:T(8,128)(2,1)} %copy-done.4, bf16[512,1280]{1,0:T(8,128)(2,1)} %collective-permute-done.7, f32[1280]{0:T(1024)S(1)} %get-tuple-element.14, f32[1280]{0:T(1024)S(1)} %get-tuple-element.15, f32[1280]{0:T(1024)S(1)} %get-tuple-element.13, ...), kind=kLoop, calls=%fused_computation.9 | loop fusion | flops 17039360 | bytes 7879681 | tf_op jit(solution)/shard_map/convert_element_type | solution.py:179
  35.6 3.5 %collective-permute-start.2 = (bf16[512,1280]{1,0:T(8,128)(2,1)S(1)}, bf16[512,1280]{1,0:T(8,128)(2,1)S(1)}, u32[]{:S(2)}, u32[]{:S(2)}) collective-permute-start(bf16[512,1280]{1,0:T(8,128)(2,1)S(1)} %get-tuple-element.17.refs_0_), channel_id=1, source_target_pairs={{0,1},{1,2},{2,3},{4,5},{5,6},{6,7},{8,9},{9,10},{10,11},{12,13},{... | collective-permute-start | bytes 3932168 | tf_op jit(solution)/shard_map/ppermute | solution.py:172
  41.5 24.3 %collective-permute-done.2 = bf16[512,1280]{1,0:T(8,128)(2,1)S(1)} collective-permute-done((bf16[512,1280]{1,0:T(8,128)(2,1)S(1)}, bf16[512,1280]{1,0:T(8,128)(2,1)S(1)}, u32[]{:S(2)}, u32[]{:S(2)}) %collective-permute-start.2) | collective-permute-done | bytes 1310752 | tf_op jit(solution)/shard_map/ppermute | solution.py:172
  65.8 3.5 %collective-permute-start.3 = (bf16[512,1280]{1,0:T(8,128)(2,1)S(1)}, bf16[512,1280]{1,0:T(8,128)(2,1)}, u32[]{:S(2)}, u32[]{:S(2)}) collective-permute-start(bf16[512,1280]{1,0:T(8,128)(2,1)S(1)} %collective-permute-done.2), channel_id=1, source_target_pairs={{0,1},{1,2},{2,3},{4,5},{5,6},{6,7},{8,9},{9,10},{10,11},{12,13},{... | collective-permute-start | bytes 3932168 | tf_op jit(solution)/shard_map/ppermute | solution.py:172
  69.7 3.0 %collective-permute-start.5 = (bf16[512,1280]{1,0:T(8,128)(2,1)}, bf16[512,1280]{1,0:T(8,128)(2,1)}, u32[]{:S(2)}, u32[]{:S(2)}) collective-permute-start(bf16[512,1280]{1,0:T(8,128)(2,1)} %collective-permute-done.1), channel_id=1, source_target_pairs={{1,0},{2,1},{3,2},{5,4},{6,5},{7,6},{9,8},{10,9},{11,10},{13,12},{... | collective-permute-start | bytes 3932168 | tf_op jit(solution)/shard_map/ppermute | solution.py:173
  75.5 4.1 %collective-permute-start.8 = (bf16[512,1280]{1,0:T(8,128)(2,1)S(1)}, bf16[512,1280]{1,0:T(8,128)(2,1)}, u32[]{:S(2)}, u32[]{:S(2)}) collective-permute-start(bf16[512,1280]{1,0:T(8,128)(2,1)S(1)} %get-tuple-element.16.refs_0_), channel_id=1, source_target_pairs={{1,0},{2,1},{3,2},{5,4},{6,5},{7,6},{9,8},{10,9},{11,10},{13,12},{... | collective-permute-start | bytes 3932168 | tf_op jit(solution)/shard_map/ppermute | solution.py:173
  79.6 17.2 %collective-permute-done.3 = bf16[512,1280]{1,0:T(8,128)(2,1)} collective-permute-done((bf16[512,1280]{1,0:T(8,128)(2,1)S(1)}, bf16[512,1280]{1,0:T(8,128)(2,1)}, u32[]{:S(2)}, u32[]{:S(2)}) %collective-permute-start.3) | collective-permute-done | bytes 1310752 | tf_op jit(solution)/shard_map/ppermute | solution.py:172
  96.7 3.5 %collective-permute-start.4 = (bf16[512,1280]{1,0:T(8,128)(2,1)}, bf16[512,1280]{1,0:T(8,128)(2,1)}, u32[]{:S(2)}, u32[]{:S(2)}) collective-permute-start(bf16[512,1280]{1,0:T(8,128)(2,1)} %collective-permute-done.3), channel_id=1, source_target_pairs={{0,1},{1,2},{2,3},{4,5},{5,6},{6,7},{8,9},{9,10},{10,11},{12,13},{... | collective-permute-start | bytes 3932168 | tf_op jit(solution)/shard_map/ppermute | solution.py:172
  104.2 20.6 %collective-permute-done.9 = bf16[512,1280]{1,0:T(8,128)(2,1)} collective-permute-done((bf16[512,1280]{1,0:T(8,128)(2,1)S(1)}, bf16[512,1280]{1,0:T(8,128)(2,1)}, u32[]{:S(2)}, u32[]{:S(2)}) %collective-permute-start.9) | collective-permute-done | bytes 1310752 | tf_op jit(solution)/shard_map/ppermute | solution.py:172
  124.8 3.5 %collective-permute-start.10 = (bf16[512,1280]{1,0:T(8,128)(2,1)}, bf16[512,1280]{1,0:T(8,128)(2,1)}, u32[]{:S(2)}, u32[]{:S(2)}) collective-permute-start(bf16[512,1280]{1,0:T(8,128)(2,1)} %collective-permute-done.9), channel_id=1, source_target_pairs={{0,1},{1,2},{2,3},{4,5},{5,6},{6,7},{8,9},{9,10},{10,11},{12,13},{... | collective-permute-start | bytes 3932168 | tf_op jit(solution)/shard_map/ppermute | solution.py:172
  129.3 2.9 %collective-permute-start.12 = (bf16[512,1280]{1,0:T(8,128)(2,1)}, bf16[512,1280]{1,0:T(8,128)(2,1)}, u32[]{:S(2)}, u32[]{:S(2)}) collective-permute-start(bf16[512,1280]{1,0:T(8,128)(2,1)} %collective-permute-done.8), channel_id=1, source_target_pairs={{1,0},{2,1},{3,2},{5,4},{6,5},{7,6},{9,8},{10,9},{11,10},{13,12},{... | collective-permute-start | bytes 3932168 | tf_op jit(solution)/shard_map/ppermute | solution.py:173
  133.7 19.2 %collective-permute-done.4 = bf16[512,1280]{1,0:T(8,128)(2,1)} collective-permute-done((bf16[512,1280]{1,0:T(8,128)(2,1)}, bf16[512,1280]{1,0:T(8,128)(2,1)}, u32[]{:S(2)}, u32[]{:S(2)}) %collective-permute-start.4) | collective-permute-done | bytes 1310752 | tf_op jit(solution)/shard_map/ppermute | solution.py:172
  154.4 2.9 %collective-permute-done.6 = bf16[512,1280]{1,0:T(8,128)(2,1)S(1)} collective-permute-done((bf16[512,1280]{1,0:T(8,128)(2,1)}, bf16[512,1280]{1,0:T(8,128)(2,1)S(1)}, u32[]{:S(2)}, u32[]{:S(2)}) %collective-permute-start.6) | collective-permute-done | bytes 1310752 | tf_op jit(solution)/shard_map/ppermute | solution.py:173
  158.5 20.5 %project.2 = (bf16[512,640]{1,0:T(8,128)(2,1)S(1)}, bf16[512,1280]{1,0:T(8,128)(2,1)S(1)}) custom-call(s32[4]{0:T(128)S(1)} %pad_add_fusion.src_ref, bf16[512,1280]{1,0:T(8,128)(2,1)S(1)} %get-tuple-element.17.refs_0_, bf16[512,1280]{1,0:T(8,128)(2,1)S(1)} %broadcast_select_fusion.8.refs_1_, bf16[512,1280]{1,0:T(8,128)(2,1)S(1)} %broadcast_select_fusion.6.refs_2_, ...), custom_call_target="tpu_custom_call" | custom-call | flops 10066329600 | bytes 26869760 | tf_op jit(solution)/shard_map/project/pallas_call | solution.py:72
  181.0 3.5 %collective-permute-start.11 = (bf16[512,1280]{1,0:T(8,128)(2,1)}, bf16[512,1280]{1,0:T(8,128)(2,1)S(1)}, u32[]{:S(2)}, u32[]{:S(2)}) collective-permute-start(bf16[512,1280]{1,0:T(8,128)(2,1)} %collective-permute-done.10), channel_id=1, source_target_pairs={{0,1},{1,2},{2,3},{4,5},{5,6},{6,7},{8,9},{9,10},{10,11},{12,13},{... | collective-permute-start | bytes 3932168 | tf_op jit(solution)/shard_map/ppermute | solution.py:172
  185.5 2.9 %collective-permute-start.13 = (bf16[512,1280]{1,0:T(8,128)(2,1)}, bf16[512,1280]{1,0:T(8,128)(2,1)S(1)}, u32[]{:S(2)}, u32[]{:S(2)}) collective-permute-start(bf16[512,1280]{1,0:T(8,128)(2,1)} %collective-permute-done.12), channel_id=1, source_target_pairs={{1,0},{2,1},{3,2},{5,4},{6,5},{7,6},{9,8},{10,9},{11,10},{13,12},{... | collective-permute-start | bytes 3932168 | tf_op jit(solution)/shard_map/ppermute | solution.py:173
  191.3 4.1 %collective-permute-start.17 = (bf16[512,1280]{1,0:T(8,128)(2,1)S(1)}, bf16[512,1280]{1,0:T(8,128)(2,1)}, u32[]{:S(2)}, u32[]{:S(2)}) collective-permute-start(bf16[512,1280]{1,0:T(8,128)(2,1)S(1)} %get-tuple-element.11.refs_1_.refs_6_), channel_id=1, source_target_pairs={{4,8},{8,12},{12,16},{16,20},{20,24},{24,28},{5,9},{9,13},{13,17},... | collective-permute-start | bytes 3932168 | tf_op jit(solution)/shard_map/ppermute | solution.py:208
  195.4 15.7 %collective-permute-done.11 = bf16[512,1280]{1,0:T(8,128)(2,1)S(1)} collective-permute-done((bf16[512,1280]{1,0:T(8,128)(2,1)}, bf16[512,1280]{1,0:T(8,128)(2,1)S(1)}, u32[]{:S(2)}, u32[]{:S(2)}) %collective-permute-start.11) | collective-permute-done | bytes 1310752 | tf_op jit(solution)/shard_map/ppermute | solution.py:172
  212.6 4.3 %collective-permute-done.13 = bf16[512,1280]{1,0:T(8,128)(2,1)S(1)} collective-permute-done((bf16[512,1280]{1,0:T(8,128)(2,1)}, bf16[512,1280]{1,0:T(8,128)(2,1)S(1)}, u32[]{:S(2)}, u32[]{:S(2)}) %collective-permute-start.13) | collective-permute-done | bytes 1310752 | tf_op jit(solution)/shard_map/ppermute | solution.py:173
  219.4 4.9 %collective-permute-done.15 = bf16[512,1280]{1,0:T(8,128)(2,1)S(1)} collective-permute-done((bf16[512,1280]{1,0:T(8,128)(2,1)S(1)}, bf16[512,1280]{1,0:T(8,128)(2,1)S(1)}, u32[]{:S(2)}, u32[]{:S(2)}) %collective-permute-start.15) | collective-permute-done | bytes 1310752 | tf_op jit(solution)/shard_map/ppermute | solution.py:159
  227.9 20.5 %project.3 = (bf16[512,640]{1,0:T(8,128)(2,1)S(1)}, bf16[512,1280]{1,0:T(8,128)(2,1)S(1)}) custom-call(s32[4]{0:T(128)S(1)} %pad_add_fusion.src_ref, bf16[512,1280]{1,0:T(8,128)(2,1)S(1)} %copy-done.1, bf16[512,1280]{1,0:T(8,128)(2,1)S(1)} %broadcast_select_fusion.7.refs_1_, bf16[512,1280]{1,0:T(8,128)(2,1)S(1)} %broadcast_select_fusion.5.refs_2_, ...), custom_call_target="tpu_custom_call" | custom-call | flops 10066329600 | bytes 26869760 | tf_op jit(solution)/shard_map/project/pallas_call | solution.py:72
  252.5 14.6 %attend.1 = bf16[2,512,640]{2,1,0:T(8,128)(2,1)} custom-call(s32[1]{0:T(128)} %bitcast.pos_ref, bf16[512,640]{1,0:T(8,128)(2,1)S(1)} %get-tuple-element.9.q1, bf16[512,640]{1,0:T(8,128)(2,1)S(1)} %copy-done.3, bf16[512,1280]{1,0:T(8,128)(2,1)S(1)} %broadcast_select_fusion.2.refs_0_.refs_5_, bf16[512,1280]{1,0:T(8,128)(2,1)S(1)} %get-tuple-element.11.refs_1_.refs_6_, ...), custom_call_target="tpu_custom_call" | custom-call | flops 2684354560 | bytes 9175040 | tf_op jit(solution)/shard_map/attend/pallas_call | solution.py:131
  (52 shorter events, 37.6 us)
Async XLA Ops:
  3.0 27.8 %collective-permute-start = (bf16[512,1280]{1,0:T(8,128)(2,1)}, bf16[512,1280]{1,0:T(8,128)(2,1)S(1)}, u32[]{:S(2)}, u32[]{:S(2)}) collective-permute-start(bf16[512,1280]{1,0:T(8,128)(2,1)} %get-tuple-element.19), channel_id=1, source_target_pairs={{4,0},{8,4},{12,8},{16,12},{20,16},{24,20},{28,24},{5,1},{9,5},{13... | collective-permute-start | bytes 3932168 | tf_op jit(solution)/shard_map/ppermute | solution.py:189
  4.9 25.9 %collective-permute-start.7 = (bf16[512,1280]{1,0:T(8,128)(2,1)S(1)}, bf16[512,1280]{1,0:T(8,128)(2,1)}, u32[]{:S(2)}, u32[]{:S(2)}) collective-permute-start(bf16[512,1280]{1,0:T(8,128)(2,1)S(1)} %get-tuple-element.18), channel_id=1, source_target_pairs={{0,4},{4,8},{8,12},{12,16},{16,20},{20,24},{24,28},{1,5},{5,9},{9,... | collective-permute-start | bytes 3932168 | tf_op jit(solution)/shard_map/ppermute | solution.py:190
  31.8 68.4 %copy-start.8 = (f32[640]{0:T(1024)S(1)}, f32[640]{0:T(1024)}, u32[]{:S(2)}) copy-start(f32[640]{0:T(1024)} %param.12) | copy-start | bytes 7684
  31.8 68.5 %copy-start.9 = (f32[640]{0:T(1024)S(1)}, f32[640]{0:T(1024)}, u32[]{:S(2)}) copy-start(f32[640]{0:T(1024)} %param.13) | copy-start | bytes 7684
  35.6 98.1 %copy-start = (bf16[512,1280]{1,0:T(8,128)(2,1)}, bf16[512,1280]{1,0:T(8,128)(2,1)S(1)}, u32[]{:S(2)}) copy-start(bf16[512,1280]{1,0:T(8,128)(2,1)S(1)} %get-tuple-element.16.refs_0_) | copy-start | bytes 3932164
  35.6 30.2 %collective-permute-start.2 = (bf16[512,1280]{1,0:T(8,128)(2,1)S(1)}, bf16[512,1280]{1,0:T(8,128)(2,1)S(1)}, u32[]{:S(2)}, u32[]{:S(2)}) collective-permute-start(bf16[512,1280]{1,0:T(8,128)(2,1)S(1)} %get-tuple-element.17.refs_0_), channel_id=1, source_target_pairs={{0,1},{1,2},{2,3},{4,5},{5,6},{6,7},{8,9},{9,10},{10,11},{12,13},{... | collective-permute-start | bytes 3932168 | tf_op jit(solution)/shard_map/ppermute | solution.py:172
  39.1 30.6 %collective-permute-start.1 = (bf16[512,1280]{1,0:T(8,128)(2,1)S(1)}, bf16[512,1280]{1,0:T(8,128)(2,1)}, u32[]{:S(2)}, u32[]{:S(2)}) collective-permute-start(bf16[512,1280]{1,0:T(8,128)(2,1)S(1)} %get-tuple-element.17.refs_0_), channel_id=1, source_target_pairs={{1,0},{2,1},{3,2},{5,4},{6,5},{7,6},{9,8},{10,9},{11,10},{13,12},{... | collective-permute-start | bytes 3932168 | tf_op jit(solution)/shard_map/ppermute | solution.py:173
  65.8 31.0 %collective-permute-start.3 = (bf16[512,1280]{1,0:T(8,128)(2,1)S(1)}, bf16[512,1280]{1,0:T(8,128)(2,1)}, u32[]{:S(2)}, u32[]{:S(2)}) collective-permute-start(bf16[512,1280]{1,0:T(8,128)(2,1)S(1)} %collective-permute-done.2), channel_id=1, source_target_pairs={{0,1},{1,2},{2,3},{4,5},{5,6},{6,7},{8,9},{9,10},{10,11},{12,13},{... | collective-permute-start | bytes 3932168 | tf_op jit(solution)/shard_map/ppermute | solution.py:172
  69.7 31.6 %collective-permute-start.5 = (bf16[512,1280]{1,0:T(8,128)(2,1)}, bf16[512,1280]{1,0:T(8,128)(2,1)}, u32[]{:S(2)}, u32[]{:S(2)}) collective-permute-start(bf16[512,1280]{1,0:T(8,128)(2,1)} %collective-permute-done.1), channel_id=1, source_target_pairs={{1,0},{2,1},{3,2},{5,4},{6,5},{7,6},{9,8},{10,9},{11,10},{13,12},{... | collective-permute-start | bytes 3932168 | tf_op jit(solution)/shard_map/ppermute | solution.py:173
  72.7 52.2 %collective-permute-start.9 = (bf16[512,1280]{1,0:T(8,128)(2,1)S(1)}, bf16[512,1280]{1,0:T(8,128)(2,1)}, u32[]{:S(2)}, u32[]{:S(2)}) collective-permute-start(bf16[512,1280]{1,0:T(8,128)(2,1)S(1)} %get-tuple-element.16.refs_0_), channel_id=1, source_target_pairs={{0,1},{1,2},{2,3},{4,5},{5,6},{6,7},{8,9},{9,10},{10,11},{12,13},{... | collective-permute-start | bytes 3932168 | tf_op jit(solution)/shard_map/ppermute | solution.py:172
  75.5 53.8 %collective-permute-start.8 = (bf16[512,1280]{1,0:T(8,128)(2,1)S(1)}, bf16[512,1280]{1,0:T(8,128)(2,1)}, u32[]{:S(2)}, u32[]{:S(2)}) collective-permute-start(bf16[512,1280]{1,0:T(8,128)(2,1)S(1)} %get-tuple-element.16.refs_0_), channel_id=1, source_target_pairs={{1,0},{2,1},{3,2},{5,4},{6,5},{7,6},{9,8},{10,9},{11,10},{13,12},{... | collective-permute-start | bytes 3932168 | tf_op jit(solution)/shard_map/ppermute | solution.py:173
  96.7 56.2 %collective-permute-start.4 = (bf16[512,1280]{1,0:T(8,128)(2,1)}, bf16[512,1280]{1,0:T(8,128)(2,1)}, u32[]{:S(2)}, u32[]{:S(2)}) collective-permute-start(bf16[512,1280]{1,0:T(8,128)(2,1)} %collective-permute-done.3), channel_id=1, source_target_pairs={{0,1},{1,2},{2,3},{4,5},{5,6},{6,7},{8,9},{9,10},{10,11},{12,13},{... | collective-permute-start | bytes 3932168 | tf_op jit(solution)/shard_map/ppermute | solution.py:172
  101.2 56.1 %collective-permute-start.6 = (bf16[512,1280]{1,0:T(8,128)(2,1)}, bf16[512,1280]{1,0:T(8,128)(2,1)S(1)}, u32[]{:S(2)}, u32[]{:S(2)}) collective-permute-start(bf16[512,1280]{1,0:T(8,128)(2,1)} %collective-permute-done.5), channel_id=1, source_target_pairs={{1,0},{2,1},{3,2},{5,4},{6,5},{7,6},{9,8},{10,9},{11,10},{13,12},{... | collective-permute-start | bytes 3932168 | tf_op jit(solution)/shard_map/ppermute | solution.py:173
  124.8 56.2 %collective-permute-start.10 = (bf16[512,1280]{1,0:T(8,128)(2,1)}, bf16[512,1280]{1,0:T(8,128)(2,1)}, u32[]{:S(2)}, u32[]{:S(2)}) collective-permute-start(bf16[512,1280]{1,0:T(8,128)(2,1)} %collective-permute-done.9), channel_id=1, source_target_pairs={{0,1},{1,2},{2,3},{4,5},{5,6},{6,7},{8,9},{9,10},{10,11},{12,13},{... | collective-permute-start | bytes 3932168 | tf_op jit(solution)/shard_map/ppermute | solution.py:172
  129.3 56.2 %collective-permute-start.12 = (bf16[512,1280]{1,0:T(8,128)(2,1)}, bf16[512,1280]{1,0:T(8,128)(2,1)}, u32[]{:S(2)}, u32[]{:S(2)}) collective-permute-start(bf16[512,1280]{1,0:T(8,128)(2,1)} %collective-permute-done.8), channel_id=1, source_target_pairs={{1,0},{2,1},{3,2},{5,4},{6,5},{7,6},{9,8},{10,9},{11,10},{13,12},{... | collective-permute-start | bytes 3932168 | tf_op jit(solution)/shard_map/ppermute | solution.py:173
  133.7 23.6 %copy-start.6 = (bf16[512,1280]{1,0:T(8,128)(2,1)S(1)}, bf16[512,1280]{1,0:T(8,128)(2,1)}, u32[]{:S(2)}) copy-start(bf16[512,1280]{1,0:T(8,128)(2,1)} %copy-done.5) | copy-start | bytes 3932164
  179.0 9.4 %collective-permute-start.14 = (bf16[512,1280]{1,0:T(8,128)(2,1)S(1)}, bf16[512,1280]{1,0:T(8,128)(2,1)}, u32[]{:S(2)}, u32[]{:S(2)}) collective-permute-start(bf16[512,1280]{1,0:T(8,128)(2,1)S(1)} %get-tuple-element.11.refs_1_.refs_6_), channel_id=1, source_target_pairs={{0,16},{1,17},{2,18},{3,19}} | collective-permute-start | bytes 3932168 | tf_op jit(solution)/shard_map/ppermute | solution.py:159
  181.0 30.1 %collective-permute-start.11 = (bf16[512,1280]{1,0:T(8,128)(2,1)}, bf16[512,1280]{1,0:T(8,128)(2,1)S(1)}, u32[]{:S(2)}, u32[]{:S(2)}) collective-permute-start(bf16[512,1280]{1,0:T(8,128)(2,1)} %collective-permute-done.10), channel_id=1, source_target_pairs={{0,1},{1,2},{2,3},{4,5},{5,6},{6,7},{8,9},{9,10},{10,11},{12,13},{... | collective-permute-start | bytes 3932168 | tf_op jit(solution)/shard_map/ppermute | solution.py:172
  185.5 31.4 %collective-permute-start.13 = (bf16[512,1280]{1,0:T(8,128)(2,1)}, bf16[512,1280]{1,0:T(8,128)(2,1)S(1)}, u32[]{:S(2)}, u32[]{:S(2)}) collective-permute-start(bf16[512,1280]{1,0:T(8,128)(2,1)} %collective-permute-done.12), channel_id=1, source_target_pairs={{1,0},{2,1},{3,2},{5,4},{6,5},{7,6},{9,8},{10,9},{11,10},{13,12},{... | collective-permute-start | bytes 3932168 | tf_op jit(solution)/shard_map/ppermute | solution.py:173
  188.6 35.7 %collective-permute-start.15 = (bf16[512,1280]{1,0:T(8,128)(2,1)S(1)}, bf16[512,1280]{1,0:T(8,128)(2,1)S(1)}, u32[]{:S(2)}, u32[]{:S(2)}) collective-permute-start(bf16[512,1280]{1,0:T(8,128)(2,1)S(1)} %broadcast_select_fusion), channel_id=1, source_target_pairs={{0,8},{16,24},{1,9},{17,25},{2,10},{18,26},{3,11},{19,27}} | collective-permute-start | bytes 3932168 | tf_op jit(solution)/shard_map/ppermute | solution.py:159
  191.3 61.1 %collective-permute-start.17 = (bf16[512,1280]{1,0:T(8,128)(2,1)S(1)}, bf16[512,1280]{1,0:T(8,128)(2,1)}, u32[]{:S(2)}, u32[]{:S(2)}) collective-permute-start(bf16[512,1280]{1,0:T(8,128)(2,1)S(1)} %get-tuple-element.11.refs_1_.refs_6_), channel_id=1, source_target_pairs={{4,8},{8,12},{12,16},{16,20},{20,24},{24,28},{5,9},{9,13},{13,17},... | collective-permute-start | bytes 3932168 | tf_op jit(solution)/shard_map/ppermute | solution.py:208
  219.4 8.5 %copy-start.1 = (bf16[512,1280]{1,0:T(8,128)(2,1)S(1)}, bf16[512,1280]{1,0:T(8,128)(2,1)}, u32[]{:S(2)}) copy-start(bf16[512,1280]{1,0:T(8,128)(2,1)} %copy-done) | copy-start | bytes 3932164
  225.5 25.4 %collective-permute-start.16 = (bf16[512,1280]{1,0:T(8,128)(2,1)}, bf16[512,1280]{1,0:T(8,128)(2,1)}, u32[]{:S(2)}, u32[]{:S(2)}) collective-permute-start(bf16[512,1280]{1,0:T(8,128)(2,1)} %broadcast_select_fusion.1), channel_id=1, source_target_pairs={{0,4},{8,12},{16,20},{24,28},{1,5},{9,13},{17,21},{25,29},{2,6},{1... | collective-permute-start | bytes 3932168 | tf_op jit(solution)/shard_map/ppermute | solution.py:159
  249.2 3.3 %collective-permute-start.18 = (bf16[512,1280]{1,0:T(8,128)(2,1)S(1)}, bf16[512,1280]{1,0:T(8,128)(2,1)}, u32[]{:S(2)}, u32[]{:S(2)}) collective-permute-start(bf16[512,1280]{1,0:T(8,128)(2,1)S(1)} %get-tuple-element.12.refs_2_.refs_7_), channel_id=1, source_target_pairs={{0,4},{1,5},{2,6},{3,7}} | collective-permute-start | bytes 3932168 | tf_op jit(solution)/shard_map/ppermute | solution.py:210
  (5 other events, 17.6 us)

commit v2 on v1

v2 whole, which is shorter than its diff:
```python
import functools

import jax
import jax.numpy as jnp
from jax import lax
from jax.experimental import pallas as pl
from jax.experimental.pallas import tpu as pltpu
from jax.sharding import PartitionSpec as P

DH = 128
BF16 = jnp.bfloat16
F32 = jnp.float32
ANY = pl.BlockSpec(memory_space=pl.ANY)


def normalized(part, gain):
    square = part * part
    high = square.astype(BF16)
    low = (square - high.astype(F32)).astype(BF16)
    ones = jnp.ones((2 * DH, DH), BF16)
    total = jnp.dot(jnp.concatenate([high, low], axis=1), ones, preferred_element_type=F32)
    return (part * lax.rsqrt(total * (1.0 / DH) + 1e-06) * gain).astype(BF16)


def store_heads(acc, qg, kg, q_out, kv_out):
    heads = q_out.shape[0]

    def columns(group, h):
        return acc[:, (group * heads + h) * DH : (group * heads + h + 1) * DH]

    for h in range(heads):
        span = slice(h * DH, (h + 1) * DH)
        q_out[h] = normalized(columns(0, h), qg[:, span])
        kv_out[0, h] = normalized(columns(1, h), kg[:, span])
        kv_out[1, h] = columns(2, h).astype(BF16)


def project_body(pairs, has_acc, final, info, *refs):
    refs = list(refs)
    count = len(pairs)
    groups = [[refs.pop(0) for _ in range(n)] for n in pairs]
    weights = [refs.pop(0) for _ in range(3)]
    gains = [refs.pop(0) for _ in range(2)] if final else None
    start = refs.pop(0) if has_acc else None
    outs = [refs.pop(0) for _ in range(2)] if final else None
    acc, xbuf, sem = refs
    step = pl.program_id(0)

    @pl.when(step == 0)
    def _():
        for i, group in enumerate(groups):
            for j, source in enumerate(group):

                @pl.when((info[0] == j) | (len(group) == 1))
                def _(i=i, source=source):
                    pltpu.make_async_copy(source, xbuf.at[i], sem.at[i]).start()

    for i in range(count):

        @pl.when(step == i)
        def _(i=i):
            pltpu.make_async_copy(groups[i][0], xbuf.at[i], sem.at[i]).wait()
            weight = jnp.concatenate([w[...] for w in weights], axis=1)
            part = jnp.dot(xbuf[i], weight, preferred_element_type=F32)
            if i == 0:
                acc[...] = part + start[...] if has_acc else part
            else:
                acc[...] += part

    if final:

        @pl.when(step == count - 1)
        def _():
            store_heads(acc, gains[0][...], gains[1][...], *outs)


def project(sources, info, weights, gains=None, acc=None):
    pairs = [len(s) for s in sources]
    count = len(pairs)
    rows, chans = sources[0][0].shape
    width = weights[0].shape[1]
    heads = width // DH
    final = gains is not None
    a_spec = pl.BlockSpec((rows, 3 * width), lambda k, info: (0, 0))
    in_specs = [ANY] * sum(pairs) + [pl.BlockSpec((chans, width), lambda k, info: (info[1 + k], 0))] * 3
    args = [x for s in sources for x in s] + list(weights)
    scratch = [pltpu.VMEM((count, rows, chans), BF16), pltpu.SemaphoreType.DMA((count,))]
    raw = jax.ShapeDtypeStruct((rows, 3 * width), F32)
    if final:
        in_specs += [pl.BlockSpec((1, width), lambda k, info: (0, 0))] * 2
        args += [g[None] for g in gains]
        out_shape = [
            jax.ShapeDtypeStruct((heads, rows, DH), BF16),
            jax.ShapeDtypeStruct((2, heads, rows, DH), BF16),
        ]
        out_specs = [
            pl.BlockSpec((heads, rows, DH), lambda k, info: (0, 0, 0)),
            pl.BlockSpec((2, heads, rows, DH), lambda k, info: (0, 0, 0, 0)),
        ]
        scratch = [pltpu.VMEM(raw.shape, F32)] + scratch
    else:
        out_shape, out_specs = raw, a_spec
    if acc is not None:
        in_specs.append(a_spec)
        args.append(acc)
    return pl.pallas_call(
        functools.partial(project_body, pairs, acc is not None, final),
        grid_spec=pltpu.PrefetchScalarGridSpec(
            num_scalar_prefetch=1,
            grid=(count,),
            in_specs=in_specs,
            out_specs=out_specs,
            scratch_shapes=scratch,
        ),
        out_shape=out_shape,
        compiler_params=pltpu.CompilerParams(vmem_limit_bytes=48 * 2**20),
        cost_estimate=pl.CostEstimate(
            flops=2 * rows * count * chans * 3 * width,
            bytes_accessed=2 * count * chans * (rows + 3 * width) + 12 * rows * width,
            transcendentals=0,
        ),
        name="project" + ("_end" if final else "_raw"),
    )(info, *args)


def attend_body(row_block, pos_ref, q1, q2, anchor, own1, own2, shift1, shift2, out):
    pos = pos_ref[0]
    slot = pl.program_id(1)

    def pick(i):
        first = jnp.where(pos == 0, own1[i, 0], own2[i, 0])
        second = jnp.where(pos == 0, own1[i, 0], jnp.where(pos == 1, shift2[i, 0], shift1[i, 0]))
        return jnp.concatenate([anchor[i, 0], jnp.where(slot == 0, first, second)], axis=0)

    factor = 1.4426950408889634 / DH**0.5
    key, value = pick(0), pick(1)
    value = jnp.concatenate([value, jnp.ones_like(value)], axis=1)
    rows = q1.shape[1]
    for r in range(rows // row_block):
        span = pl.ds(r * row_block, row_block)
        query = jnp.where(slot == 0, q1[0, span, :], q2[0, span, :])
        scores = lax.dot_general(query, key, (((1,), (1,)), ((), ())), preferred_element_type=F32)
        tops = [scores[:, c : c + DH] for c in range(0, scores.shape[1], DH)]
        top = jnp.max(functools.reduce(jnp.maximum, tops), axis=-1, keepdims=True)
        expo = jnp.exp2((scores - top) * factor).astype(BF16)
        result = jnp.dot(expo, value, preferred_element_type=F32)
        out[0, span, :] = (result[:, :DH] / result[:, DH:]).astype(BF16)


def attend(pos, q1, q2, anchor, own1, own2, shift1, shift2):
    heads, rows, _ = q1.shape
    q_spec = pl.BlockSpec((1, rows, DH), lambda h, f, pos: (h, 0, 0))
    kv_spec = pl.BlockSpec((2, 1, rows, DH), lambda h, f, pos: (0, h, 0, 0))
    return pl.pallas_call(
        functools.partial(attend_body, 128),
        grid_spec=pltpu.PrefetchScalarGridSpec(
            num_scalar_prefetch=1,
            grid=(heads, 2),
            in_specs=[q_spec] * 2 + [kv_spec] * 5,
            out_specs=pl.BlockSpec(
                (1, rows, DH), lambda h, f, pos: (jnp.where(pos[0] == 0, f, 1 - f), 0, h)
            ),
        ),
        out_shape=jax.ShapeDtypeStruct((2, rows, heads * DH), BF16),
        compiler_params=pltpu.CompilerParams(vmem_limit_bytes=32 * 2**20),
        cost_estimate=pl.CostEstimate(
            flops=16 * heads * rows * rows * DH,
            bytes_accessed=2 * heads * rows * DH * 14,
            transcendentals=4 * heads * rows * rows,
        ),
        name="attend",
    )(pos[None].astype(jnp.int32), q1, q2, anchor, own1, own2, shift1, shift2)


def broadcast_first(x, axis):
    count = lax.axis_size(axis)
    mine = lax.axis_index(axis)
    step = count // 2
    held = x
    while step:
        pairs = [(i, i + step) for i in range(0, count, 2 * step)]
        got = lax.ppermute(held, axis, pairs)
        held = jnp.where(mine % (2 * step) == step, got, held)
        step //= 2
    return held


SWAP = [(0, 1), (1, 0), (2, 3), (3, 2)]
MIDDLE = [(1, 2), (2, 1)]
OUTWARD = [(1, 0), (2, 3)]


def mix(before, centre, after, taps):
    before, centre, after = (v.astype(F32) for v in (before, centre, after))
    return (centre + taps[0] * before + taps[1] * centre + taps[2] * after).astype(BF16)


def per_device(frames, taps, w_query, w_key, w_value, q_gain, k_gain):
    count = lax.axis_size("tm")
    pos = lax.axis_index("tm")
    z = lax.axis_index("head").astype(jnp.int32)
    outer = (z == 0) | (z == 3)
    near, far = (z + 2) % 4, 3 - z
    info = jnp.stack(
        [outer.astype(jnp.int32), z, z ^ 1, jnp.where(outer, near, far), jnp.where(outer, far, near)]
    )
    first, last = frames[0], frames[1]
    ups = [(i, i + 1) for i in range(count - 1)]
    following = lax.ppermute(first, "tm", [(j, i) for i, j in ups])
    preceding = lax.ppermute(last, "tm", ups)
    start = pos == 0
    mixed1 = mix(
        jnp.where(start, jnp.zeros_like(first), first),
        jnp.where(start, first, last),
        jnp.where(start, last, following),
        taps,
    )
    mixed2 = mix(
        jnp.where(start, first, preceding),
        jnp.where(start, last, first),
        jnp.where(start, following, last),
        taps,
    )
    weights = (w_query, w_key, w_value)
    gains = (q_gain, k_gain)

    def send(x, pairs):
        return lax.ppermute(x, "head", pairs)

    swap1, middle1 = send(mixed1, SWAP), send(mixed1, MIDDLE)
    mixed2, swap1 = lax.optimization_barrier((mixed2, swap1))
    cross1, second1 = send(swap1, MIDDLE), send(middle1, OUTWARD)
    swap2, middle2 = send(mixed2, SWAP), send(mixed2, MIDDLE)
    third1 = send(cross1, OUTWARD)
    cross2, second2 = send(swap2, MIDDLE), send(middle2, OUTWARD)
    third2 = send(cross2, OUTWARD)

    q1, kv1 = project([(mixed1,), (swap1,), (middle1, second1), (cross1, third1)], info, weights, gains)
    anchor = broadcast_first(kv1, "tm")
    shift1 = lax.ppermute(kv1, "tm", [(i, i + 1) for i in range(1, count - 1)])
    raw2 = project([(mixed2,), (swap2,), (middle2, second2)], info, weights)
    info_end = jnp.stack([info[0], info[4]])
    q2, kv2 = project([(cross2, third2)], info_end, weights, gains, raw2)
    shift2 = lax.ppermute(kv2, "tm", [(0, 1)])
    return attend(pos, q1, q2, anchor, kv1, kv2, shift1, shift2)


def solution(mesh):
    placed = (
        P("tm", None, "head"),
        P(None, "head"),
        P(None, "head"),
        P(None, "head"),
        P(None, "head"),
        P("head"),
        P("head"),
    )
    return jax.shard_map(
        per_device, mesh=mesh, in_specs=placed, out_specs=P("tm", None, "head"), check_vma=False
    )
```

time: 271 us -> 267 us (0.985)
  waiting for transfers between devices: 136 us -> 152 us
  starting transfers between devices: 53.9 us -> 42.1 us
  other arithmetic: 16.2 us -> 10.4 us
  Pallas kernels: 55.6 us -> 51 us
    ppermute x12 -> x10, waiting for transfers between devices: 108 us -> 129 us  [send(): return lax.ppermute(x, 'head', pairs)]
    ppermute x12 -> x10, starting transfers between devices: 38.4 us -> 27.1 us  [send(): return lax.ppermute(x, 'head', pairs)]
    select_n x6 -> x0, other arithmetic: 9.54 us -> none  [gather_line(): jnp.where(z + k < count, down[k], up[count - k])]
    ppermute x3, waiting for transfers between devices: 4.94 us -> 0.01 us  [broadcast_first(): got = lax.ppermute(held, axis, pairs)]
    pallas_call x3 -> x4, Pallas kernels: 55.6 us -> 51 us  [the longest x3 38.2 us: project(): pl.pallas_call(functools.partial(project_body, pairs, acc is not None, fi...]
    select_n x3, other arithmetic: 2.86 us -> 6.57 us  [broadcast_first(): held = jnp.where(mine % (2 * step) == step, got, held)]
  transfers between devices with their start and end apart: 19 -> 17, of which waited for: 14 -> 8; matrix products, arithmetic and copies ran while one was open for 5% -> 3% of each run, Pallas kernels for 15% -> 15%
where the time goes in v2:
time: 267 us; the launch traced here: 263 us
  waiting for transfers between devices  152 us (57%)
  Pallas kernels  51 us (19%)
  starting transfers between devices  42.1 us (16%)
  other arithmetic  10.4 us (4%)
  local copies, waits for them, and re-layouts  7.35 us (3%)
    ppermute x10, waiting for transfers between devices, send(): return lax.ppermute(x, 'head', pairs)  129 us
    pallas_call x3, Pallas kernels, project(): pl.pallas_call(functools.partial(project_body, pairs, acc is not None, fi...  38.2 us
    ppermute x10, starting transfers between devices, send(): return lax.ppermute(x, 'head', pairs)  27.1 us
    ppermute x1, waiting for transfers between devices, per_device(): following = lax.ppermute(first, 'tm', [(j, i) for i, j in ups])  23.4 us
    pallas_call x1, Pallas kernels, attend(): pl.pallas_call(functools.partial(attend_body, 128), grid_spec=pltpu.Prefe...  12.8 us
    ppermute x3, starting transfers between devices, broadcast_first(): got = lax.ppermute(held, axis, pairs)  8 us
    select_n x3, other arithmetic, broadcast_first(): held = jnp.where(mine % (2 * step) == step, got, held)  6.57 us
  transfers between devices with their start and end apart: 17, of which 8 were waited for; matrix products, arithmetic and copies ran while one was open for 3% of the time, Pallas kernels for 15%

profile of v2, /device:TPU:10, one launch (start us, length us, event | category | flops | bytes accessed | tf_op | source)
XLA Modules:
  0.0 263.1 jit_solution(15556691388401285409)
XLA Ops:
  0.0 2.9 %slice_bitcast_fusion = (bf16[512,1280]{1,0:T(8,128)(2,1)S(1)}, bf16[512,1280]{1,0:T(8,128)(2,1)}) fusion(bf16[2,512,1280]{2,1,0:T(8,128)(2,1)} %param.7), kind=kLoop, calls=%fused_computation.10 | loop fusion | bytes 5242880 | tf_op jit(solution)/shard_map/squeeze | solution.py:207
  4.9 2.4 collective-permute-start.1
  7.4 23.4 %collective-permute-done = bf16[512,1280]{1,0:T(8,128)(2,1)S(1)} collective-permute-done((bf16[512,1280]{1,0:T(8,128)(2,1)}, bf16[512,1280]{1,0:T(8,128)(2,1)S(1)}, u32[]{:S(2)}, u32[]{:S(2)}) %collective-permute-start) | collective-permute-done | bytes 1310752 | tf_op jit(solution)/shard_map/ppermute | solution.py:209
  31.8 3.7 %fusion.5 = (bf16[512,1280]{1,0:T(8,128)(2,1)S(1)}, bf16[512,1280]{1,0:T(8,128)(2,1)S(1)}) fusion(bf16[512,1280]{1,0:T(8,128)(2,1)} %copy-done.4, bf16[512,1280]{1,0:T(8,128)(2,1)} %collective-permute-done.1, f32[1280]{0:T(1024)S(1)} %get-tuple-element.18, f32[1280]{0:T(1024)S(1)} %get-tuple-element.19, f32[1280]{0:T(1024)S(1)} %get-tuple-element.17, ...), kind=kLoop, calls=%fused_computation.9 | loop fusion | flops 17039360 | bytes 7879681 | tf_op jit(solution)/shard_map/convert_element_type | solution.py:195
  36.1 4.6 %collective-permute-start.3 = (bf16[512,1280]{1,0:T(8,128)(2,1)S(1)}, bf16[512,1280]{1,0:T(8,128)(2,1)}, u32[]{:S(2)}, u32[]{:S(2)}) collective-permute-start(bf16[512,1280]{1,0:T(8,128)(2,1)S(1)} %get-tuple-element.21.refs_0_), channel_id=1, source_target_pairs={{1,2},{2,1},{5,6},{6,5},{9,10},{10,9},{13,14},{14,13},{17,18},{18,... | collective-permute-start | bytes 3932168 | tf_op jit(solution)/shard_map/ppermute | solution.py:228
  40.7 23.2 %collective-permute-done.2.refs_1_ = bf16[512,1280]{1,0:T(8,128)(2,1)S(1)} collective-permute-done((bf16[512,1280]{1,0:T(8,128)(2,1)S(1)}, bf16[512,1280]{1,0:T(8,128)(2,1)S(1)}, u32[]{:S(2)}, u32[]{:S(2)}) %collective-permute-start.2) | collective-permute-done | bytes 1310752 | tf_op jit(solution)/shard_map/ppermute | solution.py:228
  63.9 3.5 %collective-permute-start.5 = (bf16[512,1280]{1,0:T(8,128)(2,1)S(1)}, bf16[512,1280]{1,0:T(8,128)(2,1)}, u32[]{:S(2)}, u32[]{:S(2)}) collective-permute-start(bf16[512,1280]{1,0:T(8,128)(2,1)S(1)} %collective-permute-done.2.refs_1_), channel_id=1, source_target_pairs={{1,2},{2,1},{5,6},{6,5},{9,10},{10,9},{13,14},{14,13},{17,18},{18,... | collective-permute-start | bytes 3932168 | tf_op jit(solution)/shard_map/ppermute | solution.py:228
  70.8 26.1 %collective-permute-done.5.refs_4_ = bf16[512,1280]{1,0:T(8,128)(2,1)} collective-permute-done((bf16[512,1280]{1,0:T(8,128)(2,1)S(1)}, bf16[512,1280]{1,0:T(8,128)(2,1)}, u32[]{:S(2)}, u32[]{:S(2)}) %collective-permute-start.5) | collective-permute-done | bytes 1310752 | tf_op jit(solution)/shard_map/ppermute | solution.py:228
  96.9 2.4 collective-permute-start.6
  99.4 27.6 %collective-permute-done.6.refs_5_ = bf16[512,1280]{1,0:T(8,128)(2,1)} collective-permute-done((bf16[512,1280]{1,0:T(8,128)(2,1)}, bf16[512,1280]{1,0:T(8,128)(2,1)}, u32[]{:S(2)}, u32[]{:S(2)}) %collective-permute-start.6) | collective-permute-done | bytes 1310752 | tf_op jit(solution)/shard_map/ppermute | solution.py:228
  128.3 16.6 %project_end.2 = (bf16[5,512,128]{2,1,0:T(8,128)(2,1)S(1)}, bf16[2,5,512,128]{3,2,1,0:T(8,128)(2,1)}) custom-call(s32[5]{0:T(128)S(1)} %stack.30.info, bf16[512,1280]{1,0:T(8,128)(2,1)S(1)} %get-tuple-element.21.refs_0_, bf16[512,1280]{1,0:T(8,128)(2,1)S(1)} %copy-done.1, bf16[512,1280]{1,0:T(8,128)(2,1)} %collective-permute-done.3.refs_2_, ...), custom_call_target="tpu_custom_call" | custom-call | flops 10066329600 | bytes 28835840 | tf_op jit(solution)/shard_map/project_end/pallas_call | solution.py:106
  147.5 4.5 %collective-permute-start.10 = (bf16[512,1280]{1,0:T(8,128)(2,1)S(1)}, bf16[512,1280]{1,0:T(8,128)(2,1)}, u32[]{:S(2)}, u32[]{:S(2)}) collective-permute-start(bf16[512,1280]{1,0:T(8,128)(2,1)S(1)} %get-tuple-element.13.refs_0_), channel_id=1, source_target_pairs={{1,2},{2,1},{5,6},{6,5},{9,10},{10,9},{13,14},{14,13},{17,18},{18,... | collective-permute-start | bytes 3932168 | tf_op jit(solution)/shard_map/ppermute | solution.py:228
  152.1 2.9 %collective-permute-done.7.refs_1_ = bf16[512,1280]{1,0:T(8,128)(2,1)} collective-permute-done((bf16[512,1280]{1,0:T(8,128)(2,1)S(1)}, bf16[512,1280]{1,0:T(8,128)(2,1)}, u32[]{:S(2)}, u32[]{:S(2)}) %collective-permute-start.7) | collective-permute-done | bytes 1310752 | tf_op jit(solution)/shard_map/ppermute | solution.py:228
  155.0 4.5 %collective-permute-start.8 = (bf16[512,1280]{1,0:T(8,128)(2,1)}, bf16[512,1280]{1,0:T(8,128)(2,1)S(1)}, u32[]{:S(2)}, u32[]{:S(2)}) collective-permute-start(bf16[512,1280]{1,0:T(8,128)(2,1)} %collective-permute-done.7.refs_1_), channel_id=1, source_target_pairs={{1,2},{2,1},{5,6},{6,5},{9,10},{10,9},{13,14},{14,13},{17,18},{18,... | collective-permute-start | bytes 3932168 | tf_op jit(solution)/shard_map/ppermute | solution.py:228
  159.5 2.5 broadcast_select_fusion
  163.3 18.3 %collective-permute-done.10.refs_2_ = bf16[512,1280]{1,0:T(8,128)(2,1)} collective-permute-done((bf16[512,1280]{1,0:T(8,128)(2,1)S(1)}, bf16[512,1280]{1,0:T(8,128)(2,1)}, u32[]{:S(2)}, u32[]{:S(2)}) %collective-permute-start.10) | collective-permute-done | bytes 1310752 | tf_op jit(solution)/shard_map/ppermute | solution.py:228
  184.0 25.6 %collective-permute-done.8.refs_0_ = bf16[512,1280]{1,0:T(8,128)(2,1)S(1)} collective-permute-done((bf16[512,1280]{1,0:T(8,128)(2,1)}, bf16[512,1280]{1,0:T(8,128)(2,1)S(1)}, u32[]{:S(2)}, u32[]{:S(2)}) %collective-permute-start.8) | collective-permute-done | bytes 1310752 | tf_op jit(solution)/shard_map/ppermute | solution.py:228
  209.7 2.4 collective-permute-start.9
  214.1 2.5 broadcast_select_fusion.1
  216.6 5.0 %collective-permute-start.14 = (bf16[2,5,512,128]{3,2,1,0:T(8,128)(2,1)}, bf16[2,5,512,128]{3,2,1,0:T(8,128)(2,1)}, u32[]{:S(2)}, u32[]{:S(2)}) collective-permute-start(bf16[2,5,512,128]{3,2,1,0:T(8,128)(2,1)} %broadcast_select_fusion.1), channel_id=1, source_target_pairs={{0,4},{8,12},{16,20},{24,28},{1,5},{9,13},{17,21},{25,29},{2,6},{1... | collective-permute-start | bytes 3932168 | tf_op jit(solution)/shard_map/ppermute | solution.py:182
  221.6 13.7 %project_raw.1.refs_7_ = f32[512,1920]{1,0:T(8,128)} custom-call(s32[5]{0:T(128)S(1)} %stack.30.info, bf16[512,1280]{1,0:T(8,128)(2,1)S(1)} %get-tuple-element.13.refs_0_, bf16[512,1280]{1,0:T(8,128)(2,1)} %collective-permute-done.7.refs_1_, bf16[512,1280]{1,0:T(8,128)(2,1)} %collective-permute-done.10.refs_2_, ...), custom_call_target="tpu_custom_call" | custom-call | flops 7549747200 | bytes 22609920 | tf_op jit(solution)/shard_map/project_raw/pallas_call | solution.py:106
  235.3 4.7 %collective-permute-done.9.refs_1_ = bf16[512,1280]{1,0:T(8,128)(2,1)} collective-permute-done((bf16[512,1280]{1,0:T(8,128)(2,1)S(1)}, bf16[512,1280]{1,0:T(8,128)(2,1)}, u32[]{:S(2)}, u32[]{:S(2)}) %collective-permute-start.9) | collective-permute-done | bytes 1310752 | tf_op jit(solution)/shard_map/ppermute | solution.py:228
  240.1 7.8 %project_end.3 = (bf16[5,512,128]{2,1,0:T(8,128)(2,1)S(1)}, bf16[2,5,512,128]{3,2,1,0:T(8,128)(2,1)S(1)}) custom-call(s32[2]{0:T(128)S(1)} %pad_add_fusion.info, bf16[512,1280]{1,0:T(8,128)(2,1)S(1)} %collective-permute-done.8.refs_0_, bf16[512,1280]{1,0:T(8,128)(2,1)} %collective-permute-done.9.refs_1_, bf16[5120,640]{1,0:T(8,128)(2,1)} %refs_2_.1, ...), custom_call_target="tpu_custom_call" | custom-call | flops 2516582400 | bytes 10158080 | tf_op jit(solution)/shard_map/project_end/pallas_call | solution.py:106
  250.2 12.8 %attend.1 = bf16[2,512,640]{2,1,0:T(8,128)(2,1)} custom-call(s32[1]{0:T(128)} %bitcast.pos_ref, bf16[5,512,128]{2,1,0:T(8,128)(2,1)S(1)} %copy-done.3, bf16[5,512,128]{2,1,0:T(8,128)(2,1)S(1)} %get-tuple-element.14.q2, bf16[2,5,512,128]{3,2,1,0:T(8,128)(2,1)S(1)} %broadcast_select_fusion.2.anchor, bf16[2,5,512,128]{3,2,1,0:T(8,128)(2,1)} %get-tuple-element.15.own1, ...), custom_call_target="tpu_custom_call" | custom-call | flops 2684354560 | bytes 9175040 | tf_op jit(solution)/shard_map/attend/pallas_call | solution.py:154
  (40 shorter events, 18.9 us)
Async XLA Ops:
  0.0 7.3 %copy-start.5 = (f32[3,1280]{1,0:T(4,128)S(1)}, f32[3,1280]{1,0:T(4,128)}, u32[]{:S(2)}) copy-start(f32[3,1280]{1,0:T(4,128)} %param.8) | copy-start | bytes 46084
  3.0 27.8 %collective-permute-start = (bf16[512,1280]{1,0:T(8,128)(2,1)}, bf16[512,1280]{1,0:T(8,128)(2,1)S(1)}, u32[]{:S(2)}, u32[]{:S(2)}) collective-permute-start(bf16[512,1280]{1,0:T(8,128)(2,1)} %get-tuple-element.23), channel_id=1, source_target_pairs={{4,0},{8,4},{12,8},{16,12},{20,16},{24,20},{28,24},{5,1},{9,5},{13... | collective-permute-start | bytes 3932168 | tf_op jit(solution)/shard_map/ppermute | solution.py:209
  4.9 25.9 %collective-permute-start.1 = (bf16[512,1280]{1,0:T(8,128)(2,1)S(1)}, bf16[512,1280]{1,0:T(8,128)(2,1)}, u32[]{:S(2)}, u32[]{:S(2)}) collective-permute-start(bf16[512,1280]{1,0:T(8,128)(2,1)S(1)} %get-tuple-element.22), channel_id=1, source_target_pairs={{0,4},{4,8},{8,12},{12,16},{16,20},{20,24},{24,28},{1,5},{5,9},{9,... | collective-permute-start | bytes 3932168 | tf_op jit(solution)/shard_map/ppermute | solution.py:210
  30.8 1.1 copy-start.4
  31.8 67.4 %copy-start.6 = (f32[640]{0:T(1024)S(1)}, f32[640]{0:T(1024)}, u32[]{:S(2)}) copy-start(f32[640]{0:T(1024)} %param.12) | copy-start | bytes 7684
  31.8 67.4 %copy-start.7 = (f32[640]{0:T(1024)S(1)}, f32[640]{0:T(1024)}, u32[]{:S(2)}) copy-start(f32[640]{0:T(1024)} %param.13) | copy-start | bytes 7684
  35.6 28.4 %collective-permute-start.2 = (bf16[512,1280]{1,0:T(8,128)(2,1)S(1)}, bf16[512,1280]{1,0:T(8,128)(2,1)S(1)}, u32[]{:S(2)}, u32[]{:S(2)}) collective-permute-start(bf16[512,1280]{1,0:T(8,128)(2,1)S(1)} %get-tuple-element.21.refs_0_), channel_id=1, source_target_pairs={{0,1},{1,0},{2,3},{3,2},{4,5},{5,4},{6,7},{7,6},{8,9},{9,8},{10,11... | collective-permute-start | bytes 3932168 | tf_op jit(solution)/shard_map/ppermute | solution.py:228
  36.1 32.4 %collective-permute-start.3 = (bf16[512,1280]{1,0:T(8,128)(2,1)S(1)}, bf16[512,1280]{1,0:T(8,128)(2,1)}, u32[]{:S(2)}, u32[]{:S(2)}) collective-permute-start(bf16[512,1280]{1,0:T(8,128)(2,1)S(1)} %get-tuple-element.21.refs_0_), channel_id=1, source_target_pairs={{1,2},{2,1},{5,6},{6,5},{9,10},{10,9},{13,14},{14,13},{17,18},{18,... | collective-permute-start | bytes 3932168 | tf_op jit(solution)/shard_map/ppermute | solution.py:228
  63.9 33.0 %collective-permute-start.5 = (bf16[512,1280]{1,0:T(8,128)(2,1)S(1)}, bf16[512,1280]{1,0:T(8,128)(2,1)}, u32[]{:S(2)}, u32[]{:S(2)}) collective-permute-start(bf16[512,1280]{1,0:T(8,128)(2,1)S(1)} %collective-permute-done.2.refs_1_), channel_id=1, source_target_pairs={{1,2},{2,1},{5,6},{6,5},{9,10},{10,9},{13,14},{14,13},{17,18},{18,... | collective-permute-start | bytes 3932168 | tf_op jit(solution)/shard_map/ppermute | solution.py:228
  67.4 1.1 copy-start
  68.5 30.9 %collective-permute-start.4 = (bf16[512,1280]{1,0:T(8,128)(2,1)}, bf16[512,1280]{1,0:T(8,128)(2,1)}, u32[]{:S(2)}, u32[]{:S(2)}) collective-permute-start(bf16[512,1280]{1,0:T(8,128)(2,1)} %collective-permute-done.3.refs_2_), channel_id=1, source_target_pairs={{1,0},{2,3},{5,4},{6,7},{9,8},{10,11},{13,12},{14,15},{17,16},{18,... | collective-permute-start | bytes 3932168 | tf_op jit(solution)/shard_map/ppermute | solution.py:228
  96.9 30.1 %collective-permute-start.6 = (bf16[512,1280]{1,0:T(8,128)(2,1)}, bf16[512,1280]{1,0:T(8,128)(2,1)}, u32[]{:S(2)}, u32[]{:S(2)}) collective-permute-start(bf16[512,1280]{1,0:T(8,128)(2,1)} %collective-permute-done.5.refs_4_), channel_id=1, source_target_pairs={{1,0},{2,3},{5,4},{6,7},{9,8},{10,11},{13,12},{14,15},{17,16},{18,... | collective-permute-start | bytes 3932168 | tf_op jit(solution)/shard_map/ppermute | solution.py:228
  99.4 55.6 %collective-permute-start.7 = (bf16[512,1280]{1,0:T(8,128)(2,1)S(1)}, bf16[512,1280]{1,0:T(8,128)(2,1)}, u32[]{:S(2)}, u32[]{:S(2)}) collective-permute-start(bf16[512,1280]{1,0:T(8,128)(2,1)S(1)} %get-tuple-element.13.refs_0_), channel_id=1, source_target_pairs={{0,1},{1,0},{2,3},{3,2},{4,5},{5,4},{6,7},{7,6},{8,9},{9,8},{10,11... | collective-permute-start | bytes 3932168 | tf_op jit(solution)/shard_map/ppermute | solution.py:228
  127.0 1.3 copy-start.1
  145.8 13.7 %collective-permute-start.12 = (bf16[2,5,512,128]{3,2,1,0:T(8,128)(2,1)}, bf16[2,5,512,128]{3,2,1,0:T(8,128)(2,1)}, u32[]{:S(2)}, u32[]{:S(2)}) collective-permute-start(bf16[2,5,512,128]{3,2,1,0:T(8,128)(2,1)} %get-tuple-element.15.own1), channel_id=1, source_target_pairs={{0,16},{1,17},{2,18},{3,19}} | collective-permute-start | bytes 3932168 | tf_op jit(solution)/shard_map/ppermute | solution.py:182
  147.5 34.1 %collective-permute-start.10 = (bf16[512,1280]{1,0:T(8,128)(2,1)S(1)}, bf16[512,1280]{1,0:T(8,128)(2,1)}, u32[]{:S(2)}, u32[]{:S(2)}) collective-permute-start(bf16[512,1280]{1,0:T(8,128)(2,1)S(1)} %get-tuple-element.13.refs_0_), channel_id=1, source_target_pairs={{1,2},{2,1},{5,6},{6,5},{9,10},{10,9},{13,14},{14,13},{17,18},{18,... | collective-permute-start | bytes 3932168 | tf_op jit(solution)/shard_map/ppermute | solution.py:228
  155.0 54.7 %collective-permute-start.8 = (bf16[512,1280]{1,0:T(8,128)(2,1)}, bf16[512,1280]{1,0:T(8,128)(2,1)S(1)}, u32[]{:S(2)}, u32[]{:S(2)}) collective-permute-start(bf16[512,1280]{1,0:T(8,128)(2,1)} %collective-permute-done.7.refs_1_), channel_id=1, source_target_pairs={{1,2},{2,1},{5,6},{6,5},{9,10},{10,9},{13,14},{14,13},{17,18},{18,... | collective-permute-start | bytes 3932168 | tf_op jit(solution)/shard_map/ppermute | solution.py:228
  162.0 52.1 %collective-permute-start.13 = (bf16[2,5,512,128]{3,2,1,0:T(8,128)(2,1)}, bf16[2,5,512,128]{3,2,1,0:T(8,128)(2,1)}, u32[]{:S(2)}, u32[]{:S(2)}) collective-permute-start(bf16[2,5,512,128]{3,2,1,0:T(8,128)(2,1)} %broadcast_select_fusion), channel_id=1, source_target_pairs={{0,8},{16,24},{1,9},{17,25},{2,10},{18,26},{3,11},{19,27}} | collective-permute-start | bytes 3932168 | tf_op jit(solution)/shard_map/ppermute | solution.py:182
  181.7 40.0 %collective-permute-start.11 = (bf16[512,1280]{1,0:T(8,128)(2,1)}, bf16[512,1280]{1,0:T(8,128)(2,1)}, u32[]{:S(2)}, u32[]{:S(2)}) collective-permute-start(bf16[512,1280]{1,0:T(8,128)(2,1)} %collective-permute-done.10.refs_2_), channel_id=1, source_target_pairs={{1,0},{2,3},{5,4},{6,7},{9,8},{10,11},{13,12},{14,15},{17,16},{18,... | collective-permute-start | bytes 3932168 | tf_op jit(solution)/shard_map/ppermute | solution.py:228
  209.7 30.4 %collective-permute-start.9 = (bf16[512,1280]{1,0:T(8,128)(2,1)S(1)}, bf16[512,1280]{1,0:T(8,128)(2,1)}, u32[]{:S(2)}, u32[]{:S(2)}) collective-permute-start(bf16[512,1280]{1,0:T(8,128)(2,1)S(1)} %collective-permute-done.8.refs_0_), channel_id=1, source_target_pairs={{1,0},{2,3},{5,4},{6,7},{9,8},{10,11},{13,12},{14,15},{17,16},{18,... | collective-permute-start | bytes 3932168 | tf_op jit(solution)/shard_map/ppermute | solution.py:228
  212.1 38.1 %collective-permute-start.15 = (bf16[2,5,512,128]{3,2,1,0:T(8,128)(2,1)}, bf16[2,5,512,128]{3,2,1,0:T(8,128)(2,1)}, u32[]{:S(2)}, u32[]{:S(2)}) collective-permute-start(bf16[2,5,512,128]{3,2,1,0:T(8,128)(2,1)} %get-tuple-element.15.own1), channel_id=1, source_target_pairs={{4,8},{8,12},{12,16},{16,20},{20,24},{24,28},{5,9},{9,13},{13,17},... | collective-permute-start | bytes 3932168 | tf_op jit(solution)/shard_map/ppermute | solution.py:240
  216.6 32.0 %collective-permute-start.14 = (bf16[2,5,512,128]{3,2,1,0:T(8,128)(2,1)}, bf16[2,5,512,128]{3,2,1,0:T(8,128)(2,1)}, u32[]{:S(2)}, u32[]{:S(2)}) collective-permute-start(bf16[2,5,512,128]{3,2,1,0:T(8,128)(2,1)} %broadcast_select_fusion.1), channel_id=1, source_target_pairs={{0,4},{8,12},{16,20},{24,28},{1,5},{9,13},{17,21},{25,29},{2,6},{1... | collective-permute-start | bytes 3932168 | tf_op jit(solution)/shard_map/ppermute | solution.py:182
  247.9 2.3 collective-permute-start.16
  248.6 1.6 copy-start.3
  (1 other events, 0.8 us)

commit v3 on v2

--- a/solution.py
+++ b/solution.py
@@ -35,8 +35,8 @@
         kv_out[1, h] = columns(2, h).astype(BF16)
 
 
-def project_body(pairs, has_acc, final, info, *refs):
-    refs = list(refs)
+def project_body(pairs, extra, has_acc, final, info, *refs):
+    refs = list(refs)[extra:]
     count = len(pairs)
     groups = [[refs.pop(0) for _ in range(n)] for n in pairs]
     weights = [refs.pop(0) for _ in range(3)]
@@ -74,7 +74,7 @@
             store_heads(acc, gains[0][...], gains[1][...], *outs)
 
 
-def project(sources, info, weights, gains=None, acc=None):
+def project(sources, info, weights, gains=None, acc=None, after=(), flops=1):
     pairs = [len(s) for s in sources]
     count = len(pairs)
     rows, chans = sources[0][0].shape
@@ -82,8 +82,8 @@
     heads = width // DH
     final = gains is not None
     a_spec = pl.BlockSpec((rows, 3 * width), lambda k, info: (0, 0))
-    in_specs = [ANY] * sum(pairs) + [pl.BlockSpec((chans, width), lambda k, info: (info[1 + k], 0))] * 3
-    args = [x for s in sources for x in s] + list(weights)
+    in_specs = [ANY] * (len(after) + sum(pairs)) + [pl.BlockSpec((chans, width), lambda k, info: (info[1 + k], 0))] * 3
+    args = list(after) + [x for s in sources for x in s] + list(weights)
     scratch = [pltpu.VMEM((count, rows, chans), BF16), pltpu.SemaphoreType.DMA((count,))]
     raw = jax.ShapeDtypeStruct((rows, 3 * width), F32)
     if final:
@@ -104,7 +104,7 @@
         in_specs.append(a_spec)
         args.append(acc)
     return pl.pallas_call(
-        functools.partial(project_body, pairs, acc is not None, final),
+        functools.partial(project_body, pairs, len(after), acc is not None, final),
         grid_spec=pltpu.PrefetchScalarGridSpec(
             num_scalar_prefetch=1,
             grid=(count,),
@@ -114,32 +114,45 @@
         ),
         out_shape=out_shape,
         compiler_params=pltpu.CompilerParams(vmem_limit_bytes=48 * 2**20),
-        cost_estimate=pl.CostEstimate(
-            flops=2 * rows * count * chans * 3 * width,
-            bytes_accessed=2 * count * chans * (rows + 3 * width) + 12 * rows * width,
-            transcendentals=0,
-        ),
+        cost_estimate=pl.CostEstimate(flops=flops, bytes_accessed=1, transcendentals=0),
         name="project" + ("_end" if final else "_raw"),
     )(info, *args)
 
 
-def attend_body(row_block, pos_ref, q1, q2, anchor, own1, own2, shift1, shift2, out):
-    pos = pos_ref[0]
-    slot = pl.program_id(1)
-
-    def pick(i):
-        first = jnp.where(pos == 0, own1[i, 0], own2[i, 0])
-        second = jnp.where(pos == 0, own1[i, 0], jnp.where(pos == 1, shift2[i, 0], shift1[i, 0]))
-        return jnp.concatenate([anchor[i, 0], jnp.where(slot == 0, first, second)], axis=0)
-
+def attend_body(row_block, choices, fresh, info, *refs):
+    refs = list(refs)
+    query = refs.pop(0)
+    options = [[refs.pop(0) for _ in range(n)] for n in choices]
+    if not fresh:
+        refs.pop(0)
+    out, held, sem = refs
+    h = pl.program_id(0)
+
+    def fetch(part, source, head):
+        return pltpu.make_async_copy(source.at[:, head], held.at[part, :, head], sem.at[part, head])
+
+    @pl.when(h == 0)
+    def _():
+        for head in range(held.shape[2]):
+            for part in range(2):
+                for j, source in enumerate(options[part]):
+
+                    @pl.when(info[2 * part] == j)
+                    def _(part=part, source=source, head=head):
+                        fetch(part, source, head).start()
+
+    for part in range(2):
+        fetch(part, options[part][0], h).wait()
     factor = 1.4426950408889634 / DH**0.5
-    key, value = pick(0), pick(1)
+    key = jnp.concatenate([held[0, 0, h], held[1, 0, h]], axis=0)
+    value = jnp.concatenate([held[0, 1, h], held[1, 1, h]], axis=0)
     value = jnp.concatenate([value, jnp.ones_like(value)], axis=1)
-    rows = q1.shape[1]
+    rows = query.shape[1]
     for r in range(rows // row_block):
         span = pl.ds(r * row_block, row_block)
-        query = jnp.where(slot == 0, q1[0, span, :], q2[0, span, :])
-        scores = lax.dot_general(query, key, (((1,), (1,)), ((), ())), preferred_element_type=F32)
+        scores = lax.dot_general(
+            query[0, span, :], key, (((1,), (1,)), ((), ())), preferred_element_type=F32
+        )
         tops = [scores[:, c : c + DH] for c in range(0, scores.shape[1], DH)]
         top = jnp.max(functools.reduce(jnp.maximum, tops), axis=-1, keepdims=True)
         expo = jnp.exp2((scores - top) * factor).astype(BF16)
@@ -147,45 +160,52 @@
         out[0, span, :] = (result[:, :DH] / result[:, DH:]).astype(BF16)
 
 
-def attend(pos, q1, q2, anchor, own1, own2, shift1, shift2):
-    heads, rows, _ = q1.shape
-    q_spec = pl.BlockSpec((1, rows, DH), lambda h, f, pos: (h, 0, 0))
-    kv_spec = pl.BlockSpec((2, 1, rows, DH), lambda h, f, pos: (0, h, 0, 0))
+def attend(query, anchors, anchor, options, choice, frame, partly=None):
+    heads, rows, _ = query.shape
+    in_specs = [pl.BlockSpec((1, rows, DH), lambda h, info: (h, 0, 0))]
+    in_specs += [ANY] * (len(anchors) + len(options))
+    args = [query, *anchors, *options]
+    aliases = {}
+    if partly is not None:
+        in_specs.append(ANY)
+        aliases = {1 + len(args): 0}
+        args.append(partly)
     return pl.pallas_call(
-        functools.partial(attend_body, 128),
+        functools.partial(attend_body, 128, (len(anchors), len(options)), partly is None),
         grid_spec=pltpu.PrefetchScalarGridSpec(
             num_scalar_prefetch=1,
-            grid=(heads, 2),
-            in_specs=[q_spec] * 2 + [kv_spec] * 5,
-            out_specs=pl.BlockSpec(
-                (1, rows, DH), lambda h, f, pos: (jnp.where(pos[0] == 0, f, 1 - f), 0, h)
-            ),
+            grid=(heads,),
+            in_specs=in_specs,
+            out_specs=pl.BlockSpec((1, rows, DH), lambda h, info: (info[1], 0, h)),
+            scratch_shapes=[
+                pltpu.VMEM((2, 2, heads, rows, DH), BF16),
+                pltpu.SemaphoreType.DMA((2, heads)),
+            ],
         ),
         out_shape=jax.ShapeDtypeStruct((2, rows, heads * DH), BF16),
+        input_output_aliases=aliases,
         compiler_params=pltpu.CompilerParams(vmem_limit_bytes=32 * 2**20),
         cost_estimate=pl.CostEstimate(
-            flops=16 * heads * rows * rows * DH,
-            bytes_accessed=2 * heads * rows * DH * 14,
-            transcendentals=4 * heads * rows * rows,
+            flops=8 * heads * rows * rows * DH,
+            bytes_accessed=2 * heads * rows * DH * 6,
+            transcendentals=2 * heads * rows * rows,
         ),
         name="attend",
-    )(pos[None].astype(jnp.int32), q1, q2, anchor, own1, own2, shift1, shift2)
+    )(jnp.stack([anchor, frame, choice]).astype(jnp.int32), *args)
 
 
 def broadcast_first(x, axis):
     count = lax.axis_size(axis)
     mine = lax.axis_index(axis)
-    step = count // 2
     held = x
-    while step:
-        pairs = [(i, i + step) for i in range(0, count, 2 * step)]
-        got = lax.ppermute(held, axis, pairs)
-        held = jnp.where(mine % (2 * step) == step, got, held)
-        step //= 2
-    return held
+    for to in range(2, count, 2):
+        held = jnp.where(mine == to, lax.ppermute(x, axis, [(0, to)]), held)
+    other = lax.ppermute(held, axis, [(i, i + 1) for i in range(0, count, 2)])
+    return held, other
 
 
 SWAP = [(0, 1), (1, 0), (2, 3), (3, 2)]
+INWARD = [(0, 1), (3, 2)]
 MIDDLE = [(1, 2), (2, 1)]
 OUTWARD = [(1, 0), (2, 3)]
 
@@ -206,15 +226,16 @@
     )
     first, last = frames[0], frames[1]
     ups = [(i, i + 1) for i in range(count - 1)]
+    start = pos == 0
     following = lax.ppermute(first, "tm", [(j, i) for i, j in ups])
-    preceding = lax.ppermute(last, "tm", ups)
-    start = pos == 0
     mixed1 = mix(
         jnp.where(start, jnp.zeros_like(first), first),
         jnp.where(start, first, last),
         jnp.where(start, last, following),
         taps,
     )
+    _, held_last = lax.optimization_barrier((mixed1, last))
+    preceding = lax.ppermute(held_last, "tm", ups)
     mixed2 = mix(
         jnp.where(start, first, preceding),
         jnp.where(start, last, first),
@@ -228,21 +249,28 @@
         return lax.ppermute(x, "head", pairs)
 
     swap1, middle1 = send(mixed1, SWAP), send(mixed1, MIDDLE)
-    mixed2, swap1 = lax.optimization_barrier((mixed2, swap1))
+    swap1, middle1 = lax.optimization_barrier((swap1, middle1))
     cross1, second1 = send(swap1, MIDDLE), send(middle1, OUTWARD)
-    swap2, middle2 = send(mixed2, SWAP), send(mixed2, MIDDLE)
-    third1 = send(cross1, OUTWARD)
-    cross2, second2 = send(swap2, MIDDLE), send(middle2, OUTWARD)
-    third2 = send(cross2, OUTWARD)
-
-    q1, kv1 = project([(mixed1,), (swap1,), (middle1, second1), (cross1, third1)], info, weights, gains)
+    mixed2, cross1, second1 = lax.optimization_barrier((mixed2, cross1, second1))
+    third1, inward2, middle2 = send(cross1, OUTWARD), send(mixed2, INWARD), send(mixed2, MIDDLE)
+    later2, inward2 = lax.optimization_barrier((mixed2, inward2))
+    cross2, first2 = send(inward2, MIDDLE), send(later2, OUTWARD)
+    second2, third2 = send(middle2, OUTWARD), send(cross2, OUTWARD)
+
+    sources1 = [(mixed1,), (swap1,), (middle1, second1), (cross1, third1)]
+    q1, kv1 = project(sources1, info, weights, gains, after=(inward2, middle2))
+    kv1, first2 = lax.optimization_barrier((kv1, first2))
     anchor = broadcast_first(kv1, "tm")
     shift1 = lax.ppermute(kv1, "tm", [(i, i + 1) for i in range(1, count - 1)])
-    raw2 = project([(mixed2,), (swap2,), (middle2, second2)], info, weights)
+    raw2 = project([(mixed2,), (inward2, first2), (middle2, second2)], info, weights)
     info_end = jnp.stack([info[0], info[4]])
     q2, kv2 = project([(cross2, third2)], info_end, weights, gains, raw2)
     shift2 = lax.ppermute(kv2, "tm", [(0, 1)])
-    return attend(pos, q1, q2, anchor, kv1, kv2, shift1, shift2)
+    late = jnp.where(start, 0, 1)
+    odd = pos % 2
+    result = attend(q1, anchor, odd, [kv1, kv2], late, late)
+    choice = jnp.minimum(pos, 1) + (pos == 1)
+    return attend(q2, anchor, odd, [kv1, shift1, shift2], choice, 1 - late, result)
 
 
 def solution(mesh):

time: 267 us -> 251 us (0.940)
  waiting for transfers between devices: 152 us -> 129 us
  starting transfers between devices: 42.1 us -> 50.1 us
  Pallas kernels: 51 us -> 56.3 us
  other arithmetic: 10.4 us -> 6.4 us
    ppermute x10 -> x11, waiting for transfers between devices: 129 us -> 102 us  [send(): return lax.ppermute(x, 'head', pairs)]
    ppermute x4 -> x5, waiting for transfers between devices: 0.01 us -> 10.7 us  [the longest x3 10.7 us: broadcast_first(): held = jnp.where(mine == to, lax.ppermute(x, axis, [(0, to)]), held)]
    ppermute x1, waiting for transfers between devices: 23.4 us -> 15.4 us  [per_device(): following = lax.ppermute(first, 'tm', [(j, i) for i, j in ups])]
    ppermute x10 -> x11, starting transfers between devices: 27.1 us -> 33 us  [send(): return lax.ppermute(x, 'head', pairs)]
    pallas_call x4 -> x5, Pallas kernels: 51 us -> 56.3 us  [the longest x3 41.3 us: project(): pl.pallas_call(functools.partial(project_body, pairs, len(after), acc is...]
    select_n x3 -> x1, other arithmetic: 6.57 us -> 1.55 us  [broadcast_first(): held = jnp.where(mine == to, lax.ppermute(x, axis, [(0, to)]), held)]
    ppermute x4 -> x5, starting transfers between devices: 10.4 us -> 11.3 us  [the longest x3 4.74 us: broadcast_first(): held = jnp.where(mine == to, lax.ppermute(x, axis, [(0, to)]), held)]
  transfers between devices with their start and end apart: 17 -> 19, of which waited for: 8 -> 10; matrix products, arithmetic and copies ran while one was open for 3% -> 2% of each run, Pallas kernels for 15% -> 20%
where the time goes in v3:
time: 251 us; the launch traced here: 249 us
  waiting for transfers between devices  129 us (51%)
  Pallas kernels  56.3 us (22%)
  starting transfers between devices  50.1 us (20%)
  local copies, waits for them, and re-layouts  6.92 us (3%)
  other arithmetic  6.4 us (3%)
    ppermute x11, waiting for transfers between devices, send(): return lax.ppermute(x, 'head', pairs)  102 us
    pallas_call x3, Pallas kernels, project(): pl.pallas_call(functools.partial(project_body, pairs, len(after), acc is...  41.3 us
    ppermute x11, starting transfers between devices, send(): return lax.ppermute(x, 'head', pairs)  33 us
    ppermute x1, waiting for transfers between devices, per_device(): following = lax.ppermute(first, 'tm', [(j, i) for i, j in ups])  15.4 us
    pallas_call x2, Pallas kernels, attend(): pl.pallas_call(functools.partial(attend_body, 128, (len(anchors), len(opt...  15 us
    ppermute x3, waiting for transfers between devices, broadcast_first(): held = jnp.where(mine == to, lax.ppermute(x, axis, [(0, to)]), held)  10.7 us
  transfers between devices with their start and end apart: 19, of which 10 were waited for; matrix products, arithmetic and copies ran while one was open for 2% of the time, Pallas kernels for 20%

profile of v3, /device:TPU:10, one launch (start us, length us, event | category | flops | bytes accessed | tf_op | source)
XLA Modules:
  0.0 248.8 jit_solution(935664315364034433)
XLA Ops:
  0.0 3.5 %slice_bitcast_fusion.1 = (bf16[512,1280]{1,0:T(8,128)(2,1)}, bf16[512,1280]{1,0:T(8,128)(2,1)}) fusion(bf16[2,512,1280]{2,1,0:T(8,128)(2,1)} %param.7), kind=kLoop, calls=%fused_computation.12 | loop fusion | bytes 5242880 | tf_op jit(solution)/shard_map/squeeze | solution.py:227
  5.5 15.4 %collective-permute-done = bf16[512,1280]{1,0:T(8,128)(2,1)} collective-permute-done((bf16[512,1280]{1,0:T(8,128)(2,1)}, bf16[512,1280]{1,0:T(8,128)(2,1)}, u32[]{:S(2)}, u32[]{:S(2)}) %collective-permute-start) | collective-permute-done | bytes 1310752 | tf_op jit(solution)/shard_map/ppermute | solution.py:230
  20.9 2.5 fusion.5.refs_2_
  23.9 4.6 %collective-permute-start.3 = (bf16[512,1280]{1,0:T(8,128)(2,1)S(1)}, bf16[512,1280]{1,0:T(8,128)(2,1)S(1)}, u32[]{:S(2)}, u32[]{:S(2)}) collective-permute-start(bf16[512,1280]{1,0:T(8,128)(2,1)S(1)} %fusion.5.refs_2_), channel_id=1, source_target_pairs={{1,2},{2,1},{5,6},{6,5},{9,10},{10,9},{13,14},{14,13},{17,18},{18,... | collective-permute-start | bytes 3932168 | tf_op jit(solution)/shard_map/ppermute | solution.py:249
  29.6 4.1 %collective-permute-start.1 = (bf16[512,1280]{1,0:T(8,128)(2,1)S(1)}, bf16[512,1280]{1,0:T(8,128)(2,1)S(1)}, u32[]{:S(2)}, u32[]{:S(2)}) collective-permute-start(bf16[512,1280]{1,0:T(8,128)(2,1)S(1)} %copy-done.10), channel_id=1, source_target_pairs={{0,4},{4,8},{8,12},{12,16},{16,20},{20,24},{24,28},{1,5},{5,9},{9,... | collective-permute-start | bytes 3932168 | tf_op jit(solution)/shard_map/ppermute | solution.py:238
  33.7 19.7 %collective-permute-done.2.refs_3_ = bf16[512,1280]{1,0:T(8,128)(2,1)S(1)} collective-permute-done((bf16[512,1280]{1,0:T(8,128)(2,1)S(1)}, bf16[512,1280]{1,0:T(8,128)(2,1)S(1)}, u32[]{:S(2)}, u32[]{:S(2)}) %collective-permute-start.2) | collective-permute-done | bytes 1310752 | tf_op jit(solution)/shard_map/ppermute | solution.py:249
  53.4 3.0 %collective-permute-done.3.refs_4_ = bf16[512,1280]{1,0:T(8,128)(2,1)S(1)} collective-permute-done((bf16[512,1280]{1,0:T(8,128)(2,1)S(1)}, bf16[512,1280]{1,0:T(8,128)(2,1)S(1)}, u32[]{:S(2)}, u32[]{:S(2)}) %collective-permute-start.3) | collective-permute-done | bytes 1310752 | tf_op jit(solution)/shard_map/ppermute | solution.py:249
  56.4 4.2 %collective-permute-start.4 = (bf16[512,1280]{1,0:T(8,128)(2,1)S(1)}, bf16[512,1280]{1,0:T(8,128)(2,1)}, u32[]{:S(2)}, u32[]{:S(2)}) collective-permute-start(bf16[512,1280]{1,0:T(8,128)(2,1)S(1)} %collective-permute-done.2.refs_3_), channel_id=1, source_target_pairs={{1,2},{2,1},{5,6},{6,5},{9,10},{10,9},{13,14},{14,13},{17,18},{18,... | collective-permute-start | bytes 3932168 | tf_op jit(solution)/shard_map/ppermute | solution.py:249
  64.2 25.6 %collective-permute-done.4.refs_6_ = bf16[512,1280]{1,0:T(8,128)(2,1)} collective-permute-done((bf16[512,1280]{1,0:T(8,128)(2,1)S(1)}, bf16[512,1280]{1,0:T(8,128)(2,1)}, u32[]{:S(2)}, u32[]{:S(2)}) %collective-permute-start.4) | collective-permute-done | bytes 1310752 | tf_op jit(solution)/shard_map/ppermute | solution.py:249
  92.1 3.2 %collective-permute-start.9 = (bf16[512,1280]{1,0:T(8,128)(2,1)}, bf16[512,1280]{1,0:T(8,128)(2,1)}, u32[]{:S(2)}, u32[]{:S(2)}) collective-permute-start(bf16[512,1280]{1,0:T(8,128)(2,1)} %fusion.2.refs_0_), channel_id=1, source_target_pairs={{1,2},{2,1},{5,6},{6,5},{9,10},{10,9},{13,14},{14,13},{17,18},{18,... | collective-permute-start | bytes 3932168 | tf_op jit(solution)/shard_map/ppermute | solution.py:249
  95.3 4.3 %collective-permute-start.10 = (bf16[512,1280]{1,0:T(8,128)(2,1)}, bf16[512,1280]{1,0:T(8,128)(2,1)}, u32[]{:S(2)}, u32[]{:S(2)}) collective-permute-start(bf16[512,1280]{1,0:T(8,128)(2,1)} %collective-permute-done.4.refs_6_), channel_id=1, source_target_pairs={{1,0},{2,3},{5,4},{6,7},{9,8},{10,11},{13,12},{14,15},{17,16},{18,... | collective-permute-start | bytes 3932168 | tf_op jit(solution)/shard_map/ppermute | solution.py:249
  99.5 24.4 %collective-permute-done.6.refs_0_.refs_1_ = bf16[512,1280]{1,0:T(8,128)(2,1)S(1)} collective-permute-done((bf16[512,1280]{1,0:T(8,128)(2,1)}, bf16[512,1280]{1,0:T(8,128)(2,1)S(1)}, u32[]{:S(2)}, u32[]{:S(2)}) %collective-permute-start.6) | collective-permute-done | bytes 1310752 | tf_op jit(solution)/shard_map/ppermute | solution.py:249
  124.0 2.6 %collective-permute-start.11 = (bf16[512,1280]{1,0:T(8,128)(2,1)}, bf16[512,1280]{1,0:T(8,128)(2,1)}, u32[]{:S(2)}, u32[]{:S(2)}) collective-permute-start(bf16[512,1280]{1,0:T(8,128)(2,1)} %fusion.2.refs_0_), channel_id=1, source_target_pairs={{1,0},{2,3},{5,4},{6,7},{9,8},{10,11},{13,12},{14,15},{17,16},{18,... | collective-permute-start | bytes 3932168 | tf_op jit(solution)/shard_map/ppermute | solution.py:249
  126.6 3.1 %collective-permute-start.7 = (bf16[512,1280]{1,0:T(8,128)(2,1)S(1)}, bf16[512,1280]{1,0:T(8,128)(2,1)}, u32[]{:S(2)}, u32[]{:S(2)}) collective-permute-start(bf16[512,1280]{1,0:T(8,128)(2,1)S(1)} %collective-permute-done.6.refs_0_.refs_1_), channel_id=1, source_target_pairs={{1,2},{2,1},{5,6},{6,5},{9,10},{10,9},{13,14},{14,13},{17,18},{18,... | collective-permute-start | bytes 3932168 | tf_op jit(solution)/shard_map/ppermute | solution.py:249
  131.1 15.5 %project_end.2 = (bf16[5,512,128]{2,1,0:T(8,128)(2,1)S(1)}, bf16[2,5,512,128]{3,2,1,0:T(8,128)(2,1)S(1)}) custom-call(s32[5]{0:T(128)S(1)} %stack.55.info, bf16[512,1280]{1,0:T(8,128)(2,1)S(1)} %collective-permute-done.6.refs_0_.refs_1_, bf16[512,1280]{1,0:T(8,128)(2,1)} %collective-permute-done.9.refs_1_.refs_3_, bf16[512,1280]{1,0:T(8,128)(2,1)S(1)} %copy-done.3, ...), custom_call_target="tpu_custom_call" | custom-call | flops 1 | bytes 1 | tf_op jit(solution)/shard_map/project_end/pallas_call | solution.py:106
  146.7 8.4 %collective-permute-done.11.refs_2_ = bf16[512,1280]{1,0:T(8,128)(2,1)} collective-permute-done((bf16[512,1280]{1,0:T(8,128)(2,1)}, bf16[512,1280]{1,0:T(8,128)(2,1)}, u32[]{:S(2)}, u32[]{:S(2)}) %collective-permute-start.11) | collective-permute-done | bytes 1310752 | tf_op jit(solution)/shard_map/ppermute | solution.py:249
  159.9 5.5 %collective-permute-start.12 = (bf16[512,1280]{1,0:T(8,128)(2,1)}, bf16[512,1280]{1,0:T(8,128)(2,1)}, u32[]{:S(2)}, u32[]{:S(2)}) collective-permute-start(bf16[512,1280]{1,0:T(8,128)(2,1)} %collective-permute-done.9.refs_1_.refs_3_), channel_id=1, source_target_pairs={{1,0},{2,3},{5,4},{6,7},{9,8},{10,11},{13,12},{14,15},{17,16},{18,... | collective-permute-start | bytes 3932168 | tf_op jit(solution)/shard_map/ppermute | solution.py:249
  167.8 10.7 %collective-permute-done.15 = bf16[2,5,512,128]{3,2,1,0:T(8,128)(2,1)} collective-permute-done((bf16[2,5,512,128]{3,2,1,0:T(8,128)(2,1)S(1)}, bf16[2,5,512,128]{3,2,1,0:T(8,128)(2,1)}, u32[]{:S(2)}, u32[]{:S(2)}) %collective-permute-start.15) | collective-permute-done | bytes 1310752 | tf_op jit(solution)/shard_map/ppermute | solution.py:202
  184.8 9.0 %collective-permute-done.12.refs_4_ = bf16[512,1280]{1,0:T(8,128)(2,1)} collective-permute-done((bf16[512,1280]{1,0:T(8,128)(2,1)}, bf16[512,1280]{1,0:T(8,128)(2,1)}, u32[]{:S(2)}, u32[]{:S(2)}) %collective-permute-start.12) | collective-permute-done | bytes 1310752 | tf_op jit(solution)/shard_map/ppermute | solution.py:249
  193.8 15.6 %project_raw.1.refs_7_ = f32[512,1920]{1,0:T(8,128)} custom-call(s32[5]{0:T(128)S(1)} %stack.55.info, bf16[512,1280]{1,0:T(8,128)(2,1)} %fusion.2.refs_0_, bf16[512,1280]{1,0:T(8,128)(2,1)S(1)} %copy-done.1, bf16[512,1280]{1,0:T(8,128)(2,1)} %collective-permute-done.11.refs_2_, bf16[512,1280]{1,0:T(8,128)(2,1)} %collective-permute-done.9.refs_1_.refs_3_, ...), custom_call_target="tpu_custom_call" | custom-call | flops 1 | bytes 1 | tf_op jit(solution)/shard_map/project_raw/pallas_call | solution.py:106
  209.4 11.3 %collective-permute-done.8.refs_1_ = bf16[512,1280]{1,0:T(8,128)(2,1)} collective-permute-done((bf16[512,1280]{1,0:T(8,128)(2,1)}, bf16[512,1280]{1,0:T(8,128)(2,1)}, u32[]{:S(2)}, u32[]{:S(2)}) %collective-permute-start.8) | collective-permute-done | bytes 1310752 | tf_op jit(solution)/shard_map/ppermute | solution.py:249
  220.7 10.1 %project_end.3 = (bf16[5,512,128]{2,1,0:T(8,128)(2,1)S(1)}, bf16[2,5,512,128]{3,2,1,0:T(8,128)(2,1)}) custom-call(s32[2]{0:T(128)S(1)} %pad_add_fusion.1.info, bf16[512,1280]{1,0:T(8,128)(2,1)} %collective-permute-done.7.refs_0_, bf16[512,1280]{1,0:T(8,128)(2,1)} %collective-permute-done.8.refs_1_, bf16[5120,640]{1,0:T(8,128)(2,1)} %refs_2_.1, ...), custom_call_target="tpu_custom_call" | custom-call | flops 1 | bytes 1 | tf_op jit(solution)/shard_map/project_end/pallas_call | solution.py:106
  233.5 7.5 %attend.2.refs_6_ = bf16[2,512,640]{2,1,0:T(8,128)(2,1)} custom-call(s32[3]{0:T(128)S(1)} %get-tuple-element.39.info, bf16[5,512,128]{2,1,0:T(8,128)(2,1)S(1)} %get-tuple-element.32.refs_0_, bf16[2,5,512,128]{3,2,1,0:T(8,128)(2,1)S(1)} %select_select_fusion.refs_1_, bf16[2,5,512,128]{3,2,1,0:T(8,128)(2,1)} %collective-permute-done.16.refs_2_, ...), custom_call_target="tpu_custom_call" | custom-call | flops 1342177280 | bytes 3932160 | tf_op jit(solution)/shard_map/attend/pallas_call | solution.py:173
  241.1 7.5 %attend.3 = bf16[2,512,640]{2,1,0:T(8,128)(2,1)} custom-call(s32[3]{0:T(128)S(1)} %get-tuple-element.38.info, bf16[5,512,128]{2,1,0:T(8,128)(2,1)S(1)} %copy-done.5, bf16[2,5,512,128]{3,2,1,0:T(8,128)(2,1)S(1)} %select_select_fusion.refs_1_, bf16[2,5,512,128]{3,2,1,0:T(8,128)(2,1)} %collective-permute-done.16.refs_2_, ...), custom_call_target="tpu_custom_call", output_to_operand_aliasing={{}: (7, {})} | custom-call | flops 1342177280 | bytes 3932160 | tf_op jit(solution)/shard_map/attend/pallas_call | solution.py:173
  (57 shorter events, 26.8 us)
Async XLA Ops:
  3.5 17.3 %collective-permute-start = (bf16[512,1280]{1,0:T(8,128)(2,1)}, bf16[512,1280]{1,0:T(8,128)(2,1)}, u32[]{:S(2)}, u32[]{:S(2)}) collective-permute-start(bf16[512,1280]{1,0:T(8,128)(2,1)} %get-tuple-element.37), channel_id=1, source_target_pairs={{4,0},{8,4},{12,8},{16,12},{20,16},{24,20},{28,24},{5,1},{9,5},{13... | collective-permute-start | bytes 3932168 | tf_op jit(solution)/shard_map/ppermute | solution.py:230
  23.4 30.0 %collective-permute-start.2 = (bf16[512,1280]{1,0:T(8,128)(2,1)S(1)}, bf16[512,1280]{1,0:T(8,128)(2,1)S(1)}, u32[]{:S(2)}, u32[]{:S(2)}) collective-permute-start(bf16[512,1280]{1,0:T(8,128)(2,1)S(1)} %fusion.5.refs_2_), channel_id=1, source_target_pairs={{0,1},{1,0},{2,3},{3,2},{4,5},{5,4},{6,7},{7,6},{8,9},{9,8},{10,11... | collective-permute-start | bytes 3932168 | tf_op jit(solution)/shard_map/ppermute | solution.py:249
  23.9 32.5 %collective-permute-start.3 = (bf16[512,1280]{1,0:T(8,128)(2,1)S(1)}, bf16[512,1280]{1,0:T(8,128)(2,1)S(1)}, u32[]{:S(2)}, u32[]{:S(2)}) collective-permute-start(bf16[512,1280]{1,0:T(8,128)(2,1)S(1)} %fusion.5.refs_2_), channel_id=1, source_target_pairs={{1,2},{2,1},{5,6},{6,5},{9,10},{10,9},{13,14},{14,13},{17,18},{18,... | collective-permute-start | bytes 3932168 | tf_op jit(solution)/shard_map/ppermute | solution.py:249
  29.6 100.1 %copy-start.12 = (f32[640]{0:T(1024)S(1)}, f32[640]{0:T(1024)}, u32[]{:S(2)}) copy-start(f32[640]{0:T(1024)} %param.12) | copy-start | bytes 7684
  29.6 100.1 %copy-start.13 = (f32[640]{0:T(1024)S(1)}, f32[640]{0:T(1024)}, u32[]{:S(2)}) copy-start(f32[640]{0:T(1024)} %param.13) | copy-start | bytes 7684
  29.6 32.4 %collective-permute-start.1 = (bf16[512,1280]{1,0:T(8,128)(2,1)S(1)}, bf16[512,1280]{1,0:T(8,128)(2,1)S(1)}, u32[]{:S(2)}, u32[]{:S(2)}) collective-permute-start(bf16[512,1280]{1,0:T(8,128)(2,1)S(1)} %copy-done.10), channel_id=1, source_target_pairs={{0,4},{4,8},{8,12},{12,16},{16,20},{20,24},{24,28},{1,5},{5,9},{9,... | collective-permute-start | bytes 3932168 | tf_op jit(solution)/shard_map/ppermute | solution.py:238
  56.4 33.4 %collective-permute-start.4 = (bf16[512,1280]{1,0:T(8,128)(2,1)S(1)}, bf16[512,1280]{1,0:T(8,128)(2,1)}, u32[]{:S(2)}, u32[]{:S(2)}) collective-permute-start(bf16[512,1280]{1,0:T(8,128)(2,1)S(1)} %collective-permute-done.2.refs_3_), channel_id=1, source_target_pairs={{1,2},{2,1},{5,6},{6,5},{9,10},{10,9},{13,14},{14,13},{17,18},{18,... | collective-permute-start | bytes 3932168 | tf_op jit(solution)/shard_map/ppermute | solution.py:249
  60.6 30.2 %collective-permute-start.5 = (bf16[512,1280]{1,0:T(8,128)(2,1)S(1)}, bf16[512,1280]{1,0:T(8,128)(2,1)S(1)}, u32[]{:S(2)}, u32[]{:S(2)}) collective-permute-start(bf16[512,1280]{1,0:T(8,128)(2,1)S(1)} %collective-permute-done.3.refs_4_), channel_id=1, source_target_pairs={{1,0},{2,3},{5,4},{6,7},{9,8},{10,11},{13,12},{14,15},{17,16},{18,... | collective-permute-start | bytes 3932168 | tf_op jit(solution)/shard_map/ppermute | solution.py:249
  90.8 33.2 %copy-start.9 = (bf16[512,1280]{1,0:T(8,128)(2,1)}, bf16[512,1280]{1,0:T(8,128)(2,1)S(1)}, u32[]{:S(2)}) copy-start(bf16[512,1280]{1,0:T(8,128)(2,1)S(1)} %collective-permute-done.5.refs_5_) | copy-start | bytes 3932164
  90.8 33.2 %collective-permute-start.6 = (bf16[512,1280]{1,0:T(8,128)(2,1)}, bf16[512,1280]{1,0:T(8,128)(2,1)S(1)}, u32[]{:S(2)}, u32[]{:S(2)}) collective-permute-start(bf16[512,1280]{1,0:T(8,128)(2,1)} %fusion.2.refs_0_), channel_id=1, source_target_pairs={{0,1},{3,2},{4,5},{7,6},{8,9},{11,10},{12,13},{15,14},{16,17},{19,... | collective-permute-start | bytes 3932168 | tf_op jit(solution)/shard_map/ppermute | solution.py:249
  92.1 37.8 %collective-permute-start.9 = (bf16[512,1280]{1,0:T(8,128)(2,1)}, bf16[512,1280]{1,0:T(8,128)(2,1)}, u32[]{:S(2)}, u32[]{:S(2)}) collective-permute-start(bf16[512,1280]{1,0:T(8,128)(2,1)} %fusion.2.refs_0_), channel_id=1, source_target_pairs={{1,2},{2,1},{5,6},{6,5},{9,10},{10,9},{13,14},{14,13},{17,18},{18,... | collective-permute-start | bytes 3932168 | tf_op jit(solution)/shard_map/ppermute | solution.py:249
  95.3 34.6 %collective-permute-start.10 = (bf16[512,1280]{1,0:T(8,128)(2,1)}, bf16[512,1280]{1,0:T(8,128)(2,1)}, u32[]{:S(2)}, u32[]{:S(2)}) collective-permute-start(bf16[512,1280]{1,0:T(8,128)(2,1)} %collective-permute-done.4.refs_6_), channel_id=1, source_target_pairs={{1,0},{2,3},{5,4},{6,7},{9,8},{10,11},{13,12},{14,15},{17,16},{18,... | collective-permute-start | bytes 3932168 | tf_op jit(solution)/shard_map/ppermute | solution.py:249
  124.0 22.7 %copy-start = (bf16[512,1280]{1,0:T(8,128)(2,1)}, bf16[512,1280]{1,0:T(8,128)(2,1)S(1)}, u32[]{:S(2)}) copy-start(bf16[512,1280]{1,0:T(8,128)(2,1)S(1)} %collective-permute-done.6.refs_0_.refs_1_) | copy-start | bytes 3932164
  124.0 31.2 %collective-permute-start.11 = (bf16[512,1280]{1,0:T(8,128)(2,1)}, bf16[512,1280]{1,0:T(8,128)(2,1)}, u32[]{:S(2)}, u32[]{:S(2)}) collective-permute-start(bf16[512,1280]{1,0:T(8,128)(2,1)} %fusion.2.refs_0_), channel_id=1, source_target_pairs={{1,0},{2,3},{5,4},{6,7},{9,8},{10,11},{13,12},{14,15},{17,16},{18,... | collective-permute-start | bytes 3932168 | tf_op jit(solution)/shard_map/ppermute | solution.py:249
  126.6 38.8 %collective-permute-start.7 = (bf16[512,1280]{1,0:T(8,128)(2,1)S(1)}, bf16[512,1280]{1,0:T(8,128)(2,1)}, u32[]{:S(2)}, u32[]{:S(2)}) collective-permute-start(bf16[512,1280]{1,0:T(8,128)(2,1)S(1)} %collective-permute-done.6.refs_0_.refs_1_), channel_id=1, source_target_pairs={{1,2},{2,1},{5,6},{6,5},{9,10},{10,9},{13,14},{14,13},{17,18},{18,... | collective-permute-start | bytes 3932168 | tf_op jit(solution)/shard_map/ppermute | solution.py:249
  155.2 12.6 %collective-permute-start.13 = (bf16[2,5,512,128]{3,2,1,0:T(8,128)(2,1)S(1)}, bf16[2,5,512,128]{3,2,1,0:T(8,128)(2,1)}, u32[]{:S(2)}, u32[]{:S(2)}) collective-permute-start(bf16[2,5,512,128]{3,2,1,0:T(8,128)(2,1)S(1)} %get-tuple-element.30.refs_3_), channel_id=1, source_target_pairs={{0,24},{1,25},{2,26},{3,27}} | collective-permute-start | bytes 3932168 | tf_op jit(solution)/shard_map/ppermute | solution.py:202
  156.9 10.9 %collective-permute-start.14 = (bf16[2,5,512,128]{3,2,1,0:T(8,128)(2,1)S(1)}, bf16[2,5,512,128]{3,2,1,0:T(8,128)(2,1)}, u32[]{:S(2)}, u32[]{:S(2)}) collective-permute-start(bf16[2,5,512,128]{3,2,1,0:T(8,128)(2,1)S(1)} %get-tuple-element.30.refs_3_), channel_id=1, source_target_pairs={{0,16},{1,17},{2,18},{3,19}} | collective-permute-start | bytes 3932168 | tf_op jit(solution)/shard_map/ppermute | solution.py:202
  158.6 19.9 %collective-permute-start.15 = (bf16[2,5,512,128]{3,2,1,0:T(8,128)(2,1)S(1)}, bf16[2,5,512,128]{3,2,1,0:T(8,128)(2,1)}, u32[]{:S(2)}, u32[]{:S(2)}) collective-permute-start(bf16[2,5,512,128]{3,2,1,0:T(8,128)(2,1)S(1)} %get-tuple-element.30.refs_3_), channel_id=1, source_target_pairs={{0,8},{1,9},{2,10},{3,11}} | collective-permute-start | bytes 3932168 | tf_op jit(solution)/shard_map/ppermute | solution.py:202
  159.9 33.9 %collective-permute-start.12 = (bf16[512,1280]{1,0:T(8,128)(2,1)}, bf16[512,1280]{1,0:T(8,128)(2,1)}, u32[]{:S(2)}, u32[]{:S(2)}) collective-permute-start(bf16[512,1280]{1,0:T(8,128)(2,1)} %collective-permute-done.9.refs_1_.refs_3_), channel_id=1, source_target_pairs={{1,0},{2,3},{5,4},{6,7},{9,8},{10,11},{13,12},{14,15},{17,16},{18,... | collective-permute-start | bytes 3932168 | tf_op jit(solution)/shard_map/ppermute | solution.py:249
  165.4 55.3 %collective-permute-start.8 = (bf16[512,1280]{1,0:T(8,128)(2,1)}, bf16[512,1280]{1,0:T(8,128)(2,1)}, u32[]{:S(2)}, u32[]{:S(2)}) collective-permute-start(bf16[512,1280]{1,0:T(8,128)(2,1)} %collective-permute-done.7.refs_0_), channel_id=1, source_target_pairs={{1,0},{2,3},{5,4},{6,7},{9,8},{10,11},{13,12},{14,15},{17,16},{18,... | collective-permute-start | bytes 3932168 | tf_op jit(solution)/shard_map/ppermute | solution.py:249
  167.8 26.0 %copy-start.1 = (bf16[512,1280]{1,0:T(8,128)(2,1)S(1)}, bf16[512,1280]{1,0:T(8,128)(2,1)}, u32[]{:S(2)}) copy-start(bf16[512,1280]{1,0:T(8,128)(2,1)} %copy-done) | copy-start | bytes 3932164
  180.1 53.4 %collective-permute-start.16 = (bf16[2,5,512,128]{3,2,1,0:T(8,128)(2,1)S(1)}, bf16[2,5,512,128]{3,2,1,0:T(8,128)(2,1)}, u32[]{:S(2)}, u32[]{:S(2)}) collective-permute-start(bf16[2,5,512,128]{3,2,1,0:T(8,128)(2,1)S(1)} %select_select_fusion.refs_1_), channel_id=1, source_target_pairs={{0,4},{8,12},{16,20},{24,28},{1,5},{9,13},{17,21},{25,29},{2,6},{1... | collective-permute-start | bytes 3932168 | tf_op jit(solution)/shard_map/ppermute | solution.py:203
  182.6 58.4 %collective-permute-start.17 = (bf16[2,5,512,128]{3,2,1,0:T(8,128)(2,1)S(1)}, bf16[2,5,512,128]{3,2,1,0:T(8,128)(2,1)}, u32[]{:S(2)}, u32[]{:S(2)}) collective-permute-start(bf16[2,5,512,128]{3,2,1,0:T(8,128)(2,1)S(1)} %get-tuple-element.30.refs_3_), channel_id=1, source_target_pairs={{4,8},{8,12},{12,16},{16,20},{20,24},{24,28},{5,9},{9,13},{13,17},... | collective-permute-start | bytes 3932168 | tf_op jit(solution)/shard_map/ppermute | solution.py:264
  231.7 9.3 %collective-permute-start.18 = (bf16[2,5,512,128]{3,2,1,0:T(8,128)(2,1)}, bf16[2,5,512,128]{3,2,1,0:T(8,128)(2,1)}, u32[]{:S(2)}, u32[]{:S(2)}) collective-permute-start(bf16[2,5,512,128]{3,2,1,0:T(8,128)(2,1)} %get-tuple-element.31.refs_4_), channel_id=1, source_target_pairs={{0,4},{1,5},{2,6},{3,7}} | collective-permute-start | bytes 3932168 | tf_op jit(solution)/shard_map/ppermute | solution.py:268
  (9 other events, 64.5 us)

commit v4 on v3

--- a/solution.py
+++ b/solution.py
@@ -221,9 +221,10 @@
     z = lax.axis_index("head").astype(jnp.int32)
     outer = (z == 0) | (z == 3)
     near, far = (z + 2) % 4, 3 - z
-    info = jnp.stack(
-        [outer.astype(jnp.int32), z, z ^ 1, jnp.where(outer, near, far), jnp.where(outer, far, near)]
-    )
+    side = outer.astype(jnp.int32)
+    pair, second, third = z ^ 1, jnp.where(outer, near, far), jnp.where(outer, far, near)
+    info = jnp.stack([side, z, pair, second, third])
+    info_raw, info_end = jnp.stack([side, z, second, third]), jnp.stack([side, pair])
     first, last = frames[0], frames[1]
     ups = [(i, i + 1) for i in range(count - 1)]
     start = pos == 0
@@ -234,8 +235,8 @@
         jnp.where(start, last, following),
         taps,
     )
-    _, held_last = lax.optimization_barrier((mixed1, last))
-    preceding = lax.ppermute(held_last, "tm", ups)
+    _, later = lax.optimization_barrier((mixed1, frames))
+    preceding = lax.ppermute(later[1], "tm", ups)
     mixed2 = mix(
         jnp.where(start, first, preceding),
         jnp.where(start, last, first),
@@ -248,23 +249,25 @@
     def send(x, pairs):
         return lax.ppermute(x, "head", pairs)
 
-    swap1, middle1 = send(mixed1, SWAP), send(mixed1, MIDDLE)
-    swap1, middle1 = lax.optimization_barrier((swap1, middle1))
-    cross1, second1 = send(swap1, MIDDLE), send(middle1, OUTWARD)
-    mixed2, cross1, second1 = lax.optimization_barrier((mixed2, cross1, second1))
-    third1, inward2, middle2 = send(cross1, OUTWARD), send(mixed2, INWARD), send(mixed2, MIDDLE)
-    later2, inward2 = lax.optimization_barrier((mixed2, inward2))
-    cross2, first2 = send(inward2, MIDDLE), send(later2, OUTWARD)
-    second2, third2 = send(middle2, OUTWARD), send(cross2, OUTWARD)
-
-    sources1 = [(mixed1,), (swap1,), (middle1, second1), (cross1, third1)]
-    q1, kv1 = project(sources1, info, weights, gains, after=(inward2, middle2))
-    kv1, first2 = lax.optimization_barrier((kv1, first2))
+    inward1, middle1, first1 = send(mixed1, INWARD), send(mixed1, MIDDLE), send(mixed1, OUTWARD)
+    inward1, middle1, first1 = lax.optimization_barrier((inward1, middle1, first1))
+    inward2, cross1, second1 = send(mixed2, INWARD), send(inward1, MIDDLE), send(middle1, OUTWARD)
+    later2, cross1 = lax.optimization_barrier((mixed2, cross1))
+    middle2 = send(later2, MIDDLE)
+    cross1, second1 = lax.optimization_barrier((cross1, second1))
+    third1 = send(cross1, OUTWARD)
+    middle2, inward2 = lax.optimization_barrier((middle2, inward2))
+    cross2, second2 = send(inward2, MIDDLE), send(middle2, OUTWARD)
+    third2 = send(cross2, OUTWARD)
+    later2, second2 = lax.optimization_barrier((mixed2, second2))
+    first2 = send(later2, OUTWARD)
+
+    sources1 = [(mixed1,), (inward1, first1), (middle1, second1), (cross1, third1)]
+    q1, kv1 = project(sources1, info, weights, gains, after=(inward2, middle2), flops=10**10)
     anchor = broadcast_first(kv1, "tm")
     shift1 = lax.ppermute(kv1, "tm", [(i, i + 1) for i in range(1, count - 1)])
-    raw2 = project([(mixed2,), (inward2, first2), (middle2, second2)], info, weights)
-    info_end = jnp.stack([info[0], info[4]])
-    q2, kv2 = project([(cross2, third2)], info_end, weights, gains, raw2)
+    raw2 = project([(mixed2,), (middle2, second2), (cross2, third2)], info_raw, weights, flops=10**10)
+    q2, kv2 = project([(inward2, first2)], info_end, weights, gains, raw2, flops=10**10)
     shift2 = lax.ppermute(kv2, "tm", [(0, 1)])
     late = jnp.where(start, 0, 1)
     odd = pos % 2

time: 251 us -> 242 us (0.964)
  waiting for transfers between devices: 129 us -> 125 us
  local copies, waits for them, and re-layouts: 6.92 us -> 3.62 us
    ppermute x3, waiting for transfers between devices: 10.7 us -> 7.56 us  [broadcast_first(): held = jnp.where(mine == to, lax.ppermute(x, axis, [(0, to)]), held)]
    ppermute x11 -> x12, starting transfers between devices: 33 us -> 32.1 us  [send(): return lax.ppermute(x, 'head', pairs)]
    ppermute x11 -> x12, waiting for transfers between devices: 102 us -> 103 us  [send(): return lax.ppermute(x, 'head', pairs)]
  transfers between devices with their start and end apart: 19 -> 20, of which waited for: 10 -> 11; matrix products, arithmetic and copies ran while one was open for 2% -> 2% of each run, Pallas kernels for 20% -> 20%
where the time goes in v4:
time: 242 us; the launch traced here: 240 us
  waiting for transfers between devices  125 us (52%)
  Pallas kernels  56.3 us (23%)
  starting transfers between devices  47.8 us (20%)
  other arithmetic  6.9 us (3%)
  local copies, waits for them, and re-layouts  3.62 us (1%)
    ppermute x12, waiting for transfers between devices, send(): return lax.ppermute(x, 'head', pairs)  103 us
    pallas_call x3, Pallas kernels, project(): pl.pallas_call(functools.partial(project_body, pairs, len(after), acc is...  41.3 us
    ppermute x12, starting transfers between devices, send(): return lax.ppermute(x, 'head', pairs)  32.1 us
    pallas_call x2, Pallas kernels, attend(): pl.pallas_call(functools.partial(attend_body, 128, (len(anchors), len(opt...  15 us
    ppermute x1, waiting for transfers between devices, per_device(): following = lax.ppermute(first, 'tm', [(j, i) for i, j in ups])  15 us
    ppermute x3, waiting for transfers between devices, broadcast_first(): held = jnp.where(mine == to, lax.ppermute(x, axis, [(0, to)]), held)  7.56 us
    convert_element_type x2, other arithmetic, mix(): (centre + taps[0] * before + taps[1] * centre + taps[2] * after).astype(B...  5.13 us
  transfers between devices with their start and end apart: 20, of which 11 were waited for; matrix products, arithmetic and copies ran while one was open for 2% of the time, Pallas kernels for 20%

profile of v4, /device:TPU:10, one launch (start us, length us, event | category | flops | bytes accessed | tf_op | source)
XLA Modules:
  0.0 240.2 jit_solution(14231177364953360626)
XLA Ops:
  3.4 15.0 %collective-permute-done = bf16[512,1280]{1,0:T(8,128)(2,1)S(1)} collective-permute-done((bf16[512,1280]{1,0:T(8,128)(2,1)S(1)}, bf16[512,1280]{1,0:T(8,128)(2,1)S(1)}, u32[]{:S(2)}, u32[]{:S(2)}) %collective-permute-start) | collective-permute-done | bytes 1310752 | tf_op jit(solution)/shard_map/ppermute | solution.py:231
  18.4 2.9 %fusion.5.refs_2_ = bf16[512,1280]{1,0:T(8,128)(2,1)S(1)} fusion(bf16[512,1280]{1,0:T(8,128)(2,1)S(1)} %collective-permute-done, f32[1280]{0:T(1024)S(1)} %get-tuple-element.38, f32[1280]{0:T(1024)S(1)} %get-tuple-element.39, f32[1280]{0:T(1024)S(1)} %get-tuple-element.37, pred[]{:T(512)S(6)} %eq.24, bf16[2,512,1280]{2,1,0:T(8,128)(2,1)} %param.7), kind=kLoop, calls=%fused_computation.9 | loop fusion | flops 8519680 | bytes 5258241 | tf_op jit(solution)/shard_map/convert_element_type | solution.py:215
  22.7 3.5 %collective-permute-start.3 = (bf16[512,1280]{1,0:T(8,128)(2,1)S(1)}, bf16[512,1280]{1,0:T(8,128)(2,1)S(1)}, u32[]{:S(2)}, u32[]{:S(2)}) collective-permute-start(bf16[512,1280]{1,0:T(8,128)(2,1)S(1)} %fusion.5.refs_2_), channel_id=1, source_target_pairs={{1,2},{2,1},{5,6},{6,5},{9,10},{10,9},{13,14},{14,13},{17,18},{18,... | collective-permute-start | bytes 3932168 | tf_op jit(solution)/shard_map/ppermute | solution.py:250
  28.3 4.0 %collective-permute-start.1 = (bf16[512,1280]{1,0:T(8,128)(2,1)S(1)}, bf16[512,1280]{1,0:T(8,128)(2,1)S(1)}, u32[]{:S(2)}, u32[]{:S(2)}) collective-permute-start(bf16[512,1280]{1,0:T(8,128)(2,1)S(1)} %slice_bitcast_fusion), channel_id=1, source_target_pairs={{0,4},{4,8},{8,12},{12,16},{16,20},{20,24},{24,28},{1,5},{5,9},{9,... | collective-permute-start | bytes 3932168 | tf_op jit(solution)/shard_map/ppermute | solution.py:239
  32.3 20.9 %collective-permute-done.2.refs_3_ = bf16[512,1280]{1,0:T(8,128)(2,1)S(1)} collective-permute-done((bf16[512,1280]{1,0:T(8,128)(2,1)S(1)}, bf16[512,1280]{1,0:T(8,128)(2,1)S(1)}, u32[]{:S(2)}, u32[]{:S(2)}) %collective-permute-start.2) | collective-permute-done | bytes 1310752 | tf_op jit(solution)/shard_map/ppermute | solution.py:250
  55.8 3.5 %collective-permute-start.5 = (bf16[512,1280]{1,0:T(8,128)(2,1)S(1)}, bf16[512,1280]{1,0:T(8,128)(2,1)}, u32[]{:S(2)}, u32[]{:S(2)}) collective-permute-start(bf16[512,1280]{1,0:T(8,128)(2,1)S(1)} %collective-permute-done.2.refs_3_), channel_id=1, source_target_pairs={{1,2},{2,1},{5,6},{6,5},{9,10},{10,9},{13,14},{14,13},{17,18},{18,... | collective-permute-start | bytes 3932168 | tf_op jit(solution)/shard_map/ppermute | solution.py:250
  59.3 2.7 %collective-permute-start.12 = (bf16[512,1280]{1,0:T(8,128)(2,1)S(1)}, bf16[512,1280]{1,0:T(8,128)(2,1)S(1)}, u32[]{:S(2)}, u32[]{:S(2)}) collective-permute-start(bf16[512,1280]{1,0:T(8,128)(2,1)S(1)} %collective-permute-done.3.refs_5_), channel_id=1, source_target_pairs={{1,0},{2,3},{5,4},{6,7},{9,8},{10,11},{13,12},{14,15},{17,16},{18,... | collective-permute-start | bytes 3932168 | tf_op jit(solution)/shard_map/ppermute | solution.py:250
  65.5 23.4 %collective-permute-done.5.refs_7_ = bf16[512,1280]{1,0:T(8,128)(2,1)} collective-permute-done((bf16[512,1280]{1,0:T(8,128)(2,1)S(1)}, bf16[512,1280]{1,0:T(8,128)(2,1)}, u32[]{:S(2)}, u32[]{:S(2)}) %collective-permute-start.5) | collective-permute-done | bytes 1310752 | tf_op jit(solution)/shard_map/ppermute | solution.py:250
  88.9 3.5 %collective-permute-start.6 = (bf16[512,1280]{1,0:T(8,128)(2,1)}, bf16[512,1280]{1,0:T(8,128)(2,1)}, u32[]{:S(2)}, u32[]{:S(2)}) collective-permute-start(bf16[512,1280]{1,0:T(8,128)(2,1)} %fusion.2.refs_0_), channel_id=1, source_target_pairs={{1,2},{2,1},{5,6},{6,5},{9,10},{10,9},{13,14},{14,13},{17,18},{18,... | collective-permute-start | bytes 3932168 | tf_op jit(solution)/shard_map/ppermute | solution.py:250
  93.5 3.9 %collective-permute-start.13 = (bf16[512,1280]{1,0:T(8,128)(2,1)}, bf16[512,1280]{1,0:T(8,128)(2,1)}, u32[]{:S(2)}, u32[]{:S(2)}) collective-permute-start(bf16[512,1280]{1,0:T(8,128)(2,1)} %collective-permute-done.5.refs_7_), channel_id=1, source_target_pairs={{1,0},{2,3},{5,4},{6,7},{9,8},{10,11},{13,12},{14,15},{17,16},{18,... | collective-permute-start | bytes 3932168 | tf_op jit(solution)/shard_map/ppermute | solution.py:250
  98.1 24.4 %collective-permute-done.6.refs_1_ = bf16[512,1280]{1,0:T(8,128)(2,1)} collective-permute-done((bf16[512,1280]{1,0:T(8,128)(2,1)}, bf16[512,1280]{1,0:T(8,128)(2,1)}, u32[]{:S(2)}, u32[]{:S(2)}) %collective-permute-start.6) | collective-permute-done | bytes 1310752 | tf_op jit(solution)/shard_map/ppermute | solution.py:250
  122.4 3.5 %collective-permute-start.10 = (bf16[512,1280]{1,0:T(8,128)(2,1)}, bf16[512,1280]{1,0:T(8,128)(2,1)}, u32[]{:S(2)}, u32[]{:S(2)}) collective-permute-start(bf16[512,1280]{1,0:T(8,128)(2,1)} %collective-permute-done.7.refs_0_), channel_id=1, source_target_pairs={{1,2},{2,1},{5,6},{6,5},{9,10},{10,9},{13,14},{14,13},{17,18},{18,... | collective-permute-start | bytes 3932168 | tf_op jit(solution)/shard_map/ppermute | solution.py:250
  125.9 2.4 collective-permute-start.8
  128.3 15.5 %project_end.3 = (bf16[5,512,128]{2,1,0:T(8,128)(2,1)S(1)}, bf16[2,5,512,128]{3,2,1,0:T(8,128)(2,1)S(1)}) custom-call(s32[5]{0:T(128)S(1)} %stack.65.info, bf16[512,1280]{1,0:T(8,128)(2,1)} %collective-permute-done.7.refs_0_, bf16[512,1280]{1,0:T(8,128)(2,1)} %collective-permute-done.6.refs_1_, bf16[512,1280]{1,0:T(8,128)(2,1)S(1)} %fusion.5.refs_2_, ...), custom_call_target="tpu_custom_call" | custom-call | flops 10000000000 | bytes 1 | tf_op jit(solution)/shard_map/project_end/pallas_call | solution.py:106
  147.6 7.5 %collective-permute-done.10.refs_3_ = bf16[512,1280]{1,0:T(8,128)(2,1)} collective-permute-done((bf16[512,1280]{1,0:T(8,128)(2,1)}, bf16[512,1280]{1,0:T(8,128)(2,1)}, u32[]{:S(2)}, u32[]{:S(2)}) %collective-permute-start.10) | collective-permute-done | bytes 1310752 | tf_op jit(solution)/shard_map/ppermute | solution.py:250
  155.1 2.4 %collective-permute-start.11 = (bf16[512,1280]{1,0:T(8,128)(2,1)}, bf16[512,1280]{1,0:T(8,128)(2,1)}, u32[]{:S(2)}, u32[]{:S(2)}) collective-permute-start(bf16[512,1280]{1,0:T(8,128)(2,1)} %collective-permute-done.10.refs_3_), channel_id=1, source_target_pairs={{1,0},{2,3},{5,4},{6,7},{9,8},{10,11},{13,12},{14,15},{17,16},{18,... | collective-permute-start | bytes 3932168 | tf_op jit(solution)/shard_map/ppermute | solution.py:250
  161.9 7.6 %collective-permute-done.16 = bf16[2,5,512,128]{3,2,1,0:T(8,128)(2,1)} collective-permute-done((bf16[2,5,512,128]{3,2,1,0:T(8,128)(2,1)S(1)}, bf16[2,5,512,128]{3,2,1,0:T(8,128)(2,1)}, u32[]{:S(2)}, u32[]{:S(2)}) %collective-permute-start.16) | collective-permute-done | bytes 1310752 | tf_op jit(solution)/shard_map/ppermute | solution.py:202
  171.0 2.4 collective-permute-start.17
  173.4 12.5 %collective-permute-done.11.refs_4_ = bf16[512,1280]{1,0:T(8,128)(2,1)} collective-permute-done((bf16[512,1280]{1,0:T(8,128)(2,1)}, bf16[512,1280]{1,0:T(8,128)(2,1)}, u32[]{:S(2)}, u32[]{:S(2)}) %collective-permute-start.11) | collective-permute-done | bytes 1310752 | tf_op jit(solution)/shard_map/ppermute | solution.py:250
  185.9 15.6 %project_raw.1.refs_7_ = f32[512,1920]{1,0:T(8,128)} custom-call(s32[4]{0:T(128)S(1)} %pad_add_fusion.2.info, bf16[512,1280]{1,0:T(8,128)(2,1)} %fusion.2.refs_0_, bf16[512,1280]{1,0:T(8,128)(2,1)} %collective-permute-done.6.refs_1_, bf16[512,1280]{1,0:T(8,128)(2,1)} %collective-permute-done.8.refs_2_, bf16[512,1280]{1,0:T(8,128)(2,1)} %collective-permute-done.10.refs_3_, ...), custom_call_target="tpu_custom_call" | custom-call | flops 10000000000 | bytes 1 | tf_op jit(solution)/shard_map/project_raw/pallas_call | solution.py:106
  201.5 10.6 %collective-permute-done.9.refs_1_ = bf16[512,1280]{1,0:T(8,128)(2,1)S(1)} collective-permute-done((bf16[512,1280]{1,0:T(8,128)(2,1)}, bf16[512,1280]{1,0:T(8,128)(2,1)S(1)}, u32[]{:S(2)}, u32[]{:S(2)}) %collective-permute-start.9) | collective-permute-done | bytes 1310752 | tf_op jit(solution)/shard_map/ppermute | solution.py:250
  212.1 10.1 %project_end.2 = (bf16[5,512,128]{2,1,0:T(8,128)(2,1)S(1)}, bf16[2,5,512,128]{3,2,1,0:T(8,128)(2,1)}) custom-call(s32[2]{0:T(128)S(1)} %pad_add_fusion.1.info, bf16[512,1280]{1,0:T(8,128)(2,1)} %collective-permute-done.7.refs_0_, bf16[512,1280]{1,0:T(8,128)(2,1)S(1)} %collective-permute-done.9.refs_1_, bf16[5120,640]{1,0:T(8,128)(2,1)} %refs_9_.1, ...), custom_call_target="tpu_custom_call" | custom-call | flops 10000000000 | bytes 1 | tf_op jit(solution)/shard_map/project_end/pallas_call | solution.py:106
  225.0 7.5 %attend.2.refs_6_ = bf16[2,512,640]{2,1,0:T(8,128)(2,1)} custom-call(s32[3]{0:T(128)S(1)} %get-tuple-element.41.info, bf16[5,512,128]{2,1,0:T(8,128)(2,1)S(1)} %get-tuple-element.36.refs_0_, bf16[2,5,512,128]{3,2,1,0:T(8,128)(2,1)S(1)} %select_select_fusion.refs_1_, bf16[2,5,512,128]{3,2,1,0:T(8,128)(2,1)} %collective-permute-done.17.refs_2_, ...), custom_call_target="tpu_custom_call" | custom-call | flops 1342177280 | bytes 3932160 | tf_op jit(solution)/shard_map/attend/pallas_call | solution.py:173
  232.5 7.5 %attend.3 = bf16[2,512,640]{2,1,0:T(8,128)(2,1)} custom-call(s32[3]{0:T(128)S(1)} %get-tuple-element.40.info, bf16[5,512,128]{2,1,0:T(8,128)(2,1)S(1)} %copy-done.1, bf16[2,5,512,128]{3,2,1,0:T(8,128)(2,1)S(1)} %select_select_fusion.refs_1_, bf16[2,5,512,128]{3,2,1,0:T(8,128)(2,1)} %collective-permute-done.17.refs_2_, ...), custom_call_target="tpu_custom_call", output_to_operand_aliasing={{}: (7, {})} | custom-call | flops 1342177280 | bytes 3932160 | tf_op jit(solution)/shard_map/attend/pallas_call | solution.py:173
  (55 shorter events, 27.0 us)
Async XLA Ops:
  1.4 17.0 %collective-permute-start = (bf16[512,1280]{1,0:T(8,128)(2,1)S(1)}, bf16[512,1280]{1,0:T(8,128)(2,1)S(1)}, u32[]{:S(2)}, u32[]{:S(2)}) collective-permute-start(bf16[512,1280]{1,0:T(8,128)(2,1)S(1)} %slice_bitcast_fusion.1), channel_id=1, source_target_pairs={{4,0},{8,4},{12,8},{16,12},{20,16},{24,20},{28,24},{5,1},{9,5},{13... | collective-permute-start | bytes 3932168 | tf_op jit(solution)/shard_map/ppermute | solution.py:231
  21.4 31.8 %collective-permute-start.2 = (bf16[512,1280]{1,0:T(8,128)(2,1)S(1)}, bf16[512,1280]{1,0:T(8,128)(2,1)S(1)}, u32[]{:S(2)}, u32[]{:S(2)}) collective-permute-start(bf16[512,1280]{1,0:T(8,128)(2,1)S(1)} %fusion.5.refs_2_), channel_id=1, source_target_pairs={{0,1},{3,2},{4,5},{7,6},{8,9},{11,10},{12,13},{15,14},{16,17},{19,... | collective-permute-start | bytes 3932168 | tf_op jit(solution)/shard_map/ppermute | solution.py:250
  22.7 31.8 %collective-permute-start.3 = (bf16[512,1280]{1,0:T(8,128)(2,1)S(1)}, bf16[512,1280]{1,0:T(8,128)(2,1)S(1)}, u32[]{:S(2)}, u32[]{:S(2)}) collective-permute-start(bf16[512,1280]{1,0:T(8,128)(2,1)S(1)} %fusion.5.refs_2_), channel_id=1, source_target_pairs={{1,2},{2,1},{5,6},{6,5},{9,10},{10,9},{13,14},{14,13},{17,18},{18,... | collective-permute-start | bytes 3932168 | tf_op jit(solution)/shard_map/ppermute | solution.py:250
  26.2 29.6 %collective-permute-start.4 = (bf16[512,1280]{1,0:T(8,128)(2,1)S(1)}, bf16[512,1280]{1,0:T(8,128)(2,1)S(1)}, u32[]{:S(2)}, u32[]{:S(2)}) collective-permute-start(bf16[512,1280]{1,0:T(8,128)(2,1)S(1)} %fusion.5.refs_2_), channel_id=1, source_target_pairs={{1,0},{2,3},{5,4},{6,7},{9,8},{10,11},{13,12},{14,15},{17,16},{18,... | collective-permute-start | bytes 3932168 | tf_op jit(solution)/shard_map/ppermute | solution.py:250
  28.2 69.1 %copy-start.5 = (f32[640]{0:T(1024)S(1)}, f32[640]{0:T(1024)}, u32[]{:S(2)}) copy-start(f32[640]{0:T(1024)} %param.12) | copy-start | bytes 7684
  28.3 69.1 %copy-start.6 = (f32[640]{0:T(1024)S(1)}, f32[640]{0:T(1024)}, u32[]{:S(2)}) copy-start(f32[640]{0:T(1024)} %param.13) | copy-start | bytes 7684
  28.3 33.7 %collective-permute-start.1 = (bf16[512,1280]{1,0:T(8,128)(2,1)S(1)}, bf16[512,1280]{1,0:T(8,128)(2,1)S(1)}, u32[]{:S(2)}, u32[]{:S(2)}) collective-permute-start(bf16[512,1280]{1,0:T(8,128)(2,1)S(1)} %slice_bitcast_fusion), channel_id=1, source_target_pairs={{0,4},{4,8},{8,12},{12,16},{16,20},{20,24},{24,28},{1,5},{5,9},{9,... | collective-permute-start | bytes 3932168 | tf_op jit(solution)/shard_map/ppermute | solution.py:239
  53.2 11.0 %copy-start.7 = (bf16[512,1280]{1,0:T(8,128)(2,1)}, bf16[512,1280]{1,0:T(8,128)(2,1)S(1)}, u32[]{:S(2)}) copy-start(bf16[512,1280]{1,0:T(8,128)(2,1)S(1)} %collective-permute-done.2.refs_3_) | copy-start | bytes 3932164
  54.5 9.7 %copy-start.8 = (bf16[512,1280]{1,0:T(8,128)(2,1)}, bf16[512,1280]{1,0:T(8,128)(2,1)S(1)}, u32[]{:S(2)}) copy-start(bf16[512,1280]{1,0:T(8,128)(2,1)S(1)} %collective-permute-done.3.refs_5_) | copy-start | bytes 3932164
  55.8 33.1 %collective-permute-start.5 = (bf16[512,1280]{1,0:T(8,128)(2,1)S(1)}, bf16[512,1280]{1,0:T(8,128)(2,1)}, u32[]{:S(2)}, u32[]{:S(2)}) collective-permute-start(bf16[512,1280]{1,0:T(8,128)(2,1)S(1)} %collective-permute-done.2.refs_3_), channel_id=1, source_target_pairs={{1,2},{2,1},{5,6},{6,5},{9,10},{10,9},{13,14},{14,13},{17,18},{18,... | collective-permute-start | bytes 3932168 | tf_op jit(solution)/shard_map/ppermute | solution.py:250
  59.3 33.1 %collective-permute-start.12 = (bf16[512,1280]{1,0:T(8,128)(2,1)S(1)}, bf16[512,1280]{1,0:T(8,128)(2,1)S(1)}, u32[]{:S(2)}, u32[]{:S(2)}) collective-permute-start(bf16[512,1280]{1,0:T(8,128)(2,1)S(1)} %collective-permute-done.3.refs_5_), channel_id=1, source_target_pairs={{1,0},{2,3},{5,4},{6,7},{9,8},{10,11},{13,12},{14,15},{17,16},{18,... | collective-permute-start | bytes 3932168 | tf_op jit(solution)/shard_map/ppermute | solution.py:250
  64.2 33.8 %collective-permute-start.7 = (bf16[512,1280]{1,0:T(8,128)(2,1)}, bf16[512,1280]{1,0:T(8,128)(2,1)}, u32[]{:S(2)}, u32[]{:S(2)}) collective-permute-start(bf16[512,1280]{1,0:T(8,128)(2,1)} %fusion.2.refs_0_), channel_id=1, source_target_pairs={{0,1},{3,2},{4,5},{7,6},{8,9},{11,10},{12,13},{15,14},{16,17},{19,... | collective-permute-start | bytes 3932168 | tf_op jit(solution)/shard_map/ppermute | solution.py:250
  88.9 33.5 %collective-permute-start.6 = (bf16[512,1280]{1,0:T(8,128)(2,1)}, bf16[512,1280]{1,0:T(8,128)(2,1)}, u32[]{:S(2)}, u32[]{:S(2)}) collective-permute-start(bf16[512,1280]{1,0:T(8,128)(2,1)} %fusion.2.refs_0_), channel_id=1, source_target_pairs={{1,2},{2,1},{5,6},{6,5},{9,10},{10,9},{13,14},{14,13},{17,18},{18,... | collective-permute-start | bytes 3932168 | tf_op jit(solution)/shard_map/ppermute | solution.py:250
  93.5 34.8 %collective-permute-start.13 = (bf16[512,1280]{1,0:T(8,128)(2,1)}, bf16[512,1280]{1,0:T(8,128)(2,1)}, u32[]{:S(2)}, u32[]{:S(2)}) collective-permute-start(bf16[512,1280]{1,0:T(8,128)(2,1)} %collective-permute-done.5.refs_7_), channel_id=1, source_target_pairs={{1,0},{2,3},{5,4},{6,7},{9,8},{10,11},{13,12},{14,15},{17,16},{18,... | collective-permute-start | bytes 3932168 | tf_op jit(solution)/shard_map/ppermute | solution.py:250
  122.4 32.7 %collective-permute-start.10 = (bf16[512,1280]{1,0:T(8,128)(2,1)}, bf16[512,1280]{1,0:T(8,128)(2,1)}, u32[]{:S(2)}, u32[]{:S(2)}) collective-permute-start(bf16[512,1280]{1,0:T(8,128)(2,1)} %collective-permute-done.7.refs_0_), channel_id=1, source_target_pairs={{1,2},{2,1},{5,6},{6,5},{9,10},{10,9},{13,14},{14,13},{17,18},{18,... | collective-permute-start | bytes 3932168 | tf_op jit(solution)/shard_map/ppermute | solution.py:250
  125.9 31.7 %collective-permute-start.8 = (bf16[512,1280]{1,0:T(8,128)(2,1)}, bf16[512,1280]{1,0:T(8,128)(2,1)}, u32[]{:S(2)}, u32[]{:S(2)}) collective-permute-start(bf16[512,1280]{1,0:T(8,128)(2,1)} %collective-permute-done.6.refs_1_), channel_id=1, source_target_pairs={{1,0},{2,3},{5,4},{6,7},{9,8},{10,11},{13,12},{14,15},{17,16},{18,... | collective-permute-start | bytes 3932168 | tf_op jit(solution)/shard_map/ppermute | solution.py:250
  143.8 15.7 %collective-permute-start.14 = (bf16[2,5,512,128]{3,2,1,0:T(8,128)(2,1)S(1)}, bf16[2,5,512,128]{3,2,1,0:T(8,128)(2,1)S(1)}, u32[]{:S(2)}, u32[]{:S(2)}) collective-permute-start(bf16[2,5,512,128]{3,2,1,0:T(8,128)(2,1)S(1)} %get-tuple-element.34.refs_3_), channel_id=1, source_target_pairs={{0,24},{1,25},{2,26},{3,27}} | collective-permute-start | bytes 3932168 | tf_op jit(solution)/shard_map/ppermute | solution.py:202
  144.6 17.3 %collective-permute-start.15 = (bf16[2,5,512,128]{3,2,1,0:T(8,128)(2,1)S(1)}, bf16[2,5,512,128]{3,2,1,0:T(8,128)(2,1)}, u32[]{:S(2)}, u32[]{:S(2)}) collective-permute-start(bf16[2,5,512,128]{3,2,1,0:T(8,128)(2,1)S(1)} %get-tuple-element.34.refs_3_), channel_id=1, source_target_pairs={{0,16},{1,17},{2,18},{3,19}} | collective-permute-start | bytes 3932168 | tf_op jit(solution)/shard_map/ppermute | solution.py:202
  146.3 23.2 %collective-permute-start.16 = (bf16[2,5,512,128]{3,2,1,0:T(8,128)(2,1)S(1)}, bf16[2,5,512,128]{3,2,1,0:T(8,128)(2,1)}, u32[]{:S(2)}, u32[]{:S(2)}) collective-permute-start(bf16[2,5,512,128]{3,2,1,0:T(8,128)(2,1)S(1)} %get-tuple-element.34.refs_3_), channel_id=1, source_target_pairs={{0,8},{1,9},{2,10},{3,11}} | collective-permute-start | bytes 3932168 | tf_op jit(solution)/shard_map/ppermute | solution.py:202
  155.1 30.8 %collective-permute-start.11 = (bf16[512,1280]{1,0:T(8,128)(2,1)}, bf16[512,1280]{1,0:T(8,128)(2,1)}, u32[]{:S(2)}, u32[]{:S(2)}) collective-permute-start(bf16[512,1280]{1,0:T(8,128)(2,1)} %collective-permute-done.10.refs_3_), channel_id=1, source_target_pairs={{1,0},{2,3},{5,4},{6,7},{9,8},{10,11},{13,12},{14,15},{17,16},{18,... | collective-permute-start | bytes 3932168 | tf_op jit(solution)/shard_map/ppermute | solution.py:250
  157.7 74.8 %collective-permute-start.18 = (bf16[2,5,512,128]{3,2,1,0:T(8,128)(2,1)S(1)}, bf16[2,5,512,128]{3,2,1,0:T(8,128)(2,1)}, u32[]{:S(2)}, u32[]{:S(2)}) collective-permute-start(bf16[2,5,512,128]{3,2,1,0:T(8,128)(2,1)S(1)} %get-tuple-element.34.refs_3_), channel_id=1, source_target_pairs={{4,8},{8,12},{12,16},{16,20},{20,24},{24,28},{5,9},{9,13},{13,17},... | collective-permute-start | bytes 3932168 | tf_op jit(solution)/shard_map/ppermute | solution.py:268
  159.6 52.5 %collective-permute-start.9 = (bf16[512,1280]{1,0:T(8,128)(2,1)}, bf16[512,1280]{1,0:T(8,128)(2,1)S(1)}, u32[]{:S(2)}, u32[]{:S(2)}) collective-permute-start(bf16[512,1280]{1,0:T(8,128)(2,1)} %fusion.2.refs_0_), channel_id=1, source_target_pairs={{1,0},{2,3},{5,4},{6,7},{9,8},{10,11},{13,12},{14,15},{17,16},{18,... | collective-permute-start | bytes 3932168 | tf_op jit(solution)/shard_map/ppermute | solution.py:250
  171.0 53.9 %collective-permute-start.17 = (bf16[2,5,512,128]{3,2,1,0:T(8,128)(2,1)S(1)}, bf16[2,5,512,128]{3,2,1,0:T(8,128)(2,1)}, u32[]{:S(2)}, u32[]{:S(2)}) collective-permute-start(bf16[2,5,512,128]{3,2,1,0:T(8,128)(2,1)S(1)} %select_select_fusion.refs_1_), channel_id=1, source_target_pairs={{0,4},{8,12},{16,20},{24,28},{1,5},{9,13},{17,21},{25,29},{2,6},{1... | collective-permute-start | bytes 3932168 | tf_op jit(solution)/shard_map/ppermute | solution.py:203
  223.2 9.3 %collective-permute-start.19 = (bf16[2,5,512,128]{3,2,1,0:T(8,128)(2,1)}, bf16[2,5,512,128]{3,2,1,0:T(8,128)(2,1)}, u32[]{:S(2)}, u32[]{:S(2)}) collective-permute-start(bf16[2,5,512,128]{3,2,1,0:T(8,128)(2,1)} %get-tuple-element.35.refs_4_), channel_id=1, source_target_pairs={{0,4},{1,5},{2,6},{3,7}} | collective-permute-start | bytes 3932168 | tf_op jit(solution)/shard_map/ppermute | solution.py:271
  (7 other events, 28.4 us)

commit v5 on v4

--- a/solution.py
+++ b/solution.py
@@ -35,10 +35,9 @@
         kv_out[1, h] = columns(2, h).astype(BF16)
 
 
-def project_body(pairs, extra, has_acc, final, info, *refs):
+def project_body(layout, extra, has_acc, final, info, *refs):
     refs = list(refs)[extra:]
-    count = len(pairs)
-    groups = [[refs.pop(0) for _ in range(n)] for n in pairs]
+    groups = [[[refs.pop(0) for _ in range(n)] for n in variants] for variants in layout]
     weights = [refs.pop(0) for _ in range(3)]
     gains = [refs.pop(0) for _ in range(2)] if final else None
     start = refs.pop(0) if has_acc else None
@@ -49,17 +48,21 @@
     @pl.when(step == 0)
     def _():
         for i, group in enumerate(groups):
-            for j, source in enumerate(group):
+            for j, pieces in enumerate(group):
 
                 @pl.when((info[0] == j) | (len(group) == 1))
-                def _(i=i, source=source):
-                    pltpu.make_async_copy(source, xbuf.at[i], sem.at[i]).start()
-
-    for i in range(count):
+                def _(i=i, pieces=pieces):
+                    row = 0
+                    for piece in pieces:
+                        span = pl.ds(row, piece.shape[0])
+                        pltpu.make_async_copy(piece, xbuf.at[i, span], sem.at[i]).start()
+                        row += piece.shape[0]
+
+    for i in range(len(groups)):
 
         @pl.when(step == i)
         def _(i=i):
-            pltpu.make_async_copy(groups[i][0], xbuf.at[i], sem.at[i]).wait()
+            pltpu.make_async_copy(xbuf.at[i], xbuf.at[i], sem.at[i]).wait()
             weight = jnp.concatenate([w[...] for w in weights], axis=1)
             part = jnp.dot(xbuf[i], weight, preferred_element_type=F32)
             if i == 0:
@@ -69,21 +72,23 @@
 
     if final:
 
-        @pl.when(step == count - 1)
+        @pl.when(step == len(groups) - 1)
         def _():
             store_heads(acc, gains[0][...], gains[1][...], *outs)
 
 
 def project(sources, info, weights, gains=None, acc=None, after=(), flops=1):
-    pairs = [len(s) for s in sources]
-    count = len(pairs)
-    rows, chans = sources[0][0].shape
+    layout = [[len(variant) for variant in source] for source in sources]
+    count = len(sources)
+    rows = sum(piece.shape[0] for piece in sources[0][0])
+    chans = sources[0][0][0].shape[1]
     width = weights[0].shape[1]
     heads = width // DH
     final = gains is not None
     a_spec = pl.BlockSpec((rows, 3 * width), lambda k, info: (0, 0))
-    in_specs = [ANY] * (len(after) + sum(pairs)) + [pl.BlockSpec((chans, width), lambda k, info: (info[1 + k], 0))] * 3
-    args = list(after) + [x for s in sources for x in s] + list(weights)
+    args = list(after) + [piece for source in sources for variant in source for piece in variant]
+    in_specs = [ANY] * len(args) + [pl.BlockSpec((chans, width), lambda k, info: (info[1 + k], 0))] * 3
+    args += list(weights)
     scratch = [pltpu.VMEM((count, rows, chans), BF16), pltpu.SemaphoreType.DMA((count,))]
     raw = jax.ShapeDtypeStruct((rows, 3 * width), F32)
     if final:
@@ -104,7 +109,7 @@
         in_specs.append(a_spec)
         args.append(acc)
     return pl.pallas_call(
-        functools.partial(project_body, pairs, len(after), acc is not None, final),
+        functools.partial(project_body, layout, len(after), acc is not None, final),
         grid_spec=pltpu.PrefetchScalarGridSpec(
             num_scalar_prefetch=1,
             grid=(count,),
@@ -225,49 +230,70 @@
     pair, second, third = z ^ 1, jnp.where(outer, near, far), jnp.where(outer, far, near)
     info = jnp.stack([side, z, pair, second, third])
     info_raw, info_end = jnp.stack([side, z, second, third]), jnp.stack([side, pair])
-    first, last = frames[0], frames[1]
+    half = frames.shape[1] // 2
     ups = [(i, i + 1) for i in range(count - 1)]
+    downs = [(j, i) for i, j in ups]
     start = pos == 0
-    following = lax.ppermute(first, "tm", [(j, i) for i, j in ups])
-    mixed1 = mix(
-        jnp.where(start, jnp.zeros_like(first), first),
-        jnp.where(start, first, last),
-        jnp.where(start, last, following),
+    hold = lax.optimization_barrier
+    weights = (w_query, w_key, w_value)
+    gains = (q_gain, k_gain)
+
+    def send(x, pairs):
+        return lax.ppermute(x, "head", pairs)
+
+    following, mixed1 = [], []
+    held = frames
+    for part in range(2):
+        following.append(lax.ppermute(held[0, part * half : (part + 1) * half], "tm", downs))
+        held, following[part] = hold((frames, following[part]))
+    held = frames
+    for part in range(2):
+        rows = slice(part * half, (part + 1) * half)
+        first, last = held[0, rows], held[1, rows]
+        mixed1.append(
+            mix(
+                jnp.where(start, jnp.zeros_like(first), first),
+                jnp.where(start, first, last),
+                jnp.where(start, last, following[part]),
+                taps,
+            )
+        )
+        held, mixed1[part] = hold((held, mixed1[part]))
+    inward1, middle1, first1, cross1, second1, third1 = ([None, None] for _ in range(6))
+    for p in range(2):
+        level = send(mixed1[p], INWARD), send(mixed1[p], MIDDLE), send(mixed1[p], OUTWARD)
+        inward1[p], middle1[p], first1[p] = hold(level)
+    _, later = hold((mixed1[1], frames))
+    preceding = lax.ppermute(later[1], "tm", ups)
+    after_first = jnp.concatenate(following, axis=0)
+    mixed2 = mix(
+        jnp.where(start, frames[0], preceding),
+        jnp.where(start, frames[1], frames[0]),
+        jnp.where(start, after_first, frames[1]),
         taps,
     )
-    _, later = lax.optimization_barrier((mixed1, frames))
-    preceding = lax.ppermute(later[1], "tm", ups)
-    mixed2 = mix(
-        jnp.where(start, first, preceding),
-        jnp.where(start, last, first),
-        jnp.where(start, following, last),
-        taps,
-    )
-    weights = (w_query, w_key, w_value)
-    gains = (q_gain, k_gain)
-
-    def send(x, pairs):
-        return lax.ppermute(x, "head", pairs)
-
-    inward1, middle1, first1 = send(mixed1, INWARD), send(mixed1, MIDDLE), send(mixed1, OUTWARD)
-    inward1, middle1, first1 = lax.optimization_barrier((inward1, middle1, first1))
-    inward2, cross1, second1 = send(mixed2, INWARD), send(inward1, MIDDLE), send(middle1, OUTWARD)
-    later2, cross1 = lax.optimization_barrier((mixed2, cross1))
+    inward2 = send(mixed2, INWARD)
+    for p in range(2):
+        cross1[p], second1[p] = hold((send(inward1[p], MIDDLE), send(middle1[p], OUTWARD)))
+        third1[p] = send(cross1[p], OUTWARD)
+    later2, _ = hold((mixed2, cross1[0]))
     middle2 = send(later2, MIDDLE)
-    cross1, second1 = lax.optimization_barrier((cross1, second1))
-    third1 = send(cross1, OUTWARD)
-    middle2, inward2 = lax.optimization_barrier((middle2, inward2))
+    later2, _ = hold((mixed2, cross1[1]))
+    first2 = [send(later2[:half], OUTWARD)]
+    middle2, inward2 = hold((middle2, inward2))
     cross2, second2 = send(inward2, MIDDLE), send(middle2, OUTWARD)
+    later2, second2 = hold((mixed2, second2))
+    first2.append(send(later2[half:], OUTWARD))
+
+    sources1 = [[mixed1], [inward1, first1], [middle1, second1], [cross1, third1]]
+    q1, kv1 = project(sources1, info, weights, gains, after=(inward2, middle2, first2[0]), flops=10**10)
+    kv1, cross2 = hold((kv1, cross2))
     third2 = send(cross2, OUTWARD)
-    later2, second2 = lax.optimization_barrier((mixed2, second2))
-    first2 = send(later2, OUTWARD)
-
-    sources1 = [(mixed1,), (inward1, first1), (middle1, second1), (cross1, third1)]
-    q1, kv1 = project(sources1, info, weights, gains, after=(inward2, middle2), flops=10**10)
     anchor = broadcast_first(kv1, "tm")
     shift1 = lax.ppermute(kv1, "tm", [(i, i + 1) for i in range(1, count - 1)])
-    raw2 = project([(mixed2,), (middle2, second2), (cross2, third2)], info_raw, weights, flops=10**10)
-    q2, kv2 = project([(inward2, first2)], info_end, weights, gains, raw2, flops=10**10)
+    sources2 = [[[mixed2]], [[middle2], [second2]], [[cross2], [third2]]]
+    raw2 = project(sources2, info_raw, weights, flops=10**10)
+    q2, kv2 = project([[[inward2], first2]], info_end, weights, gains, raw2, flops=10**10)
     shift2 = lax.ppermute(kv2, "tm", [(0, 1)])
     late = jnp.where(start, 0, 1)
     odd = pos % 2

time: 242 us -> 266 us (1.099)
  starting transfers between devices: 47.8 us -> 69.8 us
  local copies, waits for them, and re-layouts: 3.62 us -> 18.5 us
  waiting for transfers between devices: 125 us -> 111 us
    ppermute x12 -> x19, waiting for transfers between devices: 103 us -> 70.7 us  [send(): return lax.ppermute(x, 'head', pairs)]
    ppermute x3, waiting for transfers between devices: 7.56 us -> 32.2 us  [broadcast_first(): held = jnp.where(mine == to, lax.ppermute(x, axis, [(0, to)]), held)]
    ppermute x12 -> x19, starting transfers between devices: 32.1 us -> 48.5 us  [send(): return lax.ppermute(x, 'head', pairs)]
    unnamed x22 -> x48, local copies, waits for them, and re-layouts: 1.99 us -> 13.3 us
    ppermute x1 -> x2, waiting for transfers between devices: 15 us -> 8.08 us  [per_device(): lax.ppermute(held[0, part * half:(part + 1) * half], 'tm', downs)]
    ppermute x1 -> x2, starting transfers between devices: 1.92 us -> 5.83 us  [per_device(): lax.ppermute(held[0, part * half:(part + 1) * half], 'tm', downs)]
    convert_element_type x2 -> x3, other arithmetic: 5.13 us -> 5.84 us  [mix(): (centre + taps[0] * before + taps[1] * centre + taps[2] * after).astype(B...]
  transfers between devices with their start and end apart: 20 -> 28, of which waited for: 11 -> 12; matrix products, arithmetic and copies ran while one was open for 2% -> 4% of each run, Pallas kernels for 20% -> 19%
where the time goes in v5:
time: 266 us; the launch traced here: 264 us
  waiting for transfers between devices  111 us (42%)
  starting transfers between devices  69.8 us (26%)
  Pallas kernels  56.6 us (21%)
  local copies, waits for them, and re-layouts  18.5 us (7%)
  other arithmetic  7.62 us (3%)
    ppermute x19, waiting for transfers between devices, send(): return lax.ppermute(x, 'head', pairs)  70.7 us
    ppermute x19, starting transfers between devices, send(): return lax.ppermute(x, 'head', pairs)  48.5 us
    pallas_call x3, Pallas kernels, project(): pl.pallas_call(functools.partial(project_body, layout, len(after), acc is...  41.6 us
    ppermute x3, waiting for transfers between devices, broadcast_first(): held = jnp.where(mine == to, lax.ppermute(x, axis, [(0, to)]), held)  32.2 us
    pallas_call x2, Pallas kernels, attend(): pl.pallas_call(functools.partial(attend_body, 128, (len(anchors), len(opt...  15 us
    unnamed x48, local copies, waits for them, and re-layouts  13.3 us
    ppermute x2, waiting for transfers between devices, per_device(): lax.ppermute(held[0, part * half:(part + 1) * half], 'tm', downs)  8.08 us
    convert_element_type x3, other arithmetic, mix(): (centre + taps[0] * before + taps[1] * centre + taps[2] * after).astype(B...  5.84 us
  transfers between devices with their start and end apart: 28, of which 12 were waited for; matrix products, arithmetic and copies ran while one was open for 4% of the time, Pallas kernels for 19%

profile of v5, /device:TPU:10, one launch (start us, length us, event | category | flops | bytes accessed | tf_op | source)
XLA Modules:
  0.0 264.2 jit_solution(15984075854021605295)
XLA Ops:
  3.2 8.1 %collective-permute-done = bf16[256,1280]{1,0:T(8,128)(2,1)} collective-permute-done((bf16[256,1280]{1,0:T(8,128)(2,1)S(1)}, bf16[256,1280]{1,0:T(8,128)(2,1)}, u32[]{:S(2)}, u32[]{:S(2)}) %collective-permute-start) | collective-permute-done | bytes 655392 | tf_op jit(solution)/shard_map/ppermute | solution.py:247
  13.3 3.9 %collective-permute-start.1 = (bf16[256,1280]{1,0:T(8,128)(2,1)}, bf16[256,1280]{1,0:T(8,128)(2,1)}, u32[]{:S(2)}, u32[]{:S(2)}) collective-permute-start(bf16[256,1280]{1,0:T(8,128)(2,1)} %slice_bitcast_fusion.1), channel_id=1, source_target_pairs={{4,0},{8,4},{12,8},{16,12},{20,16},{24,20},{28,24},{5,1},{9,5},{13... | collective-permute-start | bytes 1966088 | tf_op jit(solution)/shard_map/ppermute | solution.py:247
  21.2 3.5 %collective-permute-start.4 = (bf16[256,1280]{1,0:T(8,128)(2,1)S(1)}, bf16[256,1280]{1,0:T(8,128)(2,1)S(1)}, u32[]{:S(2)}, u32[]{:S(2)}) collective-permute-start(bf16[256,1280]{1,0:T(8,128)(2,1)S(1)} %fusion.5.refs_3_), channel_id=1, source_target_pairs={{1,2},{2,1},{5,6},{6,5},{9,10},{10,9},{13,14},{14,13},{17,18},{18,... | collective-permute-start | bytes 1966088 | tf_op jit(solution)/shard_map/ppermute | solution.py:242
  28.3 4.5 %collective-permute-start.2 = (bf16[512,1280]{1,0:T(8,128)(2,1)S(1)}, bf16[512,1280]{1,0:T(8,128)(2,1)S(1)}, u32[]{:S(2)}, u32[]{:S(2)}) collective-permute-start(bf16[512,1280]{1,0:T(8,128)(2,1)S(1)} %slice_bitcast_fusion), channel_id=1, source_target_pairs={{0,4},{4,8},{8,12},{12,16},{16,20},{20,24},{24,28},{1,5},{5,9},{9,... | collective-permute-start | bytes 3932168 | tf_op jit(solution)/shard_map/ppermute | solution.py:267
  32.7 6.4 %collective-permute-done.3.refs_5_ = bf16[256,1280]{1,0:T(8,128)(2,1)S(1)} collective-permute-done((bf16[256,1280]{1,0:T(8,128)(2,1)S(1)}, bf16[256,1280]{1,0:T(8,128)(2,1)S(1)}, u32[]{:S(2)}, u32[]{:S(2)}) %collective-permute-start.3) | collective-permute-done | bytes 655392 | tf_op jit(solution)/shard_map/ppermute | solution.py:242
  41.9 3.5 %collective-permute-start.6 = (bf16[256,1280]{1,0:T(8,128)(2,1)S(1)}, bf16[256,1280]{1,0:T(8,128)(2,1)}, u32[]{:S(2)}, u32[]{:S(2)}) collective-permute-start(bf16[256,1280]{1,0:T(8,128)(2,1)S(1)} %collective-permute-done.3.refs_5_), channel_id=1, source_target_pairs={{1,2},{2,1},{5,6},{6,5},{9,10},{10,9},{13,14},{14,13},{17,18},{18,... | collective-permute-start | bytes 1966088 | tf_op jit(solution)/shard_map/ppermute | solution.py:242
  46.2 2.5 collective-permute-start.7
  50.9 3.5 %collective-permute-start.11 = (bf16[256,1280]{1,0:T(8,128)(2,1)S(1)}, bf16[256,1280]{1,0:T(8,128)(2,1)S(1)}, u32[]{:S(2)}, u32[]{:S(2)}) collective-permute-start(bf16[256,1280]{1,0:T(8,128)(2,1)S(1)} %fusion.8.refs_4_), channel_id=1, source_target_pairs={{1,2},{2,1},{5,6},{6,5},{9,10},{10,9},{13,14},{14,13},{17,18},{18,... | collective-permute-start | bytes 1966088 | tf_op jit(solution)/shard_map/ppermute | solution.py:242
  54.4 7.2 %collective-permute-done.6.refs_13_ = bf16[256,1280]{1,0:T(8,128)(2,1)} collective-permute-done((bf16[256,1280]{1,0:T(8,128)(2,1)S(1)}, bf16[256,1280]{1,0:T(8,128)(2,1)}, u32[]{:S(2)}, u32[]{:S(2)}) %collective-permute-start.6) | collective-permute-done | bytes 655392 | tf_op jit(solution)/shard_map/ppermute | solution.py:242
  67.2 3.6 %collective-permute-start.8 = (bf16[512,1280]{1,0:T(8,128)(2,1)S(1)}, bf16[512,1280]{1,0:T(8,128)(2,1)}, u32[]{:S(2)}, u32[]{:S(2)}) collective-permute-start(bf16[512,1280]{1,0:T(8,128)(2,1)S(1)} %fusion.2.refs_0_), channel_id=1, source_target_pairs={{1,2},{2,1},{5,6},{6,5},{9,10},{10,9},{13,14},{14,13},{17,18},{18,... | collective-permute-start | bytes 3932168 | tf_op jit(solution)/shard_map/ppermute | solution.py:242
  72.1 3.4 %collective-permute-done.11.refs_10_ = bf16[256,1280]{1,0:T(8,128)(2,1)S(1)} collective-permute-done((bf16[256,1280]{1,0:T(8,128)(2,1)S(1)}, bf16[256,1280]{1,0:T(8,128)(2,1)S(1)}, u32[]{:S(2)}, u32[]{:S(2)}) %collective-permute-start.11) | collective-permute-done | bytes 655392 | tf_op jit(solution)/shard_map/ppermute | solution.py:242
  77.4 3.5 %collective-permute-start.13 = (bf16[256,1280]{1,0:T(8,128)(2,1)S(1)}, bf16[256,1280]{1,0:T(8,128)(2,1)}, u32[]{:S(2)}, u32[]{:S(2)}) collective-permute-start(bf16[256,1280]{1,0:T(8,128)(2,1)S(1)} %collective-permute-done.10.refs_6_), channel_id=1, source_target_pairs={{1,2},{2,1},{5,6},{6,5},{9,10},{10,9},{13,14},{14,13},{17,18},{18,... | collective-permute-start | bytes 1966088 | tf_op jit(solution)/shard_map/ppermute | solution.py:242
  81.7 3.2 %collective-permute-start.14 = (bf16[256,1280]{1,0:T(8,128)(2,1)S(1)}, bf16[256,1280]{1,0:T(8,128)(2,1)}, u32[]{:S(2)}, u32[]{:S(2)}) collective-permute-start(bf16[256,1280]{1,0:T(8,128)(2,1)S(1)} %collective-permute-done.11.refs_10_), channel_id=1, source_target_pairs={{1,0},{2,3},{5,4},{6,7},{9,8},{10,11},{13,12},{14,15},{17,16},{18,... | collective-permute-start | bytes 1966088 | tf_op jit(solution)/shard_map/ppermute | solution.py:242
  87.1 29.3 %collective-permute-done.13.refs_14_ = bf16[256,1280]{1,0:T(8,128)(2,1)} collective-permute-done((bf16[256,1280]{1,0:T(8,128)(2,1)S(1)}, bf16[256,1280]{1,0:T(8,128)(2,1)}, u32[]{:S(2)}, u32[]{:S(2)}) %collective-permute-start.13) | collective-permute-done | bytes 655392 | tf_op jit(solution)/shard_map/ppermute | solution.py:242
  120.8 3.5 %collective-permute-start.20 = (bf16[512,1280]{1,0:T(8,128)(2,1)}, bf16[512,1280]{1,0:T(8,128)(2,1)}, u32[]{:S(2)}, u32[]{:S(2)}) collective-permute-start(bf16[512,1280]{1,0:T(8,128)(2,1)} %collective-permute-done.9.refs_0_), channel_id=1, source_target_pairs={{1,2},{2,1},{5,6},{6,5},{9,10},{10,9},{13,14},{14,13},{17,18},{18,... | collective-permute-start | bytes 3932168 | tf_op jit(solution)/shard_map/ppermute | solution.py:242
  126.8 7.2 %collective-permute-done.15.refs_2_.refs_1_ = bf16[256,1280]{1,0:T(8,128)(2,1)S(1)} collective-permute-done((bf16[256,1280]{1,0:T(8,128)(2,1)}, bf16[256,1280]{1,0:T(8,128)(2,1)S(1)}, u32[]{:S(2)}, u32[]{:S(2)}) %collective-permute-start.15) | collective-permute-done | bytes 655392 | tf_op jit(solution)/shard_map/ppermute | solution.py:242
  134.8 13.2 %collective-permute-done.19.refs_16_ = bf16[256,1280]{1,0:T(8,128)(2,1)} collective-permute-done((bf16[256,1280]{1,0:T(8,128)(2,1)}, bf16[256,1280]{1,0:T(8,128)(2,1)}, u32[]{:S(2)}, u32[]{:S(2)}) %collective-permute-start.19) | collective-permute-done | bytes 655392 | tf_op jit(solution)/shard_map/ppermute | solution.py:242
  154.6 17.7 %project_end.2 = (bf16[5,512,128]{2,1,0:T(8,128)(2,1)S(1)}, bf16[2,5,512,128]{3,2,1,0:T(8,128)(2,1)}) custom-call(s32[5]{0:T(128)S(1)} %stack.65.info, bf16[512,1280]{1,0:T(8,128)(2,1)} %collective-permute-done.9.refs_0_, bf16[512,1280]{1,0:T(8,128)(2,1)} %collective-permute-done.8.refs_1_, bf16[256,1280]{1,0:T(8,128)(2,1)S(1)} %copy-done.12, ...), custom_call_target="tpu_custom_call" | custom-call | flops 10000000000 | bytes 1 | tf_op jit(solution)/shard_map/project_end/pallas_call | solution.py:111
  177.2 5.2 %collective-permute-start.21 = (bf16[512,1280]{1,0:T(8,128)(2,1)}, bf16[512,1280]{1,0:T(8,128)(2,1)}, u32[]{:S(2)}, u32[]{:S(2)}) collective-permute-start(bf16[512,1280]{1,0:T(8,128)(2,1)} %collective-permute-done.20.refs_3_), channel_id=1, source_target_pairs={{1,0},{2,3},{5,4},{6,7},{9,8},{10,11},{13,12},{14,15},{17,16},{18,... | collective-permute-start | bytes 3932168 | tf_op jit(solution)/shard_map/ppermute | solution.py:242
  186.1 32.2 %collective-permute-done.24 = bf16[2,5,512,128]{3,2,1,0:T(8,128)(2,1)} collective-permute-done((bf16[2,5,512,128]{3,2,1,0:T(8,128)(2,1)}, bf16[2,5,512,128]{3,2,1,0:T(8,128)(2,1)}, u32[]{:S(2)}, u32[]{:S(2)}) %collective-permute-start.24) | collective-permute-done | bytes 1310752 | tf_op jit(solution)/shard_map/ppermute | solution.py:207
  222.4 13.8 %project_raw.1.refs_8_ = f32[512,1920]{1,0:T(8,128)} custom-call(s32[4]{0:T(128)S(1)} %pad_add_fusion.2.info, bf16[512,1280]{1,0:T(8,128)(2,1)S(1)} %copy-done.2, bf16[512,1280]{1,0:T(8,128)(2,1)} %collective-permute-done.8.refs_1_, bf16[512,1280]{1,0:T(8,128)(2,1)} %collective-permute-done.16.refs_2_, bf16[512,1280]{1,0:T(8,128)(2,1)} %collective-permute-done.20.refs_3_, ...), custom_call_target="tpu_custom_call" | custom-call | flops 10000000000 | bytes 1 | tf_op jit(solution)/shard_map/project_raw/pallas_call | solution.py:111
  236.2 10.1 %project_end.3 = (bf16[5,512,128]{2,1,0:T(8,128)(2,1)S(1)}, bf16[2,5,512,128]{3,2,1,0:T(8,128)(2,1)}) custom-call(s32[2]{0:T(128)S(1)} %pad_add_fusion.1.info, bf16[512,1280]{1,0:T(8,128)(2,1)} %collective-permute-done.9.refs_0_, bf16[256,1280]{1,0:T(8,128)(2,1)S(1)} %copy-done.13, bf16[256,1280]{1,0:T(8,128)(2,1)S(1)} %collective-permute-done.17.refs_2_, ...), custom_call_target="tpu_custom_call" | custom-call | flops 10000000000 | bytes 1 | tf_op jit(solution)/shard_map/project_end/pallas_call | solution.py:111
  249.0 7.5 %attend.2.refs_6_ = bf16[2,512,640]{2,1,0:T(8,128)(2,1)} custom-call(s32[3]{0:T(128)S(1)} %get-tuple-element.67.info, bf16[5,512,128]{2,1,0:T(8,128)(2,1)S(1)} %get-tuple-element.62.refs_0_, bf16[2,5,512,128]{3,2,1,0:T(8,128)(2,1)S(1)} %select_select_fusion.refs_1_, bf16[2,5,512,128]{3,2,1,0:T(8,128)(2,1)} %collective-permute-done.25.refs_2_, ...), custom_call_target="tpu_custom_call" | custom-call | flops 1342177280 | bytes 3932160 | tf_op jit(solution)/shard_map/attend/pallas_call | solution.py:178
  256.5 7.5 %attend.3 = bf16[2,512,640]{2,1,0:T(8,128)(2,1)} custom-call(s32[3]{0:T(128)S(1)} %get-tuple-element.66.info, bf16[5,512,128]{2,1,0:T(8,128)(2,1)S(1)} %copy-done.4, bf16[2,5,512,128]{3,2,1,0:T(8,128)(2,1)S(1)} %select_select_fusion.refs_1_, bf16[2,5,512,128]{3,2,1,0:T(8,128)(2,1)} %collective-permute-done.25.refs_2_, ...), custom_call_target="tpu_custom_call", output_to_operand_aliasing={{}: (7, {})} | custom-call | flops 1342177280 | bytes 3932160 | tf_op jit(solution)/shard_map/attend/pallas_call | solution.py:178
  (101 shorter events, 59.6 us)
Async XLA Ops:
  13.3 13.3 %collective-permute-start.1 = (bf16[256,1280]{1,0:T(8,128)(2,1)}, bf16[256,1280]{1,0:T(8,128)(2,1)}, u32[]{:S(2)}, u32[]{:S(2)}) collective-permute-start(bf16[256,1280]{1,0:T(8,128)(2,1)} %slice_bitcast_fusion.1), channel_id=1, source_target_pairs={{4,0},{8,4},{12,8},{16,12},{20,16},{24,20},{28,24},{5,1},{9,5},{13... | collective-permute-start | bytes 1966088 | tf_op jit(solution)/shard_map/ppermute | solution.py:247
  19.9 19.3 %collective-permute-start.3 = (bf16[256,1280]{1,0:T(8,128)(2,1)S(1)}, bf16[256,1280]{1,0:T(8,128)(2,1)S(1)}, u32[]{:S(2)}, u32[]{:S(2)}) collective-permute-start(bf16[256,1280]{1,0:T(8,128)(2,1)S(1)} %fusion.5.refs_3_), channel_id=1, source_target_pairs={{0,1},{3,2},{4,5},{7,6},{8,9},{11,10},{12,13},{15,14},{16,17},{19,... | collective-permute-start | bytes 1966088 | tf_op jit(solution)/shard_map/ppermute | solution.py:242
  21.2 19.3 %collective-permute-start.4 = (bf16[256,1280]{1,0:T(8,128)(2,1)S(1)}, bf16[256,1280]{1,0:T(8,128)(2,1)S(1)}, u32[]{:S(2)}, u32[]{:S(2)}) collective-permute-start(bf16[256,1280]{1,0:T(8,128)(2,1)S(1)} %fusion.5.refs_3_), channel_id=1, source_target_pairs={{1,2},{2,1},{5,6},{6,5},{9,10},{10,9},{13,14},{14,13},{17,18},{18,... | collective-permute-start | bytes 1966088 | tf_op jit(solution)/shard_map/ppermute | solution.py:242
  24.7 16.4 %collective-permute-start.5 = (bf16[256,1280]{1,0:T(8,128)(2,1)S(1)}, bf16[256,1280]{1,0:T(8,128)(2,1)S(1)}, u32[]{:S(2)}, u32[]{:S(2)}) collective-permute-start(bf16[256,1280]{1,0:T(8,128)(2,1)S(1)} %fusion.5.refs_3_), channel_id=1, source_target_pairs={{1,0},{2,3},{5,4},{6,7},{9,8},{10,11},{13,12},{14,15},{17,16},{18,... | collective-permute-start | bytes 1966088 | tf_op jit(solution)/shard_map/ppermute | solution.py:242
  28.3 36.5 %collective-permute-start.2 = (bf16[512,1280]{1,0:T(8,128)(2,1)S(1)}, bf16[512,1280]{1,0:T(8,128)(2,1)S(1)}, u32[]{:S(2)}, u32[]{:S(2)}) collective-permute-start(bf16[512,1280]{1,0:T(8,128)(2,1)S(1)} %slice_bitcast_fusion), channel_id=1, source_target_pairs={{0,4},{4,8},{8,12},{12,16},{16,20},{20,24},{24,28},{1,5},{5,9},{9,... | collective-permute-start | bytes 3932168 | tf_op jit(solution)/shard_map/ppermute | solution.py:267
  41.9 19.6 %collective-permute-start.6 = (bf16[256,1280]{1,0:T(8,128)(2,1)S(1)}, bf16[256,1280]{1,0:T(8,128)(2,1)}, u32[]{:S(2)}, u32[]{:S(2)}) collective-permute-start(bf16[256,1280]{1,0:T(8,128)(2,1)S(1)} %collective-permute-done.3.refs_5_), channel_id=1, source_target_pairs={{1,2},{2,1},{5,6},{6,5},{9,10},{10,9},{13,14},{14,13},{17,18},{18,... | collective-permute-start | bytes 1966088 | tf_op jit(solution)/shard_map/ppermute | solution.py:242
  46.2 17.6 %collective-permute-start.7 = (bf16[256,1280]{1,0:T(8,128)(2,1)S(1)}, bf16[256,1280]{1,0:T(8,128)(2,1)S(1)}, u32[]{:S(2)}, u32[]{:S(2)}) collective-permute-start(bf16[256,1280]{1,0:T(8,128)(2,1)S(1)} %collective-permute-done.4.refs_9_), channel_id=1, source_target_pairs={{1,0},{2,3},{5,4},{6,7},{9,8},{10,11},{13,12},{14,15},{17,16},{18,... | collective-permute-start | bytes 1966088 | tf_op jit(solution)/shard_map/ppermute | solution.py:242
  49.6 22.6 %collective-permute-start.10 = (bf16[256,1280]{1,0:T(8,128)(2,1)S(1)}, bf16[256,1280]{1,0:T(8,128)(2,1)S(1)}, u32[]{:S(2)}, u32[]{:S(2)}) collective-permute-start(bf16[256,1280]{1,0:T(8,128)(2,1)S(1)} %fusion.8.refs_4_), channel_id=1, source_target_pairs={{0,1},{3,2},{4,5},{7,6},{8,9},{11,10},{12,13},{15,14},{16,17},{19,... | collective-permute-start | bytes 1966088 | tf_op jit(solution)/shard_map/ppermute | solution.py:242
  50.9 24.6 %collective-permute-start.11 = (bf16[256,1280]{1,0:T(8,128)(2,1)S(1)}, bf16[256,1280]{1,0:T(8,128)(2,1)S(1)}, u32[]{:S(2)}, u32[]{:S(2)}) collective-permute-start(bf16[256,1280]{1,0:T(8,128)(2,1)S(1)} %fusion.8.refs_4_), channel_id=1, source_target_pairs={{1,2},{2,1},{5,6},{6,5},{9,10},{10,9},{13,14},{14,13},{17,18},{18,... | collective-permute-start | bytes 1966088 | tf_op jit(solution)/shard_map/ppermute | solution.py:242
  61.5 15.0 %collective-permute-start.12 = (bf16[256,1280]{1,0:T(8,128)(2,1)S(1)}, bf16[256,1280]{1,0:T(8,128)(2,1)S(1)}, u32[]{:S(2)}, u32[]{:S(2)}) collective-permute-start(bf16[256,1280]{1,0:T(8,128)(2,1)S(1)} %fusion.8.refs_4_), channel_id=1, source_target_pairs={{1,0},{2,3},{5,4},{6,7},{9,8},{10,11},{13,12},{14,15},{17,16},{18,... | collective-permute-start | bytes 1966088 | tf_op jit(solution)/shard_map/ppermute | solution.py:242
  67.2 53.6 %collective-permute-start.8 = (bf16[512,1280]{1,0:T(8,128)(2,1)S(1)}, bf16[512,1280]{1,0:T(8,128)(2,1)}, u32[]{:S(2)}, u32[]{:S(2)}) collective-permute-start(bf16[512,1280]{1,0:T(8,128)(2,1)S(1)} %fusion.2.refs_0_), channel_id=1, source_target_pairs={{1,2},{2,1},{5,6},{6,5},{9,10},{10,9},{13,14},{14,13},{17,18},{18,... | collective-permute-start | bytes 3932168 | tf_op jit(solution)/shard_map/ppermute | solution.py:242
  70.8 49.9 %collective-permute-start.9 = (bf16[512,1280]{1,0:T(8,128)(2,1)S(1)}, bf16[512,1280]{1,0:T(8,128)(2,1)}, u32[]{:S(2)}, u32[]{:S(2)}) collective-permute-start(bf16[512,1280]{1,0:T(8,128)(2,1)S(1)} %fusion.2.refs_0_), channel_id=1, source_target_pairs={{0,1},{3,2},{4,5},{7,6},{8,9},{11,10},{12,13},{15,14},{16,17},{19,... | collective-permute-start | bytes 3932168 | tf_op jit(solution)/shard_map/ppermute | solution.py:242
  77.4 39.0 %collective-permute-start.13 = (bf16[256,1280]{1,0:T(8,128)(2,1)S(1)}, bf16[256,1280]{1,0:T(8,128)(2,1)}, u32[]{:S(2)}, u32[]{:S(2)}) collective-permute-start(bf16[256,1280]{1,0:T(8,128)(2,1)S(1)} %collective-permute-done.10.refs_6_), channel_id=1, source_target_pairs={{1,2},{2,1},{5,6},{6,5},{9,10},{10,9},{13,14},{14,13},{17,18},{18,... | collective-permute-start | bytes 1966088 | tf_op jit(solution)/shard_map/ppermute | solution.py:242
  81.7 34.7 %collective-permute-start.14 = (bf16[256,1280]{1,0:T(8,128)(2,1)S(1)}, bf16[256,1280]{1,0:T(8,128)(2,1)}, u32[]{:S(2)}, u32[]{:S(2)}) collective-permute-start(bf16[256,1280]{1,0:T(8,128)(2,1)S(1)} %collective-permute-done.11.refs_10_), channel_id=1, source_target_pairs={{1,0},{2,3},{5,4},{6,7},{9,8},{10,11},{13,12},{14,15},{17,16},{18,... | collective-permute-start | bytes 1966088 | tf_op jit(solution)/shard_map/ppermute | solution.py:242
  84.9 41.9 %collective-permute-start.18 = (bf16[256,1280]{1,0:T(8,128)(2,1)}, bf16[256,1280]{1,0:T(8,128)(2,1)}, u32[]{:S(2)}, u32[]{:S(2)}) collective-permute-start(bf16[256,1280]{1,0:T(8,128)(2,1)} %collective-permute-done.6.refs_13_), channel_id=1, source_target_pairs={{1,0},{2,3},{5,4},{6,7},{9,8},{10,11},{13,12},{14,15},{17,16},{18,... | collective-permute-start | bytes 1966088 | tf_op jit(solution)/shard_map/ppermute | solution.py:242
  117.3 16.8 %collective-permute-start.15 = (bf16[256,1280]{1,0:T(8,128)(2,1)}, bf16[256,1280]{1,0:T(8,128)(2,1)S(1)}, u32[]{:S(2)}, u32[]{:S(2)}) collective-permute-start(bf16[256,1280]{1,0:T(8,128)(2,1)} %slice.59), channel_id=1, source_target_pairs={{1,0},{2,3},{5,4},{6,7},{9,8},{10,11},{13,12},{14,15},{17,16},{18,... | collective-permute-start | bytes 1966088 | tf_op jit(solution)/shard_map/ppermute | solution.py:242
  118.6 29.5 %collective-permute-start.19 = (bf16[256,1280]{1,0:T(8,128)(2,1)}, bf16[256,1280]{1,0:T(8,128)(2,1)}, u32[]{:S(2)}, u32[]{:S(2)}) collective-permute-start(bf16[256,1280]{1,0:T(8,128)(2,1)} %collective-permute-done.13.refs_14_), channel_id=1, source_target_pairs={{1,0},{2,3},{5,4},{6,7},{9,8},{10,11},{13,12},{14,15},{17,16},{18,... | collective-permute-start | bytes 1966088 | tf_op jit(solution)/shard_map/ppermute | solution.py:242
  120.8 51.6 %collective-permute-start.20 = (bf16[512,1280]{1,0:T(8,128)(2,1)}, bf16[512,1280]{1,0:T(8,128)(2,1)}, u32[]{:S(2)}, u32[]{:S(2)}) collective-permute-start(bf16[512,1280]{1,0:T(8,128)(2,1)} %collective-permute-done.9.refs_0_), channel_id=1, source_target_pairs={{1,2},{2,1},{5,6},{6,5},{9,10},{10,9},{13,14},{14,13},{17,18},{18,... | collective-permute-start | bytes 3932168 | tf_op jit(solution)/shard_map/ppermute | solution.py:242
  124.4 58.2 %collective-permute-start.16 = (bf16[512,1280]{1,0:T(8,128)(2,1)}, bf16[512,1280]{1,0:T(8,128)(2,1)}, u32[]{:S(2)}, u32[]{:S(2)}) collective-permute-start(bf16[512,1280]{1,0:T(8,128)(2,1)} %collective-permute-done.8.refs_1_), channel_id=1, source_target_pairs={{1,0},{2,3},{5,4},{6,7},{9,8},{10,11},{13,12},{14,15},{17,16},{18,... | collective-permute-start | bytes 3932168 | tf_op jit(solution)/shard_map/ppermute | solution.py:242
  175.9 42.4 %collective-permute-start.24 = (bf16[2,5,512,128]{3,2,1,0:T(8,128)(2,1)}, bf16[2,5,512,128]{3,2,1,0:T(8,128)(2,1)}, u32[]{:S(2)}, u32[]{:S(2)}) collective-permute-start(bf16[2,5,512,128]{3,2,1,0:T(8,128)(2,1)} %get-tuple-element.60.refs_3_), channel_id=1, source_target_pairs={{0,8},{1,9},{2,10},{3,11}} | collective-permute-start | bytes 3932168 | tf_op jit(solution)/shard_map/ppermute | solution.py:207
  177.2 45.1 %collective-permute-start.21 = (bf16[512,1280]{1,0:T(8,128)(2,1)}, bf16[512,1280]{1,0:T(8,128)(2,1)}, u32[]{:S(2)}, u32[]{:S(2)}) collective-permute-start(bf16[512,1280]{1,0:T(8,128)(2,1)} %collective-permute-done.20.refs_3_), channel_id=1, source_target_pairs={{1,0},{2,3},{5,4},{6,7},{9,8},{10,11},{13,12},{14,15},{17,16},{18,... | collective-permute-start | bytes 3932168 | tf_op jit(solution)/shard_map/ppermute | solution.py:242
  182.6 73.9 %collective-permute-start.26 = (bf16[2,5,512,128]{3,2,1,0:T(8,128)(2,1)}, bf16[2,5,512,128]{3,2,1,0:T(8,128)(2,1)}, u32[]{:S(2)}, u32[]{:S(2)}) collective-permute-start(bf16[2,5,512,128]{3,2,1,0:T(8,128)(2,1)} %get-tuple-element.60.refs_3_), channel_id=1, source_target_pairs={{4,8},{8,12},{12,16},{16,20},{20,24},{24,28},{5,9},{9,13},{13,17},... | collective-permute-start | bytes 3932168 | tf_op jit(solution)/shard_map/ppermute | solution.py:293
  184.6 51.6 %collective-permute-start.17 = (bf16[256,1280]{1,0:T(8,128)(2,1)S(1)}, bf16[256,1280]{1,0:T(8,128)(2,1)S(1)}, u32[]{:S(2)}, u32[]{:S(2)}) collective-permute-start(bf16[256,1280]{1,0:T(8,128)(2,1)S(1)} %slice.60), channel_id=1, source_target_pairs={{1,0},{2,3},{5,4},{6,7},{9,8},{10,11},{13,12},{14,15},{17,16},{18,... | collective-permute-start | bytes 1966088 | tf_op jit(solution)/shard_map/ppermute | solution.py:242
  219.9 29.1 %collective-permute-start.25 = (bf16[2,5,512,128]{3,2,1,0:T(8,128)(2,1)S(1)}, bf16[2,5,512,128]{3,2,1,0:T(8,128)(2,1)}, u32[]{:S(2)}, u32[]{:S(2)}) collective-permute-start(bf16[2,5,512,128]{3,2,1,0:T(8,128)(2,1)S(1)} %select_select_fusion.refs_1_), channel_id=1, source_target_pairs={{0,4},{8,12},{16,20},{24,28},{1,5},{9,13},{17,21},{25,29},{2,6},{1... | collective-permute-start | bytes 3932168 | tf_op jit(solution)/shard_map/ppermute | solution.py:208
  (28 other events, 463.5 us)

commit v6 on v4

--- a/solution.py
+++ b/solution.py
@@ -224,50 +224,70 @@
     side = outer.astype(jnp.int32)
     pair, second, third = z ^ 1, jnp.where(outer, near, far), jnp.where(outer, far, near)
     info = jnp.stack([side, z, pair, second, third])
-    info_raw, info_end = jnp.stack([side, z, second, third]), jnp.stack([side, pair])
-    first, last = frames[0], frames[1]
-    ups = [(i, i + 1) for i in range(count - 1)]
-    start = pos == 0
-    following = lax.ppermute(first, "tm", [(j, i) for i, j in ups])
-    mixed1 = mix(
-        jnp.where(start, jnp.zeros_like(first), first),
-        jnp.where(start, first, last),
-        jnp.where(start, last, following),
-        taps,
-    )
-    _, later = lax.optimization_barrier((mixed1, frames))
-    preceding = lax.ppermute(later[1], "tm", ups)
-    mixed2 = mix(
-        jnp.where(start, first, preceding),
-        jnp.where(start, last, first),
-        jnp.where(start, following, last),
-        taps,
-    )
+    info_raw, info_end = jnp.stack([side, z, pair, second]), jnp.stack([side, third])
+    hold = lax.optimization_barrier
     weights = (w_query, w_key, w_value)
     gains = (q_gain, k_gain)
+    ups = [(i, i + 1) for i in range(count - 1)]
+    downs = [(j, i) for i, j in ups]
+    start = pos == 0
+    tokens = frames.shape[1]
+    flat = frames.reshape(2 * tokens, frames.shape[2])
+    cuts = [0, 3 * tokens // 4, 7 * tokens // 4, 2 * tokens]
 
     def send(x, pairs):
         return lax.ppermute(x, "head", pairs)
 
-    inward1, middle1, first1 = send(mixed1, INWARD), send(mixed1, MIDDLE), send(mixed1, OUTWARD)
-    inward1, middle1, first1 = lax.optimization_barrier((inward1, middle1, first1))
+    def mix_first(first, last, following, scales):
+        return mix(
+            jnp.where(start, jnp.zeros_like(first), first),
+            jnp.where(start, first, last),
+            jnp.where(start, last, following),
+            scales,
+        )
+
+    def mix_second(first, last, following, preceding, scales):
+        return mix(
+            jnp.where(start, first, preceding),
+            jnp.where(start, last, first),
+            jnp.where(start, following, last),
+            scales,
+        )
+
+    raw = [send(flat[: cuts[1]], OUTWARD)]
+    outer_taps = send(taps, OUTWARD)
+    following = lax.ppermute(frames[0], "tm", downs)
+    later, following, raw[0], outer_taps = hold((frames, following, raw[0], outer_taps))
+    mixed1 = mix_first(frames[0], frames[1], following, taps)
+    raw.append(send(later.reshape(flat.shape)[cuts[1] : cuts[2]], OUTWARD))
+    inward1, middle1 = send(mixed1, INWARD), send(mixed1, MIDDLE)
+    later, _ = hold((frames, mixed1))
+    preceding = lax.ppermute(later[1], "tm", ups)
+    mixed2 = mix_second(frames[0], frames[1], following, preceding, taps)
+    inward1, middle1, raw[1], later = hold((inward1, middle1, raw[1], frames))
+    raw.append(send(later.reshape(flat.shape)[cuts[2] :], OUTWARD))
     inward2, cross1, second1 = send(mixed2, INWARD), send(inward1, MIDDLE), send(middle1, OUTWARD)
-    later2, cross1 = lax.optimization_barrier((mixed2, cross1))
+    later2, cross1 = hold((mixed2, cross1))
     middle2 = send(later2, MIDDLE)
-    cross1, second1 = lax.optimization_barrier((cross1, second1))
+    cross1, second1 = hold((cross1, second1))
     third1 = send(cross1, OUTWARD)
-    middle2, inward2 = lax.optimization_barrier((middle2, inward2))
+    other_first = jnp.concatenate([raw[0], raw[1][: tokens - cuts[1]]], axis=0)
+    other_last = jnp.concatenate([raw[1][tokens - cuts[1] :], raw[2]], axis=0)
+    other_following = lax.ppermute(other_first, "tm", downs)
+    other_preceding = lax.ppermute(other_last, "tm", ups)
+    first1 = mix_first(other_first, other_last, other_following, outer_taps)
+    first2 = mix_second(other_first, other_last, other_following, other_preceding, outer_taps)
+    middle2, inward2 = hold((middle2, inward2))
     cross2, second2 = send(inward2, MIDDLE), send(middle2, OUTWARD)
-    third2 = send(cross2, OUTWARD)
-    later2, second2 = lax.optimization_barrier((mixed2, second2))
-    first2 = send(later2, OUTWARD)
 
     sources1 = [(mixed1,), (inward1, first1), (middle1, second1), (cross1, third1)]
     q1, kv1 = project(sources1, info, weights, gains, after=(inward2, middle2), flops=10**10)
+    kv1, cross2 = hold((kv1, cross2))
+    third2 = send(cross2, OUTWARD)
     anchor = broadcast_first(kv1, "tm")
     shift1 = lax.ppermute(kv1, "tm", [(i, i + 1) for i in range(1, count - 1)])
-    raw2 = project([(mixed2,), (middle2, second2), (cross2, third2)], info_raw, weights, flops=10**10)
-    q2, kv2 = project([(inward2, first2)], info_end, weights, gains, raw2, flops=10**10)
+    raw2 = project([(mixed2,), (inward2, first2), (middle2, second2)], info_raw, weights, flops=10**10)
+    q2, kv2 = project([(cross2, third2)], info_end, weights, gains, raw2, flops=10**10)
     shift2 = lax.ppermute(kv2, "tm", [(0, 1)])
     late = jnp.where(start, 0, 1)
     odd = pos % 2

time: 242 us -> 244 us (level)
  waiting for transfers between devices: 125 us -> 108 us
  starting transfers between devices: 47.8 us -> 59.3 us
  other arithmetic: 6.9 us -> 13.3 us
  local copies, waits for them, and re-layouts: 3.62 us -> 8.41 us
  Pallas kernels: 56.3 us -> 53.3 us
    ppermute x12 -> x14, waiting for transfers between devices: 103 us -> 86.7 us  [send(): return lax.ppermute(x, 'head', pairs)]
    ppermute x1 -> x3, waiting for transfers between devices: 15 us -> 0.01 us  [the longest x1 0.01 us: per_device(): following = lax.ppermute(frames[0], 'tm', downs)]
    ppermute x3, waiting for transfers between devices: 7.56 us -> 21.4 us  [broadcast_first(): held = jnp.where(mine == to, lax.ppermute(x, axis, [(0, to)]), held)]
    ppermute x12 -> x14, starting transfers between devices: 32.1 us -> 40.7 us  [send(): return lax.ppermute(x, 'head', pairs)]
    ppermute x1 -> x3, starting transfers between devices: 1.92 us -> 5.86 us  [the longest x1 2.04 us: per_device(): following = lax.ppermute(frames[0], 'tm', downs)]
    concatenate x0 -> x2, other arithmetic: none -> 3.48 us  [the longest x1 2.34 us: per_device(): other_first = jnp.concatenate([raw[0], raw[1][:tokens - cuts[1]]], axis=0)]
    pallas_call x3, Pallas kernels: 41.3 us -> 38.3 us  [project(): pl.pallas_call(functools.partial(project_body, pairs, len(after), acc is...]
    convert_element_type x2 -> x3, other arithmetic: 5.13 us -> 8.06 us  [mix(): (centre + taps[0] * before + taps[1] * centre + taps[2] * after).astype(B...]
  transfers between devices with their start and end apart: 20 -> 24, of which waited for: 11 -> 11; matrix products, arithmetic and copies ran while one was open for 2% -> 5% of each run, Pallas kernels for 20% -> 19%
where the time goes in v6:
time: 244 us; the launch traced here: 243 us
  waiting for transfers between devices  108 us (44%)
  starting transfers between devices  59.3 us (24%)
  Pallas kernels  53.3 us (22%)
  other arithmetic  13.3 us (5%)
  local copies, waits for them, and re-layouts  8.41 us (3%)
    ppermute x14, waiting for transfers between devices, send(): return lax.ppermute(x, 'head', pairs)  86.7 us
    ppermute x14, starting transfers between devices, send(): return lax.ppermute(x, 'head', pairs)  40.7 us
    pallas_call x3, Pallas kernels, project(): pl.pallas_call(functools.partial(project_body, pairs, len(after), acc is...  38.3 us
    ppermute x3, waiting for transfers between devices, broadcast_first(): held = jnp.where(mine == to, lax.ppermute(x, axis, [(0, to)]), held)  21.4 us
    pallas_call x2, Pallas kernels, attend(): pl.pallas_call(functools.partial(attend_body, 128, (len(anchors), len(opt...  15 us
    convert_element_type x3, other arithmetic, mix(): (centre + taps[0] * before + taps[1] * centre + taps[2] * after).astype(B...  8.06 us
  transfers between devices with their start and end apart: 24, of which 11 were waited for; matrix products, arithmetic and copies ran while one was open for 5% of the time, Pallas kernels for 19%

profile of v6, /device:TPU:10, one launch (start us, length us, event | category | flops | bytes accessed | tf_op | source)
XLA Modules:
  0.0 243.2 jit_solution(11810160183570425614)
XLA Ops:
  0.0 2.6 %slice_bitcast_fusion.1 = bf16[512,1280]{1,0:T(8,128)(2,1)} fusion(bf16[2,512,1280]{2,1,0:T(8,128)(2,1)} %param.7), kind=kLoop, calls=%fused_computation.28 | loop fusion | bytes 2621440 | tf_op jit(solution)/shard_map/squeeze | solution.py:266
  5.7 3.3 %collective-permute-start.1 = (bf16[384,1280]{1,0:T(8,128)(2,1)}, bf16[384,1280]{1,0:T(8,128)(2,1)}, u32[]{:S(2)}, u32[]{:S(2)}) collective-permute-start(bf16[384,1280]{1,0:T(8,128)(2,1)} %slice.65), channel_id=1, source_target_pairs={{1,0},{2,3},{5,4},{6,7},{9,8},{10,11},{13,12},{14,15},{17,16},{18,... | collective-permute-start | bytes 2949128 | tf_op jit(solution)/shard_map/ppermute | solution.py:239
  10.4 20.0 %collective-permute-done.2 = f32[3,1280]{1,0:T(4,128)S(1)} collective-permute-done((f32[3,1280]{1,0:T(4,128)S(1)}, f32[3,1280]{1,0:T(4,128)S(1)}, u32[]{:S(2)}, u32[]{:S(2)}) %collective-permute-start.2) | collective-permute-done | bytes 15392 | tf_op jit(solution)/shard_map/ppermute | solution.py:239
  34.1 4.6 %collective-permute-start.5 = (bf16[512,1280]{1,0:T(8,128)(2,1)S(1)}, bf16[512,1280]{1,0:T(8,128)(2,1)S(1)}, u32[]{:S(2)}, u32[]{:S(2)}) collective-permute-start(bf16[512,1280]{1,0:T(8,128)(2,1)S(1)} %fusion.5.refs_2_), channel_id=1, source_target_pairs={{1,2},{2,1},{5,6},{6,5},{9,10},{10,9},{13,14},{14,13},{17,18},{18,... | collective-permute-start | bytes 3932168 | tf_op jit(solution)/shard_map/ppermute | solution.py:239
  42.2 23.1 %collective-permute-done.4.refs_3_ = bf16[512,1280]{1,0:T(8,128)(2,1)S(1)} collective-permute-done((bf16[512,1280]{1,0:T(8,128)(2,1)S(1)}, bf16[512,1280]{1,0:T(8,128)(2,1)S(1)}, u32[]{:S(2)}, u32[]{:S(2)}) %collective-permute-start.4) | collective-permute-done | bytes 1310752 | tf_op jit(solution)/shard_map/ppermute | solution.py:239
  68.0 4.0 %collective-permute-start.7 = (bf16[512,1280]{1,0:T(8,128)(2,1)S(1)}, bf16[512,1280]{1,0:T(8,128)(2,1)}, u32[]{:S(2)}, u32[]{:S(2)}) collective-permute-start(bf16[512,1280]{1,0:T(8,128)(2,1)S(1)} %collective-permute-done.4.refs_3_), channel_id=1, source_target_pairs={{1,2},{2,1},{5,6},{6,5},{9,10},{10,9},{13,14},{14,13},{17,18},{18,... | collective-permute-start | bytes 3932168 | tf_op jit(solution)/shard_map/ppermute | solution.py:239
  72.2 2.5 %collective-permute-start.10 = (bf16[128,1280]{1,0:T(8,128)(2,1)S(1)}, bf16[128,1280]{1,0:T(8,128)(2,1)S(1)}, u32[]{:S(2)}, u32[]{:S(2)}) collective-permute-start(bf16[128,1280]{1,0:T(8,128)(2,1)S(1)} %slice.67), channel_id=1, source_target_pairs={{1,0},{2,3},{5,4},{6,7},{9,8},{10,11},{13,12},{14,15},{17,16},{18,... | collective-permute-start | bytes 983048 | tf_op jit(solution)/shard_map/ppermute | solution.py:239
  83.0 16.8 %collective-permute-done.7.refs_7_ = bf16[512,1280]{1,0:T(8,128)(2,1)} collective-permute-done((bf16[512,1280]{1,0:T(8,128)(2,1)S(1)}, bf16[512,1280]{1,0:T(8,128)(2,1)}, u32[]{:S(2)}, u32[]{:S(2)}) %collective-permute-start.7) | collective-permute-done | bytes 1310752 | tf_op jit(solution)/shard_map/ppermute | solution.py:239
  99.8 3.6 %collective-permute-start.8 = (bf16[512,1280]{1,0:T(8,128)(2,1)S(1)}, bf16[512,1280]{1,0:T(8,128)(2,1)}, u32[]{:S(2)}, u32[]{:S(2)}) collective-permute-start(bf16[512,1280]{1,0:T(8,128)(2,1)S(1)} %fusion.2.refs_0_), channel_id=1, source_target_pairs={{1,2},{2,1},{5,6},{6,5},{9,10},{10,9},{13,14},{14,13},{17,18},{18,... | collective-permute-start | bytes 3932168 | tf_op jit(solution)/shard_map/ppermute | solution.py:239
  106.5 2.7 %collective-permute-done.12.refs_6_ = bf16[512,1280]{1,0:T(8,128)(2,1)S(1)} collective-permute-done((bf16[512,1280]{1,0:T(8,128)(2,1)S(1)}, bf16[512,1280]{1,0:T(8,128)(2,1)S(1)}, u32[]{:S(2)}, u32[]{:S(2)}) %collective-permute-start.12) | collective-permute-done | bytes 1310752 | tf_op jit(solution)/shard_map/ppermute | solution.py:239
  110.2 5.5 %collective-permute-start.13 = (bf16[512,1280]{1,0:T(8,128)(2,1)}, bf16[512,1280]{1,0:T(8,128)(2,1)}, u32[]{:S(2)}, u32[]{:S(2)}) collective-permute-start(bf16[512,1280]{1,0:T(8,128)(2,1)} %collective-permute-done.7.refs_7_), channel_id=1, source_target_pairs={{1,0},{2,3},{5,4},{6,7},{9,8},{10,11},{13,12},{14,15},{17,16},{18,... | collective-permute-start | bytes 3932168 | tf_op jit(solution)/shard_map/ppermute | solution.py:239
  115.9 14.7 %collective-permute-done.8.refs_1_.refs_3_ = bf16[512,1280]{1,0:T(8,128)(2,1)} collective-permute-done((bf16[512,1280]{1,0:T(8,128)(2,1)S(1)}, bf16[512,1280]{1,0:T(8,128)(2,1)}, u32[]{:S(2)}, u32[]{:S(2)}) %collective-permute-start.8) | collective-permute-done | bytes 1310752 | tf_op jit(solution)/shard_map/ppermute | solution.py:239
  130.6 3.4 %collective-permute-start.14 = (bf16[512,1280]{1,0:T(8,128)(2,1)}, bf16[512,1280]{1,0:T(8,128)(2,1)S(1)}, u32[]{:S(2)}, u32[]{:S(2)}) collective-permute-start(bf16[512,1280]{1,0:T(8,128)(2,1)} %collective-permute-done.9.refs_0_.refs_1_), channel_id=1, source_target_pairs={{1,2},{2,1},{5,6},{6,5},{9,10},{10,9},{13,14},{14,13},{17,18},{18,... | collective-permute-start | bytes 3932168 | tf_op jit(solution)/shard_map/ppermute | solution.py:239
  135.0 4.5 %fusion.11 = (bf16[512,1280]{1,0:T(8,128)(2,1)S(1)}, bf16[512,1280]{1,0:T(8,128)(2,1)}) fusion(bf16[512,1280]{1,0:T(8,128)(2,1)} %copy-done.13, bf16[512,1280]{1,0:T(8,128)(2,1)} %collective-permute-done.16, f32[1280]{0:T(1024)S(1)} %get-tuple-element.48, f32[1280]{0:T(1024)S(1)} %get-tuple-element.49, f32[1280]{0:T(1024)S(1)} %get-tuple-element.47, ...), kind=kLoop, calls=%fused_computation.19 | loop fusion | flops 22282240 | bytes 7879681 | tf_op jit(solution)/shard_map/convert_element_type | solution.py:215
  139.5 2.4 collective-permute-start.17
  144.1 15.5 %project_end.2 = (bf16[5,512,128]{2,1,0:T(8,128)(2,1)S(1)}, bf16[2,5,512,128]{3,2,1,0:T(8,128)(2,1)S(1)}) custom-call(s32[5]{0:T(128)S(1)} %stack.64.info, bf16[512,1280]{1,0:T(8,128)(2,1)} %collective-permute-done.9.refs_0_.refs_1_, bf16[512,1280]{1,0:T(8,128)(2,1)} %collective-permute-done.8.refs_1_.refs_3_, bf16[512,1280]{1,0:T(8,128)(2,1)S(1)} %copy-done.1, ...), custom_call_target="tpu_custom_call" | custom-call | flops 10000000000 | bytes 1 | tf_op jit(solution)/shard_map/project_end/pallas_call | solution.py:106
  167.5 3.6 %collective-permute-done.17.refs_4_ = bf16[512,1280]{1,0:T(8,128)(2,1)} collective-permute-done((bf16[512,1280]{1,0:T(8,128)(2,1)}, bf16[512,1280]{1,0:T(8,128)(2,1)}, u32[]{:S(2)}, u32[]{:S(2)}) %collective-permute-start.17) | collective-permute-done | bytes 1310752 | tf_op jit(solution)/shard_map/ppermute | solution.py:239
  171.1 4.7 %collective-permute-start.15 = (bf16[512,1280]{1,0:T(8,128)(2,1)}, bf16[512,1280]{1,0:T(8,128)(2,1)S(1)}, u32[]{:S(2)}, u32[]{:S(2)}) collective-permute-start(bf16[512,1280]{1,0:T(8,128)(2,1)} %copy-done.6), channel_id=1, source_target_pairs={{1,0},{2,3},{5,4},{6,7},{9,8},{10,11},{13,12},{14,15},{17,16},{18,... | collective-permute-start | bytes 3932168 | tf_op jit(solution)/shard_map/ppermute | solution.py:239
  177.1 13.7 %project_raw.1.refs_7_ = f32[512,1920]{1,0:T(8,128)} custom-call(s32[4]{0:T(128)S(1)} %pad_add_fusion.2.info, bf16[512,1280]{1,0:T(8,128)(2,1)S(1)} %copy-done.3, bf16[512,1280]{1,0:T(8,128)(2,1)} %collective-permute-done.9.refs_0_.refs_1_, bf16[512,1280]{1,0:T(8,128)(2,1)S(1)} %get-tuple-element.53.refs_2_, ...), custom_call_target="tpu_custom_call" | custom-call | flops 10000000000 | bytes 1 | tf_op jit(solution)/shard_map/project_raw/pallas_call | solution.py:106
  190.9 21.4 %collective-permute-done.20 = bf16[2,5,512,128]{3,2,1,0:T(8,128)(2,1)} collective-permute-done((bf16[2,5,512,128]{3,2,1,0:T(8,128)(2,1)S(1)}, bf16[2,5,512,128]{3,2,1,0:T(8,128)(2,1)}, u32[]{:S(2)}, u32[]{:S(2)}) %collective-permute-start.20) | collective-permute-done | bytes 1310752 | tf_op jit(solution)/shard_map/ppermute | solution.py:202
  213.9 2.4 collective-permute-start.21
  216.3 9.0 %project_end.3 = (bf16[5,512,128]{2,1,0:T(8,128)(2,1)S(1)}, bf16[2,5,512,128]{3,2,1,0:T(8,128)(2,1)}) custom-call(s32[2]{0:T(128)S(1)} %pad_add_fusion.1.info, bf16[512,1280]{1,0:T(8,128)(2,1)S(1)} %copy-done.7, bf16[512,1280]{1,0:T(8,128)(2,1)S(1)} %collective-permute-done.15.refs_1_, bf16[5120,640]{1,0:T(8,128)(2,1)} %refs_2_.1, ...), custom_call_target="tpu_custom_call" | custom-call | flops 10000000000 | bytes 1 | tf_op jit(solution)/shard_map/project_end/pallas_call | solution.py:106
  227.9 7.5 %attend.2.refs_6_ = bf16[2,512,640]{2,1,0:T(8,128)(2,1)} custom-call(s32[3]{0:T(128)S(1)} %get-tuple-element.56.info, bf16[5,512,128]{2,1,0:T(8,128)(2,1)S(1)} %get-tuple-element.46.refs_0_, bf16[2,5,512,128]{3,2,1,0:T(8,128)(2,1)S(1)} %select_select_fusion.refs_1_, bf16[2,5,512,128]{3,2,1,0:T(8,128)(2,1)} %collective-permute-done.21.refs_2_, ...), custom_call_target="tpu_custom_call" | custom-call | flops 1342177280 | bytes 3932160 | tf_op jit(solution)/shard_map/attend/pallas_call | solution.py:173
  235.4 7.5 %attend.3 = bf16[2,512,640]{2,1,0:T(8,128)(2,1)} custom-call(s32[3]{0:T(128)S(1)} %get-tuple-element.55.info, bf16[5,512,128]{2,1,0:T(8,128)(2,1)S(1)} %copy-done.5, bf16[2,5,512,128]{3,2,1,0:T(8,128)(2,1)S(1)} %select_select_fusion.refs_1_, bf16[2,5,512,128]{3,2,1,0:T(8,128)(2,1)} %collective-permute-done.21.refs_2_, ...), custom_call_target="tpu_custom_call", output_to_operand_aliasing={{}: (7, {})} | custom-call | flops 1342177280 | bytes 3932160 | tf_op jit(solution)/shard_map/attend/pallas_call | solution.py:173
  (90 shorter events, 43.4 us)
Async XLA Ops:
  2.6 27.8 %collective-permute-start = (bf16[512,1280]{1,0:T(8,128)(2,1)}, bf16[512,1280]{1,0:T(8,128)(2,1)}, u32[]{:S(2)}, u32[]{:S(2)}) collective-permute-start(bf16[512,1280]{1,0:T(8,128)(2,1)} %slice_bitcast_fusion.1), channel_id=1, source_target_pairs={{4,0},{8,4},{12,8},{16,12},{20,16},{24,20},{28,24},{5,1},{9,5},{13... | collective-permute-start | bytes 3932168 | tf_op jit(solution)/shard_map/ppermute | solution.py:259
  5.7 24.7 %collective-permute-start.1 = (bf16[384,1280]{1,0:T(8,128)(2,1)}, bf16[384,1280]{1,0:T(8,128)(2,1)}, u32[]{:S(2)}, u32[]{:S(2)}) collective-permute-start(bf16[384,1280]{1,0:T(8,128)(2,1)} %slice.65), channel_id=1, source_target_pairs={{1,0},{2,3},{5,4},{6,7},{9,8},{10,11},{13,12},{14,15},{17,16},{18,... | collective-permute-start | bytes 2949128 | tf_op jit(solution)/shard_map/ppermute | solution.py:239
  9.0 21.3 %collective-permute-start.2 = (f32[3,1280]{1,0:T(4,128)S(1)}, f32[3,1280]{1,0:T(4,128)S(1)}, u32[]{:S(2)}, u32[]{:S(2)}) collective-permute-start(f32[3,1280]{1,0:T(4,128)S(1)} %copy-done.14), channel_id=1, source_target_pairs={{1,0},{2,3},{5,4},{6,7},{9,8},{10,11},{13,12},{14,15},{17,16},{18,... | collective-permute-start | bytes 46088 | tf_op jit(solution)/shard_map/ppermute | solution.py:239
  32.8 32.5 %collective-permute-start.4 = (bf16[512,1280]{1,0:T(8,128)(2,1)S(1)}, bf16[512,1280]{1,0:T(8,128)(2,1)S(1)}, u32[]{:S(2)}, u32[]{:S(2)}) collective-permute-start(bf16[512,1280]{1,0:T(8,128)(2,1)S(1)} %fusion.5.refs_2_), channel_id=1, source_target_pairs={{0,1},{3,2},{4,5},{7,6},{8,9},{11,10},{12,13},{15,14},{16,17},{19,... | collective-permute-start | bytes 3932168 | tf_op jit(solution)/shard_map/ppermute | solution.py:239
  34.1 33.3 %collective-permute-start.5 = (bf16[512,1280]{1,0:T(8,128)(2,1)S(1)}, bf16[512,1280]{1,0:T(8,128)(2,1)S(1)}, u32[]{:S(2)}, u32[]{:S(2)}) collective-permute-start(bf16[512,1280]{1,0:T(8,128)(2,1)S(1)} %fusion.5.refs_2_), channel_id=1, source_target_pairs={{1,2},{2,1},{5,6},{6,5},{9,10},{10,9},{13,14},{14,13},{17,18},{18,... | collective-permute-start | bytes 3932168 | tf_op jit(solution)/shard_map/ppermute | solution.py:239
  38.8 29.2 %collective-permute-start.6 = (bf16[512,1280]{1,0:T(8,128)(2,1)S(1)}, bf16[512,1280]{1,0:T(8,128)(2,1)S(1)}, u32[]{:S(2)}, u32[]{:S(2)}) collective-permute-start(bf16[512,1280]{1,0:T(8,128)(2,1)S(1)} %slice.66), channel_id=1, source_target_pairs={{1,0},{2,3},{5,4},{6,7},{9,8},{10,11},{13,12},{14,15},{17,16},{18,... | collective-permute-start | bytes 3932168 | tf_op jit(solution)/shard_map/ppermute | solution.py:239
  40.3 40.0 %collective-permute-start.3 = (bf16[512,1280]{1,0:T(8,128)(2,1)S(1)}, bf16[512,1280]{1,0:T(8,128)(2,1)S(1)}, u32[]{:S(2)}, u32[]{:S(2)}) collective-permute-start(bf16[512,1280]{1,0:T(8,128)(2,1)S(1)} %slice_bitcast_fusion), channel_id=1, source_target_pairs={{0,4},{4,8},{8,12},{12,16},{16,20},{20,24},{24,28},{1,5},{5,9},{9,... | collective-permute-start | bytes 3932168 | tf_op jit(solution)/shard_map/ppermute | solution.py:265
  68.0 31.8 %collective-permute-start.7 = (bf16[512,1280]{1,0:T(8,128)(2,1)S(1)}, bf16[512,1280]{1,0:T(8,128)(2,1)}, u32[]{:S(2)}, u32[]{:S(2)}) collective-permute-start(bf16[512,1280]{1,0:T(8,128)(2,1)S(1)} %collective-permute-done.4.refs_3_), channel_id=1, source_target_pairs={{1,2},{2,1},{5,6},{6,5},{9,10},{10,9},{13,14},{14,13},{17,18},{18,... | collective-permute-start | bytes 3932168 | tf_op jit(solution)/shard_map/ppermute | solution.py:239
  72.2 31.3 %collective-permute-start.10 = (bf16[128,1280]{1,0:T(8,128)(2,1)S(1)}, bf16[128,1280]{1,0:T(8,128)(2,1)S(1)}, u32[]{:S(2)}, u32[]{:S(2)}) collective-permute-start(bf16[128,1280]{1,0:T(8,128)(2,1)S(1)} %slice.67), channel_id=1, source_target_pairs={{1,0},{2,3},{5,4},{6,7},{9,8},{10,11},{13,12},{14,15},{17,16},{18,... | collective-permute-start | bytes 983048 | tf_op jit(solution)/shard_map/ppermute | solution.py:239
  77.0 57.0 %collective-permute-start.11 = (bf16[512,1280]{1,0:T(8,128)(2,1)}, bf16[512,1280]{1,0:T(8,128)(2,1)S(1)}, u32[]{:S(2)}, u32[]{:S(2)}) collective-permute-start(bf16[512,1280]{1,0:T(8,128)(2,1)} %pad_maximum_fusion), channel_id=1, source_target_pairs={{4,0},{8,4},{12,8},{16,12},{20,16},{24,20},{28,24},{5,1},{9,5},{13... | collective-permute-start | bytes 3932168 | tf_op jit(solution)/shard_map/ppermute | solution.py:276
  78.9 30.3 %collective-permute-start.12 = (bf16[512,1280]{1,0:T(8,128)(2,1)S(1)}, bf16[512,1280]{1,0:T(8,128)(2,1)S(1)}, u32[]{:S(2)}, u32[]{:S(2)}) collective-permute-start(bf16[512,1280]{1,0:T(8,128)(2,1)S(1)} %collective-permute-done.5.refs_5_), channel_id=1, source_target_pairs={{1,0},{2,3},{5,4},{6,7},{9,8},{10,11},{13,12},{14,15},{17,16},{18,... | collective-permute-start | bytes 3932168 | tf_op jit(solution)/shard_map/ppermute | solution.py:239
  81.5 34.4 %collective-permute-start.9 = (bf16[512,1280]{1,0:T(8,128)(2,1)S(1)}, bf16[512,1280]{1,0:T(8,128)(2,1)}, u32[]{:S(2)}, u32[]{:S(2)}) collective-permute-start(bf16[512,1280]{1,0:T(8,128)(2,1)S(1)} %fusion.2.refs_0_), channel_id=1, source_target_pairs={{0,1},{3,2},{4,5},{7,6},{8,9},{11,10},{12,13},{15,14},{16,17},{19,... | collective-permute-start | bytes 3932168 | tf_op jit(solution)/shard_map/ppermute | solution.py:239
  99.8 30.8 %collective-permute-start.8 = (bf16[512,1280]{1,0:T(8,128)(2,1)S(1)}, bf16[512,1280]{1,0:T(8,128)(2,1)}, u32[]{:S(2)}, u32[]{:S(2)}) collective-permute-start(bf16[512,1280]{1,0:T(8,128)(2,1)S(1)} %fusion.2.refs_0_), channel_id=1, source_target_pairs={{1,2},{2,1},{5,6},{6,5},{9,10},{10,9},{13,14},{14,13},{17,18},{18,... | collective-permute-start | bytes 3932168 | tf_op jit(solution)/shard_map/ppermute | solution.py:239
  104.6 29.4 %collective-permute-start.16 = (bf16[512,1280]{1,0:T(8,128)(2,1)}, bf16[512,1280]{1,0:T(8,128)(2,1)}, u32[]{:S(2)}, u32[]{:S(2)}) collective-permute-start(bf16[512,1280]{1,0:T(8,128)(2,1)} %pad_maximum_fusion.1), channel_id=1, source_target_pairs={{0,4},{4,8},{8,12},{12,16},{16,20},{20,24},{24,28},{1,5},{5,9},{9,... | collective-permute-start | bytes 3932168 | tf_op jit(solution)/shard_map/ppermute | solution.py:277
  110.2 33.9 %collective-permute-start.13 = (bf16[512,1280]{1,0:T(8,128)(2,1)}, bf16[512,1280]{1,0:T(8,128)(2,1)}, u32[]{:S(2)}, u32[]{:S(2)}) collective-permute-start(bf16[512,1280]{1,0:T(8,128)(2,1)} %collective-permute-done.7.refs_7_), channel_id=1, source_target_pairs={{1,0},{2,3},{5,4},{6,7},{9,8},{10,11},{13,12},{14,15},{17,16},{18,... | collective-permute-start | bytes 3932168 | tf_op jit(solution)/shard_map/ppermute | solution.py:239
  130.6 30.0 %collective-permute-start.14 = (bf16[512,1280]{1,0:T(8,128)(2,1)}, bf16[512,1280]{1,0:T(8,128)(2,1)S(1)}, u32[]{:S(2)}, u32[]{:S(2)}) collective-permute-start(bf16[512,1280]{1,0:T(8,128)(2,1)} %collective-permute-done.9.refs_0_.refs_1_), channel_id=1, source_target_pairs={{1,2},{2,1},{5,6},{6,5},{9,10},{10,9},{13,14},{14,13},{17,18},{18,... | collective-permute-start | bytes 3932168 | tf_op jit(solution)/shard_map/ppermute | solution.py:239
  139.5 31.6 %collective-permute-start.17 = (bf16[512,1280]{1,0:T(8,128)(2,1)}, bf16[512,1280]{1,0:T(8,128)(2,1)}, u32[]{:S(2)}, u32[]{:S(2)}) collective-permute-start(bf16[512,1280]{1,0:T(8,128)(2,1)} %collective-permute-done.8.refs_1_.refs_3_), channel_id=1, source_target_pairs={{1,0},{2,3},{5,4},{6,7},{9,8},{10,11},{13,12},{14,15},{17,16},{18,... | collective-permute-start | bytes 3932168 | tf_op jit(solution)/shard_map/ppermute | solution.py:239
  160.6 30.3 %collective-permute-start.18 = (bf16[2,5,512,128]{3,2,1,0:T(8,128)(2,1)S(1)}, bf16[2,5,512,128]{3,2,1,0:T(8,128)(2,1)}, u32[]{:S(2)}, u32[]{:S(2)}) collective-permute-start(bf16[2,5,512,128]{3,2,1,0:T(8,128)(2,1)S(1)} %get-tuple-element.44.refs_3_), channel_id=1, source_target_pairs={{0,24},{1,25},{2,26},{3,27}} | collective-permute-start | bytes 3932168 | tf_op jit(solution)/shard_map/ppermute | solution.py:202
  162.4 28.5 %collective-permute-start.19 = (bf16[2,5,512,128]{3,2,1,0:T(8,128)(2,1)S(1)}, bf16[2,5,512,128]{3,2,1,0:T(8,128)(2,1)}, u32[]{:S(2)}, u32[]{:S(2)}) collective-permute-start(bf16[2,5,512,128]{3,2,1,0:T(8,128)(2,1)S(1)} %get-tuple-element.44.refs_3_), channel_id=1, source_target_pairs={{0,16},{1,17},{2,18},{3,19}} | collective-permute-start | bytes 3932168 | tf_op jit(solution)/shard_map/ppermute | solution.py:202
  164.1 48.2 %collective-permute-start.20 = (bf16[2,5,512,128]{3,2,1,0:T(8,128)(2,1)S(1)}, bf16[2,5,512,128]{3,2,1,0:T(8,128)(2,1)}, u32[]{:S(2)}, u32[]{:S(2)}) collective-permute-start(bf16[2,5,512,128]{3,2,1,0:T(8,128)(2,1)S(1)} %get-tuple-element.44.refs_3_), channel_id=1, source_target_pairs={{0,8},{1,9},{2,10},{3,11}} | collective-permute-start | bytes 3932168 | tf_op jit(solution)/shard_map/ppermute | solution.py:202
  165.6 69.9 %collective-permute-start.22 = (bf16[2,5,512,128]{3,2,1,0:T(8,128)(2,1)S(1)}, bf16[2,5,512,128]{3,2,1,0:T(8,128)(2,1)}, u32[]{:S(2)}, u32[]{:S(2)}) collective-permute-start(bf16[2,5,512,128]{3,2,1,0:T(8,128)(2,1)S(1)} %get-tuple-element.44.refs_3_), channel_id=1, source_target_pairs={{4,8},{8,12},{12,16},{16,20},{20,24},{24,28},{5,9},{9,13},{13,17},... | collective-permute-start | bytes 3932168 | tf_op jit(solution)/shard_map/ppermute | solution.py:288
  171.1 45.1 %collective-permute-start.15 = (bf16[512,1280]{1,0:T(8,128)(2,1)}, bf16[512,1280]{1,0:T(8,128)(2,1)S(1)}, u32[]{:S(2)}, u32[]{:S(2)}) collective-permute-start(bf16[512,1280]{1,0:T(8,128)(2,1)} %copy-done.6), channel_id=1, source_target_pairs={{1,0},{2,3},{5,4},{6,7},{9,8},{10,11},{13,12},{14,15},{17,16},{18,... | collective-permute-start | bytes 3932168 | tf_op jit(solution)/shard_map/ppermute | solution.py:239
  213.9 14.0 %collective-permute-start.21 = (bf16[2,5,512,128]{3,2,1,0:T(8,128)(2,1)S(1)}, bf16[2,5,512,128]{3,2,1,0:T(8,128)(2,1)}, u32[]{:S(2)}, u32[]{:S(2)}) collective-permute-start(bf16[2,5,512,128]{3,2,1,0:T(8,128)(2,1)S(1)} %select_select_fusion.refs_1_), channel_id=1, source_target_pairs={{0,4},{8,12},{16,20},{24,28},{1,5},{9,13},{17,21},{25,29},{2,6},{1... | collective-permute-start | bytes 3932168 | tf_op jit(solution)/shard_map/ppermute | solution.py:203
  226.1 9.3 %collective-permute-start.23 = (bf16[2,5,512,128]{3,2,1,0:T(8,128)(2,1)}, bf16[2,5,512,128]{3,2,1,0:T(8,128)(2,1)}, u32[]{:S(2)}, u32[]{:S(2)}) collective-permute-start(bf16[2,5,512,128]{3,2,1,0:T(8,128)(2,1)} %get-tuple-element.45.refs_4_), channel_id=1, source_target_pairs={{0,4},{1,5},{2,6},{3,7}} | collective-permute-start | bytes 3932168 | tf_op jit(solution)/shard_map/ppermute | solution.py:291
  (20 other events, 273.1 us)

commit v7 on v6

--- a/solution.py
+++ b/solution.py
@@ -194,17 +194,17 @@
     )(jnp.stack([anchor, frame, choice]).astype(jnp.int32), *args)
 
 
-def broadcast_first(x, axis):
+def broadcast_first(x, axis, before):
     count = lax.axis_size(axis)
     mine = lax.axis_index(axis)
     held = x
     for to in range(2, count, 2):
         held = jnp.where(mine == to, lax.ppermute(x, axis, [(0, to)]), held)
+    held, before = lax.optimization_barrier((held, before))
     other = lax.ppermute(held, axis, [(i, i + 1) for i in range(0, count, 2)])
-    return held, other
-
-
-SWAP = [(0, 1), (1, 0), (2, 3), (3, 2)]
+    return (held, other), before
+
+
 INWARD = [(0, 1), (3, 2)]
 MIDDLE = [(1, 2), (2, 1)]
 OUTWARD = [(1, 0), (2, 3)]
@@ -231,9 +231,7 @@
     ups = [(i, i + 1) for i in range(count - 1)]
     downs = [(j, i) for i, j in ups]
     start = pos == 0
-    tokens = frames.shape[1]
-    flat = frames.reshape(2 * tokens, frames.shape[2])
-    cuts = [0, 3 * tokens // 4, 7 * tokens // 4, 2 * tokens]
+    cut = 3 * frames.shape[1] // 4
 
     def send(x, pairs):
         return lax.ppermute(x, "head", pairs)
@@ -254,29 +252,27 @@
             scales,
         )
 
-    raw = [send(flat[: cuts[1]], OUTWARD)]
+    raw = [send(frames[0], OUTWARD)]
+    following = lax.ppermute(frames[0], "tm", downs)
+    mixed1 = mix_first(frames[0], frames[1], following, taps)
     outer_taps = send(taps, OUTWARD)
-    following = lax.ppermute(frames[0], "tm", downs)
-    later, following, raw[0], outer_taps = hold((frames, following, raw[0], outer_taps))
-    mixed1 = mix_first(frames[0], frames[1], following, taps)
-    raw.append(send(later.reshape(flat.shape)[cuts[1] : cuts[2]], OUTWARD))
     inward1, middle1 = send(mixed1, INWARD), send(mixed1, MIDDLE)
-    later, _ = hold((frames, mixed1))
+    later, raw[0], outer_taps, _ = hold((frames, raw[0], outer_taps, mixed1))
     preceding = lax.ppermute(later[1], "tm", ups)
+    raw.append(send(later[1, :cut], OUTWARD))
     mixed2 = mix_second(frames[0], frames[1], following, preceding, taps)
     inward1, middle1, raw[1], later = hold((inward1, middle1, raw[1], frames))
-    raw.append(send(later.reshape(flat.shape)[cuts[2] :], OUTWARD))
     inward2, cross1, second1 = send(mixed2, INWARD), send(inward1, MIDDLE), send(middle1, OUTWARD)
+    raw.append(send(later[1, cut:], OUTWARD))
     later2, cross1 = hold((mixed2, cross1))
     middle2 = send(later2, MIDDLE)
     cross1, second1 = hold((cross1, second1))
     third1 = send(cross1, OUTWARD)
-    other_first = jnp.concatenate([raw[0], raw[1][: tokens - cuts[1]]], axis=0)
-    other_last = jnp.concatenate([raw[1][tokens - cuts[1] :], raw[2]], axis=0)
-    other_following = lax.ppermute(other_first, "tm", downs)
+    other_last = jnp.concatenate(raw[1:], axis=0)
+    other_following = lax.ppermute(raw[0], "tm", downs)
     other_preceding = lax.ppermute(other_last, "tm", ups)
-    first1 = mix_first(other_first, other_last, other_following, outer_taps)
-    first2 = mix_second(other_first, other_last, other_following, other_preceding, outer_taps)
+    first1 = mix_first(raw[0], other_last, other_following, outer_taps)
+    first2 = mix_second(raw[0], other_last, other_following, other_preceding, outer_taps)
     middle2, inward2 = hold((middle2, inward2))
     cross2, second2 = send(inward2, MIDDLE), send(middle2, OUTWARD)
 
@@ -284,8 +280,8 @@
     q1, kv1 = project(sources1, info, weights, gains, after=(inward2, middle2), flops=10**10)
     kv1, cross2 = hold((kv1, cross2))
     third2 = send(cross2, OUTWARD)
-    anchor = broadcast_first(kv1, "tm")
     shift1 = lax.ppermute(kv1, "tm", [(i, i + 1) for i in range(1, count - 1)])
+    anchor, shift1 = broadcast_first(kv1, "tm", shift1)
     raw2 = project([(mixed2,), (inward2, first2), (middle2, second2)], info_raw, weights, flops=10**10)
     q2, kv2 = project([(cross2, third2)], info_end, weights, gains, raw2, flops=10**10)
     shift2 = lax.ppermute(kv2, "tm", [(0, 1)])

time: 244 us -> 238 us (0.975)
  waiting for transfers between devices: 108 us -> 99 us
  starting transfers between devices: 59.3 us -> 67.4 us
  other arithmetic: 13.3 us -> 9.94 us
    ppermute x14, waiting for transfers between devices: 86.7 us -> 70 us  [send(): return lax.ppermute(x, 'head', pairs)]
    ppermute x1, waiting for transfers between devices: 0.01 us -> 9.82 us  [per_device(): following = lax.ppermute(frames[0], 'tm', downs)]
    ppermute x14, starting transfers between devices: 40.7 us -> 47.2 us  [send(): return lax.ppermute(x, 'head', pairs)]
    concatenate x2 -> x0, other arithmetic: 3.48 us -> none  [the longest x1 2.34 us: per_device(): other_first = jnp.concatenate([raw[0], raw[1][:tokens - cuts[1]]], axis=0)]
  transfers between devices with their start and end apart: 24 -> 24, of which waited for: 11 -> 9; matrix products, arithmetic and copies ran while one was open for 5% -> 5% of each run, Pallas kernels for 19% -> 19%
where the time goes in v7:
time: 238 us; the launch traced here: 237 us
  waiting for transfers between devices  99 us (42%)
  starting transfers between devices  67.4 us (28%)
  Pallas kernels  52.5 us (22%)
  other arithmetic  9.94 us (4%)
  local copies, waits for them, and re-layouts  7.22 us (3%)
    ppermute x14, waiting for transfers between devices, send(): return lax.ppermute(x, 'head', pairs)  70 us
    ppermute x14, starting transfers between devices, send(): return lax.ppermute(x, 'head', pairs)  47.2 us
    pallas_call x3, Pallas kernels, project(): pl.pallas_call(functools.partial(project_body, pairs, len(after), acc is...  38.1 us
    ppermute x3, waiting for transfers between devices, broadcast_first(): held = jnp.where(mine == to, lax.ppermute(x, axis, [(0, to)]), held)  19.2 us
    pallas_call x2, Pallas kernels, attend(): pl.pallas_call(functools.partial(attend_body, 128, (len(anchors), len(opt...  14.3 us
    ppermute x1, waiting for transfers between devices, per_device(): following = lax.ppermute(frames[0], 'tm', downs)  9.82 us
    convert_element_type x3, other arithmetic, mix(): (centre + taps[0] * before + taps[1] * centre + taps[2] * after).astype(B...  8.17 us
    ppermute x3, starting transfers between devices, broadcast_first(): held = jnp.where(mine == to, lax.ppermute(x, axis, [(0, to)]), held)  4.84 us
  transfers between devices with their start and end apart: 24, of which 9 were waited for; matrix products, arithmetic and copies ran while one was open for 5% of the time, Pallas kernels for 19%

profile of v7, /device:TPU:10, one launch (start us, length us, event | category | flops | bytes accessed | tf_op | source)
XLA Modules:
  0.0 236.8 jit_solution(17686273202973815701)
XLA Ops:
  4.5 3.5 %collective-permute-start = (bf16[512,1280]{1,0:T(8,128)(2,1)}, bf16[512,1280]{1,0:T(8,128)(2,1)}, u32[]{:S(2)}, u32[]{:S(2)}) collective-permute-start(bf16[512,1280]{1,0:T(8,128)(2,1)} %slice_bitcast_fusion.1), channel_id=1, source_target_pairs={{1,0},{2,3},{5,4},{6,7},{9,8},{10,11},{13,12},{14,15},{17,16},{18,... | collective-permute-start | bytes 3932168 | tf_op jit(solution)/shard_map/ppermute | solution.py:237
  10.1 9.8 %collective-permute-done.2 = bf16[512,1280]{1,0:T(8,128)(2,1)} collective-permute-done((bf16[512,1280]{1,0:T(8,128)(2,1)}, bf16[512,1280]{1,0:T(8,128)(2,1)}, u32[]{:S(2)}, u32[]{:S(2)}) %collective-permute-start.2) | collective-permute-done | bytes 1310752 | tf_op jit(solution)/shard_map/ppermute | solution.py:256
  23.6 3.5 %collective-permute-start.5 = (bf16[512,1280]{1,0:T(8,128)(2,1)S(1)}, bf16[512,1280]{1,0:T(8,128)(2,1)S(1)}, u32[]{:S(2)}, u32[]{:S(2)}) collective-permute-start(bf16[512,1280]{1,0:T(8,128)(2,1)S(1)} %fusion.5.refs_2_), channel_id=1, source_target_pairs={{1,2},{2,1},{5,6},{6,5},{9,10},{10,9},{13,14},{14,13},{17,18},{18,... | collective-permute-start | bytes 3932168 | tf_op jit(solution)/shard_map/ppermute | solution.py:237
  27.1 9.1 %collective-permute-done.1 = f32[3,1280]{1,0:T(4,128)S(1)} collective-permute-done((f32[3,1280]{1,0:T(4,128)}, f32[3,1280]{1,0:T(4,128)S(1)}, u32[]{:S(2)}, u32[]{:S(2)}) %collective-permute-start.1) | collective-permute-done | bytes 15392 | tf_op jit(solution)/shard_map/ppermute | solution.py:237
  36.3 4.7 %collective-permute-start.6 = (bf16[384,1280]{1,0:T(8,128)(2,1)S(1)}, bf16[384,1280]{1,0:T(8,128)(2,1)S(1)}, u32[]{:S(2)}, u32[]{:S(2)}) collective-permute-start(bf16[384,1280]{1,0:T(8,128)(2,1)S(1)} %slice_bitcast_fusion.2), channel_id=1, source_target_pairs={{1,0},{2,3},{5,4},{6,7},{9,8},{10,11},{13,12},{14,15},{17,16},{18,... | collective-permute-start | bytes 2949128 | tf_op jit(solution)/shard_map/ppermute | solution.py:237
  43.1 3.6 %collective-permute-start.11 = (bf16[512,1280]{1,0:T(8,128)(2,1)}, bf16[512,1280]{1,0:T(8,128)(2,1)}, u32[]{:S(2)}, u32[]{:S(2)}) collective-permute-start(bf16[512,1280]{1,0:T(8,128)(2,1)} %collective-permute-done), channel_id=1, source_target_pairs={{4,0},{8,4},{12,8},{16,12},{20,16},{24,20},{28,24},{5,1},{9,5},{13... | collective-permute-start | bytes 3932168 | tf_op jit(solution)/shard_map/ppermute | solution.py:272
  46.7 15.2 %collective-permute-done.6 = bf16[384,1280]{1,0:T(8,128)(2,1)S(1)} collective-permute-done((bf16[384,1280]{1,0:T(8,128)(2,1)S(1)}, bf16[384,1280]{1,0:T(8,128)(2,1)S(1)}, u32[]{:S(2)}, u32[]{:S(2)}) %collective-permute-start.6) | collective-permute-done | bytes 983072 | tf_op jit(solution)/shard_map/ppermute | solution.py:237
  62.0 4.6 %collective-permute-start.7 = (bf16[512,1280]{1,0:T(8,128)(2,1)S(1)}, bf16[512,1280]{1,0:T(8,128)(2,1)}, u32[]{:S(2)}, u32[]{:S(2)}) collective-permute-start(bf16[512,1280]{1,0:T(8,128)(2,1)S(1)} %collective-permute-done.4.refs_3_), channel_id=1, source_target_pairs={{1,2},{2,1},{5,6},{6,5},{9,10},{10,9},{13,14},{14,13},{17,18},{18,... | collective-permute-start | bytes 3932168 | tf_op jit(solution)/shard_map/ppermute | solution.py:237
  71.0 5.7 %collective-permute-start.12 = (bf16[512,1280]{1,0:T(8,128)(2,1)S(1)}, bf16[512,1280]{1,0:T(8,128)(2,1)S(1)}, u32[]{:S(2)}, u32[]{:S(2)}) collective-permute-start(bf16[512,1280]{1,0:T(8,128)(2,1)S(1)} %collective-permute-done.5.refs_5_), channel_id=1, source_target_pairs={{1,0},{2,3},{5,4},{6,7},{9,8},{10,11},{13,12},{14,15},{17,16},{18,... | collective-permute-start | bytes 3932168 | tf_op jit(solution)/shard_map/ppermute | solution.py:237
  76.8 17.8 %collective-permute-done.7.refs_7_ = bf16[512,1280]{1,0:T(8,128)(2,1)} collective-permute-done((bf16[512,1280]{1,0:T(8,128)(2,1)S(1)}, bf16[512,1280]{1,0:T(8,128)(2,1)}, u32[]{:S(2)}, u32[]{:S(2)}) %collective-permute-start.7) | collective-permute-done | bytes 1310752 | tf_op jit(solution)/shard_map/ppermute | solution.py:237
  94.6 3.6 %collective-permute-start.8 = (bf16[512,1280]{1,0:T(8,128)(2,1)S(1)}, bf16[512,1280]{1,0:T(8,128)(2,1)}, u32[]{:S(2)}, u32[]{:S(2)}) collective-permute-start(bf16[512,1280]{1,0:T(8,128)(2,1)S(1)} %fusion.2.refs_0_), channel_id=1, source_target_pairs={{1,2},{2,1},{5,6},{6,5},{9,10},{10,9},{13,14},{14,13},{17,18},{18,... | collective-permute-start | bytes 3932168 | tf_op jit(solution)/shard_map/ppermute | solution.py:237
  100.2 5.1 %collective-permute-done.12.refs_6_ = bf16[512,1280]{1,0:T(8,128)(2,1)S(1)} collective-permute-done((bf16[512,1280]{1,0:T(8,128)(2,1)S(1)}, bf16[512,1280]{1,0:T(8,128)(2,1)S(1)}, u32[]{:S(2)}, u32[]{:S(2)}) %collective-permute-start.12) | collective-permute-done | bytes 1310752 | tf_op jit(solution)/shard_map/ppermute | solution.py:237
  106.4 5.4 %collective-permute-start.13 = (bf16[512,1280]{1,0:T(8,128)(2,1)}, bf16[512,1280]{1,0:T(8,128)(2,1)}, u32[]{:S(2)}, u32[]{:S(2)}) collective-permute-start(bf16[512,1280]{1,0:T(8,128)(2,1)} %collective-permute-done.7.refs_7_), channel_id=1, source_target_pairs={{1,0},{2,3},{5,4},{6,7},{9,8},{10,11},{13,12},{14,15},{17,16},{18,... | collective-permute-start | bytes 3932168 | tf_op jit(solution)/shard_map/ppermute | solution.py:237
  112.0 13.5 %collective-permute-done.8.refs_1_.refs_3_ = bf16[512,1280]{1,0:T(8,128)(2,1)} collective-permute-done((bf16[512,1280]{1,0:T(8,128)(2,1)S(1)}, bf16[512,1280]{1,0:T(8,128)(2,1)}, u32[]{:S(2)}, u32[]{:S(2)}) %collective-permute-start.8) | collective-permute-done | bytes 1310752 | tf_op jit(solution)/shard_map/ppermute | solution.py:237
  128.9 4.6 %fusion.11 = (bf16[512,1280]{1,0:T(8,128)(2,1)S(1)}, bf16[512,1280]{1,0:T(8,128)(2,1)}) fusion(bf16[512,1280]{1,0:T(8,128)(2,1)} %collective-permute-done.11, bf16[512,1280]{1,0:T(8,128)(2,1)} %copy-done.12, bf16[512,1280]{1,0:T(8,128)(2,1)} %collective-permute-done, bf16[512,1280]{1,0:T(8,128)(2,1)} %collective-permute-done.16, ...), kind=kLoop, calls=%fused_computation.19 | loop fusion | flops 17039360 | bytes 7879681 | tf_op jit(solution)/shard_map/convert_element_type | solution.py:215
  135.9 4.3 %collective-permute-done.13.refs_8_ = bf16[512,1280]{1,0:T(8,128)(2,1)} collective-permute-done((bf16[512,1280]{1,0:T(8,128)(2,1)}, bf16[512,1280]{1,0:T(8,128)(2,1)}, u32[]{:S(2)}, u32[]{:S(2)}) %collective-permute-start.13) | collective-permute-done | bytes 1310752 | tf_op jit(solution)/shard_map/ppermute | solution.py:237
  140.2 15.5 %project_end.2 = (bf16[5,512,128]{2,1,0:T(8,128)(2,1)S(1)}, bf16[2,5,512,128]{3,2,1,0:T(8,128)(2,1)S(1)}) custom-call(s32[5]{0:T(128)S(1)} %stack.64.info, bf16[512,1280]{1,0:T(8,128)(2,1)} %collective-permute-done.9.refs_0_.refs_1_, bf16[512,1280]{1,0:T(8,128)(2,1)} %collective-permute-done.8.refs_1_.refs_3_, bf16[512,1280]{1,0:T(8,128)(2,1)S(1)} %copy-done.3, ...), custom_call_target="tpu_custom_call" | custom-call | flops 10000000000 | bytes 1 | tf_op jit(solution)/shard_map/project_end/pallas_call | solution.py:106
  162.7 5.0 %collective-permute-done.17.refs_4_ = bf16[512,1280]{1,0:T(8,128)(2,1)} collective-permute-done((bf16[512,1280]{1,0:T(8,128)(2,1)}, bf16[512,1280]{1,0:T(8,128)(2,1)}, u32[]{:S(2)}, u32[]{:S(2)}) %collective-permute-start.17) | collective-permute-done | bytes 1310752 | tf_op jit(solution)/shard_map/ppermute | solution.py:237
  167.7 4.7 %collective-permute-start.15 = (bf16[512,1280]{1,0:T(8,128)(2,1)}, bf16[512,1280]{1,0:T(8,128)(2,1)S(1)}, u32[]{:S(2)}, u32[]{:S(2)}) collective-permute-start(bf16[512,1280]{1,0:T(8,128)(2,1)} %copy-done.8), channel_id=1, source_target_pairs={{1,0},{2,3},{5,4},{6,7},{9,8},{10,11},{13,12},{14,15},{17,16},{18,... | collective-permute-start | bytes 3932168 | tf_op jit(solution)/shard_map/ppermute | solution.py:237
  173.7 13.7 %project_raw.1.refs_7_ = f32[512,1920]{1,0:T(8,128)} custom-call(s32[4]{0:T(128)S(1)} %pad_add_fusion.2.info, bf16[512,1280]{1,0:T(8,128)(2,1)S(1)} %copy-done.5, bf16[512,1280]{1,0:T(8,128)(2,1)} %collective-permute-done.9.refs_0_.refs_1_, bf16[512,1280]{1,0:T(8,128)(2,1)S(1)} %get-tuple-element.53.refs_2_, ...), custom_call_target="tpu_custom_call" | custom-call | flops 10000000000 | bytes 1 | tf_op jit(solution)/shard_map/project_raw/pallas_call | solution.py:106
  187.5 19.2 %collective-permute-done.20 = bf16[2,5,512,128]{3,2,1,0:T(8,128)(2,1)} collective-permute-done((bf16[2,5,512,128]{3,2,1,0:T(8,128)(2,1)S(1)}, bf16[2,5,512,128]{3,2,1,0:T(8,128)(2,1)}, u32[]{:S(2)}, u32[]{:S(2)}) %collective-permute-start.20) | collective-permute-done | bytes 1310752 | tf_op jit(solution)/shard_map/ppermute | solution.py:202
  210.7 8.9 %project_end.3 = (bf16[5,512,128]{2,1,0:T(8,128)(2,1)S(1)}, bf16[2,5,512,128]{3,2,1,0:T(8,128)(2,1)}) custom-call(s32[2]{0:T(128)S(1)} %pad_add_fusion.1.info, bf16[512,1280]{1,0:T(8,128)(2,1)S(1)} %copy-done.9, bf16[512,1280]{1,0:T(8,128)(2,1)S(1)} %collective-permute-done.15.refs_1_, bf16[5120,640]{1,0:T(8,128)(2,1)} %refs_2_.1, ...), custom_call_target="tpu_custom_call" | custom-call | flops 10000000000 | bytes 1 | tf_op jit(solution)/shard_map/project_end/pallas_call | solution.py:106
  222.2 7.5 %attend.2.refs_6_ = bf16[2,512,640]{2,1,0:T(8,128)(2,1)} custom-call(s32[3]{0:T(128)S(1)} %get-tuple-element.56.info, bf16[5,512,128]{2,1,0:T(8,128)(2,1)S(1)} %get-tuple-element.46.refs_0_, bf16[2,5,512,128]{3,2,1,0:T(8,128)(2,1)S(1)} %select_select_fusion.refs_1_, bf16[2,5,512,128]{3,2,1,0:T(8,128)(2,1)} %collective-permute-done.22.refs_2_, ...), custom_call_target="tpu_custom_call" | custom-call | flops 1342177280 | bytes 3932160 | tf_op jit(solution)/shard_map/attend/pallas_call | solution.py:173
  229.8 6.8 %attend.3 = bf16[2,512,640]{2,1,0:T(8,128)(2,1)} custom-call(s32[3]{0:T(128)S(1)} %get-tuple-element.55.info, bf16[5,512,128]{2,1,0:T(8,128)(2,1)S(1)} %copy-done.7, bf16[2,5,512,128]{3,2,1,0:T(8,128)(2,1)S(1)} %select_select_fusion.refs_1_, bf16[2,5,512,128]{3,2,1,0:T(8,128)(2,1)} %collective-permute-done.22.refs_2_, ...), custom_call_target="tpu_custom_call", output_to_operand_aliasing={{}: (7, {})} | custom-call | flops 1342177280 | bytes 3932160 | tf_op jit(solution)/shard_map/attend/pallas_call | solution.py:173
  (83 shorter events, 40.7 us)
Async XLA Ops:
  2.6 17.3 %collective-permute-start.2 = (bf16[512,1280]{1,0:T(8,128)(2,1)}, bf16[512,1280]{1,0:T(8,128)(2,1)}, u32[]{:S(2)}, u32[]{:S(2)}) collective-permute-start(bf16[512,1280]{1,0:T(8,128)(2,1)} %slice_bitcast_fusion.1), channel_id=1, source_target_pairs={{4,0},{8,4},{12,8},{16,12},{20,16},{24,20},{28,24},{5,1},{9,5},{13... | collective-permute-start | bytes 3932168 | tf_op jit(solution)/shard_map/ppermute | solution.py:256
  4.5 31.7 %collective-permute-start = (bf16[512,1280]{1,0:T(8,128)(2,1)}, bf16[512,1280]{1,0:T(8,128)(2,1)}, u32[]{:S(2)}, u32[]{:S(2)}) collective-permute-start(bf16[512,1280]{1,0:T(8,128)(2,1)} %slice_bitcast_fusion.1), channel_id=1, source_target_pairs={{1,0},{2,3},{5,4},{6,7},{9,8},{10,11},{13,12},{14,15},{17,16},{18,... | collective-permute-start | bytes 3932168 | tf_op jit(solution)/shard_map/ppermute | solution.py:237
  8.0 28.2 %collective-permute-start.1 = (f32[3,1280]{1,0:T(4,128)}, f32[3,1280]{1,0:T(4,128)S(1)}, u32[]{:S(2)}, u32[]{:S(2)}) collective-permute-start(f32[3,1280]{1,0:T(4,128)} %param.8), channel_id=1, source_target_pairs={{1,0},{2,3},{5,4},{6,7},{9,8},{10,11},{13,12},{14,15},{17,16},{18,... | collective-permute-start | bytes 46088 | tf_op jit(solution)/shard_map/ppermute | solution.py:237
  22.3 39.6 %collective-permute-start.4 = (bf16[512,1280]{1,0:T(8,128)(2,1)S(1)}, bf16[512,1280]{1,0:T(8,128)(2,1)S(1)}, u32[]{:S(2)}, u32[]{:S(2)}) collective-permute-start(bf16[512,1280]{1,0:T(8,128)(2,1)S(1)} %fusion.5.refs_2_), channel_id=1, source_target_pairs={{0,1},{3,2},{4,5},{7,6},{8,9},{11,10},{12,13},{15,14},{16,17},{19,... | collective-permute-start | bytes 3932168 | tf_op jit(solution)/shard_map/ppermute | solution.py:237
  23.6 38.3 %collective-permute-start.5 = (bf16[512,1280]{1,0:T(8,128)(2,1)S(1)}, bf16[512,1280]{1,0:T(8,128)(2,1)S(1)}, u32[]{:S(2)}, u32[]{:S(2)}) collective-permute-start(bf16[512,1280]{1,0:T(8,128)(2,1)S(1)} %fusion.5.refs_2_), channel_id=1, source_target_pairs={{1,2},{2,1},{5,6},{6,5},{9,10},{10,9},{13,14},{14,13},{17,18},{18,... | collective-permute-start | bytes 3932168 | tf_op jit(solution)/shard_map/ppermute | solution.py:237
  36.3 25.6 %collective-permute-start.6 = (bf16[384,1280]{1,0:T(8,128)(2,1)S(1)}, bf16[384,1280]{1,0:T(8,128)(2,1)S(1)}, u32[]{:S(2)}, u32[]{:S(2)}) collective-permute-start(bf16[384,1280]{1,0:T(8,128)(2,1)S(1)} %slice_bitcast_fusion.2), channel_id=1, source_target_pairs={{1,0},{2,3},{5,4},{6,7},{9,8},{10,11},{13,12},{14,15},{17,16},{18,... | collective-permute-start | bytes 2949128 | tf_op jit(solution)/shard_map/ppermute | solution.py:237
  41.1 27.2 %collective-permute-start.3 = (bf16[512,1280]{1,0:T(8,128)(2,1)S(1)}, bf16[512,1280]{1,0:T(8,128)(2,1)S(1)}, u32[]{:S(2)}, u32[]{:S(2)}) collective-permute-start(bf16[512,1280]{1,0:T(8,128)(2,1)S(1)} %slice_bitcast_fusion), channel_id=1, source_target_pairs={{0,4},{4,8},{8,12},{12,16},{16,20},{20,24},{24,28},{1,5},{5,9},{9,... | collective-permute-start | bytes 3932168 | tf_op jit(solution)/shard_map/ppermute | solution.py:261
  43.1 85.8 %collective-permute-start.11 = (bf16[512,1280]{1,0:T(8,128)(2,1)}, bf16[512,1280]{1,0:T(8,128)(2,1)}, u32[]{:S(2)}, u32[]{:S(2)}) collective-permute-start(bf16[512,1280]{1,0:T(8,128)(2,1)} %collective-permute-done), channel_id=1, source_target_pairs={{4,0},{8,4},{12,8},{16,12},{20,16},{24,20},{28,24},{5,1},{9,5},{13... | collective-permute-start | bytes 3932168 | tf_op jit(solution)/shard_map/ppermute | solution.py:272
  62.0 32.6 %collective-permute-start.7 = (bf16[512,1280]{1,0:T(8,128)(2,1)S(1)}, bf16[512,1280]{1,0:T(8,128)(2,1)}, u32[]{:S(2)}, u32[]{:S(2)}) collective-permute-start(bf16[512,1280]{1,0:T(8,128)(2,1)S(1)} %collective-permute-done.4.refs_3_), channel_id=1, source_target_pairs={{1,2},{2,1},{5,6},{6,5},{9,10},{10,9},{13,14},{14,13},{17,18},{18,... | collective-permute-start | bytes 3932168 | tf_op jit(solution)/shard_map/ppermute | solution.py:237
  66.6 31.6 %collective-permute-start.10 = (bf16[128,1280]{1,0:T(8,128)(2,1)S(1)}, bf16[128,1280]{1,0:T(8,128)(2,1)S(1)}, u32[]{:S(2)}, u32[]{:S(2)}) collective-permute-start(bf16[128,1280]{1,0:T(8,128)(2,1)S(1)} %slice_bitcast_fusion.3), channel_id=1, source_target_pairs={{1,0},{2,3},{5,4},{6,7},{9,8},{10,11},{13,12},{14,15},{17,16},{18,... | collective-permute-start | bytes 983048 | tf_op jit(solution)/shard_map/ppermute | solution.py:237
  69.6 42.4 %collective-permute-start.9 = (bf16[512,1280]{1,0:T(8,128)(2,1)S(1)}, bf16[512,1280]{1,0:T(8,128)(2,1)}, u32[]{:S(2)}, u32[]{:S(2)}) collective-permute-start(bf16[512,1280]{1,0:T(8,128)(2,1)S(1)} %fusion.2.refs_0_), channel_id=1, source_target_pairs={{0,1},{3,2},{4,5},{7,6},{8,9},{11,10},{12,13},{15,14},{16,17},{19,... | collective-permute-start | bytes 3932168 | tf_op jit(solution)/shard_map/ppermute | solution.py:237
  71.0 34.3 %collective-permute-start.12 = (bf16[512,1280]{1,0:T(8,128)(2,1)S(1)}, bf16[512,1280]{1,0:T(8,128)(2,1)S(1)}, u32[]{:S(2)}, u32[]{:S(2)}) collective-permute-start(bf16[512,1280]{1,0:T(8,128)(2,1)S(1)} %collective-permute-done.5.refs_5_), channel_id=1, source_target_pairs={{1,0},{2,3},{5,4},{6,7},{9,8},{10,11},{13,12},{14,15},{17,16},{18,... | collective-permute-start | bytes 3932168 | tf_op jit(solution)/shard_map/ppermute | solution.py:237
  94.6 31.0 %collective-permute-start.8 = (bf16[512,1280]{1,0:T(8,128)(2,1)S(1)}, bf16[512,1280]{1,0:T(8,128)(2,1)}, u32[]{:S(2)}, u32[]{:S(2)}) collective-permute-start(bf16[512,1280]{1,0:T(8,128)(2,1)S(1)} %fusion.2.refs_0_), channel_id=1, source_target_pairs={{1,2},{2,1},{5,6},{6,5},{9,10},{10,9},{13,14},{14,13},{17,18},{18,... | collective-permute-start | bytes 3932168 | tf_op jit(solution)/shard_map/ppermute | solution.py:237
  98.3 30.6 %collective-permute-start.16 = (bf16[512,1280]{1,0:T(8,128)(2,1)S(1)}, bf16[512,1280]{1,0:T(8,128)(2,1)}, u32[]{:S(2)}, u32[]{:S(2)}) collective-permute-start(bf16[512,1280]{1,0:T(8,128)(2,1)S(1)} %constant_dynamic-update-slice_fusion), channel_id=1, source_target_pairs={{0,4},{4,8},{8,12},{12,16},{16,20},{20,24},{24,28},{1,5},{5,9},{9,... | collective-permute-start | bytes 3932168 | tf_op jit(solution)/shard_map/ppermute | solution.py:273
  106.4 33.8 %collective-permute-start.13 = (bf16[512,1280]{1,0:T(8,128)(2,1)}, bf16[512,1280]{1,0:T(8,128)(2,1)}, u32[]{:S(2)}, u32[]{:S(2)}) collective-permute-start(bf16[512,1280]{1,0:T(8,128)(2,1)} %collective-permute-done.7.refs_7_), channel_id=1, source_target_pairs={{1,0},{2,3},{5,4},{6,7},{9,8},{10,11},{13,12},{14,15},{17,16},{18,... | collective-permute-start | bytes 3932168 | tf_op jit(solution)/shard_map/ppermute | solution.py:237
  125.5 30.2 %collective-permute-start.14 = (bf16[512,1280]{1,0:T(8,128)(2,1)}, bf16[512,1280]{1,0:T(8,128)(2,1)S(1)}, u32[]{:S(2)}, u32[]{:S(2)}) collective-permute-start(bf16[512,1280]{1,0:T(8,128)(2,1)} %collective-permute-done.9.refs_0_.refs_1_), channel_id=1, source_target_pairs={{1,2},{2,1},{5,6},{6,5},{9,10},{10,9},{13,14},{14,13},{17,18},{18,... | collective-permute-start | bytes 3932168 | tf_op jit(solution)/shard_map/ppermute | solution.py:237
  133.6 34.2 %collective-permute-start.17 = (bf16[512,1280]{1,0:T(8,128)(2,1)}, bf16[512,1280]{1,0:T(8,128)(2,1)}, u32[]{:S(2)}, u32[]{:S(2)}) collective-permute-start(bf16[512,1280]{1,0:T(8,128)(2,1)} %collective-permute-done.8.refs_1_.refs_3_), channel_id=1, source_target_pairs={{1,0},{2,3},{5,4},{6,7},{9,8},{10,11},{13,12},{14,15},{17,16},{18,... | collective-permute-start | bytes 3932168 | tf_op jit(solution)/shard_map/ppermute | solution.py:237
  155.8 31.7 %collective-permute-start.18 = (bf16[2,5,512,128]{3,2,1,0:T(8,128)(2,1)S(1)}, bf16[2,5,512,128]{3,2,1,0:T(8,128)(2,1)}, u32[]{:S(2)}, u32[]{:S(2)}) collective-permute-start(bf16[2,5,512,128]{3,2,1,0:T(8,128)(2,1)S(1)} %get-tuple-element.42.refs_3_), channel_id=1, source_target_pairs={{0,24},{1,25},{2,26},{3,27}} | collective-permute-start | bytes 3932168 | tf_op jit(solution)/shard_map/ppermute | solution.py:202
  157.5 29.9 %collective-permute-start.19 = (bf16[2,5,512,128]{3,2,1,0:T(8,128)(2,1)S(1)}, bf16[2,5,512,128]{3,2,1,0:T(8,128)(2,1)}, u32[]{:S(2)}, u32[]{:S(2)}) collective-permute-start(bf16[2,5,512,128]{3,2,1,0:T(8,128)(2,1)S(1)} %get-tuple-element.42.refs_3_), channel_id=1, source_target_pairs={{0,16},{1,17},{2,18},{3,19}} | collective-permute-start | bytes 3932168 | tf_op jit(solution)/shard_map/ppermute | solution.py:202
  159.3 47.4 %collective-permute-start.20 = (bf16[2,5,512,128]{3,2,1,0:T(8,128)(2,1)S(1)}, bf16[2,5,512,128]{3,2,1,0:T(8,128)(2,1)}, u32[]{:S(2)}, u32[]{:S(2)}) collective-permute-start(bf16[2,5,512,128]{3,2,1,0:T(8,128)(2,1)S(1)} %get-tuple-element.42.refs_3_), channel_id=1, source_target_pairs={{0,8},{1,9},{2,10},{3,11}} | collective-permute-start | bytes 3932168 | tf_op jit(solution)/shard_map/ppermute | solution.py:202
  160.8 47.5 %collective-permute-start.21 = (bf16[2,5,512,128]{3,2,1,0:T(8,128)(2,1)S(1)}, bf16[2,5,512,128]{3,2,1,0:T(8,128)(2,1)S(1)}, u32[]{:S(2)}, u32[]{:S(2)}) collective-permute-start(bf16[2,5,512,128]{3,2,1,0:T(8,128)(2,1)S(1)} %get-tuple-element.42.refs_3_), channel_id=1, source_target_pairs={{4,8},{8,12},{12,16},{16,20},{20,24},{24,28},{5,9},{9,13},{13,17},... | collective-permute-start | bytes 3932168 | tf_op jit(solution)/shard_map/ppermute | solution.py:283
  167.7 42.9 %collective-permute-start.15 = (bf16[512,1280]{1,0:T(8,128)(2,1)}, bf16[512,1280]{1,0:T(8,128)(2,1)S(1)}, u32[]{:S(2)}, u32[]{:S(2)}) collective-permute-start(bf16[512,1280]{1,0:T(8,128)(2,1)} %copy-done.8), channel_id=1, source_target_pairs={{1,0},{2,3},{5,4},{6,7},{9,8},{10,11},{13,12},{14,15},{17,16},{18,... | collective-permute-start | bytes 3932168 | tf_op jit(solution)/shard_map/ppermute | solution.py:237
  208.3 14.0 %collective-permute-start.22 = (bf16[2,5,512,128]{3,2,1,0:T(8,128)(2,1)S(1)}, bf16[2,5,512,128]{3,2,1,0:T(8,128)(2,1)}, u32[]{:S(2)}, u32[]{:S(2)}) collective-permute-start(bf16[2,5,512,128]{3,2,1,0:T(8,128)(2,1)S(1)} %select_select_fusion.refs_1_), channel_id=1, source_target_pairs={{0,4},{8,12},{16,20},{24,28},{1,5},{9,13},{17,21},{25,29},{2,6},{1... | collective-permute-start | bytes 3932168 | tf_op jit(solution)/shard_map/ppermute | solution.py:204
  220.4 9.4 %collective-permute-start.23 = (bf16[2,5,512,128]{3,2,1,0:T(8,128)(2,1)}, bf16[2,5,512,128]{3,2,1,0:T(8,128)(2,1)}, u32[]{:S(2)}, u32[]{:S(2)}) collective-permute-start(bf16[2,5,512,128]{3,2,1,0:T(8,128)(2,1)} %get-tuple-element.45.refs_4_), channel_id=1, source_target_pairs={{0,4},{1,5},{2,6},{3,7}} | collective-permute-start | bytes 3932168 | tf_op jit(solution)/shard_map/ppermute | solution.py:287
  (18 other events, 297.4 us)

commit v8 on v7

--- a/solution.py
+++ b/solution.py
@@ -194,15 +194,13 @@
     )(jnp.stack([anchor, frame, choice]).astype(jnp.int32), *args)
 
 
-def broadcast_first(x, axis, before):
+def broadcast_first(x, axis):
     count = lax.axis_size(axis)
     mine = lax.axis_index(axis)
     held = x
     for to in range(2, count, 2):
         held = jnp.where(mine == to, lax.ppermute(x, axis, [(0, to)]), held)
-    held, before = lax.optimization_barrier((held, before))
-    other = lax.ppermute(held, axis, [(i, i + 1) for i in range(0, count, 2)])
-    return (held, other), before
+    return held, lax.ppermute(held, axis, [(i, i + 1) for i in range(0, count, 2)])
 
 
 INWARD = [(0, 1), (3, 2)]
@@ -262,26 +260,26 @@
     raw.append(send(later[1, :cut], OUTWARD))
     mixed2 = mix_second(frames[0], frames[1], following, preceding, taps)
     inward1, middle1, raw[1], later = hold((inward1, middle1, raw[1], frames))
-    inward2, cross1, second1 = send(mixed2, INWARD), send(inward1, MIDDLE), send(middle1, OUTWARD)
+    cross1, second1 = send(inward1, MIDDLE), send(middle1, OUTWARD)
     raw.append(send(later[1, cut:], OUTWARD))
-    later2, cross1 = hold((mixed2, cross1))
-    middle2 = send(later2, MIDDLE)
-    cross1, second1 = hold((cross1, second1))
+    later2, cross1, second1, raw[0] = hold((mixed2, cross1, second1, raw[0]))
+    middle2, inward2 = send(later2, MIDDLE), send(later2, INWARD)
     third1 = send(cross1, OUTWARD)
     other_last = jnp.concatenate(raw[1:], axis=0)
     other_following = lax.ppermute(raw[0], "tm", downs)
     other_preceding = lax.ppermute(other_last, "tm", ups)
     first1 = mix_first(raw[0], other_last, other_following, outer_taps)
     first2 = mix_second(raw[0], other_last, other_following, other_preceding, outer_taps)
-    middle2, inward2 = hold((middle2, inward2))
+    middle2, inward2, first1, first2 = hold((middle2, inward2, first1, first2))
     cross2, second2 = send(inward2, MIDDLE), send(middle2, OUTWARD)
 
     sources1 = [(mixed1,), (inward1, first1), (middle1, second1), (cross1, third1)]
     q1, kv1 = project(sources1, info, weights, gains, after=(inward2, middle2), flops=10**10)
     kv1, cross2 = hold((kv1, cross2))
     third2 = send(cross2, OUTWARD)
-    shift1 = lax.ppermute(kv1, "tm", [(i, i + 1) for i in range(1, count - 1)])
-    anchor, shift1 = broadcast_first(kv1, "tm", shift1)
+    anchor = broadcast_first(kv1, "tm")
+    later1, _ = hold((kv1, anchor[0]))
+    shift1 = lax.ppermute(later1, "tm", [(i, i + 1) for i in range(1, count - 1)])
     raw2 = project([(mixed2,), (inward2, first2), (middle2, second2)], info_raw, weights, flops=10**10)
     q2, kv2 = project([(cross2, third2)], info_end, weights, gains, raw2, flops=10**10)
     shift2 = lax.ppermute(kv2, "tm", [(0, 1)])

time: 238 us -> 246 us (1.034); the launches traced: 237 us -> 242 us
  waiting for transfers between devices: 99 us -> 111 us
  starting transfers between devices: 67.4 us -> 59.2 us
    ppermute x1, waiting for transfers between devices: 0.01 us -> 11.1 us  [per_device(): other_following = lax.ppermute(raw[0], 'tm', downs)]
    ppermute x14, starting transfers between devices: 47.2 us -> 39 us  [send(): return lax.ppermute(x, 'head', pairs)]
    ppermute x3, waiting for transfers between devices: 19.2 us -> 11.9 us  [broadcast_first(): held = jnp.where(mine == to, lax.ppermute(x, axis, [(0, to)]), held)]
    ppermute x14, waiting for transfers between devices: 70 us -> 74.9 us  [send(): return lax.ppermute(x, 'head', pairs)]
    ppermute x1, waiting for transfers between devices: 0.01 us -> 3.53 us  [per_device(): other_preceding = lax.ppermute(other_last, 'tm', ups)]
  transfers between devices with their start and end apart: 24 -> 24, of which waited for: 9 -> 10; matrix products, arithmetic and copies ran while one was open for 5% -> 4% of each run, Pallas kernels for 19% -> 19%
where the time goes in v8:
time: 246 us; the launch traced here: 242 us
  waiting for transfers between devices  111 us (45%)
  starting transfers between devices  59.2 us (24%)
  Pallas kernels  54.5 us (22%)
  other arithmetic  9.35 us (4%)
  local copies, waits for them, and re-layouts  7.38 us (3%)
    ppermute x14, waiting for transfers between devices, send(): return lax.ppermute(x, 'head', pairs)  74.9 us
    pallas_call x3, Pallas kernels, project(): pl.pallas_call(functools.partial(project_body, pairs, len(after), acc is...  39.4 us
    ppermute x14, starting transfers between devices, send(): return lax.ppermute(x, 'head', pairs)  39 us
    pallas_call x2, Pallas kernels, attend(): pl.pallas_call(functools.partial(attend_body, 128, (len(anchors), len(opt...  15 us
    ppermute x3, waiting for transfers between devices, broadcast_first(): held = jnp.where(mine == to, lax.ppermute(x, axis, [(0, to)]), held)  11.9 us
    ppermute x1, waiting for transfers between devices, per_device(): other_following = lax.ppermute(raw[0], 'tm', downs)  11.1 us
    ppermute x1, waiting for transfers between devices, per_device(): following = lax.ppermute(frames[0], 'tm', downs)  9.82 us
    convert_element_type x3, other arithmetic, mix(): (centre + taps[0] * before + taps[1] * centre + taps[2] * after).astype(B...  7.57 us
  transfers between devices with their start and end apart: 24, of which 10 were waited for; matrix products, arithmetic and copies ran while one was open for 4% of the time, Pallas kernels for 19%

profile of v8, /device:TPU:10, one launch (start us, length us, event | category | flops | bytes accessed | tf_op | source)
XLA Modules:
  0.0 242.4 jit_solution(17001214005350330463)
XLA Ops:
  0.0 2.6 %slice_bitcast_fusion.1 = bf16[512,1280]{1,0:T(8,128)(2,1)} fusion(bf16[2,512,1280]{2,1,0:T(8,128)(2,1)} %param.7), kind=kLoop, calls=%fused_computation.26 | loop fusion | bytes 2621440 | tf_op jit(solution)/shard_map/squeeze | solution.py:261
  4.5 3.5 %collective-permute-start = (bf16[512,1280]{1,0:T(8,128)(2,1)}, bf16[512,1280]{1,0:T(8,128)(2,1)}, u32[]{:S(2)}, u32[]{:S(2)}) collective-permute-start(bf16[512,1280]{1,0:T(8,128)(2,1)} %slice_bitcast_fusion.1), channel_id=1, source_target_pairs={{1,0},{2,3},{5,4},{6,7},{9,8},{10,11},{13,12},{14,15},{17,16},{18,... | collective-permute-start | bytes 3932168 | tf_op jit(solution)/shard_map/ppermute | solution.py:235
  10.1 9.8 %collective-permute-done.2 = bf16[512,1280]{1,0:T(8,128)(2,1)} collective-permute-done((bf16[512,1280]{1,0:T(8,128)(2,1)}, bf16[512,1280]{1,0:T(8,128)(2,1)}, u32[]{:S(2)}, u32[]{:S(2)}) %collective-permute-start.2) | collective-permute-done | bytes 1310752 | tf_op jit(solution)/shard_map/ppermute | solution.py:254
  23.6 3.5 %collective-permute-start.5 = (bf16[512,1280]{1,0:T(8,128)(2,1)S(1)}, bf16[512,1280]{1,0:T(8,128)(2,1)S(1)}, u32[]{:S(2)}, u32[]{:S(2)}) collective-permute-start(bf16[512,1280]{1,0:T(8,128)(2,1)S(1)} %fusion.5.refs_2_), channel_id=1, source_target_pairs={{1,2},{2,1},{5,6},{6,5},{9,10},{10,9},{13,14},{14,13},{17,18},{18,... | collective-permute-start | bytes 3932168 | tf_op jit(solution)/shard_map/ppermute | solution.py:235
  27.1 9.1 %collective-permute-done.1 = f32[3,1280]{1,0:T(4,128)S(1)} collective-permute-done((f32[3,1280]{1,0:T(4,128)}, f32[3,1280]{1,0:T(4,128)S(1)}, u32[]{:S(2)}, u32[]{:S(2)}) %collective-permute-start.1) | collective-permute-done | bytes 15392 | tf_op jit(solution)/shard_map/ppermute | solution.py:235
  36.3 4.4 %collective-permute-start.6 = (bf16[384,1280]{1,0:T(8,128)(2,1)S(1)}, bf16[384,1280]{1,0:T(8,128)(2,1)S(1)}, u32[]{:S(2)}, u32[]{:S(2)}) collective-permute-start(bf16[384,1280]{1,0:T(8,128)(2,1)S(1)} %slice_bitcast_fusion.2), channel_id=1, source_target_pairs={{1,0},{2,3},{5,4},{6,7},{9,8},{10,11},{13,12},{14,15},{17,16},{18,... | collective-permute-start | bytes 2949128 | tf_op jit(solution)/shard_map/ppermute | solution.py:235
  42.8 18.9 %collective-permute-done.6 = bf16[384,1280]{1,0:T(8,128)(2,1)S(1)} collective-permute-done((bf16[384,1280]{1,0:T(8,128)(2,1)S(1)}, bf16[384,1280]{1,0:T(8,128)(2,1)S(1)}, u32[]{:S(2)}, u32[]{:S(2)}) %collective-permute-start.6) | collective-permute-done | bytes 983072 | tf_op jit(solution)/shard_map/ppermute | solution.py:235
  61.7 4.6 %collective-permute-start.7 = (bf16[512,1280]{1,0:T(8,128)(2,1)S(1)}, bf16[512,1280]{1,0:T(8,128)(2,1)}, u32[]{:S(2)}, u32[]{:S(2)}) collective-permute-start(bf16[512,1280]{1,0:T(8,128)(2,1)S(1)} %collective-permute-done.4.refs_3_), channel_id=1, source_target_pairs={{1,2},{2,1},{5,6},{6,5},{9,10},{10,9},{13,14},{14,13},{17,18},{18,... | collective-permute-start | bytes 3932168 | tf_op jit(solution)/shard_map/ppermute | solution.py:235
  70.7 31.4 %collective-permute-done.11 = bf16[128,1280]{1,0:T(8,128)(2,1)S(1)} collective-permute-done((bf16[128,1280]{1,0:T(8,128)(2,1)S(1)}, bf16[128,1280]{1,0:T(8,128)(2,1)S(1)}, u32[]{:S(2)}, u32[]{:S(2)}) %collective-permute-start.11) | collective-permute-done | bytes 327712 | tf_op jit(solution)/shard_map/ppermute | solution.py:235
  104.1 3.6 %collective-permute-start.12 = (bf16[512,1280]{1,0:T(8,128)(2,1)}, bf16[512,1280]{1,0:T(8,128)(2,1)S(1)}, u32[]{:S(2)}, u32[]{:S(2)}) collective-permute-start(bf16[512,1280]{1,0:T(8,128)(2,1)} %collective-permute-done), channel_id=1, source_target_pairs={{4,0},{8,4},{12,8},{16,12},{20,16},{24,20},{28,24},{5,1},{9,5},{13... | collective-permute-start | bytes 3932168 | tf_op jit(solution)/shard_map/ppermute | solution.py:269
  109.1 4.6 %collective-permute-start.9 = (bf16[512,1280]{1,0:T(8,128)(2,1)S(1)}, bf16[512,1280]{1,0:T(8,128)(2,1)}, u32[]{:S(2)}, u32[]{:S(2)}) collective-permute-start(bf16[512,1280]{1,0:T(8,128)(2,1)S(1)} %fusion.2.refs_0_), channel_id=1, source_target_pairs={{1,2},{2,1},{5,6},{6,5},{9,10},{10,9},{13,14},{14,13},{17,18},{18,... | collective-permute-start | bytes 3932168 | tf_op jit(solution)/shard_map/ppermute | solution.py:235
  113.7 3.8 %collective-permute-start.14 = (bf16[512,1280]{1,0:T(8,128)(2,1)}, bf16[512,1280]{1,0:T(8,128)(2,1)}, u32[]{:S(2)}, u32[]{:S(2)}) collective-permute-start(bf16[512,1280]{1,0:T(8,128)(2,1)} %collective-permute-done.7.refs_7_), channel_id=1, source_target_pairs={{1,0},{2,3},{5,4},{6,7},{9,8},{10,11},{13,12},{14,15},{17,16},{18,... | collective-permute-start | bytes 3932168 | tf_op jit(solution)/shard_map/ppermute | solution.py:235
  117.5 3.5 %collective-permute-done.13 = bf16[512,1280]{1,0:T(8,128)(2,1)S(1)} collective-permute-done((bf16[512,1280]{1,0:T(8,128)(2,1)S(1)}, bf16[512,1280]{1,0:T(8,128)(2,1)S(1)}, u32[]{:S(2)}, u32[]{:S(2)}) %collective-permute-start.13) | collective-permute-done | bytes 1310752 | tf_op jit(solution)/shard_map/ppermute | solution.py:270
  121.1 11.1 %collective-permute-done.12 = bf16[512,1280]{1,0:T(8,128)(2,1)S(1)} collective-permute-done((bf16[512,1280]{1,0:T(8,128)(2,1)}, bf16[512,1280]{1,0:T(8,128)(2,1)S(1)}, u32[]{:S(2)}, u32[]{:S(2)}) %collective-permute-start.12) | collective-permute-done | bytes 1310752 | tf_op jit(solution)/shard_map/ppermute | solution.py:269
  132.2 4.0 %fusion.11 = (bf16[512,1280]{1,0:T(8,128)(2,1)S(1)}, bf16[512,1280]{1,0:T(8,128)(2,1)}) fusion(bf16[512,1280]{1,0:T(8,128)(2,1)S(1)} %collective-permute-done.12, bf16[512,1280]{1,0:T(8,128)(2,1)S(1)} %constant_dynamic-update-slice_fusion, bf16[512,1280]{1,0:T(8,128)(2,1)} %collective-permute-done, bf16[512,1280]{1,0:T(8,128)(2,1)S(1)} %collective-permute-done.13, ...), kind=kLoop, calls=%fused_computation.19 | loop fusion | flops 17039360 | bytes 7879681 | tf_op jit(solution)/shard_map/convert_element_type | solution.py:213
  136.3 3.1 %collective-permute-done.10.refs_0_.refs_1_ = bf16[512,1280]{1,0:T(8,128)(2,1)} collective-permute-done((bf16[512,1280]{1,0:T(8,128)(2,1)S(1)}, bf16[512,1280]{1,0:T(8,128)(2,1)}, u32[]{:S(2)}, u32[]{:S(2)}) %collective-permute-start.10) | collective-permute-done | bytes 1310752 | tf_op jit(solution)/shard_map/ppermute | solution.py:235
  141.5 3.6 %collective-permute-start.15 = (bf16[512,1280]{1,0:T(8,128)(2,1)}, bf16[512,1280]{1,0:T(8,128)(2,1)}, u32[]{:S(2)}, u32[]{:S(2)}) collective-permute-start(bf16[512,1280]{1,0:T(8,128)(2,1)} %collective-permute-done.10.refs_0_.refs_1_), channel_id=1, source_target_pairs={{1,2},{2,1},{5,6},{6,5},{9,10},{10,9},{13,14},{14,13},{17,18},{18,... | collective-permute-start | bytes 3932168 | tf_op jit(solution)/shard_map/ppermute | solution.py:235
  149.1 15.5 %project_end.2 = (bf16[5,512,128]{2,1,0:T(8,128)(2,1)S(1)}, bf16[2,5,512,128]{3,2,1,0:T(8,128)(2,1)S(1)}) custom-call(s32[5]{0:T(128)S(1)} %stack.64.info, bf16[512,1280]{1,0:T(8,128)(2,1)} %collective-permute-done.10.refs_0_.refs_1_, bf16[512,1280]{1,0:T(8,128)(2,1)} %collective-permute-done.9.refs_1_.refs_3_, bf16[512,1280]{1,0:T(8,128)(2,1)S(1)} %copy-done.1, ...), custom_call_target="tpu_custom_call" | custom-call | flops 10000000000 | bytes 1 | tf_op jit(solution)/shard_map/project_end/pallas_call | solution.py:106
  164.6 10.3 %collective-permute-done.15.refs_0_ = bf16[512,1280]{1,0:T(8,128)(2,1)} collective-permute-done((bf16[512,1280]{1,0:T(8,128)(2,1)}, bf16[512,1280]{1,0:T(8,128)(2,1)}, u32[]{:S(2)}, u32[]{:S(2)}) %collective-permute-start.15) | collective-permute-done | bytes 1310752 | tf_op jit(solution)/shard_map/ppermute | solution.py:235
  182.7 13.7 %project_raw.1.refs_7_ = f32[512,1920]{1,0:T(8,128)} custom-call(s32[4]{0:T(128)S(1)} %pad_add_fusion.2.info, bf16[512,1280]{1,0:T(8,128)(2,1)S(1)} %copy-done.3, bf16[512,1280]{1,0:T(8,128)(2,1)} %collective-permute-done.10.refs_0_.refs_1_, bf16[512,1280]{1,0:T(8,128)(2,1)S(1)} %get-tuple-element.43.refs_2_, ...), custom_call_target="tpu_custom_call" | custom-call | flops 10000000000 | bytes 1 | tf_op jit(solution)/shard_map/project_raw/pallas_call | solution.py:106
  196.5 11.9 %collective-permute-done.20 = bf16[2,5,512,128]{3,2,1,0:T(8,128)(2,1)} collective-permute-done((bf16[2,5,512,128]{3,2,1,0:T(8,128)(2,1)S(1)}, bf16[2,5,512,128]{3,2,1,0:T(8,128)(2,1)}, u32[]{:S(2)}, u32[]{:S(2)}) %collective-permute-start.20) | collective-permute-done | bytes 1310752 | tf_op jit(solution)/shard_map/ppermute | solution.py:202
  214.2 10.2 %project_end.3 = (bf16[5,512,128]{2,1,0:T(8,128)(2,1)S(1)}, bf16[2,5,512,128]{3,2,1,0:T(8,128)(2,1)}) custom-call(s32[2]{0:T(128)S(1)} %pad_add_fusion.1.info, bf16[512,1280]{1,0:T(8,128)(2,1)} %collective-permute-done.15.refs_0_, bf16[512,1280]{1,0:T(8,128)(2,1)S(1)} %collective-permute-done.16.refs_1_, bf16[5120,640]{1,0:T(8,128)(2,1)} %refs_2_.1, ...), custom_call_target="tpu_custom_call" | custom-call | flops 10000000000 | bytes 1 | tf_op jit(solution)/shard_map/project_end/pallas_call | solution.py:106
  227.1 7.5 %attend.2.refs_6_ = bf16[2,512,640]{2,1,0:T(8,128)(2,1)} custom-call(s32[3]{0:T(128)S(1)} %get-tuple-element.58.info, bf16[5,512,128]{2,1,0:T(8,128)(2,1)S(1)} %get-tuple-element.48.refs_0_, bf16[2,5,512,128]{3,2,1,0:T(8,128)(2,1)S(1)} %select_select_fusion.refs_1_, bf16[2,5,512,128]{3,2,1,0:T(8,128)(2,1)} %collective-permute-done.21.refs_2_, ...), custom_call_target="tpu_custom_call" | custom-call | flops 1342177280 | bytes 3932160 | tf_op jit(solution)/shard_map/attend/pallas_call | solution.py:173
  234.7 7.5 %attend.3 = bf16[2,512,640]{2,1,0:T(8,128)(2,1)} custom-call(s32[3]{0:T(128)S(1)} %get-tuple-element.57.info, bf16[5,512,128]{2,1,0:T(8,128)(2,1)S(1)} %copy-done.5, bf16[2,5,512,128]{3,2,1,0:T(8,128)(2,1)S(1)} %select_select_fusion.refs_1_, bf16[2,5,512,128]{3,2,1,0:T(8,128)(2,1)} %collective-permute-done.21.refs_2_, ...), custom_call_target="tpu_custom_call", output_to_operand_aliasing={{}: (7, {})} | custom-call | flops 1342177280 | bytes 3932160 | tf_op jit(solution)/shard_map/attend/pallas_call | solution.py:173
  (71 shorter events, 39.7 us)
Async XLA Ops:
  2.6 17.3 %collective-permute-start.2 = (bf16[512,1280]{1,0:T(8,128)(2,1)}, bf16[512,1280]{1,0:T(8,128)(2,1)}, u32[]{:S(2)}, u32[]{:S(2)}) collective-permute-start(bf16[512,1280]{1,0:T(8,128)(2,1)} %slice_bitcast_fusion.1), channel_id=1, source_target_pairs={{4,0},{8,4},{12,8},{16,12},{20,16},{24,20},{28,24},{5,1},{9,5},{13... | collective-permute-start | bytes 3932168 | tf_op jit(solution)/shard_map/ppermute | solution.py:254
  4.5 31.7 %collective-permute-start = (bf16[512,1280]{1,0:T(8,128)(2,1)}, bf16[512,1280]{1,0:T(8,128)(2,1)}, u32[]{:S(2)}, u32[]{:S(2)}) collective-permute-start(bf16[512,1280]{1,0:T(8,128)(2,1)} %slice_bitcast_fusion.1), channel_id=1, source_target_pairs={{1,0},{2,3},{5,4},{6,7},{9,8},{10,11},{13,12},{14,15},{17,16},{18,... | collective-permute-start | bytes 3932168 | tf_op jit(solution)/shard_map/ppermute | solution.py:235
  8.0 28.2 %collective-permute-start.1 = (f32[3,1280]{1,0:T(4,128)}, f32[3,1280]{1,0:T(4,128)S(1)}, u32[]{:S(2)}, u32[]{:S(2)}) collective-permute-start(f32[3,1280]{1,0:T(4,128)} %param.8), channel_id=1, source_target_pairs={{1,0},{2,3},{5,4},{6,7},{9,8},{10,11},{13,12},{14,15},{17,16},{18,... | collective-permute-start | bytes 46088 | tf_op jit(solution)/shard_map/ppermute | solution.py:235
  22.3 39.3 %collective-permute-start.4 = (bf16[512,1280]{1,0:T(8,128)(2,1)S(1)}, bf16[512,1280]{1,0:T(8,128)(2,1)S(1)}, u32[]{:S(2)}, u32[]{:S(2)}) collective-permute-start(bf16[512,1280]{1,0:T(8,128)(2,1)S(1)} %fusion.5.refs_2_), channel_id=1, source_target_pairs={{0,1},{3,2},{4,5},{7,6},{8,9},{11,10},{12,13},{15,14},{16,17},{19,... | collective-permute-start | bytes 3932168 | tf_op jit(solution)/shard_map/ppermute | solution.py:235
  23.6 38.0 %collective-permute-start.5 = (bf16[512,1280]{1,0:T(8,128)(2,1)S(1)}, bf16[512,1280]{1,0:T(8,128)(2,1)S(1)}, u32[]{:S(2)}, u32[]{:S(2)}) collective-permute-start(bf16[512,1280]{1,0:T(8,128)(2,1)S(1)} %fusion.5.refs_2_), channel_id=1, source_target_pairs={{1,2},{2,1},{5,6},{6,5},{9,10},{10,9},{13,14},{14,13},{17,18},{18,... | collective-permute-start | bytes 3932168 | tf_op jit(solution)/shard_map/ppermute | solution.py:235
  36.3 25.4 %collective-permute-start.6 = (bf16[384,1280]{1,0:T(8,128)(2,1)S(1)}, bf16[384,1280]{1,0:T(8,128)(2,1)S(1)}, u32[]{:S(2)}, u32[]{:S(2)}) collective-permute-start(bf16[384,1280]{1,0:T(8,128)(2,1)S(1)} %slice_bitcast_fusion.2), channel_id=1, source_target_pairs={{1,0},{2,3},{5,4},{6,7},{9,8},{10,11},{13,12},{14,15},{17,16},{18,... | collective-permute-start | bytes 2949128 | tf_op jit(solution)/shard_map/ppermute | solution.py:235
  40.9 28.5 %collective-permute-start.3 = (bf16[512,1280]{1,0:T(8,128)(2,1)S(1)}, bf16[512,1280]{1,0:T(8,128)(2,1)S(1)}, u32[]{:S(2)}, u32[]{:S(2)}) collective-permute-start(bf16[512,1280]{1,0:T(8,128)(2,1)S(1)} %slice_bitcast_fusion), channel_id=1, source_target_pairs={{0,4},{4,8},{8,12},{12,16},{16,20},{20,24},{24,28},{1,5},{5,9},{9,... | collective-permute-start | bytes 3932168 | tf_op jit(solution)/shard_map/ppermute | solution.py:259
  61.7 42.4 %collective-permute-start.7 = (bf16[512,1280]{1,0:T(8,128)(2,1)S(1)}, bf16[512,1280]{1,0:T(8,128)(2,1)}, u32[]{:S(2)}, u32[]{:S(2)}) collective-permute-start(bf16[512,1280]{1,0:T(8,128)(2,1)S(1)} %collective-permute-done.4.refs_3_), channel_id=1, source_target_pairs={{1,2},{2,1},{5,6},{6,5},{9,10},{10,9},{13,14},{14,13},{17,18},{18,... | collective-permute-start | bytes 3932168 | tf_op jit(solution)/shard_map/ppermute | solution.py:235
  66.3 37.8 %collective-permute-start.8 = (bf16[512,1280]{1,0:T(8,128)(2,1)S(1)}, bf16[512,1280]{1,0:T(8,128)(2,1)S(1)}, u32[]{:S(2)}, u32[]{:S(2)}) collective-permute-start(bf16[512,1280]{1,0:T(8,128)(2,1)S(1)} %collective-permute-done.5.refs_5_), channel_id=1, source_target_pairs={{1,0},{2,3},{5,4},{6,7},{9,8},{10,11},{13,12},{14,15},{17,16},{18,... | collective-permute-start | bytes 3932168 | tf_op jit(solution)/shard_map/ppermute | solution.py:235
  68.1 34.0 %collective-permute-start.11 = (bf16[128,1280]{1,0:T(8,128)(2,1)S(1)}, bf16[128,1280]{1,0:T(8,128)(2,1)S(1)}, u32[]{:S(2)}, u32[]{:S(2)}) collective-permute-start(bf16[128,1280]{1,0:T(8,128)(2,1)S(1)} %slice_bitcast_fusion.3), channel_id=1, source_target_pairs={{1,0},{2,3},{5,4},{6,7},{9,8},{10,11},{13,12},{14,15},{17,16},{18,... | collective-permute-start | bytes 983048 | tf_op jit(solution)/shard_map/ppermute | solution.py:235
  102.1 18.9 %collective-permute-start.13 = (bf16[512,1280]{1,0:T(8,128)(2,1)S(1)}, bf16[512,1280]{1,0:T(8,128)(2,1)S(1)}, u32[]{:S(2)}, u32[]{:S(2)}) collective-permute-start(bf16[512,1280]{1,0:T(8,128)(2,1)S(1)} %constant_dynamic-update-slice_fusion), channel_id=1, source_target_pairs={{0,4},{4,8},{8,12},{12,16},{16,20},{20,24},{24,28},{1,5},{5,9},{9,... | collective-permute-start | bytes 3932168 | tf_op jit(solution)/shard_map/ppermute | solution.py:270
  104.1 28.1 %collective-permute-start.12 = (bf16[512,1280]{1,0:T(8,128)(2,1)}, bf16[512,1280]{1,0:T(8,128)(2,1)S(1)}, u32[]{:S(2)}, u32[]{:S(2)}) collective-permute-start(bf16[512,1280]{1,0:T(8,128)(2,1)} %collective-permute-done), channel_id=1, source_target_pairs={{4,0},{8,4},{12,8},{16,12},{20,16},{24,20},{28,24},{5,1},{9,5},{13... | collective-permute-start | bytes 3932168 | tf_op jit(solution)/shard_map/ppermute | solution.py:269
  107.7 31.6 %collective-permute-start.10 = (bf16[512,1280]{1,0:T(8,128)(2,1)S(1)}, bf16[512,1280]{1,0:T(8,128)(2,1)}, u32[]{:S(2)}, u32[]{:S(2)}) collective-permute-start(bf16[512,1280]{1,0:T(8,128)(2,1)S(1)} %fusion.2.refs_0_), channel_id=1, source_target_pairs={{0,1},{3,2},{4,5},{7,6},{8,9},{11,10},{12,13},{15,14},{16,17},{19,... | collective-permute-start | bytes 3932168 | tf_op jit(solution)/shard_map/ppermute | solution.py:235
  109.1 32.4 %collective-permute-start.9 = (bf16[512,1280]{1,0:T(8,128)(2,1)S(1)}, bf16[512,1280]{1,0:T(8,128)(2,1)}, u32[]{:S(2)}, u32[]{:S(2)}) collective-permute-start(bf16[512,1280]{1,0:T(8,128)(2,1)S(1)} %fusion.2.refs_0_), channel_id=1, source_target_pairs={{1,2},{2,1},{5,6},{6,5},{9,10},{10,9},{13,14},{14,13},{17,18},{18,... | collective-permute-start | bytes 3932168 | tf_op jit(solution)/shard_map/ppermute | solution.py:235
  113.7 34.0 %collective-permute-start.14 = (bf16[512,1280]{1,0:T(8,128)(2,1)}, bf16[512,1280]{1,0:T(8,128)(2,1)}, u32[]{:S(2)}, u32[]{:S(2)}) collective-permute-start(bf16[512,1280]{1,0:T(8,128)(2,1)} %collective-permute-done.7.refs_7_), channel_id=1, source_target_pairs={{1,0},{2,3},{5,4},{6,7},{9,8},{10,11},{13,12},{14,15},{17,16},{18,... | collective-permute-start | bytes 3932168 | tf_op jit(solution)/shard_map/ppermute | solution.py:235
  141.5 33.4 %collective-permute-start.15 = (bf16[512,1280]{1,0:T(8,128)(2,1)}, bf16[512,1280]{1,0:T(8,128)(2,1)}, u32[]{:S(2)}, u32[]{:S(2)}) collective-permute-start(bf16[512,1280]{1,0:T(8,128)(2,1)} %collective-permute-done.10.refs_0_.refs_1_), channel_id=1, source_target_pairs={{1,2},{2,1},{5,6},{6,5},{9,10},{10,9},{13,14},{14,13},{17,18},{18,... | collective-permute-start | bytes 3932168 | tf_op jit(solution)/shard_map/ppermute | solution.py:235
  145.3 36.1 %collective-permute-start.17 = (bf16[512,1280]{1,0:T(8,128)(2,1)}, bf16[512,1280]{1,0:T(8,128)(2,1)}, u32[]{:S(2)}, u32[]{:S(2)}) collective-permute-start(bf16[512,1280]{1,0:T(8,128)(2,1)} %collective-permute-done.9.refs_1_.refs_3_), channel_id=1, source_target_pairs={{1,0},{2,3},{5,4},{6,7},{9,8},{10,11},{13,12},{14,15},{17,16},{18,... | collective-permute-start | bytes 3932168 | tf_op jit(solution)/shard_map/ppermute | solution.py:235
  174.9 21.5 %collective-permute-start.18 = (bf16[2,5,512,128]{3,2,1,0:T(8,128)(2,1)S(1)}, bf16[2,5,512,128]{3,2,1,0:T(8,128)(2,1)}, u32[]{:S(2)}, u32[]{:S(2)}) collective-permute-start(bf16[2,5,512,128]{3,2,1,0:T(8,128)(2,1)S(1)} %get-tuple-element.46.refs_3_), channel_id=1, source_target_pairs={{0,24},{1,25},{2,26},{3,27}} | collective-permute-start | bytes 3932168 | tf_op jit(solution)/shard_map/ppermute | solution.py:202
  176.6 19.8 %collective-permute-start.19 = (bf16[2,5,512,128]{3,2,1,0:T(8,128)(2,1)S(1)}, bf16[2,5,512,128]{3,2,1,0:T(8,128)(2,1)}, u32[]{:S(2)}, u32[]{:S(2)}) collective-permute-start(bf16[2,5,512,128]{3,2,1,0:T(8,128)(2,1)S(1)} %get-tuple-element.46.refs_3_), channel_id=1, source_target_pairs={{0,16},{1,17},{2,18},{3,19}} | collective-permute-start | bytes 3932168 | tf_op jit(solution)/shard_map/ppermute | solution.py:202
  178.3 30.0 %collective-permute-start.20 = (bf16[2,5,512,128]{3,2,1,0:T(8,128)(2,1)S(1)}, bf16[2,5,512,128]{3,2,1,0:T(8,128)(2,1)}, u32[]{:S(2)}, u32[]{:S(2)}) collective-permute-start(bf16[2,5,512,128]{3,2,1,0:T(8,128)(2,1)S(1)} %get-tuple-element.46.refs_3_), channel_id=1, source_target_pairs={{0,8},{1,9},{2,10},{3,11}} | collective-permute-start | bytes 3932168 | tf_op jit(solution)/shard_map/ppermute | solution.py:202
  179.8 34.4 %collective-permute-start.16 = (bf16[512,1280]{1,0:T(8,128)(2,1)}, bf16[512,1280]{1,0:T(8,128)(2,1)S(1)}, u32[]{:S(2)}, u32[]{:S(2)}) collective-permute-start(bf16[512,1280]{1,0:T(8,128)(2,1)} %collective-permute-done.15.refs_0_), channel_id=1, source_target_pairs={{1,0},{2,3},{5,4},{6,7},{9,8},{10,11},{13,12},{14,15},{17,16},{18,... | collective-permute-start | bytes 3932168 | tf_op jit(solution)/shard_map/ppermute | solution.py:235
  209.9 17.2 %collective-permute-start.21 = (bf16[2,5,512,128]{3,2,1,0:T(8,128)(2,1)S(1)}, bf16[2,5,512,128]{3,2,1,0:T(8,128)(2,1)}, u32[]{:S(2)}, u32[]{:S(2)}) collective-permute-start(bf16[2,5,512,128]{3,2,1,0:T(8,128)(2,1)S(1)} %select_select_fusion.refs_1_), channel_id=1, source_target_pairs={{0,4},{8,12},{16,20},{24,28},{1,5},{9,13},{17,21},{25,29},{2,6},{1... | collective-permute-start | bytes 3932168 | tf_op jit(solution)/shard_map/ppermute | solution.py:203
  212.3 22.3 %collective-permute-start.22 = (bf16[2,5,512,128]{3,2,1,0:T(8,128)(2,1)S(1)}, bf16[2,5,512,128]{3,2,1,0:T(8,128)(2,1)}, u32[]{:S(2)}, u32[]{:S(2)}) collective-permute-start(bf16[2,5,512,128]{3,2,1,0:T(8,128)(2,1)S(1)} %get-tuple-element.46.refs_3_), channel_id=1, source_target_pairs={{4,8},{8,12},{12,16},{16,20},{20,24},{24,28},{5,9},{9,13},{13,17},... | collective-permute-start | bytes 3932168 | tf_op jit(solution)/shard_map/ppermute | solution.py:282
  225.3 9.3 %collective-permute-start.23 = (bf16[2,5,512,128]{3,2,1,0:T(8,128)(2,1)}, bf16[2,5,512,128]{3,2,1,0:T(8,128)(2,1)}, u32[]{:S(2)}, u32[]{:S(2)}) collective-permute-start(bf16[2,5,512,128]{3,2,1,0:T(8,128)(2,1)} %get-tuple-element.47.refs_4_), channel_id=1, source_target_pairs={{0,4},{1,5},{2,6},{3,7}} | collective-permute-start | bytes 3932168 | tf_op jit(solution)/shard_map/ppermute | solution.py:285
  (12 other events, 163.8 us)

commit v9 on v8

--- a/solution.py
+++ b/solution.py
@@ -229,7 +229,6 @@
     ups = [(i, i + 1) for i in range(count - 1)]
     downs = [(j, i) for i, j in ups]
     start = pos == 0
-    cut = 3 * frames.shape[1] // 4
 
     def send(x, pairs):
         return lax.ppermute(x, "head", pairs)
@@ -250,26 +249,24 @@
             scales,
         )
 
-    raw = [send(frames[0], OUTWARD)]
+    raw_first, raw_last = send(frames[0], OUTWARD), send(frames[1], OUTWARD)
+    all_taps = lax.all_gather(taps, "head", axis=0)
+    outer_taps = lax.dynamic_index_in_dim(all_taps, pair, axis=0, keepdims=False)
     following = lax.ppermute(frames[0], "tm", downs)
     mixed1 = mix_first(frames[0], frames[1], following, taps)
-    outer_taps = send(taps, OUTWARD)
     inward1, middle1 = send(mixed1, INWARD), send(mixed1, MIDDLE)
-    later, raw[0], outer_taps, _ = hold((frames, raw[0], outer_taps, mixed1))
+    later, _ = hold((frames, mixed1))
     preceding = lax.ppermute(later[1], "tm", ups)
-    raw.append(send(later[1, :cut], OUTWARD))
     mixed2 = mix_second(frames[0], frames[1], following, preceding, taps)
-    inward1, middle1, raw[1], later = hold((inward1, middle1, raw[1], frames))
+    raw_following = lax.ppermute(raw_first, "tm", downs)
+    inward1, middle1, raw_last = hold((inward1, middle1, raw_last))
     cross1, second1 = send(inward1, MIDDLE), send(middle1, OUTWARD)
-    raw.append(send(later[1, cut:], OUTWARD))
-    later2, cross1, second1, raw[0] = hold((mixed2, cross1, second1, raw[0]))
+    raw_preceding = lax.ppermute(raw_last, "tm", ups)
+    later2, cross1, second1, raw_following = hold((mixed2, cross1, second1, raw_following))
     middle2, inward2 = send(later2, MIDDLE), send(later2, INWARD)
     third1 = send(cross1, OUTWARD)
-    other_last = jnp.concatenate(raw[1:], axis=0)
-    other_following = lax.ppermute(raw[0], "tm", downs)
-    other_preceding = lax.ppermute(other_last, "tm", ups)
-    first1 = mix_first(raw[0], other_last, other_following, outer_taps)
-    first2 = mix_second(raw[0], other_last, other_following, other_preceding, outer_taps)
+    first1 = mix_first(raw_first, raw_last, raw_following, outer_taps)
+    first2 = mix_second(raw_first, raw_last, raw_following, raw_preceding, outer_taps)
     middle2, inward2, first1, first2 = hold((middle2, inward2, first1, first2))
     cross2, second2 = send(inward2, MIDDLE), send(middle2, OUTWARD)
 

time: 246 us -> 264 us (1.073)
  the two profiles are of different devices: /device:TPU:10 before, /device:TPU:0 now
where the time goes in v9:
time: 264 us
  waiting for transfers between devices  91.7 us (35%)
  starting transfers between devices  66.3 us (25%)
  Pallas kernels  51.9 us (20%)
  blocking collectives  35.4 us (13%)
  local copies, waits for them, and re-layouts  9.45 us (4%)
  other arithmetic  8.41 us (3%)
    ppermute x12, waiting for transfers between devices, send(): return lax.ppermute(x, 'head', pairs)  84 us
    pallas_call x3, Pallas kernels, project(): pl.pallas_call(functools.partial(project_body, pairs, len(after), acc is...  38.3 us
    all_gather x1, blocking collectives, per_device(): all_taps = lax.all_gather(taps, 'head', axis=0)  35.4 us
    ppermute x12, starting transfers between devices, send(): return lax.ppermute(x, 'head', pairs)  21.8 us
    ppermute x1, starting transfers between devices, per_device(): preceding = lax.ppermute(later[1], 'tm', ups)  16.2 us
    pallas_call x2, Pallas kernels, attend(): pl.pallas_call(functools.partial(attend_body, 128, (len(anchors), len(opt...  13.6 us
    ppermute x3, starting transfers between devices, broadcast_first(): held = jnp.where(mine == to, lax.ppermute(x, axis, [(0, to)]), held)  11.2 us
    ppermute x1, starting transfers between devices, per_device(): shift2 = lax.ppermute(kv2, 'tm', [(0, 1)])  8.24 us
  transfers between devices with their start and end apart: 22, of which 6 were waited for; matrix products, arithmetic and copies ran while one was open for 3% of the time, Pallas kernels for 17%

profile of v9, /device:TPU:0, one launch (start us, length us, event | category | flops | bytes accessed | tf_op | source)
XLA Modules:
  0.0 263.7 jit_solution(6204193797776170417)
XLA Ops:
  0.0 3.5 %slice_bitcast_fusion.2 = (bf16[512,1280]{1,0:T(8,128)(2,1)}, bf16[512,1280]{1,0:T(8,128)(2,1)}) fusion(bf16[2,512,1280]{2,1,0:T(8,128)(2,1)} %param.7), kind=kLoop, calls=%fused_computation.23 | loop fusion | bytes 5242880 | tf_op jit(solution)/shard_map/squeeze | solution.py:260
  9.9 6.1 %collective-permute-start.2 = (bf16[512,1280]{1,0:T(8,128)(2,1)S(1)}, bf16[512,1280]{1,0:T(8,128)(2,1)S(1)}, u32[]{:S(2)}, u32[]{:S(2)}) collective-permute-start(bf16[512,1280]{1,0:T(8,128)(2,1)S(1)} %fusion.5.refs_2_), channel_id=1, source_target_pairs={{0,1},{3,2},{4,5},{7,6},{8,9},{11,10},{12,13},{15,14},{16,17},{19,... | collective-permute-start | bytes 3932168 | tf_op jit(solution)/shard_map/ppermute | solution.py:234
  17.9 16.2 %collective-permute-start.1 = (bf16[512,1280]{1,0:T(8,128)(2,1)S(1)}, bf16[512,1280]{1,0:T(8,128)(2,1)S(1)}, u32[]{:S(2)}, u32[]{:S(2)}) collective-permute-start(bf16[512,1280]{1,0:T(8,128)(2,1)S(1)} %slice_bitcast_fusion), channel_id=1, source_target_pairs={{0,4},{4,8},{8,12},{12,16},{16,20},{20,24},{24,28},{1,5},{5,9},{9,... | collective-permute-start | bytes 3932168 | tf_op jit(solution)/shard_map/ppermute | solution.py:259
  34.2 4.6 %collective-permute-done.7 = bf16[512,1280]{1,0:T(8,128)(2,1)} collective-permute-done((bf16[512,1280]{1,0:T(8,128)(2,1)}, bf16[512,1280]{1,0:T(8,128)(2,1)}, u32[]{:S(2)}, u32[]{:S(2)}) %collective-permute-start.7) | collective-permute-done | bytes 1310752 | tf_op jit(solution)/shard_map/ppermute | solution.py:234
  40.0 26.8 %collective-permute-done.4 = bf16[512,1280]{1,0:T(8,128)(2,1)} collective-permute-done((bf16[512,1280]{1,0:T(8,128)(2,1)}, bf16[512,1280]{1,0:T(8,128)(2,1)}, u32[]{:S(2)}, u32[]{:S(2)}) %collective-permute-start.4) | collective-permute-done | bytes 1310752 | tf_op jit(solution)/shard_map/ppermute | solution.py:234
  68.9 2.2 collective-permute-start.11
  71.1 2.5 fusion.2.refs_0_
  73.7 28.8 %collective-permute-done.6.refs_6_ = bf16[512,1280]{1,0:T(8,128)(2,1)S(1)} collective-permute-done((bf16[512,1280]{1,0:T(8,128)(2,1)S(1)}, bf16[512,1280]{1,0:T(8,128)(2,1)S(1)}, u32[]{:S(2)}, u32[]{:S(2)}) %collective-permute-start.6) | collective-permute-done | bytes 1310752 | tf_op jit(solution)/shard_map/ppermute | solution.py:234
  102.5 2.5 collective-permute-start.10
  106.8 35.4 %all-gather.1 = f32[4,3,1280]{2,1,0:T(4,128)S(1)} all-gather(f32[1,3,1280]{2,1,0:T(4,128)S(1)} %bitcast.24), channel_id=2, replica_groups=mesh['tm'=8,'head'=4] {'head'}, dimensions={0}, use_global_device_ids=true | all-gather | bytes 76800 | tf_op jit(solution)/shard_map/all_gather | solution.py:253
  144.5 4.4 %fusion.11 = (bf16[512,1280]{1,0:T(8,128)(2,1)S(1)}, bf16[512,1280]{1,0:T(8,128)(2,1)}) fusion(bf16[512,1280]{1,0:T(8,128)(2,1)} %copy-done.8, bf16[512,1280]{1,0:T(8,128)(2,1)} %collective-permute-done.4, bf16[512,1280]{1,0:T(8,128)(2,1)} %collective-permute-done.7, bf16[512,1280]{1,0:T(8,128)(2,1)} %copy-done.9, f32[1280]{0:T(1024)S(1)} %get-tuple-element.45, ...), kind=kLoop, calls=%fused_computation.19 | loop fusion | flops 17039360 | bytes 7879681 | tf_op jit(solution)/shard_map/convert_element_type | solution.py:213
  148.9 1.8 collective-permute-start.13
  152.3 23.8 %collective-permute-done.12.refs_8_ = bf16[512,1280]{1,0:T(8,128)(2,1)} collective-permute-done((bf16[512,1280]{1,0:T(8,128)(2,1)}, bf16[512,1280]{1,0:T(8,128)(2,1)}, u32[]{:S(2)}, u32[]{:S(2)}) %collective-permute-start.12) | collective-permute-done | bytes 1310752 | tf_op jit(solution)/shard_map/ppermute | solution.py:234
  177.4 15.5 %project_end.2 = (bf16[5,512,128]{2,1,0:T(8,128)(2,1)S(1)}, bf16[2,5,512,128]{3,2,1,0:T(8,128)(2,1)S(1)}) custom-call(s32[5]{0:T(128)S(1)} %stack.64.info, bf16[512,1280]{1,0:T(8,128)(2,1)} %collective-permute-done.10.refs_0_.refs_1_, bf16[512,1280]{1,0:T(8,128)(2,1)} %collective-permute-done.9.refs_1_.refs_3_, bf16[512,1280]{1,0:T(8,128)(2,1)S(1)} %copy-done.1, ...), custom_call_target="tpu_custom_call" | custom-call | flops 10000000000 | bytes 1 | tf_op jit(solution)/shard_map/project_end/pallas_call | solution.py:106
  193.0 6.4 %collective-permute-start.16 = (bf16[2,5,512,128]{3,2,1,0:T(8,128)(2,1)S(1)}, bf16[2,5,512,128]{3,2,1,0:T(8,128)(2,1)}, u32[]{:S(2)}, u32[]{:S(2)}) collective-permute-start(bf16[2,5,512,128]{3,2,1,0:T(8,128)(2,1)S(1)} %get-tuple-element.40.refs_3_), channel_id=1, source_target_pairs={{0,24},{1,25},{2,26},{3,27}} | collective-permute-start | bytes 3932168 | tf_op jit(solution)/shard_map/ppermute | solution.py:202
  199.4 2.4 collective-permute-start.17
  201.8 2.4 collective-permute-start.18
  207.2 13.8 %project_raw.1.refs_7_ = f32[512,1920]{1,0:T(8,128)} custom-call(s32[4]{0:T(128)S(1)} %pad_add_fusion.2.info, bf16[512,1280]{1,0:T(8,128)(2,1)S(1)} %copy-done.3, bf16[512,1280]{1,0:T(8,128)(2,1)} %collective-permute-done.10.refs_0_.refs_1_, bf16[512,1280]{1,0:T(8,128)(2,1)S(1)} %get-tuple-element.37.refs_2_, ...), custom_call_target="tpu_custom_call" | custom-call | flops 10000000000 | bytes 1 | tf_op jit(solution)/shard_map/project_raw/pallas_call | solution.py:106
  221.0 6.4 %collective-permute-done.18 = bf16[2,5,512,128]{3,2,1,0:T(8,128)(2,1)} collective-permute-done((bf16[2,5,512,128]{3,2,1,0:T(8,128)(2,1)S(1)}, bf16[2,5,512,128]{3,2,1,0:T(8,128)(2,1)}, u32[]{:S(2)}, u32[]{:S(2)}) %collective-permute-start.18) | collective-permute-done | bytes 1310752 | tf_op jit(solution)/shard_map/ppermute | solution.py:202
  227.6 2.4 collective-permute-start.19
  231.8 9.0 %project_end.3 = (bf16[5,512,128]{2,1,0:T(8,128)(2,1)S(1)}, bf16[2,5,512,128]{3,2,1,0:T(8,128)(2,1)}) custom-call(s32[2]{0:T(128)S(1)} %pad_add_fusion.1.info, bf16[512,1280]{1,0:T(8,128)(2,1)} %collective-permute-done.13.refs_0_, bf16[512,1280]{1,0:T(8,128)(2,1)S(1)} %collective-permute-done.14.refs_1_, bf16[5120,640]{1,0:T(8,128)(2,1)} %refs_2_.1, ...), custom_call_target="tpu_custom_call" | custom-call | flops 10000000000 | bytes 1 | tf_op jit(solution)/shard_map/project_end/pallas_call | solution.py:106
  241.6 8.2 %collective-permute-start.21 = (bf16[2,5,512,128]{3,2,1,0:T(8,128)(2,1)}, bf16[2,5,512,128]{3,2,1,0:T(8,128)(2,1)}, u32[]{:S(2)}, u32[]{:S(2)}) collective-permute-start(bf16[2,5,512,128]{3,2,1,0:T(8,128)(2,1)} %get-tuple-element.41.refs_4_), channel_id=1, source_target_pairs={{0,4},{1,5},{2,6},{3,7}} | collective-permute-start | bytes 3932168 | tf_op jit(solution)/shard_map/ppermute | solution.py:282
  249.9 6.8 %attend.2.refs_6_ = bf16[2,512,640]{2,1,0:T(8,128)(2,1)} custom-call(s32[3]{0:T(128)S(1)} %get-tuple-element.54.info, bf16[5,512,128]{2,1,0:T(8,128)(2,1)S(1)} %get-tuple-element.42.refs_0_, bf16[2,5,512,128]{3,2,1,0:T(8,128)(2,1)S(1)} %select_select_fusion.refs_1_, bf16[2,5,512,128]{3,2,1,0:T(8,128)(2,1)} %collective-permute-done.19.refs_2_, ...), custom_call_target="tpu_custom_call" | custom-call | flops 1342177280 | bytes 3932160 | tf_op jit(solution)/shard_map/attend/pallas_call | solution.py:173
  256.7 6.8 %attend.3 = bf16[2,512,640]{2,1,0:T(8,128)(2,1)} custom-call(s32[3]{0:T(128)S(1)} %get-tuple-element.53.info, bf16[5,512,128]{2,1,0:T(8,128)(2,1)S(1)} %copy-done.5, bf16[2,5,512,128]{3,2,1,0:T(8,128)(2,1)S(1)} %select_select_fusion.refs_1_, bf16[2,5,512,128]{3,2,1,0:T(8,128)(2,1)} %collective-permute-done.19.refs_2_, ...), custom_call_target="tpu_custom_call", output_to_operand_aliasing={{}: (7, {})} | custom-call | flops 1342177280 | bytes 3932160 | tf_op jit(solution)/shard_map/attend/pallas_call | solution.py:173
  (74 shorter events, 24.4 us)
Async XLA Ops:
  3.5 5.3 %collective-permute-start = (bf16[512,1280]{1,0:T(8,128)(2,1)}, bf16[512,1280]{1,0:T(8,128)(2,1)}, u32[]{:S(2)}, u32[]{:S(2)}) collective-permute-start(bf16[512,1280]{1,0:T(8,128)(2,1)} %get-tuple-element.52), channel_id=1, source_target_pairs={{4,0},{8,4},{12,8},{16,12},{20,16},{24,20},{28,24},{5,1},{9,5},{13... | collective-permute-start | bytes 3932168 | tf_op jit(solution)/shard_map/ppermute | solution.py:255
  4.8 33.9 %collective-permute-start.7 = (bf16[512,1280]{1,0:T(8,128)(2,1)}, bf16[512,1280]{1,0:T(8,128)(2,1)}, u32[]{:S(2)}, u32[]{:S(2)}) collective-permute-start(bf16[512,1280]{1,0:T(8,128)(2,1)} %get-tuple-element.52), channel_id=1, source_target_pairs={{1,0},{2,3},{5,4},{6,7},{9,8},{10,11},{13,12},{14,15},{17,16},{18,... | collective-permute-start | bytes 3932168 | tf_op jit(solution)/shard_map/ppermute | solution.py:234
  6.1 60.7 %collective-permute-start.4 = (bf16[512,1280]{1,0:T(8,128)(2,1)}, bf16[512,1280]{1,0:T(8,128)(2,1)}, u32[]{:S(2)}, u32[]{:S(2)}) collective-permute-start(bf16[512,1280]{1,0:T(8,128)(2,1)} %get-tuple-element.51), channel_id=1, source_target_pairs={{1,0},{2,3},{5,4},{6,7},{9,8},{10,11},{13,12},{14,15},{17,16},{18,... | collective-permute-start | bytes 3932168 | tf_op jit(solution)/shard_map/ppermute | solution.py:234
  9.9 61.2 %copy-start.7 = (bf16[2,512,1280]{2,1,0:T(8,128)(2,1)S(1)}, bf16[2,512,1280]{2,1,0:T(8,128)(2,1)}, u32[]{:S(2)}) copy-start(bf16[2,512,1280]{2,1,0:T(8,128)(2,1)} %param.7) | copy-start | bytes 7864324
  9.9 56.9 %collective-permute-start.2 = (bf16[512,1280]{1,0:T(8,128)(2,1)S(1)}, bf16[512,1280]{1,0:T(8,128)(2,1)S(1)}, u32[]{:S(2)}, u32[]{:S(2)}) collective-permute-start(bf16[512,1280]{1,0:T(8,128)(2,1)S(1)} %fusion.5.refs_2_), channel_id=1, source_target_pairs={{0,1},{3,2},{4,5},{7,6},{8,9},{11,10},{12,13},{15,14},{16,17},{19,... | collective-permute-start | bytes 3932168 | tf_op jit(solution)/shard_map/ppermute | solution.py:234
  16.0 50.8 %collective-permute-start.3 = (bf16[512,1280]{1,0:T(8,128)(2,1)S(1)}, bf16[512,1280]{1,0:T(8,128)(2,1)S(1)}, u32[]{:S(2)}, u32[]{:S(2)}) collective-permute-start(bf16[512,1280]{1,0:T(8,128)(2,1)S(1)} %fusion.5.refs_2_), channel_id=1, source_target_pairs={{1,2},{2,1},{5,6},{6,5},{9,10},{10,9},{13,14},{14,13},{17,18},{18,... | collective-permute-start | bytes 3932168 | tf_op jit(solution)/shard_map/ppermute | solution.py:234
  17.9 53.1 %collective-permute-start.1 = (bf16[512,1280]{1,0:T(8,128)(2,1)S(1)}, bf16[512,1280]{1,0:T(8,128)(2,1)S(1)}, u32[]{:S(2)}, u32[]{:S(2)}) collective-permute-start(bf16[512,1280]{1,0:T(8,128)(2,1)S(1)} %slice_bitcast_fusion), channel_id=1, source_target_pairs={{0,4},{4,8},{8,12},{12,16},{16,20},{20,24},{24,28},{1,5},{5,9},{9,... | collective-permute-start | bytes 3932168 | tf_op jit(solution)/shard_map/ppermute | solution.py:259
  38.7 34.9 %collective-permute-start.8 = (bf16[512,1280]{1,0:T(8,128)(2,1)}, bf16[512,1280]{1,0:T(8,128)(2,1)S(1)}, u32[]{:S(2)}, u32[]{:S(2)}) collective-permute-start(bf16[512,1280]{1,0:T(8,128)(2,1)} %collective-permute-done.7), channel_id=1, source_target_pairs={{4,0},{8,4},{12,8},{16,12},{20,16},{24,20},{28,24},{5,1},{9,5},{13... | collective-permute-start | bytes 3932168 | tf_op jit(solution)/shard_map/ppermute | solution.py:261
  66.8 6.8 %collective-permute-start.5 = (bf16[512,1280]{1,0:T(8,128)(2,1)S(1)}, bf16[512,1280]{1,0:T(8,128)(2,1)S(1)}, u32[]{:S(2)}, u32[]{:S(2)}) collective-permute-start(bf16[512,1280]{1,0:T(8,128)(2,1)S(1)} %collective-permute-done.2.refs_3_), channel_id=1, source_target_pairs={{1,2},{2,1},{5,6},{6,5},{9,10},{10,9},{13,14},{14,13},{17,18},{18,... | collective-permute-start | bytes 3932168 | tf_op jit(solution)/shard_map/ppermute | solution.py:234
  67.6 34.9 %collective-permute-start.6 = (bf16[512,1280]{1,0:T(8,128)(2,1)S(1)}, bf16[512,1280]{1,0:T(8,128)(2,1)S(1)}, u32[]{:S(2)}, u32[]{:S(2)}) collective-permute-start(bf16[512,1280]{1,0:T(8,128)(2,1)S(1)} %collective-permute-done.3.refs_5_), channel_id=1, source_target_pairs={{1,0},{2,3},{5,4},{6,7},{9,8},{10,11},{13,12},{14,15},{17,16},{18,... | collective-permute-start | bytes 3932168 | tf_op jit(solution)/shard_map/ppermute | solution.py:234
  68.9 74.6 %collective-permute-start.11 = (bf16[512,1280]{1,0:T(8,128)(2,1)}, bf16[512,1280]{1,0:T(8,128)(2,1)S(1)}, u32[]{:S(2)}, u32[]{:S(2)}) collective-permute-start(bf16[512,1280]{1,0:T(8,128)(2,1)} %collective-permute-done.4), channel_id=1, source_target_pairs={{0,4},{4,8},{8,12},{12,16},{16,20},{20,24},{24,28},{1,5},{5,9},{9,... | collective-permute-start | bytes 3932168 | tf_op jit(solution)/shard_map/ppermute | solution.py:264
  73.6 75.3 %copy-start.2 = (bf16[512,1280]{1,0:T(8,128)(2,1)}, bf16[512,1280]{1,0:T(8,128)(2,1)S(1)}, u32[]{:S(2)}) copy-start(bf16[512,1280]{1,0:T(8,128)(2,1)S(1)} %fusion.2.refs_0_) | copy-start | bytes 3932164
  102.5 46.5 %collective-permute-start.10 = (bf16[512,1280]{1,0:T(8,128)(2,1)S(1)}, bf16[512,1280]{1,0:T(8,128)(2,1)}, u32[]{:S(2)}, u32[]{:S(2)}) collective-permute-start(bf16[512,1280]{1,0:T(8,128)(2,1)S(1)} %fusion.2.refs_0_), channel_id=1, source_target_pairs={{0,1},{3,2},{4,5},{7,6},{8,9},{11,10},{12,13},{15,14},{16,17},{19,... | collective-permute-start | bytes 3932168 | tf_op jit(solution)/shard_map/ppermute | solution.py:234
  105.0 43.9 %collective-permute-start.9 = (bf16[512,1280]{1,0:T(8,128)(2,1)S(1)}, bf16[512,1280]{1,0:T(8,128)(2,1)}, u32[]{:S(2)}, u32[]{:S(2)}) collective-permute-start(bf16[512,1280]{1,0:T(8,128)(2,1)S(1)} %fusion.2.refs_0_), channel_id=1, source_target_pairs={{1,2},{2,1},{5,6},{6,5},{9,10},{10,9},{13,14},{14,13},{17,18},{18,... | collective-permute-start | bytes 3932168 | tf_op jit(solution)/shard_map/ppermute | solution.py:234
  142.2 33.9 %collective-permute-start.12 = (bf16[512,1280]{1,0:T(8,128)(2,1)}, bf16[512,1280]{1,0:T(8,128)(2,1)}, u32[]{:S(2)}, u32[]{:S(2)}) collective-permute-start(bf16[512,1280]{1,0:T(8,128)(2,1)} %copy-done.15), channel_id=1, source_target_pairs={{1,0},{2,3},{5,4},{6,7},{9,8},{10,11},{13,12},{14,15},{17,16},{18,... | collective-permute-start | bytes 3932168 | tf_op jit(solution)/shard_map/ppermute | solution.py:234
  148.9 44.0 %collective-permute-start.13 = (bf16[512,1280]{1,0:T(8,128)(2,1)}, bf16[512,1280]{1,0:T(8,128)(2,1)}, u32[]{:S(2)}, u32[]{:S(2)}) collective-permute-start(bf16[512,1280]{1,0:T(8,128)(2,1)} %collective-permute-done.10.refs_0_.refs_1_), channel_id=1, source_target_pairs={{1,2},{2,1},{5,6},{6,5},{9,10},{10,9},{13,14},{14,13},{17,18},{18,... | collective-permute-start | bytes 3932168 | tf_op jit(solution)/shard_map/ppermute | solution.py:234
  150.8 55.1 %collective-permute-start.15 = (bf16[512,1280]{1,0:T(8,128)(2,1)}, bf16[512,1280]{1,0:T(8,128)(2,1)}, u32[]{:S(2)}, u32[]{:S(2)}) collective-permute-start(bf16[512,1280]{1,0:T(8,128)(2,1)} %collective-permute-done.9.refs_1_.refs_3_), channel_id=1, source_target_pairs={{1,0},{2,3},{5,4},{6,7},{9,8},{10,11},{13,12},{14,15},{17,16},{18,... | collective-permute-start | bytes 3932168 | tf_op jit(solution)/shard_map/ppermute | solution.py:234
  193.0 28.0 %collective-permute-start.16 = (bf16[2,5,512,128]{3,2,1,0:T(8,128)(2,1)S(1)}, bf16[2,5,512,128]{3,2,1,0:T(8,128)(2,1)}, u32[]{:S(2)}, u32[]{:S(2)}) collective-permute-start(bf16[2,5,512,128]{3,2,1,0:T(8,128)(2,1)S(1)} %get-tuple-element.40.refs_3_), channel_id=1, source_target_pairs={{0,24},{1,25},{2,26},{3,27}} | collective-permute-start | bytes 3932168 | tf_op jit(solution)/shard_map/ppermute | solution.py:202
  199.4 21.6 %collective-permute-start.17 = (bf16[2,5,512,128]{3,2,1,0:T(8,128)(2,1)S(1)}, bf16[2,5,512,128]{3,2,1,0:T(8,128)(2,1)}, u32[]{:S(2)}, u32[]{:S(2)}) collective-permute-start(bf16[2,5,512,128]{3,2,1,0:T(8,128)(2,1)S(1)} %get-tuple-element.40.refs_3_), channel_id=1, source_target_pairs={{0,16},{1,17},{2,18},{3,19}} | collective-permute-start | bytes 3932168 | tf_op jit(solution)/shard_map/ppermute | solution.py:202
  201.8 25.6 %collective-permute-start.18 = (bf16[2,5,512,128]{3,2,1,0:T(8,128)(2,1)S(1)}, bf16[2,5,512,128]{3,2,1,0:T(8,128)(2,1)}, u32[]{:S(2)}, u32[]{:S(2)}) collective-permute-start(bf16[2,5,512,128]{3,2,1,0:T(8,128)(2,1)S(1)} %get-tuple-element.40.refs_3_), channel_id=1, source_target_pairs={{0,8},{1,9},{2,10},{3,11}} | collective-permute-start | bytes 3932168 | tf_op jit(solution)/shard_map/ppermute | solution.py:202
  204.3 27.4 %collective-permute-start.14 = (bf16[512,1280]{1,0:T(8,128)(2,1)}, bf16[512,1280]{1,0:T(8,128)(2,1)S(1)}, u32[]{:S(2)}, u32[]{:S(2)}) collective-permute-start(bf16[512,1280]{1,0:T(8,128)(2,1)} %collective-permute-done.13.refs_0_), channel_id=1, source_target_pairs={{1,0},{2,3},{5,4},{6,7},{9,8},{10,11},{13,12},{14,15},{17,16},{18,... | collective-permute-start | bytes 3932168 | tf_op jit(solution)/shard_map/ppermute | solution.py:234
  227.6 22.3 %collective-permute-start.19 = (bf16[2,5,512,128]{3,2,1,0:T(8,128)(2,1)S(1)}, bf16[2,5,512,128]{3,2,1,0:T(8,128)(2,1)}, u32[]{:S(2)}, u32[]{:S(2)}) collective-permute-start(bf16[2,5,512,128]{3,2,1,0:T(8,128)(2,1)S(1)} %select_select_fusion.refs_1_), channel_id=1, source_target_pairs={{0,4},{8,12},{16,20},{24,28},{1,5},{9,13},{17,21},{25,29},{2,6},{1... | collective-permute-start | bytes 3932168 | tf_op jit(solution)/shard_map/ppermute | solution.py:203
  230.0 26.7 %collective-permute-start.20 = (bf16[2,5,512,128]{3,2,1,0:T(8,128)(2,1)S(1)}, bf16[2,5,512,128]{3,2,1,0:T(8,128)(2,1)}, u32[]{:S(2)}, u32[]{:S(2)}) collective-permute-start(bf16[2,5,512,128]{3,2,1,0:T(8,128)(2,1)S(1)} %get-tuple-element.40.refs_3_), channel_id=1, source_target_pairs={{4,8},{8,12},{12,16},{16,20},{20,24},{24,28},{5,9},{9,13},{13,17},... | collective-permute-start | bytes 3932168 | tf_op jit(solution)/shard_map/ppermute | solution.py:279
  241.6 15.1 %collective-permute-start.21 = (bf16[2,5,512,128]{3,2,1,0:T(8,128)(2,1)}, bf16[2,5,512,128]{3,2,1,0:T(8,128)(2,1)}, u32[]{:S(2)}, u32[]{:S(2)}) collective-permute-start(bf16[2,5,512,128]{3,2,1,0:T(8,128)(2,1)} %get-tuple-element.41.refs_4_), channel_id=1, source_target_pairs={{0,4},{1,5},{2,6},{3,7}} | collective-permute-start | bytes 3932168 | tf_op jit(solution)/shard_map/ppermute | solution.py:282
  (15 other events, 117.3 us)

commit v10 on v9

--- a/solution.py
+++ b/solution.py
@@ -249,14 +249,14 @@
             scales,
         )
 
-    raw_first, raw_last = send(frames[0], OUTWARD), send(frames[1], OUTWARD)
-    all_taps = lax.all_gather(taps, "head", axis=0)
-    outer_taps = lax.dynamic_index_in_dim(all_taps, pair, axis=0, keepdims=False)
-    following = lax.ppermute(frames[0], "tm", downs)
+    first, last = frames[0], frames[1]
+    following = lax.ppermute(first, "tm", downs)
+    first, outer_taps = hold((first, send(taps, OUTWARD)))
+    raw_first = send(first, OUTWARD)
     mixed1 = mix_first(frames[0], frames[1], following, taps)
     inward1, middle1 = send(mixed1, INWARD), send(mixed1, MIDDLE)
-    later, _ = hold((frames, mixed1))
-    preceding = lax.ppermute(later[1], "tm", ups)
+    last, _ = hold((last, mixed1))
+    raw_last, preceding = send(last, OUTWARD), lax.ppermute(last, "tm", ups)
     mixed2 = mix_second(frames[0], frames[1], following, preceding, taps)
     raw_following = lax.ppermute(raw_first, "tm", downs)
     inward1, middle1, raw_last = hold((inward1, middle1, raw_last))

time: 264 us -> 243 us (0.920)
  the two profiles are of different devices: /device:TPU:0 before, /device:TPU:10 now
where the time goes in v10:
time: 243 us; the launch traced here: 239 us
  waiting for transfers between devices  107 us (44%)
  starting transfers between devices  60.6 us (25%)
  Pallas kernels  54.5 us (22%)
  other arithmetic  8.34 us (3%)
  local copies, waits for them, and re-layouts  8.27 us (3%)
    ppermute x13, waiting for transfers between devices, send(): return lax.ppermute(x, 'head', pairs)  81.9 us
    ppermute x13, starting transfers between devices, send(): return lax.ppermute(x, 'head', pairs)  40.2 us
    pallas_call x3, Pallas kernels, project(): pl.pallas_call(functools.partial(project_body, pairs, len(after), acc is...  39.5 us
    ppermute x3, waiting for transfers between devices, broadcast_first(): held = jnp.where(mine == to, lax.ppermute(x, axis, [(0, to)]), held)  17.8 us
    pallas_call x2, Pallas kernels, attend(): pl.pallas_call(functools.partial(attend_body, 128, (len(anchors), len(opt...  15 us
    ppermute x1, waiting for transfers between devices, per_device(): following = lax.ppermute(first, 'tm', downs)  7.3 us
    convert_element_type x3, other arithmetic, mix(): (centre + taps[0] * before + taps[1] * centre + taps[2] * after).astype(B...  6.56 us
  transfers between devices with their start and end apart: 23, of which 10 were waited for; matrix products, arithmetic and copies ran while one was open for 4% of the time, Pallas kernels for 20%

profile of v10, /device:TPU:10, one launch (start us, length us, event | category | flops | bytes accessed | tf_op | source)
XLA Modules:
  0.0 239.3 jit_solution(5844610992153435876)
XLA Ops:
  0.0 3.5 %slice_bitcast_fusion.1 = (bf16[512,1280]{1,0:T(8,128)(2,1)}, bf16[512,1280]{1,0:T(8,128)(2,1)}) fusion(bf16[2,512,1280]{2,1,0:T(8,128)(2,1)} %param.7), kind=kLoop, calls=%fused_computation.22 | loop fusion | bytes 5242880 | tf_op jit(solution)/shard_map/squeeze | solution.py:260
  9.3 4.3 %collective-permute-start.8 = (bf16[512,1280]{1,0:T(8,128)(2,1)}, bf16[512,1280]{1,0:T(8,128)(2,1)S(1)}, u32[]{:S(2)}, u32[]{:S(2)}) collective-permute-start(bf16[512,1280]{1,0:T(8,128)(2,1)} %get-tuple-element.29), channel_id=1, source_target_pairs={{1,0},{2,3},{5,4},{6,7},{9,8},{10,11},{13,12},{14,15},{17,16},{18,... | collective-permute-start | bytes 3932168 | tf_op jit(solution)/shard_map/ppermute | solution.py:234
  13.6 7.3 %collective-permute-done = bf16[512,1280]{1,0:T(8,128)(2,1)} collective-permute-done((bf16[512,1280]{1,0:T(8,128)(2,1)}, bf16[512,1280]{1,0:T(8,128)(2,1)}, u32[]{:S(2)}, u32[]{:S(2)}) %collective-permute-start) | collective-permute-done | bytes 1310752 | tf_op jit(solution)/shard_map/ppermute | solution.py:253
  20.9 2.5 %fusion.5.refs_2_ = bf16[512,1280]{1,0:T(8,128)(2,1)S(1)} fusion(bf16[512,1280]{1,0:T(8,128)(2,1)} %collective-permute-done, f32[1280]{0:T(1024)S(1)} %get-tuple-element.52, f32[1280]{0:T(1024)S(1)} %get-tuple-element.51, f32[1280]{0:T(1024)S(1)} %get-tuple-element.50, pred[]{:T(512)S(6)} %eq.24, bf16[2,512,1280]{2,1,0:T(8,128)(2,1)S(1)} %copy-done.6), kind=kLoop, calls=%fused_computation.13 | loop fusion | flops 8519680 | bytes 5258241 | tf_op jit(solution)/shard_map/convert_element_type | solution.py:213
  23.4 2.4 %collective-permute-start.4 = (bf16[512,1280]{1,0:T(8,128)(2,1)S(1)}, bf16[512,1280]{1,0:T(8,128)(2,1)S(1)}, u32[]{:S(2)}, u32[]{:S(2)}) collective-permute-start(bf16[512,1280]{1,0:T(8,128)(2,1)S(1)} %copy-done.7), channel_id=1, source_target_pairs={{1,0},{2,3},{5,4},{6,7},{9,8},{10,11},{13,12},{14,15},{17,16},{18,... | collective-permute-start | bytes 3932168 | tf_op jit(solution)/shard_map/ppermute | solution.py:234
  27.1 4.6 %collective-permute-start.3 = (bf16[512,1280]{1,0:T(8,128)(2,1)S(1)}, bf16[512,1280]{1,0:T(8,128)(2,1)S(1)}, u32[]{:S(2)}, u32[]{:S(2)}) collective-permute-start(bf16[512,1280]{1,0:T(8,128)(2,1)S(1)} %fusion.5.refs_2_), channel_id=1, source_target_pairs={{1,2},{2,1},{5,6},{6,5},{9,10},{10,9},{13,14},{14,13},{17,18},{18,... | collective-permute-start | bytes 3932168 | tf_op jit(solution)/shard_map/ppermute | solution.py:234
  32.8 4.0 %collective-permute-start.1 = (bf16[512,1280]{1,0:T(8,128)(2,1)S(1)}, bf16[512,1280]{1,0:T(8,128)(2,1)S(1)}, u32[]{:S(2)}, u32[]{:S(2)}) collective-permute-start(bf16[512,1280]{1,0:T(8,128)(2,1)S(1)} %copy-done.7), channel_id=1, source_target_pairs={{0,4},{4,8},{8,12},{12,16},{16,20},{20,24},{24,28},{1,5},{5,9},{9,... | collective-permute-start | bytes 3932168 | tf_op jit(solution)/shard_map/ppermute | solution.py:259
  36.8 6.2 %collective-permute-done.8 = bf16[512,1280]{1,0:T(8,128)(2,1)S(1)} collective-permute-done((bf16[512,1280]{1,0:T(8,128)(2,1)}, bf16[512,1280]{1,0:T(8,128)(2,1)S(1)}, u32[]{:S(2)}, u32[]{:S(2)}) %collective-permute-start.8) | collective-permute-done | bytes 1310752 | tf_op jit(solution)/shard_map/ppermute | solution.py:234
  44.9 24.4 %collective-permute-done.4 = bf16[512,1280]{1,0:T(8,128)(2,1)S(1)} collective-permute-done((bf16[512,1280]{1,0:T(8,128)(2,1)S(1)}, bf16[512,1280]{1,0:T(8,128)(2,1)S(1)}, u32[]{:S(2)}, u32[]{:S(2)}) %collective-permute-start.4) | collective-permute-done | bytes 1310752 | tf_op jit(solution)/shard_map/ppermute | solution.py:234
  69.3 4.6 %collective-permute-start.5 = (bf16[512,1280]{1,0:T(8,128)(2,1)S(1)}, bf16[512,1280]{1,0:T(8,128)(2,1)}, u32[]{:S(2)}, u32[]{:S(2)}) collective-permute-start(bf16[512,1280]{1,0:T(8,128)(2,1)S(1)} %collective-permute-done.2.refs_3_), channel_id=1, source_target_pairs={{1,2},{2,1},{5,6},{6,5},{9,10},{10,9},{13,14},{14,13},{17,18},{18,... | collective-permute-start | bytes 3932168 | tf_op jit(solution)/shard_map/ppermute | solution.py:234
  78.9 22.5 %collective-permute-done.5.refs_7_ = bf16[512,1280]{1,0:T(8,128)(2,1)} collective-permute-done((bf16[512,1280]{1,0:T(8,128)(2,1)S(1)}, bf16[512,1280]{1,0:T(8,128)(2,1)}, u32[]{:S(2)}, u32[]{:S(2)}) %collective-permute-start.5) | collective-permute-done | bytes 1310752 | tf_op jit(solution)/shard_map/ppermute | solution.py:234
  102.2 4.6 %collective-permute-start.10 = (bf16[512,1280]{1,0:T(8,128)(2,1)S(1)}, bf16[512,1280]{1,0:T(8,128)(2,1)}, u32[]{:S(2)}, u32[]{:S(2)}) collective-permute-start(bf16[512,1280]{1,0:T(8,128)(2,1)S(1)} %fusion.2.refs_0_), channel_id=1, source_target_pairs={{1,2},{2,1},{5,6},{6,5},{9,10},{10,9},{13,14},{14,13},{17,18},{18,... | collective-permute-start | bytes 3932168 | tf_op jit(solution)/shard_map/ppermute | solution.py:234
  108.2 6.7 %collective-permute-start.13 = (bf16[512,1280]{1,0:T(8,128)(2,1)}, bf16[512,1280]{1,0:T(8,128)(2,1)}, u32[]{:S(2)}, u32[]{:S(2)}) collective-permute-start(bf16[512,1280]{1,0:T(8,128)(2,1)} %collective-permute-done.5.refs_7_), channel_id=1, source_target_pairs={{1,0},{2,3},{5,4},{6,7},{9,8},{10,11},{13,12},{14,15},{17,16},{18,... | collective-permute-start | bytes 3932168 | tf_op jit(solution)/shard_map/ppermute | solution.py:234
  114.9 2.9 %fusion.11 = (bf16[512,1280]{1,0:T(8,128)(2,1)S(1)}, bf16[512,1280]{1,0:T(8,128)(2,1)}) fusion(bf16[512,1280]{1,0:T(8,128)(2,1)S(1)} %collective-permute-done.9, bf16[512,1280]{1,0:T(8,128)(2,1)S(1)} %collective-permute-done.4, bf16[512,1280]{1,0:T(8,128)(2,1)S(1)} %collective-permute-done.8, bf16[512,1280]{1,0:T(8,128)(2,1)S(1)} %collective-permute-done.12, ...), kind=kLoop, calls=%fused_computation.19 | loop fusion | flops 17039360 | bytes 7879681 | tf_op jit(solution)/shard_map/convert_element_type | solution.py:213
  117.8 15.6 %collective-permute-done.10.refs_1_.refs_3_ = bf16[512,1280]{1,0:T(8,128)(2,1)} collective-permute-done((bf16[512,1280]{1,0:T(8,128)(2,1)S(1)}, bf16[512,1280]{1,0:T(8,128)(2,1)}, u32[]{:S(2)}, u32[]{:S(2)}) %collective-permute-start.10) | collective-permute-done | bytes 1310752 | tf_op jit(solution)/shard_map/ppermute | solution.py:234
  133.4 3.4 %collective-permute-done.11.refs_0_.refs_1_ = bf16[512,1280]{1,0:T(8,128)(2,1)} collective-permute-done((bf16[512,1280]{1,0:T(8,128)(2,1)S(1)}, bf16[512,1280]{1,0:T(8,128)(2,1)}, u32[]{:S(2)}, u32[]{:S(2)}) %collective-permute-start.11) | collective-permute-done | bytes 1310752 | tf_op jit(solution)/shard_map/ppermute | solution.py:234
  139.1 2.5 %collective-permute-start.16 = (bf16[512,1280]{1,0:T(8,128)(2,1)}, bf16[512,1280]{1,0:T(8,128)(2,1)}, u32[]{:S(2)}, u32[]{:S(2)}) collective-permute-start(bf16[512,1280]{1,0:T(8,128)(2,1)} %collective-permute-done.10.refs_1_.refs_3_), channel_id=1, source_target_pairs={{1,0},{2,3},{5,4},{6,7},{9,8},{10,11},{13,12},{14,15},{17,16},{18,... | collective-permute-start | bytes 3932168 | tf_op jit(solution)/shard_map/ppermute | solution.py:234
  142.9 15.5 %project_end.2 = (bf16[5,512,128]{2,1,0:T(8,128)(2,1)S(1)}, bf16[2,5,512,128]{3,2,1,0:T(8,128)(2,1)S(1)}) custom-call(s32[5]{0:T(128)S(1)} %stack.64.info, bf16[512,1280]{1,0:T(8,128)(2,1)} %collective-permute-done.11.refs_0_.refs_1_, bf16[512,1280]{1,0:T(8,128)(2,1)} %collective-permute-done.10.refs_1_.refs_3_, bf16[512,1280]{1,0:T(8,128)(2,1)S(1)} %copy-done.1, ...), custom_call_target="tpu_custom_call" | custom-call | flops 10000000000 | bytes 1 | tf_op jit(solution)/shard_map/project_end/pallas_call | solution.py:106
  158.4 7.5 %collective-permute-done.14.refs_0_ = bf16[512,1280]{1,0:T(8,128)(2,1)} collective-permute-done((bf16[512,1280]{1,0:T(8,128)(2,1)}, bf16[512,1280]{1,0:T(8,128)(2,1)}, u32[]{:S(2)}, u32[]{:S(2)}) %collective-permute-start.14) | collective-permute-done | bytes 1310752 | tf_op jit(solution)/shard_map/ppermute | solution.py:234
  173.8 13.7 %project_raw.1.refs_7_ = f32[512,1920]{1,0:T(8,128)} custom-call(s32[4]{0:T(128)S(1)} %pad_add_fusion.2.info, bf16[512,1280]{1,0:T(8,128)(2,1)S(1)} %copy-done.3, bf16[512,1280]{1,0:T(8,128)(2,1)} %collective-permute-done.11.refs_0_.refs_1_, bf16[512,1280]{1,0:T(8,128)(2,1)S(1)} %get-tuple-element.41.refs_2_, ...), custom_call_target="tpu_custom_call" | custom-call | flops 10000000000 | bytes 1 | tf_op jit(solution)/shard_map/project_raw/pallas_call | solution.py:106
  187.5 17.8 %collective-permute-done.19 = bf16[2,5,512,128]{3,2,1,0:T(8,128)(2,1)} collective-permute-done((bf16[2,5,512,128]{3,2,1,0:T(8,128)(2,1)S(1)}, bf16[2,5,512,128]{3,2,1,0:T(8,128)(2,1)}, u32[]{:S(2)}, u32[]{:S(2)}) %collective-permute-start.19) | collective-permute-done | bytes 1310752 | tf_op jit(solution)/shard_map/ppermute | solution.py:202
  211.2 10.2 %project_end.3 = (bf16[5,512,128]{2,1,0:T(8,128)(2,1)S(1)}, bf16[2,5,512,128]{3,2,1,0:T(8,128)(2,1)}) custom-call(s32[2]{0:T(128)S(1)} %pad_add_fusion.1.info, bf16[512,1280]{1,0:T(8,128)(2,1)} %collective-permute-done.14.refs_0_, bf16[512,1280]{1,0:T(8,128)(2,1)S(1)} %collective-permute-done.15.refs_1_, bf16[5120,640]{1,0:T(8,128)(2,1)} %refs_2_.1, ...), custom_call_target="tpu_custom_call" | custom-call | flops 10000000000 | bytes 1 | tf_op jit(solution)/shard_map/project_end/pallas_call | solution.py:106
  224.0 7.5 %attend.2.refs_6_ = bf16[2,512,640]{2,1,0:T(8,128)(2,1)} custom-call(s32[3]{0:T(128)S(1)} %get-tuple-element.58.info, bf16[5,512,128]{2,1,0:T(8,128)(2,1)S(1)} %get-tuple-element.46.refs_0_, bf16[2,5,512,128]{3,2,1,0:T(8,128)(2,1)S(1)} %select_select_fusion.refs_1_, bf16[2,5,512,128]{3,2,1,0:T(8,128)(2,1)} %collective-permute-done.20.refs_2_, ...), custom_call_target="tpu_custom_call" | custom-call | flops 1342177280 | bytes 3932160 | tf_op jit(solution)/shard_map/attend/pallas_call | solution.py:173
  231.6 7.5 %attend.3 = bf16[2,512,640]{2,1,0:T(8,128)(2,1)} custom-call(s32[3]{0:T(128)S(1)} %get-tuple-element.57.info, bf16[5,512,128]{2,1,0:T(8,128)(2,1)S(1)} %copy-done.5, bf16[2,5,512,128]{3,2,1,0:T(8,128)(2,1)S(1)} %select_select_fusion.refs_1_, bf16[2,5,512,128]{3,2,1,0:T(8,128)(2,1)} %collective-permute-done.20.refs_2_, ...), custom_call_target="tpu_custom_call", output_to_operand_aliasing={{}: (7, {})} | custom-call | flops 1342177280 | bytes 3932160 | tf_op jit(solution)/shard_map/attend/pallas_call | solution.py:173
  (68 shorter events, 37.0 us)
Async XLA Ops:
  3.5 17.3 %collective-permute-start = (bf16[512,1280]{1,0:T(8,128)(2,1)}, bf16[512,1280]{1,0:T(8,128)(2,1)}, u32[]{:S(2)}, u32[]{:S(2)}) collective-permute-start(bf16[512,1280]{1,0:T(8,128)(2,1)} %get-tuple-element.29), channel_id=1, source_target_pairs={{4,0},{8,4},{12,8},{16,12},{20,16},{24,20},{28,24},{5,1},{9,5},{13... | collective-permute-start | bytes 3932168 | tf_op jit(solution)/shard_map/ppermute | solution.py:253
  5.4 3.8 %collective-permute-start.7 = (f32[3,1280]{1,0:T(4,128)S(1)}, f32[3,1280]{1,0:T(4,128)S(1)}, u32[]{:S(2)}, u32[]{:S(2)}) collective-permute-start(f32[3,1280]{1,0:T(4,128)S(1)} %copy-done.8), channel_id=1, source_target_pairs={{1,0},{2,3},{5,4},{6,7},{9,8},{10,11},{13,12},{14,15},{17,16},{18,... | collective-permute-start | bytes 46088 | tf_op jit(solution)/shard_map/ppermute | solution.py:234
  9.3 33.7 %collective-permute-start.8 = (bf16[512,1280]{1,0:T(8,128)(2,1)}, bf16[512,1280]{1,0:T(8,128)(2,1)S(1)}, u32[]{:S(2)}, u32[]{:S(2)}) collective-permute-start(bf16[512,1280]{1,0:T(8,128)(2,1)} %get-tuple-element.29), channel_id=1, source_target_pairs={{1,0},{2,3},{5,4},{6,7},{9,8},{10,11},{13,12},{14,15},{17,16},{18,... | collective-permute-start | bytes 3932168 | tf_op jit(solution)/shard_map/ppermute | solution.py:234
  23.4 45.9 %collective-permute-start.4 = (bf16[512,1280]{1,0:T(8,128)(2,1)S(1)}, bf16[512,1280]{1,0:T(8,128)(2,1)S(1)}, u32[]{:S(2)}, u32[]{:S(2)}) collective-permute-start(bf16[512,1280]{1,0:T(8,128)(2,1)S(1)} %copy-done.7), channel_id=1, source_target_pairs={{1,0},{2,3},{5,4},{6,7},{9,8},{10,11},{13,12},{14,15},{17,16},{18,... | collective-permute-start | bytes 3932168 | tf_op jit(solution)/shard_map/ppermute | solution.py:234
  25.8 43.5 %collective-permute-start.2 = (bf16[512,1280]{1,0:T(8,128)(2,1)S(1)}, bf16[512,1280]{1,0:T(8,128)(2,1)S(1)}, u32[]{:S(2)}, u32[]{:S(2)}) collective-permute-start(bf16[512,1280]{1,0:T(8,128)(2,1)S(1)} %fusion.5.refs_2_), channel_id=1, source_target_pairs={{0,1},{3,2},{4,5},{7,6},{8,9},{11,10},{12,13},{15,14},{16,17},{19,... | collective-permute-start | bytes 3932168 | tf_op jit(solution)/shard_map/ppermute | solution.py:234
  27.1 42.2 %collective-permute-start.3 = (bf16[512,1280]{1,0:T(8,128)(2,1)S(1)}, bf16[512,1280]{1,0:T(8,128)(2,1)S(1)}, u32[]{:S(2)}, u32[]{:S(2)}) collective-permute-start(bf16[512,1280]{1,0:T(8,128)(2,1)S(1)} %fusion.5.refs_2_), channel_id=1, source_target_pairs={{1,2},{2,1},{5,6},{6,5},{9,10},{10,9},{13,14},{14,13},{17,18},{18,... | collective-permute-start | bytes 3932168 | tf_op jit(solution)/shard_map/ppermute | solution.py:234
  32.8 44.9 %collective-permute-start.1 = (bf16[512,1280]{1,0:T(8,128)(2,1)S(1)}, bf16[512,1280]{1,0:T(8,128)(2,1)S(1)}, u32[]{:S(2)}, u32[]{:S(2)}) collective-permute-start(bf16[512,1280]{1,0:T(8,128)(2,1)S(1)} %copy-done.7), channel_id=1, source_target_pairs={{0,4},{4,8},{8,12},{12,16},{16,20},{20,24},{24,28},{1,5},{5,9},{9,... | collective-permute-start | bytes 3932168 | tf_op jit(solution)/shard_map/ppermute | solution.py:259
  43.0 35.9 %collective-permute-start.9 = (bf16[512,1280]{1,0:T(8,128)(2,1)S(1)}, bf16[512,1280]{1,0:T(8,128)(2,1)S(1)}, u32[]{:S(2)}, u32[]{:S(2)}) collective-permute-start(bf16[512,1280]{1,0:T(8,128)(2,1)S(1)} %collective-permute-done.8), channel_id=1, source_target_pairs={{4,0},{8,4},{12,8},{16,12},{20,16},{24,20},{28,24},{5,1},{9,5},{13... | collective-permute-start | bytes 3932168 | tf_op jit(solution)/shard_map/ppermute | solution.py:261
  69.3 32.1 %collective-permute-start.5 = (bf16[512,1280]{1,0:T(8,128)(2,1)S(1)}, bf16[512,1280]{1,0:T(8,128)(2,1)}, u32[]{:S(2)}, u32[]{:S(2)}) collective-permute-start(bf16[512,1280]{1,0:T(8,128)(2,1)S(1)} %collective-permute-done.2.refs_3_), channel_id=1, source_target_pairs={{1,2},{2,1},{5,6},{6,5},{9,10},{10,9},{13,14},{14,13},{17,18},{18,... | collective-permute-start | bytes 3932168 | tf_op jit(solution)/shard_map/ppermute | solution.py:234
  73.9 28.3 %collective-permute-start.6 = (bf16[512,1280]{1,0:T(8,128)(2,1)S(1)}, bf16[512,1280]{1,0:T(8,128)(2,1)S(1)}, u32[]{:S(2)}, u32[]{:S(2)}) collective-permute-start(bf16[512,1280]{1,0:T(8,128)(2,1)S(1)} %collective-permute-done.3.refs_5_), channel_id=1, source_target_pairs={{1,0},{2,3},{5,4},{6,7},{9,8},{10,11},{13,12},{14,15},{17,16},{18,... | collective-permute-start | bytes 3932168 | tf_op jit(solution)/shard_map/ppermute | solution.py:234
  75.7 39.2 %collective-permute-start.12 = (bf16[512,1280]{1,0:T(8,128)(2,1)S(1)}, bf16[512,1280]{1,0:T(8,128)(2,1)S(1)}, u32[]{:S(2)}, u32[]{:S(2)}) collective-permute-start(bf16[512,1280]{1,0:T(8,128)(2,1)S(1)} %collective-permute-done.4), channel_id=1, source_target_pairs={{0,4},{4,8},{8,12},{12,16},{16,20},{20,24},{24,28},{1,5},{5,9},{9,... | collective-permute-start | bytes 3932168 | tf_op jit(solution)/shard_map/ppermute | solution.py:264
  78.8 39.0 %copy-start.2 = (bf16[512,1280]{1,0:T(8,128)(2,1)}, bf16[512,1280]{1,0:T(8,128)(2,1)S(1)}, u32[]{:S(2)}) copy-start(bf16[512,1280]{1,0:T(8,128)(2,1)S(1)} %fusion.2.refs_0_) | copy-start | bytes 3932164
  102.2 31.1 %collective-permute-start.10 = (bf16[512,1280]{1,0:T(8,128)(2,1)S(1)}, bf16[512,1280]{1,0:T(8,128)(2,1)}, u32[]{:S(2)}, u32[]{:S(2)}) collective-permute-start(bf16[512,1280]{1,0:T(8,128)(2,1)S(1)} %fusion.2.refs_0_), channel_id=1, source_target_pairs={{1,2},{2,1},{5,6},{6,5},{9,10},{10,9},{13,14},{14,13},{17,18},{18,... | collective-permute-start | bytes 3932168 | tf_op jit(solution)/shard_map/ppermute | solution.py:234
  106.9 29.9 %collective-permute-start.11 = (bf16[512,1280]{1,0:T(8,128)(2,1)S(1)}, bf16[512,1280]{1,0:T(8,128)(2,1)}, u32[]{:S(2)}, u32[]{:S(2)}) collective-permute-start(bf16[512,1280]{1,0:T(8,128)(2,1)S(1)} %fusion.2.refs_0_), channel_id=1, source_target_pairs={{0,1},{3,2},{4,5},{7,6},{8,9},{11,10},{12,13},{15,14},{16,17},{19,... | collective-permute-start | bytes 3932168 | tf_op jit(solution)/shard_map/ppermute | solution.py:234
  108.2 33.4 %collective-permute-start.13 = (bf16[512,1280]{1,0:T(8,128)(2,1)}, bf16[512,1280]{1,0:T(8,128)(2,1)}, u32[]{:S(2)}, u32[]{:S(2)}) collective-permute-start(bf16[512,1280]{1,0:T(8,128)(2,1)} %collective-permute-done.5.refs_7_), channel_id=1, source_target_pairs={{1,0},{2,3},{5,4},{6,7},{9,8},{10,11},{13,12},{14,15},{17,16},{18,... | collective-permute-start | bytes 3932168 | tf_op jit(solution)/shard_map/ppermute | solution.py:234
  136.8 29.2 %collective-permute-start.14 = (bf16[512,1280]{1,0:T(8,128)(2,1)}, bf16[512,1280]{1,0:T(8,128)(2,1)}, u32[]{:S(2)}, u32[]{:S(2)}) collective-permute-start(bf16[512,1280]{1,0:T(8,128)(2,1)} %collective-permute-done.11.refs_0_.refs_1_), channel_id=1, source_target_pairs={{1,2},{2,1},{5,6},{6,5},{9,10},{10,9},{13,14},{14,13},{17,18},{18,... | collective-permute-start | bytes 3932168 | tf_op jit(solution)/shard_map/ppermute | solution.py:234
  139.1 33.3 %collective-permute-start.16 = (bf16[512,1280]{1,0:T(8,128)(2,1)}, bf16[512,1280]{1,0:T(8,128)(2,1)}, u32[]{:S(2)}, u32[]{:S(2)}) collective-permute-start(bf16[512,1280]{1,0:T(8,128)(2,1)} %collective-permute-done.10.refs_1_.refs_3_), channel_id=1, source_target_pairs={{1,0},{2,3},{5,4},{6,7},{9,8},{10,11},{13,12},{14,15},{17,16},{18,... | collective-permute-start | bytes 3932168 | tf_op jit(solution)/shard_map/ppermute | solution.py:234
  165.9 21.6 %collective-permute-start.17 = (bf16[2,5,512,128]{3,2,1,0:T(8,128)(2,1)S(1)}, bf16[2,5,512,128]{3,2,1,0:T(8,128)(2,1)}, u32[]{:S(2)}, u32[]{:S(2)}) collective-permute-start(bf16[2,5,512,128]{3,2,1,0:T(8,128)(2,1)S(1)} %get-tuple-element.44.refs_3_), channel_id=1, source_target_pairs={{0,24},{1,25},{2,26},{3,27}} | collective-permute-start | bytes 3932168 | tf_op jit(solution)/shard_map/ppermute | solution.py:202
  167.7 19.8 %collective-permute-start.18 = (bf16[2,5,512,128]{3,2,1,0:T(8,128)(2,1)S(1)}, bf16[2,5,512,128]{3,2,1,0:T(8,128)(2,1)}, u32[]{:S(2)}, u32[]{:S(2)}) collective-permute-start(bf16[2,5,512,128]{3,2,1,0:T(8,128)(2,1)S(1)} %get-tuple-element.44.refs_3_), channel_id=1, source_target_pairs={{0,16},{1,17},{2,18},{3,19}} | collective-permute-start | bytes 3932168 | tf_op jit(solution)/shard_map/ppermute | solution.py:202
  169.4 35.9 %collective-permute-start.19 = (bf16[2,5,512,128]{3,2,1,0:T(8,128)(2,1)S(1)}, bf16[2,5,512,128]{3,2,1,0:T(8,128)(2,1)}, u32[]{:S(2)}, u32[]{:S(2)}) collective-permute-start(bf16[2,5,512,128]{3,2,1,0:T(8,128)(2,1)S(1)} %get-tuple-element.44.refs_3_), channel_id=1, source_target_pairs={{0,8},{1,9},{2,10},{3,11}} | collective-permute-start | bytes 3932168 | tf_op jit(solution)/shard_map/ppermute | solution.py:202
  170.9 40.3 %collective-permute-start.15 = (bf16[512,1280]{1,0:T(8,128)(2,1)}, bf16[512,1280]{1,0:T(8,128)(2,1)S(1)}, u32[]{:S(2)}, u32[]{:S(2)}) collective-permute-start(bf16[512,1280]{1,0:T(8,128)(2,1)} %collective-permute-done.14.refs_0_), channel_id=1, source_target_pairs={{1,0},{2,3},{5,4},{6,7},{9,8},{10,11},{13,12},{14,15},{17,16},{18,... | collective-permute-start | bytes 3932168 | tf_op jit(solution)/shard_map/ppermute | solution.py:234
  206.9 17.2 %collective-permute-start.20 = (bf16[2,5,512,128]{3,2,1,0:T(8,128)(2,1)S(1)}, bf16[2,5,512,128]{3,2,1,0:T(8,128)(2,1)}, u32[]{:S(2)}, u32[]{:S(2)}) collective-permute-start(bf16[2,5,512,128]{3,2,1,0:T(8,128)(2,1)S(1)} %select_select_fusion.refs_1_), channel_id=1, source_target_pairs={{0,4},{8,12},{16,20},{24,28},{1,5},{9,13},{17,21},{25,29},{2,6},{1... | collective-permute-start | bytes 3932168 | tf_op jit(solution)/shard_map/ppermute | solution.py:203
  209.2 22.3 %collective-permute-start.21 = (bf16[2,5,512,128]{3,2,1,0:T(8,128)(2,1)S(1)}, bf16[2,5,512,128]{3,2,1,0:T(8,128)(2,1)}, u32[]{:S(2)}, u32[]{:S(2)}) collective-permute-start(bf16[2,5,512,128]{3,2,1,0:T(8,128)(2,1)S(1)} %get-tuple-element.44.refs_3_), channel_id=1, source_target_pairs={{4,8},{8,12},{12,16},{16,20},{20,24},{24,28},{5,9},{9,13},{13,17},... | collective-permute-start | bytes 3932168 | tf_op jit(solution)/shard_map/ppermute | solution.py:279
  222.2 9.3 %collective-permute-start.22 = (bf16[2,5,512,128]{3,2,1,0:T(8,128)(2,1)}, bf16[2,5,512,128]{3,2,1,0:T(8,128)(2,1)}, u32[]{:S(2)}, u32[]{:S(2)}) collective-permute-start(bf16[2,5,512,128]{3,2,1,0:T(8,128)(2,1)} %get-tuple-element.45.refs_4_), channel_id=1, source_target_pairs={{0,4},{1,5},{2,6},{3,7}} | collective-permute-start | bytes 3932168 | tf_op jit(solution)/shard_map/ppermute | solution.py:282
  (13 other events, 123.7 us)

commit v11 on v10

--- a/solution.py
+++ b/solution.py
@@ -272,12 +272,13 @@
 
     sources1 = [(mixed1,), (inward1, first1), (middle1, second1), (cross1, third1)]
     q1, kv1 = project(sources1, info, weights, gains, after=(inward2, middle2), flops=10**10)
-    kv1, cross2 = hold((kv1, cross2))
+    beside = lax.ppermute(middle2[:16], "tm", [(i, i ^ 1) for i in range(count)])
+    kv1, beside = hold((kv1, beside))
     third2 = send(cross2, OUTWARD)
     anchor = broadcast_first(kv1, "tm")
     later1, _ = hold((kv1, anchor[0]))
     shift1 = lax.ppermute(later1, "tm", [(i, i + 1) for i in range(1, count - 1)])
-    raw2 = project([(mixed2,), (inward2, first2), (middle2, second2)], info_raw, weights, flops=10**10)
+    raw2 = project([(mixed2,), (inward2, first2), (middle2, second2)], info_raw, weights, after=(beside,), flops=10**10)
     q2, kv2 = project([(cross2, third2)], info_end, weights, gains, raw2, flops=10**10)
     shift2 = lax.ppermute(kv2, "tm", [(0, 1)])
     late = jnp.where(start, 0, 1)

time: 243 us -> 238 us (0.979)
  the two profiles are of different devices: /device:TPU:10 before, /device:TPU:6 now
where the time goes in v11:
time: 238 us; the launch traced here: 237 us
  waiting for transfers between devices  119 us (50%)
  Pallas kernels  53.4 us (22%)
  starting transfers between devices  44.4 us (19%)
  other arithmetic  10.1 us (4%)
  local copies, waits for them, and re-layouts  8.84 us (4%)
    ppermute x13, waiting for transfers between devices, send(): return lax.ppermute(x, 'head', pairs)  111 us
    pallas_call x3, Pallas kernels, project(): pl.pallas_call(functools.partial(project_body, pairs, len(after), acc is...  38.3 us
    ppermute x13, starting transfers between devices, send(): return lax.ppermute(x, 'head', pairs)  25.9 us
    pallas_call x2, Pallas kernels, attend(): pl.pallas_call(functools.partial(attend_body, 128, (len(anchors), len(opt...  15 us
    ppermute x1, waiting for transfers between devices, per_device(): following = lax.ppermute(first, 'tm', downs)  8.44 us
    convert_element_type x3, other arithmetic, mix(): (centre + taps[0] * before + taps[1] * centre + taps[2] * after).astype(B...  8.36 us
    ppermute x3, starting transfers between devices, broadcast_first(): held = jnp.where(mine == to, lax.ppermute(x, axis, [(0, to)]), held)  4.82 us
  transfers between devices with their start and end apart: 24, of which 9 were waited for; matrix products, arithmetic and copies ran while one was open for 5% of the time, Pallas kernels for 19%

profile of v11, /device:TPU:6, one launch (start us, length us, event | category | flops | bytes accessed | tf_op | source)
XLA Modules:
  0.0 236.7 jit_solution(4944562646959597453)
XLA Ops:
  0.0 3.5 %slice_bitcast_fusion.1 = (bf16[512,1280]{1,0:T(8,128)(2,1)}, bf16[512,1280]{1,0:T(8,128)(2,1)}) fusion(bf16[2,512,1280]{2,1,0:T(8,128)(2,1)} %param.7), kind=kLoop, calls=%fused_computation.22 | loop fusion | bytes 5242880 | tf_op jit(solution)/shard_map/squeeze | solution.py:260
  3.5 1.9 collective-permute-start
  6.8 4.3 %collective-permute-done.7 = f32[3,1280]{1,0:T(4,128)S(1)} collective-permute-done((f32[3,1280]{1,0:T(4,128)S(1)}, f32[3,1280]{1,0:T(4,128)S(1)}, u32[]{:S(2)}, u32[]{:S(2)}) %collective-permute-start.7) | collective-permute-done | bytes 15392 | tf_op jit(solution)/shard_map/ppermute | solution.py:234
  12.4 8.4 %collective-permute-done = bf16[512,1280]{1,0:T(8,128)(2,1)} collective-permute-done((bf16[512,1280]{1,0:T(8,128)(2,1)}, bf16[512,1280]{1,0:T(8,128)(2,1)}, u32[]{:S(2)}, u32[]{:S(2)}) %collective-permute-start) | collective-permute-done | bytes 1310752 | tf_op jit(solution)/shard_map/ppermute | solution.py:253
  20.9 2.5 %fusion.5.refs_2_ = bf16[512,1280]{1,0:T(8,128)(2,1)S(1)} fusion(bf16[512,1280]{1,0:T(8,128)(2,1)} %collective-permute-done, f32[1280]{0:T(1024)S(1)} %get-tuple-element.52, f32[1280]{0:T(1024)S(1)} %get-tuple-element.51, f32[1280]{0:T(1024)S(1)} %get-tuple-element.50, pred[]{:T(512)S(6)} %eq.24, bf16[2,512,1280]{2,1,0:T(8,128)(2,1)S(1)} %copy-done.6), kind=kLoop, calls=%fused_computation.13 | loop fusion | flops 8519680 | bytes 5258241 | tf_op jit(solution)/shard_map/convert_element_type | solution.py:213
  24.7 4.7 %collective-permute-start.2 = (bf16[512,1280]{1,0:T(8,128)(2,1)S(1)}, bf16[512,1280]{1,0:T(8,128)(2,1)S(1)}, u32[]{:S(2)}, u32[]{:S(2)}) collective-permute-start(bf16[512,1280]{1,0:T(8,128)(2,1)S(1)} %fusion.5.refs_2_), channel_id=1, source_target_pairs={{0,1},{3,2},{4,5},{7,6},{8,9},{11,10},{12,13},{15,14},{16,17},{19,... | collective-permute-start | bytes 3932168 | tf_op jit(solution)/shard_map/ppermute | solution.py:234
  33.2 11.6 %collective-permute-done.8 = bf16[512,1280]{1,0:T(8,128)(2,1)S(1)} collective-permute-done((bf16[512,1280]{1,0:T(8,128)(2,1)}, bf16[512,1280]{1,0:T(8,128)(2,1)S(1)}, u32[]{:S(2)}, u32[]{:S(2)}) %collective-permute-start.8) | collective-permute-done | bytes 1310752 | tf_op jit(solution)/shard_map/ppermute | solution.py:234
  44.9 1.9 collective-permute-start.9
  46.8 25.6 %collective-permute-done.4 = bf16[512,1280]{1,0:T(8,128)(2,1)S(1)} collective-permute-done((bf16[512,1280]{1,0:T(8,128)(2,1)S(1)}, bf16[512,1280]{1,0:T(8,128)(2,1)S(1)}, u32[]{:S(2)}, u32[]{:S(2)}) %collective-permute-start.4) | collective-permute-done | bytes 1310752 | tf_op jit(solution)/shard_map/ppermute | solution.py:234
  72.4 2.3 collective-permute-start.5
  76.0 1.9 collective-permute-start.12
  79.2 27.7 %collective-permute-done.6.refs_6_ = bf16[512,1280]{1,0:T(8,128)(2,1)S(1)} collective-permute-done((bf16[512,1280]{1,0:T(8,128)(2,1)S(1)}, bf16[512,1280]{1,0:T(8,128)(2,1)S(1)}, u32[]{:S(2)}, u32[]{:S(2)}) %collective-permute-start.6) | collective-permute-done | bytes 1310752 | tf_op jit(solution)/shard_map/ppermute | solution.py:234
  109.6 5.4 %collective-permute-start.11 = (bf16[512,1280]{1,0:T(8,128)(2,1)S(1)}, bf16[512,1280]{1,0:T(8,128)(2,1)}, u32[]{:S(2)}, u32[]{:S(2)}) collective-permute-start(bf16[512,1280]{1,0:T(8,128)(2,1)S(1)} %fusion.2.refs_1_), channel_id=1, source_target_pairs={{0,1},{3,2},{4,5},{7,6},{8,9},{11,10},{12,13},{15,14},{16,17},{19,... | collective-permute-start | bytes 3932168 | tf_op jit(solution)/shard_map/ppermute | solution.py:234
  116.6 4.7 %fusion.11 = (bf16[512,1280]{1,0:T(8,128)(2,1)S(1)}, bf16[512,1280]{1,0:T(8,128)(2,1)}) fusion(bf16[512,1280]{1,0:T(8,128)(2,1)} %collective-permute-done.9, bf16[512,1280]{1,0:T(8,128)(2,1)} %copy-done.9, bf16[512,1280]{1,0:T(8,128)(2,1)} %copy-done.8, bf16[512,1280]{1,0:T(8,128)(2,1)} %collective-permute-done.12, f32[1280]{0:T(1024)S(1)} %get-tuple-element.48, ...), kind=kLoop, calls=%fused_computation.19 | loop fusion | flops 17039360 | bytes 7879681 | tf_op jit(solution)/shard_map/convert_element_type | solution.py:213
  121.2 19.3 %collective-permute-done.11.refs_0_.refs_2_ = bf16[512,1280]{1,0:T(8,128)(2,1)} collective-permute-done((bf16[512,1280]{1,0:T(8,128)(2,1)S(1)}, bf16[512,1280]{1,0:T(8,128)(2,1)}, u32[]{:S(2)}, u32[]{:S(2)}) %collective-permute-start.11) | collective-permute-done | bytes 1310752 | tf_op jit(solution)/shard_map/ppermute | solution.py:234
  144.4 3.8 %collective-permute-done.15.refs_8_ = bf16[512,1280]{1,0:T(8,128)(2,1)} collective-permute-done((bf16[512,1280]{1,0:T(8,128)(2,1)}, bf16[512,1280]{1,0:T(8,128)(2,1)}, u32[]{:S(2)}, u32[]{:S(2)}) %collective-permute-start.15) | collective-permute-done | bytes 1310752 | tf_op jit(solution)/shard_map/ppermute | solution.py:234
  148.2 15.5 %project_end.2 = (bf16[5,512,128]{2,1,0:T(8,128)(2,1)S(1)}, bf16[2,5,512,128]{3,2,1,0:T(8,128)(2,1)S(1)}) custom-call(s32[5]{0:T(128)S(1)} %stack.65.info, bf16[512,1280]{1,0:T(8,128)(2,1)} %collective-permute-done.11.refs_0_.refs_2_, bf16[512,1280]{1,0:T(8,128)(2,1)} %collective-permute-done.10.refs_1_.refs_4_, bf16[512,1280]{1,0:T(8,128)(2,1)S(1)} %copy-done.1, ...), custom_call_target="tpu_custom_call" | custom-call | flops 10000000000 | bytes 1 | tf_op jit(solution)/shard_map/project_end/pallas_call | solution.py:106
  170.3 3.8 %collective-permute-done.17.refs_5_ = bf16[512,1280]{1,0:T(8,128)(2,1)} collective-permute-done((bf16[512,1280]{1,0:T(8,128)(2,1)}, bf16[512,1280]{1,0:T(8,128)(2,1)}, u32[]{:S(2)}, u32[]{:S(2)}) %collective-permute-start.17) | collective-permute-done | bytes 1310752 | tf_op jit(solution)/shard_map/ppermute | solution.py:234
  175.4 13.8 %project_raw.1.refs_7_ = f32[512,1920]{1,0:T(8,128)} custom-call(s32[4]{0:T(128)S(1)} %pad_add_fusion.2.info, bf16[16,1280]{1,0:T(8,128)(2,1)S(1)} %collective-permute-done.16.refs_0_, bf16[512,1280]{1,0:T(8,128)(2,1)S(1)} %copy-done.3, bf16[512,1280]{1,0:T(8,128)(2,1)} %collective-permute-done.11.refs_0_.refs_2_, ...), custom_call_target="tpu_custom_call" | custom-call | flops 10000000000 | bytes 1 | tf_op jit(solution)/shard_map/project_raw/pallas_call | solution.py:106
  190.8 2.4 %collective-permute-start.21 = (bf16[2,5,512,128]{3,2,1,0:T(8,128)(2,1)S(1)}, bf16[2,5,512,128]{3,2,1,0:T(8,128)(2,1)}, u32[]{:S(2)}, u32[]{:S(2)}) collective-permute-start(bf16[2,5,512,128]{3,2,1,0:T(8,128)(2,1)S(1)} %select_select_fusion.refs_1_), channel_id=1, source_target_pairs={{0,4},{8,12},{16,20},{24,28},{1,5},{9,13},{17,21},{25,29},{2,6},{1... | collective-permute-start | bytes 3932168 | tf_op jit(solution)/shard_map/ppermute | solution.py:203
  195.1 14.7 %collective-permute-done.14.refs_1_ = bf16[512,1280]{1,0:T(8,128)(2,1)S(1)} collective-permute-done((bf16[512,1280]{1,0:T(8,128)(2,1)}, bf16[512,1280]{1,0:T(8,128)(2,1)S(1)}, u32[]{:S(2)}, u32[]{:S(2)}) %collective-permute-start.14) | collective-permute-done | bytes 1310752 | tf_op jit(solution)/shard_map/ppermute | solution.py:234
  209.9 9.0 %project_end.3 = (bf16[5,512,128]{2,1,0:T(8,128)(2,1)S(1)}, bf16[2,5,512,128]{3,2,1,0:T(8,128)(2,1)}) custom-call(s32[2]{0:T(128)S(1)} %pad_add_fusion.1.info, bf16[512,1280]{1,0:T(8,128)(2,1)} %collective-permute-done.13.refs_0_, bf16[512,1280]{1,0:T(8,128)(2,1)S(1)} %collective-permute-done.14.refs_1_, bf16[5120,640]{1,0:T(8,128)(2,1)} %refs_2_.1, ...), custom_call_target="tpu_custom_call" | custom-call | flops 10000000000 | bytes 1 | tf_op jit(solution)/shard_map/project_end/pallas_call | solution.py:106
  221.5 7.5 %attend.2.refs_6_ = bf16[2,512,640]{2,1,0:T(8,128)(2,1)} custom-call(s32[3]{0:T(128)S(1)} %get-tuple-element.58.info, bf16[5,512,128]{2,1,0:T(8,128)(2,1)S(1)} %get-tuple-element.46.refs_0_, bf16[2,5,512,128]{3,2,1,0:T(8,128)(2,1)S(1)} %select_select_fusion.refs_1_, bf16[2,5,512,128]{3,2,1,0:T(8,128)(2,1)} %collective-permute-done.21.refs_2_, ...), custom_call_target="tpu_custom_call" | custom-call | flops 1342177280 | bytes 3932160 | tf_op jit(solution)/shard_map/attend/pallas_call | solution.py:173
  229.0 7.5 %attend.3 = bf16[2,512,640]{2,1,0:T(8,128)(2,1)} custom-call(s32[3]{0:T(128)S(1)} %get-tuple-element.57.info, bf16[5,512,128]{2,1,0:T(8,128)(2,1)S(1)} %copy-done.5, bf16[2,5,512,128]{3,2,1,0:T(8,128)(2,1)S(1)} %select_select_fusion.refs_1_, bf16[2,5,512,128]{3,2,1,0:T(8,128)(2,1)} %collective-permute-done.21.refs_2_, ...), custom_call_target="tpu_custom_call", output_to_operand_aliasing={{}: (7, {})} | custom-call | flops 1342177280 | bytes 3932160 | tf_op jit(solution)/shard_map/attend/pallas_call | solution.py:173
  (77 shorter events, 32.2 us)
Async XLA Ops:
  3.5 17.3 %collective-permute-start = (bf16[512,1280]{1,0:T(8,128)(2,1)}, bf16[512,1280]{1,0:T(8,128)(2,1)}, u32[]{:S(2)}, u32[]{:S(2)}) collective-permute-start(bf16[512,1280]{1,0:T(8,128)(2,1)} %get-tuple-element.29), channel_id=1, source_target_pairs={{4,0},{8,4},{12,8},{16,12},{20,16},{24,20},{28,24},{5,1},{9,5},{13... | collective-permute-start | bytes 3932168 | tf_op jit(solution)/shard_map/ppermute | solution.py:253
  5.5 5.7 %collective-permute-start.7 = (f32[3,1280]{1,0:T(4,128)S(1)}, f32[3,1280]{1,0:T(4,128)S(1)}, u32[]{:S(2)}, u32[]{:S(2)}) collective-permute-start(f32[3,1280]{1,0:T(4,128)S(1)} %copy-done.11), channel_id=1, source_target_pairs={{1,0},{2,3},{5,4},{6,7},{9,8},{10,11},{13,12},{14,15},{17,16},{18,... | collective-permute-start | bytes 46088 | tf_op jit(solution)/shard_map/ppermute | solution.py:234
  11.1 33.7 %collective-permute-start.8 = (bf16[512,1280]{1,0:T(8,128)(2,1)}, bf16[512,1280]{1,0:T(8,128)(2,1)S(1)}, u32[]{:S(2)}, u32[]{:S(2)}) collective-permute-start(bf16[512,1280]{1,0:T(8,128)(2,1)} %get-tuple-element.29), channel_id=1, source_target_pairs={{1,0},{2,3},{5,4},{6,7},{9,8},{10,11},{13,12},{14,15},{17,16},{18,... | collective-permute-start | bytes 3932168 | tf_op jit(solution)/shard_map/ppermute | solution.py:234
  23.4 48.9 %collective-permute-start.4 = (bf16[512,1280]{1,0:T(8,128)(2,1)S(1)}, bf16[512,1280]{1,0:T(8,128)(2,1)S(1)}, u32[]{:S(2)}, u32[]{:S(2)}) collective-permute-start(bf16[512,1280]{1,0:T(8,128)(2,1)S(1)} %copy-done.10), channel_id=1, source_target_pairs={{1,0},{2,3},{5,4},{6,7},{9,8},{10,11},{13,12},{14,15},{17,16},{18,... | collective-permute-start | bytes 3932168 | tf_op jit(solution)/shard_map/ppermute | solution.py:234
  24.7 47.6 %collective-permute-start.2 = (bf16[512,1280]{1,0:T(8,128)(2,1)S(1)}, bf16[512,1280]{1,0:T(8,128)(2,1)S(1)}, u32[]{:S(2)}, u32[]{:S(2)}) collective-permute-start(bf16[512,1280]{1,0:T(8,128)(2,1)S(1)} %fusion.5.refs_2_), channel_id=1, source_target_pairs={{0,1},{3,2},{4,5},{7,6},{8,9},{11,10},{12,13},{15,14},{16,17},{19,... | collective-permute-start | bytes 3932168 | tf_op jit(solution)/shard_map/ppermute | solution.py:234
  29.5 42.9 %collective-permute-start.3 = (bf16[512,1280]{1,0:T(8,128)(2,1)S(1)}, bf16[512,1280]{1,0:T(8,128)(2,1)S(1)}, u32[]{:S(2)}, u32[]{:S(2)}) collective-permute-start(bf16[512,1280]{1,0:T(8,128)(2,1)S(1)} %fusion.5.refs_2_), channel_id=1, source_target_pairs={{1,2},{2,1},{5,6},{6,5},{9,10},{10,9},{13,14},{14,13},{17,18},{18,... | collective-permute-start | bytes 3932168 | tf_op jit(solution)/shard_map/ppermute | solution.py:234
  31.3 46.6 %collective-permute-start.1 = (bf16[512,1280]{1,0:T(8,128)(2,1)S(1)}, bf16[512,1280]{1,0:T(8,128)(2,1)S(1)}, u32[]{:S(2)}, u32[]{:S(2)}) collective-permute-start(bf16[512,1280]{1,0:T(8,128)(2,1)S(1)} %copy-done.10), channel_id=1, source_target_pairs={{0,4},{4,8},{8,12},{12,16},{16,20},{20,24},{24,28},{1,5},{5,9},{9,... | collective-permute-start | bytes 3932168 | tf_op jit(solution)/shard_map/ppermute | solution.py:259
  44.9 34.3 %collective-permute-start.9 = (bf16[512,1280]{1,0:T(8,128)(2,1)S(1)}, bf16[512,1280]{1,0:T(8,128)(2,1)}, u32[]{:S(2)}, u32[]{:S(2)}) collective-permute-start(bf16[512,1280]{1,0:T(8,128)(2,1)S(1)} %collective-permute-done.8), channel_id=1, source_target_pairs={{4,0},{8,4},{12,8},{16,12},{20,16},{24,20},{28,24},{5,1},{9,5},{13... | collective-permute-start | bytes 3932168 | tf_op jit(solution)/shard_map/ppermute | solution.py:261
  72.4 6.8 %collective-permute-start.5 = (bf16[512,1280]{1,0:T(8,128)(2,1)S(1)}, bf16[512,1280]{1,0:T(8,128)(2,1)}, u32[]{:S(2)}, u32[]{:S(2)}) collective-permute-start(bf16[512,1280]{1,0:T(8,128)(2,1)S(1)} %collective-permute-done.2.refs_3_), channel_id=1, source_target_pairs={{1,2},{2,1},{5,6},{6,5},{9,10},{10,9},{13,14},{14,13},{17,18},{18,... | collective-permute-start | bytes 3932168 | tf_op jit(solution)/shard_map/ppermute | solution.py:234
  74.7 32.1 %collective-permute-start.6 = (bf16[512,1280]{1,0:T(8,128)(2,1)S(1)}, bf16[512,1280]{1,0:T(8,128)(2,1)S(1)}, u32[]{:S(2)}, u32[]{:S(2)}) collective-permute-start(bf16[512,1280]{1,0:T(8,128)(2,1)S(1)} %collective-permute-done.3.refs_5_), channel_id=1, source_target_pairs={{1,0},{2,3},{5,4},{6,7},{9,8},{10,11},{13,12},{14,15},{17,16},{18,... | collective-permute-start | bytes 3932168 | tf_op jit(solution)/shard_map/ppermute | solution.py:234
  76.0 40.5 %collective-permute-start.12 = (bf16[512,1280]{1,0:T(8,128)(2,1)S(1)}, bf16[512,1280]{1,0:T(8,128)(2,1)}, u32[]{:S(2)}, u32[]{:S(2)}) collective-permute-start(bf16[512,1280]{1,0:T(8,128)(2,1)S(1)} %collective-permute-done.4), channel_id=1, source_target_pairs={{0,4},{4,8},{8,12},{12,16},{16,20},{20,24},{24,28},{1,5},{5,9},{9,... | collective-permute-start | bytes 3932168 | tf_op jit(solution)/shard_map/ppermute | solution.py:264
  107.9 13.3 %collective-permute-start.10 = (bf16[512,1280]{1,0:T(8,128)(2,1)S(1)}, bf16[512,1280]{1,0:T(8,128)(2,1)}, u32[]{:S(2)}, u32[]{:S(2)}) collective-permute-start(bf16[512,1280]{1,0:T(8,128)(2,1)S(1)} %fusion.2.refs_1_), channel_id=1, source_target_pairs={{1,2},{2,1},{5,6},{6,5},{9,10},{10,9},{13,14},{14,13},{17,18},{18,... | collective-permute-start | bytes 3932168 | tf_op jit(solution)/shard_map/ppermute | solution.py:234
  109.6 30.9 %collective-permute-start.11 = (bf16[512,1280]{1,0:T(8,128)(2,1)S(1)}, bf16[512,1280]{1,0:T(8,128)(2,1)}, u32[]{:S(2)}, u32[]{:S(2)}) collective-permute-start(bf16[512,1280]{1,0:T(8,128)(2,1)S(1)} %fusion.2.refs_1_), channel_id=1, source_target_pairs={{0,1},{3,2},{4,5},{7,6},{8,9},{11,10},{12,13},{15,14},{16,17},{19,... | collective-permute-start | bytes 3932168 | tf_op jit(solution)/shard_map/ppermute | solution.py:234
  115.1 33.2 %collective-permute-start.15 = (bf16[512,1280]{1,0:T(8,128)(2,1)}, bf16[512,1280]{1,0:T(8,128)(2,1)}, u32[]{:S(2)}, u32[]{:S(2)}) collective-permute-start(bf16[512,1280]{1,0:T(8,128)(2,1)} %collective-permute-done.5.refs_7_), channel_id=1, source_target_pairs={{1,0},{2,3},{5,4},{6,7},{9,8},{10,11},{13,12},{14,15},{17,16},{18,... | collective-permute-start | bytes 3932168 | tf_op jit(solution)/shard_map/ppermute | solution.py:234
  141.3 32.8 %collective-permute-start.17 = (bf16[512,1280]{1,0:T(8,128)(2,1)}, bf16[512,1280]{1,0:T(8,128)(2,1)}, u32[]{:S(2)}, u32[]{:S(2)}) collective-permute-start(bf16[512,1280]{1,0:T(8,128)(2,1)} %collective-permute-done.10.refs_1_.refs_4_), channel_id=1, source_target_pairs={{1,0},{2,3},{5,4},{6,7},{9,8},{10,11},{13,12},{14,15},{17,16},{18,... | collective-permute-start | bytes 3932168 | tf_op jit(solution)/shard_map/ppermute | solution.py:234
  142.6 21.2 %collective-permute-start.16 = (bf16[16,1280]{1,0:T(8,128)(2,1)S(1)}, bf16[16,1280]{1,0:T(8,128)(2,1)S(1)}, u32[]{:S(2)}, u32[]{:S(2)}) collective-permute-start(bf16[16,1280]{1,0:T(8,128)(2,1)S(1)} %slice.45), channel_id=1, source_target_pairs={{0,4},{4,0},{8,12},{12,8},{16,20},{20,16},{24,28},{28,24},{1,5},{5... | collective-permute-start | bytes 122888 | tf_op jit(solution)/shard_map/ppermute | solution.py:275
  142.7 26.1 %collective-permute-start.13 = (bf16[512,1280]{1,0:T(8,128)(2,1)}, bf16[512,1280]{1,0:T(8,128)(2,1)}, u32[]{:S(2)}, u32[]{:S(2)}) collective-permute-start(bf16[512,1280]{1,0:T(8,128)(2,1)} %collective-permute-done.11.refs_0_.refs_2_), channel_id=1, source_target_pairs={{1,2},{2,1},{5,6},{6,5},{9,10},{10,9},{13,14},{14,13},{17,18},{18,... | collective-permute-start | bytes 3932168 | tf_op jit(solution)/shard_map/ppermute | solution.py:234
  163.8 25.5 %collective-permute-start.18 = (bf16[2,5,512,128]{3,2,1,0:T(8,128)(2,1)S(1)}, bf16[2,5,512,128]{3,2,1,0:T(8,128)(2,1)}, u32[]{:S(2)}, u32[]{:S(2)}) collective-permute-start(bf16[2,5,512,128]{3,2,1,0:T(8,128)(2,1)S(1)} %get-tuple-element.44.refs_3_), channel_id=1, source_target_pairs={{0,24},{1,25},{2,26},{3,27}} | collective-permute-start | bytes 3932168 | tf_op jit(solution)/shard_map/ppermute | solution.py:202
  165.1 24.2 %collective-permute-start.19 = (bf16[2,5,512,128]{3,2,1,0:T(8,128)(2,1)S(1)}, bf16[2,5,512,128]{3,2,1,0:T(8,128)(2,1)}, u32[]{:S(2)}, u32[]{:S(2)}) collective-permute-start(bf16[2,5,512,128]{3,2,1,0:T(8,128)(2,1)S(1)} %get-tuple-element.44.refs_3_), channel_id=1, source_target_pairs={{0,16},{1,17},{2,18},{3,19}} | collective-permute-start | bytes 3932168 | tf_op jit(solution)/shard_map/ppermute | solution.py:202
  166.8 22.5 %collective-permute-start.20 = (bf16[2,5,512,128]{3,2,1,0:T(8,128)(2,1)S(1)}, bf16[2,5,512,128]{3,2,1,0:T(8,128)(2,1)}, u32[]{:S(2)}, u32[]{:S(2)}) collective-permute-start(bf16[2,5,512,128]{3,2,1,0:T(8,128)(2,1)S(1)} %get-tuple-element.44.refs_3_), channel_id=1, source_target_pairs={{0,8},{1,9},{2,10},{3,11}} | collective-permute-start | bytes 3932168 | tf_op jit(solution)/shard_map/ppermute | solution.py:202
  168.8 41.1 %collective-permute-start.14 = (bf16[512,1280]{1,0:T(8,128)(2,1)}, bf16[512,1280]{1,0:T(8,128)(2,1)S(1)}, u32[]{:S(2)}, u32[]{:S(2)}) collective-permute-start(bf16[512,1280]{1,0:T(8,128)(2,1)} %collective-permute-done.13.refs_0_), channel_id=1, source_target_pairs={{1,0},{2,3},{5,4},{6,7},{9,8},{10,11},{13,12},{14,15},{17,16},{18,... | collective-permute-start | bytes 3932168 | tf_op jit(solution)/shard_map/ppermute | solution.py:234
  190.8 30.7 %collective-permute-start.21 = (bf16[2,5,512,128]{3,2,1,0:T(8,128)(2,1)S(1)}, bf16[2,5,512,128]{3,2,1,0:T(8,128)(2,1)}, u32[]{:S(2)}, u32[]{:S(2)}) collective-permute-start(bf16[2,5,512,128]{3,2,1,0:T(8,128)(2,1)S(1)} %select_select_fusion.refs_1_), channel_id=1, source_target_pairs={{0,4},{8,12},{16,20},{24,28},{1,5},{9,13},{17,21},{25,29},{2,6},{1... | collective-permute-start | bytes 3932168 | tf_op jit(solution)/shard_map/ppermute | solution.py:203
  193.2 35.8 %collective-permute-start.22 = (bf16[2,5,512,128]{3,2,1,0:T(8,128)(2,1)S(1)}, bf16[2,5,512,128]{3,2,1,0:T(8,128)(2,1)}, u32[]{:S(2)}, u32[]{:S(2)}) collective-permute-start(bf16[2,5,512,128]{3,2,1,0:T(8,128)(2,1)S(1)} %get-tuple-element.44.refs_3_), channel_id=1, source_target_pairs={{4,8},{8,12},{12,16},{16,20},{20,24},{24,28},{5,9},{9,13},{13,17},... | collective-permute-start | bytes 3932168 | tf_op jit(solution)/shard_map/ppermute | solution.py:280
  219.7 9.3 %collective-permute-start.23 = (bf16[2,5,512,128]{3,2,1,0:T(8,128)(2,1)}, bf16[2,5,512,128]{3,2,1,0:T(8,128)(2,1)}, u32[]{:S(2)}, u32[]{:S(2)}) collective-permute-start(bf16[2,5,512,128]{3,2,1,0:T(8,128)(2,1)} %get-tuple-element.45.refs_4_), channel_id=1, source_target_pairs={{0,4},{1,5},{2,6},{3,7}} | collective-permute-start | bytes 3932168 | tf_op jit(solution)/shard_map/ppermute | solution.py:283
  (17 other events, 411.9 us)

commit v12 on v11

--- a/solution.py
+++ b/solution.py
@@ -22,28 +22,21 @@
     return (part * lax.rsqrt(total * (1.0 / DH) + 1e-06) * gain).astype(BF16)
 
 
-def store_heads(acc, qg, kg, q_out, kv_out):
-    heads = q_out.shape[0]
-
-    def columns(group, h):
-        return acc[:, (group * heads + h) * DH : (group * heads + h + 1) * DH]
-
-    for h in range(heads):
-        span = slice(h * DH, (h + 1) * DH)
-        q_out[h] = normalized(columns(0, h), qg[:, span])
-        kv_out[0, h] = normalized(columns(1, h), kg[:, span])
-        kv_out[1, h] = columns(2, h).astype(BF16)
-
-
-def project_body(pairs, extra, has_acc, final, info, *refs):
+def store_head(raw, gains, q_out, kv_out, h):
+    q_out[h] = normalized(raw[0], gains[0])
+    kv_out[0, h] = normalized(raw[1], gains[1])
+    kv_out[1, h] = raw[2].astype(BF16)
+
+
+def project_body(pairs, extra, final, info, *refs):
     refs = list(refs)[extra:]
     count = len(pairs)
     groups = [[refs.pop(0) for _ in range(n)] for n in pairs]
     weights = [refs.pop(0) for _ in range(3)]
     gains = [refs.pop(0) for _ in range(2)] if final else None
-    start = refs.pop(0) if has_acc else None
     outs = [refs.pop(0) for _ in range(2)] if final else None
     acc, xbuf, sem = refs
+    heads = weights[0].shape[1] // DH
     step = pl.program_id(0)
 
     @pl.when(step == 0)
@@ -62,30 +55,35 @@
             pltpu.make_async_copy(groups[i][0], xbuf.at[i], sem.at[i]).wait()
             weight = jnp.concatenate([w[...] for w in weights], axis=1)
             part = jnp.dot(xbuf[i], weight, preferred_element_type=F32)
-            if i == 0:
-                acc[...] = part + start[...] if has_acc else part
+            if final:
+                acc[...] = part if i == 0 else acc[...] + part
             else:
-                acc[...] += part
+                for group in range(3):
+                    for h in range(heads):
+                        columns = part[:, (group * heads + h) * DH : (group * heads + h + 1) * DH]
+                        acc[group, h] = columns if i == 0 else acc[group, h] + columns
 
     if final:
 
         @pl.when(step == count - 1)
         def _():
-            store_heads(acc, gains[0][...], gains[1][...], *outs)
-
-
-def project(sources, info, weights, gains=None, acc=None, after=(), flops=1):
+            for h in range(heads):
+                total = [acc[:, (group * heads + h) * DH : (group * heads + h + 1) * DH] for group in range(3)]
+                store_head(total, [g[:, h * DH : (h + 1) * DH] for g in gains], *outs, h)
+
+
+def project(sources, info, weights, gains=None, after=(), flops=1):
     pairs = [len(s) for s in sources]
     count = len(pairs)
     rows, chans = sources[0][0].shape
     width = weights[0].shape[1]
     heads = width // DH
     final = gains is not None
-    a_spec = pl.BlockSpec((rows, 3 * width), lambda k, info: (0, 0))
+    a_spec = pl.BlockSpec((3, heads, rows, DH), lambda k, info: (0, 0, 0, 0))
     in_specs = [ANY] * (len(after) + sum(pairs)) + [pl.BlockSpec((chans, width), lambda k, info: (info[1 + k], 0))] * 3
     args = list(after) + [x for s in sources for x in s] + list(weights)
     scratch = [pltpu.VMEM((count, rows, chans), BF16), pltpu.SemaphoreType.DMA((count,))]
-    raw = jax.ShapeDtypeStruct((rows, 3 * width), F32)
+    raw = jax.ShapeDtypeStruct((3, heads, rows, DH), F32)
     if final:
         in_specs += [pl.BlockSpec((1, width), lambda k, info: (0, 0))] * 2
         args += [g[None] for g in gains]
@@ -97,14 +95,11 @@
             pl.BlockSpec((heads, rows, DH), lambda k, info: (0, 0, 0)),
             pl.BlockSpec((2, heads, rows, DH), lambda k, info: (0, 0, 0, 0)),
         ]
-        scratch = [pltpu.VMEM(raw.shape, F32)] + scratch
+        scratch = [pltpu.VMEM((rows, 3 * width), F32)] + scratch
     else:
         out_shape, out_specs = raw, a_spec
-    if acc is not None:
-        in_specs.append(a_spec)
-        args.append(acc)
     return pl.pallas_call(
-        functools.partial(project_body, pairs, len(after), acc is not None, final),
+        functools.partial(project_body, pairs, len(after), final),
         grid_spec=pltpu.PrefetchScalarGridSpec(
             num_scalar_prefetch=1,
             grid=(count,),
@@ -119,6 +114,53 @@
     )(info, *args)
 
 
+def finish_body(info, inner, outer, wq, wk, wv, qg, kg, raw, q_out, kv_out, rows, sem):
+    @pl.when(pl.program_id(0) == 0)
+    def _():
+        for side, source in enumerate((inner, outer)):
+
+            @pl.when(info[0] == side)
+            def _(source=source):
+                pltpu.make_async_copy(source, rows, sem).start()
+
+        pltpu.make_async_copy(inner, rows, sem).wait()
+
+    weight = jnp.concatenate([wq[...], wk[...], wv[...]], axis=1)
+    part = jnp.dot(rows[...], weight, preferred_element_type=F32)
+    total = [raw[group, 0] + part[:, group * DH : (group + 1) * DH] for group in range(3)]
+    store_head(total, (qg[...], kg[...]), q_out, kv_out, 0)
+
+
+def finish(raw, inner, outer, info, weights, gains, flops):
+    rows, chans = inner.shape
+    heads = raw.shape[1]
+    w_spec = pl.BlockSpec((chans, DH), lambda h, info: (info[1], h))
+    g_spec = pl.BlockSpec((1, DH), lambda h, info: (0, h))
+    return pl.pallas_call(
+        finish_body,
+        grid_spec=pltpu.PrefetchScalarGridSpec(
+            num_scalar_prefetch=1,
+            grid=(heads,),
+            in_specs=[ANY] * 2
+            + [w_spec] * 3
+            + [g_spec] * 2
+            + [pl.BlockSpec((3, 1, rows, DH), lambda h, info: (0, h, 0, 0))],
+            out_specs=[
+                pl.BlockSpec((1, rows, DH), lambda h, info: (h, 0, 0)),
+                pl.BlockSpec((2, 1, rows, DH), lambda h, info: (0, h, 0, 0)),
+            ],
+            scratch_shapes=[pltpu.VMEM((rows, chans), BF16), pltpu.SemaphoreType.DMA],
+        ),
+        out_shape=[
+            jax.ShapeDtypeStruct((heads, rows, DH), BF16),
+            jax.ShapeDtypeStruct((2, heads, rows, DH), BF16),
+        ],
+        compiler_params=pltpu.CompilerParams(vmem_limit_bytes=32 * 2**20),
+        cost_estimate=pl.CostEstimate(flops=flops, bytes_accessed=1, transcendentals=0),
+        name="finish",
+    )(info, inner, outer, *weights, *(g[None] for g in gains), raw)
+
+
 def attend_body(row_block, choices, fresh, info, *refs):
     refs = list(refs)
     query = refs.pop(0)
@@ -147,12 +189,18 @@
     key = jnp.concatenate([held[0, 0, h], held[1, 0, h]], axis=0)
     value = jnp.concatenate([held[0, 1, h], held[1, 1, h]], axis=0)
     value = jnp.concatenate([value, jnp.ones_like(value)], axis=1)
-    rows = query.shape[1]
-    for r in range(rows // row_block):
-        span = pl.ds(r * row_block, row_block)
-        scores = lax.dot_general(
+    spans = [pl.ds(row, row_block) for row in range(0, query.shape[1], row_block)]
+
+    def score(span):
+        return lax.dot_general(
             query[0, span, :], key, (((1,), (1,)), ((), ())), preferred_element_type=F32
         )
+
+    ahead = score(spans[0])
+    for r, span in enumerate(spans):
+        scores = ahead
+        if r + 1 < len(spans):
+            ahead = score(spans[r + 1])
         tops = [scores[:, c : c + DH] for c in range(0, scores.shape[1], DH)]
         top = jnp.max(functools.reduce(jnp.maximum, tops), axis=-1, keepdims=True)
         expo = jnp.exp2((scores - top) * factor).astype(BF16)
@@ -162,20 +210,17 @@
 
 def attend(query, anchors, anchor, options, choice, frame, partly=None):
     heads, rows, _ = query.shape
-    in_specs = [pl.BlockSpec((1, rows, DH), lambda h, info: (h, 0, 0))]
-    in_specs += [ANY] * (len(anchors) + len(options))
     args = [query, *anchors, *options]
     aliases = {}
     if partly is not None:
-        in_specs.append(ANY)
         aliases = {1 + len(args): 0}
         args.append(partly)
     return pl.pallas_call(
-        functools.partial(attend_body, 128, (len(anchors), len(options)), partly is None),
+        functools.partial(attend_body, 256, (len(anchors), len(options)), partly is None),
         grid_spec=pltpu.PrefetchScalarGridSpec(
             num_scalar_prefetch=1,
             grid=(heads,),
-            in_specs=in_specs,
+            in_specs=[pl.BlockSpec((1, rows, DH), lambda h, info: (h, 0, 0))] + [ANY] * (len(args) - 1),
             out_specs=pl.BlockSpec((1, rows, DH), lambda h, info: (info[1], 0, h)),
             scratch_shapes=[
                 pltpu.VMEM((2, 2, heads, rows, DH), BF16),
@@ -259,11 +304,12 @@
     raw_last, preceding = send(last, OUTWARD), lax.ppermute(last, "tm", ups)
     mixed2 = mix_second(frames[0], frames[1], following, preceding, taps)
     raw_following = lax.ppermute(raw_first, "tm", downs)
-    inward1, middle1, raw_last = hold((inward1, middle1, raw_last))
+    inward1, middle1 = hold((inward1, middle1))
     cross1, second1 = send(inward1, MIDDLE), send(middle1, OUTWARD)
     raw_preceding = lax.ppermute(raw_last, "tm", ups)
-    later2, cross1, second1, raw_following = hold((mixed2, cross1, second1, raw_following))
-    middle2, inward2 = send(later2, MIDDLE), send(later2, INWARD)
+    level = (mixed2, cross1, second1, raw_following, raw_preceding)
+    later2, cross1, second1, raw_following, raw_preceding = hold(level)
+    middle2, inward2 = send(later2, MIDDLE), send(mixed2, INWARD)
     third1 = send(cross1, OUTWARD)
     first1 = mix_first(raw_first, raw_last, raw_following, outer_taps)
     first2 = mix_second(raw_first, raw_last, raw_following, raw_preceding, outer_taps)
@@ -272,14 +318,14 @@
 
     sources1 = [(mixed1,), (inward1, first1), (middle1, second1), (cross1, third1)]
     q1, kv1 = project(sources1, info, weights, gains, after=(inward2, middle2), flops=10**10)
-    beside = lax.ppermute(middle2[:16], "tm", [(i, i ^ 1) for i in range(count)])
+    beside = lax.ppermute(inward2[:16], "tm", [(i, i ^ 1) for i in range(count)])
     kv1, beside = hold((kv1, beside))
     third2 = send(cross2, OUTWARD)
     anchor = broadcast_first(kv1, "tm")
     later1, _ = hold((kv1, anchor[0]))
     shift1 = lax.ppermute(later1, "tm", [(i, i + 1) for i in range(1, count - 1)])
     raw2 = project([(mixed2,), (inward2, first2), (middle2, second2)], info_raw, weights, after=(beside,), flops=10**10)
-    q2, kv2 = project([(cross2, third2)], info_end, weights, gains, raw2, flops=10**10)
+    q2, kv2 = finish(raw2, cross2, third2, info_end, weights, gains, 10**10)
     shift2 = lax.ppermute(kv2, "tm", [(0, 1)])
     late = jnp.where(start, 0, 1)
     odd = pos % 2

time: 238 us -> 230 us (0.966)
  the two profiles are of different devices: /device:TPU:6 before, /device:TPU:10 now
where the time goes in v12:
time: 230 us; the launch traced here: 227 us
  waiting for transfers between devices  94.5 us (41%)
  starting transfers between devices  55.3 us (24%)
  Pallas kernels  52.9 us (23%)
  local copies, waits for them, and re-layouts  13.5 us (6%)
  other arithmetic  10.1 us (4%)
    ppermute x13, waiting for transfers between devices, send(): return lax.ppermute(x, 'head', pairs)  78.2 us
    ppermute x13, starting transfers between devices, send(): return lax.ppermute(x, 'head', pairs)  34.6 us
    pallas_call x2, Pallas kernels, project(): pl.pallas_call(functools.partial(project_body, pairs, len(after), final),...  29.3 us
    pallas_call x2, Pallas kernels, attend(): pl.pallas_call(functools.partial(attend_body, 256, (len(anchors), len(opt...  14.2 us
    pallas_call x1, Pallas kernels, finish(): pl.pallas_call(finish_body, grid_spec=pltpu.PrefetchScalarGridSpec(num_sc...  9.42 us
    unnamed x44, local copies, waits for them, and re-layouts  9.02 us
    ppermute x3, waiting for transfers between devices, broadcast_first(): held = jnp.where(mine == to, lax.ppermute(x, axis, [(0, to)]), held)  8.97 us
    convert_element_type x3, other arithmetic, mix(): (centre + taps[0] * before + taps[1] * centre + taps[2] * after).astype(B...  8.37 us
  transfers between devices with their start and end apart: 24, of which 12 were waited for; matrix products, arithmetic and copies ran while one was open for 5% of the time, Pallas kernels for 20%

profile of v12, /device:TPU:10, one launch (start us, length us, event | category | flops | bytes accessed | tf_op | source)
XLA Modules:
  0.0 227.0 jit_solution(1919083605249843343)
XLA Ops:
  0.0 3.5 %slice_bitcast_fusion.1 = (bf16[512,1280]{1,0:T(8,128)(2,1)}, bf16[512,1280]{1,0:T(8,128)(2,1)}) fusion(bf16[2,512,1280]{2,1,0:T(8,128)(2,1)} %param.7), kind=kLoop, calls=%fused_computation.22 | loop fusion | bytes 5242880 | tf_op jit(solution)/shard_map/squeeze | solution.py:305
  9.3 4.3 %collective-permute-start.7 = (bf16[512,1280]{1,0:T(8,128)(2,1)}, bf16[512,1280]{1,0:T(8,128)(2,1)S(1)}, u32[]{:S(2)}, u32[]{:S(2)}) collective-permute-start(bf16[512,1280]{1,0:T(8,128)(2,1)} %get-tuple-element.29), channel_id=1, source_target_pairs={{1,0},{2,3},{5,4},{6,7},{9,8},{10,11},{13,12},{14,15},{17,16},{18,... | collective-permute-start | bytes 3932168 | tf_op jit(solution)/shard_map/ppermute | solution.py:279
  13.6 7.3 %collective-permute-done = bf16[512,1280]{1,0:T(8,128)(2,1)} collective-permute-done((bf16[512,1280]{1,0:T(8,128)(2,1)}, bf16[512,1280]{1,0:T(8,128)(2,1)}, u32[]{:S(2)}, u32[]{:S(2)}) %collective-permute-start) | collective-permute-done | bytes 1310752 | tf_op jit(solution)/shard_map/ppermute | solution.py:298
  24.7 3.5 %collective-permute-start.3 = (bf16[512,1280]{1,0:T(8,128)(2,1)S(1)}, bf16[512,1280]{1,0:T(8,128)(2,1)S(1)}, u32[]{:S(2)}, u32[]{:S(2)}) collective-permute-start(bf16[512,1280]{1,0:T(8,128)(2,1)S(1)} %fusion.5.refs_2_), channel_id=1, source_target_pairs={{1,2},{2,1},{5,6},{6,5},{9,10},{10,9},{13,14},{14,13},{17,18},{18,... | collective-permute-start | bytes 3932168 | tf_op jit(solution)/shard_map/ppermute | solution.py:279
  31.4 4.0 %collective-permute-start.1 = (bf16[512,1280]{1,0:T(8,128)(2,1)S(1)}, bf16[512,1280]{1,0:T(8,128)(2,1)S(1)}, u32[]{:S(2)}, u32[]{:S(2)}) collective-permute-start(bf16[512,1280]{1,0:T(8,128)(2,1)S(1)} %copy-done.15), channel_id=1, source_target_pairs={{0,4},{4,8},{8,12},{12,16},{16,20},{20,24},{24,28},{1,5},{5,9},{9,... | collective-permute-start | bytes 3932168 | tf_op jit(solution)/shard_map/ppermute | solution.py:304
  35.4 7.7 %collective-permute-done.7 = bf16[512,1280]{1,0:T(8,128)(2,1)S(1)} collective-permute-done((bf16[512,1280]{1,0:T(8,128)(2,1)}, bf16[512,1280]{1,0:T(8,128)(2,1)S(1)}, u32[]{:S(2)}, u32[]{:S(2)}) %collective-permute-start.7) | collective-permute-done | bytes 1310752 | tf_op jit(solution)/shard_map/ppermute | solution.py:279
  44.9 10.3 %collective-permute-done.2.refs_3_ = bf16[512,1280]{1,0:T(8,128)(2,1)S(1)} collective-permute-done((bf16[512,1280]{1,0:T(8,128)(2,1)S(1)}, bf16[512,1280]{1,0:T(8,128)(2,1)S(1)}, u32[]{:S(2)}, u32[]{:S(2)}) %collective-permute-start.2) | collective-permute-done | bytes 1310752 | tf_op jit(solution)/shard_map/ppermute | solution.py:279
  56.5 3.5 %collective-permute-start.4 = (bf16[512,1280]{1,0:T(8,128)(2,1)S(1)}, bf16[512,1280]{1,0:T(8,128)(2,1)}, u32[]{:S(2)}, u32[]{:S(2)}) collective-permute-start(bf16[512,1280]{1,0:T(8,128)(2,1)S(1)} %collective-permute-done.2.refs_3_), channel_id=1, source_target_pairs={{1,2},{2,1},{5,6},{6,5},{9,10},{10,9},{13,14},{14,13},{17,18},{18,... | collective-permute-start | bytes 3932168 | tf_op jit(solution)/shard_map/ppermute | solution.py:279
  61.4 9.6 %collective-permute-done.9 = bf16[512,1280]{1,0:T(8,128)(2,1)S(1)} collective-permute-done((bf16[512,1280]{1,0:T(8,128)(2,1)S(1)}, bf16[512,1280]{1,0:T(8,128)(2,1)S(1)}, u32[]{:S(2)}, u32[]{:S(2)}) %collective-permute-start.9) | collective-permute-done | bytes 1310752 | tf_op jit(solution)/shard_map/ppermute | solution.py:279
  75.5 14.2 %collective-permute-done.4.refs_7_ = bf16[512,1280]{1,0:T(8,128)(2,1)} collective-permute-done((bf16[512,1280]{1,0:T(8,128)(2,1)S(1)}, bf16[512,1280]{1,0:T(8,128)(2,1)}, u32[]{:S(2)}, u32[]{:S(2)}) %collective-permute-start.4) | collective-permute-done | bytes 1310752 | tf_op jit(solution)/shard_map/ppermute | solution.py:279
  89.7 7.8 %collective-permute-done.5.refs_6_ = bf16[512,1280]{1,0:T(8,128)(2,1)S(1)} collective-permute-done((bf16[512,1280]{1,0:T(8,128)(2,1)S(1)}, bf16[512,1280]{1,0:T(8,128)(2,1)S(1)}, u32[]{:S(2)}, u32[]{:S(2)}) %collective-permute-start.5) | collective-permute-done | bytes 1310752 | tf_op jit(solution)/shard_map/ppermute | solution.py:279
  97.4 4.6 %collective-permute-start.11 = (bf16[512,1280]{1,0:T(8,128)(2,1)S(1)}, bf16[512,1280]{1,0:T(8,128)(2,1)}, u32[]{:S(2)}, u32[]{:S(2)}) collective-permute-start(bf16[512,1280]{1,0:T(8,128)(2,1)S(1)} %fusion.2.refs_1_), channel_id=1, source_target_pairs={{1,2},{2,1},{5,6},{6,5},{9,10},{10,9},{13,14},{14,13},{17,18},{18,... | collective-permute-start | bytes 3932168 | tf_op jit(solution)/shard_map/ppermute | solution.py:279
  105.0 4.7 %fusion.11 = (bf16[512,1280]{1,0:T(8,128)(2,1)S(1)}, bf16[512,1280]{1,0:T(8,128)(2,1)}) fusion(bf16[512,1280]{1,0:T(8,128)(2,1)} %copy-done.13, bf16[512,1280]{1,0:T(8,128)(2,1)} %copy-done.12, bf16[512,1280]{1,0:T(8,128)(2,1)} %copy-done.11, bf16[512,1280]{1,0:T(8,128)(2,1)} %copy-done.14, f32[1280]{0:T(1024)S(1)} %get-tuple-element.48, ...), kind=kLoop, calls=%fused_computation.19 | loop fusion | flops 17039360 | bytes 7879681 | tf_op jit(solution)/shard_map/convert_element_type | solution.py:258
  109.7 19.8 %collective-permute-done.11.refs_1_.refs_4_ = bf16[512,1280]{1,0:T(8,128)(2,1)} collective-permute-done((bf16[512,1280]{1,0:T(8,128)(2,1)S(1)}, bf16[512,1280]{1,0:T(8,128)(2,1)}, u32[]{:S(2)}, u32[]{:S(2)}) %collective-permute-start.11) | collective-permute-done | bytes 1310752 | tf_op jit(solution)/shard_map/ppermute | solution.py:279
  130.3 3.6 %collective-permute-start.13 = (bf16[512,1280]{1,0:T(8,128)(2,1)}, bf16[512,1280]{1,0:T(8,128)(2,1)}, u32[]{:S(2)}, u32[]{:S(2)}) collective-permute-start(bf16[512,1280]{1,0:T(8,128)(2,1)} %collective-permute-done.12.refs_0_.refs_2_), channel_id=1, source_target_pairs={{1,2},{2,1},{5,6},{6,5},{9,10},{10,9},{13,14},{14,13},{17,18},{18,... | collective-permute-start | bytes 3932168 | tf_op jit(solution)/shard_map/ppermute | solution.py:279
  136.4 15.5 %project_end.1 = (bf16[5,512,128]{2,1,0:T(8,128)(2,1)S(1)}, bf16[2,5,512,128]{3,2,1,0:T(8,128)(2,1)S(1)}) custom-call(s32[5]{0:T(128)S(1)} %stack.65.info, bf16[512,1280]{1,0:T(8,128)(2,1)} %collective-permute-done.12.refs_0_.refs_2_, bf16[512,1280]{1,0:T(8,128)(2,1)} %collective-permute-done.11.refs_1_.refs_4_, bf16[512,1280]{1,0:T(8,128)(2,1)S(1)} %copy-done.1, ...), custom_call_target="tpu_custom_call" | custom-call | flops 10000000000 | bytes 1 | tf_op jit(solution)/shard_map/project_end/pallas_call | solution.py:101
  156.9 4.0 %collective-permute-done.13.inner = bf16[512,1280]{1,0:T(8,128)(2,1)} collective-permute-done((bf16[512,1280]{1,0:T(8,128)(2,1)}, bf16[512,1280]{1,0:T(8,128)(2,1)}, u32[]{:S(2)}, u32[]{:S(2)}) %collective-permute-start.13) | collective-permute-done | bytes 1310752 | tf_op jit(solution)/shard_map/ppermute | solution.py:279
  166.1 13.7 %project_raw.1.raw = f32[3,5,512,128]{3,2,1,0:T(8,128)} custom-call(s32[4]{0:T(128)S(1)} %pad_add_fusion.2.info, bf16[16,1280]{1,0:T(8,128)(2,1)S(1)} %collective-permute-done.16.refs_0_, bf16[512,1280]{1,0:T(8,128)(2,1)S(1)} %copy-done.3, bf16[512,1280]{1,0:T(8,128)(2,1)} %collective-permute-done.12.refs_0_.refs_2_, ...), custom_call_target="tpu_custom_call" | custom-call | flops 10000000000 | bytes 1 | tf_op jit(solution)/shard_map/project_raw/pallas_call | solution.py:101
  179.9 9.0 %collective-permute-done.20 = bf16[2,5,512,128]{3,2,1,0:T(8,128)(2,1)} collective-permute-done((bf16[2,5,512,128]{3,2,1,0:T(8,128)(2,1)S(1)}, bf16[2,5,512,128]{3,2,1,0:T(8,128)(2,1)}, u32[]{:S(2)}, u32[]{:S(2)}) %collective-permute-start.20) | collective-permute-done | bytes 1310752 | tf_op jit(solution)/shard_map/ppermute | solution.py:247
  194.7 2.9 %copy-done.6 = bf16[5120,640]{1,0:T(8,128)(2,1)S(1)} copy-done((bf16[5120,640]{1,0:T(8,128)(2,1)S(1)}, bf16[5120,640]{1,0:T(8,128)(2,1)}, u32[]{:S(2)}) %copy-start.6) | copy-done | bytes 6553624
  197.6 2.9 %copy-done.7 = bf16[5120,640]{1,0:T(8,128)(2,1)S(1)} copy-done((bf16[5120,640]{1,0:T(8,128)(2,1)S(1)}, bf16[5120,640]{1,0:T(8,128)(2,1)}, u32[]{:S(2)}) %copy-start.7) | copy-done | bytes 6553624
  200.4 9.4 %finish.1 = (bf16[5,512,128]{2,1,0:T(8,128)(2,1)S(1)}, bf16[2,5,512,128]{3,2,1,0:T(8,128)(2,1)}) custom-call(s32[2]{0:T(128)S(1)} %pad_add_fusion.1.info, bf16[512,1280]{1,0:T(8,128)(2,1)} %collective-permute-done.13.inner, bf16[512,1280]{1,0:T(8,128)(2,1)S(1)} %collective-permute-done.14.outer, bf16[5120,640]{1,0:T(8,128)(2,1)S(1)} %copy-done.6, ...), custom_call_target="tpu_custom_call" | custom-call | flops 10000000000 | bytes 1 | tf_op jit(solution)/shard_map/finish/pallas_call | solution.py:139
  212.6 7.1 %attend.2.refs_6_ = bf16[2,512,640]{2,1,0:T(8,128)(2,1)} custom-call(s32[3]{0:T(128)S(1)} %get-tuple-element.58.info, bf16[5,512,128]{2,1,0:T(8,128)(2,1)S(1)} %get-tuple-element.46.refs_0_, bf16[2,5,512,128]{3,2,1,0:T(8,128)(2,1)S(1)} %select_select_fusion.refs_1_, bf16[2,5,512,128]{3,2,1,0:T(8,128)(2,1)} %collective-permute-done.21.refs_2_, ...), custom_call_target="tpu_custom_call" | custom-call | flops 1342177280 | bytes 3932160 | tf_op jit(solution)/shard_map/attend/pallas_call | solution.py:218
  219.7 7.1 %attend.3 = bf16[2,512,640]{2,1,0:T(8,128)(2,1)} custom-call(s32[3]{0:T(128)S(1)} %get-tuple-element.57.info, bf16[5,512,128]{2,1,0:T(8,128)(2,1)S(1)} %copy-done.5, bf16[2,5,512,128]{3,2,1,0:T(8,128)(2,1)S(1)} %select_select_fusion.refs_1_, bf16[2,5,512,128]{3,2,1,0:T(8,128)(2,1)} %collective-permute-done.21.refs_2_, ...), custom_call_target="tpu_custom_call", output_to_operand_aliasing={{}: (7, {})} | custom-call | flops 1342177280 | bytes 3932160 | tf_op jit(solution)/shard_map/attend/pallas_call | solution.py:218
  (87 shorter events, 46.5 us)
Async XLA Ops:
  3.5 17.3 %collective-permute-start = (bf16[512,1280]{1,0:T(8,128)(2,1)}, bf16[512,1280]{1,0:T(8,128)(2,1)}, u32[]{:S(2)}, u32[]{:S(2)}) collective-permute-start(bf16[512,1280]{1,0:T(8,128)(2,1)} %get-tuple-element.29), channel_id=1, source_target_pairs={{4,0},{8,4},{12,8},{16,12},{20,16},{24,20},{28,24},{5,1},{9,5},{13... | collective-permute-start | bytes 3932168 | tf_op jit(solution)/shard_map/ppermute | solution.py:298
  5.5 3.8 %collective-permute-start.6 = (f32[3,1280]{1,0:T(4,128)S(1)}, f32[3,1280]{1,0:T(4,128)S(1)}, u32[]{:S(2)}, u32[]{:S(2)}) collective-permute-start(f32[3,1280]{1,0:T(4,128)S(1)} %copy-done.16), channel_id=1, source_target_pairs={{1,0},{2,3},{5,4},{6,7},{9,8},{10,11},{13,12},{14,15},{17,16},{18,... | collective-permute-start | bytes 46088 | tf_op jit(solution)/shard_map/ppermute | solution.py:279
  9.3 33.7 %collective-permute-start.7 = (bf16[512,1280]{1,0:T(8,128)(2,1)}, bf16[512,1280]{1,0:T(8,128)(2,1)S(1)}, u32[]{:S(2)}, u32[]{:S(2)}) collective-permute-start(bf16[512,1280]{1,0:T(8,128)(2,1)} %get-tuple-element.29), channel_id=1, source_target_pairs={{1,0},{2,3},{5,4},{6,7},{9,8},{10,11},{13,12},{14,15},{17,16},{18,... | collective-permute-start | bytes 3932168 | tf_op jit(solution)/shard_map/ppermute | solution.py:279
  23.4 31.8 %collective-permute-start.2 = (bf16[512,1280]{1,0:T(8,128)(2,1)S(1)}, bf16[512,1280]{1,0:T(8,128)(2,1)S(1)}, u32[]{:S(2)}, u32[]{:S(2)}) collective-permute-start(bf16[512,1280]{1,0:T(8,128)(2,1)S(1)} %fusion.5.refs_2_), channel_id=1, source_target_pairs={{0,1},{3,2},{4,5},{7,6},{8,9},{11,10},{12,13},{15,14},{16,17},{19,... | collective-permute-start | bytes 3932168 | tf_op jit(solution)/shard_map/ppermute | solution.py:279
  24.7 31.8 %collective-permute-start.3 = (bf16[512,1280]{1,0:T(8,128)(2,1)S(1)}, bf16[512,1280]{1,0:T(8,128)(2,1)S(1)}, u32[]{:S(2)}, u32[]{:S(2)}) collective-permute-start(bf16[512,1280]{1,0:T(8,128)(2,1)S(1)} %fusion.5.refs_2_), channel_id=1, source_target_pairs={{1,2},{2,1},{5,6},{6,5},{9,10},{10,9},{13,14},{14,13},{17,18},{18,... | collective-permute-start | bytes 3932168 | tf_op jit(solution)/shard_map/ppermute | solution.py:279
  29.3 41.7 %collective-permute-start.9 = (bf16[512,1280]{1,0:T(8,128)(2,1)S(1)}, bf16[512,1280]{1,0:T(8,128)(2,1)S(1)}, u32[]{:S(2)}, u32[]{:S(2)}) collective-permute-start(bf16[512,1280]{1,0:T(8,128)(2,1)S(1)} %copy-done.15), channel_id=1, source_target_pairs={{1,0},{2,3},{5,4},{6,7},{9,8},{10,11},{13,12},{14,15},{17,16},{18,... | collective-permute-start | bytes 3932168 | tf_op jit(solution)/shard_map/ppermute | solution.py:279
  31.4 41.5 %collective-permute-start.1 = (bf16[512,1280]{1,0:T(8,128)(2,1)S(1)}, bf16[512,1280]{1,0:T(8,128)(2,1)S(1)}, u32[]{:S(2)}, u32[]{:S(2)}) collective-permute-start(bf16[512,1280]{1,0:T(8,128)(2,1)S(1)} %copy-done.15), channel_id=1, source_target_pairs={{0,4},{4,8},{8,12},{12,16},{16,20},{20,24},{24,28},{1,5},{5,9},{9,... | collective-permute-start | bytes 3932168 | tf_op jit(solution)/shard_map/ppermute | solution.py:304
  43.0 32.4 %collective-permute-start.8 = (bf16[512,1280]{1,0:T(8,128)(2,1)S(1)}, bf16[512,1280]{1,0:T(8,128)(2,1)S(1)}, u32[]{:S(2)}, u32[]{:S(2)}) collective-permute-start(bf16[512,1280]{1,0:T(8,128)(2,1)S(1)} %collective-permute-done.7), channel_id=1, source_target_pairs={{4,0},{8,4},{12,8},{16,12},{20,16},{24,20},{28,24},{5,1},{9,5},{13... | collective-permute-start | bytes 3932168 | tf_op jit(solution)/shard_map/ppermute | solution.py:306
  56.5 33.1 %collective-permute-start.4 = (bf16[512,1280]{1,0:T(8,128)(2,1)S(1)}, bf16[512,1280]{1,0:T(8,128)(2,1)}, u32[]{:S(2)}, u32[]{:S(2)}) collective-permute-start(bf16[512,1280]{1,0:T(8,128)(2,1)S(1)} %collective-permute-done.2.refs_3_), channel_id=1, source_target_pairs={{1,2},{2,1},{5,6},{6,5},{9,10},{10,9},{13,14},{14,13},{17,18},{18,... | collective-permute-start | bytes 3932168 | tf_op jit(solution)/shard_map/ppermute | solution.py:279
  60.0 37.4 %collective-permute-start.5 = (bf16[512,1280]{1,0:T(8,128)(2,1)S(1)}, bf16[512,1280]{1,0:T(8,128)(2,1)S(1)}, u32[]{:S(2)}, u32[]{:S(2)}) collective-permute-start(bf16[512,1280]{1,0:T(8,128)(2,1)S(1)} %collective-permute-done.3.refs_5_), channel_id=1, source_target_pairs={{1,0},{2,3},{5,4},{6,7},{9,8},{10,11},{13,12},{14,15},{17,16},{18,... | collective-permute-start | bytes 3932168 | tf_op jit(solution)/shard_map/ppermute | solution.py:279
  71.0 26.4 %collective-permute-start.10 = (bf16[512,1280]{1,0:T(8,128)(2,1)S(1)}, bf16[512,1280]{1,0:T(8,128)(2,1)S(1)}, u32[]{:S(2)}, u32[]{:S(2)}) collective-permute-start(bf16[512,1280]{1,0:T(8,128)(2,1)S(1)} %collective-permute-done.9), channel_id=1, source_target_pairs={{0,4},{4,8},{8,12},{12,16},{16,20},{20,24},{24,28},{1,5},{5,9},{9,... | collective-permute-start | bytes 3932168 | tf_op jit(solution)/shard_map/ppermute | solution.py:309
  74.2 35.6 %collective-permute-start.12 = (bf16[512,1280]{1,0:T(8,128)(2,1)S(1)}, bf16[512,1280]{1,0:T(8,128)(2,1)}, u32[]{:S(2)}, u32[]{:S(2)}) collective-permute-start(bf16[512,1280]{1,0:T(8,128)(2,1)S(1)} %fusion.2.refs_1_), channel_id=1, source_target_pairs={{0,1},{3,2},{4,5},{7,6},{8,9},{11,10},{12,13},{15,14},{16,17},{19,... | collective-permute-start | bytes 3932168 | tf_op jit(solution)/shard_map/ppermute | solution.py:279
  97.4 32.1 %collective-permute-start.11 = (bf16[512,1280]{1,0:T(8,128)(2,1)S(1)}, bf16[512,1280]{1,0:T(8,128)(2,1)}, u32[]{:S(2)}, u32[]{:S(2)}) collective-permute-start(bf16[512,1280]{1,0:T(8,128)(2,1)S(1)} %fusion.2.refs_1_), channel_id=1, source_target_pairs={{1,2},{2,1},{5,6},{6,5},{9,10},{10,9},{13,14},{14,13},{17,18},{18,... | collective-permute-start | bytes 3932168 | tf_op jit(solution)/shard_map/ppermute | solution.py:279
  102.1 34.3 %collective-permute-start.15 = (bf16[512,1280]{1,0:T(8,128)(2,1)}, bf16[512,1280]{1,0:T(8,128)(2,1)}, u32[]{:S(2)}, u32[]{:S(2)}) collective-permute-start(bf16[512,1280]{1,0:T(8,128)(2,1)} %collective-permute-done.4.refs_7_), channel_id=1, source_target_pairs={{1,0},{2,3},{5,4},{6,7},{9,8},{10,11},{13,12},{14,15},{17,16},{18,... | collective-permute-start | bytes 3932168 | tf_op jit(solution)/shard_map/ppermute | solution.py:279
  130.3 30.7 %collective-permute-start.13 = (bf16[512,1280]{1,0:T(8,128)(2,1)}, bf16[512,1280]{1,0:T(8,128)(2,1)}, u32[]{:S(2)}, u32[]{:S(2)}) collective-permute-start(bf16[512,1280]{1,0:T(8,128)(2,1)} %collective-permute-done.12.refs_0_.refs_2_), channel_id=1, source_target_pairs={{1,2},{2,1},{5,6},{6,5},{9,10},{10,9},{13,14},{14,13},{17,18},{18,... | collective-permute-start | bytes 3932168 | tf_op jit(solution)/shard_map/ppermute | solution.py:279
  133.9 18.0 %collective-permute-start.16 = (bf16[16,1280]{1,0:T(8,128)(2,1)S(1)}, bf16[16,1280]{1,0:T(8,128)(2,1)S(1)}, u32[]{:S(2)}, u32[]{:S(2)}) collective-permute-start(bf16[16,1280]{1,0:T(8,128)(2,1)S(1)} %slice.45), channel_id=1, source_target_pairs={{0,4},{4,0},{8,12},{12,8},{16,20},{20,16},{24,28},{28,24},{1,5},{5... | collective-permute-start | bytes 122888 | tf_op jit(solution)/shard_map/ppermute | solution.py:321
  134.0 30.8 %collective-permute-start.17 = (bf16[512,1280]{1,0:T(8,128)(2,1)}, bf16[512,1280]{1,0:T(8,128)(2,1)}, u32[]{:S(2)}, u32[]{:S(2)}) collective-permute-start(bf16[512,1280]{1,0:T(8,128)(2,1)} %collective-permute-done.11.refs_1_.refs_4_), channel_id=1, source_target_pairs={{1,0},{2,3},{5,4},{6,7},{9,8},{10,11},{13,12},{14,15},{17,16},{18,... | collective-permute-start | bytes 3932168 | tf_op jit(solution)/shard_map/ppermute | solution.py:279
  151.9 27.9 %collective-permute-start.18 = (bf16[2,5,512,128]{3,2,1,0:T(8,128)(2,1)S(1)}, bf16[2,5,512,128]{3,2,1,0:T(8,128)(2,1)}, u32[]{:S(2)}, u32[]{:S(2)}) collective-permute-start(bf16[2,5,512,128]{3,2,1,0:T(8,128)(2,1)S(1)} %get-tuple-element.44.refs_3_), channel_id=1, source_target_pairs={{0,24},{1,25},{2,26},{3,27}} | collective-permute-start | bytes 3932168 | tf_op jit(solution)/shard_map/ppermute | solution.py:247
  153.7 26.1 %collective-permute-start.19 = (bf16[2,5,512,128]{3,2,1,0:T(8,128)(2,1)S(1)}, bf16[2,5,512,128]{3,2,1,0:T(8,128)(2,1)}, u32[]{:S(2)}, u32[]{:S(2)}) collective-permute-start(bf16[2,5,512,128]{3,2,1,0:T(8,128)(2,1)S(1)} %get-tuple-element.44.refs_3_), channel_id=1, source_target_pairs={{0,16},{1,17},{2,18},{3,19}} | collective-permute-start | bytes 3932168 | tf_op jit(solution)/shard_map/ppermute | solution.py:247
  155.5 33.3 %collective-permute-start.20 = (bf16[2,5,512,128]{3,2,1,0:T(8,128)(2,1)S(1)}, bf16[2,5,512,128]{3,2,1,0:T(8,128)(2,1)}, u32[]{:S(2)}, u32[]{:S(2)}) collective-permute-start(bf16[2,5,512,128]{3,2,1,0:T(8,128)(2,1)S(1)} %get-tuple-element.44.refs_3_), channel_id=1, source_target_pairs={{0,8},{1,9},{2,10},{3,11}} | collective-permute-start | bytes 3932168 | tf_op jit(solution)/shard_map/ppermute | solution.py:247
  161.0 33.7 %collective-permute-start.14 = (bf16[512,1280]{1,0:T(8,128)(2,1)}, bf16[512,1280]{1,0:T(8,128)(2,1)S(1)}, u32[]{:S(2)}, u32[]{:S(2)}) collective-permute-start(bf16[512,1280]{1,0:T(8,128)(2,1)} %collective-permute-done.13.inner), channel_id=1, source_target_pairs={{1,0},{2,3},{5,4},{6,7},{9,8},{10,11},{13,12},{14,15},{17,16},{18,... | collective-permute-start | bytes 3932168 | tf_op jit(solution)/shard_map/ppermute | solution.py:279
  190.4 22.2 %collective-permute-start.21 = (bf16[2,5,512,128]{3,2,1,0:T(8,128)(2,1)S(1)}, bf16[2,5,512,128]{3,2,1,0:T(8,128)(2,1)}, u32[]{:S(2)}, u32[]{:S(2)}) collective-permute-start(bf16[2,5,512,128]{3,2,1,0:T(8,128)(2,1)S(1)} %select_select_fusion.refs_1_), channel_id=1, source_target_pairs={{0,4},{8,12},{16,20},{24,28},{1,5},{9,13},{17,21},{25,29},{2,6},{1... | collective-permute-start | bytes 3932168 | tf_op jit(solution)/shard_map/ppermute | solution.py:248
  192.8 26.9 %collective-permute-start.22 = (bf16[2,5,512,128]{3,2,1,0:T(8,128)(2,1)S(1)}, bf16[2,5,512,128]{3,2,1,0:T(8,128)(2,1)}, u32[]{:S(2)}, u32[]{:S(2)}) collective-permute-start(bf16[2,5,512,128]{3,2,1,0:T(8,128)(2,1)S(1)} %get-tuple-element.44.refs_3_), channel_id=1, source_target_pairs={{4,8},{8,12},{12,16},{16,20},{20,24},{24,28},{5,9},{9,13},{13,17},... | collective-permute-start | bytes 3932168 | tf_op jit(solution)/shard_map/ppermute | solution.py:326
  210.7 9.0 %collective-permute-start.23 = (bf16[2,5,512,128]{3,2,1,0:T(8,128)(2,1)}, bf16[2,5,512,128]{3,2,1,0:T(8,128)(2,1)}, u32[]{:S(2)}, u32[]{:S(2)}) collective-permute-start(bf16[2,5,512,128]{3,2,1,0:T(8,128)(2,1)} %get-tuple-element.45.refs_4_), channel_id=1, source_target_pairs={{0,4},{1,5},{2,6},{3,7}} | collective-permute-start | bytes 3932168 | tf_op jit(solution)/shard_map/ppermute | solution.py:329
  (22 other events, 437.8 us)

commit v13 on v12

--- a/solution.py
+++ b/solution.py
@@ -155,7 +155,7 @@
             jax.ShapeDtypeStruct((heads, rows, DH), BF16),
             jax.ShapeDtypeStruct((2, heads, rows, DH), BF16),
         ],
-        compiler_params=pltpu.CompilerParams(vmem_limit_bytes=32 * 2**20),
+        compiler_params=pltpu.CompilerParams(vmem_limit_bytes=48 * 2**20),
         cost_estimate=pl.CostEstimate(flops=flops, bytes_accessed=1, transcendentals=0),
         name="finish",
     )(info, inner, outer, *weights, *(g[None] for g in gains), raw)
@@ -258,6 +258,21 @@
     return (centre + taps[0] * before + taps[1] * centre + taps[2] * after).astype(BF16)
 
 
+def split_rows(scales):
+    parts, rest = [], scales
+    for _ in range(3):
+        part = lax.reduce_precision(rest, 8, 7)
+        parts.append(part.astype(BF16))
+        rest = rest - part
+    rows = jnp.concatenate(parts, axis=0)
+    return jnp.pad(rows, ((0, 16 - rows.shape[0]), (0, 0)))
+
+
+def joined_rows(rows, count):
+    high, middle, low = (rows[i * count : (i + 1) * count].astype(F32) for i in range(3))
+    return high + middle + low
+
+
 def per_device(frames, taps, w_query, w_key, w_value, q_gain, k_gain):
     count = lax.axis_size("tm")
     pos = lax.axis_index("tm")
@@ -294,22 +309,26 @@
             scales,
         )
 
-    first, last = frames[0], frames[1]
-    following = lax.ppermute(first, "tm", downs)
-    first, outer_taps = hold((first, send(taps, OUTWARD)))
-    raw_first = send(first, OUTWARD)
+    raw_first = send(frames[0], OUTWARD)
+    following = lax.ppermute(frames[0], "tm", downs)
     mixed1 = mix_first(frames[0], frames[1], following, taps)
+    last = jnp.concatenate([frames[1], split_rows(taps)], axis=0)
+    later, last, mixed1 = hold((frames[1], last, mixed1))
     inward1, middle1 = send(mixed1, INWARD), send(mixed1, MIDDLE)
-    last, _ = hold((last, mixed1))
-    raw_last, preceding = send(last, OUTWARD), lax.ppermute(last, "tm", ups)
+    raw_last = send(last, OUTWARD)
+    later, raw_first = hold((later, raw_first))
+    preceding = lax.ppermute(later, "tm", ups)
     mixed2 = mix_second(frames[0], frames[1], following, preceding, taps)
     raw_following = lax.ppermute(raw_first, "tm", downs)
     inward1, middle1 = hold((inward1, middle1))
     cross1, second1 = send(inward1, MIDDLE), send(middle1, OUTWARD)
+    outer_taps = joined_rows(raw_last[later.shape[0] :], taps.shape[0])
+    raw_last = raw_last[: later.shape[0]]
     raw_preceding = lax.ppermute(raw_last, "tm", ups)
-    level = (mixed2, cross1, second1, raw_following, raw_preceding)
-    later2, cross1, second1, raw_following, raw_preceding = hold(level)
+    later2, cross1 = hold((mixed2, cross1))
     middle2, inward2 = send(later2, MIDDLE), send(mixed2, INWARD)
+    level = (cross1, second1, raw_following, raw_preceding)
+    cross1, second1, raw_following, raw_preceding = hold(level)
     third1 = send(cross1, OUTWARD)
     first1 = mix_first(raw_first, raw_last, raw_following, outer_taps)
     first2 = mix_second(raw_first, raw_last, raw_following, raw_preceding, outer_taps)

time: 230 us -> 220 us (0.957)
  waiting for transfers between devices: 94.5 us -> 84.8 us
  other arithmetic: 10.1 us -> 14.1 us
  local copies, waits for them, and re-layouts: 13.5 us -> 10 us
    ppermute x13 -> x12, waiting for transfers between devices: 78.2 us -> 72.3 us  [send(): return lax.ppermute(x, 'head', pairs)]
    ppermute x3, waiting for transfers between devices: 8.97 us -> 3.32 us  [broadcast_first(): held = jnp.where(mine == to, lax.ppermute(x, axis, [(0, to)]), held)]
    unnamed x44 -> x28, local copies, waits for them, and re-layouts: 9.02 us -> 4.37 us
    concatenate x0 -> x2, other arithmetic: none -> 2.7 us  [the longest x1 2.66 us: per_device(): last = jnp.concatenate([frames[1], split_rows(taps)], axis=0)]
    ppermute x13 -> x12, starting transfers between devices: 34.6 us -> 34.9 us  [send(): return lax.ppermute(x, 'head', pairs)]
  transfers between devices with their start and end apart: 24 -> 23, of which waited for: 12 -> 11; matrix products, arithmetic and copies ran while one was open for 5% -> 7% of each run, Pallas kernels for 20% -> 21%
where the time goes in v13:
time: 220 us; the launch traced here: 218 us
  waiting for transfers between devices  84.8 us (39%)
  starting transfers between devices  54.3 us (25%)
  Pallas kernels  53.9 us (24%)
  other arithmetic  14.1 us (6%)
  local copies, waits for them, and re-layouts  10 us (5%)
    ppermute x12, waiting for transfers between devices, send(): return lax.ppermute(x, 'head', pairs)  72.3 us
    ppermute x12, starting transfers between devices, send(): return lax.ppermute(x, 'head', pairs)  34.9 us
    pallas_call x2, Pallas kernels, project(): pl.pallas_call(functools.partial(project_body, pairs, len(after), final),...  29.3 us
    pallas_call x2, Pallas kernels, attend(): pl.pallas_call(functools.partial(attend_body, 256, (len(anchors), len(opt...  14.2 us
    pallas_call x1, Pallas kernels, finish(): pl.pallas_call(finish_body, grid_spec=pltpu.PrefetchScalarGridSpec(num_sc...  10.4 us
    convert_element_type x3, other arithmetic, mix(): (centre + taps[0] * before + taps[1] * centre + taps[2] * after).astype(B...  9.58 us
    ppermute x1, waiting for transfers between devices, per_device(): following = lax.ppermute(frames[0], 'tm', downs)  9.2 us
    ppermute x3, starting transfers between devices, broadcast_first(): held = jnp.where(mine == to, lax.ppermute(x, axis, [(0, to)]), held)  4.78 us
  transfers between devices with their start and end apart: 23, of which 11 were waited for; matrix products, arithmetic and copies ran while one was open for 7% of the time, Pallas kernels for 21%

profile of v13, /device:TPU:10, one launch (start us, length us, event | category | flops | bytes accessed | tf_op | source)
XLA Modules:
  0.0 217.8 jit_solution(14453053093707698656)
XLA Ops:
  0.0 3.5 %slice_bitcast_fusion.1 = (bf16[512,1280]{1,0:T(8,128)(2,1)}, bf16[512,1280]{1,0:T(8,128)(2,1)}) fusion(bf16[2,512,1280]{2,1,0:T(8,128)(2,1)} %param.7), kind=kLoop, calls=%fused_computation.23 | loop fusion | bytes 5242880 | tf_op jit(solution)/shard_map/squeeze | solution.py:321
  5.4 3.4 %collective-permute-start.1 = (bf16[512,1280]{1,0:T(8,128)(2,1)}, bf16[512,1280]{1,0:T(8,128)(2,1)}, u32[]{:S(2)}, u32[]{:S(2)}) collective-permute-start(bf16[512,1280]{1,0:T(8,128)(2,1)} %get-tuple-element.62), channel_id=1, source_target_pairs={{1,0},{2,3},{5,4},{6,7},{9,8},{10,11},{13,12},{14,15},{17,16},{18,... | collective-permute-start | bytes 3932168 | tf_op jit(solution)/shard_map/ppermute | solution.py:294
  8.9 2.7 %pad_maximum_fusion = bf16[528,1280]{1,0:T(8,128)(2,1)} fusion(bf16[16,1280]{1,0:T(8,128)(2,1)S(1)} %fusion.16, bf16[512,1280]{1,0:T(8,128)(2,1)} %get-tuple-element.30), kind=kLoop, calls=%fused_computation.20 | loop fusion | flops 2703360 | bytes 2703360 | tf_op jit(solution)/shard_map/concatenate | solution.py:315
  11.6 9.2 %collective-permute-done = bf16[512,1280]{1,0:T(8,128)(2,1)} collective-permute-done((bf16[512,1280]{1,0:T(8,128)(2,1)}, bf16[512,1280]{1,0:T(8,128)(2,1)}, u32[]{:S(2)}, u32[]{:S(2)}) %collective-permute-start) | collective-permute-done | bytes 1310752 | tf_op jit(solution)/shard_map/ppermute | solution.py:313
  27.2 4.6 %collective-permute-start.4 = (bf16[512,1280]{1,0:T(8,128)(2,1)S(1)}, bf16[512,1280]{1,0:T(8,128)(2,1)}, u32[]{:S(2)}, u32[]{:S(2)}) collective-permute-start(bf16[512,1280]{1,0:T(8,128)(2,1)S(1)} %fusion.5.refs_2_), channel_id=1, source_target_pairs={{1,2},{2,1},{5,6},{6,5},{9,10},{10,9},{13,14},{14,13},{17,18},{18,... | collective-permute-start | bytes 3932168 | tf_op jit(solution)/shard_map/ppermute | solution.py:294
  31.9 5.3 %collective-permute-done.1 = bf16[512,1280]{1,0:T(8,128)(2,1)} collective-permute-done((bf16[512,1280]{1,0:T(8,128)(2,1)}, bf16[512,1280]{1,0:T(8,128)(2,1)}, u32[]{:S(2)}, u32[]{:S(2)}) %collective-permute-start.1) | collective-permute-done | bytes 1310752 | tf_op jit(solution)/shard_map/ppermute | solution.py:294
  39.1 19.1 %collective-permute-done.3.refs_3_ = bf16[512,1280]{1,0:T(8,128)(2,1)} collective-permute-done((bf16[512,1280]{1,0:T(8,128)(2,1)S(1)}, bf16[512,1280]{1,0:T(8,128)(2,1)}, u32[]{:S(2)}, u32[]{:S(2)}) %collective-permute-start.3) | collective-permute-done | bytes 1310752 | tf_op jit(solution)/shard_map/ppermute | solution.py:294
  59.9 4.2 %collective-permute-start.5 = (bf16[512,1280]{1,0:T(8,128)(2,1)}, bf16[512,1280]{1,0:T(8,128)(2,1)}, u32[]{:S(2)}, u32[]{:S(2)}) collective-permute-start(bf16[512,1280]{1,0:T(8,128)(2,1)} %collective-permute-done.3.refs_3_), channel_id=1, source_target_pairs={{1,2},{2,1},{5,6},{6,5},{9,10},{10,9},{13,14},{14,13},{17,18},{18,... | collective-permute-start | bytes 3932168 | tf_op jit(solution)/shard_map/ppermute | solution.py:294
  70.7 2.9 %collective-permute-start.11 = (bf16[512,1280]{1,0:T(8,128)(2,1)}, bf16[512,1280]{1,0:T(8,128)(2,1)}, u32[]{:S(2)}, u32[]{:S(2)}) collective-permute-start(bf16[512,1280]{1,0:T(8,128)(2,1)} %slice.68), channel_id=1, source_target_pairs={{0,4},{4,8},{8,12},{12,16},{16,20},{20,24},{24,28},{1,5},{5,9},{9,... | collective-permute-start | bytes 3932168 | tf_op jit(solution)/shard_map/ppermute | solution.py:327
  73.7 2.6 %fusion.2.refs_1_ = bf16[512,1280]{1,0:T(8,128)(2,1)S(1)} fusion(bf16[512,1280]{1,0:T(8,128)(2,1)} %collective-permute-done, bf16[512,1280]{1,0:T(8,128)(2,1)} %collective-permute-done.2, f32[1280]{0:T(1024)S(1)} %get-tuple-element.57, f32[1280]{0:T(1024)S(1)} %get-tuple-element.58, f32[1280]{0:T(1024)S(1)} %get-tuple-element.56, pred[]{:T(512)S(6)} %eq.24, ...), kind=kLoop, calls=%fused_computation.10 | loop fusion | flops 8519680 | bytes 6568961 | tf_op jit(solution)/shard_map/convert_element_type | solution.py:258
  77.6 15.9 %collective-permute-done.5.refs_7_ = bf16[512,1280]{1,0:T(8,128)(2,1)} collective-permute-done((bf16[512,1280]{1,0:T(8,128)(2,1)}, bf16[512,1280]{1,0:T(8,128)(2,1)}, u32[]{:S(2)}, u32[]{:S(2)}) %collective-permute-start.5) | collective-permute-done | bytes 1310752 | tf_op jit(solution)/shard_map/ppermute | solution.py:294
  93.5 4.1 %collective-permute-start.6 = (bf16[512,1280]{1,0:T(8,128)(2,1)S(1)}, bf16[512,1280]{1,0:T(8,128)(2,1)}, u32[]{:S(2)}, u32[]{:S(2)}) collective-permute-start(bf16[512,1280]{1,0:T(8,128)(2,1)S(1)} %fusion.2.refs_1_), channel_id=1, source_target_pairs={{1,2},{2,1},{5,6},{6,5},{9,10},{10,9},{13,14},{14,13},{17,18},{18,... | collective-permute-start | bytes 3932168 | tf_op jit(solution)/shard_map/ppermute | solution.py:294
  97.7 3.3 %collective-permute-start.14 = (bf16[512,1280]{1,0:T(8,128)(2,1)}, bf16[512,1280]{1,0:T(8,128)(2,1)S(1)}, u32[]{:S(2)}, u32[]{:S(2)}) collective-permute-start(bf16[512,1280]{1,0:T(8,128)(2,1)} %collective-permute-done.5.refs_7_), channel_id=1, source_target_pairs={{1,0},{2,3},{5,4},{6,7},{9,8},{10,11},{13,12},{14,15},{17,16},{18,... | collective-permute-start | bytes 3932168 | tf_op jit(solution)/shard_map/ppermute | solution.py:294
  101.0 4.5 %fusion.11 = (bf16[512,1280]{1,0:T(8,128)(2,1)S(1)}, bf16[512,1280]{1,0:T(8,128)(2,1)}) fusion(bf16[512,1280]{1,0:T(8,128)(2,1)} %collective-permute-done.10, bf16[512,1280]{1,0:T(8,128)(2,1)} %collective-permute-done.1, bf16[512,1280]{1,0:T(8,128)(2,1)} %collective-permute-done.11, f32[1280]{0:T(1024)S(1)} %get-tuple-element.54, ...), kind=kLoop, calls=%fused_computation.19 | loop fusion | flops 17039360 | bytes 7879681 | tf_op jit(solution)/shard_map/convert_element_type | solution.py:258
  108.0 19.1 %collective-permute-done.6.refs_1_.refs_4_ = bf16[512,1280]{1,0:T(8,128)(2,1)} collective-permute-done((bf16[512,1280]{1,0:T(8,128)(2,1)S(1)}, bf16[512,1280]{1,0:T(8,128)(2,1)}, u32[]{:S(2)}, u32[]{:S(2)}) %collective-permute-start.6) | collective-permute-done | bytes 1310752 | tf_op jit(solution)/shard_map/ppermute | solution.py:294
  127.9 3.7 %collective-permute-start.12 = (bf16[512,1280]{1,0:T(8,128)(2,1)}, bf16[512,1280]{1,0:T(8,128)(2,1)}, u32[]{:S(2)}, u32[]{:S(2)}) collective-permute-start(bf16[512,1280]{1,0:T(8,128)(2,1)} %collective-permute-done.7.refs_0_.refs_2_), channel_id=1, source_target_pairs={{1,2},{2,1},{5,6},{6,5},{9,10},{10,9},{13,14},{14,13},{17,18},{18,... | collective-permute-start | bytes 3932168 | tf_op jit(solution)/shard_map/ppermute | solution.py:294
  135.1 15.5 %project_end.1 = (bf16[5,512,128]{2,1,0:T(8,128)(2,1)S(1)}, bf16[2,5,512,128]{3,2,1,0:T(8,128)(2,1)S(1)}) custom-call(s32[5]{0:T(128)S(1)} %stack.65.info, bf16[512,1280]{1,0:T(8,128)(2,1)} %collective-permute-done.7.refs_0_.refs_2_, bf16[512,1280]{1,0:T(8,128)(2,1)} %collective-permute-done.6.refs_1_.refs_4_, bf16[512,1280]{1,0:T(8,128)(2,1)S(1)} %copy-done.1, ...), custom_call_target="tpu_custom_call" | custom-call | flops 10000000000 | bytes 1 | tf_op jit(solution)/shard_map/project_end/pallas_call | solution.py:101
  155.6 4.9 %collective-permute-done.12.inner = bf16[512,1280]{1,0:T(8,128)(2,1)} collective-permute-done((bf16[512,1280]{1,0:T(8,128)(2,1)}, bf16[512,1280]{1,0:T(8,128)(2,1)}, u32[]{:S(2)}, u32[]{:S(2)}) %collective-permute-start.12) | collective-permute-done | bytes 1310752 | tf_op jit(solution)/shard_map/ppermute | solution.py:294
  163.7 13.7 %project_raw.1.raw = f32[3,5,512,128]{3,2,1,0:T(8,128)} custom-call(s32[4]{0:T(128)S(1)} %pad_add_fusion.2.info, bf16[16,1280]{1,0:T(8,128)(2,1)S(1)} %collective-permute-done.15.refs_0_, bf16[512,1280]{1,0:T(8,128)(2,1)S(1)} %copy-done.3, bf16[512,1280]{1,0:T(8,128)(2,1)} %collective-permute-done.7.refs_0_.refs_2_, ...), custom_call_target="tpu_custom_call" | custom-call | flops 10000000000 | bytes 1 | tf_op jit(solution)/shard_map/project_raw/pallas_call | solution.py:101
  177.4 3.3 %collective-permute-done.19 = bf16[2,5,512,128]{3,2,1,0:T(8,128)(2,1)} collective-permute-done((bf16[2,5,512,128]{3,2,1,0:T(8,128)(2,1)S(1)}, bf16[2,5,512,128]{3,2,1,0:T(8,128)(2,1)}, u32[]{:S(2)}, u32[]{:S(2)}) %collective-permute-start.19) | collective-permute-done | bytes 1310752 | tf_op jit(solution)/shard_map/ppermute | solution.py:247
  186.6 3.7 %collective-permute-done.13.outer = bf16[512,1280]{1,0:T(8,128)(2,1)S(1)} collective-permute-done((bf16[512,1280]{1,0:T(8,128)(2,1)}, bf16[512,1280]{1,0:T(8,128)(2,1)S(1)}, u32[]{:S(2)}, u32[]{:S(2)}) %collective-permute-start.13) | collective-permute-done | bytes 1310752 | tf_op jit(solution)/shard_map/ppermute | solution.py:294
  190.3 10.4 %finish.1 = (bf16[5,512,128]{2,1,0:T(8,128)(2,1)S(1)}, bf16[2,5,512,128]{3,2,1,0:T(8,128)(2,1)}) custom-call(s32[2]{0:T(128)S(1)} %pad_add_fusion.1.info, bf16[512,1280]{1,0:T(8,128)(2,1)} %collective-permute-done.12.inner, bf16[512,1280]{1,0:T(8,128)(2,1)S(1)} %collective-permute-done.13.outer, bf16[5120,640]{1,0:T(8,128)(2,1)} %wq.1, ...), custom_call_target="tpu_custom_call" | custom-call | flops 10000000000 | bytes 1 | tf_op jit(solution)/shard_map/finish/pallas_call | solution.py:139
  203.3 7.1 %attend.2.refs_6_ = bf16[2,512,640]{2,1,0:T(8,128)(2,1)} custom-call(s32[3]{0:T(128)S(1)} %get-tuple-element.67.info, bf16[5,512,128]{2,1,0:T(8,128)(2,1)S(1)} %get-tuple-element.52.refs_0_, bf16[2,5,512,128]{3,2,1,0:T(8,128)(2,1)S(1)} %select_select_fusion.refs_1_, bf16[2,5,512,128]{3,2,1,0:T(8,128)(2,1)} %collective-permute-done.20.refs_2_, ...), custom_call_target="tpu_custom_call" | custom-call | flops 1342177280 | bytes 3932160 | tf_op jit(solution)/shard_map/attend/pallas_call | solution.py:218
  210.5 7.1 %attend.3 = bf16[2,512,640]{2,1,0:T(8,128)(2,1)} custom-call(s32[3]{0:T(128)S(1)} %get-tuple-element.66.info, bf16[5,512,128]{2,1,0:T(8,128)(2,1)S(1)} %copy-done.5, bf16[2,5,512,128]{3,2,1,0:T(8,128)(2,1)S(1)} %select_select_fusion.refs_1_, bf16[2,5,512,128]{3,2,1,0:T(8,128)(2,1)} %collective-permute-done.20.refs_2_, ...), custom_call_target="tpu_custom_call", output_to_operand_aliasing={{}: (7, {})} | custom-call | flops 1342177280 | bytes 3932160 | tf_op jit(solution)/shard_map/attend/pallas_call | solution.py:218
  (74 shorter events, 43.4 us)
Async XLA Ops:
  3.5 17.3 %collective-permute-start = (bf16[512,1280]{1,0:T(8,128)(2,1)}, bf16[512,1280]{1,0:T(8,128)(2,1)}, u32[]{:S(2)}, u32[]{:S(2)}) collective-permute-start(bf16[512,1280]{1,0:T(8,128)(2,1)} %get-tuple-element.62), channel_id=1, source_target_pairs={{4,0},{8,4},{12,8},{16,12},{20,16},{24,20},{28,24},{5,1},{9,5},{13... | collective-permute-start | bytes 3932168 | tf_op jit(solution)/shard_map/ppermute | solution.py:313
  5.4 31.8 %collective-permute-start.1 = (bf16[512,1280]{1,0:T(8,128)(2,1)}, bf16[512,1280]{1,0:T(8,128)(2,1)}, u32[]{:S(2)}, u32[]{:S(2)}) collective-permute-start(bf16[512,1280]{1,0:T(8,128)(2,1)} %get-tuple-element.62), channel_id=1, source_target_pairs={{1,0},{2,3},{5,4},{6,7},{9,8},{10,11},{13,12},{14,15},{17,16},{18,... | collective-permute-start | bytes 3932168 | tf_op jit(solution)/shard_map/ppermute | solution.py:294
  23.4 50.2 %copy-start.12 = (f32[640]{0:T(1024)S(1)}, f32[640]{0:T(1024)}, u32[]{:S(2)}) copy-start(f32[640]{0:T(1024)} %param.13) | copy-start | bytes 7684
  23.4 45.0 %collective-permute-start.8 = (bf16[528,1280]{1,0:T(8,128)(2,1)S(1)}, bf16[528,1280]{1,0:T(8,128)(2,1)S(1)}, u32[]{:S(2)}, u32[]{:S(2)}) collective-permute-start(bf16[528,1280]{1,0:T(8,128)(2,1)S(1)} %copy-done.9), channel_id=1, source_target_pairs={{1,0},{2,3},{5,4},{6,7},{9,8},{10,11},{13,12},{14,15},{17,16},{18,... | collective-permute-start | bytes 4055048 | tf_op jit(solution)/shard_map/ppermute | solution.py:294
  25.9 32.2 %collective-permute-start.3 = (bf16[512,1280]{1,0:T(8,128)(2,1)S(1)}, bf16[512,1280]{1,0:T(8,128)(2,1)}, u32[]{:S(2)}, u32[]{:S(2)}) collective-permute-start(bf16[512,1280]{1,0:T(8,128)(2,1)S(1)} %fusion.5.refs_2_), channel_id=1, source_target_pairs={{0,1},{3,2},{4,5},{7,6},{8,9},{11,10},{12,13},{15,14},{16,17},{19,... | collective-permute-start | bytes 3932168 | tf_op jit(solution)/shard_map/ppermute | solution.py:294
  27.2 32.6 %collective-permute-start.4 = (bf16[512,1280]{1,0:T(8,128)(2,1)S(1)}, bf16[512,1280]{1,0:T(8,128)(2,1)}, u32[]{:S(2)}, u32[]{:S(2)}) collective-permute-start(bf16[512,1280]{1,0:T(8,128)(2,1)S(1)} %fusion.5.refs_2_), channel_id=1, source_target_pairs={{1,2},{2,1},{5,6},{6,5},{9,10},{10,9},{13,14},{14,13},{17,18},{18,... | collective-permute-start | bytes 3932168 | tf_op jit(solution)/shard_map/ppermute | solution.py:294
  37.2 36.6 %collective-permute-start.2 = (bf16[512,1280]{1,0:T(8,128)(2,1)}, bf16[512,1280]{1,0:T(8,128)(2,1)}, u32[]{:S(2)}, u32[]{:S(2)}) collective-permute-start(bf16[512,1280]{1,0:T(8,128)(2,1)} %get-tuple-element.30), channel_id=1, source_target_pairs={{0,4},{4,8},{8,12},{12,16},{16,20},{20,24},{24,28},{1,5},{5,9},{9,... | collective-permute-start | bytes 3932168 | tf_op jit(solution)/shard_map/ppermute | solution.py:320
  59.9 33.6 %collective-permute-start.5 = (bf16[512,1280]{1,0:T(8,128)(2,1)}, bf16[512,1280]{1,0:T(8,128)(2,1)}, u32[]{:S(2)}, u32[]{:S(2)}) collective-permute-start(bf16[512,1280]{1,0:T(8,128)(2,1)} %collective-permute-done.3.refs_3_), channel_id=1, source_target_pairs={{1,2},{2,1},{5,6},{6,5},{9,10},{10,9},{13,14},{14,13},{17,18},{18,... | collective-permute-start | bytes 3932168 | tf_op jit(solution)/shard_map/ppermute | solution.py:294
  64.1 33.6 %collective-permute-start.10 = (bf16[512,1280]{1,0:T(8,128)(2,1)}, bf16[512,1280]{1,0:T(8,128)(2,1)}, u32[]{:S(2)}, u32[]{:S(2)}) collective-permute-start(bf16[512,1280]{1,0:T(8,128)(2,1)} %collective-permute-done.1), channel_id=1, source_target_pairs={{4,0},{8,4},{12,8},{16,12},{20,16},{24,20},{28,24},{5,1},{9,5},{13... | collective-permute-start | bytes 3932168 | tf_op jit(solution)/shard_map/ppermute | solution.py:322
  66.0 31.6 %collective-permute-start.9 = (bf16[512,1280]{1,0:T(8,128)(2,1)}, bf16[512,1280]{1,0:T(8,128)(2,1)}, u32[]{:S(2)}, u32[]{:S(2)}) collective-permute-start(bf16[512,1280]{1,0:T(8,128)(2,1)} %collective-permute-done.4.refs_5_), channel_id=1, source_target_pairs={{1,0},{2,3},{5,4},{6,7},{9,8},{10,11},{13,12},{14,15},{17,16},{18,... | collective-permute-start | bytes 3932168 | tf_op jit(solution)/shard_map/ppermute | solution.py:294
  70.7 27.0 %collective-permute-start.11 = (bf16[512,1280]{1,0:T(8,128)(2,1)}, bf16[512,1280]{1,0:T(8,128)(2,1)}, u32[]{:S(2)}, u32[]{:S(2)}) collective-permute-start(bf16[512,1280]{1,0:T(8,128)(2,1)} %slice.68), channel_id=1, source_target_pairs={{0,4},{4,8},{8,12},{12,16},{16,20},{20,24},{24,28},{1,5},{5,9},{9,... | collective-permute-start | bytes 3932168 | tf_op jit(solution)/shard_map/ppermute | solution.py:327
  76.3 31.7 %collective-permute-start.7 = (bf16[512,1280]{1,0:T(8,128)(2,1)S(1)}, bf16[512,1280]{1,0:T(8,128)(2,1)}, u32[]{:S(2)}, u32[]{:S(2)}) collective-permute-start(bf16[512,1280]{1,0:T(8,128)(2,1)S(1)} %fusion.2.refs_1_), channel_id=1, source_target_pairs={{0,1},{3,2},{4,5},{7,6},{8,9},{11,10},{12,13},{15,14},{16,17},{19,... | collective-permute-start | bytes 3932168 | tf_op jit(solution)/shard_map/ppermute | solution.py:294
  93.5 33.6 %collective-permute-start.6 = (bf16[512,1280]{1,0:T(8,128)(2,1)S(1)}, bf16[512,1280]{1,0:T(8,128)(2,1)}, u32[]{:S(2)}, u32[]{:S(2)}) collective-permute-start(bf16[512,1280]{1,0:T(8,128)(2,1)S(1)} %fusion.2.refs_1_), channel_id=1, source_target_pairs={{1,2},{2,1},{5,6},{6,5},{9,10},{10,9},{13,14},{14,13},{17,18},{18,... | collective-permute-start | bytes 3932168 | tf_op jit(solution)/shard_map/ppermute | solution.py:294
  97.7 36.4 %collective-permute-start.14 = (bf16[512,1280]{1,0:T(8,128)(2,1)}, bf16[512,1280]{1,0:T(8,128)(2,1)S(1)}, u32[]{:S(2)}, u32[]{:S(2)}) collective-permute-start(bf16[512,1280]{1,0:T(8,128)(2,1)} %collective-permute-done.5.refs_7_), channel_id=1, source_target_pairs={{1,0},{2,3},{5,4},{6,7},{9,8},{10,11},{13,12},{14,15},{17,16},{18,... | collective-permute-start | bytes 3932168 | tf_op jit(solution)/shard_map/ppermute | solution.py:294
  127.9 32.7 %collective-permute-start.12 = (bf16[512,1280]{1,0:T(8,128)(2,1)}, bf16[512,1280]{1,0:T(8,128)(2,1)}, u32[]{:S(2)}, u32[]{:S(2)}) collective-permute-start(bf16[512,1280]{1,0:T(8,128)(2,1)} %collective-permute-done.7.refs_0_.refs_2_), channel_id=1, source_target_pairs={{1,2},{2,1},{5,6},{6,5},{9,10},{10,9},{13,14},{14,13},{17,18},{18,... | collective-permute-start | bytes 3932168 | tf_op jit(solution)/shard_map/ppermute | solution.py:294
  131.5 19.1 %collective-permute-start.15 = (bf16[16,1280]{1,0:T(8,128)(2,1)S(1)}, bf16[16,1280]{1,0:T(8,128)(2,1)S(1)}, u32[]{:S(2)}, u32[]{:S(2)}) collective-permute-start(bf16[16,1280]{1,0:T(8,128)(2,1)S(1)} %slice.67), channel_id=1, source_target_pairs={{0,4},{4,0},{8,12},{12,8},{16,20},{20,16},{24,28},{28,24},{1,5},{5... | collective-permute-start | bytes 122888 | tf_op jit(solution)/shard_map/ppermute | solution.py:340
  131.6 30.8 %collective-permute-start.16 = (bf16[512,1280]{1,0:T(8,128)(2,1)}, bf16[512,1280]{1,0:T(8,128)(2,1)}, u32[]{:S(2)}, u32[]{:S(2)}) collective-permute-start(bf16[512,1280]{1,0:T(8,128)(2,1)} %collective-permute-done.6.refs_1_.refs_4_), channel_id=1, source_target_pairs={{1,0},{2,3},{5,4},{6,7},{9,8},{10,11},{13,12},{14,15},{17,16},{18,... | collective-permute-start | bytes 3932168 | tf_op jit(solution)/shard_map/ppermute | solution.py:294
  150.7 26.7 %collective-permute-start.17 = (bf16[2,5,512,128]{3,2,1,0:T(8,128)(2,1)S(1)}, bf16[2,5,512,128]{3,2,1,0:T(8,128)(2,1)}, u32[]{:S(2)}, u32[]{:S(2)}) collective-permute-start(bf16[2,5,512,128]{3,2,1,0:T(8,128)(2,1)S(1)} %get-tuple-element.50.refs_3_), channel_id=1, source_target_pairs={{0,24},{1,25},{2,26},{3,27}} | collective-permute-start | bytes 3932168 | tf_op jit(solution)/shard_map/ppermute | solution.py:247
  152.4 25.0 %collective-permute-start.18 = (bf16[2,5,512,128]{3,2,1,0:T(8,128)(2,1)S(1)}, bf16[2,5,512,128]{3,2,1,0:T(8,128)(2,1)}, u32[]{:S(2)}, u32[]{:S(2)}) collective-permute-start(bf16[2,5,512,128]{3,2,1,0:T(8,128)(2,1)S(1)} %get-tuple-element.50.refs_3_), channel_id=1, source_target_pairs={{0,16},{1,17},{2,18},{3,19}} | collective-permute-start | bytes 3932168 | tf_op jit(solution)/shard_map/ppermute | solution.py:247
  154.2 26.6 %collective-permute-start.19 = (bf16[2,5,512,128]{3,2,1,0:T(8,128)(2,1)S(1)}, bf16[2,5,512,128]{3,2,1,0:T(8,128)(2,1)}, u32[]{:S(2)}, u32[]{:S(2)}) collective-permute-start(bf16[2,5,512,128]{3,2,1,0:T(8,128)(2,1)S(1)} %get-tuple-element.50.refs_3_), channel_id=1, source_target_pairs={{0,8},{1,9},{2,10},{3,11}} | collective-permute-start | bytes 3932168 | tf_op jit(solution)/shard_map/ppermute | solution.py:247
  160.6 29.7 %collective-permute-start.13 = (bf16[512,1280]{1,0:T(8,128)(2,1)}, bf16[512,1280]{1,0:T(8,128)(2,1)S(1)}, u32[]{:S(2)}, u32[]{:S(2)}) collective-permute-start(bf16[512,1280]{1,0:T(8,128)(2,1)} %collective-permute-done.12.inner), channel_id=1, source_target_pairs={{1,0},{2,3},{5,4},{6,7},{9,8},{10,11},{13,12},{14,15},{17,16},{18,... | collective-permute-start | bytes 3932168 | tf_op jit(solution)/shard_map/ppermute | solution.py:294
  182.3 21.0 %collective-permute-start.20 = (bf16[2,5,512,128]{3,2,1,0:T(8,128)(2,1)S(1)}, bf16[2,5,512,128]{3,2,1,0:T(8,128)(2,1)}, u32[]{:S(2)}, u32[]{:S(2)}) collective-permute-start(bf16[2,5,512,128]{3,2,1,0:T(8,128)(2,1)S(1)} %select_select_fusion.refs_1_), channel_id=1, source_target_pairs={{0,4},{8,12},{16,20},{24,28},{1,5},{9,13},{17,21},{25,29},{2,6},{1... | collective-permute-start | bytes 3932168 | tf_op jit(solution)/shard_map/ppermute | solution.py:248
  184.7 25.8 %collective-permute-start.21 = (bf16[2,5,512,128]{3,2,1,0:T(8,128)(2,1)S(1)}, bf16[2,5,512,128]{3,2,1,0:T(8,128)(2,1)}, u32[]{:S(2)}, u32[]{:S(2)}) collective-permute-start(bf16[2,5,512,128]{3,2,1,0:T(8,128)(2,1)S(1)} %get-tuple-element.50.refs_3_), channel_id=1, source_target_pairs={{4,8},{8,12},{12,16},{16,20},{20,24},{24,28},{5,9},{9,13},{13,17},... | collective-permute-start | bytes 3932168 | tf_op jit(solution)/shard_map/ppermute | solution.py:345
  201.5 9.0 %collective-permute-start.22 = (bf16[2,5,512,128]{3,2,1,0:T(8,128)(2,1)}, bf16[2,5,512,128]{3,2,1,0:T(8,128)(2,1)}, u32[]{:S(2)}, u32[]{:S(2)}) collective-permute-start(bf16[2,5,512,128]{3,2,1,0:T(8,128)(2,1)} %get-tuple-element.51.refs_4_), channel_id=1, source_target_pairs={{0,4},{1,5},{2,6},{3,7}} | collective-permute-start | bytes 3932168 | tf_op jit(solution)/shard_map/ppermute | solution.py:348
  (13 other events, 222.9 us)

commit v14 on v13

--- a/solution.py
+++ b/solution.py
@@ -243,7 +243,7 @@
     count = lax.axis_size(axis)
     mine = lax.axis_index(axis)
     held = x
-    for to in range(2, count, 2):
+    for to in reversed(range(2, count, 2)):
         held = jnp.where(mine == to, lax.ppermute(x, axis, [(0, to)]), held)
     return held, lax.ppermute(held, axis, [(i, i + 1) for i in range(0, count, 2)])
 
@@ -313,10 +313,10 @@
     following = lax.ppermute(frames[0], "tm", downs)
     mixed1 = mix_first(frames[0], frames[1], following, taps)
     last = jnp.concatenate([frames[1], split_rows(taps)], axis=0)
-    later, last, mixed1 = hold((frames[1], last, mixed1))
+    later, last, mixed1 = hold((frames, last, mixed1))
     inward1, middle1 = send(mixed1, INWARD), send(mixed1, MIDDLE)
     raw_last = send(last, OUTWARD)
-    later, raw_first = hold((later, raw_first))
+    later, raw_first = hold((later[1], raw_first))
     preceding = lax.ppermute(later, "tm", ups)
     mixed2 = mix_second(frames[0], frames[1], following, preceding, taps)
     raw_following = lax.ppermute(raw_first, "tm", downs)

time: 220 us -> 220 us (level)
    ppermute x3, waiting for transfers between devices: 3.32 us -> 0.01 us  [broadcast_first(): held = jnp.where(mine == to, lax.ppermute(x, axis, [(0, to)]), held)]
    ppermute x12, waiting for transfers between devices: 72.3 us -> 75.2 us  [send(): return lax.ppermute(x, 'head', pairs)]
  transfers between devices with their start and end apart: 23 -> 23, of which waited for: 11 -> 10; matrix products, arithmetic and copies ran while one was open for 7% -> 7% of each run, Pallas kernels for 21% -> 22%
where the time goes in v14:
time: 220 us; the launch traced here: 217 us
  waiting for transfers between devices  85.9 us (39%)
  starting transfers between devices  54.2 us (25%)
  Pallas kernels  53.9 us (24%)
  other arithmetic  12.6 us (6%)
  local copies, waits for them, and re-layouts  9.87 us (4%)
    ppermute x12, waiting for transfers between devices, send(): return lax.ppermute(x, 'head', pairs)  75.2 us
    ppermute x12, starting transfers between devices, send(): return lax.ppermute(x, 'head', pairs)  34.7 us
    pallas_call x2, Pallas kernels, project(): pl.pallas_call(functools.partial(project_body, pairs, len(after), final),...  29.3 us
    pallas_call x2, Pallas kernels, attend(): pl.pallas_call(functools.partial(attend_body, 256, (len(anchors), len(opt...  14.3 us
    ppermute x1, waiting for transfers between devices, per_device(): following = lax.ppermute(frames[0], 'tm', downs)  10.7 us
    pallas_call x1, Pallas kernels, finish(): pl.pallas_call(finish_body, grid_spec=pltpu.PrefetchScalarGridSpec(num_sc...  10.4 us
    convert_element_type x3, other arithmetic, mix(): (centre + taps[0] * before + taps[1] * centre + taps[2] * after).astype(B...  9.58 us
    ppermute x3, starting transfers between devices, broadcast_first(): held = jnp.where(mine == to, lax.ppermute(x, axis, [(0, to)]), held)  4.76 us
  transfers between devices with their start and end apart: 23, of which 10 were waited for; matrix products, arithmetic and copies ran while one was open for 7% of the time, Pallas kernels for 22%

profile of v14, /device:TPU:10, one launch (start us, length us, event | category | flops | bytes accessed | tf_op | source)
XLA Modules:
  0.0 217.1 jit_solution(9063398777651475685)
XLA Ops:
  0.0 2.9 %slice_bitcast_fusion.2 = (bf16[512,1280]{1,0:T(8,128)(2,1)S(1)}, bf16[512,1280]{1,0:T(8,128)(2,1)}) fusion(bf16[2,512,1280]{2,1,0:T(8,128)(2,1)} %param.7), kind=kLoop, calls=%fused_computation.24 | loop fusion | bytes 5242880 | tf_op jit(solution)/shard_map/squeeze | solution.py:321
  4.9 3.4 %collective-permute-start.1 = (bf16[512,1280]{1,0:T(8,128)(2,1)}, bf16[512,1280]{1,0:T(8,128)(2,1)}, u32[]{:S(2)}, u32[]{:S(2)}) collective-permute-start(bf16[512,1280]{1,0:T(8,128)(2,1)} %get-tuple-element.62), channel_id=1, source_target_pairs={{1,0},{2,3},{5,4},{6,7},{9,8},{10,11},{13,12},{14,15},{17,16},{18,... | collective-permute-start | bytes 3932168 | tf_op jit(solution)/shard_map/ppermute | solution.py:294
  9.6 10.7 %collective-permute-done = bf16[512,1280]{1,0:T(8,128)(2,1)} collective-permute-done((bf16[512,1280]{1,0:T(8,128)(2,1)}, bf16[512,1280]{1,0:T(8,128)(2,1)}, u32[]{:S(2)}, u32[]{:S(2)}) %collective-permute-start) | collective-permute-done | bytes 1310752 | tf_op jit(solution)/shard_map/ppermute | solution.py:313
  20.3 2.5 %fusion.5.refs_2_ = bf16[512,1280]{1,0:T(8,128)(2,1)S(1)} fusion(bf16[512,1280]{1,0:T(8,128)(2,1)} %collective-permute-done, f32[1280]{0:T(1024)S(1)} %get-tuple-element.57, f32[1280]{0:T(1024)S(1)} %get-tuple-element.58, f32[1280]{0:T(1024)S(1)} %get-tuple-element.56, pred[]{:T(512)S(6)} %eq.24, bf16[2,512,1280]{2,1,0:T(8,128)(2,1)S(1)} %copy-done.6), kind=kLoop, calls=%fused_computation.13 | loop fusion | flops 8519680 | bytes 5258241 | tf_op jit(solution)/shard_map/convert_element_type | solution.py:258
  22.8 2.4 %collective-permute-start.8 = (bf16[528,1280]{1,0:T(8,128)(2,1)S(1)}, bf16[528,1280]{1,0:T(8,128)(2,1)S(1)}, u32[]{:S(2)}, u32[]{:S(2)}) collective-permute-start(bf16[528,1280]{1,0:T(8,128)(2,1)S(1)} %copy-done.9), channel_id=1, source_target_pairs={{1,0},{2,3},{5,4},{6,7},{9,8},{10,11},{13,12},{14,15},{17,16},{18,... | collective-permute-start | bytes 4055048 | tf_op jit(solution)/shard_map/ppermute | solution.py:294
  26.6 4.6 %collective-permute-start.4 = (bf16[512,1280]{1,0:T(8,128)(2,1)S(1)}, bf16[512,1280]{1,0:T(8,128)(2,1)}, u32[]{:S(2)}, u32[]{:S(2)}) collective-permute-start(bf16[512,1280]{1,0:T(8,128)(2,1)S(1)} %fusion.5.refs_2_), channel_id=1, source_target_pairs={{1,2},{2,1},{5,6},{6,5},{9,10},{10,9},{13,14},{14,13},{17,18},{18,... | collective-permute-start | bytes 3932168 | tf_op jit(solution)/shard_map/ppermute | solution.py:294
  32.4 4.2 %collective-permute-done.1 = bf16[512,1280]{1,0:T(8,128)(2,1)} collective-permute-done((bf16[512,1280]{1,0:T(8,128)(2,1)}, bf16[512,1280]{1,0:T(8,128)(2,1)}, u32[]{:S(2)}, u32[]{:S(2)}) %collective-permute-start.1) | collective-permute-done | bytes 1310752 | tf_op jit(solution)/shard_map/ppermute | solution.py:294
  38.5 18.9 %collective-permute-done.3.refs_3_ = bf16[512,1280]{1,0:T(8,128)(2,1)} collective-permute-done((bf16[512,1280]{1,0:T(8,128)(2,1)S(1)}, bf16[512,1280]{1,0:T(8,128)(2,1)}, u32[]{:S(2)}, u32[]{:S(2)}) %collective-permute-start.3) | collective-permute-done | bytes 1310752 | tf_op jit(solution)/shard_map/ppermute | solution.py:294
  59.2 4.2 %collective-permute-start.5 = (bf16[512,1280]{1,0:T(8,128)(2,1)}, bf16[512,1280]{1,0:T(8,128)(2,1)}, u32[]{:S(2)}, u32[]{:S(2)}) collective-permute-start(bf16[512,1280]{1,0:T(8,128)(2,1)} %collective-permute-done.3.refs_3_), channel_id=1, source_target_pairs={{1,2},{2,1},{5,6},{6,5},{9,10},{10,9},{13,14},{14,13},{17,18},{18,... | collective-permute-start | bytes 3932168 | tf_op jit(solution)/shard_map/ppermute | solution.py:294
  69.2 2.9 %collective-permute-start.11 = (bf16[512,1280]{1,0:T(8,128)(2,1)}, bf16[512,1280]{1,0:T(8,128)(2,1)}, u32[]{:S(2)}, u32[]{:S(2)}) collective-permute-start(bf16[512,1280]{1,0:T(8,128)(2,1)} %slice.71), channel_id=1, source_target_pairs={{0,4},{4,8},{8,12},{12,16},{16,20},{20,24},{24,28},{1,5},{5,9},{9,... | collective-permute-start | bytes 3932168 | tf_op jit(solution)/shard_map/ppermute | solution.py:327
  72.2 2.6 %fusion.2.refs_1_ = bf16[512,1280]{1,0:T(8,128)(2,1)S(1)} fusion(bf16[512,1280]{1,0:T(8,128)(2,1)} %collective-permute-done, bf16[512,1280]{1,0:T(8,128)(2,1)} %collective-permute-done.2, f32[1280]{0:T(1024)S(1)} %get-tuple-element.57, f32[1280]{0:T(1024)S(1)} %get-tuple-element.58, f32[1280]{0:T(1024)S(1)} %get-tuple-element.56, pred[]{:T(512)S(6)} %eq.24, ...), kind=kLoop, calls=%fused_computation.10 | loop fusion | flops 8519680 | bytes 6568961 | tf_op jit(solution)/shard_map/convert_element_type | solution.py:258
  76.1 16.7 %collective-permute-done.5.refs_7_ = bf16[512,1280]{1,0:T(8,128)(2,1)} collective-permute-done((bf16[512,1280]{1,0:T(8,128)(2,1)}, bf16[512,1280]{1,0:T(8,128)(2,1)}, u32[]{:S(2)}, u32[]{:S(2)}) %collective-permute-start.5) | collective-permute-done | bytes 1310752 | tf_op jit(solution)/shard_map/ppermute | solution.py:294
  92.8 4.1 %collective-permute-start.6 = (bf16[512,1280]{1,0:T(8,128)(2,1)S(1)}, bf16[512,1280]{1,0:T(8,128)(2,1)}, u32[]{:S(2)}, u32[]{:S(2)}) collective-permute-start(bf16[512,1280]{1,0:T(8,128)(2,1)S(1)} %fusion.2.refs_1_), channel_id=1, source_target_pairs={{1,2},{2,1},{5,6},{6,5},{9,10},{10,9},{13,14},{14,13},{17,18},{18,... | collective-permute-start | bytes 3932168 | tf_op jit(solution)/shard_map/ppermute | solution.py:294
  97.0 3.3 %collective-permute-start.14 = (bf16[512,1280]{1,0:T(8,128)(2,1)}, bf16[512,1280]{1,0:T(8,128)(2,1)S(1)}, u32[]{:S(2)}, u32[]{:S(2)}) collective-permute-start(bf16[512,1280]{1,0:T(8,128)(2,1)} %collective-permute-done.5.refs_7_), channel_id=1, source_target_pairs={{1,0},{2,3},{5,4},{6,7},{9,8},{10,11},{13,12},{14,15},{17,16},{18,... | collective-permute-start | bytes 3932168 | tf_op jit(solution)/shard_map/ppermute | solution.py:294
  100.4 4.5 %fusion.11 = (bf16[512,1280]{1,0:T(8,128)(2,1)S(1)}, bf16[512,1280]{1,0:T(8,128)(2,1)}) fusion(bf16[512,1280]{1,0:T(8,128)(2,1)} %collective-permute-done.10, bf16[512,1280]{1,0:T(8,128)(2,1)} %collective-permute-done.1, bf16[512,1280]{1,0:T(8,128)(2,1)} %collective-permute-done.11, f32[1280]{0:T(1024)S(1)} %get-tuple-element.54, ...), kind=kLoop, calls=%fused_computation.19 | loop fusion | flops 17039360 | bytes 7879681 | tf_op jit(solution)/shard_map/convert_element_type | solution.py:258
  106.5 19.9 %collective-permute-done.6.refs_1_.refs_4_ = bf16[512,1280]{1,0:T(8,128)(2,1)} collective-permute-done((bf16[512,1280]{1,0:T(8,128)(2,1)S(1)}, bf16[512,1280]{1,0:T(8,128)(2,1)}, u32[]{:S(2)}, u32[]{:S(2)}) %collective-permute-start.6) | collective-permute-done | bytes 1310752 | tf_op jit(solution)/shard_map/ppermute | solution.py:294
  127.2 3.7 %collective-permute-start.12 = (bf16[512,1280]{1,0:T(8,128)(2,1)}, bf16[512,1280]{1,0:T(8,128)(2,1)}, u32[]{:S(2)}, u32[]{:S(2)}) collective-permute-start(bf16[512,1280]{1,0:T(8,128)(2,1)} %collective-permute-done.7.refs_0_.refs_2_), channel_id=1, source_target_pairs={{1,2},{2,1},{5,6},{6,5},{9,10},{10,9},{13,14},{14,13},{17,18},{18,... | collective-permute-start | bytes 3932168 | tf_op jit(solution)/shard_map/ppermute | solution.py:294
  134.4 15.5 %project_end.1 = (bf16[5,512,128]{2,1,0:T(8,128)(2,1)S(1)}, bf16[2,5,512,128]{3,2,1,0:T(8,128)(2,1)S(1)}) custom-call(s32[5]{0:T(128)S(1)} %stack.65.info, bf16[512,1280]{1,0:T(8,128)(2,1)} %collective-permute-done.7.refs_0_.refs_2_, bf16[512,1280]{1,0:T(8,128)(2,1)} %collective-permute-done.6.refs_1_.refs_4_, bf16[512,1280]{1,0:T(8,128)(2,1)S(1)} %copy-done.1, ...), custom_call_target="tpu_custom_call" | custom-call | flops 10000000000 | bytes 1 | tf_op jit(solution)/shard_map/project_end/pallas_call | solution.py:101
  154.9 5.0 %collective-permute-done.12.inner = bf16[512,1280]{1,0:T(8,128)(2,1)} collective-permute-done((bf16[512,1280]{1,0:T(8,128)(2,1)}, bf16[512,1280]{1,0:T(8,128)(2,1)}, u32[]{:S(2)}, u32[]{:S(2)}) %collective-permute-start.12) | collective-permute-done | bytes 1310752 | tf_op jit(solution)/shard_map/ppermute | solution.py:294
  163.0 13.7 %project_raw.1.raw = f32[3,5,512,128]{3,2,1,0:T(8,128)} custom-call(s32[4]{0:T(128)S(1)} %pad_add_fusion.2.info, bf16[16,1280]{1,0:T(8,128)(2,1)S(1)} %collective-permute-done.15.refs_0_, bf16[512,1280]{1,0:T(8,128)(2,1)S(1)} %copy-done.3, bf16[512,1280]{1,0:T(8,128)(2,1)} %collective-permute-done.7.refs_0_.refs_2_, ...), custom_call_target="tpu_custom_call" | custom-call | flops 10000000000 | bytes 1 | tf_op jit(solution)/shard_map/project_raw/pallas_call | solution.py:101
  182.6 6.9 %collective-permute-done.13.outer = bf16[512,1280]{1,0:T(8,128)(2,1)S(1)} collective-permute-done((bf16[512,1280]{1,0:T(8,128)(2,1)}, bf16[512,1280]{1,0:T(8,128)(2,1)S(1)}, u32[]{:S(2)}, u32[]{:S(2)}) %collective-permute-start.13) | collective-permute-done | bytes 1310752 | tf_op jit(solution)/shard_map/ppermute | solution.py:294
  189.6 10.4 %finish.1 = (bf16[5,512,128]{2,1,0:T(8,128)(2,1)S(1)}, bf16[2,5,512,128]{3,2,1,0:T(8,128)(2,1)}) custom-call(s32[2]{0:T(128)S(1)} %pad_add_fusion.1.info, bf16[512,1280]{1,0:T(8,128)(2,1)} %collective-permute-done.12.inner, bf16[512,1280]{1,0:T(8,128)(2,1)S(1)} %collective-permute-done.13.outer, bf16[5120,640]{1,0:T(8,128)(2,1)} %wq.1, ...), custom_call_target="tpu_custom_call" | custom-call | flops 10000000000 | bytes 1 | tf_op jit(solution)/shard_map/finish/pallas_call | solution.py:139
  202.6 7.1 %attend.2.refs_6_ = bf16[2,512,640]{2,1,0:T(8,128)(2,1)} custom-call(s32[3]{0:T(128)S(1)} %get-tuple-element.67.info, bf16[5,512,128]{2,1,0:T(8,128)(2,1)S(1)} %get-tuple-element.52.refs_0_, bf16[2,5,512,128]{3,2,1,0:T(8,128)(2,1)S(1)} %select_select_fusion.refs_1_, bf16[2,5,512,128]{3,2,1,0:T(8,128)(2,1)} %collective-permute-done.20.refs_2_, ...), custom_call_target="tpu_custom_call" | custom-call | flops 1342177280 | bytes 3932160 | tf_op jit(solution)/shard_map/attend/pallas_call | solution.py:218
  209.8 7.1 %attend.3 = bf16[2,512,640]{2,1,0:T(8,128)(2,1)} custom-call(s32[3]{0:T(128)S(1)} %get-tuple-element.66.info, bf16[5,512,128]{2,1,0:T(8,128)(2,1)S(1)} %copy-done.5, bf16[2,5,512,128]{3,2,1,0:T(8,128)(2,1)S(1)} %select_select_fusion.refs_1_, bf16[2,5,512,128]{3,2,1,0:T(8,128)(2,1)} %collective-permute-done.20.refs_2_, ...), custom_call_target="tpu_custom_call", output_to_operand_aliasing={{}: (7, {})} | custom-call | flops 1342177280 | bytes 3932160 | tf_op jit(solution)/shard_map/attend/pallas_call | solution.py:218
  (75 shorter events, 39.1 us)
Async XLA Ops:
  3.0 17.3 %collective-permute-start = (bf16[512,1280]{1,0:T(8,128)(2,1)}, bf16[512,1280]{1,0:T(8,128)(2,1)}, u32[]{:S(2)}, u32[]{:S(2)}) collective-permute-start(bf16[512,1280]{1,0:T(8,128)(2,1)} %get-tuple-element.62), channel_id=1, source_target_pairs={{4,0},{8,4},{12,8},{16,12},{20,16},{24,20},{28,24},{5,1},{9,5},{13... | collective-permute-start | bytes 3932168 | tf_op jit(solution)/shard_map/ppermute | solution.py:313
  4.9 31.8 %collective-permute-start.1 = (bf16[512,1280]{1,0:T(8,128)(2,1)}, bf16[512,1280]{1,0:T(8,128)(2,1)}, u32[]{:S(2)}, u32[]{:S(2)}) collective-permute-start(bf16[512,1280]{1,0:T(8,128)(2,1)} %get-tuple-element.62), channel_id=1, source_target_pairs={{1,0},{2,3},{5,4},{6,7},{9,8},{10,11},{13,12},{14,15},{17,16},{18,... | collective-permute-start | bytes 3932168 | tf_op jit(solution)/shard_map/ppermute | solution.py:294
  22.8 44.9 %collective-permute-start.8 = (bf16[528,1280]{1,0:T(8,128)(2,1)S(1)}, bf16[528,1280]{1,0:T(8,128)(2,1)S(1)}, u32[]{:S(2)}, u32[]{:S(2)}) collective-permute-start(bf16[528,1280]{1,0:T(8,128)(2,1)S(1)} %copy-done.9), channel_id=1, source_target_pairs={{1,0},{2,3},{5,4},{6,7},{9,8},{10,11},{13,12},{14,15},{17,16},{18,... | collective-permute-start | bytes 4055048 | tf_op jit(solution)/shard_map/ppermute | solution.py:294
  25.2 32.2 %collective-permute-start.3 = (bf16[512,1280]{1,0:T(8,128)(2,1)S(1)}, bf16[512,1280]{1,0:T(8,128)(2,1)}, u32[]{:S(2)}, u32[]{:S(2)}) collective-permute-start(bf16[512,1280]{1,0:T(8,128)(2,1)S(1)} %fusion.5.refs_2_), channel_id=1, source_target_pairs={{0,1},{3,2},{4,5},{7,6},{8,9},{11,10},{12,13},{15,14},{16,17},{19,... | collective-permute-start | bytes 3932168 | tf_op jit(solution)/shard_map/ppermute | solution.py:294
  26.6 32.6 %collective-permute-start.4 = (bf16[512,1280]{1,0:T(8,128)(2,1)S(1)}, bf16[512,1280]{1,0:T(8,128)(2,1)}, u32[]{:S(2)}, u32[]{:S(2)}) collective-permute-start(bf16[512,1280]{1,0:T(8,128)(2,1)S(1)} %fusion.5.refs_2_), channel_id=1, source_target_pairs={{1,2},{2,1},{5,6},{6,5},{9,10},{10,9},{13,14},{14,13},{17,18},{18,... | collective-permute-start | bytes 3932168 | tf_op jit(solution)/shard_map/ppermute | solution.py:294
  32.4 39.7 %copy-start.12 = (f32[640]{0:T(1024)S(1)}, f32[640]{0:T(1024)}, u32[]{:S(2)}) copy-start(f32[640]{0:T(1024)} %param.13) | copy-start | bytes 7684
  36.6 35.6 %collective-permute-start.2 = (bf16[512,1280]{1,0:T(8,128)(2,1)}, bf16[512,1280]{1,0:T(8,128)(2,1)}, u32[]{:S(2)}, u32[]{:S(2)}) collective-permute-start(bf16[512,1280]{1,0:T(8,128)(2,1)} %slice_bitcast_fusion), channel_id=1, source_target_pairs={{0,4},{4,8},{8,12},{12,16},{16,20},{20,24},{24,28},{1,5},{5,9},{9,... | collective-permute-start | bytes 3932168 | tf_op jit(solution)/shard_map/ppermute | solution.py:320
  59.2 33.6 %collective-permute-start.5 = (bf16[512,1280]{1,0:T(8,128)(2,1)}, bf16[512,1280]{1,0:T(8,128)(2,1)}, u32[]{:S(2)}, u32[]{:S(2)}) collective-permute-start(bf16[512,1280]{1,0:T(8,128)(2,1)} %collective-permute-done.3.refs_3_), channel_id=1, source_target_pairs={{1,2},{2,1},{5,6},{6,5},{9,10},{10,9},{13,14},{14,13},{17,18},{18,... | collective-permute-start | bytes 3932168 | tf_op jit(solution)/shard_map/ppermute | solution.py:294
  63.4 33.6 %collective-permute-start.10 = (bf16[512,1280]{1,0:T(8,128)(2,1)}, bf16[512,1280]{1,0:T(8,128)(2,1)}, u32[]{:S(2)}, u32[]{:S(2)}) collective-permute-start(bf16[512,1280]{1,0:T(8,128)(2,1)} %collective-permute-done.1), channel_id=1, source_target_pairs={{4,0},{8,4},{12,8},{16,12},{20,16},{24,20},{28,24},{5,1},{9,5},{13... | collective-permute-start | bytes 3932168 | tf_op jit(solution)/shard_map/ppermute | solution.py:322
  65.3 31.6 %collective-permute-start.9 = (bf16[512,1280]{1,0:T(8,128)(2,1)}, bf16[512,1280]{1,0:T(8,128)(2,1)}, u32[]{:S(2)}, u32[]{:S(2)}) collective-permute-start(bf16[512,1280]{1,0:T(8,128)(2,1)} %collective-permute-done.4.refs_5_), channel_id=1, source_target_pairs={{1,0},{2,3},{5,4},{6,7},{9,8},{10,11},{13,12},{14,15},{17,16},{18,... | collective-permute-start | bytes 3932168 | tf_op jit(solution)/shard_map/ppermute | solution.py:294
  69.2 27.8 %collective-permute-start.11 = (bf16[512,1280]{1,0:T(8,128)(2,1)}, bf16[512,1280]{1,0:T(8,128)(2,1)}, u32[]{:S(2)}, u32[]{:S(2)}) collective-permute-start(bf16[512,1280]{1,0:T(8,128)(2,1)} %slice.71), channel_id=1, source_target_pairs={{0,4},{4,8},{8,12},{12,16},{16,20},{20,24},{24,28},{1,5},{5,9},{9,... | collective-permute-start | bytes 3932168 | tf_op jit(solution)/shard_map/ppermute | solution.py:327
  74.8 31.7 %collective-permute-start.7 = (bf16[512,1280]{1,0:T(8,128)(2,1)S(1)}, bf16[512,1280]{1,0:T(8,128)(2,1)}, u32[]{:S(2)}, u32[]{:S(2)}) collective-permute-start(bf16[512,1280]{1,0:T(8,128)(2,1)S(1)} %fusion.2.refs_1_), channel_id=1, source_target_pairs={{0,1},{3,2},{4,5},{7,6},{8,9},{11,10},{12,13},{15,14},{16,17},{19,... | collective-permute-start | bytes 3932168 | tf_op jit(solution)/shard_map/ppermute | solution.py:294
  92.8 33.6 %collective-permute-start.6 = (bf16[512,1280]{1,0:T(8,128)(2,1)S(1)}, bf16[512,1280]{1,0:T(8,128)(2,1)}, u32[]{:S(2)}, u32[]{:S(2)}) collective-permute-start(bf16[512,1280]{1,0:T(8,128)(2,1)S(1)} %fusion.2.refs_1_), channel_id=1, source_target_pairs={{1,2},{2,1},{5,6},{6,5},{9,10},{10,9},{13,14},{14,13},{17,18},{18,... | collective-permute-start | bytes 3932168 | tf_op jit(solution)/shard_map/ppermute | solution.py:294
  97.0 36.4 %collective-permute-start.14 = (bf16[512,1280]{1,0:T(8,128)(2,1)}, bf16[512,1280]{1,0:T(8,128)(2,1)S(1)}, u32[]{:S(2)}, u32[]{:S(2)}) collective-permute-start(bf16[512,1280]{1,0:T(8,128)(2,1)} %collective-permute-done.5.refs_7_), channel_id=1, source_target_pairs={{1,0},{2,3},{5,4},{6,7},{9,8},{10,11},{13,12},{14,15},{17,16},{18,... | collective-permute-start | bytes 3932168 | tf_op jit(solution)/shard_map/ppermute | solution.py:294
  127.2 32.7 %collective-permute-start.12 = (bf16[512,1280]{1,0:T(8,128)(2,1)}, bf16[512,1280]{1,0:T(8,128)(2,1)}, u32[]{:S(2)}, u32[]{:S(2)}) collective-permute-start(bf16[512,1280]{1,0:T(8,128)(2,1)} %collective-permute-done.7.refs_0_.refs_2_), channel_id=1, source_target_pairs={{1,2},{2,1},{5,6},{6,5},{9,10},{10,9},{13,14},{14,13},{17,18},{18,... | collective-permute-start | bytes 3932168 | tf_op jit(solution)/shard_map/ppermute | solution.py:294
  130.8 19.1 %collective-permute-start.15 = (bf16[16,1280]{1,0:T(8,128)(2,1)S(1)}, bf16[16,1280]{1,0:T(8,128)(2,1)S(1)}, u32[]{:S(2)}, u32[]{:S(2)}) collective-permute-start(bf16[16,1280]{1,0:T(8,128)(2,1)S(1)} %slice.70), channel_id=1, source_target_pairs={{0,4},{4,0},{8,12},{12,8},{16,20},{20,16},{24,28},{28,24},{1,5},{5... | collective-permute-start | bytes 122888 | tf_op jit(solution)/shard_map/ppermute | solution.py:340
  130.9 30.8 %collective-permute-start.16 = (bf16[512,1280]{1,0:T(8,128)(2,1)}, bf16[512,1280]{1,0:T(8,128)(2,1)}, u32[]{:S(2)}, u32[]{:S(2)}) collective-permute-start(bf16[512,1280]{1,0:T(8,128)(2,1)} %collective-permute-done.6.refs_1_.refs_4_), channel_id=1, source_target_pairs={{1,0},{2,3},{5,4},{6,7},{9,8},{10,11},{13,12},{14,15},{17,16},{18,... | collective-permute-start | bytes 3932168 | tf_op jit(solution)/shard_map/ppermute | solution.py:294
  150.0 26.8 %collective-permute-start.17 = (bf16[2,5,512,128]{3,2,1,0:T(8,128)(2,1)S(1)}, bf16[2,5,512,128]{3,2,1,0:T(8,128)(2,1)}, u32[]{:S(2)}, u32[]{:S(2)}) collective-permute-start(bf16[2,5,512,128]{3,2,1,0:T(8,128)(2,1)S(1)} %get-tuple-element.50.refs_3_), channel_id=1, source_target_pairs={{0,8},{1,9},{2,10},{3,11}} | collective-permute-start | bytes 3932168 | tf_op jit(solution)/shard_map/ppermute | solution.py:247
  151.3 25.5 %collective-permute-start.18 = (bf16[2,5,512,128]{3,2,1,0:T(8,128)(2,1)S(1)}, bf16[2,5,512,128]{3,2,1,0:T(8,128)(2,1)}, u32[]{:S(2)}, u32[]{:S(2)}) collective-permute-start(bf16[2,5,512,128]{3,2,1,0:T(8,128)(2,1)S(1)} %get-tuple-element.50.refs_3_), channel_id=1, source_target_pairs={{0,16},{1,17},{2,18},{3,19}} | collective-permute-start | bytes 3932168 | tf_op jit(solution)/shard_map/ppermute | solution.py:247
  153.0 23.7 %collective-permute-start.19 = (bf16[2,5,512,128]{3,2,1,0:T(8,128)(2,1)S(1)}, bf16[2,5,512,128]{3,2,1,0:T(8,128)(2,1)}, u32[]{:S(2)}, u32[]{:S(2)}) collective-permute-start(bf16[2,5,512,128]{3,2,1,0:T(8,128)(2,1)S(1)} %get-tuple-element.50.refs_3_), channel_id=1, source_target_pairs={{0,24},{1,25},{2,26},{3,27}} | collective-permute-start | bytes 3932168 | tf_op jit(solution)/shard_map/ppermute | solution.py:247
  159.9 29.7 %collective-permute-start.13 = (bf16[512,1280]{1,0:T(8,128)(2,1)}, bf16[512,1280]{1,0:T(8,128)(2,1)S(1)}, u32[]{:S(2)}, u32[]{:S(2)}) collective-permute-start(bf16[512,1280]{1,0:T(8,128)(2,1)} %collective-permute-done.12.inner), channel_id=1, source_target_pairs={{1,0},{2,3},{5,4},{6,7},{9,8},{10,11},{13,12},{14,15},{17,16},{18,... | collective-permute-start | bytes 3932168 | tf_op jit(solution)/shard_map/ppermute | solution.py:294
  178.3 24.3 %collective-permute-start.20 = (bf16[2,5,512,128]{3,2,1,0:T(8,128)(2,1)S(1)}, bf16[2,5,512,128]{3,2,1,0:T(8,128)(2,1)}, u32[]{:S(2)}, u32[]{:S(2)}) collective-permute-start(bf16[2,5,512,128]{3,2,1,0:T(8,128)(2,1)S(1)} %select_select_fusion.refs_1_), channel_id=1, source_target_pairs={{0,4},{8,12},{16,20},{24,28},{1,5},{9,13},{17,21},{25,29},{2,6},{1... | collective-permute-start | bytes 3932168 | tf_op jit(solution)/shard_map/ppermute | solution.py:248
  180.7 29.1 %collective-permute-start.21 = (bf16[2,5,512,128]{3,2,1,0:T(8,128)(2,1)S(1)}, bf16[2,5,512,128]{3,2,1,0:T(8,128)(2,1)}, u32[]{:S(2)}, u32[]{:S(2)}) collective-permute-start(bf16[2,5,512,128]{3,2,1,0:T(8,128)(2,1)S(1)} %get-tuple-element.50.refs_3_), channel_id=1, source_target_pairs={{4,8},{8,12},{12,16},{16,20},{20,24},{24,28},{5,9},{9,13},{13,17},... | collective-permute-start | bytes 3932168 | tf_op jit(solution)/shard_map/ppermute | solution.py:345
  200.8 9.0 %collective-permute-start.22 = (bf16[2,5,512,128]{3,2,1,0:T(8,128)(2,1)}, bf16[2,5,512,128]{3,2,1,0:T(8,128)(2,1)}, u32[]{:S(2)}, u32[]{:S(2)}) collective-permute-start(bf16[2,5,512,128]{3,2,1,0:T(8,128)(2,1)} %get-tuple-element.51.refs_4_), channel_id=1, source_target_pairs={{0,4},{1,5},{2,6},{3,7}} | collective-permute-start | bytes 3932168 | tf_op jit(solution)/shard_map/ppermute | solution.py:348
  (13 other events, 176.1 us)

commit v15 on v14

--- a/solution.py
+++ b/solution.py
@@ -325,14 +325,13 @@
     outer_taps = joined_rows(raw_last[later.shape[0] :], taps.shape[0])
     raw_last = raw_last[: later.shape[0]]
     raw_preceding = lax.ppermute(raw_last, "tm", ups)
-    later2, cross1 = hold((mixed2, cross1))
-    middle2, inward2 = send(later2, MIDDLE), send(mixed2, INWARD)
+    middle2, inward2 = send(mixed2, MIDDLE), send(mixed2, INWARD)
     level = (cross1, second1, raw_following, raw_preceding)
     cross1, second1, raw_following, raw_preceding = hold(level)
     third1 = send(cross1, OUTWARD)
     first1 = mix_first(raw_first, raw_last, raw_following, outer_taps)
     first2 = mix_second(raw_first, raw_last, raw_following, raw_preceding, outer_taps)
-    middle2, inward2, first1, first2 = hold((middle2, inward2, first1, first2))
+    middle2, first1, first2 = hold((middle2, first1, first2))
     cross2, second2 = send(inward2, MIDDLE), send(middle2, OUTWARD)
 
     sources1 = [(mixed1,), (inward1, first1), (middle1, second1), (cross1, third1)]
@@ -346,6 +345,7 @@
     raw2 = project([(mixed2,), (inward2, first2), (middle2, second2)], info_raw, weights, after=(beside,), flops=10**10)
     q2, kv2 = finish(raw2, cross2, third2, info_end, weights, gains, 10**10)
     shift2 = lax.ppermute(kv2, "tm", [(0, 1)])
+    anchor, shift1 = hold((anchor, shift1))
     late = jnp.where(start, 0, 1)
     odd = pos % 2
     result = attend(q1, anchor, odd, [kv1, kv2], late, late)

time: 220 us -> 218 us (level)
  the two profiles are of different devices: /device:TPU:10 before, /device:TPU:6 now
where the time goes in v15:
time: 218 us; the launch traced here: 217 us
  waiting for transfers between devices  102 us (47%)
  Pallas kernels  52.6 us (24%)
  starting transfers between devices  42.5 us (19%)
  other arithmetic  9.76 us (4%)
  local copies, waits for them, and re-layouts  8.84 us (4%)
    ppermute x12, waiting for transfers between devices, send(): return lax.ppermute(x, 'head', pairs)  76.3 us
    pallas_call x2, Pallas kernels, project(): pl.pallas_call(functools.partial(project_body, pairs, len(after), final),...  29.4 us
    ppermute x12, starting transfers between devices, send(): return lax.ppermute(x, 'head', pairs)  22.1 us
    pallas_call x2, Pallas kernels, attend(): pl.pallas_call(functools.partial(attend_body, 256, (len(anchors), len(opt...  14.2 us
    ppermute x1, waiting for transfers between devices, per_device(): following = lax.ppermute(frames[0], 'tm', downs)  13.9 us
    pallas_call x1, Pallas kernels, finish(): pl.pallas_call(finish_body, grid_spec=pltpu.PrefetchScalarGridSpec(num_sc...  9.04 us
    convert_element_type x3, other arithmetic, mix(): (centre + taps[0] * before + taps[1] * centre + taps[2] * after).astype(B...  6.93 us
    ppermute x3, waiting for transfers between devices, broadcast_first(): held = jnp.where(mine == to, lax.ppermute(x, axis, [(0, to)]), held)  6.88 us
  transfers between devices with their start and end apart: 23, of which 9 were waited for; matrix products, arithmetic and copies ran while one was open for 6% of the time, Pallas kernels for 21%

profile of v15, /device:TPU:6, one launch (start us, length us, event | category | flops | bytes accessed | tf_op | source)
XLA Modules:
  0.0 216.8 jit_solution(3005954818327367034)
XLA Ops:
  0.0 2.9 %slice_bitcast_fusion.2 = (bf16[512,1280]{1,0:T(8,128)(2,1)S(1)}, bf16[512,1280]{1,0:T(8,128)(2,1)}) fusion(bf16[2,512,1280]{2,1,0:T(8,128)(2,1)} %param.7), kind=kLoop, calls=%fused_computation.24 | loop fusion | bytes 5242880 | tf_op jit(solution)/shard_map/squeeze | solution.py:321
  3.0 1.9 collective-permute-start
  6.4 13.9 %collective-permute-done = bf16[512,1280]{1,0:T(8,128)(2,1)S(1)} collective-permute-done((bf16[512,1280]{1,0:T(8,128)(2,1)}, bf16[512,1280]{1,0:T(8,128)(2,1)S(1)}, u32[]{:S(2)}, u32[]{:S(2)}) %collective-permute-start) | collective-permute-done | bytes 1310752 | tf_op jit(solution)/shard_map/ppermute | solution.py:313
  21.4 4.6 %collective-permute-start.8 = (bf16[512,1280]{1,0:T(8,128)(2,1)S(1)}, bf16[512,1280]{1,0:T(8,128)(2,1)}, u32[]{:S(2)}, u32[]{:S(2)}) collective-permute-start(bf16[512,1280]{1,0:T(8,128)(2,1)S(1)} %fusion.5.refs_2_), channel_id=1, source_target_pairs={{0,1},{3,2},{4,5},{7,6},{8,9},{11,10},{12,13},{15,14},{16,17},{19,... | collective-permute-start | bytes 3932168 | tf_op jit(solution)/shard_map/ppermute | solution.py:294
  29.1 9.6 %collective-permute-done.1 = bf16[512,1280]{1,0:T(8,128)(2,1)} collective-permute-done((bf16[512,1280]{1,0:T(8,128)(2,1)}, bf16[512,1280]{1,0:T(8,128)(2,1)}, u32[]{:S(2)}, u32[]{:S(2)}) %collective-permute-start.1) | collective-permute-done | bytes 1310752 | tf_op jit(solution)/shard_map/ppermute | solution.py:294
  38.6 1.9 collective-permute-start.2
  40.6 3.6 %collective-permute-start.12 = (bf16[512,1280]{1,0:T(8,128)(2,1)}, bf16[512,1280]{1,0:T(8,128)(2,1)}, u32[]{:S(2)}, u32[]{:S(2)}) collective-permute-start(bf16[512,1280]{1,0:T(8,128)(2,1)} %collective-permute-done.1), channel_id=1, source_target_pairs={{4,0},{8,4},{12,8},{16,12},{20,16},{24,20},{28,24},{5,1},{9,5},{13... | collective-permute-start | bytes 3932168 | tf_op jit(solution)/shard_map/ppermute | solution.py:322
  47.3 20.2 %collective-permute-done.7 = bf16[528,1280]{1,0:T(8,128)(2,1)S(1)} collective-permute-done((bf16[528,1280]{1,0:T(8,128)(2,1)S(1)}, bf16[528,1280]{1,0:T(8,128)(2,1)S(1)}, u32[]{:S(2)}, u32[]{:S(2)}) %collective-permute-start.7) | collective-permute-done | bytes 1351712 | tf_op jit(solution)/shard_map/ppermute | solution.py:294
  69.0 2.0 collective-permute-start.13
  72.3 2.5 %collective-permute-start.3 = (bf16[512,1280]{1,0:T(8,128)(2,1)S(1)}, bf16[512,1280]{1,0:T(8,128)(2,1)}, u32[]{:S(2)}, u32[]{:S(2)}) collective-permute-start(bf16[512,1280]{1,0:T(8,128)(2,1)S(1)} %fusion.2.refs_1_), channel_id=1, source_target_pairs={{0,1},{3,2},{4,5},{7,6},{8,9},{11,10},{12,13},{15,14},{16,17},{19,... | collective-permute-start | bytes 3932168 | tf_op jit(solution)/shard_map/ppermute | solution.py:294
  76.6 18.8 %collective-permute-done.11.refs_6_ = bf16[512,1280]{1,0:T(8,128)(2,1)} collective-permute-done((bf16[512,1280]{1,0:T(8,128)(2,1)}, bf16[512,1280]{1,0:T(8,128)(2,1)}, u32[]{:S(2)}, u32[]{:S(2)}) %collective-permute-start.11) | collective-permute-done | bytes 1310752 | tf_op jit(solution)/shard_map/ppermute | solution.py:294
  97.6 3.2 %collective-permute-done.3.refs_0_.refs_2_ = bf16[512,1280]{1,0:T(8,128)(2,1)} collective-permute-done((bf16[512,1280]{1,0:T(8,128)(2,1)S(1)}, bf16[512,1280]{1,0:T(8,128)(2,1)}, u32[]{:S(2)}, u32[]{:S(2)}) %collective-permute-start.3) | collective-permute-done | bytes 1310752 | tf_op jit(solution)/shard_map/ppermute | solution.py:294
  103.4 4.7 %fusion.11 = (bf16[512,1280]{1,0:T(8,128)(2,1)S(1)}, bf16[512,1280]{1,0:T(8,128)(2,1)}) fusion(bf16[512,1280]{1,0:T(8,128)(2,1)} %collective-permute-done.12, bf16[512,1280]{1,0:T(8,128)(2,1)} %collective-permute-done.1, bf16[512,1280]{1,0:T(8,128)(2,1)} %collective-permute-done.13, f32[1280]{0:T(1024)S(1)} %get-tuple-element.54, ...), kind=kLoop, calls=%fused_computation.19 | loop fusion | flops 17039360 | bytes 7879681 | tf_op jit(solution)/shard_map/convert_element_type | solution.py:258
  109.6 19.6 %collective-permute-done.14.refs_8_ = bf16[512,1280]{1,0:T(8,128)(2,1)S(1)} collective-permute-done((bf16[512,1280]{1,0:T(8,128)(2,1)}, bf16[512,1280]{1,0:T(8,128)(2,1)S(1)}, u32[]{:S(2)}, u32[]{:S(2)}) %collective-permute-start.14) | collective-permute-done | bytes 1310752 | tf_op jit(solution)/shard_map/ppermute | solution.py:294
  130.3 15.5 %project_end.1 = (bf16[5,512,128]{2,1,0:T(8,128)(2,1)S(1)}, bf16[2,5,512,128]{3,2,1,0:T(8,128)(2,1)S(1)}) custom-call(s32[5]{0:T(128)S(1)} %stack.65.info, bf16[512,1280]{1,0:T(8,128)(2,1)} %collective-permute-done.3.refs_0_.refs_2_, bf16[512,1280]{1,0:T(8,128)(2,1)} %collective-permute-done.6.refs_1_.refs_4_, bf16[512,1280]{1,0:T(8,128)(2,1)S(1)} %copy-done.1, ...), custom_call_target="tpu_custom_call" | custom-call | flops 10000000000 | bytes 1 | tf_op jit(solution)/shard_map/project_end/pallas_call | solution.py:101
  152.4 4.9 %collective-permute-done.16.refs_5_ = bf16[512,1280]{1,0:T(8,128)(2,1)} collective-permute-done((bf16[512,1280]{1,0:T(8,128)(2,1)}, bf16[512,1280]{1,0:T(8,128)(2,1)}, u32[]{:S(2)}, u32[]{:S(2)}) %collective-permute-start.16) | collective-permute-done | bytes 1310752 | tf_op jit(solution)/shard_map/ppermute | solution.py:294
  158.7 13.8 %project_raw.1.raw = f32[3,5,512,128]{3,2,1,0:T(8,128)} custom-call(s32[4]{0:T(128)S(1)} %pad_add_fusion.2.info, bf16[16,1280]{1,0:T(8,128)(2,1)S(1)} %collective-permute-done.15.refs_0_, bf16[512,1280]{1,0:T(8,128)(2,1)S(1)} %copy-done.3, bf16[512,1280]{1,0:T(8,128)(2,1)} %collective-permute-done.3.refs_0_.refs_2_, ...), custom_call_target="tpu_custom_call" | custom-call | flops 10000000000 | bytes 1 | tf_op jit(solution)/shard_map/project_raw/pallas_call | solution.py:101
  172.5 6.9 %collective-permute-done.19 = bf16[2,5,512,128]{3,2,1,0:T(8,128)(2,1)} collective-permute-done((bf16[2,5,512,128]{3,2,1,0:T(8,128)(2,1)S(1)}, bf16[2,5,512,128]{3,2,1,0:T(8,128)(2,1)}, u32[]{:S(2)}, u32[]{:S(2)}) %collective-permute-start.19) | collective-permute-done | bytes 1310752 | tf_op jit(solution)/shard_map/ppermute | solution.py:247
  180.9 2.4 %collective-permute-start.20 = (bf16[2,5,512,128]{3,2,1,0:T(8,128)(2,1)S(1)}, bf16[2,5,512,128]{3,2,1,0:T(8,128)(2,1)}, u32[]{:S(2)}, u32[]{:S(2)}) collective-permute-start(bf16[2,5,512,128]{3,2,1,0:T(8,128)(2,1)S(1)} %select_select_fusion.refs_1_), channel_id=1, source_target_pairs={{0,4},{8,12},{16,20},{24,28},{1,5},{9,13},{17,21},{25,29},{2,6},{1... | collective-permute-start | bytes 3932168 | tf_op jit(solution)/shard_map/ppermute | solution.py:248
  183.3 1.9 collective-permute-start.21
  185.2 9.0 %finish.1 = (bf16[5,512,128]{2,1,0:T(8,128)(2,1)S(1)}, bf16[2,5,512,128]{3,2,1,0:T(8,128)(2,1)}) custom-call(s32[2]{0:T(128)S(1)} %pad_add_fusion.1.info, bf16[512,1280]{1,0:T(8,128)(2,1)} %collective-permute-done.4.inner, bf16[512,1280]{1,0:T(8,128)(2,1)S(1)} %collective-permute-done.5.outer, bf16[5120,640]{1,0:T(8,128)(2,1)} %wq.1, bf16[5120,640]{1,0:T(8,128)(2,1)} %wk.1, ...), custom_call_target="tpu_custom_call" | custom-call | flops 10000000000 | bytes 1 | tf_op jit(solution)/shard_map/finish/pallas_call | solution.py:139
  196.9 5.4 %collective-permute-done.21.refs_4_ = bf16[2,5,512,128]{3,2,1,0:T(8,128)(2,1)} collective-permute-done((bf16[2,5,512,128]{3,2,1,0:T(8,128)(2,1)S(1)}, bf16[2,5,512,128]{3,2,1,0:T(8,128)(2,1)}, u32[]{:S(2)}, u32[]{:S(2)}) %collective-permute-start.21) | collective-permute-done | bytes 1310752 | tf_op jit(solution)/shard_map/ppermute | solution.py:344
  202.3 7.1 %attend.2.refs_6_ = bf16[2,512,640]{2,1,0:T(8,128)(2,1)} custom-call(s32[3]{0:T(128)S(1)} %get-tuple-element.67.info, bf16[5,512,128]{2,1,0:T(8,128)(2,1)S(1)} %get-tuple-element.52.refs_0_, bf16[2,5,512,128]{3,2,1,0:T(8,128)(2,1)S(1)} %select_select_fusion.refs_1_, bf16[2,5,512,128]{3,2,1,0:T(8,128)(2,1)} %collective-permute-done.20.refs_2_, ...), custom_call_target="tpu_custom_call" | custom-call | flops 1342177280 | bytes 3932160 | tf_op jit(solution)/shard_map/attend/pallas_call | solution.py:218
  209.5 7.1 %attend.3 = bf16[2,512,640]{2,1,0:T(8,128)(2,1)} custom-call(s32[3]{0:T(128)S(1)} %get-tuple-element.66.info, bf16[5,512,128]{2,1,0:T(8,128)(2,1)S(1)} %copy-done.5, bf16[2,5,512,128]{3,2,1,0:T(8,128)(2,1)S(1)} %select_select_fusion.refs_1_, bf16[2,5,512,128]{3,2,1,0:T(8,128)(2,1)} %collective-permute-done.20.refs_2_, ...), custom_call_target="tpu_custom_call", output_to_operand_aliasing={{}: (7, {})} | custom-call | flops 1342177280 | bytes 3932160 | tf_op jit(solution)/shard_map/attend/pallas_call | solution.py:218
  (71 shorter events, 32.6 us)
Async XLA Ops:
  3.0 17.3 %collective-permute-start = (bf16[512,1280]{1,0:T(8,128)(2,1)}, bf16[512,1280]{1,0:T(8,128)(2,1)S(1)}, u32[]{:S(2)}, u32[]{:S(2)}) collective-permute-start(bf16[512,1280]{1,0:T(8,128)(2,1)} %get-tuple-element.62), channel_id=1, source_target_pairs={{4,0},{8,4},{12,8},{16,12},{20,16},{24,20},{28,24},{5,1},{9,5},{13... | collective-permute-start | bytes 3932168 | tf_op jit(solution)/shard_map/ppermute | solution.py:313
  4.9 33.8 %collective-permute-start.1 = (bf16[512,1280]{1,0:T(8,128)(2,1)}, bf16[512,1280]{1,0:T(8,128)(2,1)}, u32[]{:S(2)}, u32[]{:S(2)}) collective-permute-start(bf16[512,1280]{1,0:T(8,128)(2,1)} %get-tuple-element.62), channel_id=1, source_target_pairs={{1,0},{2,3},{5,4},{6,7},{9,8},{10,11},{13,12},{14,15},{17,16},{18,... | collective-permute-start | bytes 3932168 | tf_op jit(solution)/shard_map/ppermute | solution.py:294
  21.4 22.8 %collective-permute-start.8 = (bf16[512,1280]{1,0:T(8,128)(2,1)S(1)}, bf16[512,1280]{1,0:T(8,128)(2,1)}, u32[]{:S(2)}, u32[]{:S(2)}) collective-permute-start(bf16[512,1280]{1,0:T(8,128)(2,1)S(1)} %fusion.5.refs_2_), channel_id=1, source_target_pairs={{0,1},{3,2},{4,5},{7,6},{8,9},{11,10},{12,13},{15,14},{16,17},{19,... | collective-permute-start | bytes 3932168 | tf_op jit(solution)/shard_map/ppermute | solution.py:294
  25.9 18.3 %collective-permute-start.9 = (bf16[512,1280]{1,0:T(8,128)(2,1)S(1)}, bf16[512,1280]{1,0:T(8,128)(2,1)}, u32[]{:S(2)}, u32[]{:S(2)}) collective-permute-start(bf16[512,1280]{1,0:T(8,128)(2,1)S(1)} %fusion.5.refs_2_), channel_id=1, source_target_pairs={{1,2},{2,1},{5,6},{6,5},{9,10},{10,9},{13,14},{14,13},{17,18},{18,... | collective-permute-start | bytes 3932168 | tf_op jit(solution)/shard_map/ppermute | solution.py:294
  27.7 39.8 %collective-permute-start.7 = (bf16[528,1280]{1,0:T(8,128)(2,1)S(1)}, bf16[528,1280]{1,0:T(8,128)(2,1)S(1)}, u32[]{:S(2)}, u32[]{:S(2)}) collective-permute-start(bf16[528,1280]{1,0:T(8,128)(2,1)S(1)} %pad_maximum_fusion), channel_id=1, source_target_pairs={{1,0},{2,3},{5,4},{6,7},{9,8},{10,11},{13,12},{14,15},{17,16},{18,... | collective-permute-start | bytes 4055048 | tf_op jit(solution)/shard_map/ppermute | solution.py:294
  38.6 32.4 %collective-permute-start.2 = (bf16[512,1280]{1,0:T(8,128)(2,1)S(1)}, bf16[512,1280]{1,0:T(8,128)(2,1)S(1)}, u32[]{:S(2)}, u32[]{:S(2)}) collective-permute-start(bf16[512,1280]{1,0:T(8,128)(2,1)S(1)} %slice_bitcast_fusion), channel_id=1, source_target_pairs={{0,4},{4,8},{8,12},{12,16},{16,20},{20,24},{24,28},{1,5},{5,9},{9,... | collective-permute-start | bytes 3932168 | tf_op jit(solution)/shard_map/ppermute | solution.py:320
  40.6 34.3 %collective-permute-start.12 = (bf16[512,1280]{1,0:T(8,128)(2,1)}, bf16[512,1280]{1,0:T(8,128)(2,1)}, u32[]{:S(2)}, u32[]{:S(2)}) collective-permute-start(bf16[512,1280]{1,0:T(8,128)(2,1)} %collective-permute-done.1), channel_id=1, source_target_pairs={{4,0},{8,4},{12,8},{16,12},{20,16},{24,20},{28,24},{5,1},{9,5},{13... | collective-permute-start | bytes 3932168 | tf_op jit(solution)/shard_map/ppermute | solution.py:322
  44.2 32.4 %collective-permute-start.10 = (bf16[512,1280]{1,0:T(8,128)(2,1)}, bf16[512,1280]{1,0:T(8,128)(2,1)}, u32[]{:S(2)}, u32[]{:S(2)}) collective-permute-start(bf16[512,1280]{1,0:T(8,128)(2,1)} %collective-permute-done.8.refs_3_), channel_id=1, source_target_pairs={{1,2},{2,1},{5,6},{6,5},{9,10},{10,9},{13,14},{14,13},{17,18},{18,... | collective-permute-start | bytes 3932168 | tf_op jit(solution)/shard_map/ppermute | solution.py:294
  46.0 49.4 %collective-permute-start.11 = (bf16[512,1280]{1,0:T(8,128)(2,1)}, bf16[512,1280]{1,0:T(8,128)(2,1)}, u32[]{:S(2)}, u32[]{:S(2)}) collective-permute-start(bf16[512,1280]{1,0:T(8,128)(2,1)} %collective-permute-done.9.refs_5_), channel_id=1, source_target_pairs={{1,0},{2,3},{5,4},{6,7},{9,8},{10,11},{13,12},{14,15},{17,16},{18,... | collective-permute-start | bytes 3932168 | tf_op jit(solution)/shard_map/ppermute | solution.py:294
  69.0 26.4 %collective-permute-start.13 = (bf16[512,1280]{1,0:T(8,128)(2,1)}, bf16[512,1280]{1,0:T(8,128)(2,1)}, u32[]{:S(2)}, u32[]{:S(2)}) collective-permute-start(bf16[512,1280]{1,0:T(8,128)(2,1)} %slice.71), channel_id=1, source_target_pairs={{0,4},{4,8},{8,12},{12,16},{16,20},{20,24},{24,28},{1,5},{5,9},{9,... | collective-permute-start | bytes 3932168 | tf_op jit(solution)/shard_map/ppermute | solution.py:327
  72.2 35.9 %copy-start.2 = (bf16[512,1280]{1,0:T(8,128)(2,1)}, bf16[512,1280]{1,0:T(8,128)(2,1)S(1)}, u32[]{:S(2)}) copy-start(bf16[512,1280]{1,0:T(8,128)(2,1)S(1)} %fusion.2.refs_1_) | copy-start | bytes 3932164
  72.3 28.6 %collective-permute-start.3 = (bf16[512,1280]{1,0:T(8,128)(2,1)S(1)}, bf16[512,1280]{1,0:T(8,128)(2,1)}, u32[]{:S(2)}, u32[]{:S(2)}) collective-permute-start(bf16[512,1280]{1,0:T(8,128)(2,1)S(1)} %fusion.2.refs_1_), channel_id=1, source_target_pairs={{0,1},{3,2},{4,5},{7,6},{8,9},{11,10},{12,13},{15,14},{16,17},{19,... | collective-permute-start | bytes 3932168 | tf_op jit(solution)/shard_map/ppermute | solution.py:294
  74.9 33.2 %collective-permute-start.6 = (bf16[512,1280]{1,0:T(8,128)(2,1)S(1)}, bf16[512,1280]{1,0:T(8,128)(2,1)}, u32[]{:S(2)}, u32[]{:S(2)}) collective-permute-start(bf16[512,1280]{1,0:T(8,128)(2,1)S(1)} %fusion.2.refs_1_), channel_id=1, source_target_pairs={{1,2},{2,1},{5,6},{6,5},{9,10},{10,9},{13,14},{14,13},{17,18},{18,... | collective-permute-start | bytes 3932168 | tf_op jit(solution)/shard_map/ppermute | solution.py:294
  95.4 33.8 %collective-permute-start.14 = (bf16[512,1280]{1,0:T(8,128)(2,1)}, bf16[512,1280]{1,0:T(8,128)(2,1)S(1)}, u32[]{:S(2)}, u32[]{:S(2)}) collective-permute-start(bf16[512,1280]{1,0:T(8,128)(2,1)} %collective-permute-done.10.refs_7_), channel_id=1, source_target_pairs={{1,0},{2,3},{5,4},{6,7},{9,8},{10,11},{13,12},{14,15},{17,16},{18,... | collective-permute-start | bytes 3932168 | tf_op jit(solution)/shard_map/ppermute | solution.py:294
  101.7 44.2 %collective-permute-start.15 = (bf16[16,1280]{1,0:T(8,128)(2,1)S(1)}, bf16[16,1280]{1,0:T(8,128)(2,1)S(1)}, u32[]{:S(2)}, u32[]{:S(2)}) collective-permute-start(bf16[16,1280]{1,0:T(8,128)(2,1)S(1)} %slice.78), channel_id=1, source_target_pairs={{0,4},{4,0},{8,12},{12,8},{16,20},{20,16},{24,28},{28,24},{1,5},{5... | collective-permute-start | bytes 122888 | tf_op jit(solution)/shard_map/ppermute | solution.py:339
  101.7 49.2 %collective-permute-start.4 = (bf16[512,1280]{1,0:T(8,128)(2,1)}, bf16[512,1280]{1,0:T(8,128)(2,1)}, u32[]{:S(2)}, u32[]{:S(2)}) collective-permute-start(bf16[512,1280]{1,0:T(8,128)(2,1)} %collective-permute-done.3.refs_0_.refs_2_), channel_id=1, source_target_pairs={{1,2},{2,1},{5,6},{6,5},{9,10},{10,9},{13,14},{14,13},{17,18},{18,... | collective-permute-start | bytes 3932168 | tf_op jit(solution)/shard_map/ppermute | solution.py:294
  108.1 49.2 %collective-permute-start.16 = (bf16[512,1280]{1,0:T(8,128)(2,1)}, bf16[512,1280]{1,0:T(8,128)(2,1)}, u32[]{:S(2)}, u32[]{:S(2)}) collective-permute-start(bf16[512,1280]{1,0:T(8,128)(2,1)} %collective-permute-done.6.refs_1_.refs_4_), channel_id=1, source_target_pairs={{1,0},{2,3},{5,4},{6,7},{9,8},{10,11},{13,12},{14,15},{17,16},{18,... | collective-permute-start | bytes 3932168 | tf_op jit(solution)/shard_map/ppermute | solution.py:294
  145.9 26.6 %collective-permute-start.17 = (bf16[2,5,512,128]{3,2,1,0:T(8,128)(2,1)S(1)}, bf16[2,5,512,128]{3,2,1,0:T(8,128)(2,1)}, u32[]{:S(2)}, u32[]{:S(2)}) collective-permute-start(bf16[2,5,512,128]{3,2,1,0:T(8,128)(2,1)S(1)} %get-tuple-element.47.refs_3_), channel_id=1, source_target_pairs={{0,8},{1,9},{2,10},{3,11}} | collective-permute-start | bytes 3932168 | tf_op jit(solution)/shard_map/ppermute | solution.py:247
  147.7 24.8 %collective-permute-start.18 = (bf16[2,5,512,128]{3,2,1,0:T(8,128)(2,1)S(1)}, bf16[2,5,512,128]{3,2,1,0:T(8,128)(2,1)}, u32[]{:S(2)}, u32[]{:S(2)}) collective-permute-start(bf16[2,5,512,128]{3,2,1,0:T(8,128)(2,1)S(1)} %get-tuple-element.47.refs_3_), channel_id=1, source_target_pairs={{0,16},{1,17},{2,18},{3,19}} | collective-permute-start | bytes 3932168 | tf_op jit(solution)/shard_map/ppermute | solution.py:247
  149.5 29.9 %collective-permute-start.19 = (bf16[2,5,512,128]{3,2,1,0:T(8,128)(2,1)S(1)}, bf16[2,5,512,128]{3,2,1,0:T(8,128)(2,1)}, u32[]{:S(2)}, u32[]{:S(2)}) collective-permute-start(bf16[2,5,512,128]{3,2,1,0:T(8,128)(2,1)S(1)} %get-tuple-element.47.refs_3_), channel_id=1, source_target_pairs={{0,24},{1,25},{2,26},{3,27}} | collective-permute-start | bytes 3932168 | tf_op jit(solution)/shard_map/ppermute | solution.py:247
  150.9 34.3 %collective-permute-start.5 = (bf16[512,1280]{1,0:T(8,128)(2,1)}, bf16[512,1280]{1,0:T(8,128)(2,1)S(1)}, u32[]{:S(2)}, u32[]{:S(2)}) collective-permute-start(bf16[512,1280]{1,0:T(8,128)(2,1)} %collective-permute-done.4.inner), channel_id=1, source_target_pairs={{1,0},{2,3},{5,4},{6,7},{9,8},{10,11},{13,12},{14,15},{17,16},{18,... | collective-permute-start | bytes 3932168 | tf_op jit(solution)/shard_map/ppermute | solution.py:294
  180.9 21.4 %collective-permute-start.20 = (bf16[2,5,512,128]{3,2,1,0:T(8,128)(2,1)S(1)}, bf16[2,5,512,128]{3,2,1,0:T(8,128)(2,1)}, u32[]{:S(2)}, u32[]{:S(2)}) collective-permute-start(bf16[2,5,512,128]{3,2,1,0:T(8,128)(2,1)S(1)} %select_select_fusion.refs_1_), channel_id=1, source_target_pairs={{0,4},{8,12},{16,20},{24,28},{1,5},{9,13},{17,21},{25,29},{2,6},{1... | collective-permute-start | bytes 3932168 | tf_op jit(solution)/shard_map/ppermute | solution.py:248
  183.3 19.0 %collective-permute-start.21 = (bf16[2,5,512,128]{3,2,1,0:T(8,128)(2,1)S(1)}, bf16[2,5,512,128]{3,2,1,0:T(8,128)(2,1)}, u32[]{:S(2)}, u32[]{:S(2)}) collective-permute-start(bf16[2,5,512,128]{3,2,1,0:T(8,128)(2,1)S(1)} %get-tuple-element.47.refs_3_), channel_id=1, source_target_pairs={{4,8},{8,12},{12,16},{16,20},{20,24},{24,28},{5,9},{9,13},{13,17},... | collective-permute-start | bytes 3932168 | tf_op jit(solution)/shard_map/ppermute | solution.py:344
  195.1 14.3 %collective-permute-start.22 = (bf16[2,5,512,128]{3,2,1,0:T(8,128)(2,1)}, bf16[2,5,512,128]{3,2,1,0:T(8,128)(2,1)}, u32[]{:S(2)}, u32[]{:S(2)}) collective-permute-start(bf16[2,5,512,128]{3,2,1,0:T(8,128)(2,1)} %get-tuple-element.51.refs_4_), channel_id=1, source_target_pairs={{0,4},{1,5},{2,6},{3,7}} | collective-permute-start | bytes 3932168 | tf_op jit(solution)/shard_map/ppermute | solution.py:347
  (11 other events, 78.3 us)

commit v16 on v15

--- a/solution.py
+++ b/solution.py
@@ -243,7 +243,7 @@
     count = lax.axis_size(axis)
     mine = lax.axis_index(axis)
     held = x
-    for to in reversed(range(2, count, 2)):
+    for to in range(2, count, 2):
         held = jnp.where(mine == to, lax.ppermute(x, axis, [(0, to)]), held)
     return held, lax.ppermute(held, axis, [(i, i + 1) for i in range(0, count, 2)])
 

time: 218 us -> 219 us (level)
  the two profiles are of different devices: /device:TPU:6 before, /device:TPU:10 now
where the time goes in v16:
time: 219 us; the launch traced here: 216 us
  waiting for transfers between devices  80.6 us (37%)
  starting transfers between devices  62.2 us (28%)
  Pallas kernels  53.9 us (25%)
  other arithmetic  9.76 us (4%)
  local copies, waits for them, and re-layouts  8.85 us (4%)
    ppermute x12, waiting for transfers between devices, send(): return lax.ppermute(x, 'head', pairs)  56.6 us
    ppermute x12, starting transfers between devices, send(): return lax.ppermute(x, 'head', pairs)  40 us
    pallas_call x2, Pallas kernels, project(): pl.pallas_call(functools.partial(project_body, pairs, len(after), final),...  29.3 us
    pallas_call x2, Pallas kernels, attend(): pl.pallas_call(functools.partial(attend_body, 256, (len(anchors), len(opt...  14.2 us
    ppermute x1, waiting for transfers between devices, per_device(): following = lax.ppermute(frames[0], 'tm', downs)  11.8 us
    pallas_call x1, Pallas kernels, finish(): pl.pallas_call(finish_body, grid_spec=pltpu.PrefetchScalarGridSpec(num_sc...  10.4 us
    ppermute x3, waiting for transfers between devices, broadcast_first(): held = jnp.where(mine == to, lax.ppermute(x, axis, [(0, to)]), held)  8.21 us
    convert_element_type x3, other arithmetic, mix(): (centre + taps[0] * before + taps[1] * centre + taps[2] * after).astype(B...  6.94 us
  transfers between devices with their start and end apart: 23, of which 13 were waited for; matrix products, arithmetic and copies ran while one was open for 6% of the time, Pallas kernels for 22%

profile of v16, /device:TPU:10, one launch (start us, length us, event | category | flops | bytes accessed | tf_op | source)
XLA Modules:
  0.0 215.9 jit_solution(3330488352294630953)
XLA Ops:
  4.9 3.4 %collective-permute-start.1 = (bf16[512,1280]{1,0:T(8,128)(2,1)}, bf16[512,1280]{1,0:T(8,128)(2,1)}, u32[]{:S(2)}, u32[]{:S(2)}) collective-permute-start(bf16[512,1280]{1,0:T(8,128)(2,1)} %get-tuple-element.62), channel_id=1, source_target_pairs={{1,0},{2,3},{5,4},{6,7},{9,8},{10,11},{13,12},{14,15},{17,16},{18,... | collective-permute-start | bytes 3932168 | tf_op jit(solution)/shard_map/ppermute | solution.py:294
  8.5 11.8 %collective-permute-done = bf16[512,1280]{1,0:T(8,128)(2,1)S(1)} collective-permute-done((bf16[512,1280]{1,0:T(8,128)(2,1)}, bf16[512,1280]{1,0:T(8,128)(2,1)S(1)}, u32[]{:S(2)}, u32[]{:S(2)}) %collective-permute-start) | collective-permute-done | bytes 1310752 | tf_op jit(solution)/shard_map/ppermute | solution.py:313
  22.7 3.5 %collective-permute-start.9 = (bf16[512,1280]{1,0:T(8,128)(2,1)S(1)}, bf16[512,1280]{1,0:T(8,128)(2,1)}, u32[]{:S(2)}, u32[]{:S(2)}) collective-permute-start(bf16[512,1280]{1,0:T(8,128)(2,1)S(1)} %fusion.5.refs_2_), channel_id=1, source_target_pairs={{1,2},{2,1},{5,6},{6,5},{9,10},{10,9},{13,14},{14,13},{17,18},{18,... | collective-permute-start | bytes 3932168 | tf_op jit(solution)/shard_map/ppermute | solution.py:294
  26.2 3.9 %collective-permute-start.7 = (bf16[528,1280]{1,0:T(8,128)(2,1)S(1)}, bf16[528,1280]{1,0:T(8,128)(2,1)S(1)}, u32[]{:S(2)}, u32[]{:S(2)}) collective-permute-start(bf16[528,1280]{1,0:T(8,128)(2,1)S(1)} %pad_maximum_fusion), channel_id=1, source_target_pairs={{1,0},{2,3},{5,4},{6,7},{9,8},{10,11},{13,12},{14,15},{17,16},{18,... | collective-permute-start | bytes 4055048 | tf_op jit(solution)/shard_map/ppermute | solution.py:294
  30.2 6.4 %collective-permute-done.1 = bf16[512,1280]{1,0:T(8,128)(2,1)} collective-permute-done((bf16[512,1280]{1,0:T(8,128)(2,1)}, bf16[512,1280]{1,0:T(8,128)(2,1)}, u32[]{:S(2)}, u32[]{:S(2)}) %collective-permute-start.1) | collective-permute-done | bytes 1310752 | tf_op jit(solution)/shard_map/ppermute | solution.py:294
  38.5 3.6 %collective-permute-start.12 = (bf16[512,1280]{1,0:T(8,128)(2,1)}, bf16[512,1280]{1,0:T(8,128)(2,1)}, u32[]{:S(2)}, u32[]{:S(2)}) collective-permute-start(bf16[512,1280]{1,0:T(8,128)(2,1)} %collective-permute-done.1), channel_id=1, source_target_pairs={{4,0},{8,4},{12,8},{16,12},{20,16},{24,20},{28,24},{5,1},{9,5},{13... | collective-permute-start | bytes 3932168 | tf_op jit(solution)/shard_map/ppermute | solution.py:322
  42.2 11.2 %collective-permute-done.8.refs_3_ = bf16[512,1280]{1,0:T(8,128)(2,1)} collective-permute-done((bf16[512,1280]{1,0:T(8,128)(2,1)S(1)}, bf16[512,1280]{1,0:T(8,128)(2,1)}, u32[]{:S(2)}, u32[]{:S(2)}) %collective-permute-start.8) | collective-permute-done | bytes 1310752 | tf_op jit(solution)/shard_map/ppermute | solution.py:294
  54.7 3.5 %collective-permute-start.10 = (bf16[512,1280]{1,0:T(8,128)(2,1)}, bf16[512,1280]{1,0:T(8,128)(2,1)}, u32[]{:S(2)}, u32[]{:S(2)}) collective-permute-start(bf16[512,1280]{1,0:T(8,128)(2,1)} %collective-permute-done.8.refs_3_), channel_id=1, source_target_pairs={{1,2},{2,1},{5,6},{6,5},{9,10},{10,9},{13,14},{14,13},{17,18},{18,... | collective-permute-start | bytes 3932168 | tf_op jit(solution)/shard_map/ppermute | solution.py:294
  60.7 4.8 %collective-permute-done.7 = bf16[528,1280]{1,0:T(8,128)(2,1)S(1)} collective-permute-done((bf16[528,1280]{1,0:T(8,128)(2,1)S(1)}, bf16[528,1280]{1,0:T(8,128)(2,1)S(1)}, u32[]{:S(2)}, u32[]{:S(2)}) %collective-permute-start.7) | collective-permute-done | bytes 1351712 | tf_op jit(solution)/shard_map/ppermute | solution.py:294
  71.7 4.6 %collective-permute-start.6 = (bf16[512,1280]{1,0:T(8,128)(2,1)S(1)}, bf16[512,1280]{1,0:T(8,128)(2,1)}, u32[]{:S(2)}, u32[]{:S(2)}) collective-permute-start(bf16[512,1280]{1,0:T(8,128)(2,1)S(1)} %fusion.2.refs_1_), channel_id=1, source_target_pairs={{1,2},{2,1},{5,6},{6,5},{9,10},{10,9},{13,14},{14,13},{17,18},{18,... | collective-permute-start | bytes 3932168 | tf_op jit(solution)/shard_map/ppermute | solution.py:294
  76.3 11.8 %collective-permute-done.10.refs_7_ = bf16[512,1280]{1,0:T(8,128)(2,1)} collective-permute-done((bf16[512,1280]{1,0:T(8,128)(2,1)}, bf16[512,1280]{1,0:T(8,128)(2,1)}, u32[]{:S(2)}, u32[]{:S(2)}) %collective-permute-start.10) | collective-permute-done | bytes 1310752 | tf_op jit(solution)/shard_map/ppermute | solution.py:294
  88.1 5.2 %collective-permute-done.11.refs_6_ = bf16[512,1280]{1,0:T(8,128)(2,1)} collective-permute-done((bf16[512,1280]{1,0:T(8,128)(2,1)}, bf16[512,1280]{1,0:T(8,128)(2,1)}, u32[]{:S(2)}, u32[]{:S(2)}) %collective-permute-start.11) | collective-permute-done | bytes 1310752 | tf_op jit(solution)/shard_map/ppermute | solution.py:294
  93.3 4.5 %collective-permute-start.14 = (bf16[512,1280]{1,0:T(8,128)(2,1)}, bf16[512,1280]{1,0:T(8,128)(2,1)S(1)}, u32[]{:S(2)}, u32[]{:S(2)}) collective-permute-start(bf16[512,1280]{1,0:T(8,128)(2,1)} %collective-permute-done.10.refs_7_), channel_id=1, source_target_pairs={{1,0},{2,3},{5,4},{6,7},{9,8},{10,11},{13,12},{14,15},{17,16},{18,... | collective-permute-start | bytes 3932168 | tf_op jit(solution)/shard_map/ppermute | solution.py:294
  104.8 4.6 %collective-permute-start.4 = (bf16[512,1280]{1,0:T(8,128)(2,1)}, bf16[512,1280]{1,0:T(8,128)(2,1)}, u32[]{:S(2)}, u32[]{:S(2)}) collective-permute-start(bf16[512,1280]{1,0:T(8,128)(2,1)} %collective-permute-done.3.refs_0_.refs_2_), channel_id=1, source_target_pairs={{1,2},{2,1},{5,6},{6,5},{9,10},{10,9},{13,14},{14,13},{17,18},{18,... | collective-permute-start | bytes 3932168 | tf_op jit(solution)/shard_map/ppermute | solution.py:294
  109.4 4.7 %fusion.11 = (bf16[512,1280]{1,0:T(8,128)(2,1)S(1)}, bf16[512,1280]{1,0:T(8,128)(2,1)}) fusion(bf16[512,1280]{1,0:T(8,128)(2,1)} %collective-permute-done.12, bf16[512,1280]{1,0:T(8,128)(2,1)} %collective-permute-done.1, bf16[512,1280]{1,0:T(8,128)(2,1)} %collective-permute-done.13, f32[1280]{0:T(1024)S(1)} %get-tuple-element.54, ...), kind=kLoop, calls=%fused_computation.19 | loop fusion | flops 17039360 | bytes 7879681 | tf_op jit(solution)/shard_map/convert_element_type | solution.py:258
  118.6 8.6 %collective-permute-done.14.refs_8_ = bf16[512,1280]{1,0:T(8,128)(2,1)S(1)} collective-permute-done((bf16[512,1280]{1,0:T(8,128)(2,1)}, bf16[512,1280]{1,0:T(8,128)(2,1)S(1)}, u32[]{:S(2)}, u32[]{:S(2)}) %collective-permute-start.14) | collective-permute-done | bytes 1310752 | tf_op jit(solution)/shard_map/ppermute | solution.py:294
  128.3 15.5 %project_end.1 = (bf16[5,512,128]{2,1,0:T(8,128)(2,1)S(1)}, bf16[2,5,512,128]{3,2,1,0:T(8,128)(2,1)S(1)}) custom-call(s32[5]{0:T(128)S(1)} %stack.65.info, bf16[512,1280]{1,0:T(8,128)(2,1)} %collective-permute-done.3.refs_0_.refs_2_, bf16[512,1280]{1,0:T(8,128)(2,1)} %collective-permute-done.6.refs_1_.refs_4_, bf16[512,1280]{1,0:T(8,128)(2,1)S(1)} %copy-done.1, ...), custom_call_target="tpu_custom_call" | custom-call | flops 10000000000 | bytes 1 | tf_op jit(solution)/shard_map/project_end/pallas_call | solution.py:101
  148.9 4.6 %collective-permute-start.5 = (bf16[512,1280]{1,0:T(8,128)(2,1)}, bf16[512,1280]{1,0:T(8,128)(2,1)S(1)}, u32[]{:S(2)}, u32[]{:S(2)}) collective-permute-start(bf16[512,1280]{1,0:T(8,128)(2,1)} %collective-permute-done.4.inner), channel_id=1, source_target_pairs={{1,0},{2,3},{5,4},{6,7},{9,8},{10,11},{13,12},{14,15},{17,16},{18,... | collective-permute-start | bytes 3932168 | tf_op jit(solution)/shard_map/ppermute | solution.py:294
  156.6 13.7 %project_raw.1.raw = f32[3,5,512,128]{3,2,1,0:T(8,128)} custom-call(s32[4]{0:T(128)S(1)} %pad_add_fusion.2.info, bf16[16,1280]{1,0:T(8,128)(2,1)S(1)} %collective-permute-done.15.refs_0_, bf16[512,1280]{1,0:T(8,128)(2,1)S(1)} %copy-done.3, bf16[512,1280]{1,0:T(8,128)(2,1)} %collective-permute-done.3.refs_0_.refs_2_, ...), custom_call_target="tpu_custom_call" | custom-call | flops 10000000000 | bytes 1 | tf_op jit(solution)/shard_map/project_raw/pallas_call | solution.py:101
  170.3 8.2 %collective-permute-done.19 = bf16[2,5,512,128]{3,2,1,0:T(8,128)(2,1)} collective-permute-done((bf16[2,5,512,128]{3,2,1,0:T(8,128)(2,1)S(1)}, bf16[2,5,512,128]{3,2,1,0:T(8,128)(2,1)}, u32[]{:S(2)}, u32[]{:S(2)}) %collective-permute-start.19) | collective-permute-done | bytes 1310752 | tf_op jit(solution)/shard_map/ppermute | solution.py:247
  184.4 10.4 %finish.1 = (bf16[5,512,128]{2,1,0:T(8,128)(2,1)S(1)}, bf16[2,5,512,128]{3,2,1,0:T(8,128)(2,1)}) custom-call(s32[2]{0:T(128)S(1)} %pad_add_fusion.1.info, bf16[512,1280]{1,0:T(8,128)(2,1)} %collective-permute-done.4.inner, bf16[512,1280]{1,0:T(8,128)(2,1)S(1)} %collective-permute-done.5.outer, bf16[5120,640]{1,0:T(8,128)(2,1)} %wq.1, bf16[5120,640]{1,0:T(8,128)(2,1)} %wk.1, ...), custom_call_target="tpu_custom_call" | custom-call | flops 10000000000 | bytes 1 | tf_op jit(solution)/shard_map/finish/pallas_call | solution.py:139
  197.4 4.0 %collective-permute-done.21.refs_4_ = bf16[2,5,512,128]{3,2,1,0:T(8,128)(2,1)} collective-permute-done((bf16[2,5,512,128]{3,2,1,0:T(8,128)(2,1)S(1)}, bf16[2,5,512,128]{3,2,1,0:T(8,128)(2,1)}, u32[]{:S(2)}, u32[]{:S(2)}) %collective-permute-start.21) | collective-permute-done | bytes 1310752 | tf_op jit(solution)/shard_map/ppermute | solution.py:344
  201.5 7.1 %attend.2.refs_6_ = bf16[2,512,640]{2,1,0:T(8,128)(2,1)} custom-call(s32[3]{0:T(128)S(1)} %get-tuple-element.67.info, bf16[5,512,128]{2,1,0:T(8,128)(2,1)S(1)} %get-tuple-element.52.refs_0_, bf16[2,5,512,128]{3,2,1,0:T(8,128)(2,1)S(1)} %select_select_fusion.refs_1_, bf16[2,5,512,128]{3,2,1,0:T(8,128)(2,1)} %collective-permute-done.20.refs_2_, ...), custom_call_target="tpu_custom_call" | custom-call | flops 1342177280 | bytes 3932160 | tf_op jit(solution)/shard_map/attend/pallas_call | solution.py:218
  208.6 7.1 %attend.3 = bf16[2,512,640]{2,1,0:T(8,128)(2,1)} custom-call(s32[3]{0:T(128)S(1)} %get-tuple-element.66.info, bf16[5,512,128]{2,1,0:T(8,128)(2,1)S(1)} %copy-done.5, bf16[2,5,512,128]{3,2,1,0:T(8,128)(2,1)S(1)} %select_select_fusion.refs_1_, bf16[2,5,512,128]{3,2,1,0:T(8,128)(2,1)} %collective-permute-done.20.refs_2_, ...), custom_call_target="tpu_custom_call", output_to_operand_aliasing={{}: (7, {})} | custom-call | flops 1342177280 | bytes 3932160 | tf_op jit(solution)/shard_map/attend/pallas_call | solution.py:218
  (71 shorter events, 48.5 us)
Async XLA Ops:
  3.0 17.3 %collective-permute-start = (bf16[512,1280]{1,0:T(8,128)(2,1)}, bf16[512,1280]{1,0:T(8,128)(2,1)S(1)}, u32[]{:S(2)}, u32[]{:S(2)}) collective-permute-start(bf16[512,1280]{1,0:T(8,128)(2,1)} %get-tuple-element.62), channel_id=1, source_target_pairs={{4,0},{8,4},{12,8},{16,12},{20,16},{24,20},{28,24},{5,1},{9,5},{13... | collective-permute-start | bytes 3932168 | tf_op jit(solution)/shard_map/ppermute | solution.py:313
  4.9 31.8 %collective-permute-start.1 = (bf16[512,1280]{1,0:T(8,128)(2,1)}, bf16[512,1280]{1,0:T(8,128)(2,1)}, u32[]{:S(2)}, u32[]{:S(2)}) collective-permute-start(bf16[512,1280]{1,0:T(8,128)(2,1)} %get-tuple-element.62), channel_id=1, source_target_pairs={{1,0},{2,3},{5,4},{6,7},{9,8},{10,11},{13,12},{14,15},{17,16},{18,... | collective-permute-start | bytes 3932168 | tf_op jit(solution)/shard_map/ppermute | solution.py:294
  21.4 32.0 %collective-permute-start.8 = (bf16[512,1280]{1,0:T(8,128)(2,1)S(1)}, bf16[512,1280]{1,0:T(8,128)(2,1)}, u32[]{:S(2)}, u32[]{:S(2)}) collective-permute-start(bf16[512,1280]{1,0:T(8,128)(2,1)S(1)} %fusion.5.refs_2_), channel_id=1, source_target_pairs={{0,1},{3,2},{4,5},{7,6},{8,9},{11,10},{12,13},{15,14},{16,17},{19,... | collective-permute-start | bytes 3932168 | tf_op jit(solution)/shard_map/ppermute | solution.py:294
  22.7 32.0 %collective-permute-start.9 = (bf16[512,1280]{1,0:T(8,128)(2,1)S(1)}, bf16[512,1280]{1,0:T(8,128)(2,1)}, u32[]{:S(2)}, u32[]{:S(2)}) collective-permute-start(bf16[512,1280]{1,0:T(8,128)(2,1)S(1)} %fusion.5.refs_2_), channel_id=1, source_target_pairs={{1,2},{2,1},{5,6},{6,5},{9,10},{10,9},{13,14},{14,13},{17,18},{18,... | collective-permute-start | bytes 3932168 | tf_op jit(solution)/shard_map/ppermute | solution.py:294
  26.2 39.3 %collective-permute-start.7 = (bf16[528,1280]{1,0:T(8,128)(2,1)S(1)}, bf16[528,1280]{1,0:T(8,128)(2,1)S(1)}, u32[]{:S(2)}, u32[]{:S(2)}) collective-permute-start(bf16[528,1280]{1,0:T(8,128)(2,1)S(1)} %pad_maximum_fusion), channel_id=1, source_target_pairs={{1,0},{2,3},{5,4},{6,7},{9,8},{10,11},{13,12},{14,15},{17,16},{18,... | collective-permute-start | bytes 4055048 | tf_op jit(solution)/shard_map/ppermute | solution.py:294
  36.6 32.4 %collective-permute-start.2 = (bf16[512,1280]{1,0:T(8,128)(2,1)S(1)}, bf16[512,1280]{1,0:T(8,128)(2,1)S(1)}, u32[]{:S(2)}, u32[]{:S(2)}) collective-permute-start(bf16[512,1280]{1,0:T(8,128)(2,1)S(1)} %slice_bitcast_fusion), channel_id=1, source_target_pairs={{0,4},{4,8},{8,12},{12,16},{16,20},{20,24},{24,28},{1,5},{5,9},{9,... | collective-permute-start | bytes 3932168 | tf_op jit(solution)/shard_map/ppermute | solution.py:320
  38.5 33.2 %collective-permute-start.12 = (bf16[512,1280]{1,0:T(8,128)(2,1)}, bf16[512,1280]{1,0:T(8,128)(2,1)}, u32[]{:S(2)}, u32[]{:S(2)}) collective-permute-start(bf16[512,1280]{1,0:T(8,128)(2,1)} %collective-permute-done.1), channel_id=1, source_target_pairs={{4,0},{8,4},{12,8},{16,12},{20,16},{24,20},{28,24},{5,1},{9,5},{13... | collective-permute-start | bytes 3932168 | tf_op jit(solution)/shard_map/ppermute | solution.py:322
  54.7 33.4 %collective-permute-start.10 = (bf16[512,1280]{1,0:T(8,128)(2,1)}, bf16[512,1280]{1,0:T(8,128)(2,1)}, u32[]{:S(2)}, u32[]{:S(2)}) collective-permute-start(bf16[512,1280]{1,0:T(8,128)(2,1)} %collective-permute-done.8.refs_3_), channel_id=1, source_target_pairs={{1,2},{2,1},{5,6},{6,5},{9,10},{10,9},{13,14},{14,13},{17,18},{18,... | collective-permute-start | bytes 3932168 | tf_op jit(solution)/shard_map/ppermute | solution.py:294
  58.2 35.1 %collective-permute-start.11 = (bf16[512,1280]{1,0:T(8,128)(2,1)}, bf16[512,1280]{1,0:T(8,128)(2,1)}, u32[]{:S(2)}, u32[]{:S(2)}) collective-permute-start(bf16[512,1280]{1,0:T(8,128)(2,1)} %collective-permute-done.9.refs_5_), channel_id=1, source_target_pairs={{1,0},{2,3},{5,4},{6,7},{9,8},{10,11},{13,12},{14,15},{17,16},{18,... | collective-permute-start | bytes 3932168 | tf_op jit(solution)/shard_map/ppermute | solution.py:294
  67.0 26.3 %collective-permute-start.13 = (bf16[512,1280]{1,0:T(8,128)(2,1)}, bf16[512,1280]{1,0:T(8,128)(2,1)}, u32[]{:S(2)}, u32[]{:S(2)}) collective-permute-start(bf16[512,1280]{1,0:T(8,128)(2,1)} %slice.71), channel_id=1, source_target_pairs={{0,4},{4,8},{8,12},{12,16},{16,20},{20,24},{24,28},{1,5},{5,9},{9,... | collective-permute-start | bytes 3932168 | tf_op jit(solution)/shard_map/ppermute | solution.py:327
  70.2 43.9 %copy-start.2 = (bf16[512,1280]{1,0:T(8,128)(2,1)}, bf16[512,1280]{1,0:T(8,128)(2,1)S(1)}, u32[]{:S(2)}) copy-start(bf16[512,1280]{1,0:T(8,128)(2,1)S(1)} %fusion.2.refs_1_) | copy-start | bytes 3932164
  70.2 31.9 %collective-permute-start.3 = (bf16[512,1280]{1,0:T(8,128)(2,1)S(1)}, bf16[512,1280]{1,0:T(8,128)(2,1)}, u32[]{:S(2)}, u32[]{:S(2)}) collective-permute-start(bf16[512,1280]{1,0:T(8,128)(2,1)S(1)} %fusion.2.refs_1_), channel_id=1, source_target_pairs={{0,1},{3,2},{4,5},{7,6},{8,9},{11,10},{12,13},{15,14},{16,17},{19,... | collective-permute-start | bytes 3932168 | tf_op jit(solution)/shard_map/ppermute | solution.py:294
  71.7 44.5 %collective-permute-start.6 = (bf16[512,1280]{1,0:T(8,128)(2,1)S(1)}, bf16[512,1280]{1,0:T(8,128)(2,1)}, u32[]{:S(2)}, u32[]{:S(2)}) collective-permute-start(bf16[512,1280]{1,0:T(8,128)(2,1)S(1)} %fusion.2.refs_1_), channel_id=1, source_target_pairs={{1,2},{2,1},{5,6},{6,5},{9,10},{10,9},{13,14},{14,13},{17,18},{18,... | collective-permute-start | bytes 3932168 | tf_op jit(solution)/shard_map/ppermute | solution.py:294
  93.3 33.9 %collective-permute-start.14 = (bf16[512,1280]{1,0:T(8,128)(2,1)}, bf16[512,1280]{1,0:T(8,128)(2,1)S(1)}, u32[]{:S(2)}, u32[]{:S(2)}) collective-permute-start(bf16[512,1280]{1,0:T(8,128)(2,1)} %collective-permute-done.10.refs_7_), channel_id=1, source_target_pairs={{1,0},{2,3},{5,4},{6,7},{9,8},{10,11},{13,12},{14,15},{17,16},{18,... | collective-permute-start | bytes 3932168 | tf_op jit(solution)/shard_map/ppermute | solution.py:294
  102.9 41.0 %collective-permute-start.15 = (bf16[16,1280]{1,0:T(8,128)(2,1)S(1)}, bf16[16,1280]{1,0:T(8,128)(2,1)S(1)}, u32[]{:S(2)}, u32[]{:S(2)}) collective-permute-start(bf16[16,1280]{1,0:T(8,128)(2,1)S(1)} %slice.78), channel_id=1, source_target_pairs={{0,4},{4,0},{8,12},{12,8},{16,20},{20,16},{24,28},{28,24},{1,5},{5... | collective-permute-start | bytes 122888 | tf_op jit(solution)/shard_map/ppermute | solution.py:339
  104.8 44.1 %collective-permute-start.4 = (bf16[512,1280]{1,0:T(8,128)(2,1)}, bf16[512,1280]{1,0:T(8,128)(2,1)}, u32[]{:S(2)}, u32[]{:S(2)}) collective-permute-start(bf16[512,1280]{1,0:T(8,128)(2,1)} %collective-permute-done.3.refs_0_.refs_2_), channel_id=1, source_target_pairs={{1,2},{2,1},{5,6},{6,5},{9,10},{10,9},{13,14},{14,13},{17,18},{18,... | collective-permute-start | bytes 3932168 | tf_op jit(solution)/shard_map/ppermute | solution.py:294
  116.2 39.0 %collective-permute-start.16 = (bf16[512,1280]{1,0:T(8,128)(2,1)}, bf16[512,1280]{1,0:T(8,128)(2,1)}, u32[]{:S(2)}, u32[]{:S(2)}) collective-permute-start(bf16[512,1280]{1,0:T(8,128)(2,1)} %collective-permute-done.6.refs_1_.refs_4_), channel_id=1, source_target_pairs={{1,0},{2,3},{5,4},{6,7},{9,8},{10,11},{13,12},{14,15},{17,16},{18,... | collective-permute-start | bytes 3932168 | tf_op jit(solution)/shard_map/ppermute | solution.py:294
  143.9 26.4 %collective-permute-start.17 = (bf16[2,5,512,128]{3,2,1,0:T(8,128)(2,1)S(1)}, bf16[2,5,512,128]{3,2,1,0:T(8,128)(2,1)}, u32[]{:S(2)}, u32[]{:S(2)}) collective-permute-start(bf16[2,5,512,128]{3,2,1,0:T(8,128)(2,1)S(1)} %get-tuple-element.47.refs_3_), channel_id=1, source_target_pairs={{0,24},{1,25},{2,26},{3,27}} | collective-permute-start | bytes 3932168 | tf_op jit(solution)/shard_map/ppermute | solution.py:247
  145.7 24.6 %collective-permute-start.18 = (bf16[2,5,512,128]{3,2,1,0:T(8,128)(2,1)S(1)}, bf16[2,5,512,128]{3,2,1,0:T(8,128)(2,1)}, u32[]{:S(2)}, u32[]{:S(2)}) collective-permute-start(bf16[2,5,512,128]{3,2,1,0:T(8,128)(2,1)S(1)} %get-tuple-element.47.refs_3_), channel_id=1, source_target_pairs={{0,16},{1,17},{2,18},{3,19}} | collective-permute-start | bytes 3932168 | tf_op jit(solution)/shard_map/ppermute | solution.py:247
  147.5 31.1 %collective-permute-start.19 = (bf16[2,5,512,128]{3,2,1,0:T(8,128)(2,1)S(1)}, bf16[2,5,512,128]{3,2,1,0:T(8,128)(2,1)}, u32[]{:S(2)}, u32[]{:S(2)}) collective-permute-start(bf16[2,5,512,128]{3,2,1,0:T(8,128)(2,1)S(1)} %get-tuple-element.47.refs_3_), channel_id=1, source_target_pairs={{0,8},{1,9},{2,10},{3,11}} | collective-permute-start | bytes 3932168 | tf_op jit(solution)/shard_map/ppermute | solution.py:247
  148.9 35.5 %collective-permute-start.5 = (bf16[512,1280]{1,0:T(8,128)(2,1)}, bf16[512,1280]{1,0:T(8,128)(2,1)S(1)}, u32[]{:S(2)}, u32[]{:S(2)}) collective-permute-start(bf16[512,1280]{1,0:T(8,128)(2,1)} %collective-permute-done.4.inner), channel_id=1, source_target_pairs={{1,0},{2,3},{5,4},{6,7},{9,8},{10,11},{13,12},{14,15},{17,16},{18,... | collective-permute-start | bytes 3932168 | tf_op jit(solution)/shard_map/ppermute | solution.py:294
  180.1 21.4 %collective-permute-start.20 = (bf16[2,5,512,128]{3,2,1,0:T(8,128)(2,1)S(1)}, bf16[2,5,512,128]{3,2,1,0:T(8,128)(2,1)}, u32[]{:S(2)}, u32[]{:S(2)}) collective-permute-start(bf16[2,5,512,128]{3,2,1,0:T(8,128)(2,1)S(1)} %select_select_fusion.refs_1_), channel_id=1, source_target_pairs={{0,4},{8,12},{16,20},{24,28},{1,5},{9,13},{17,21},{25,29},{2,6},{1... | collective-permute-start | bytes 3932168 | tf_op jit(solution)/shard_map/ppermute | solution.py:248
  182.4 19.0 %collective-permute-start.21 = (bf16[2,5,512,128]{3,2,1,0:T(8,128)(2,1)S(1)}, bf16[2,5,512,128]{3,2,1,0:T(8,128)(2,1)}, u32[]{:S(2)}, u32[]{:S(2)}) collective-permute-start(bf16[2,5,512,128]{3,2,1,0:T(8,128)(2,1)S(1)} %get-tuple-element.47.refs_3_), channel_id=1, source_target_pairs={{4,8},{8,12},{12,16},{16,20},{20,24},{24,28},{5,9},{9,13},{13,17},... | collective-permute-start | bytes 3932168 | tf_op jit(solution)/shard_map/ppermute | solution.py:344
  195.6 13.0 %collective-permute-start.22 = (bf16[2,5,512,128]{3,2,1,0:T(8,128)(2,1)}, bf16[2,5,512,128]{3,2,1,0:T(8,128)(2,1)}, u32[]{:S(2)}, u32[]{:S(2)}) collective-permute-start(bf16[2,5,512,128]{3,2,1,0:T(8,128)(2,1)} %get-tuple-element.51.refs_4_), channel_id=1, source_target_pairs={{0,4},{1,5},{2,6},{3,7}} | collective-permute-start | bytes 3932168 | tf_op jit(solution)/shard_map/ppermute | solution.py:347
  (11 other events, 69.1 us)

commit v17 on v16

--- a/solution.py
+++ b/solution.py
@@ -340,8 +340,7 @@
     kv1, beside = hold((kv1, beside))
     third2 = send(cross2, OUTWARD)
     anchor = broadcast_first(kv1, "tm")
-    later1, _ = hold((kv1, anchor[0]))
-    shift1 = lax.ppermute(later1, "tm", [(i, i + 1) for i in range(1, count - 1)])
+    shift1 = lax.ppermute(kv1, "tm", [(i, i + 1) for i in range(1, count - 1)])
     raw2 = project([(mixed2,), (inward2, first2), (middle2, second2)], info_raw, weights, after=(beside,), flops=10**10)
     q2, kv2 = finish(raw2, cross2, third2, info_end, weights, gains, 10**10)
     shift2 = lax.ppermute(kv2, "tm", [(0, 1)])

time: 219 us -> 226 us (1.032)
  waiting for transfers between devices: 80.6 us -> 88.7 us
    ppermute x3, waiting for transfers between devices: 8.21 us -> 20.1 us  [broadcast_first(): held = jnp.where(mine == to, lax.ppermute(x, axis, [(0, to)]), held)]
    ppermute x1, waiting for transfers between devices: 4.04 us -> 0.01 us  [per_device(): shift1 = lax.ppermute(kv1, 'tm', [(i, i + 1) for i in range(1, count - 1)])]
  transfers between devices with their start and end apart: 23 -> 23, of which waited for: 13 -> 12; matrix products, arithmetic and copies ran while one was open for 6% -> 5% of each run, Pallas kernels for 22% -> 21%
where the time goes in v17:
time: 226 us; the launch traced here: 224 us
  waiting for transfers between devices  88.7 us (39%)
  starting transfers between devices  62.2 us (28%)
  Pallas kernels  53.9 us (24%)
  other arithmetic  9.76 us (4%)
  local copies, waits for them, and re-layouts  8.79 us (4%)
    ppermute x12, waiting for transfers between devices, send(): return lax.ppermute(x, 'head', pairs)  56.8 us
    ppermute x12, starting transfers between devices, send(): return lax.ppermute(x, 'head', pairs)  39.7 us
    pallas_call x2, Pallas kernels, project(): pl.pallas_call(functools.partial(project_body, pairs, len(after), final),...  29.3 us
    ppermute x3, waiting for transfers between devices, broadcast_first(): held = jnp.where(mine == to, lax.ppermute(x, axis, [(0, to)]), held)  20.1 us
    pallas_call x2, Pallas kernels, attend(): pl.pallas_call(functools.partial(attend_body, 256, (len(anchors), len(opt...  14.2 us
    ppermute x1, waiting for transfers between devices, per_device(): following = lax.ppermute(frames[0], 'tm', downs)  11.8 us
    pallas_call x1, Pallas kernels, finish(): pl.pallas_call(finish_body, grid_spec=pltpu.PrefetchScalarGridSpec(num_sc...  10.4 us
    convert_element_type x3, other arithmetic, mix(): (centre + taps[0] * before + taps[1] * centre + taps[2] * after).astype(B...  6.94 us
  transfers between devices with their start and end apart: 23, of which 12 were waited for; matrix products, arithmetic and copies ran while one was open for 5% of the time, Pallas kernels for 21%

profile of v17, /device:TPU:10, one launch (start us, length us, event | category | flops | bytes accessed | tf_op | source)
XLA Modules:
  0.0 224.0 jit_solution(1409347982138735080)
XLA Ops:
  4.9 3.4 %collective-permute-start.1 = (bf16[512,1280]{1,0:T(8,128)(2,1)}, bf16[512,1280]{1,0:T(8,128)(2,1)}, u32[]{:S(2)}, u32[]{:S(2)}) collective-permute-start(bf16[512,1280]{1,0:T(8,128)(2,1)} %get-tuple-element.60), channel_id=1, source_target_pairs={{1,0},{2,3},{5,4},{6,7},{9,8},{10,11},{13,12},{14,15},{17,16},{18,... | collective-permute-start | bytes 3932168 | tf_op jit(solution)/shard_map/ppermute | solution.py:294
  8.5 11.8 %collective-permute-done = bf16[512,1280]{1,0:T(8,128)(2,1)S(1)} collective-permute-done((bf16[512,1280]{1,0:T(8,128)(2,1)}, bf16[512,1280]{1,0:T(8,128)(2,1)S(1)}, u32[]{:S(2)}, u32[]{:S(2)}) %collective-permute-start) | collective-permute-done | bytes 1310752 | tf_op jit(solution)/shard_map/ppermute | solution.py:313
  22.7 3.5 %collective-permute-start.9 = (bf16[512,1280]{1,0:T(8,128)(2,1)S(1)}, bf16[512,1280]{1,0:T(8,128)(2,1)}, u32[]{:S(2)}, u32[]{:S(2)}) collective-permute-start(bf16[512,1280]{1,0:T(8,128)(2,1)S(1)} %fusion.5.refs_2_), channel_id=1, source_target_pairs={{1,2},{2,1},{5,6},{6,5},{9,10},{10,9},{13,14},{14,13},{17,18},{18,... | collective-permute-start | bytes 3932168 | tf_op jit(solution)/shard_map/ppermute | solution.py:294
  26.2 3.9 %collective-permute-start.7 = (bf16[528,1280]{1,0:T(8,128)(2,1)S(1)}, bf16[528,1280]{1,0:T(8,128)(2,1)S(1)}, u32[]{:S(2)}, u32[]{:S(2)}) collective-permute-start(bf16[528,1280]{1,0:T(8,128)(2,1)S(1)} %pad_maximum_fusion), channel_id=1, source_target_pairs={{1,0},{2,3},{5,4},{6,7},{9,8},{10,11},{13,12},{14,15},{17,16},{18,... | collective-permute-start | bytes 4055048 | tf_op jit(solution)/shard_map/ppermute | solution.py:294
  30.2 6.4 %collective-permute-done.1 = bf16[512,1280]{1,0:T(8,128)(2,1)} collective-permute-done((bf16[512,1280]{1,0:T(8,128)(2,1)}, bf16[512,1280]{1,0:T(8,128)(2,1)}, u32[]{:S(2)}, u32[]{:S(2)}) %collective-permute-start.1) | collective-permute-done | bytes 1310752 | tf_op jit(solution)/shard_map/ppermute | solution.py:294
  38.5 3.6 %collective-permute-start.12 = (bf16[512,1280]{1,0:T(8,128)(2,1)}, bf16[512,1280]{1,0:T(8,128)(2,1)}, u32[]{:S(2)}, u32[]{:S(2)}) collective-permute-start(bf16[512,1280]{1,0:T(8,128)(2,1)} %collective-permute-done.1), channel_id=1, source_target_pairs={{4,0},{8,4},{12,8},{16,12},{20,16},{24,20},{28,24},{5,1},{9,5},{13... | collective-permute-start | bytes 3932168 | tf_op jit(solution)/shard_map/ppermute | solution.py:322
  42.2 11.2 %collective-permute-done.8.refs_3_ = bf16[512,1280]{1,0:T(8,128)(2,1)} collective-permute-done((bf16[512,1280]{1,0:T(8,128)(2,1)S(1)}, bf16[512,1280]{1,0:T(8,128)(2,1)}, u32[]{:S(2)}, u32[]{:S(2)}) %collective-permute-start.8) | collective-permute-done | bytes 1310752 | tf_op jit(solution)/shard_map/ppermute | solution.py:294
  54.7 3.5 %collective-permute-start.10 = (bf16[512,1280]{1,0:T(8,128)(2,1)}, bf16[512,1280]{1,0:T(8,128)(2,1)}, u32[]{:S(2)}, u32[]{:S(2)}) collective-permute-start(bf16[512,1280]{1,0:T(8,128)(2,1)} %collective-permute-done.8.refs_3_), channel_id=1, source_target_pairs={{1,2},{2,1},{5,6},{6,5},{9,10},{10,9},{13,14},{14,13},{17,18},{18,... | collective-permute-start | bytes 3932168 | tf_op jit(solution)/shard_map/ppermute | solution.py:294
  60.7 4.8 %collective-permute-done.7 = bf16[528,1280]{1,0:T(8,128)(2,1)S(1)} collective-permute-done((bf16[528,1280]{1,0:T(8,128)(2,1)S(1)}, bf16[528,1280]{1,0:T(8,128)(2,1)S(1)}, u32[]{:S(2)}, u32[]{:S(2)}) %collective-permute-start.7) | collective-permute-done | bytes 1351712 | tf_op jit(solution)/shard_map/ppermute | solution.py:294
  71.6 4.6 %collective-permute-start.6 = (bf16[512,1280]{1,0:T(8,128)(2,1)S(1)}, bf16[512,1280]{1,0:T(8,128)(2,1)}, u32[]{:S(2)}, u32[]{:S(2)}) collective-permute-start(bf16[512,1280]{1,0:T(8,128)(2,1)S(1)} %fusion.2.refs_1_), channel_id=1, source_target_pairs={{1,2},{2,1},{5,6},{6,5},{9,10},{10,9},{13,14},{14,13},{17,18},{18,... | collective-permute-start | bytes 3932168 | tf_op jit(solution)/shard_map/ppermute | solution.py:294
  76.3 11.9 %collective-permute-done.10.refs_7_ = bf16[512,1280]{1,0:T(8,128)(2,1)} collective-permute-done((bf16[512,1280]{1,0:T(8,128)(2,1)}, bf16[512,1280]{1,0:T(8,128)(2,1)}, u32[]{:S(2)}, u32[]{:S(2)}) %collective-permute-start.10) | collective-permute-done | bytes 1310752 | tf_op jit(solution)/shard_map/ppermute | solution.py:294
  88.1 5.2 %collective-permute-done.11.refs_6_ = bf16[512,1280]{1,0:T(8,128)(2,1)} collective-permute-done((bf16[512,1280]{1,0:T(8,128)(2,1)}, bf16[512,1280]{1,0:T(8,128)(2,1)}, u32[]{:S(2)}, u32[]{:S(2)}) %collective-permute-start.11) | collective-permute-done | bytes 1310752 | tf_op jit(solution)/shard_map/ppermute | solution.py:294
  93.3 4.5 %collective-permute-start.14 = (bf16[512,1280]{1,0:T(8,128)(2,1)}, bf16[512,1280]{1,0:T(8,128)(2,1)S(1)}, u32[]{:S(2)}, u32[]{:S(2)}) collective-permute-start(bf16[512,1280]{1,0:T(8,128)(2,1)} %collective-permute-done.10.refs_7_), channel_id=1, source_target_pairs={{1,0},{2,3},{5,4},{6,7},{9,8},{10,11},{13,12},{14,15},{17,16},{18,... | collective-permute-start | bytes 3932168 | tf_op jit(solution)/shard_map/ppermute | solution.py:294
  98.7 3.3 %collective-permute-done.3.refs_0_.refs_2_ = bf16[512,1280]{1,0:T(8,128)(2,1)} collective-permute-done((bf16[512,1280]{1,0:T(8,128)(2,1)S(1)}, bf16[512,1280]{1,0:T(8,128)(2,1)}, u32[]{:S(2)}, u32[]{:S(2)}) %collective-permute-start.3) | collective-permute-done | bytes 1310752 | tf_op jit(solution)/shard_map/ppermute | solution.py:294
  104.7 4.6 %collective-permute-start.4 = (bf16[512,1280]{1,0:T(8,128)(2,1)}, bf16[512,1280]{1,0:T(8,128)(2,1)}, u32[]{:S(2)}, u32[]{:S(2)}) collective-permute-start(bf16[512,1280]{1,0:T(8,128)(2,1)} %collective-permute-done.3.refs_0_.refs_2_), channel_id=1, source_target_pairs={{1,2},{2,1},{5,6},{6,5},{9,10},{10,9},{13,14},{14,13},{17,18},{18,... | collective-permute-start | bytes 3932168 | tf_op jit(solution)/shard_map/ppermute | solution.py:294
  109.4 4.7 %fusion.11 = (bf16[512,1280]{1,0:T(8,128)(2,1)S(1)}, bf16[512,1280]{1,0:T(8,128)(2,1)}) fusion(bf16[512,1280]{1,0:T(8,128)(2,1)} %collective-permute-done.12, bf16[512,1280]{1,0:T(8,128)(2,1)} %collective-permute-done.1, bf16[512,1280]{1,0:T(8,128)(2,1)} %collective-permute-done.13, f32[1280]{0:T(1024)S(1)} %get-tuple-element.52, ...), kind=kLoop, calls=%fused_computation.19 | loop fusion | flops 17039360 | bytes 7879681 | tf_op jit(solution)/shard_map/convert_element_type | solution.py:258
  118.6 8.6 %collective-permute-done.14.refs_8_ = bf16[512,1280]{1,0:T(8,128)(2,1)S(1)} collective-permute-done((bf16[512,1280]{1,0:T(8,128)(2,1)}, bf16[512,1280]{1,0:T(8,128)(2,1)S(1)}, u32[]{:S(2)}, u32[]{:S(2)}) %collective-permute-start.14) | collective-permute-done | bytes 1310752 | tf_op jit(solution)/shard_map/ppermute | solution.py:294
  128.3 15.5 %project_end.1 = (bf16[5,512,128]{2,1,0:T(8,128)(2,1)S(1)}, bf16[2,5,512,128]{3,2,1,0:T(8,128)(2,1)S(1)}) custom-call(s32[5]{0:T(128)S(1)} %stack.65.info, bf16[512,1280]{1,0:T(8,128)(2,1)} %collective-permute-done.3.refs_0_.refs_2_, bf16[512,1280]{1,0:T(8,128)(2,1)} %collective-permute-done.6.refs_1_.refs_4_, bf16[512,1280]{1,0:T(8,128)(2,1)S(1)} %copy-done.1, ...), custom_call_target="tpu_custom_call" | custom-call | flops 10000000000 | bytes 1 | tf_op jit(solution)/shard_map/project_end/pallas_call | solution.py:101
  148.9 4.4 %collective-permute-start.5 = (bf16[512,1280]{1,0:T(8,128)(2,1)}, bf16[512,1280]{1,0:T(8,128)(2,1)S(1)}, u32[]{:S(2)}, u32[]{:S(2)}) collective-permute-start(bf16[512,1280]{1,0:T(8,128)(2,1)} %collective-permute-done.4.inner), channel_id=1, source_target_pairs={{1,0},{2,3},{5,4},{6,7},{9,8},{10,11},{13,12},{14,15},{17,16},{18,... | collective-permute-start | bytes 3932168 | tf_op jit(solution)/shard_map/ppermute | solution.py:294
  158.7 13.7 %project_raw.1.raw = f32[3,5,512,128]{3,2,1,0:T(8,128)} custom-call(s32[4]{0:T(128)S(1)} %pad_add_fusion.2.info, bf16[16,1280]{1,0:T(8,128)(2,1)S(1)} %collective-permute-done.15.refs_0_, bf16[512,1280]{1,0:T(8,128)(2,1)S(1)} %copy-done.3, bf16[512,1280]{1,0:T(8,128)(2,1)} %collective-permute-done.3.refs_0_.refs_2_, ...), custom_call_target="tpu_custom_call" | custom-call | flops 10000000000 | bytes 1 | tf_op jit(solution)/shard_map/project_raw/pallas_call | solution.py:101
  172.5 20.1 %collective-permute-done.19 = bf16[2,5,512,128]{3,2,1,0:T(8,128)(2,1)} collective-permute-done((bf16[2,5,512,128]{3,2,1,0:T(8,128)(2,1)S(1)}, bf16[2,5,512,128]{3,2,1,0:T(8,128)(2,1)}, u32[]{:S(2)}, u32[]{:S(2)}) %collective-permute-start.19) | collective-permute-done | bytes 1310752 | tf_op jit(solution)/shard_map/ppermute | solution.py:247
  196.5 10.4 %finish.1 = (bf16[5,512,128]{2,1,0:T(8,128)(2,1)S(1)}, bf16[2,5,512,128]{3,2,1,0:T(8,128)(2,1)}) custom-call(s32[2]{0:T(128)S(1)} %pad_add_fusion.1.info, bf16[512,1280]{1,0:T(8,128)(2,1)} %collective-permute-done.4.inner, bf16[512,1280]{1,0:T(8,128)(2,1)S(1)} %collective-permute-done.5.outer, bf16[5120,640]{1,0:T(8,128)(2,1)} %wq.1, bf16[5120,640]{1,0:T(8,128)(2,1)} %wk.1, ...), custom_call_target="tpu_custom_call" | custom-call | flops 10000000000 | bytes 1 | tf_op jit(solution)/shard_map/finish/pallas_call | solution.py:139
  209.5 7.1 %attend.2.refs_6_ = bf16[2,512,640]{2,1,0:T(8,128)(2,1)} custom-call(s32[3]{0:T(128)S(1)} %get-tuple-element.65.info, bf16[5,512,128]{2,1,0:T(8,128)(2,1)S(1)} %get-tuple-element.50.refs_0_, bf16[2,5,512,128]{3,2,1,0:T(8,128)(2,1)S(1)} %select_select_fusion.refs_1_, bf16[2,5,512,128]{3,2,1,0:T(8,128)(2,1)} %collective-permute-done.20.refs_2_, ...), custom_call_target="tpu_custom_call" | custom-call | flops 1342177280 | bytes 3932160 | tf_op jit(solution)/shard_map/attend/pallas_call | solution.py:218
  216.7 7.1 %attend.3 = bf16[2,512,640]{2,1,0:T(8,128)(2,1)} custom-call(s32[3]{0:T(128)S(1)} %get-tuple-element.64.info, bf16[5,512,128]{2,1,0:T(8,128)(2,1)S(1)} %copy-done.5, bf16[2,5,512,128]{3,2,1,0:T(8,128)(2,1)S(1)} %select_select_fusion.refs_1_, bf16[2,5,512,128]{3,2,1,0:T(8,128)(2,1)} %collective-permute-done.20.refs_2_, ...), custom_call_target="tpu_custom_call", output_to_operand_aliasing={{}: (7, {})} | custom-call | flops 1342177280 | bytes 3932160 | tf_op jit(solution)/shard_map/attend/pallas_call | solution.py:218
  (71 shorter events, 45.5 us)
Async XLA Ops:
  3.0 17.3 %collective-permute-start = (bf16[512,1280]{1,0:T(8,128)(2,1)}, bf16[512,1280]{1,0:T(8,128)(2,1)S(1)}, u32[]{:S(2)}, u32[]{:S(2)}) collective-permute-start(bf16[512,1280]{1,0:T(8,128)(2,1)} %get-tuple-element.60), channel_id=1, source_target_pairs={{4,0},{8,4},{12,8},{16,12},{20,16},{24,20},{28,24},{5,1},{9,5},{13... | collective-permute-start | bytes 3932168 | tf_op jit(solution)/shard_map/ppermute | solution.py:313
  4.9 31.8 %collective-permute-start.1 = (bf16[512,1280]{1,0:T(8,128)(2,1)}, bf16[512,1280]{1,0:T(8,128)(2,1)}, u32[]{:S(2)}, u32[]{:S(2)}) collective-permute-start(bf16[512,1280]{1,0:T(8,128)(2,1)} %get-tuple-element.60), channel_id=1, source_target_pairs={{1,0},{2,3},{5,4},{6,7},{9,8},{10,11},{13,12},{14,15},{17,16},{18,... | collective-permute-start | bytes 3932168 | tf_op jit(solution)/shard_map/ppermute | solution.py:294
  21.4 32.0 %collective-permute-start.8 = (bf16[512,1280]{1,0:T(8,128)(2,1)S(1)}, bf16[512,1280]{1,0:T(8,128)(2,1)}, u32[]{:S(2)}, u32[]{:S(2)}) collective-permute-start(bf16[512,1280]{1,0:T(8,128)(2,1)S(1)} %fusion.5.refs_2_), channel_id=1, source_target_pairs={{0,1},{3,2},{4,5},{7,6},{8,9},{11,10},{12,13},{15,14},{16,17},{19,... | collective-permute-start | bytes 3932168 | tf_op jit(solution)/shard_map/ppermute | solution.py:294
  22.7 32.0 %collective-permute-start.9 = (bf16[512,1280]{1,0:T(8,128)(2,1)S(1)}, bf16[512,1280]{1,0:T(8,128)(2,1)}, u32[]{:S(2)}, u32[]{:S(2)}) collective-permute-start(bf16[512,1280]{1,0:T(8,128)(2,1)S(1)} %fusion.5.refs_2_), channel_id=1, source_target_pairs={{1,2},{2,1},{5,6},{6,5},{9,10},{10,9},{13,14},{14,13},{17,18},{18,... | collective-permute-start | bytes 3932168 | tf_op jit(solution)/shard_map/ppermute | solution.py:294
  26.2 39.3 %collective-permute-start.7 = (bf16[528,1280]{1,0:T(8,128)(2,1)S(1)}, bf16[528,1280]{1,0:T(8,128)(2,1)S(1)}, u32[]{:S(2)}, u32[]{:S(2)}) collective-permute-start(bf16[528,1280]{1,0:T(8,128)(2,1)S(1)} %pad_maximum_fusion), channel_id=1, source_target_pairs={{1,0},{2,3},{5,4},{6,7},{9,8},{10,11},{13,12},{14,15},{17,16},{18,... | collective-permute-start | bytes 4055048 | tf_op jit(solution)/shard_map/ppermute | solution.py:294
  36.6 32.4 %collective-permute-start.2 = (bf16[512,1280]{1,0:T(8,128)(2,1)S(1)}, bf16[512,1280]{1,0:T(8,128)(2,1)S(1)}, u32[]{:S(2)}, u32[]{:S(2)}) collective-permute-start(bf16[512,1280]{1,0:T(8,128)(2,1)S(1)} %slice_bitcast_fusion), channel_id=1, source_target_pairs={{0,4},{4,8},{8,12},{12,16},{16,20},{20,24},{24,28},{1,5},{5,9},{9,... | collective-permute-start | bytes 3932168 | tf_op jit(solution)/shard_map/ppermute | solution.py:320
  38.5 33.1 %collective-permute-start.12 = (bf16[512,1280]{1,0:T(8,128)(2,1)}, bf16[512,1280]{1,0:T(8,128)(2,1)}, u32[]{:S(2)}, u32[]{:S(2)}) collective-permute-start(bf16[512,1280]{1,0:T(8,128)(2,1)} %collective-permute-done.1), channel_id=1, source_target_pairs={{4,0},{8,4},{12,8},{16,12},{20,16},{24,20},{28,24},{5,1},{9,5},{13... | collective-permute-start | bytes 3932168 | tf_op jit(solution)/shard_map/ppermute | solution.py:322
  54.7 33.4 %collective-permute-start.10 = (bf16[512,1280]{1,0:T(8,128)(2,1)}, bf16[512,1280]{1,0:T(8,128)(2,1)}, u32[]{:S(2)}, u32[]{:S(2)}) collective-permute-start(bf16[512,1280]{1,0:T(8,128)(2,1)} %collective-permute-done.8.refs_3_), channel_id=1, source_target_pairs={{1,2},{2,1},{5,6},{6,5},{9,10},{10,9},{13,14},{14,13},{17,18},{18,... | collective-permute-start | bytes 3932168 | tf_op jit(solution)/shard_map/ppermute | solution.py:294
  58.2 35.1 %collective-permute-start.11 = (bf16[512,1280]{1,0:T(8,128)(2,1)}, bf16[512,1280]{1,0:T(8,128)(2,1)}, u32[]{:S(2)}, u32[]{:S(2)}) collective-permute-start(bf16[512,1280]{1,0:T(8,128)(2,1)} %collective-permute-done.9.refs_5_), channel_id=1, source_target_pairs={{1,0},{2,3},{5,4},{6,7},{9,8},{10,11},{13,12},{14,15},{17,16},{18,... | collective-permute-start | bytes 3932168 | tf_op jit(solution)/shard_map/ppermute | solution.py:294
  67.0 26.3 %collective-permute-start.13 = (bf16[512,1280]{1,0:T(8,128)(2,1)}, bf16[512,1280]{1,0:T(8,128)(2,1)}, u32[]{:S(2)}, u32[]{:S(2)}) collective-permute-start(bf16[512,1280]{1,0:T(8,128)(2,1)} %slice.71), channel_id=1, source_target_pairs={{0,4},{4,8},{8,12},{12,16},{16,20},{20,24},{24,28},{1,5},{5,9},{9,... | collective-permute-start | bytes 3932168 | tf_op jit(solution)/shard_map/ppermute | solution.py:327
  70.2 43.9 %copy-start.2 = (bf16[512,1280]{1,0:T(8,128)(2,1)}, bf16[512,1280]{1,0:T(8,128)(2,1)S(1)}, u32[]{:S(2)}) copy-start(bf16[512,1280]{1,0:T(8,128)(2,1)S(1)} %fusion.2.refs_1_) | copy-start | bytes 3932164
  70.2 31.9 %collective-permute-start.3 = (bf16[512,1280]{1,0:T(8,128)(2,1)S(1)}, bf16[512,1280]{1,0:T(8,128)(2,1)}, u32[]{:S(2)}, u32[]{:S(2)}) collective-permute-start(bf16[512,1280]{1,0:T(8,128)(2,1)S(1)} %fusion.2.refs_1_), channel_id=1, source_target_pairs={{0,1},{3,2},{4,5},{7,6},{8,9},{11,10},{12,13},{15,14},{16,17},{19,... | collective-permute-start | bytes 3932168 | tf_op jit(solution)/shard_map/ppermute | solution.py:294
  71.6 44.6 %collective-permute-start.6 = (bf16[512,1280]{1,0:T(8,128)(2,1)S(1)}, bf16[512,1280]{1,0:T(8,128)(2,1)}, u32[]{:S(2)}, u32[]{:S(2)}) collective-permute-start(bf16[512,1280]{1,0:T(8,128)(2,1)S(1)} %fusion.2.refs_1_), channel_id=1, source_target_pairs={{1,2},{2,1},{5,6},{6,5},{9,10},{10,9},{13,14},{14,13},{17,18},{18,... | collective-permute-start | bytes 3932168 | tf_op jit(solution)/shard_map/ppermute | solution.py:294
  93.3 33.9 %collective-permute-start.14 = (bf16[512,1280]{1,0:T(8,128)(2,1)}, bf16[512,1280]{1,0:T(8,128)(2,1)S(1)}, u32[]{:S(2)}, u32[]{:S(2)}) collective-permute-start(bf16[512,1280]{1,0:T(8,128)(2,1)} %collective-permute-done.10.refs_7_), channel_id=1, source_target_pairs={{1,0},{2,3},{5,4},{6,7},{9,8},{10,11},{13,12},{14,15},{17,16},{18,... | collective-permute-start | bytes 3932168 | tf_op jit(solution)/shard_map/ppermute | solution.py:294
  102.8 41.0 %collective-permute-start.15 = (bf16[16,1280]{1,0:T(8,128)(2,1)S(1)}, bf16[16,1280]{1,0:T(8,128)(2,1)S(1)}, u32[]{:S(2)}, u32[]{:S(2)}) collective-permute-start(bf16[16,1280]{1,0:T(8,128)(2,1)S(1)} %slice.78), channel_id=1, source_target_pairs={{0,4},{4,0},{8,12},{12,8},{16,20},{20,16},{24,28},{28,24},{1,5},{5... | collective-permute-start | bytes 122888 | tf_op jit(solution)/shard_map/ppermute | solution.py:339
  104.7 44.2 %collective-permute-start.4 = (bf16[512,1280]{1,0:T(8,128)(2,1)}, bf16[512,1280]{1,0:T(8,128)(2,1)}, u32[]{:S(2)}, u32[]{:S(2)}) collective-permute-start(bf16[512,1280]{1,0:T(8,128)(2,1)} %collective-permute-done.3.refs_0_.refs_2_), channel_id=1, source_target_pairs={{1,2},{2,1},{5,6},{6,5},{9,10},{10,9},{13,14},{14,13},{17,18},{18,... | collective-permute-start | bytes 3932168 | tf_op jit(solution)/shard_map/ppermute | solution.py:294
  116.2 39.0 %collective-permute-start.16 = (bf16[512,1280]{1,0:T(8,128)(2,1)}, bf16[512,1280]{1,0:T(8,128)(2,1)}, u32[]{:S(2)}, u32[]{:S(2)}) collective-permute-start(bf16[512,1280]{1,0:T(8,128)(2,1)} %collective-permute-done.6.refs_1_.refs_4_), channel_id=1, source_target_pairs={{1,0},{2,3},{5,4},{6,7},{9,8},{10,11},{13,12},{14,15},{17,16},{18,... | collective-permute-start | bytes 3932168 | tf_op jit(solution)/shard_map/ppermute | solution.py:294
  143.9 28.6 %collective-permute-start.17 = (bf16[2,5,512,128]{3,2,1,0:T(8,128)(2,1)S(1)}, bf16[2,5,512,128]{3,2,1,0:T(8,128)(2,1)}, u32[]{:S(2)}, u32[]{:S(2)}) collective-permute-start(bf16[2,5,512,128]{3,2,1,0:T(8,128)(2,1)S(1)} %get-tuple-element.45.refs_3_), channel_id=1, source_target_pairs={{0,24},{1,25},{2,26},{3,27}} | collective-permute-start | bytes 3932168 | tf_op jit(solution)/shard_map/ppermute | solution.py:247
  145.7 26.8 %collective-permute-start.18 = (bf16[2,5,512,128]{3,2,1,0:T(8,128)(2,1)S(1)}, bf16[2,5,512,128]{3,2,1,0:T(8,128)(2,1)}, u32[]{:S(2)}, u32[]{:S(2)}) collective-permute-start(bf16[2,5,512,128]{3,2,1,0:T(8,128)(2,1)S(1)} %get-tuple-element.45.refs_3_), channel_id=1, source_target_pairs={{0,16},{1,17},{2,18},{3,19}} | collective-permute-start | bytes 3932168 | tf_op jit(solution)/shard_map/ppermute | solution.py:247
  147.5 45.1 %collective-permute-start.19 = (bf16[2,5,512,128]{3,2,1,0:T(8,128)(2,1)S(1)}, bf16[2,5,512,128]{3,2,1,0:T(8,128)(2,1)}, u32[]{:S(2)}, u32[]{:S(2)}) collective-permute-start(bf16[2,5,512,128]{3,2,1,0:T(8,128)(2,1)S(1)} %get-tuple-element.45.refs_3_), channel_id=1, source_target_pairs={{0,8},{1,9},{2,10},{3,11}} | collective-permute-start | bytes 3932168 | tf_op jit(solution)/shard_map/ppermute | solution.py:247
  148.9 47.6 %collective-permute-start.5 = (bf16[512,1280]{1,0:T(8,128)(2,1)}, bf16[512,1280]{1,0:T(8,128)(2,1)S(1)}, u32[]{:S(2)}, u32[]{:S(2)}) collective-permute-start(bf16[512,1280]{1,0:T(8,128)(2,1)} %collective-permute-done.4.inner), channel_id=1, source_target_pairs={{1,0},{2,3},{5,4},{6,7},{9,8},{10,11},{13,12},{14,15},{17,16},{18,... | collective-permute-start | bytes 3932168 | tf_op jit(solution)/shard_map/ppermute | solution.py:294
  155.3 54.3 %collective-permute-start.21 = (bf16[2,5,512,128]{3,2,1,0:T(8,128)(2,1)S(1)}, bf16[2,5,512,128]{3,2,1,0:T(8,128)(2,1)}, u32[]{:S(2)}, u32[]{:S(2)}) collective-permute-start(bf16[2,5,512,128]{3,2,1,0:T(8,128)(2,1)S(1)} %get-tuple-element.45.refs_3_), channel_id=1, source_target_pairs={{4,8},{8,12},{12,16},{16,20},{20,24},{24,28},{5,9},{9,13},{13,17},... | collective-permute-start | bytes 3932168 | tf_op jit(solution)/shard_map/ppermute | solution.py:343
  194.1 15.4 %collective-permute-start.20 = (bf16[2,5,512,128]{3,2,1,0:T(8,128)(2,1)S(1)}, bf16[2,5,512,128]{3,2,1,0:T(8,128)(2,1)}, u32[]{:S(2)}, u32[]{:S(2)}) collective-permute-start(bf16[2,5,512,128]{3,2,1,0:T(8,128)(2,1)S(1)} %select_select_fusion.refs_1_), channel_id=1, source_target_pairs={{0,4},{8,12},{16,20},{24,28},{1,5},{9,13},{17,21},{25,29},{2,6},{1... | collective-permute-start | bytes 3932168 | tf_op jit(solution)/shard_map/ppermute | solution.py:248
  207.7 8.9 %collective-permute-start.22 = (bf16[2,5,512,128]{3,2,1,0:T(8,128)(2,1)}, bf16[2,5,512,128]{3,2,1,0:T(8,128)(2,1)}, u32[]{:S(2)}, u32[]{:S(2)}) collective-permute-start(bf16[2,5,512,128]{3,2,1,0:T(8,128)(2,1)} %get-tuple-element.49.refs_4_), channel_id=1, source_target_pairs={{0,4},{1,5},{2,6},{3,7}} | collective-permute-start | bytes 3932168 | tf_op jit(solution)/shard_map/ppermute | solution.py:346
  (11 other events, 69.1 us)

commit v18 on v15

--- a/solution.py
+++ b/solution.py
@@ -161,17 +161,21 @@
     )(info, inner, outer, *weights, *(g[None] for g in gains), raw)
 
 
-def attend_body(row_block, choices, fresh, info, *refs):
+def attend_body(row_block, asked, choices, fresh, info, *refs):
     refs = list(refs)
-    query = refs.pop(0)
-    options = [[refs.pop(0) for _ in range(n)] for n in choices]
+    queries = [refs.pop(0) for _ in range(asked)]
+    options = [[[refs.pop(0) for _ in range(n)] for n in counts] for counts in choices]
     if not fresh:
         refs.pop(0)
     out, held, sem = refs
     h = pl.program_id(0)
 
-    def fetch(part, source, head):
-        return pltpu.make_async_copy(source.at[:, head], held.at[part, :, head], sem.at[part, head])
+    def fetch(part, pieces, head):
+        row = 0
+        for piece in pieces:
+            place = held.at[part, :, head, pl.ds(row, piece.shape[2])]
+            pltpu.make_async_copy(piece.at[:, head], place, sem.at[part, head]).start()
+            row += piece.shape[2]
 
     @pl.when(h == 0)
     def _():
@@ -181,46 +185,47 @@
 
                     @pl.when(info[2 * part] == j)
                     def _(part=part, source=source, head=head):
-                        fetch(part, source, head).start()
+                        fetch(part, source, head)
 
     for part in range(2):
-        fetch(part, options[part][0], h).wait()
+        pltpu.make_async_copy(held.at[part, :, h], held.at[part, :, h], sem.at[part, h]).wait()
     factor = 1.4426950408889634 / DH**0.5
     key = jnp.concatenate([held[0, 0, h], held[1, 0, h]], axis=0)
     value = jnp.concatenate([held[0, 1, h], held[1, 1, h]], axis=0)
     value = jnp.concatenate([value, jnp.ones_like(value)], axis=1)
-    spans = [pl.ds(row, row_block) for row in range(0, query.shape[1], row_block)]
-
-    def score(span):
-        return lax.dot_general(
-            query[0, span, :], key, (((1,), (1,)), ((), ())), preferred_element_type=F32
-        )
-
-    ahead = score(spans[0])
-    for r, span in enumerate(spans):
+    blocks = [query[0, r : r + row_block, :] for query in queries for r in range(0, query.shape[1], row_block)]
+
+    def score(block):
+        return lax.dot_general(block, key, (((1,), (1,)), ((), ())), preferred_element_type=F32)
+
+    ahead = score(blocks[0])
+    for r in range(len(blocks)):
         scores = ahead
-        if r + 1 < len(spans):
-            ahead = score(spans[r + 1])
+        if r + 1 < len(blocks):
+            ahead = score(blocks[r + 1])
         tops = [scores[:, c : c + DH] for c in range(0, scores.shape[1], DH)]
         top = jnp.max(functools.reduce(jnp.maximum, tops), axis=-1, keepdims=True)
         expo = jnp.exp2((scores - top) * factor).astype(BF16)
         result = jnp.dot(expo, value, preferred_element_type=F32)
-        out[0, span, :] = (result[:, :DH] / result[:, DH:]).astype(BF16)
-
-
-def attend(query, anchors, anchor, options, choice, frame, partly=None):
-    heads, rows, _ = query.shape
-    args = [query, *anchors, *options]
+        out[0, r * row_block : (r + 1) * row_block, :] = (result[:, :DH] / result[:, DH:]).astype(BF16)
+
+
+def attend(queries, anchors, anchor, options, choice, frame, partly=None):
+    heads = queries[0].shape[0]
+    rows = sum(query.shape[1] for query in queries)
+    args = list(queries) + [piece for pieces in (*anchors, *options) for piece in pieces]
+    counts = [[len(pieces) for pieces in group] for group in (anchors, options)]
     aliases = {}
     if partly is not None:
         aliases = {1 + len(args): 0}
         args.append(partly)
     return pl.pallas_call(
-        functools.partial(attend_body, 256, (len(anchors), len(options)), partly is None),
+        functools.partial(attend_body, 256, len(queries), counts, partly is None),
         grid_spec=pltpu.PrefetchScalarGridSpec(
             num_scalar_prefetch=1,
             grid=(heads,),
-            in_specs=[pl.BlockSpec((1, rows, DH), lambda h, info: (h, 0, 0))] + [ANY] * (len(args) - 1),
+            in_specs=[pl.BlockSpec((1, q.shape[1], DH), lambda h, info: (h, 0, 0)) for q in queries]
+            + [ANY] * (len(args) - len(queries)),
             out_specs=pl.BlockSpec((1, rows, DH), lambda h, info: (info[1], 0, h)),
             scratch_shapes=[
                 pltpu.VMEM((2, 2, heads, rows, DH), BF16),
@@ -231,7 +236,7 @@
         input_output_aliases=aliases,
         compiler_params=pltpu.CompilerParams(vmem_limit_bytes=32 * 2**20),
         cost_estimate=pl.CostEstimate(
-            flops=8 * heads * rows * rows * DH,
+            flops=10 * 8 * heads * rows * rows * DH,
             bytes_accessed=2 * heads * rows * DH * 6,
             transcendentals=2 * heads * rows * rows,
         ),
@@ -340,17 +345,19 @@
     kv1, beside = hold((kv1, beside))
     third2 = send(cross2, OUTWARD)
     anchor = broadcast_first(kv1, "tm")
-    later1, _ = hold((kv1, anchor[0]))
-    shift1 = lax.ppermute(later1, "tm", [(i, i + 1) for i in range(1, count - 1)])
+    half = kv1.shape[2] // 2
+    halves = hold((kv1[:, :, :half], kv1[:, :, half:], anchor[0]))
+    shift1 = [lax.ppermute(x, "tm", [(i, i + 1) for i in range(1, count - 1)]) for x in halves[:2]]
     raw2 = project([(mixed2,), (inward2, first2), (middle2, second2)], info_raw, weights, after=(beside,), flops=10**10)
-    q2, kv2 = finish(raw2, cross2, third2, info_end, weights, gains, 10**10)
+    q2, kv2 = finish(raw2, cross2, third2, info_end, weights, gains, 10**11)
     shift2 = lax.ppermute(kv2, "tm", [(0, 1)])
-    anchor, shift1 = hold((anchor, shift1))
+    anchor, shift1[0] = hold((anchor, shift1[0]))
+    anchors = [[x] for x in anchor]
     late = jnp.where(start, 0, 1)
     odd = pos % 2
-    result = attend(q1, anchor, odd, [kv1, kv2], late, late)
+    result = attend([q1], anchors, odd, [[kv1], [kv2]], late, late)
     choice = jnp.minimum(pos, 1) + (pos == 1)
-    return attend(q2, anchor, odd, [kv1, shift1, shift2], choice, 1 - late, result)
+    return attend([q2], anchors, odd, [[kv1], shift1, [shift2]], choice, 1 - late, result)
 
 
 def solution(mesh):

time: 218 us -> 214 us (0.982)
  the two profiles are of different devices: /device:TPU:6 before, /device:TPU:10 now
where the time goes in v18:
time: 214 us; the launch traced here: 210 us
  waiting for transfers between devices  83.4 us (39%)
  starting transfers between devices  59.9 us (28%)
  Pallas kernels  51.4 us (24%)
  other arithmetic  8.27 us (4%)
  local copies, waits for them, and re-layouts  6.81 us (3%)
    ppermute x12, waiting for transfers between devices, send(): return lax.ppermute(x, 'head', pairs)  68.1 us
    ppermute x12, starting transfers between devices, send(): return lax.ppermute(x, 'head', pairs)  39.8 us
    pallas_call x2, Pallas kernels, project(): pl.pallas_call(functools.partial(project_body, pairs, len(after), final),...  29.4 us
    pallas_call x2, Pallas kernels, attend(): pl.pallas_call(functools.partial(attend_body, 256, len(queries), counts,...  13.7 us
    ppermute x1, waiting for transfers between devices, per_device(): following = lax.ppermute(frames[0], 'tm', downs)  11.8 us
    pallas_call x1, Pallas kernels, finish(): pl.pallas_call(finish_body, grid_spec=pltpu.PrefetchScalarGridSpec(num_sc...  8.23 us
    convert_element_type x3, other arithmetic, mix(): (centre + taps[0] * before + taps[1] * centre + taps[2] * after).astype(B...  6.76 us
  transfers between devices with their start and end apart: 24, of which 13 were waited for; matrix products, arithmetic and copies ran while one was open for 5% of the time, Pallas kernels for 21%

profile of v18, /device:TPU:10, one launch (start us, length us, event | category | flops | bytes accessed | tf_op | source)
XLA Modules:
  0.0 210.4 jit_solution(3006268311942518999)
XLA Ops:
  8.5 11.8 %collective-permute-done = bf16[512,1280]{1,0:T(8,128)(2,1)S(1)} collective-permute-done((bf16[512,1280]{1,0:T(8,128)(2,1)}, bf16[512,1280]{1,0:T(8,128)(2,1)S(1)}, u32[]{:S(2)}, u32[]{:S(2)}) %collective-permute-start) | collective-permute-done | bytes 1310752 | tf_op jit(solution)/shard_map/ppermute | solution.py:318
  22.7 3.5 %collective-permute-start.9 = (bf16[512,1280]{1,0:T(8,128)(2,1)S(1)}, bf16[512,1280]{1,0:T(8,128)(2,1)}, u32[]{:S(2)}, u32[]{:S(2)}) collective-permute-start(bf16[512,1280]{1,0:T(8,128)(2,1)S(1)} %fusion.5.refs_2_), channel_id=1, source_target_pairs={{1,2},{2,1},{5,6},{6,5},{9,10},{10,9},{13,14},{14,13},{17,18},{18,... | collective-permute-start | bytes 3932168 | tf_op jit(solution)/shard_map/ppermute | solution.py:299
  26.2 3.9 %collective-permute-start.7 = (bf16[528,1280]{1,0:T(8,128)(2,1)S(1)}, bf16[528,1280]{1,0:T(8,128)(2,1)S(1)}, u32[]{:S(2)}, u32[]{:S(2)}) collective-permute-start(bf16[528,1280]{1,0:T(8,128)(2,1)S(1)} %pad_maximum_fusion), channel_id=1, source_target_pairs={{1,0},{2,3},{5,4},{6,7},{9,8},{10,11},{13,12},{14,15},{17,16},{18,... | collective-permute-start | bytes 4055048 | tf_op jit(solution)/shard_map/ppermute | solution.py:299
  30.2 6.4 %collective-permute-done.1 = bf16[512,1280]{1,0:T(8,128)(2,1)} collective-permute-done((bf16[512,1280]{1,0:T(8,128)(2,1)}, bf16[512,1280]{1,0:T(8,128)(2,1)}, u32[]{:S(2)}, u32[]{:S(2)}) %collective-permute-start.1) | collective-permute-done | bytes 1310752 | tf_op jit(solution)/shard_map/ppermute | solution.py:299
  38.5 3.6 %collective-permute-start.12 = (bf16[512,1280]{1,0:T(8,128)(2,1)}, bf16[512,1280]{1,0:T(8,128)(2,1)}, u32[]{:S(2)}, u32[]{:S(2)}) collective-permute-start(bf16[512,1280]{1,0:T(8,128)(2,1)} %collective-permute-done.1), channel_id=1, source_target_pairs={{4,0},{8,4},{12,8},{16,12},{20,16},{24,20},{28,24},{5,1},{9,5},{13... | collective-permute-start | bytes 3932168 | tf_op jit(solution)/shard_map/ppermute | solution.py:327
  42.2 11.2 %collective-permute-done.8.refs_3_ = bf16[512,1280]{1,0:T(8,128)(2,1)} collective-permute-done((bf16[512,1280]{1,0:T(8,128)(2,1)S(1)}, bf16[512,1280]{1,0:T(8,128)(2,1)}, u32[]{:S(2)}, u32[]{:S(2)}) %collective-permute-start.8) | collective-permute-done | bytes 1310752 | tf_op jit(solution)/shard_map/ppermute | solution.py:299
  54.7 3.5 %collective-permute-start.10 = (bf16[512,1280]{1,0:T(8,128)(2,1)}, bf16[512,1280]{1,0:T(8,128)(2,1)}, u32[]{:S(2)}, u32[]{:S(2)}) collective-permute-start(bf16[512,1280]{1,0:T(8,128)(2,1)} %collective-permute-done.8.refs_3_), channel_id=1, source_target_pairs={{1,2},{2,1},{5,6},{6,5},{9,10},{10,9},{13,14},{14,13},{17,18},{18,... | collective-permute-start | bytes 3932168 | tf_op jit(solution)/shard_map/ppermute | solution.py:299
  60.5 4.9 %collective-permute-done.7 = bf16[528,1280]{1,0:T(8,128)(2,1)S(1)} collective-permute-done((bf16[528,1280]{1,0:T(8,128)(2,1)S(1)}, bf16[528,1280]{1,0:T(8,128)(2,1)S(1)}, u32[]{:S(2)}, u32[]{:S(2)}) %collective-permute-start.7) | collective-permute-done | bytes 1351712 | tf_op jit(solution)/shard_map/ppermute | solution.py:299
  71.8 4.6 %collective-permute-start.6 = (bf16[512,1280]{1,0:T(8,128)(2,1)S(1)}, bf16[512,1280]{1,0:T(8,128)(2,1)S(1)}, u32[]{:S(2)}, u32[]{:S(2)}) collective-permute-start(bf16[512,1280]{1,0:T(8,128)(2,1)S(1)} %fusion.2.refs_1_), channel_id=1, source_target_pairs={{1,2},{2,1},{5,6},{6,5},{9,10},{10,9},{13,14},{14,13},{17,18},{18,... | collective-permute-start | bytes 3932168 | tf_op jit(solution)/shard_map/ppermute | solution.py:299
  76.4 11.7 %collective-permute-done.10.refs_7_ = bf16[512,1280]{1,0:T(8,128)(2,1)} collective-permute-done((bf16[512,1280]{1,0:T(8,128)(2,1)}, bf16[512,1280]{1,0:T(8,128)(2,1)}, u32[]{:S(2)}, u32[]{:S(2)}) %collective-permute-start.10) | collective-permute-done | bytes 1310752 | tf_op jit(solution)/shard_map/ppermute | solution.py:299
  88.1 5.2 %collective-permute-done.11.refs_6_ = bf16[512,1280]{1,0:T(8,128)(2,1)} collective-permute-done((bf16[512,1280]{1,0:T(8,128)(2,1)}, bf16[512,1280]{1,0:T(8,128)(2,1)}, u32[]{:S(2)}, u32[]{:S(2)}) %collective-permute-start.11) | collective-permute-done | bytes 1310752 | tf_op jit(solution)/shard_map/ppermute | solution.py:299
  93.3 4.5 %collective-permute-start.14 = (bf16[512,1280]{1,0:T(8,128)(2,1)}, bf16[512,1280]{1,0:T(8,128)(2,1)S(1)}, u32[]{:S(2)}, u32[]{:S(2)}) collective-permute-start(bf16[512,1280]{1,0:T(8,128)(2,1)} %collective-permute-done.10.refs_7_), channel_id=1, source_target_pairs={{1,0},{2,3},{5,4},{6,7},{9,8},{10,11},{13,12},{14,15},{17,16},{18,... | collective-permute-start | bytes 3932168 | tf_op jit(solution)/shard_map/ppermute | solution.py:299
  104.7 4.6 %collective-permute-start.4 = (bf16[512,1280]{1,0:T(8,128)(2,1)}, bf16[512,1280]{1,0:T(8,128)(2,1)S(1)}, u32[]{:S(2)}, u32[]{:S(2)}) collective-permute-start(bf16[512,1280]{1,0:T(8,128)(2,1)} %collective-permute-done.3.refs_0_.refs_2_), channel_id=1, source_target_pairs={{1,2},{2,1},{5,6},{6,5},{9,10},{10,9},{13,14},{14,13},{17,18},{18,... | collective-permute-start | bytes 3932168 | tf_op jit(solution)/shard_map/ppermute | solution.py:299
  109.3 4.5 %fusion.11 = (bf16[512,1280]{1,0:T(8,128)(2,1)S(1)}, bf16[512,1280]{1,0:T(8,128)(2,1)}) fusion(bf16[512,1280]{1,0:T(8,128)(2,1)} %collective-permute-done.12, bf16[512,1280]{1,0:T(8,128)(2,1)} %collective-permute-done.1, bf16[512,1280]{1,0:T(8,128)(2,1)} %collective-permute-done.13, f32[1280]{0:T(1024)S(1)} %get-tuple-element.56, ...), kind=kLoop, calls=%fused_computation.19 | loop fusion | flops 17039360 | bytes 7879681 | tf_op jit(solution)/shard_map/convert_element_type | solution.py:263
  118.5 8.7 %collective-permute-done.14.refs_8_ = bf16[512,1280]{1,0:T(8,128)(2,1)S(1)} collective-permute-done((bf16[512,1280]{1,0:T(8,128)(2,1)}, bf16[512,1280]{1,0:T(8,128)(2,1)S(1)}, u32[]{:S(2)}, u32[]{:S(2)}) %collective-permute-start.14) | collective-permute-done | bytes 1310752 | tf_op jit(solution)/shard_map/ppermute | solution.py:299
  128.3 15.5 %project_end.1 = (bf16[5,512,128]{2,1,0:T(8,128)(2,1)S(1)}, bf16[2,5,512,128]{3,2,1,0:T(8,128)(2,1)S(1)}) custom-call(s32[5]{0:T(128)S(1)} %stack.65.info, bf16[512,1280]{1,0:T(8,128)(2,1)} %collective-permute-done.3.refs_0_.refs_2_, bf16[512,1280]{1,0:T(8,128)(2,1)S(1)} %collective-permute-done.6.refs_1_.refs_4_, bf16[512,1280]{1,0:T(8,128)(2,1)S(1)} %fusion.5.refs_2_, ...), custom_call_target="tpu_custom_call" | custom-call | flops 10000000000 | bytes 1 | tf_op jit(solution)/shard_map/project_end/pallas_call | solution.py:101
  146.8 4.6 %collective-permute-start.5 = (bf16[512,1280]{1,0:T(8,128)(2,1)S(1)}, bf16[512,1280]{1,0:T(8,128)(2,1)S(1)}, u32[]{:S(2)}, u32[]{:S(2)}) collective-permute-start(bf16[512,1280]{1,0:T(8,128)(2,1)S(1)} %collective-permute-done.4.inner), channel_id=1, source_target_pairs={{1,0},{2,3},{5,4},{6,7},{9,8},{10,11},{13,12},{14,15},{17,16},{18,... | collective-permute-start | bytes 3932168 | tf_op jit(solution)/shard_map/ppermute | solution.py:299
  151.5 3.7 %collective-permute-done.16.refs_5_ = bf16[512,1280]{1,0:T(8,128)(2,1)} collective-permute-done((bf16[512,1280]{1,0:T(8,128)(2,1)S(1)}, bf16[512,1280]{1,0:T(8,128)(2,1)}, u32[]{:S(2)}, u32[]{:S(2)}) %collective-permute-start.16) | collective-permute-done | bytes 1310752 | tf_op jit(solution)/shard_map/ppermute | solution.py:299
  155.1 13.9 %project_raw.1.raw = f32[3,5,512,128]{3,2,1,0:T(8,128)} custom-call(s32[4]{0:T(128)S(1)} %pad_add_fusion.2.info, bf16[16,1280]{1,0:T(8,128)(2,1)S(1)} %collective-permute-done.15.refs_0_, bf16[512,1280]{1,0:T(8,128)(2,1)S(1)} %fusion.2.refs_1_, bf16[512,1280]{1,0:T(8,128)(2,1)} %collective-permute-done.3.refs_0_.refs_2_, ...), custom_call_target="tpu_custom_call" | custom-call | flops 10000000000 | bytes 1 | tf_op jit(solution)/shard_map/project_raw/pallas_call | solution.py:101
  172.6 9.3 %collective-permute-done.5.outer = bf16[512,1280]{1,0:T(8,128)(2,1)S(1)} collective-permute-done((bf16[512,1280]{1,0:T(8,128)(2,1)S(1)}, bf16[512,1280]{1,0:T(8,128)(2,1)S(1)}, u32[]{:S(2)}, u32[]{:S(2)}) %collective-permute-start.5) | collective-permute-done | bytes 1310752 | tf_op jit(solution)/shard_map/ppermute | solution.py:299
  182.0 8.2 %finish.1 = (bf16[5,512,128]{2,1,0:T(8,128)(2,1)S(1)}, bf16[2,5,512,128]{3,2,1,0:T(8,128)(2,1)S(1)}) custom-call(s32[2]{0:T(128)S(1)} %pad_add_fusion.1.info, bf16[512,1280]{1,0:T(8,128)(2,1)S(1)} %collective-permute-done.4.inner, bf16[512,1280]{1,0:T(8,128)(2,1)S(1)} %collective-permute-done.5.outer, bf16[5120,640]{1,0:T(8,128)(2,1)} %wq.1, ...), custom_call_target="tpu_custom_call" | custom-call | flops 99999997952 | bytes 1 | tf_op jit(solution)/shard_map/finish/pallas_call | solution.py:139
  193.0 6.5 %attend.2.refs_7_ = bf16[2,512,640]{2,1,0:T(8,128)(2,1)} custom-call(s32[3]{0:T(128)S(1)} %get-tuple-element.71.info, bf16[5,512,128]{2,1,0:T(8,128)(2,1)S(1)} %get-tuple-element.54.refs_0_, bf16[2,5,512,128]{3,2,1,0:T(8,128)(2,1)S(1)} %select_select_fusion.refs_1_, bf16[2,5,512,128]{3,2,1,0:T(8,128)(2,1)S(1)} %collective-permute-done.20.refs_2_, ...), custom_call_target="tpu_custom_call" | custom-call | flops 13421772800 | bytes 3932160 | tf_op jit(solution)/shard_map/attend/pallas_call | solution.py:222
  199.4 3.5 %collective-permute-done.22.refs_5_ = bf16[2,5,256,128]{3,2,1,0:T(8,128)(2,1)S(1)} collective-permute-done((bf16[2,5,256,128]{3,2,1,0:T(8,128)(2,1)S(1)}, bf16[2,5,256,128]{3,2,1,0:T(8,128)(2,1)S(1)}, u32[]{:S(2)}, u32[]{:S(2)}) %collective-permute-start.22) | collective-permute-done | bytes 655392 | tf_op jit(solution)/shard_map/ppermute | solution.py:350
  202.9 7.3 %attend.3 = bf16[2,512,640]{2,1,0:T(8,128)(2,1)} custom-call(s32[3]{0:T(128)S(1)} %get-tuple-element.70.info, bf16[5,512,128]{2,1,0:T(8,128)(2,1)S(1)} %get-tuple-element.46.refs_0_, bf16[2,5,512,128]{3,2,1,0:T(8,128)(2,1)S(1)} %select_select_fusion.refs_1_, ...), custom_call_target="tpu_custom_call", output_to_operand_aliasing={{}: (8, {})} | custom-call | flops 13421772800 | bytes 3932160 | tf_op jit(solution)/shard_map/attend/pallas_call | solution.py:222
  (66 shorter events, 44.6 us)
Async XLA Ops:
  3.0 17.3 %collective-permute-start = (bf16[512,1280]{1,0:T(8,128)(2,1)}, bf16[512,1280]{1,0:T(8,128)(2,1)S(1)}, u32[]{:S(2)}, u32[]{:S(2)}) collective-permute-start(bf16[512,1280]{1,0:T(8,128)(2,1)} %get-tuple-element.64), channel_id=1, source_target_pairs={{4,0},{8,4},{12,8},{16,12},{20,16},{24,20},{28,24},{5,1},{9,5},{13... | collective-permute-start | bytes 3932168 | tf_op jit(solution)/shard_map/ppermute | solution.py:318
  4.9 31.8 %collective-permute-start.1 = (bf16[512,1280]{1,0:T(8,128)(2,1)}, bf16[512,1280]{1,0:T(8,128)(2,1)}, u32[]{:S(2)}, u32[]{:S(2)}) collective-permute-start(bf16[512,1280]{1,0:T(8,128)(2,1)} %get-tuple-element.64), channel_id=1, source_target_pairs={{1,0},{2,3},{5,4},{6,7},{9,8},{10,11},{13,12},{14,15},{17,16},{18,... | collective-permute-start | bytes 3932168 | tf_op jit(solution)/shard_map/ppermute | solution.py:299
  21.4 32.0 %collective-permute-start.8 = (bf16[512,1280]{1,0:T(8,128)(2,1)S(1)}, bf16[512,1280]{1,0:T(8,128)(2,1)}, u32[]{:S(2)}, u32[]{:S(2)}) collective-permute-start(bf16[512,1280]{1,0:T(8,128)(2,1)S(1)} %fusion.5.refs_2_), channel_id=1, source_target_pairs={{0,1},{3,2},{4,5},{7,6},{8,9},{11,10},{12,13},{15,14},{16,17},{19,... | collective-permute-start | bytes 3932168 | tf_op jit(solution)/shard_map/ppermute | solution.py:299
  22.7 32.0 %collective-permute-start.9 = (bf16[512,1280]{1,0:T(8,128)(2,1)S(1)}, bf16[512,1280]{1,0:T(8,128)(2,1)}, u32[]{:S(2)}, u32[]{:S(2)}) collective-permute-start(bf16[512,1280]{1,0:T(8,128)(2,1)S(1)} %fusion.5.refs_2_), channel_id=1, source_target_pairs={{1,2},{2,1},{5,6},{6,5},{9,10},{10,9},{13,14},{14,13},{17,18},{18,... | collective-permute-start | bytes 3932168 | tf_op jit(solution)/shard_map/ppermute | solution.py:299
  26.2 39.3 %collective-permute-start.7 = (bf16[528,1280]{1,0:T(8,128)(2,1)S(1)}, bf16[528,1280]{1,0:T(8,128)(2,1)S(1)}, u32[]{:S(2)}, u32[]{:S(2)}) collective-permute-start(bf16[528,1280]{1,0:T(8,128)(2,1)S(1)} %pad_maximum_fusion), channel_id=1, source_target_pairs={{1,0},{2,3},{5,4},{6,7},{9,8},{10,11},{13,12},{14,15},{17,16},{18,... | collective-permute-start | bytes 4055048 | tf_op jit(solution)/shard_map/ppermute | solution.py:299
  36.6 32.4 %collective-permute-start.2 = (bf16[512,1280]{1,0:T(8,128)(2,1)S(1)}, bf16[512,1280]{1,0:T(8,128)(2,1)S(1)}, u32[]{:S(2)}, u32[]{:S(2)}) collective-permute-start(bf16[512,1280]{1,0:T(8,128)(2,1)S(1)} %slice_bitcast_fusion), channel_id=1, source_target_pairs={{0,4},{4,8},{8,12},{12,16},{16,20},{20,24},{24,28},{1,5},{5,9},{9,... | collective-permute-start | bytes 3932168 | tf_op jit(solution)/shard_map/ppermute | solution.py:325
  38.5 33.3 %collective-permute-start.12 = (bf16[512,1280]{1,0:T(8,128)(2,1)}, bf16[512,1280]{1,0:T(8,128)(2,1)}, u32[]{:S(2)}, u32[]{:S(2)}) collective-permute-start(bf16[512,1280]{1,0:T(8,128)(2,1)} %collective-permute-done.1), channel_id=1, source_target_pairs={{4,0},{8,4},{12,8},{16,12},{20,16},{24,20},{28,24},{5,1},{9,5},{13... | collective-permute-start | bytes 3932168 | tf_op jit(solution)/shard_map/ppermute | solution.py:327
  54.7 33.4 %collective-permute-start.10 = (bf16[512,1280]{1,0:T(8,128)(2,1)}, bf16[512,1280]{1,0:T(8,128)(2,1)}, u32[]{:S(2)}, u32[]{:S(2)}) collective-permute-start(bf16[512,1280]{1,0:T(8,128)(2,1)} %collective-permute-done.8.refs_3_), channel_id=1, source_target_pairs={{1,2},{2,1},{5,6},{6,5},{9,10},{10,9},{13,14},{14,13},{17,18},{18,... | collective-permute-start | bytes 3932168 | tf_op jit(solution)/shard_map/ppermute | solution.py:299
  58.2 35.1 %collective-permute-start.11 = (bf16[512,1280]{1,0:T(8,128)(2,1)}, bf16[512,1280]{1,0:T(8,128)(2,1)}, u32[]{:S(2)}, u32[]{:S(2)}) collective-permute-start(bf16[512,1280]{1,0:T(8,128)(2,1)} %collective-permute-done.9.refs_5_), channel_id=1, source_target_pairs={{1,0},{2,3},{5,4},{6,7},{9,8},{10,11},{13,12},{14,15},{17,16},{18,... | collective-permute-start | bytes 3932168 | tf_op jit(solution)/shard_map/ppermute | solution.py:299
  67.0 26.3 %collective-permute-start.13 = (bf16[512,1280]{1,0:T(8,128)(2,1)}, bf16[512,1280]{1,0:T(8,128)(2,1)}, u32[]{:S(2)}, u32[]{:S(2)}) collective-permute-start(bf16[512,1280]{1,0:T(8,128)(2,1)} %slice.79), channel_id=1, source_target_pairs={{0,4},{4,8},{8,12},{12,16},{16,20},{20,24},{24,28},{1,5},{5,9},{9,... | collective-permute-start | bytes 3932168 | tf_op jit(solution)/shard_map/ppermute | solution.py:332
  70.2 31.9 %collective-permute-start.3 = (bf16[512,1280]{1,0:T(8,128)(2,1)S(1)}, bf16[512,1280]{1,0:T(8,128)(2,1)}, u32[]{:S(2)}, u32[]{:S(2)}) collective-permute-start(bf16[512,1280]{1,0:T(8,128)(2,1)S(1)} %fusion.2.refs_1_), channel_id=1, source_target_pairs={{0,1},{3,2},{4,5},{7,6},{8,9},{11,10},{12,13},{15,14},{16,17},{19,... | collective-permute-start | bytes 3932168 | tf_op jit(solution)/shard_map/ppermute | solution.py:299
  71.8 44.3 %collective-permute-start.6 = (bf16[512,1280]{1,0:T(8,128)(2,1)S(1)}, bf16[512,1280]{1,0:T(8,128)(2,1)S(1)}, u32[]{:S(2)}, u32[]{:S(2)}) collective-permute-start(bf16[512,1280]{1,0:T(8,128)(2,1)S(1)} %fusion.2.refs_1_), channel_id=1, source_target_pairs={{1,2},{2,1},{5,6},{6,5},{9,10},{10,9},{13,14},{14,13},{17,18},{18,... | collective-permute-start | bytes 3932168 | tf_op jit(solution)/shard_map/ppermute | solution.py:299
  93.3 33.9 %collective-permute-start.14 = (bf16[512,1280]{1,0:T(8,128)(2,1)}, bf16[512,1280]{1,0:T(8,128)(2,1)S(1)}, u32[]{:S(2)}, u32[]{:S(2)}) collective-permute-start(bf16[512,1280]{1,0:T(8,128)(2,1)} %collective-permute-done.10.refs_7_), channel_id=1, source_target_pairs={{1,0},{2,3},{5,4},{6,7},{9,8},{10,11},{13,12},{14,15},{17,16},{18,... | collective-permute-start | bytes 3932168 | tf_op jit(solution)/shard_map/ppermute | solution.py:299
  102.9 41.0 %collective-permute-start.15 = (bf16[16,1280]{1,0:T(8,128)(2,1)S(1)}, bf16[16,1280]{1,0:T(8,128)(2,1)S(1)}, u32[]{:S(2)}, u32[]{:S(2)}) collective-permute-start(bf16[16,1280]{1,0:T(8,128)(2,1)S(1)} %slice.86), channel_id=1, source_target_pairs={{0,4},{4,0},{8,12},{12,8},{16,20},{20,16},{24,28},{28,24},{1,5},{5... | collective-permute-start | bytes 122888 | tf_op jit(solution)/shard_map/ppermute | solution.py:344
  104.7 42.1 %collective-permute-start.4 = (bf16[512,1280]{1,0:T(8,128)(2,1)}, bf16[512,1280]{1,0:T(8,128)(2,1)S(1)}, u32[]{:S(2)}, u32[]{:S(2)}) collective-permute-start(bf16[512,1280]{1,0:T(8,128)(2,1)} %collective-permute-done.3.refs_0_.refs_2_), channel_id=1, source_target_pairs={{1,2},{2,1},{5,6},{6,5},{9,10},{10,9},{13,14},{14,13},{17,18},{18,... | collective-permute-start | bytes 3932168 | tf_op jit(solution)/shard_map/ppermute | solution.py:299
  116.1 39.0 %collective-permute-start.16 = (bf16[512,1280]{1,0:T(8,128)(2,1)S(1)}, bf16[512,1280]{1,0:T(8,128)(2,1)}, u32[]{:S(2)}, u32[]{:S(2)}) collective-permute-start(bf16[512,1280]{1,0:T(8,128)(2,1)S(1)} %collective-permute-done.6.refs_1_.refs_4_), channel_id=1, source_target_pairs={{1,0},{2,3},{5,4},{6,7},{9,8},{10,11},{13,12},{14,15},{17,16},{18,... | collective-permute-start | bytes 3932168 | tf_op jit(solution)/shard_map/ppermute | solution.py:299
  143.9 25.1 %collective-permute-start.17 = (bf16[2,5,512,128]{3,2,1,0:T(8,128)(2,1)S(1)}, bf16[2,5,512,128]{3,2,1,0:T(8,128)(2,1)S(1)}, u32[]{:S(2)}, u32[]{:S(2)}) collective-permute-start(bf16[2,5,512,128]{3,2,1,0:T(8,128)(2,1)S(1)} %get-tuple-element.47.refs_3_), channel_id=1, source_target_pairs={{0,8},{1,9},{2,10},{3,11}} | collective-permute-start | bytes 3932168 | tf_op jit(solution)/shard_map/ppermute | solution.py:252
  145.2 23.8 %collective-permute-start.18 = (bf16[2,5,512,128]{3,2,1,0:T(8,128)(2,1)S(1)}, bf16[2,5,512,128]{3,2,1,0:T(8,128)(2,1)S(1)}, u32[]{:S(2)}, u32[]{:S(2)}) collective-permute-start(bf16[2,5,512,128]{3,2,1,0:T(8,128)(2,1)S(1)} %get-tuple-element.47.refs_3_), channel_id=1, source_target_pairs={{0,16},{1,17},{2,18},{3,19}} | collective-permute-start | bytes 3932168 | tf_op jit(solution)/shard_map/ppermute | solution.py:252
  146.0 23.1 %collective-permute-start.19 = (bf16[2,5,512,128]{3,2,1,0:T(8,128)(2,1)S(1)}, bf16[2,5,512,128]{3,2,1,0:T(8,128)(2,1)S(1)}, u32[]{:S(2)}, u32[]{:S(2)}) collective-permute-start(bf16[2,5,512,128]{3,2,1,0:T(8,128)(2,1)S(1)} %get-tuple-element.47.refs_3_), channel_id=1, source_target_pairs={{0,24},{1,25},{2,26},{3,27}} | collective-permute-start | bytes 3932168 | tf_op jit(solution)/shard_map/ppermute | solution.py:252
  146.8 35.2 %collective-permute-start.5 = (bf16[512,1280]{1,0:T(8,128)(2,1)S(1)}, bf16[512,1280]{1,0:T(8,128)(2,1)S(1)}, u32[]{:S(2)}, u32[]{:S(2)}) collective-permute-start(bf16[512,1280]{1,0:T(8,128)(2,1)S(1)} %collective-permute-done.4.inner), channel_id=1, source_target_pairs={{1,0},{2,3},{5,4},{6,7},{9,8},{10,11},{13,12},{14,15},{17,16},{18,... | collective-permute-start | bytes 3932168 | tf_op jit(solution)/shard_map/ppermute | solution.py:299
  169.3 23.7 %collective-permute-start.20 = (bf16[2,5,512,128]{3,2,1,0:T(8,128)(2,1)S(1)}, bf16[2,5,512,128]{3,2,1,0:T(8,128)(2,1)S(1)}, u32[]{:S(2)}, u32[]{:S(2)}) collective-permute-start(bf16[2,5,512,128]{3,2,1,0:T(8,128)(2,1)S(1)} %select_select_fusion.refs_1_), channel_id=1, source_target_pairs={{0,4},{8,12},{16,20},{24,28},{1,5},{9,13},{17,21},{25,29},{2,6},{1... | collective-permute-start | bytes 3932168 | tf_op jit(solution)/shard_map/ppermute | solution.py:253
  170.7 22.3 %collective-permute-start.21 = (bf16[2,5,256,128]{3,2,1,0:T(8,128)(2,1)S(1)}, bf16[2,5,256,128]{3,2,1,0:T(8,128)(2,1)S(1)}, u32[]{:S(2)}, u32[]{:S(2)}) collective-permute-start(bf16[2,5,256,128]{3,2,1,0:T(8,128)(2,1)S(1)} %get-tuple-element.48), channel_id=1, source_target_pairs={{4,8},{8,12},{12,16},{16,20},{20,24},{24,28},{5,9},{9,13},{13,17},... | collective-permute-start | bytes 1966088 | tf_op jit(solution)/shard_map/ppermute | solution.py:350
  190.2 12.7 %collective-permute-start.23 = (bf16[2,5,512,128]{3,2,1,0:T(8,128)(2,1)S(1)}, bf16[2,5,512,128]{3,2,1,0:T(8,128)(2,1)S(1)}, u32[]{:S(2)}, u32[]{:S(2)}) collective-permute-start(bf16[2,5,512,128]{3,2,1,0:T(8,128)(2,1)S(1)} %get-tuple-element.53.refs_4_), channel_id=1, source_target_pairs={{0,4},{1,5},{2,6},{3,7}} | collective-permute-start | bytes 3932168 | tf_op jit(solution)/shard_map/ppermute | solution.py:353
  191.0 11.9 %collective-permute-start.22 = (bf16[2,5,256,128]{3,2,1,0:T(8,128)(2,1)S(1)}, bf16[2,5,256,128]{3,2,1,0:T(8,128)(2,1)S(1)}, u32[]{:S(2)}, u32[]{:S(2)}) collective-permute-start(bf16[2,5,256,128]{3,2,1,0:T(8,128)(2,1)S(1)} %get-tuple-element.52), channel_id=1, source_target_pairs={{4,8},{8,12},{12,16},{16,20},{20,24},{24,28},{5,9},{9,13},{13,17},... | collective-permute-start | bytes 1966088 | tf_op jit(solution)/shard_map/ppermute | solution.py:350
  (8 other events, 72.1 us)

commit v19 on v18

--- a/solution.py
+++ b/solution.py
@@ -345,9 +345,9 @@
     kv1, beside = hold((kv1, beside))
     third2 = send(cross2, OUTWARD)
     anchor = broadcast_first(kv1, "tm")
-    half = kv1.shape[2] // 2
-    halves = hold((kv1[:, :, :half], kv1[:, :, half:], anchor[0]))
-    shift1 = [lax.ppermute(x, "tm", [(i, i + 1) for i in range(1, count - 1)]) for x in halves[:2]]
+    cut = 3 * kv1.shape[2] // 4
+    pieces = hold((kv1[:, :, :cut], kv1[:, :, cut:], anchor[0]))
+    shift1 = [lax.ppermute(x, "tm", [(i, i + 1) for i in range(1, count - 1)]) for x in pieces[:2]]
     raw2 = project([(mixed2,), (inward2, first2), (middle2, second2)], info_raw, weights, after=(beside,), flops=10**10)
     q2, kv2 = finish(raw2, cross2, third2, info_end, weights, gains, 10**11)
     shift2 = lax.ppermute(kv2, "tm", [(0, 1)])

time: 214 us -> 213 us (level)
  the two profiles are of different devices: /device:TPU:10 before, /device:TPU:21 now
where the time goes in v19:
time: 213 us; the launch traced here: 212 us
  starting transfers between devices  76 us (36%)
  waiting for transfers between devices  67.4 us (32%)
  Pallas kernels  52.7 us (25%)
  other arithmetic  8.5 us (4%)
  local copies, waits for them, and re-layouts  6.73 us (3%)
    ppermute x12, waiting for transfers between devices, send(): return lax.ppermute(x, 'head', pairs)  55.4 us
    ppermute x12, starting transfers between devices, send(): return lax.ppermute(x, 'head', pairs)  33.2 us
    pallas_call x2, Pallas kernels, project(): pl.pallas_call(functools.partial(project_body, pairs, len(after), final),...  29.4 us
    ppermute x2, starting transfers between devices, per_device(): lax.ppermute(x, 'tm', [(i, i + 1) for i in range(1, count - 1)])  19.9 us
    pallas_call x2, Pallas kernels, attend(): pl.pallas_call(functools.partial(attend_body, 256, len(queries), counts,...  13.7 us
    ppermute x1, waiting for transfers between devices, per_device(): following = lax.ppermute(frames[0], 'tm', downs)  12 us
    pallas_call x1, Pallas kernels, finish(): pl.pallas_call(finish_body, grid_spec=pltpu.PrefetchScalarGridSpec(num_sc...  9.59 us
    convert_element_type x3, other arithmetic, mix(): (centre + taps[0] * before + taps[1] * centre + taps[2] * after).astype(B...  6.91 us
  transfers between devices with their start and end apart: 24, of which 11 were waited for; matrix products, arithmetic and copies ran while one was open for 5% of the time, Pallas kernels for 21%

profile of v19, /device:TPU:21, one launch (start us, length us, event | category | flops | bytes accessed | tf_op | source)
XLA Modules:
  0.0 211.9 jit_solution(746985205402606164)
XLA Ops:
  0.0 2.9 %slice_bitcast_fusion.2 = (bf16[512,1280]{1,0:T(8,128)(2,1)S(1)}, bf16[512,1280]{1,0:T(8,128)(2,1)}) fusion(bf16[2,512,1280]{2,1,0:T(8,128)(2,1)} %param.7), kind=kLoop, calls=%fused_computation.24 | loop fusion | bytes 5242880 | tf_op jit(solution)/shard_map/squeeze | solution.py:326
  3.0 2.6 %collective-permute-start = (bf16[512,1280]{1,0:T(8,128)(2,1)}, bf16[512,1280]{1,0:T(8,128)(2,1)S(1)}, u32[]{:S(2)}, u32[]{:S(2)}) collective-permute-start(bf16[512,1280]{1,0:T(8,128)(2,1)} %get-tuple-element.64), channel_id=1, source_target_pairs={{4,0},{8,4},{12,8},{16,12},{20,16},{24,20},{28,24},{5,1},{9,5},{13... | collective-permute-start | bytes 3932168 | tf_op jit(solution)/shard_map/ppermute | solution.py:318
  5.5 4.4 %collective-permute-start.1 = (bf16[512,1280]{1,0:T(8,128)(2,1)}, bf16[512,1280]{1,0:T(8,128)(2,1)}, u32[]{:S(2)}, u32[]{:S(2)}) collective-permute-start(bf16[512,1280]{1,0:T(8,128)(2,1)} %get-tuple-element.64), channel_id=1, source_target_pairs={{1,0},{2,3},{5,4},{6,7},{9,8},{10,11},{13,12},{14,15},{17,16},{18,... | collective-permute-start | bytes 3932168 | tf_op jit(solution)/shard_map/ppermute | solution.py:299
  10.1 12.0 %collective-permute-done = bf16[512,1280]{1,0:T(8,128)(2,1)S(1)} collective-permute-done((bf16[512,1280]{1,0:T(8,128)(2,1)}, bf16[512,1280]{1,0:T(8,128)(2,1)S(1)}, u32[]{:S(2)}, u32[]{:S(2)}) %collective-permute-start) | collective-permute-done | bytes 1310752 | tf_op jit(solution)/shard_map/ppermute | solution.py:318
  26.6 4.8 %collective-permute-start.7 = (bf16[528,1280]{1,0:T(8,128)(2,1)S(1)}, bf16[528,1280]{1,0:T(8,128)(2,1)S(1)}, u32[]{:S(2)}, u32[]{:S(2)}) collective-permute-start(bf16[528,1280]{1,0:T(8,128)(2,1)S(1)} %pad_maximum_fusion), channel_id=1, source_target_pairs={{1,0},{2,3},{5,4},{6,7},{9,8},{10,11},{13,12},{14,15},{17,16},{18,... | collective-permute-start | bytes 4055048 | tf_op jit(solution)/shard_map/ppermute | solution.py:299
  31.5 4.8 %collective-permute-done.1 = bf16[512,1280]{1,0:T(8,128)(2,1)} collective-permute-done((bf16[512,1280]{1,0:T(8,128)(2,1)}, bf16[512,1280]{1,0:T(8,128)(2,1)}, u32[]{:S(2)}, u32[]{:S(2)}) %collective-permute-start.1) | collective-permute-done | bytes 1310752 | tf_op jit(solution)/shard_map/ppermute | solution.py:299
  36.3 5.1 %collective-permute-start.2 = (bf16[512,1280]{1,0:T(8,128)(2,1)S(1)}, bf16[512,1280]{1,0:T(8,128)(2,1)S(1)}, u32[]{:S(2)}, u32[]{:S(2)}) collective-permute-start(bf16[512,1280]{1,0:T(8,128)(2,1)S(1)} %slice_bitcast_fusion), channel_id=1, source_target_pairs={{0,4},{4,8},{8,12},{12,16},{16,20},{20,24},{24,28},{1,5},{5,9},{9,... | collective-permute-start | bytes 3932168 | tf_op jit(solution)/shard_map/ppermute | solution.py:325
  43.3 12.5 %collective-permute-done.8.refs_3_ = bf16[512,1280]{1,0:T(8,128)(2,1)} collective-permute-done((bf16[512,1280]{1,0:T(8,128)(2,1)S(1)}, bf16[512,1280]{1,0:T(8,128)(2,1)}, u32[]{:S(2)}, u32[]{:S(2)}) %collective-permute-start.8) | collective-permute-done | bytes 1310752 | tf_op jit(solution)/shard_map/ppermute | solution.py:299
  61.6 3.5 %collective-permute-done.7 = bf16[528,1280]{1,0:T(8,128)(2,1)S(1)} collective-permute-done((bf16[528,1280]{1,0:T(8,128)(2,1)S(1)}, bf16[528,1280]{1,0:T(8,128)(2,1)S(1)}, u32[]{:S(2)}, u32[]{:S(2)}) %collective-permute-start.7) | collective-permute-done | bytes 1351712 | tf_op jit(solution)/shard_map/ppermute | solution.py:299
  66.6 5.3 %collective-permute-start.13 = (bf16[512,1280]{1,0:T(8,128)(2,1)}, bf16[512,1280]{1,0:T(8,128)(2,1)}, u32[]{:S(2)}, u32[]{:S(2)}) collective-permute-start(bf16[512,1280]{1,0:T(8,128)(2,1)} %slice.79), channel_id=1, source_target_pairs={{0,4},{4,8},{8,12},{12,16},{16,20},{20,24},{24,28},{1,5},{5,9},{9,... | collective-permute-start | bytes 3932168 | tf_op jit(solution)/shard_map/ppermute | solution.py:332
  76.5 12.6 %collective-permute-done.10.refs_7_ = bf16[512,1280]{1,0:T(8,128)(2,1)} collective-permute-done((bf16[512,1280]{1,0:T(8,128)(2,1)}, bf16[512,1280]{1,0:T(8,128)(2,1)}, u32[]{:S(2)}, u32[]{:S(2)}) %collective-permute-start.10) | collective-permute-done | bytes 1310752 | tf_op jit(solution)/shard_map/ppermute | solution.py:299
  89.1 4.2 %collective-permute-done.11.refs_6_ = bf16[512,1280]{1,0:T(8,128)(2,1)} collective-permute-done((bf16[512,1280]{1,0:T(8,128)(2,1)}, bf16[512,1280]{1,0:T(8,128)(2,1)}, u32[]{:S(2)}, u32[]{:S(2)}) %collective-permute-start.11) | collective-permute-done | bytes 1310752 | tf_op jit(solution)/shard_map/ppermute | solution.py:299
  93.3 4.2 %collective-permute-start.14 = (bf16[512,1280]{1,0:T(8,128)(2,1)}, bf16[512,1280]{1,0:T(8,128)(2,1)S(1)}, u32[]{:S(2)}, u32[]{:S(2)}) collective-permute-start(bf16[512,1280]{1,0:T(8,128)(2,1)} %collective-permute-done.10.refs_7_), channel_id=1, source_target_pairs={{1,0},{2,3},{5,4},{6,7},{9,8},{10,11},{13,12},{14,15},{17,16},{18,... | collective-permute-start | bytes 3932168 | tf_op jit(solution)/shard_map/ppermute | solution.py:299
  98.5 7.3 %collective-permute-done.3.refs_0_.refs_2_ = bf16[512,1280]{1,0:T(8,128)(2,1)} collective-permute-done((bf16[512,1280]{1,0:T(8,128)(2,1)S(1)}, bf16[512,1280]{1,0:T(8,128)(2,1)}, u32[]{:S(2)}, u32[]{:S(2)}) %collective-permute-start.3) | collective-permute-done | bytes 1310752 | tf_op jit(solution)/shard_map/ppermute | solution.py:299
  109.1 4.7 %fusion.11 = (bf16[512,1280]{1,0:T(8,128)(2,1)S(1)}, bf16[512,1280]{1,0:T(8,128)(2,1)}) fusion(bf16[512,1280]{1,0:T(8,128)(2,1)} %collective-permute-done.12, bf16[512,1280]{1,0:T(8,128)(2,1)} %collective-permute-done.1, bf16[512,1280]{1,0:T(8,128)(2,1)} %collective-permute-done.13, f32[1280]{0:T(1024)S(1)} %get-tuple-element.56, ...), kind=kLoop, calls=%fused_computation.19 | loop fusion | flops 17039360 | bytes 7879681 | tf_op jit(solution)/shard_map/convert_element_type | solution.py:263
  113.8 3.4 %collective-permute-done.6.refs_1_.refs_4_ = bf16[512,1280]{1,0:T(8,128)(2,1)} collective-permute-done((bf16[512,1280]{1,0:T(8,128)(2,1)S(1)}, bf16[512,1280]{1,0:T(8,128)(2,1)}, u32[]{:S(2)}, u32[]{:S(2)}) %collective-permute-start.6) | collective-permute-done | bytes 1310752 | tf_op jit(solution)/shard_map/ppermute | solution.py:299
  119.7 4.3 %collective-permute-done.14.refs_8_ = bf16[512,1280]{1,0:T(8,128)(2,1)S(1)} collective-permute-done((bf16[512,1280]{1,0:T(8,128)(2,1)}, bf16[512,1280]{1,0:T(8,128)(2,1)S(1)}, u32[]{:S(2)}, u32[]{:S(2)}) %collective-permute-start.14) | collective-permute-done | bytes 1310752 | tf_op jit(solution)/shard_map/ppermute | solution.py:299
  125.1 15.5 %project_end.1 = (bf16[5,512,128]{2,1,0:T(8,128)(2,1)S(1)}, bf16[2,5,512,128]{3,2,1,0:T(8,128)(2,1)S(1)}) custom-call(s32[5]{0:T(128)S(1)} %stack.65.info, bf16[512,1280]{1,0:T(8,128)(2,1)} %collective-permute-done.3.refs_0_.refs_2_, bf16[512,1280]{1,0:T(8,128)(2,1)} %collective-permute-done.6.refs_1_.refs_4_, bf16[512,1280]{1,0:T(8,128)(2,1)S(1)} %copy-done.3, ...), custom_call_target="tpu_custom_call" | custom-call | flops 10000000000 | bytes 1 | tf_op jit(solution)/shard_map/project_end/pallas_call | solution.py:101
  146.1 4.4 %collective-permute-start.5 = (bf16[512,1280]{1,0:T(8,128)(2,1)}, bf16[512,1280]{1,0:T(8,128)(2,1)S(1)}, u32[]{:S(2)}, u32[]{:S(2)}) collective-permute-start(bf16[512,1280]{1,0:T(8,128)(2,1)} %collective-permute-done.4.inner), channel_id=1, source_target_pairs={{1,0},{2,3},{5,4},{6,7},{9,8},{10,11},{13,12},{14,15},{17,16},{18,... | collective-permute-start | bytes 3932168 | tf_op jit(solution)/shard_map/ppermute | solution.py:299
  152.1 13.8 %project_raw.1.raw = f32[3,5,512,128]{3,2,1,0:T(8,128)} custom-call(s32[4]{0:T(128)S(1)} %pad_add_fusion.2.info, bf16[16,1280]{1,0:T(8,128)(2,1)S(1)} %collective-permute-done.15.refs_0_, bf16[512,1280]{1,0:T(8,128)(2,1)S(1)} %copy-done.1, bf16[512,1280]{1,0:T(8,128)(2,1)} %collective-permute-done.3.refs_0_.refs_2_, ...), custom_call_target="tpu_custom_call" | custom-call | flops 10000000000 | bytes 1 | tf_op jit(solution)/shard_map/project_raw/pallas_call | solution.py:101
  167.6 18.0 %collective-permute-start.21 = (bf16[2,5,384,128]{3,2,1,0:T(8,128)(2,1)S(1)}, bf16[2,5,384,128]{3,2,1,0:T(8,128)(2,1)S(1)}, u32[]{:S(2)}, u32[]{:S(2)}) collective-permute-start(bf16[2,5,384,128]{3,2,1,0:T(8,128)(2,1)S(1)} %slice.77), channel_id=1, source_target_pairs={{4,8},{8,12},{12,16},{16,20},{20,24},{24,28},{5,9},{9,13},{13,17},... | collective-permute-start | bytes 2949128 | tf_op jit(solution)/shard_map/ppermute | solution.py:350
  185.6 9.6 %finish.1 = (bf16[5,512,128]{2,1,0:T(8,128)(2,1)S(1)}, bf16[2,5,512,128]{3,2,1,0:T(8,128)(2,1)S(1)}) custom-call(s32[2]{0:T(128)S(1)} %pad_add_fusion.1.info, bf16[512,1280]{1,0:T(8,128)(2,1)} %collective-permute-done.4.inner, bf16[512,1280]{1,0:T(8,128)(2,1)S(1)} %collective-permute-done.5.outer, bf16[5120,640]{1,0:T(8,128)(2,1)} %wq.1, ...), custom_call_target="tpu_custom_call" | custom-call | flops 99999997952 | bytes 1 | tf_op jit(solution)/shard_map/finish/pallas_call | solution.py:139
  198.0 6.5 %attend.2.refs_7_ = bf16[2,512,640]{2,1,0:T(8,128)(2,1)} custom-call(s32[3]{0:T(128)S(1)} %get-tuple-element.69.info, bf16[5,512,128]{2,1,0:T(8,128)(2,1)S(1)} %get-tuple-element.54.refs_0_, bf16[2,5,512,128]{3,2,1,0:T(8,128)(2,1)S(1)} %select_select_fusion.refs_1_, bf16[2,5,512,128]{3,2,1,0:T(8,128)(2,1)S(1)} %collective-permute-done.20.refs_2_, ...), custom_call_target="tpu_custom_call" | custom-call | flops 13421772800 | bytes 3932160 | tf_op jit(solution)/shard_map/attend/pallas_call | solution.py:222
  204.5 7.3 %attend.3 = bf16[2,512,640]{2,1,0:T(8,128)(2,1)} custom-call(s32[3]{0:T(128)S(1)} %get-tuple-element.68.info, bf16[5,512,128]{2,1,0:T(8,128)(2,1)S(1)} %get-tuple-element.46.refs_0_, bf16[2,5,512,128]{3,2,1,0:T(8,128)(2,1)S(1)} %select_select_fusion.refs_1_, ...), custom_call_target="tpu_custom_call", output_to_operand_aliasing={{}: (8, {})} | custom-call | flops 13421772800 | bytes 3932160 | tf_op jit(solution)/shard_map/attend/pallas_call | solution.py:222
  (71 shorter events, 37.6 us)
Async XLA Ops:
  3.0 19.2 %collective-permute-start = (bf16[512,1280]{1,0:T(8,128)(2,1)}, bf16[512,1280]{1,0:T(8,128)(2,1)S(1)}, u32[]{:S(2)}, u32[]{:S(2)}) collective-permute-start(bf16[512,1280]{1,0:T(8,128)(2,1)} %get-tuple-element.64), channel_id=1, source_target_pairs={{4,0},{8,4},{12,8},{16,12},{20,16},{24,20},{28,24},{5,1},{9,5},{13... | collective-permute-start | bytes 3932168 | tf_op jit(solution)/shard_map/ppermute | solution.py:318
  5.5 30.7 %collective-permute-start.1 = (bf16[512,1280]{1,0:T(8,128)(2,1)}, bf16[512,1280]{1,0:T(8,128)(2,1)}, u32[]{:S(2)}, u32[]{:S(2)}) collective-permute-start(bf16[512,1280]{1,0:T(8,128)(2,1)} %get-tuple-element.64), channel_id=1, source_target_pairs={{1,0},{2,3},{5,4},{6,7},{9,8},{10,11},{13,12},{14,15},{17,16},{18,... | collective-permute-start | bytes 3932168 | tf_op jit(solution)/shard_map/ppermute | solution.py:299
  23.2 32.6 %collective-permute-start.8 = (bf16[512,1280]{1,0:T(8,128)(2,1)S(1)}, bf16[512,1280]{1,0:T(8,128)(2,1)}, u32[]{:S(2)}, u32[]{:S(2)}) collective-permute-start(bf16[512,1280]{1,0:T(8,128)(2,1)S(1)} %fusion.5.refs_2_), channel_id=1, source_target_pairs={{0,1},{3,2},{4,5},{7,6},{8,9},{11,10},{12,13},{15,14},{16,17},{19,... | collective-permute-start | bytes 3932168 | tf_op jit(solution)/shard_map/ppermute | solution.py:299
  24.5 32.6 %collective-permute-start.9 = (bf16[512,1280]{1,0:T(8,128)(2,1)S(1)}, bf16[512,1280]{1,0:T(8,128)(2,1)}, u32[]{:S(2)}, u32[]{:S(2)}) collective-permute-start(bf16[512,1280]{1,0:T(8,128)(2,1)S(1)} %fusion.5.refs_2_), channel_id=1, source_target_pairs={{1,2},{2,1},{5,6},{6,5},{9,10},{10,9},{13,14},{14,13},{17,18},{18,... | collective-permute-start | bytes 3932168 | tf_op jit(solution)/shard_map/ppermute | solution.py:299
  26.6 38.5 %collective-permute-start.7 = (bf16[528,1280]{1,0:T(8,128)(2,1)S(1)}, bf16[528,1280]{1,0:T(8,128)(2,1)S(1)}, u32[]{:S(2)}, u32[]{:S(2)}) collective-permute-start(bf16[528,1280]{1,0:T(8,128)(2,1)S(1)} %pad_maximum_fusion), channel_id=1, source_target_pairs={{1,0},{2,3},{5,4},{6,7},{9,8},{10,11},{13,12},{14,15},{17,16},{18,... | collective-permute-start | bytes 4055048 | tf_op jit(solution)/shard_map/ppermute | solution.py:299
  36.3 35.6 %collective-permute-start.2 = (bf16[512,1280]{1,0:T(8,128)(2,1)S(1)}, bf16[512,1280]{1,0:T(8,128)(2,1)S(1)}, u32[]{:S(2)}, u32[]{:S(2)}) collective-permute-start(bf16[512,1280]{1,0:T(8,128)(2,1)S(1)} %slice_bitcast_fusion), channel_id=1, source_target_pairs={{0,4},{4,8},{8,12},{12,16},{16,20},{20,24},{24,28},{1,5},{5,9},{9,... | collective-permute-start | bytes 3932168 | tf_op jit(solution)/shard_map/ppermute | solution.py:325
  41.4 33.1 %collective-permute-start.12 = (bf16[512,1280]{1,0:T(8,128)(2,1)}, bf16[512,1280]{1,0:T(8,128)(2,1)}, u32[]{:S(2)}, u32[]{:S(2)}) collective-permute-start(bf16[512,1280]{1,0:T(8,128)(2,1)} %collective-permute-done.1), channel_id=1, source_target_pairs={{4,0},{8,4},{12,8},{16,12},{20,16},{24,20},{28,24},{5,1},{9,5},{13... | collective-permute-start | bytes 3932168 | tf_op jit(solution)/shard_map/ppermute | solution.py:327
  57.1 32.0 %collective-permute-start.10 = (bf16[512,1280]{1,0:T(8,128)(2,1)}, bf16[512,1280]{1,0:T(8,128)(2,1)}, u32[]{:S(2)}, u32[]{:S(2)}) collective-permute-start(bf16[512,1280]{1,0:T(8,128)(2,1)} %collective-permute-done.8.refs_3_), channel_id=1, source_target_pairs={{1,2},{2,1},{5,6},{6,5},{9,10},{10,9},{13,14},{14,13},{17,18},{18,... | collective-permute-start | bytes 3932168 | tf_op jit(solution)/shard_map/ppermute | solution.py:299
  59.2 34.1 %collective-permute-start.11 = (bf16[512,1280]{1,0:T(8,128)(2,1)}, bf16[512,1280]{1,0:T(8,128)(2,1)}, u32[]{:S(2)}, u32[]{:S(2)}) collective-permute-start(bf16[512,1280]{1,0:T(8,128)(2,1)} %collective-permute-done.9.refs_5_), channel_id=1, source_target_pairs={{1,0},{2,3},{5,4},{6,7},{9,8},{10,11},{13,12},{14,15},{17,16},{18,... | collective-permute-start | bytes 3932168 | tf_op jit(solution)/shard_map/ppermute | solution.py:299
  66.6 26.7 %collective-permute-start.13 = (bf16[512,1280]{1,0:T(8,128)(2,1)}, bf16[512,1280]{1,0:T(8,128)(2,1)}, u32[]{:S(2)}, u32[]{:S(2)}) collective-permute-start(bf16[512,1280]{1,0:T(8,128)(2,1)} %slice.79), channel_id=1, source_target_pairs={{0,4},{4,8},{8,12},{12,16},{16,20},{20,24},{24,28},{1,5},{5,9},{9,... | collective-permute-start | bytes 3932168 | tf_op jit(solution)/shard_map/ppermute | solution.py:332
  73.1 32.7 %collective-permute-start.3 = (bf16[512,1280]{1,0:T(8,128)(2,1)S(1)}, bf16[512,1280]{1,0:T(8,128)(2,1)}, u32[]{:S(2)}, u32[]{:S(2)}) collective-permute-start(bf16[512,1280]{1,0:T(8,128)(2,1)S(1)} %fusion.2.refs_1_), channel_id=1, source_target_pairs={{0,1},{3,2},{4,5},{7,6},{8,9},{11,10},{12,13},{15,14},{16,17},{19,... | collective-permute-start | bytes 3932168 | tf_op jit(solution)/shard_map/ppermute | solution.py:299
  74.5 42.6 %collective-permute-start.6 = (bf16[512,1280]{1,0:T(8,128)(2,1)S(1)}, bf16[512,1280]{1,0:T(8,128)(2,1)}, u32[]{:S(2)}, u32[]{:S(2)}) collective-permute-start(bf16[512,1280]{1,0:T(8,128)(2,1)S(1)} %fusion.2.refs_1_), channel_id=1, source_target_pairs={{1,2},{2,1},{5,6},{6,5},{9,10},{10,9},{13,14},{14,13},{17,18},{18,... | collective-permute-start | bytes 3932168 | tf_op jit(solution)/shard_map/ppermute | solution.py:299
  93.3 30.7 %collective-permute-start.14 = (bf16[512,1280]{1,0:T(8,128)(2,1)}, bf16[512,1280]{1,0:T(8,128)(2,1)S(1)}, u32[]{:S(2)}, u32[]{:S(2)}) collective-permute-start(bf16[512,1280]{1,0:T(8,128)(2,1)} %collective-permute-done.10.refs_7_), channel_id=1, source_target_pairs={{1,0},{2,3},{5,4},{6,7},{9,8},{10,11},{13,12},{14,15},{17,16},{18,... | collective-permute-start | bytes 3932168 | tf_op jit(solution)/shard_map/ppermute | solution.py:299
  106.5 34.1 %collective-permute-start.15 = (bf16[16,1280]{1,0:T(8,128)(2,1)S(1)}, bf16[16,1280]{1,0:T(8,128)(2,1)S(1)}, u32[]{:S(2)}, u32[]{:S(2)}) collective-permute-start(bf16[16,1280]{1,0:T(8,128)(2,1)S(1)} %slice.86), channel_id=1, source_target_pairs={{0,4},{4,0},{8,12},{12,8},{16,20},{20,16},{24,28},{28,24},{1,5},{5... | collective-permute-start | bytes 122888 | tf_op jit(solution)/shard_map/ppermute | solution.py:344
  107.2 38.9 %collective-permute-start.4 = (bf16[512,1280]{1,0:T(8,128)(2,1)}, bf16[512,1280]{1,0:T(8,128)(2,1)}, u32[]{:S(2)}, u32[]{:S(2)}) collective-permute-start(bf16[512,1280]{1,0:T(8,128)(2,1)} %collective-permute-done.3.refs_0_.refs_2_), channel_id=1, source_target_pairs={{1,2},{2,1},{5,6},{6,5},{9,10},{10,9},{13,14},{14,13},{17,18},{18,... | collective-permute-start | bytes 3932168 | tf_op jit(solution)/shard_map/ppermute | solution.py:299
  117.2 34.9 %collective-permute-start.16 = (bf16[512,1280]{1,0:T(8,128)(2,1)}, bf16[512,1280]{1,0:T(8,128)(2,1)}, u32[]{:S(2)}, u32[]{:S(2)}) collective-permute-start(bf16[512,1280]{1,0:T(8,128)(2,1)} %collective-permute-done.6.refs_1_.refs_4_), channel_id=1, source_target_pairs={{1,0},{2,3},{5,4},{6,7},{9,8},{10,11},{13,12},{14,15},{17,16},{18,... | collective-permute-start | bytes 3932168 | tf_op jit(solution)/shard_map/ppermute | solution.py:299
  140.7 25.2 %collective-permute-start.17 = (bf16[2,5,512,128]{3,2,1,0:T(8,128)(2,1)S(1)}, bf16[2,5,512,128]{3,2,1,0:T(8,128)(2,1)}, u32[]{:S(2)}, u32[]{:S(2)}) collective-permute-start(bf16[2,5,512,128]{3,2,1,0:T(8,128)(2,1)S(1)} %get-tuple-element.47.refs_3_), channel_id=1, source_target_pairs={{0,8},{1,9},{2,10},{3,11}} | collective-permute-start | bytes 3932168 | tf_op jit(solution)/shard_map/ppermute | solution.py:252
  142.5 23.5 %collective-permute-start.18 = (bf16[2,5,512,128]{3,2,1,0:T(8,128)(2,1)S(1)}, bf16[2,5,512,128]{3,2,1,0:T(8,128)(2,1)}, u32[]{:S(2)}, u32[]{:S(2)}) collective-permute-start(bf16[2,5,512,128]{3,2,1,0:T(8,128)(2,1)S(1)} %get-tuple-element.47.refs_3_), channel_id=1, source_target_pairs={{0,16},{1,17},{2,18},{3,19}} | collective-permute-start | bytes 3932168 | tf_op jit(solution)/shard_map/ppermute | solution.py:252
  144.2 21.8 %collective-permute-start.19 = (bf16[2,5,512,128]{3,2,1,0:T(8,128)(2,1)S(1)}, bf16[2,5,512,128]{3,2,1,0:T(8,128)(2,1)}, u32[]{:S(2)}, u32[]{:S(2)}) collective-permute-start(bf16[2,5,512,128]{3,2,1,0:T(8,128)(2,1)S(1)} %get-tuple-element.47.refs_3_), channel_id=1, source_target_pairs={{0,24},{1,25},{2,26},{3,27}} | collective-permute-start | bytes 3932168 | tf_op jit(solution)/shard_map/ppermute | solution.py:252
  146.1 39.5 %collective-permute-start.5 = (bf16[512,1280]{1,0:T(8,128)(2,1)}, bf16[512,1280]{1,0:T(8,128)(2,1)S(1)}, u32[]{:S(2)}, u32[]{:S(2)}) collective-permute-start(bf16[512,1280]{1,0:T(8,128)(2,1)} %collective-permute-done.4.inner), channel_id=1, source_target_pairs={{1,0},{2,3},{5,4},{6,7},{9,8},{10,11},{13,12},{14,15},{17,16},{18,... | collective-permute-start | bytes 3932168 | tf_op jit(solution)/shard_map/ppermute | solution.py:299
  166.3 31.7 %collective-permute-start.20 = (bf16[2,5,512,128]{3,2,1,0:T(8,128)(2,1)S(1)}, bf16[2,5,512,128]{3,2,1,0:T(8,128)(2,1)S(1)}, u32[]{:S(2)}, u32[]{:S(2)}) collective-permute-start(bf16[2,5,512,128]{3,2,1,0:T(8,128)(2,1)S(1)} %select_select_fusion.refs_1_), channel_id=1, source_target_pairs={{0,4},{8,12},{16,20},{24,28},{1,5},{9,13},{17,21},{25,29},{2,6},{1... | collective-permute-start | bytes 3932168 | tf_op jit(solution)/shard_map/ppermute | solution.py:253
  167.6 30.4 %collective-permute-start.21 = (bf16[2,5,384,128]{3,2,1,0:T(8,128)(2,1)S(1)}, bf16[2,5,384,128]{3,2,1,0:T(8,128)(2,1)S(1)}, u32[]{:S(2)}, u32[]{:S(2)}) collective-permute-start(bf16[2,5,384,128]{3,2,1,0:T(8,128)(2,1)S(1)} %slice.77), channel_id=1, source_target_pairs={{4,8},{8,12},{12,16},{16,20},{20,24},{24,28},{5,9},{9,13},{13,17},... | collective-permute-start | bytes 2949128 | tf_op jit(solution)/shard_map/ppermute | solution.py:350
  195.2 9.3 %collective-permute-start.23 = (bf16[2,5,512,128]{3,2,1,0:T(8,128)(2,1)S(1)}, bf16[2,5,512,128]{3,2,1,0:T(8,128)(2,1)S(1)}, u32[]{:S(2)}, u32[]{:S(2)}) collective-permute-start(bf16[2,5,512,128]{3,2,1,0:T(8,128)(2,1)S(1)} %get-tuple-element.53.refs_4_), channel_id=1, source_target_pairs={{0,4},{1,5},{2,6},{3,7}} | collective-permute-start | bytes 3932168 | tf_op jit(solution)/shard_map/ppermute | solution.py:353
  196.0 8.4 %collective-permute-start.22 = (bf16[2,5,128,128]{3,2,1,0:T(8,128)(2,1)S(1)}, bf16[2,5,128,128]{3,2,1,0:T(8,128)(2,1)S(1)}, u32[]{:S(2)}, u32[]{:S(2)}) collective-permute-start(bf16[2,5,128,128]{3,2,1,0:T(8,128)(2,1)S(1)} %slice.78), channel_id=1, source_target_pairs={{4,8},{8,12},{12,16},{16,20},{20,24},{24,28},{5,9},{9,13},{13,17},... | collective-permute-start | bytes 983048 | tf_op jit(solution)/shard_map/ppermute | solution.py:350
  (10 other events, 111.3 us)

commit v20 on v19

--- a/solution.py
+++ b/solution.py
@@ -345,7 +345,7 @@
     kv1, beside = hold((kv1, beside))
     third2 = send(cross2, OUTWARD)
     anchor = broadcast_first(kv1, "tm")
-    cut = 3 * kv1.shape[2] // 4
+    cut = 5 * kv1.shape[2] // 8
     pieces = hold((kv1[:, :, :cut], kv1[:, :, cut:], anchor[0]))
     shift1 = [lax.ppermute(x, "tm", [(i, i + 1) for i in range(1, count - 1)]) for x in pieces[:2]]
     raw2 = project([(mixed2,), (inward2, first2), (middle2, second2)], info_raw, weights, after=(beside,), flops=10**10)

time: 213 us -> 213 us (level)
  the two profiles are of different devices: /device:TPU:21 before, /device:TPU:10 now
where the time goes in v20:
time: 213 us; the launch traced here: 210 us
  waiting for transfers between devices  77.9 us (37%)
  starting transfers between devices  62.4 us (29%)
  Pallas kernels  52.7 us (25%)
  other arithmetic  9.81 us (5%)
  local copies, waits for them, and re-layouts  6.73 us (3%)
    ppermute x12, waiting for transfers between devices, send(): return lax.ppermute(x, 'head', pairs)  64.5 us
    ppermute x12, starting transfers between devices, send(): return lax.ppermute(x, 'head', pairs)  40.2 us
    pallas_call x2, Pallas kernels, project(): pl.pallas_call(functools.partial(project_body, pairs, len(after), final),...  29.4 us
    pallas_call x2, Pallas kernels, attend(): pl.pallas_call(functools.partial(attend_body, 256, len(queries), counts,...  13.7 us
    ppermute x1, waiting for transfers between devices, per_device(): following = lax.ppermute(frames[0], 'tm', downs)  11.7 us
    pallas_call x1, Pallas kernels, finish(): pl.pallas_call(finish_body, grid_spec=pltpu.PrefetchScalarGridSpec(num_sc...  9.58 us
    convert_element_type x3, other arithmetic, mix(): (centre + taps[0] * before + taps[1] * centre + taps[2] * after).astype(B...  6.91 us
    ppermute x3, starting transfers between devices, broadcast_first(): held = jnp.where(mine == to, lax.ppermute(x, axis, [(0, to)]), held)  4.76 us
  transfers between devices with their start and end apart: 24, of which 13 were waited for; matrix products, arithmetic and copies ran while one was open for 6% of the time, Pallas kernels for 22%

profile of v20, /device:TPU:10, one launch (start us, length us, event | category | flops | bytes accessed | tf_op | source)
XLA Modules:
  0.0 210.1 jit_solution(13819309272665776305)
XLA Ops:
  4.9 3.5 %collective-permute-start.1 = (bf16[512,1280]{1,0:T(8,128)(2,1)}, bf16[512,1280]{1,0:T(8,128)(2,1)}, u32[]{:S(2)}, u32[]{:S(2)}) collective-permute-start(bf16[512,1280]{1,0:T(8,128)(2,1)} %get-tuple-element.64), channel_id=1, source_target_pairs={{1,0},{2,3},{5,4},{6,7},{9,8},{10,11},{13,12},{14,15},{17,16},{18,... | collective-permute-start | bytes 3932168 | tf_op jit(solution)/shard_map/ppermute | solution.py:299
  8.6 11.7 %collective-permute-done = bf16[512,1280]{1,0:T(8,128)(2,1)S(1)} collective-permute-done((bf16[512,1280]{1,0:T(8,128)(2,1)}, bf16[512,1280]{1,0:T(8,128)(2,1)S(1)}, u32[]{:S(2)}, u32[]{:S(2)}) %collective-permute-start) | collective-permute-done | bytes 1310752 | tf_op jit(solution)/shard_map/ppermute | solution.py:318
  22.7 3.5 %collective-permute-start.9 = (bf16[512,1280]{1,0:T(8,128)(2,1)S(1)}, bf16[512,1280]{1,0:T(8,128)(2,1)}, u32[]{:S(2)}, u32[]{:S(2)}) collective-permute-start(bf16[512,1280]{1,0:T(8,128)(2,1)S(1)} %fusion.5.refs_2_), channel_id=1, source_target_pairs={{1,2},{2,1},{5,6},{6,5},{9,10},{10,9},{13,14},{14,13},{17,18},{18,... | collective-permute-start | bytes 3932168 | tf_op jit(solution)/shard_map/ppermute | solution.py:299
  26.2 3.9 %collective-permute-start.7 = (bf16[528,1280]{1,0:T(8,128)(2,1)S(1)}, bf16[528,1280]{1,0:T(8,128)(2,1)S(1)}, u32[]{:S(2)}, u32[]{:S(2)}) collective-permute-start(bf16[528,1280]{1,0:T(8,128)(2,1)S(1)} %pad_maximum_fusion), channel_id=1, source_target_pairs={{1,0},{2,3},{5,4},{6,7},{9,8},{10,11},{13,12},{14,15},{17,16},{18,... | collective-permute-start | bytes 4055048 | tf_op jit(solution)/shard_map/ppermute | solution.py:299
  30.2 6.4 %collective-permute-done.1 = bf16[512,1280]{1,0:T(8,128)(2,1)} collective-permute-done((bf16[512,1280]{1,0:T(8,128)(2,1)}, bf16[512,1280]{1,0:T(8,128)(2,1)}, u32[]{:S(2)}, u32[]{:S(2)}) %collective-permute-start.1) | collective-permute-done | bytes 1310752 | tf_op jit(solution)/shard_map/ppermute | solution.py:299
  38.5 3.6 %collective-permute-start.12 = (bf16[512,1280]{1,0:T(8,128)(2,1)}, bf16[512,1280]{1,0:T(8,128)(2,1)}, u32[]{:S(2)}, u32[]{:S(2)}) collective-permute-start(bf16[512,1280]{1,0:T(8,128)(2,1)} %collective-permute-done.1), channel_id=1, source_target_pairs={{4,0},{8,4},{12,8},{16,12},{20,16},{24,20},{28,24},{5,1},{9,5},{13... | collective-permute-start | bytes 3932168 | tf_op jit(solution)/shard_map/ppermute | solution.py:327
  42.2 11.2 %collective-permute-done.8.refs_3_ = bf16[512,1280]{1,0:T(8,128)(2,1)} collective-permute-done((bf16[512,1280]{1,0:T(8,128)(2,1)S(1)}, bf16[512,1280]{1,0:T(8,128)(2,1)}, u32[]{:S(2)}, u32[]{:S(2)}) %collective-permute-start.8) | collective-permute-done | bytes 1310752 | tf_op jit(solution)/shard_map/ppermute | solution.py:299
  54.7 3.5 %collective-permute-start.10 = (bf16[512,1280]{1,0:T(8,128)(2,1)}, bf16[512,1280]{1,0:T(8,128)(2,1)}, u32[]{:S(2)}, u32[]{:S(2)}) collective-permute-start(bf16[512,1280]{1,0:T(8,128)(2,1)} %collective-permute-done.8.refs_3_), channel_id=1, source_target_pairs={{1,2},{2,1},{5,6},{6,5},{9,10},{10,9},{13,14},{14,13},{17,18},{18,... | collective-permute-start | bytes 3932168 | tf_op jit(solution)/shard_map/ppermute | solution.py:299
  60.6 4.9 %collective-permute-done.7 = bf16[528,1280]{1,0:T(8,128)(2,1)S(1)} collective-permute-done((bf16[528,1280]{1,0:T(8,128)(2,1)S(1)}, bf16[528,1280]{1,0:T(8,128)(2,1)S(1)}, u32[]{:S(2)}, u32[]{:S(2)}) %collective-permute-start.7) | collective-permute-done | bytes 1351712 | tf_op jit(solution)/shard_map/ppermute | solution.py:299
  71.7 4.6 %collective-permute-start.6 = (bf16[512,1280]{1,0:T(8,128)(2,1)S(1)}, bf16[512,1280]{1,0:T(8,128)(2,1)}, u32[]{:S(2)}, u32[]{:S(2)}) collective-permute-start(bf16[512,1280]{1,0:T(8,128)(2,1)S(1)} %fusion.2.refs_1_), channel_id=1, source_target_pairs={{1,2},{2,1},{5,6},{6,5},{9,10},{10,9},{13,14},{14,13},{17,18},{18,... | collective-permute-start | bytes 3932168 | tf_op jit(solution)/shard_map/ppermute | solution.py:299
  76.3 11.8 %collective-permute-done.10.refs_7_ = bf16[512,1280]{1,0:T(8,128)(2,1)} collective-permute-done((bf16[512,1280]{1,0:T(8,128)(2,1)}, bf16[512,1280]{1,0:T(8,128)(2,1)}, u32[]{:S(2)}, u32[]{:S(2)}) %collective-permute-start.10) | collective-permute-done | bytes 1310752 | tf_op jit(solution)/shard_map/ppermute | solution.py:299
  88.1 5.2 %collective-permute-done.11.refs_6_ = bf16[512,1280]{1,0:T(8,128)(2,1)} collective-permute-done((bf16[512,1280]{1,0:T(8,128)(2,1)}, bf16[512,1280]{1,0:T(8,128)(2,1)}, u32[]{:S(2)}, u32[]{:S(2)}) %collective-permute-start.11) | collective-permute-done | bytes 1310752 | tf_op jit(solution)/shard_map/ppermute | solution.py:299
  93.3 4.5 %collective-permute-start.14 = (bf16[512,1280]{1,0:T(8,128)(2,1)}, bf16[512,1280]{1,0:T(8,128)(2,1)S(1)}, u32[]{:S(2)}, u32[]{:S(2)}) collective-permute-start(bf16[512,1280]{1,0:T(8,128)(2,1)} %collective-permute-done.10.refs_7_), channel_id=1, source_target_pairs={{1,0},{2,3},{5,4},{6,7},{9,8},{10,11},{13,12},{14,15},{17,16},{18,... | collective-permute-start | bytes 3932168 | tf_op jit(solution)/shard_map/ppermute | solution.py:299
  98.7 3.4 %collective-permute-done.3.refs_0_.refs_2_ = bf16[512,1280]{1,0:T(8,128)(2,1)} collective-permute-done((bf16[512,1280]{1,0:T(8,128)(2,1)S(1)}, bf16[512,1280]{1,0:T(8,128)(2,1)}, u32[]{:S(2)}, u32[]{:S(2)}) %collective-permute-start.3) | collective-permute-done | bytes 1310752 | tf_op jit(solution)/shard_map/ppermute | solution.py:299
  104.8 4.6 %collective-permute-start.4 = (bf16[512,1280]{1,0:T(8,128)(2,1)}, bf16[512,1280]{1,0:T(8,128)(2,1)}, u32[]{:S(2)}, u32[]{:S(2)}) collective-permute-start(bf16[512,1280]{1,0:T(8,128)(2,1)} %collective-permute-done.3.refs_0_.refs_2_), channel_id=1, source_target_pairs={{1,2},{2,1},{5,6},{6,5},{9,10},{10,9},{13,14},{14,13},{17,18},{18,... | collective-permute-start | bytes 3932168 | tf_op jit(solution)/shard_map/ppermute | solution.py:299
  109.4 4.7 %fusion.11 = (bf16[512,1280]{1,0:T(8,128)(2,1)S(1)}, bf16[512,1280]{1,0:T(8,128)(2,1)}) fusion(bf16[512,1280]{1,0:T(8,128)(2,1)} %collective-permute-done.12, bf16[512,1280]{1,0:T(8,128)(2,1)} %collective-permute-done.1, bf16[512,1280]{1,0:T(8,128)(2,1)} %collective-permute-done.13, f32[1280]{0:T(1024)S(1)} %get-tuple-element.56, ...), kind=kLoop, calls=%fused_computation.19 | loop fusion | flops 17039360 | bytes 7879681 | tf_op jit(solution)/shard_map/convert_element_type | solution.py:263
  118.7 8.5 %collective-permute-done.14.refs_8_ = bf16[512,1280]{1,0:T(8,128)(2,1)S(1)} collective-permute-done((bf16[512,1280]{1,0:T(8,128)(2,1)}, bf16[512,1280]{1,0:T(8,128)(2,1)S(1)}, u32[]{:S(2)}, u32[]{:S(2)}) %collective-permute-start.14) | collective-permute-done | bytes 1310752 | tf_op jit(solution)/shard_map/ppermute | solution.py:299
  128.3 15.5 %project_end.1 = (bf16[5,512,128]{2,1,0:T(8,128)(2,1)S(1)}, bf16[2,5,512,128]{3,2,1,0:T(8,128)(2,1)S(1)}) custom-call(s32[5]{0:T(128)S(1)} %stack.65.info, bf16[512,1280]{1,0:T(8,128)(2,1)} %collective-permute-done.3.refs_0_.refs_2_, bf16[512,1280]{1,0:T(8,128)(2,1)} %collective-permute-done.6.refs_1_.refs_4_, bf16[512,1280]{1,0:T(8,128)(2,1)S(1)} %copy-done.3, ...), custom_call_target="tpu_custom_call" | custom-call | flops 10000000000 | bytes 1 | tf_op jit(solution)/shard_map/project_end/pallas_call | solution.py:101
  148.8 4.7 %collective-permute-start.5 = (bf16[512,1280]{1,0:T(8,128)(2,1)}, bf16[512,1280]{1,0:T(8,128)(2,1)S(1)}, u32[]{:S(2)}, u32[]{:S(2)}) collective-permute-start(bf16[512,1280]{1,0:T(8,128)(2,1)} %collective-permute-done.4.inner), channel_id=1, source_target_pairs={{1,0},{2,3},{5,4},{6,7},{9,8},{10,11},{13,12},{14,15},{17,16},{18,... | collective-permute-start | bytes 3932168 | tf_op jit(solution)/shard_map/ppermute | solution.py:299
  155.3 13.8 %project_raw.1.raw = f32[3,5,512,128]{3,2,1,0:T(8,128)} custom-call(s32[4]{0:T(128)S(1)} %pad_add_fusion.2.info, bf16[16,1280]{1,0:T(8,128)(2,1)S(1)} %collective-permute-done.15.refs_0_, bf16[512,1280]{1,0:T(8,128)(2,1)S(1)} %copy-done.1, bf16[512,1280]{1,0:T(8,128)(2,1)} %collective-permute-done.3.refs_0_.refs_2_, ...), custom_call_target="tpu_custom_call" | custom-call | flops 10000000000 | bytes 1 | tf_op jit(solution)/shard_map/project_raw/pallas_call | solution.py:101
  174.0 8.0 %collective-permute-done.5.outer = bf16[512,1280]{1,0:T(8,128)(2,1)S(1)} collective-permute-done((bf16[512,1280]{1,0:T(8,128)(2,1)}, bf16[512,1280]{1,0:T(8,128)(2,1)S(1)}, u32[]{:S(2)}, u32[]{:S(2)}) %collective-permute-start.5) | collective-permute-done | bytes 1310752 | tf_op jit(solution)/shard_map/ppermute | solution.py:299
  182.1 9.6 %finish.1 = (bf16[5,512,128]{2,1,0:T(8,128)(2,1)S(1)}, bf16[2,5,512,128]{3,2,1,0:T(8,128)(2,1)S(1)}) custom-call(s32[2]{0:T(128)S(1)} %pad_add_fusion.1.info, bf16[512,1280]{1,0:T(8,128)(2,1)} %collective-permute-done.4.inner, bf16[512,1280]{1,0:T(8,128)(2,1)S(1)} %collective-permute-done.5.outer, bf16[5120,640]{1,0:T(8,128)(2,1)} %wq.1, ...), custom_call_target="tpu_custom_call" | custom-call | flops 99999997952 | bytes 1 | tf_op jit(solution)/shard_map/finish/pallas_call | solution.py:139
  194.4 6.5 %attend.2.refs_7_ = bf16[2,512,640]{2,1,0:T(8,128)(2,1)} custom-call(s32[3]{0:T(128)S(1)} %get-tuple-element.69.info, bf16[5,512,128]{2,1,0:T(8,128)(2,1)S(1)} %get-tuple-element.54.refs_0_, bf16[2,5,512,128]{3,2,1,0:T(8,128)(2,1)S(1)} %select_select_fusion.refs_1_, bf16[2,5,512,128]{3,2,1,0:T(8,128)(2,1)S(1)} %collective-permute-done.20.refs_2_, ...), custom_call_target="tpu_custom_call" | custom-call | flops 13421772800 | bytes 3932160 | tf_op jit(solution)/shard_map/attend/pallas_call | solution.py:222
  202.6 7.3 %attend.3 = bf16[2,512,640]{2,1,0:T(8,128)(2,1)} custom-call(s32[3]{0:T(128)S(1)} %get-tuple-element.68.info, bf16[5,512,128]{2,1,0:T(8,128)(2,1)S(1)} %get-tuple-element.46.refs_0_, bf16[2,5,512,128]{3,2,1,0:T(8,128)(2,1)S(1)} %select_select_fusion.refs_1_, ...), custom_call_target="tpu_custom_call", output_to_operand_aliasing={{}: (8, {})} | custom-call | flops 13421772800 | bytes 3932160 | tf_op jit(solution)/shard_map/attend/pallas_call | solution.py:222
  (71 shorter events, 44.6 us)
Async XLA Ops:
  3.0 17.3 %collective-permute-start = (bf16[512,1280]{1,0:T(8,128)(2,1)}, bf16[512,1280]{1,0:T(8,128)(2,1)S(1)}, u32[]{:S(2)}, u32[]{:S(2)}) collective-permute-start(bf16[512,1280]{1,0:T(8,128)(2,1)} %get-tuple-element.64), channel_id=1, source_target_pairs={{4,0},{8,4},{12,8},{16,12},{20,16},{24,20},{28,24},{5,1},{9,5},{13... | collective-permute-start | bytes 3932168 | tf_op jit(solution)/shard_map/ppermute | solution.py:318
  4.9 31.8 %collective-permute-start.1 = (bf16[512,1280]{1,0:T(8,128)(2,1)}, bf16[512,1280]{1,0:T(8,128)(2,1)}, u32[]{:S(2)}, u32[]{:S(2)}) collective-permute-start(bf16[512,1280]{1,0:T(8,128)(2,1)} %get-tuple-element.64), channel_id=1, source_target_pairs={{1,0},{2,3},{5,4},{6,7},{9,8},{10,11},{13,12},{14,15},{17,16},{18,... | collective-permute-start | bytes 3932168 | tf_op jit(solution)/shard_map/ppermute | solution.py:299
  21.4 32.0 %collective-permute-start.8 = (bf16[512,1280]{1,0:T(8,128)(2,1)S(1)}, bf16[512,1280]{1,0:T(8,128)(2,1)}, u32[]{:S(2)}, u32[]{:S(2)}) collective-permute-start(bf16[512,1280]{1,0:T(8,128)(2,1)S(1)} %fusion.5.refs_2_), channel_id=1, source_target_pairs={{0,1},{3,2},{4,5},{7,6},{8,9},{11,10},{12,13},{15,14},{16,17},{19,... | collective-permute-start | bytes 3932168 | tf_op jit(solution)/shard_map/ppermute | solution.py:299
  22.7 32.0 %collective-permute-start.9 = (bf16[512,1280]{1,0:T(8,128)(2,1)S(1)}, bf16[512,1280]{1,0:T(8,128)(2,1)}, u32[]{:S(2)}, u32[]{:S(2)}) collective-permute-start(bf16[512,1280]{1,0:T(8,128)(2,1)S(1)} %fusion.5.refs_2_), channel_id=1, source_target_pairs={{1,2},{2,1},{5,6},{6,5},{9,10},{10,9},{13,14},{14,13},{17,18},{18,... | collective-permute-start | bytes 3932168 | tf_op jit(solution)/shard_map/ppermute | solution.py:299
  26.2 39.3 %collective-permute-start.7 = (bf16[528,1280]{1,0:T(8,128)(2,1)S(1)}, bf16[528,1280]{1,0:T(8,128)(2,1)S(1)}, u32[]{:S(2)}, u32[]{:S(2)}) collective-permute-start(bf16[528,1280]{1,0:T(8,128)(2,1)S(1)} %pad_maximum_fusion), channel_id=1, source_target_pairs={{1,0},{2,3},{5,4},{6,7},{9,8},{10,11},{13,12},{14,15},{17,16},{18,... | collective-permute-start | bytes 4055048 | tf_op jit(solution)/shard_map/ppermute | solution.py:299
  36.6 32.4 %collective-permute-start.2 = (bf16[512,1280]{1,0:T(8,128)(2,1)S(1)}, bf16[512,1280]{1,0:T(8,128)(2,1)S(1)}, u32[]{:S(2)}, u32[]{:S(2)}) collective-permute-start(bf16[512,1280]{1,0:T(8,128)(2,1)S(1)} %slice_bitcast_fusion), channel_id=1, source_target_pairs={{0,4},{4,8},{8,12},{12,16},{16,20},{20,24},{24,28},{1,5},{5,9},{9,... | collective-permute-start | bytes 3932168 | tf_op jit(solution)/shard_map/ppermute | solution.py:325
  38.5 33.1 %collective-permute-start.12 = (bf16[512,1280]{1,0:T(8,128)(2,1)}, bf16[512,1280]{1,0:T(8,128)(2,1)}, u32[]{:S(2)}, u32[]{:S(2)}) collective-permute-start(bf16[512,1280]{1,0:T(8,128)(2,1)} %collective-permute-done.1), channel_id=1, source_target_pairs={{4,0},{8,4},{12,8},{16,12},{20,16},{24,20},{28,24},{5,1},{9,5},{13... | collective-permute-start | bytes 3932168 | tf_op jit(solution)/shard_map/ppermute | solution.py:327
  54.7 33.4 %collective-permute-start.10 = (bf16[512,1280]{1,0:T(8,128)(2,1)}, bf16[512,1280]{1,0:T(8,128)(2,1)}, u32[]{:S(2)}, u32[]{:S(2)}) collective-permute-start(bf16[512,1280]{1,0:T(8,128)(2,1)} %collective-permute-done.8.refs_3_), channel_id=1, source_target_pairs={{1,2},{2,1},{5,6},{6,5},{9,10},{10,9},{13,14},{14,13},{17,18},{18,... | collective-permute-start | bytes 3932168 | tf_op jit(solution)/shard_map/ppermute | solution.py:299
  58.2 35.1 %collective-permute-start.11 = (bf16[512,1280]{1,0:T(8,128)(2,1)}, bf16[512,1280]{1,0:T(8,128)(2,1)}, u32[]{:S(2)}, u32[]{:S(2)}) collective-permute-start(bf16[512,1280]{1,0:T(8,128)(2,1)} %collective-permute-done.9.refs_5_), channel_id=1, source_target_pairs={{1,0},{2,3},{5,4},{6,7},{9,8},{10,11},{13,12},{14,15},{17,16},{18,... | collective-permute-start | bytes 3932168 | tf_op jit(solution)/shard_map/ppermute | solution.py:299
  67.0 26.3 %collective-permute-start.13 = (bf16[512,1280]{1,0:T(8,128)(2,1)}, bf16[512,1280]{1,0:T(8,128)(2,1)}, u32[]{:S(2)}, u32[]{:S(2)}) collective-permute-start(bf16[512,1280]{1,0:T(8,128)(2,1)} %slice.79), channel_id=1, source_target_pairs={{0,4},{4,8},{8,12},{12,16},{16,20},{20,24},{24,28},{1,5},{5,9},{9,... | collective-permute-start | bytes 3932168 | tf_op jit(solution)/shard_map/ppermute | solution.py:332
  70.2 31.9 %collective-permute-start.3 = (bf16[512,1280]{1,0:T(8,128)(2,1)S(1)}, bf16[512,1280]{1,0:T(8,128)(2,1)}, u32[]{:S(2)}, u32[]{:S(2)}) collective-permute-start(bf16[512,1280]{1,0:T(8,128)(2,1)S(1)} %fusion.2.refs_1_), channel_id=1, source_target_pairs={{0,1},{3,2},{4,5},{7,6},{8,9},{11,10},{12,13},{15,14},{16,17},{19,... | collective-permute-start | bytes 3932168 | tf_op jit(solution)/shard_map/ppermute | solution.py:299
  71.7 44.5 %collective-permute-start.6 = (bf16[512,1280]{1,0:T(8,128)(2,1)S(1)}, bf16[512,1280]{1,0:T(8,128)(2,1)}, u32[]{:S(2)}, u32[]{:S(2)}) collective-permute-start(bf16[512,1280]{1,0:T(8,128)(2,1)S(1)} %fusion.2.refs_1_), channel_id=1, source_target_pairs={{1,2},{2,1},{5,6},{6,5},{9,10},{10,9},{13,14},{14,13},{17,18},{18,... | collective-permute-start | bytes 3932168 | tf_op jit(solution)/shard_map/ppermute | solution.py:299
  93.3 33.9 %collective-permute-start.14 = (bf16[512,1280]{1,0:T(8,128)(2,1)}, bf16[512,1280]{1,0:T(8,128)(2,1)S(1)}, u32[]{:S(2)}, u32[]{:S(2)}) collective-permute-start(bf16[512,1280]{1,0:T(8,128)(2,1)} %collective-permute-done.10.refs_7_), channel_id=1, source_target_pairs={{1,0},{2,3},{5,4},{6,7},{9,8},{10,11},{13,12},{14,15},{17,16},{18,... | collective-permute-start | bytes 3932168 | tf_op jit(solution)/shard_map/ppermute | solution.py:299
  102.9 41.0 %collective-permute-start.15 = (bf16[16,1280]{1,0:T(8,128)(2,1)S(1)}, bf16[16,1280]{1,0:T(8,128)(2,1)S(1)}, u32[]{:S(2)}, u32[]{:S(2)}) collective-permute-start(bf16[16,1280]{1,0:T(8,128)(2,1)S(1)} %slice.86), channel_id=1, source_target_pairs={{0,4},{4,0},{8,12},{12,8},{16,20},{20,16},{24,28},{28,24},{1,5},{5... | collective-permute-start | bytes 122888 | tf_op jit(solution)/shard_map/ppermute | solution.py:344
  104.8 44.0 %collective-permute-start.4 = (bf16[512,1280]{1,0:T(8,128)(2,1)}, bf16[512,1280]{1,0:T(8,128)(2,1)}, u32[]{:S(2)}, u32[]{:S(2)}) collective-permute-start(bf16[512,1280]{1,0:T(8,128)(2,1)} %collective-permute-done.3.refs_0_.refs_2_), channel_id=1, source_target_pairs={{1,2},{2,1},{5,6},{6,5},{9,10},{10,9},{13,14},{14,13},{17,18},{18,... | collective-permute-start | bytes 3932168 | tf_op jit(solution)/shard_map/ppermute | solution.py:299
  116.2 39.0 %collective-permute-start.16 = (bf16[512,1280]{1,0:T(8,128)(2,1)}, bf16[512,1280]{1,0:T(8,128)(2,1)}, u32[]{:S(2)}, u32[]{:S(2)}) collective-permute-start(bf16[512,1280]{1,0:T(8,128)(2,1)} %collective-permute-done.6.refs_1_.refs_4_), channel_id=1, source_target_pairs={{1,0},{2,3},{5,4},{6,7},{9,8},{10,11},{13,12},{14,15},{17,16},{18,... | collective-permute-start | bytes 3932168 | tf_op jit(solution)/shard_map/ppermute | solution.py:299
  143.9 25.2 %collective-permute-start.17 = (bf16[2,5,512,128]{3,2,1,0:T(8,128)(2,1)S(1)}, bf16[2,5,512,128]{3,2,1,0:T(8,128)(2,1)}, u32[]{:S(2)}, u32[]{:S(2)}) collective-permute-start(bf16[2,5,512,128]{3,2,1,0:T(8,128)(2,1)S(1)} %get-tuple-element.47.refs_3_), channel_id=1, source_target_pairs={{0,8},{1,9},{2,10},{3,11}} | collective-permute-start | bytes 3932168 | tf_op jit(solution)/shard_map/ppermute | solution.py:252
  145.2 23.9 %collective-permute-start.18 = (bf16[2,5,512,128]{3,2,1,0:T(8,128)(2,1)S(1)}, bf16[2,5,512,128]{3,2,1,0:T(8,128)(2,1)}, u32[]{:S(2)}, u32[]{:S(2)}) collective-permute-start(bf16[2,5,512,128]{3,2,1,0:T(8,128)(2,1)S(1)} %get-tuple-element.47.refs_3_), channel_id=1, source_target_pairs={{0,16},{1,17},{2,18},{3,19}} | collective-permute-start | bytes 3932168 | tf_op jit(solution)/shard_map/ppermute | solution.py:252
  146.9 22.2 %collective-permute-start.19 = (bf16[2,5,512,128]{3,2,1,0:T(8,128)(2,1)S(1)}, bf16[2,5,512,128]{3,2,1,0:T(8,128)(2,1)}, u32[]{:S(2)}, u32[]{:S(2)}) collective-permute-start(bf16[2,5,512,128]{3,2,1,0:T(8,128)(2,1)S(1)} %get-tuple-element.47.refs_3_), channel_id=1, source_target_pairs={{0,24},{1,25},{2,26},{3,27}} | collective-permute-start | bytes 3932168 | tf_op jit(solution)/shard_map/ppermute | solution.py:252
  148.8 33.3 %collective-permute-start.5 = (bf16[512,1280]{1,0:T(8,128)(2,1)}, bf16[512,1280]{1,0:T(8,128)(2,1)S(1)}, u32[]{:S(2)}, u32[]{:S(2)}) collective-permute-start(bf16[512,1280]{1,0:T(8,128)(2,1)} %collective-permute-done.4.inner), channel_id=1, source_target_pairs={{1,0},{2,3},{5,4},{6,7},{9,8},{10,11},{13,12},{14,15},{17,16},{18,... | collective-permute-start | bytes 3932168 | tf_op jit(solution)/shard_map/ppermute | solution.py:299
  170.7 23.7 %collective-permute-start.20 = (bf16[2,5,512,128]{3,2,1,0:T(8,128)(2,1)S(1)}, bf16[2,5,512,128]{3,2,1,0:T(8,128)(2,1)S(1)}, u32[]{:S(2)}, u32[]{:S(2)}) collective-permute-start(bf16[2,5,512,128]{3,2,1,0:T(8,128)(2,1)S(1)} %select_select_fusion.refs_1_), channel_id=1, source_target_pairs={{0,4},{8,12},{16,20},{24,28},{1,5},{9,13},{17,21},{25,29},{2,6},{1... | collective-permute-start | bytes 3932168 | tf_op jit(solution)/shard_map/ppermute | solution.py:253
  172.1 22.3 %collective-permute-start.21 = (bf16[2,5,320,128]{3,2,1,0:T(8,128)(2,1)S(1)}, bf16[2,5,320,128]{3,2,1,0:T(8,128)(2,1)S(1)}, u32[]{:S(2)}, u32[]{:S(2)}) collective-permute-start(bf16[2,5,320,128]{3,2,1,0:T(8,128)(2,1)S(1)} %slice.77), channel_id=1, source_target_pairs={{4,8},{8,12},{12,16},{16,20},{20,24},{24,28},{5,9},{9,13},{13,17},... | collective-permute-start | bytes 2457608 | tf_op jit(solution)/shard_map/ppermute | solution.py:350
  191.6 11.0 %collective-permute-start.23 = (bf16[2,5,512,128]{3,2,1,0:T(8,128)(2,1)S(1)}, bf16[2,5,512,128]{3,2,1,0:T(8,128)(2,1)S(1)}, u32[]{:S(2)}, u32[]{:S(2)}) collective-permute-start(bf16[2,5,512,128]{3,2,1,0:T(8,128)(2,1)S(1)} %get-tuple-element.53.refs_4_), channel_id=1, source_target_pairs={{0,4},{1,5},{2,6},{3,7}} | collective-permute-start | bytes 3932168 | tf_op jit(solution)/shard_map/ppermute | solution.py:353
  192.5 10.1 %collective-permute-start.22 = (bf16[2,5,192,128]{3,2,1,0:T(8,128)(2,1)S(1)}, bf16[2,5,192,128]{3,2,1,0:T(8,128)(2,1)S(1)}, u32[]{:S(2)}, u32[]{:S(2)}) collective-permute-start(bf16[2,5,192,128]{3,2,1,0:T(8,128)(2,1)S(1)} %slice.78), channel_id=1, source_target_pairs={{4,8},{8,12},{12,16},{16,20},{20,24},{24,28},{5,9},{9,13},{13,17},... | collective-permute-start | bytes 1474568 | tf_op jit(solution)/shard_map/ppermute | solution.py:350
  (10 other events, 110.1 us)

commit v21 on v19

--- a/solution.py
+++ b/solution.py
@@ -28,13 +28,13 @@
     kv_out[1, h] = raw[2].astype(BF16)
 
 
-def project_body(pairs, extra, final, info, *refs):
+def project_body(pairs, extra, wide, final, info, *refs):
     refs = list(refs)[extra:]
     count = len(pairs)
     groups = [[refs.pop(0) for _ in range(n)] for n in pairs]
-    weights = [refs.pop(0) for _ in range(3)]
-    gains = [refs.pop(0) for _ in range(2)] if final else None
-    outs = [refs.pop(0) for _ in range(2)] if final else None
+    weights = [refs.pop(0) for _ in range(wide)]
+    gain = refs.pop(0) if final else None
+    out = refs.pop(0) if final else None
     acc, xbuf, sem = refs
     heads = weights[0].shape[1] // DH
     step = pl.program_id(0)
@@ -68,38 +68,38 @@
         @pl.when(step == count - 1)
         def _():
             for h in range(heads):
-                total = [acc[:, (group * heads + h) * DH : (group * heads + h + 1) * DH] for group in range(3)]
-                store_head(total, [g[:, h * DH : (h + 1) * DH] for g in gains], *outs, h)
-
-
-def project(sources, info, weights, gains=None, after=(), flops=1):
+                span = slice(h * DH, (h + 1) * DH)
+                scaled = normalized(acc[:, span], gain[:, span])
+                if wide == 1:
+                    out[h] = scaled
+                else:
+                    out[0, h] = scaled
+                    out[1, h] = acc[:, (heads + h) * DH : (heads + h + 1) * DH].astype(BF16)
+
+
+def project(sources, info, weights, gain=None, after=(), flops=1):
     pairs = [len(s) for s in sources]
     count = len(pairs)
     rows, chans = sources[0][0].shape
     width = weights[0].shape[1]
     heads = width // DH
-    final = gains is not None
+    final, wide = gain is not None, len(weights)
     a_spec = pl.BlockSpec((3, heads, rows, DH), lambda k, info: (0, 0, 0, 0))
-    in_specs = [ANY] * (len(after) + sum(pairs)) + [pl.BlockSpec((chans, width), lambda k, info: (info[1 + k], 0))] * 3
+    in_specs = [ANY] * (len(after) + sum(pairs)) + [pl.BlockSpec((chans, width), lambda k, info: (info[1 + k], 0))] * wide
     args = list(after) + [x for s in sources for x in s] + list(weights)
     scratch = [pltpu.VMEM((count, rows, chans), BF16), pltpu.SemaphoreType.DMA((count,))]
     raw = jax.ShapeDtypeStruct((3, heads, rows, DH), F32)
     if final:
-        in_specs += [pl.BlockSpec((1, width), lambda k, info: (0, 0))] * 2
-        args += [g[None] for g in gains]
-        out_shape = [
-            jax.ShapeDtypeStruct((heads, rows, DH), BF16),
-            jax.ShapeDtypeStruct((2, heads, rows, DH), BF16),
-        ]
-        out_specs = [
-            pl.BlockSpec((heads, rows, DH), lambda k, info: (0, 0, 0)),
-            pl.BlockSpec((2, heads, rows, DH), lambda k, info: (0, 0, 0, 0)),
-        ]
-        scratch = [pltpu.VMEM((rows, 3 * width), F32)] + scratch
+        in_specs += [pl.BlockSpec((1, width), lambda k, info: (0, 0))]
+        args += [gain[None]]
+        shape = (heads, rows, DH) if wide == 1 else (2, heads, rows, DH)
+        out_shape = jax.ShapeDtypeStruct(shape, BF16)
+        out_specs = pl.BlockSpec(shape, lambda k, info: (0,) * len(shape))
+        scratch = [pltpu.VMEM((rows, wide * width), F32)] + scratch
     else:
         out_shape, out_specs = raw, a_spec
     return pl.pallas_call(
-        functools.partial(project_body, pairs, len(after), final),
+        functools.partial(project_body, pairs, len(after), wide, final),
         grid_spec=pltpu.PrefetchScalarGridSpec(
             num_scalar_prefetch=1,
             grid=(count,),
@@ -340,7 +340,8 @@
     cross2, second2 = send(inward2, MIDDLE), send(middle2, OUTWARD)
 
     sources1 = [(mixed1,), (inward1, first1), (middle1, second1), (cross1, third1)]
-    q1, kv1 = project(sources1, info, weights, gains, after=(inward2, middle2), flops=10**10)
+    kv1 = project(sources1, info, weights[1:], k_gain, after=(inward2, middle2), flops=10**10)
+    q1 = project(sources1, info, weights[:1], q_gain, after=(kv1,), flops=10**9)
     beside = lax.ppermute(inward2[:16], "tm", [(i, i ^ 1) for i in range(count)])
     kv1, beside = hold((kv1, beside))
     third2 = send(cross2, OUTWARD)
@@ -348,7 +349,7 @@
     cut = 3 * kv1.shape[2] // 4
     pieces = hold((kv1[:, :, :cut], kv1[:, :, cut:], anchor[0]))
     shift1 = [lax.ppermute(x, "tm", [(i, i + 1) for i in range(1, count - 1)]) for x in pieces[:2]]
-    raw2 = project([(mixed2,), (inward2, first2), (middle2, second2)], info_raw, weights, after=(beside,), flops=10**10)
+    raw2 = project([(mixed2,), (inward2, first2), (middle2, second2)], info_raw, weights, after=(beside, q1), flops=10**10)
     q2, kv2 = finish(raw2, cross2, third2, info_end, weights, gains, 10**11)
     shift2 = lax.ppermute(kv2, "tm", [(0, 1)])
     anchor, shift1[0] = hold((anchor, shift1[0]))

time: 213 us -> 213 us (level)
  the two profiles are of different devices: /device:TPU:21 before, /device:TPU:10 now
where the time goes in v21:
time: 213 us; the launch traced here: 209 us
  waiting for transfers between devices  71.9 us (34%)
  starting transfers between devices  60.1 us (28%)
  Pallas kernels  57.4 us (27%)
  other arithmetic  11.1 us (5%)
  local copies, waits for them, and re-layouts  7.53 us (4%)
    ppermute x12, waiting for transfers between devices, send(): return lax.ppermute(x, 'head', pairs)  60.1 us
    ppermute x12, starting transfers between devices, send(): return lax.ppermute(x, 'head', pairs)  37.7 us
    pallas_call x3, Pallas kernels, project(): pl.pallas_call(functools.partial(project_body, pairs, len(after), wide, f...  34.1 us
    pallas_call x2, Pallas kernels, attend(): pl.pallas_call(functools.partial(attend_body, 256, len(queries), counts,...  13.7 us
    ppermute x1, waiting for transfers between devices, per_device(): following = lax.ppermute(frames[0], 'tm', downs)  11.8 us
    pallas_call x1, Pallas kernels, finish(): pl.pallas_call(finish_body, grid_spec=pltpu.PrefetchScalarGridSpec(num_sc...  9.58 us
    convert_element_type x3, other arithmetic, mix(): (centre + taps[0] * before + taps[1] * centre + taps[2] * after).astype(B...  8.15 us
    ppermute x3, starting transfers between devices, broadcast_first(): held = jnp.where(mine == to, lax.ppermute(x, axis, [(0, to)]), held)  4.77 us
  transfers between devices with their start and end apart: 24, of which 12 were waited for; matrix products, arithmetic and copies ran while one was open for 6% of the time, Pallas kernels for 24%

profile of v21, /device:TPU:10, one launch (start us, length us, event | category | flops | bytes accessed | tf_op | source)
XLA Modules:
  0.0 208.6 jit_solution(11086517264867582996)
XLA Ops:
  4.9 3.4 %collective-permute-start.1 = (bf16[512,1280]{1,0:T(8,128)(2,1)}, bf16[512,1280]{1,0:T(8,128)(2,1)}, u32[]{:S(2)}, u32[]{:S(2)}) collective-permute-start(bf16[512,1280]{1,0:T(8,128)(2,1)} %get-tuple-element.60), channel_id=1, source_target_pairs={{1,0},{2,3},{5,4},{6,7},{9,8},{10,11},{13,12},{14,15},{17,16},{18,... | collective-permute-start | bytes 3932168 | tf_op jit(solution)/shard_map/ppermute | solution.py:299
  8.5 11.8 %collective-permute-done = bf16[512,1280]{1,0:T(8,128)(2,1)S(1)} collective-permute-done((bf16[512,1280]{1,0:T(8,128)(2,1)}, bf16[512,1280]{1,0:T(8,128)(2,1)S(1)}, u32[]{:S(2)}, u32[]{:S(2)}) %collective-permute-start) | collective-permute-done | bytes 1310752 | tf_op jit(solution)/shard_map/ppermute | solution.py:318
  23.7 3.5 %collective-permute-start.9 = (bf16[512,1280]{1,0:T(8,128)(2,1)S(1)}, bf16[512,1280]{1,0:T(8,128)(2,1)}, u32[]{:S(2)}, u32[]{:S(2)}) collective-permute-start(bf16[512,1280]{1,0:T(8,128)(2,1)S(1)} %fusion.5.refs_2_.refs_1_), channel_id=1, source_target_pairs={{1,2},{2,1},{5,6},{6,5},{9,10},{10,9},{13,14},{14,13},{17,18},{18,... | collective-permute-start | bytes 3932168 | tf_op jit(solution)/shard_map/ppermute | solution.py:299
  30.3 6.3 %collective-permute-done.1 = bf16[512,1280]{1,0:T(8,128)(2,1)} collective-permute-done((bf16[512,1280]{1,0:T(8,128)(2,1)}, bf16[512,1280]{1,0:T(8,128)(2,1)}, u32[]{:S(2)}, u32[]{:S(2)}) %collective-permute-start.1) | collective-permute-done | bytes 1310752 | tf_op jit(solution)/shard_map/ppermute | solution.py:299
  38.5 3.6 %collective-permute-start.12 = (bf16[512,1280]{1,0:T(8,128)(2,1)}, bf16[512,1280]{1,0:T(8,128)(2,1)}, u32[]{:S(2)}, u32[]{:S(2)}) collective-permute-start(bf16[512,1280]{1,0:T(8,128)(2,1)} %collective-permute-done.1), channel_id=1, source_target_pairs={{4,0},{8,4},{12,8},{16,12},{20,16},{24,20},{28,24},{5,1},{9,5},{13... | collective-permute-start | bytes 3932168 | tf_op jit(solution)/shard_map/ppermute | solution.py:327
  42.2 12.2 %collective-permute-done.8.refs_3_.refs_2_ = bf16[512,1280]{1,0:T(8,128)(2,1)S(1)} collective-permute-done((bf16[512,1280]{1,0:T(8,128)(2,1)S(1)}, bf16[512,1280]{1,0:T(8,128)(2,1)S(1)}, u32[]{:S(2)}, u32[]{:S(2)}) %collective-permute-start.8) | collective-permute-done | bytes 1310752 | tf_op jit(solution)/shard_map/ppermute | solution.py:299
  55.8 3.5 %collective-permute-start.10 = (bf16[512,1280]{1,0:T(8,128)(2,1)S(1)}, bf16[512,1280]{1,0:T(8,128)(2,1)}, u32[]{:S(2)}, u32[]{:S(2)}) collective-permute-start(bf16[512,1280]{1,0:T(8,128)(2,1)S(1)} %collective-permute-done.8.refs_3_.refs_2_), channel_id=1, source_target_pairs={{1,2},{2,1},{5,6},{6,5},{9,10},{10,9},{13,14},{14,13},{17,18},{18,... | collective-permute-start | bytes 3932168 | tf_op jit(solution)/shard_map/ppermute | solution.py:299
  61.6 3.9 %collective-permute-done.7 = bf16[528,1280]{1,0:T(8,128)(2,1)S(1)} collective-permute-done((bf16[528,1280]{1,0:T(8,128)(2,1)S(1)}, bf16[528,1280]{1,0:T(8,128)(2,1)S(1)}, u32[]{:S(2)}, u32[]{:S(2)}) %collective-permute-start.7) | collective-permute-done | bytes 1351712 | tf_op jit(solution)/shard_map/ppermute | solution.py:299
  72.4 4.6 %collective-permute-start.6 = (bf16[512,1280]{1,0:T(8,128)(2,1)}, bf16[512,1280]{1,0:T(8,128)(2,1)}, u32[]{:S(2)}, u32[]{:S(2)}) collective-permute-start(bf16[512,1280]{1,0:T(8,128)(2,1)} %fusion.2.refs_2_), channel_id=1, source_target_pairs={{1,2},{2,1},{5,6},{6,5},{9,10},{10,9},{13,14},{14,13},{17,18},{18,... | collective-permute-start | bytes 3932168 | tf_op jit(solution)/shard_map/ppermute | solution.py:299
  77.0 12.0 %collective-permute-done.10.refs_7_.refs_6_ = bf16[512,1280]{1,0:T(8,128)(2,1)} collective-permute-done((bf16[512,1280]{1,0:T(8,128)(2,1)S(1)}, bf16[512,1280]{1,0:T(8,128)(2,1)}, u32[]{:S(2)}, u32[]{:S(2)}) %collective-permute-start.10) | collective-permute-done | bytes 1310752 | tf_op jit(solution)/shard_map/ppermute | solution.py:299
  89.0 4.3 %collective-permute-done.11.refs_6_.refs_5_ = bf16[512,1280]{1,0:T(8,128)(2,1)} collective-permute-done((bf16[512,1280]{1,0:T(8,128)(2,1)}, bf16[512,1280]{1,0:T(8,128)(2,1)}, u32[]{:S(2)}, u32[]{:S(2)}) %collective-permute-start.11) | collective-permute-done | bytes 1310752 | tf_op jit(solution)/shard_map/ppermute | solution.py:299
  93.3 4.5 %collective-permute-start.14 = (bf16[512,1280]{1,0:T(8,128)(2,1)}, bf16[512,1280]{1,0:T(8,128)(2,1)S(1)}, u32[]{:S(2)}, u32[]{:S(2)}) collective-permute-start(bf16[512,1280]{1,0:T(8,128)(2,1)} %collective-permute-done.10.refs_7_.refs_6_), channel_id=1, source_target_pairs={{1,0},{2,3},{5,4},{6,7},{9,8},{10,11},{13,12},{14,15},{17,16},{18,... | collective-permute-start | bytes 3932168 | tf_op jit(solution)/shard_map/ppermute | solution.py:299
  98.7 4.3 %collective-permute-done.3.refs_0_.refs_3_ = bf16[512,1280]{1,0:T(8,128)(2,1)} collective-permute-done((bf16[512,1280]{1,0:T(8,128)(2,1)}, bf16[512,1280]{1,0:T(8,128)(2,1)}, u32[]{:S(2)}, u32[]{:S(2)}) %collective-permute-start.3) | collective-permute-done | bytes 1310752 | tf_op jit(solution)/shard_map/ppermute | solution.py:299
  105.7 4.6 %collective-permute-start.4 = (bf16[512,1280]{1,0:T(8,128)(2,1)}, bf16[512,1280]{1,0:T(8,128)(2,1)}, u32[]{:S(2)}, u32[]{:S(2)}) collective-permute-start(bf16[512,1280]{1,0:T(8,128)(2,1)} %collective-permute-done.3.refs_0_.refs_3_), channel_id=1, source_target_pairs={{1,2},{2,1},{5,6},{6,5},{9,10},{10,9},{13,14},{14,13},{17,18},{18,... | collective-permute-start | bytes 3932168 | tf_op jit(solution)/shard_map/ppermute | solution.py:299
  110.4 4.9 %fusion.11 = (bf16[512,1280]{1,0:T(8,128)(2,1)}, bf16[512,1280]{1,0:T(8,128)(2,1)}) fusion(bf16[512,1280]{1,0:T(8,128)(2,1)} %collective-permute-done.12, bf16[512,1280]{1,0:T(8,128)(2,1)} %collective-permute-done.1, bf16[512,1280]{1,0:T(8,128)(2,1)} %collective-permute-done.13, f32[1280]{0:T(1024)S(1)} %get-tuple-element.52, ...), kind=kLoop, calls=%fused_computation.19 | loop fusion | flops 17039360 | bytes 7879681 | tf_op jit(solution)/shard_map/convert_element_type | solution.py:263
  119.6 7.6 %collective-permute-done.14.refs_8_.refs_7_ = bf16[512,1280]{1,0:T(8,128)(2,1)S(1)} collective-permute-done((bf16[512,1280]{1,0:T(8,128)(2,1)}, bf16[512,1280]{1,0:T(8,128)(2,1)S(1)}, u32[]{:S(2)}, u32[]{:S(2)}) %collective-permute-start.14) | collective-permute-done | bytes 1310752 | tf_op jit(solution)/shard_map/ppermute | solution.py:299
  128.3 10.7 %project_end.2.refs_0_.refs_3_ = bf16[2,5,512,128]{3,2,1,0:T(8,128)(2,1)S(1)} custom-call(s32[5]{0:T(128)S(1)} %stack.65.info, bf16[512,1280]{1,0:T(8,128)(2,1)} %collective-permute-done.3.refs_0_.refs_3_, bf16[512,1280]{1,0:T(8,128)(2,1)} %collective-permute-done.6.refs_1_.refs_5_, bf16[512,1280]{1,0:T(8,128)(2,1)S(1)} %fusion.5.refs_2_.refs_1_, ...), custom_call_target="tpu_custom_call" | custom-call | flops 10000000000 | bytes 1 | tf_op jit(solution)/shard_map/project_end/pallas_call | solution.py:101
  145.2 3.3 %collective-permute-start.5 = (bf16[512,1280]{1,0:T(8,128)(2,1)}, bf16[512,1280]{1,0:T(8,128)(2,1)S(1)}, u32[]{:S(2)}, u32[]{:S(2)}) collective-permute-start(bf16[512,1280]{1,0:T(8,128)(2,1)} %collective-permute-done.4.inner), channel_id=1, source_target_pairs={{1,0},{2,3},{5,4},{6,7},{9,8},{10,11},{13,12},{14,15},{17,16},{18,... | collective-permute-start | bytes 3932168 | tf_op jit(solution)/shard_map/ppermute | solution.py:299
  148.7 7.8 %project_end.3.refs_1_.refs_0_ = bf16[5,512,128]{2,1,0:T(8,128)(2,1)S(1)} custom-call(s32[5]{0:T(128)S(1)} %stack.65.info, bf16[2,5,512,128]{3,2,1,0:T(8,128)(2,1)S(1)} %project_end.2.refs_0_.refs_3_, bf16[512,1280]{1,0:T(8,128)(2,1)S(1)} %fusion.5.refs_2_.refs_1_, bf16[512,1280]{1,0:T(8,128)(2,1)S(1)} %copy-done.2, bf16[512,1280]{1,0:T(8,128)(2,1)S(1)} %copy-done, ...), custom_call_target="tpu_custom_call" | custom-call | flops 1000000000 | bytes 1 | tf_op jit(solution)/shard_map/project_end/pallas_call | solution.py:101
  156.5 15.6 %project_raw.1.raw = f32[3,5,512,128]{3,2,1,0:T(8,128)} custom-call(s32[4]{0:T(128)S(1)} %pad_add_fusion.2.info, bf16[16,1280]{1,0:T(8,128)(2,1)S(1)} %collective-permute-done.15.refs_0_, bf16[5,512,128]{2,1,0:T(8,128)(2,1)S(1)} %project_end.3.refs_1_.refs_0_, bf16[512,1280]{1,0:T(8,128)(2,1)} %fusion.2.refs_2_, ...), custom_call_target="tpu_custom_call" | custom-call | flops 10000000000 | bytes 1 | tf_op jit(solution)/shard_map/project_raw/pallas_call | solution.py:101
  177.1 5.0 %collective-permute-done.5.outer = bf16[512,1280]{1,0:T(8,128)(2,1)S(1)} collective-permute-done((bf16[512,1280]{1,0:T(8,128)(2,1)}, bf16[512,1280]{1,0:T(8,128)(2,1)S(1)}, u32[]{:S(2)}, u32[]{:S(2)}) %collective-permute-start.5) | collective-permute-done | bytes 1310752 | tf_op jit(solution)/shard_map/ppermute | solution.py:299
  182.1 9.6 %finish.1 = (bf16[5,512,128]{2,1,0:T(8,128)(2,1)S(1)}, bf16[2,5,512,128]{3,2,1,0:T(8,128)(2,1)S(1)}) custom-call(s32[2]{0:T(128)S(1)} %pad_add_fusion.1.info, bf16[512,1280]{1,0:T(8,128)(2,1)} %collective-permute-done.4.inner, bf16[512,1280]{1,0:T(8,128)(2,1)S(1)} %collective-permute-done.5.outer, bf16[5120,640]{1,0:T(8,128)(2,1)} %wq.1, ...), custom_call_target="tpu_custom_call" | custom-call | flops 99999997952 | bytes 1 | tf_op jit(solution)/shard_map/finish/pallas_call | solution.py:139
  194.6 6.5 %attend.2.refs_7_ = bf16[2,512,640]{2,1,0:T(8,128)(2,1)} custom-call(s32[3]{0:T(128)S(1)} %get-tuple-element.65.info, bf16[5,512,128]{2,1,0:T(8,128)(2,1)S(1)} %project_end.3.refs_1_.refs_0_, bf16[2,5,512,128]{3,2,1,0:T(8,128)(2,1)S(1)} %select_select_fusion.refs_1_, bf16[2,5,512,128]{3,2,1,0:T(8,128)(2,1)S(1)} %collective-permute-done.20.refs_2_, ...), custom_call_target="tpu_custom_call" | custom-call | flops 13421772800 | bytes 3932160 | tf_op jit(solution)/shard_map/attend/pallas_call | solution.py:222
  201.1 7.3 %attend.3 = bf16[2,512,640]{2,1,0:T(8,128)(2,1)} custom-call(s32[3]{0:T(128)S(1)} %get-tuple-element.64.info, bf16[5,512,128]{2,1,0:T(8,128)(2,1)S(1)} %get-tuple-element.43.refs_0_, bf16[2,5,512,128]{3,2,1,0:T(8,128)(2,1)S(1)} %select_select_fusion.refs_1_, ...), custom_call_target="tpu_custom_call", output_to_operand_aliasing={{}: (8, {})} | custom-call | flops 13421772800 | bytes 3932160 | tf_op jit(solution)/shard_map/attend/pallas_call | solution.py:222
  (76 shorter events, 47.4 us)
Async XLA Ops:
  3.0 17.3 %collective-permute-start = (bf16[512,1280]{1,0:T(8,128)(2,1)}, bf16[512,1280]{1,0:T(8,128)(2,1)S(1)}, u32[]{:S(2)}, u32[]{:S(2)}) collective-permute-start(bf16[512,1280]{1,0:T(8,128)(2,1)} %get-tuple-element.60), channel_id=1, source_target_pairs={{4,0},{8,4},{12,8},{16,12},{20,16},{24,20},{28,24},{5,1},{9,5},{13... | collective-permute-start | bytes 3932168 | tf_op jit(solution)/shard_map/ppermute | solution.py:318
  4.9 31.8 %collective-permute-start.1 = (bf16[512,1280]{1,0:T(8,128)(2,1)}, bf16[512,1280]{1,0:T(8,128)(2,1)}, u32[]{:S(2)}, u32[]{:S(2)}) collective-permute-start(bf16[512,1280]{1,0:T(8,128)(2,1)} %get-tuple-element.60), channel_id=1, source_target_pairs={{1,0},{2,3},{5,4},{6,7},{9,8},{10,11},{13,12},{14,15},{17,16},{18,... | collective-permute-start | bytes 3932168 | tf_op jit(solution)/shard_map/ppermute | solution.py:299
  22.4 31.9 %collective-permute-start.8 = (bf16[512,1280]{1,0:T(8,128)(2,1)S(1)}, bf16[512,1280]{1,0:T(8,128)(2,1)S(1)}, u32[]{:S(2)}, u32[]{:S(2)}) collective-permute-start(bf16[512,1280]{1,0:T(8,128)(2,1)S(1)} %fusion.5.refs_2_.refs_1_), channel_id=1, source_target_pairs={{0,1},{3,2},{4,5},{7,6},{8,9},{11,10},{12,13},{15,14},{16,17},{19,... | collective-permute-start | bytes 3932168 | tf_op jit(solution)/shard_map/ppermute | solution.py:299
  23.7 32.0 %collective-permute-start.9 = (bf16[512,1280]{1,0:T(8,128)(2,1)S(1)}, bf16[512,1280]{1,0:T(8,128)(2,1)}, u32[]{:S(2)}, u32[]{:S(2)}) collective-permute-start(bf16[512,1280]{1,0:T(8,128)(2,1)S(1)} %fusion.5.refs_2_.refs_1_), channel_id=1, source_target_pairs={{1,2},{2,1},{5,6},{6,5},{9,10},{10,9},{13,14},{14,13},{17,18},{18,... | collective-permute-start | bytes 3932168 | tf_op jit(solution)/shard_map/ppermute | solution.py:299
  27.2 38.2 %collective-permute-start.7 = (bf16[528,1280]{1,0:T(8,128)(2,1)S(1)}, bf16[528,1280]{1,0:T(8,128)(2,1)S(1)}, u32[]{:S(2)}, u32[]{:S(2)}) collective-permute-start(bf16[528,1280]{1,0:T(8,128)(2,1)S(1)} %pad_maximum_fusion), channel_id=1, source_target_pairs={{1,0},{2,3},{5,4},{6,7},{9,8},{10,11},{13,12},{14,15},{17,16},{18,... | collective-permute-start | bytes 4055048 | tf_op jit(solution)/shard_map/ppermute | solution.py:299
  36.6 32.2 %collective-permute-start.2 = (bf16[512,1280]{1,0:T(8,128)(2,1)S(1)}, bf16[512,1280]{1,0:T(8,128)(2,1)S(1)}, u32[]{:S(2)}, u32[]{:S(2)}) collective-permute-start(bf16[512,1280]{1,0:T(8,128)(2,1)S(1)} %slice_bitcast_fusion), channel_id=1, source_target_pairs={{0,4},{4,8},{8,12},{12,16},{16,20},{20,24},{24,28},{1,5},{5,9},{9,... | collective-permute-start | bytes 3932168 | tf_op jit(solution)/shard_map/ppermute | solution.py:325
  38.5 33.9 %collective-permute-start.12 = (bf16[512,1280]{1,0:T(8,128)(2,1)}, bf16[512,1280]{1,0:T(8,128)(2,1)}, u32[]{:S(2)}, u32[]{:S(2)}) collective-permute-start(bf16[512,1280]{1,0:T(8,128)(2,1)} %collective-permute-done.1), channel_id=1, source_target_pairs={{4,0},{8,4},{12,8},{16,12},{20,16},{24,20},{28,24},{5,1},{9,5},{13... | collective-permute-start | bytes 3932168 | tf_op jit(solution)/shard_map/ppermute | solution.py:327
  55.8 33.2 %collective-permute-start.10 = (bf16[512,1280]{1,0:T(8,128)(2,1)S(1)}, bf16[512,1280]{1,0:T(8,128)(2,1)}, u32[]{:S(2)}, u32[]{:S(2)}) collective-permute-start(bf16[512,1280]{1,0:T(8,128)(2,1)S(1)} %collective-permute-done.8.refs_3_.refs_2_), channel_id=1, source_target_pairs={{1,2},{2,1},{5,6},{6,5},{9,10},{10,9},{13,14},{14,13},{17,18},{18,... | collective-permute-start | bytes 3932168 | tf_op jit(solution)/shard_map/ppermute | solution.py:299
  59.3 34.0 %collective-permute-start.11 = (bf16[512,1280]{1,0:T(8,128)(2,1)}, bf16[512,1280]{1,0:T(8,128)(2,1)}, u32[]{:S(2)}, u32[]{:S(2)}) collective-permute-start(bf16[512,1280]{1,0:T(8,128)(2,1)} %collective-permute-done.9.refs_5_.refs_4_), channel_id=1, source_target_pairs={{1,0},{2,3},{5,4},{6,7},{9,8},{10,11},{13,12},{14,15},{17,16},{18,... | collective-permute-start | bytes 3932168 | tf_op jit(solution)/shard_map/ppermute | solution.py:299
  66.7 26.6 %collective-permute-start.13 = (bf16[512,1280]{1,0:T(8,128)(2,1)}, bf16[512,1280]{1,0:T(8,128)(2,1)}, u32[]{:S(2)}, u32[]{:S(2)}) collective-permute-start(bf16[512,1280]{1,0:T(8,128)(2,1)} %slice.79), channel_id=1, source_target_pairs={{0,4},{4,8},{8,12},{12,16},{16,20},{20,24},{24,28},{1,5},{5,9},{9,... | collective-permute-start | bytes 3932168 | tf_op jit(solution)/shard_map/ppermute | solution.py:332
  71.0 32.1 %collective-permute-start.3 = (bf16[512,1280]{1,0:T(8,128)(2,1)}, bf16[512,1280]{1,0:T(8,128)(2,1)}, u32[]{:S(2)}, u32[]{:S(2)}) collective-permute-start(bf16[512,1280]{1,0:T(8,128)(2,1)} %fusion.2.refs_2_), channel_id=1, source_target_pairs={{0,1},{3,2},{4,5},{7,6},{8,9},{11,10},{12,13},{15,14},{16,17},{19,... | collective-permute-start | bytes 3932168 | tf_op jit(solution)/shard_map/ppermute | solution.py:299
  72.4 44.7 %collective-permute-start.6 = (bf16[512,1280]{1,0:T(8,128)(2,1)}, bf16[512,1280]{1,0:T(8,128)(2,1)}, u32[]{:S(2)}, u32[]{:S(2)}) collective-permute-start(bf16[512,1280]{1,0:T(8,128)(2,1)} %fusion.2.refs_2_), channel_id=1, source_target_pairs={{1,2},{2,1},{5,6},{6,5},{9,10},{10,9},{13,14},{14,13},{17,18},{18,... | collective-permute-start | bytes 3932168 | tf_op jit(solution)/shard_map/ppermute | solution.py:299
  93.3 33.9 %collective-permute-start.14 = (bf16[512,1280]{1,0:T(8,128)(2,1)}, bf16[512,1280]{1,0:T(8,128)(2,1)S(1)}, u32[]{:S(2)}, u32[]{:S(2)}) collective-permute-start(bf16[512,1280]{1,0:T(8,128)(2,1)} %collective-permute-done.10.refs_7_.refs_6_), channel_id=1, source_target_pairs={{1,0},{2,3},{5,4},{6,7},{9,8},{10,11},{13,12},{14,15},{17,16},{18,... | collective-permute-start | bytes 3932168 | tf_op jit(solution)/shard_map/ppermute | solution.py:299
  103.8 35.1 %collective-permute-start.15 = (bf16[16,1280]{1,0:T(8,128)(2,1)S(1)}, bf16[16,1280]{1,0:T(8,128)(2,1)S(1)}, u32[]{:S(2)}, u32[]{:S(2)}) collective-permute-start(bf16[16,1280]{1,0:T(8,128)(2,1)S(1)} %slice.86), channel_id=1, source_target_pairs={{0,4},{4,0},{8,12},{12,8},{16,20},{20,16},{24,28},{28,24},{1,5},{5... | collective-permute-start | bytes 122888 | tf_op jit(solution)/shard_map/ppermute | solution.py:345
  105.7 39.4 %collective-permute-start.4 = (bf16[512,1280]{1,0:T(8,128)(2,1)}, bf16[512,1280]{1,0:T(8,128)(2,1)}, u32[]{:S(2)}, u32[]{:S(2)}) collective-permute-start(bf16[512,1280]{1,0:T(8,128)(2,1)} %collective-permute-done.3.refs_0_.refs_3_), channel_id=1, source_target_pairs={{1,2},{2,1},{5,6},{6,5},{9,10},{10,9},{13,14},{14,13},{17,18},{18,... | collective-permute-start | bytes 3932168 | tf_op jit(solution)/shard_map/ppermute | solution.py:299
  117.1 39.3 %collective-permute-start.16 = (bf16[512,1280]{1,0:T(8,128)(2,1)}, bf16[512,1280]{1,0:T(8,128)(2,1)}, u32[]{:S(2)}, u32[]{:S(2)}) collective-permute-start(bf16[512,1280]{1,0:T(8,128)(2,1)} %collective-permute-done.6.refs_1_.refs_5_), channel_id=1, source_target_pairs={{1,0},{2,3},{5,4},{6,7},{9,8},{10,11},{13,12},{14,15},{17,16},{18,... | collective-permute-start | bytes 3932168 | tf_op jit(solution)/shard_map/ppermute | solution.py:299
  139.0 33.1 %collective-permute-start.17 = (bf16[2,5,512,128]{3,2,1,0:T(8,128)(2,1)S(1)}, bf16[2,5,512,128]{3,2,1,0:T(8,128)(2,1)}, u32[]{:S(2)}, u32[]{:S(2)}) collective-permute-start(bf16[2,5,512,128]{3,2,1,0:T(8,128)(2,1)S(1)} %project_end.2.refs_0_.refs_3_), channel_id=1, source_target_pairs={{0,8},{1,9},{2,10},{3,11}} | collective-permute-start | bytes 3932168 | tf_op jit(solution)/shard_map/ppermute | solution.py:252
  140.3 31.9 %collective-permute-start.18 = (bf16[2,5,512,128]{3,2,1,0:T(8,128)(2,1)S(1)}, bf16[2,5,512,128]{3,2,1,0:T(8,128)(2,1)}, u32[]{:S(2)}, u32[]{:S(2)}) collective-permute-start(bf16[2,5,512,128]{3,2,1,0:T(8,128)(2,1)S(1)} %project_end.2.refs_0_.refs_3_), channel_id=1, source_target_pairs={{0,16},{1,17},{2,18},{3,19}} | collective-permute-start | bytes 3932168 | tf_op jit(solution)/shard_map/ppermute | solution.py:252
  142.0 30.1 %collective-permute-start.19 = (bf16[2,5,512,128]{3,2,1,0:T(8,128)(2,1)S(1)}, bf16[2,5,512,128]{3,2,1,0:T(8,128)(2,1)}, u32[]{:S(2)}, u32[]{:S(2)}) collective-permute-start(bf16[2,5,512,128]{3,2,1,0:T(8,128)(2,1)S(1)} %project_end.2.refs_0_.refs_3_), channel_id=1, source_target_pairs={{0,24},{1,25},{2,26},{3,27}} | collective-permute-start | bytes 3932168 | tf_op jit(solution)/shard_map/ppermute | solution.py:252
  145.2 36.9 %collective-permute-start.5 = (bf16[512,1280]{1,0:T(8,128)(2,1)}, bf16[512,1280]{1,0:T(8,128)(2,1)S(1)}, u32[]{:S(2)}, u32[]{:S(2)}) collective-permute-start(bf16[512,1280]{1,0:T(8,128)(2,1)} %collective-permute-done.4.inner), channel_id=1, source_target_pairs={{1,0},{2,3},{5,4},{6,7},{9,8},{10,11},{13,12},{14,15},{17,16},{18,... | collective-permute-start | bytes 3932168 | tf_op jit(solution)/shard_map/ppermute | solution.py:299
  173.8 20.8 %collective-permute-start.20 = (bf16[2,5,512,128]{3,2,1,0:T(8,128)(2,1)S(1)}, bf16[2,5,512,128]{3,2,1,0:T(8,128)(2,1)S(1)}, u32[]{:S(2)}, u32[]{:S(2)}) collective-permute-start(bf16[2,5,512,128]{3,2,1,0:T(8,128)(2,1)S(1)} %select_select_fusion.refs_1_), channel_id=1, source_target_pairs={{0,4},{8,12},{16,20},{24,28},{1,5},{9,13},{17,21},{25,29},{2,6},{1... | collective-permute-start | bytes 3932168 | tf_op jit(solution)/shard_map/ppermute | solution.py:253
  175.2 19.4 %collective-permute-start.21 = (bf16[2,5,384,128]{3,2,1,0:T(8,128)(2,1)S(1)}, bf16[2,5,384,128]{3,2,1,0:T(8,128)(2,1)S(1)}, u32[]{:S(2)}, u32[]{:S(2)}) collective-permute-start(bf16[2,5,384,128]{3,2,1,0:T(8,128)(2,1)S(1)} %slice.77), channel_id=1, source_target_pairs={{4,8},{8,12},{12,16},{16,20},{20,24},{24,28},{5,9},{9,13},{13,17},... | collective-permute-start | bytes 2949128 | tf_op jit(solution)/shard_map/ppermute | solution.py:351
  191.6 9.5 %collective-permute-start.23 = (bf16[2,5,512,128]{3,2,1,0:T(8,128)(2,1)S(1)}, bf16[2,5,512,128]{3,2,1,0:T(8,128)(2,1)S(1)}, u32[]{:S(2)}, u32[]{:S(2)}) collective-permute-start(bf16[2,5,512,128]{3,2,1,0:T(8,128)(2,1)S(1)} %get-tuple-element.50.refs_4_), channel_id=1, source_target_pairs={{0,4},{1,5},{2,6},{3,7}} | collective-permute-start | bytes 3932168 | tf_op jit(solution)/shard_map/ppermute | solution.py:354
  192.5 8.6 %collective-permute-start.22 = (bf16[2,5,128,128]{3,2,1,0:T(8,128)(2,1)S(1)}, bf16[2,5,128,128]{3,2,1,0:T(8,128)(2,1)S(1)}, u32[]{:S(2)}, u32[]{:S(2)}) collective-permute-start(bf16[2,5,128,128]{3,2,1,0:T(8,128)(2,1)S(1)} %slice.78), channel_id=1, source_target_pairs={{4,8},{8,12},{12,16},{16,20},{20,24},{24,28},{5,9},{9,13},{13,17},... | collective-permute-start | bytes 983048 | tf_op jit(solution)/shard_map/ppermute | solution.py:351
  (12 other events, 127.1 us)

commit v22 on v21

--- a/solution.py
+++ b/solution.py
@@ -346,7 +346,7 @@
     kv1, beside = hold((kv1, beside))
     third2 = send(cross2, OUTWARD)
     anchor = broadcast_first(kv1, "tm")
-    cut = 3 * kv1.shape[2] // 4
+    cut = 5 * kv1.shape[2] // 8
     pieces = hold((kv1[:, :, :cut], kv1[:, :, cut:], anchor[0]))
     shift1 = [lax.ppermute(x, "tm", [(i, i + 1) for i in range(1, count - 1)]) for x in pieces[:2]]
     raw2 = project([(mixed2,), (inward2, first2), (middle2, second2)], info_raw, weights, after=(beside, q1), flops=10**10)

time: 213 us -> 213 us (level)
  transfers between devices with their start and end apart: 24 -> 24, of which waited for: 12 -> 13; matrix products, arithmetic and copies ran while one was open for 6% -> 6% of each run, Pallas kernels for 24% -> 24%
where the time goes in v22:
time: 213 us; the launch traced here: 210 us
  waiting for transfers between devices  73.4 us (34%)
  starting transfers between devices  60.1 us (28%)
  Pallas kernels  57.4 us (27%)
  other arithmetic  11.1 us (5%)
  local copies, waits for them, and re-layouts  7.53 us (4%)
    ppermute x12, waiting for transfers between devices, send(): return lax.ppermute(x, 'head', pairs)  60.1 us
    ppermute x12, starting transfers between devices, send(): return lax.ppermute(x, 'head', pairs)  37.7 us
    pallas_call x3, Pallas kernels, project(): pl.pallas_call(functools.partial(project_body, pairs, len(after), wide, f...  34.1 us
    pallas_call x2, Pallas kernels, attend(): pl.pallas_call(functools.partial(attend_body, 256, len(queries), counts,...  13.7 us
    ppermute x1, waiting for transfers between devices, per_device(): following = lax.ppermute(frames[0], 'tm', downs)  11.8 us
    pallas_call x1, Pallas kernels, finish(): pl.pallas_call(finish_body, grid_spec=pltpu.PrefetchScalarGridSpec(num_sc...  9.58 us
    convert_element_type x3, other arithmetic, mix(): (centre + taps[0] * before + taps[1] * centre + taps[2] * after).astype(B...  8.15 us
    ppermute x3, starting transfers between devices, broadcast_first(): held = jnp.where(mine == to, lax.ppermute(x, axis, [(0, to)]), held)  4.77 us
  transfers between devices with their start and end apart: 24, of which 13 were waited for; matrix products, arithmetic and copies ran while one was open for 6% of the time, Pallas kernels for 24%

profile of v22, /device:TPU:10, one launch (start us, length us, event | category | flops | bytes accessed | tf_op | source)
XLA Modules:
  0.0 210.1 jit_solution(3388153115147227253)
XLA Ops:
  4.9 3.4 %collective-permute-start.1 = (bf16[512,1280]{1,0:T(8,128)(2,1)}, bf16[512,1280]{1,0:T(8,128)(2,1)}, u32[]{:S(2)}, u32[]{:S(2)}) collective-permute-start(bf16[512,1280]{1,0:T(8,128)(2,1)} %get-tuple-element.60), channel_id=1, source_target_pairs={{1,0},{2,3},{5,4},{6,7},{9,8},{10,11},{13,12},{14,15},{17,16},{18,... | collective-permute-start | bytes 3932168 | tf_op jit(solution)/shard_map/ppermute | solution.py:299
  8.5 11.8 %collective-permute-done = bf16[512,1280]{1,0:T(8,128)(2,1)S(1)} collective-permute-done((bf16[512,1280]{1,0:T(8,128)(2,1)}, bf16[512,1280]{1,0:T(8,128)(2,1)S(1)}, u32[]{:S(2)}, u32[]{:S(2)}) %collective-permute-start) | collective-permute-done | bytes 1310752 | tf_op jit(solution)/shard_map/ppermute | solution.py:318
  23.7 3.5 %collective-permute-start.9 = (bf16[512,1280]{1,0:T(8,128)(2,1)S(1)}, bf16[512,1280]{1,0:T(8,128)(2,1)}, u32[]{:S(2)}, u32[]{:S(2)}) collective-permute-start(bf16[512,1280]{1,0:T(8,128)(2,1)S(1)} %fusion.5.refs_2_.refs_1_), channel_id=1, source_target_pairs={{1,2},{2,1},{5,6},{6,5},{9,10},{10,9},{13,14},{14,13},{17,18},{18,... | collective-permute-start | bytes 3932168 | tf_op jit(solution)/shard_map/ppermute | solution.py:299
  30.3 6.3 %collective-permute-done.1 = bf16[512,1280]{1,0:T(8,128)(2,1)} collective-permute-done((bf16[512,1280]{1,0:T(8,128)(2,1)}, bf16[512,1280]{1,0:T(8,128)(2,1)}, u32[]{:S(2)}, u32[]{:S(2)}) %collective-permute-start.1) | collective-permute-done | bytes 1310752 | tf_op jit(solution)/shard_map/ppermute | solution.py:299
  38.5 3.6 %collective-permute-start.12 = (bf16[512,1280]{1,0:T(8,128)(2,1)}, bf16[512,1280]{1,0:T(8,128)(2,1)}, u32[]{:S(2)}, u32[]{:S(2)}) collective-permute-start(bf16[512,1280]{1,0:T(8,128)(2,1)} %collective-permute-done.1), channel_id=1, source_target_pairs={{4,0},{8,4},{12,8},{16,12},{20,16},{24,20},{28,24},{5,1},{9,5},{13... | collective-permute-start | bytes 3932168 | tf_op jit(solution)/shard_map/ppermute | solution.py:327
  42.2 12.2 %collective-permute-done.8.refs_3_.refs_2_ = bf16[512,1280]{1,0:T(8,128)(2,1)S(1)} collective-permute-done((bf16[512,1280]{1,0:T(8,128)(2,1)S(1)}, bf16[512,1280]{1,0:T(8,128)(2,1)S(1)}, u32[]{:S(2)}, u32[]{:S(2)}) %collective-permute-start.8) | collective-permute-done | bytes 1310752 | tf_op jit(solution)/shard_map/ppermute | solution.py:299
  55.8 3.5 %collective-permute-start.10 = (bf16[512,1280]{1,0:T(8,128)(2,1)S(1)}, bf16[512,1280]{1,0:T(8,128)(2,1)}, u32[]{:S(2)}, u32[]{:S(2)}) collective-permute-start(bf16[512,1280]{1,0:T(8,128)(2,1)S(1)} %collective-permute-done.8.refs_3_.refs_2_), channel_id=1, source_target_pairs={{1,2},{2,1},{5,6},{6,5},{9,10},{10,9},{13,14},{14,13},{17,18},{18,... | collective-permute-start | bytes 3932168 | tf_op jit(solution)/shard_map/ppermute | solution.py:299
  61.6 3.9 %collective-permute-done.7 = bf16[528,1280]{1,0:T(8,128)(2,1)S(1)} collective-permute-done((bf16[528,1280]{1,0:T(8,128)(2,1)S(1)}, bf16[528,1280]{1,0:T(8,128)(2,1)S(1)}, u32[]{:S(2)}, u32[]{:S(2)}) %collective-permute-start.7) | collective-permute-done | bytes 1351712 | tf_op jit(solution)/shard_map/ppermute | solution.py:299
  72.4 4.6 %collective-permute-start.6 = (bf16[512,1280]{1,0:T(8,128)(2,1)}, bf16[512,1280]{1,0:T(8,128)(2,1)}, u32[]{:S(2)}, u32[]{:S(2)}) collective-permute-start(bf16[512,1280]{1,0:T(8,128)(2,1)} %fusion.2.refs_2_), channel_id=1, source_target_pairs={{1,2},{2,1},{5,6},{6,5},{9,10},{10,9},{13,14},{14,13},{17,18},{18,... | collective-permute-start | bytes 3932168 | tf_op jit(solution)/shard_map/ppermute | solution.py:299
  77.0 12.0 %collective-permute-done.10.refs_7_.refs_6_ = bf16[512,1280]{1,0:T(8,128)(2,1)} collective-permute-done((bf16[512,1280]{1,0:T(8,128)(2,1)S(1)}, bf16[512,1280]{1,0:T(8,128)(2,1)}, u32[]{:S(2)}, u32[]{:S(2)}) %collective-permute-start.10) | collective-permute-done | bytes 1310752 | tf_op jit(solution)/shard_map/ppermute | solution.py:299
  89.0 4.3 %collective-permute-done.11.refs_6_.refs_5_ = bf16[512,1280]{1,0:T(8,128)(2,1)} collective-permute-done((bf16[512,1280]{1,0:T(8,128)(2,1)}, bf16[512,1280]{1,0:T(8,128)(2,1)}, u32[]{:S(2)}, u32[]{:S(2)}) %collective-permute-start.11) | collective-permute-done | bytes 1310752 | tf_op jit(solution)/shard_map/ppermute | solution.py:299
  93.3 4.5 %collective-permute-start.14 = (bf16[512,1280]{1,0:T(8,128)(2,1)}, bf16[512,1280]{1,0:T(8,128)(2,1)S(1)}, u32[]{:S(2)}, u32[]{:S(2)}) collective-permute-start(bf16[512,1280]{1,0:T(8,128)(2,1)} %collective-permute-done.10.refs_7_.refs_6_), channel_id=1, source_target_pairs={{1,0},{2,3},{5,4},{6,7},{9,8},{10,11},{13,12},{14,15},{17,16},{18,... | collective-permute-start | bytes 3932168 | tf_op jit(solution)/shard_map/ppermute | solution.py:299
  98.7 4.3 %collective-permute-done.3.refs_0_.refs_3_ = bf16[512,1280]{1,0:T(8,128)(2,1)} collective-permute-done((bf16[512,1280]{1,0:T(8,128)(2,1)}, bf16[512,1280]{1,0:T(8,128)(2,1)}, u32[]{:S(2)}, u32[]{:S(2)}) %collective-permute-start.3) | collective-permute-done | bytes 1310752 | tf_op jit(solution)/shard_map/ppermute | solution.py:299
  105.7 4.6 %collective-permute-start.4 = (bf16[512,1280]{1,0:T(8,128)(2,1)}, bf16[512,1280]{1,0:T(8,128)(2,1)}, u32[]{:S(2)}, u32[]{:S(2)}) collective-permute-start(bf16[512,1280]{1,0:T(8,128)(2,1)} %collective-permute-done.3.refs_0_.refs_3_), channel_id=1, source_target_pairs={{1,2},{2,1},{5,6},{6,5},{9,10},{10,9},{13,14},{14,13},{17,18},{18,... | collective-permute-start | bytes 3932168 | tf_op jit(solution)/shard_map/ppermute | solution.py:299
  110.4 4.9 %fusion.11 = (bf16[512,1280]{1,0:T(8,128)(2,1)}, bf16[512,1280]{1,0:T(8,128)(2,1)}) fusion(bf16[512,1280]{1,0:T(8,128)(2,1)} %collective-permute-done.12, bf16[512,1280]{1,0:T(8,128)(2,1)} %collective-permute-done.1, bf16[512,1280]{1,0:T(8,128)(2,1)} %collective-permute-done.13, f32[1280]{0:T(1024)S(1)} %get-tuple-element.52, ...), kind=kLoop, calls=%fused_computation.19 | loop fusion | flops 17039360 | bytes 7879681 | tf_op jit(solution)/shard_map/convert_element_type | solution.py:263
  119.6 7.6 %collective-permute-done.14.refs_8_.refs_7_ = bf16[512,1280]{1,0:T(8,128)(2,1)S(1)} collective-permute-done((bf16[512,1280]{1,0:T(8,128)(2,1)}, bf16[512,1280]{1,0:T(8,128)(2,1)S(1)}, u32[]{:S(2)}, u32[]{:S(2)}) %collective-permute-start.14) | collective-permute-done | bytes 1310752 | tf_op jit(solution)/shard_map/ppermute | solution.py:299
  128.3 10.7 %project_end.2.refs_0_.refs_3_ = bf16[2,5,512,128]{3,2,1,0:T(8,128)(2,1)S(1)} custom-call(s32[5]{0:T(128)S(1)} %stack.65.info, bf16[512,1280]{1,0:T(8,128)(2,1)} %collective-permute-done.3.refs_0_.refs_3_, bf16[512,1280]{1,0:T(8,128)(2,1)} %collective-permute-done.6.refs_1_.refs_5_, bf16[512,1280]{1,0:T(8,128)(2,1)S(1)} %fusion.5.refs_2_.refs_1_, ...), custom_call_target="tpu_custom_call" | custom-call | flops 10000000000 | bytes 1 | tf_op jit(solution)/shard_map/project_end/pallas_call | solution.py:101
  145.2 3.3 %collective-permute-start.5 = (bf16[512,1280]{1,0:T(8,128)(2,1)}, bf16[512,1280]{1,0:T(8,128)(2,1)S(1)}, u32[]{:S(2)}, u32[]{:S(2)}) collective-permute-start(bf16[512,1280]{1,0:T(8,128)(2,1)} %collective-permute-done.4.inner), channel_id=1, source_target_pairs={{1,0},{2,3},{5,4},{6,7},{9,8},{10,11},{13,12},{14,15},{17,16},{18,... | collective-permute-start | bytes 3932168 | tf_op jit(solution)/shard_map/ppermute | solution.py:299
  148.7 7.8 %project_end.3.refs_1_.refs_0_ = bf16[5,512,128]{2,1,0:T(8,128)(2,1)S(1)} custom-call(s32[5]{0:T(128)S(1)} %stack.65.info, bf16[2,5,512,128]{3,2,1,0:T(8,128)(2,1)S(1)} %project_end.2.refs_0_.refs_3_, bf16[512,1280]{1,0:T(8,128)(2,1)S(1)} %fusion.5.refs_2_.refs_1_, bf16[512,1280]{1,0:T(8,128)(2,1)S(1)} %copy-done.2, bf16[512,1280]{1,0:T(8,128)(2,1)S(1)} %copy-done, ...), custom_call_target="tpu_custom_call" | custom-call | flops 1000000000 | bytes 1 | tf_op jit(solution)/shard_map/project_end/pallas_call | solution.py:101
  156.5 15.6 %project_raw.1.raw = f32[3,5,512,128]{3,2,1,0:T(8,128)} custom-call(s32[4]{0:T(128)S(1)} %pad_add_fusion.2.info, bf16[16,1280]{1,0:T(8,128)(2,1)S(1)} %collective-permute-done.15.refs_0_, bf16[5,512,128]{2,1,0:T(8,128)(2,1)S(1)} %project_end.3.refs_1_.refs_0_, bf16[512,1280]{1,0:T(8,128)(2,1)} %fusion.2.refs_2_, ...), custom_call_target="tpu_custom_call" | custom-call | flops 10000000000 | bytes 1 | tf_op jit(solution)/shard_map/project_raw/pallas_call | solution.py:101
  177.1 5.0 %collective-permute-done.5.outer = bf16[512,1280]{1,0:T(8,128)(2,1)S(1)} collective-permute-done((bf16[512,1280]{1,0:T(8,128)(2,1)}, bf16[512,1280]{1,0:T(8,128)(2,1)S(1)}, u32[]{:S(2)}, u32[]{:S(2)}) %collective-permute-start.5) | collective-permute-done | bytes 1310752 | tf_op jit(solution)/shard_map/ppermute | solution.py:299
  182.1 9.6 %finish.1 = (bf16[5,512,128]{2,1,0:T(8,128)(2,1)S(1)}, bf16[2,5,512,128]{3,2,1,0:T(8,128)(2,1)S(1)}) custom-call(s32[2]{0:T(128)S(1)} %pad_add_fusion.1.info, bf16[512,1280]{1,0:T(8,128)(2,1)} %collective-permute-done.4.inner, bf16[512,1280]{1,0:T(8,128)(2,1)S(1)} %collective-permute-done.5.outer, bf16[5120,640]{1,0:T(8,128)(2,1)} %wq.1, ...), custom_call_target="tpu_custom_call" | custom-call | flops 99999997952 | bytes 1 | tf_op jit(solution)/shard_map/finish/pallas_call | solution.py:139
  194.6 6.5 %attend.2.refs_7_ = bf16[2,512,640]{2,1,0:T(8,128)(2,1)} custom-call(s32[3]{0:T(128)S(1)} %get-tuple-element.65.info, bf16[5,512,128]{2,1,0:T(8,128)(2,1)S(1)} %project_end.3.refs_1_.refs_0_, bf16[2,5,512,128]{3,2,1,0:T(8,128)(2,1)S(1)} %select_select_fusion.refs_1_, bf16[2,5,512,128]{3,2,1,0:T(8,128)(2,1)S(1)} %collective-permute-done.20.refs_2_, ...), custom_call_target="tpu_custom_call" | custom-call | flops 13421772800 | bytes 3932160 | tf_op jit(solution)/shard_map/attend/pallas_call | solution.py:222
  202.6 7.3 %attend.3 = bf16[2,512,640]{2,1,0:T(8,128)(2,1)} custom-call(s32[3]{0:T(128)S(1)} %get-tuple-element.64.info, bf16[5,512,128]{2,1,0:T(8,128)(2,1)S(1)} %get-tuple-element.43.refs_0_, bf16[2,5,512,128]{3,2,1,0:T(8,128)(2,1)S(1)} %select_select_fusion.refs_1_, ...), custom_call_target="tpu_custom_call", output_to_operand_aliasing={{}: (8, {})} | custom-call | flops 13421772800 | bytes 3932160 | tf_op jit(solution)/shard_map/attend/pallas_call | solution.py:222
  (76 shorter events, 48.9 us)
Async XLA Ops:
  3.0 17.3 %collective-permute-start = (bf16[512,1280]{1,0:T(8,128)(2,1)}, bf16[512,1280]{1,0:T(8,128)(2,1)S(1)}, u32[]{:S(2)}, u32[]{:S(2)}) collective-permute-start(bf16[512,1280]{1,0:T(8,128)(2,1)} %get-tuple-element.60), channel_id=1, source_target_pairs={{4,0},{8,4},{12,8},{16,12},{20,16},{24,20},{28,24},{5,1},{9,5},{13... | collective-permute-start | bytes 3932168 | tf_op jit(solution)/shard_map/ppermute | solution.py:318
  4.9 31.8 %collective-permute-start.1 = (bf16[512,1280]{1,0:T(8,128)(2,1)}, bf16[512,1280]{1,0:T(8,128)(2,1)}, u32[]{:S(2)}, u32[]{:S(2)}) collective-permute-start(bf16[512,1280]{1,0:T(8,128)(2,1)} %get-tuple-element.60), channel_id=1, source_target_pairs={{1,0},{2,3},{5,4},{6,7},{9,8},{10,11},{13,12},{14,15},{17,16},{18,... | collective-permute-start | bytes 3932168 | tf_op jit(solution)/shard_map/ppermute | solution.py:299
  22.4 31.9 %collective-permute-start.8 = (bf16[512,1280]{1,0:T(8,128)(2,1)S(1)}, bf16[512,1280]{1,0:T(8,128)(2,1)S(1)}, u32[]{:S(2)}, u32[]{:S(2)}) collective-permute-start(bf16[512,1280]{1,0:T(8,128)(2,1)S(1)} %fusion.5.refs_2_.refs_1_), channel_id=1, source_target_pairs={{0,1},{3,2},{4,5},{7,6},{8,9},{11,10},{12,13},{15,14},{16,17},{19,... | collective-permute-start | bytes 3932168 | tf_op jit(solution)/shard_map/ppermute | solution.py:299
  23.7 32.0 %collective-permute-start.9 = (bf16[512,1280]{1,0:T(8,128)(2,1)S(1)}, bf16[512,1280]{1,0:T(8,128)(2,1)}, u32[]{:S(2)}, u32[]{:S(2)}) collective-permute-start(bf16[512,1280]{1,0:T(8,128)(2,1)S(1)} %fusion.5.refs_2_.refs_1_), channel_id=1, source_target_pairs={{1,2},{2,1},{5,6},{6,5},{9,10},{10,9},{13,14},{14,13},{17,18},{18,... | collective-permute-start | bytes 3932168 | tf_op jit(solution)/shard_map/ppermute | solution.py:299
  27.2 38.2 %collective-permute-start.7 = (bf16[528,1280]{1,0:T(8,128)(2,1)S(1)}, bf16[528,1280]{1,0:T(8,128)(2,1)S(1)}, u32[]{:S(2)}, u32[]{:S(2)}) collective-permute-start(bf16[528,1280]{1,0:T(8,128)(2,1)S(1)} %pad_maximum_fusion), channel_id=1, source_target_pairs={{1,0},{2,3},{5,4},{6,7},{9,8},{10,11},{13,12},{14,15},{17,16},{18,... | collective-permute-start | bytes 4055048 | tf_op jit(solution)/shard_map/ppermute | solution.py:299
  36.6 32.2 %collective-permute-start.2 = (bf16[512,1280]{1,0:T(8,128)(2,1)S(1)}, bf16[512,1280]{1,0:T(8,128)(2,1)S(1)}, u32[]{:S(2)}, u32[]{:S(2)}) collective-permute-start(bf16[512,1280]{1,0:T(8,128)(2,1)S(1)} %slice_bitcast_fusion), channel_id=1, source_target_pairs={{0,4},{4,8},{8,12},{12,16},{16,20},{20,24},{24,28},{1,5},{5,9},{9,... | collective-permute-start | bytes 3932168 | tf_op jit(solution)/shard_map/ppermute | solution.py:325
  38.5 33.9 %collective-permute-start.12 = (bf16[512,1280]{1,0:T(8,128)(2,1)}, bf16[512,1280]{1,0:T(8,128)(2,1)}, u32[]{:S(2)}, u32[]{:S(2)}) collective-permute-start(bf16[512,1280]{1,0:T(8,128)(2,1)} %collective-permute-done.1), channel_id=1, source_target_pairs={{4,0},{8,4},{12,8},{16,12},{20,16},{24,20},{28,24},{5,1},{9,5},{13... | collective-permute-start | bytes 3932168 | tf_op jit(solution)/shard_map/ppermute | solution.py:327
  55.8 33.2 %collective-permute-start.10 = (bf16[512,1280]{1,0:T(8,128)(2,1)S(1)}, bf16[512,1280]{1,0:T(8,128)(2,1)}, u32[]{:S(2)}, u32[]{:S(2)}) collective-permute-start(bf16[512,1280]{1,0:T(8,128)(2,1)S(1)} %collective-permute-done.8.refs_3_.refs_2_), channel_id=1, source_target_pairs={{1,2},{2,1},{5,6},{6,5},{9,10},{10,9},{13,14},{14,13},{17,18},{18,... | collective-permute-start | bytes 3932168 | tf_op jit(solution)/shard_map/ppermute | solution.py:299
  59.3 34.0 %collective-permute-start.11 = (bf16[512,1280]{1,0:T(8,128)(2,1)}, bf16[512,1280]{1,0:T(8,128)(2,1)}, u32[]{:S(2)}, u32[]{:S(2)}) collective-permute-start(bf16[512,1280]{1,0:T(8,128)(2,1)} %collective-permute-done.9.refs_5_.refs_4_), channel_id=1, source_target_pairs={{1,0},{2,3},{5,4},{6,7},{9,8},{10,11},{13,12},{14,15},{17,16},{18,... | collective-permute-start | bytes 3932168 | tf_op jit(solution)/shard_map/ppermute | solution.py:299
  66.7 26.6 %collective-permute-start.13 = (bf16[512,1280]{1,0:T(8,128)(2,1)}, bf16[512,1280]{1,0:T(8,128)(2,1)}, u32[]{:S(2)}, u32[]{:S(2)}) collective-permute-start(bf16[512,1280]{1,0:T(8,128)(2,1)} %slice.79), channel_id=1, source_target_pairs={{0,4},{4,8},{8,12},{12,16},{16,20},{20,24},{24,28},{1,5},{5,9},{9,... | collective-permute-start | bytes 3932168 | tf_op jit(solution)/shard_map/ppermute | solution.py:332
  71.0 32.1 %collective-permute-start.3 = (bf16[512,1280]{1,0:T(8,128)(2,1)}, bf16[512,1280]{1,0:T(8,128)(2,1)}, u32[]{:S(2)}, u32[]{:S(2)}) collective-permute-start(bf16[512,1280]{1,0:T(8,128)(2,1)} %fusion.2.refs_2_), channel_id=1, source_target_pairs={{0,1},{3,2},{4,5},{7,6},{8,9},{11,10},{12,13},{15,14},{16,17},{19,... | collective-permute-start | bytes 3932168 | tf_op jit(solution)/shard_map/ppermute | solution.py:299
  72.4 44.7 %collective-permute-start.6 = (bf16[512,1280]{1,0:T(8,128)(2,1)}, bf16[512,1280]{1,0:T(8,128)(2,1)}, u32[]{:S(2)}, u32[]{:S(2)}) collective-permute-start(bf16[512,1280]{1,0:T(8,128)(2,1)} %fusion.2.refs_2_), channel_id=1, source_target_pairs={{1,2},{2,1},{5,6},{6,5},{9,10},{10,9},{13,14},{14,13},{17,18},{18,... | collective-permute-start | bytes 3932168 | tf_op jit(solution)/shard_map/ppermute | solution.py:299
  93.3 33.9 %collective-permute-start.14 = (bf16[512,1280]{1,0:T(8,128)(2,1)}, bf16[512,1280]{1,0:T(8,128)(2,1)S(1)}, u32[]{:S(2)}, u32[]{:S(2)}) collective-permute-start(bf16[512,1280]{1,0:T(8,128)(2,1)} %collective-permute-done.10.refs_7_.refs_6_), channel_id=1, source_target_pairs={{1,0},{2,3},{5,4},{6,7},{9,8},{10,11},{13,12},{14,15},{17,16},{18,... | collective-permute-start | bytes 3932168 | tf_op jit(solution)/shard_map/ppermute | solution.py:299
  103.8 35.1 %collective-permute-start.15 = (bf16[16,1280]{1,0:T(8,128)(2,1)S(1)}, bf16[16,1280]{1,0:T(8,128)(2,1)S(1)}, u32[]{:S(2)}, u32[]{:S(2)}) collective-permute-start(bf16[16,1280]{1,0:T(8,128)(2,1)S(1)} %slice.86), channel_id=1, source_target_pairs={{0,4},{4,0},{8,12},{12,8},{16,20},{20,16},{24,28},{28,24},{1,5},{5... | collective-permute-start | bytes 122888 | tf_op jit(solution)/shard_map/ppermute | solution.py:345
  105.7 39.4 %collective-permute-start.4 = (bf16[512,1280]{1,0:T(8,128)(2,1)}, bf16[512,1280]{1,0:T(8,128)(2,1)}, u32[]{:S(2)}, u32[]{:S(2)}) collective-permute-start(bf16[512,1280]{1,0:T(8,128)(2,1)} %collective-permute-done.3.refs_0_.refs_3_), channel_id=1, source_target_pairs={{1,2},{2,1},{5,6},{6,5},{9,10},{10,9},{13,14},{14,13},{17,18},{18,... | collective-permute-start | bytes 3932168 | tf_op jit(solution)/shard_map/ppermute | solution.py:299
  117.1 39.3 %collective-permute-start.16 = (bf16[512,1280]{1,0:T(8,128)(2,1)}, bf16[512,1280]{1,0:T(8,128)(2,1)}, u32[]{:S(2)}, u32[]{:S(2)}) collective-permute-start(bf16[512,1280]{1,0:T(8,128)(2,1)} %collective-permute-done.6.refs_1_.refs_5_), channel_id=1, source_target_pairs={{1,0},{2,3},{5,4},{6,7},{9,8},{10,11},{13,12},{14,15},{17,16},{18,... | collective-permute-start | bytes 3932168 | tf_op jit(solution)/shard_map/ppermute | solution.py:299
  139.0 33.1 %collective-permute-start.17 = (bf16[2,5,512,128]{3,2,1,0:T(8,128)(2,1)S(1)}, bf16[2,5,512,128]{3,2,1,0:T(8,128)(2,1)}, u32[]{:S(2)}, u32[]{:S(2)}) collective-permute-start(bf16[2,5,512,128]{3,2,1,0:T(8,128)(2,1)S(1)} %project_end.2.refs_0_.refs_3_), channel_id=1, source_target_pairs={{0,8},{1,9},{2,10},{3,11}} | collective-permute-start | bytes 3932168 | tf_op jit(solution)/shard_map/ppermute | solution.py:252
  140.3 31.9 %collective-permute-start.18 = (bf16[2,5,512,128]{3,2,1,0:T(8,128)(2,1)S(1)}, bf16[2,5,512,128]{3,2,1,0:T(8,128)(2,1)}, u32[]{:S(2)}, u32[]{:S(2)}) collective-permute-start(bf16[2,5,512,128]{3,2,1,0:T(8,128)(2,1)S(1)} %project_end.2.refs_0_.refs_3_), channel_id=1, source_target_pairs={{0,16},{1,17},{2,18},{3,19}} | collective-permute-start | bytes 3932168 | tf_op jit(solution)/shard_map/ppermute | solution.py:252
  142.0 30.1 %collective-permute-start.19 = (bf16[2,5,512,128]{3,2,1,0:T(8,128)(2,1)S(1)}, bf16[2,5,512,128]{3,2,1,0:T(8,128)(2,1)}, u32[]{:S(2)}, u32[]{:S(2)}) collective-permute-start(bf16[2,5,512,128]{3,2,1,0:T(8,128)(2,1)S(1)} %project_end.2.refs_0_.refs_3_), channel_id=1, source_target_pairs={{0,24},{1,25},{2,26},{3,27}} | collective-permute-start | bytes 3932168 | tf_op jit(solution)/shard_map/ppermute | solution.py:252
  145.2 36.9 %collective-permute-start.5 = (bf16[512,1280]{1,0:T(8,128)(2,1)}, bf16[512,1280]{1,0:T(8,128)(2,1)S(1)}, u32[]{:S(2)}, u32[]{:S(2)}) collective-permute-start(bf16[512,1280]{1,0:T(8,128)(2,1)} %collective-permute-done.4.inner), channel_id=1, source_target_pairs={{1,0},{2,3},{5,4},{6,7},{9,8},{10,11},{13,12},{14,15},{17,16},{18,... | collective-permute-start | bytes 3932168 | tf_op jit(solution)/shard_map/ppermute | solution.py:299
  173.8 20.8 %collective-permute-start.20 = (bf16[2,5,512,128]{3,2,1,0:T(8,128)(2,1)S(1)}, bf16[2,5,512,128]{3,2,1,0:T(8,128)(2,1)S(1)}, u32[]{:S(2)}, u32[]{:S(2)}) collective-permute-start(bf16[2,5,512,128]{3,2,1,0:T(8,128)(2,1)S(1)} %select_select_fusion.refs_1_), channel_id=1, source_target_pairs={{0,4},{8,12},{16,20},{24,28},{1,5},{9,13},{17,21},{25,29},{2,6},{1... | collective-permute-start | bytes 3932168 | tf_op jit(solution)/shard_map/ppermute | solution.py:253
  175.2 19.4 %collective-permute-start.21 = (bf16[2,5,320,128]{3,2,1,0:T(8,128)(2,1)S(1)}, bf16[2,5,320,128]{3,2,1,0:T(8,128)(2,1)S(1)}, u32[]{:S(2)}, u32[]{:S(2)}) collective-permute-start(bf16[2,5,320,128]{3,2,1,0:T(8,128)(2,1)S(1)} %slice.77), channel_id=1, source_target_pairs={{4,8},{8,12},{12,16},{16,20},{20,24},{24,28},{5,9},{9,13},{13,17},... | collective-permute-start | bytes 2457608 | tf_op jit(solution)/shard_map/ppermute | solution.py:351
  191.6 11.0 %collective-permute-start.23 = (bf16[2,5,512,128]{3,2,1,0:T(8,128)(2,1)S(1)}, bf16[2,5,512,128]{3,2,1,0:T(8,128)(2,1)S(1)}, u32[]{:S(2)}, u32[]{:S(2)}) collective-permute-start(bf16[2,5,512,128]{3,2,1,0:T(8,128)(2,1)S(1)} %get-tuple-element.50.refs_4_), channel_id=1, source_target_pairs={{0,4},{1,5},{2,6},{3,7}} | collective-permute-start | bytes 3932168 | tf_op jit(solution)/shard_map/ppermute | solution.py:354
  192.5 10.1 %collective-permute-start.22 = (bf16[2,5,192,128]{3,2,1,0:T(8,128)(2,1)S(1)}, bf16[2,5,192,128]{3,2,1,0:T(8,128)(2,1)S(1)}, u32[]{:S(2)}, u32[]{:S(2)}) collective-permute-start(bf16[2,5,192,128]{3,2,1,0:T(8,128)(2,1)S(1)} %slice.78), channel_id=1, source_target_pairs={{4,8},{8,12},{12,16},{16,20},{20,24},{24,28},{5,9},{9,13},{13,17},... | collective-permute-start | bytes 1474568 | tf_op jit(solution)/shard_map/ppermute | solution.py:351
  (12 other events, 127.1 us)

commit v23 on v22

--- a/solution.py
+++ b/solution.py
@@ -346,7 +346,7 @@
     kv1, beside = hold((kv1, beside))
     third2 = send(cross2, OUTWARD)
     anchor = broadcast_first(kv1, "tm")
-    cut = 5 * kv1.shape[2] // 8
+    cut = kv1.shape[2] // 2
     pieces = hold((kv1[:, :, :cut], kv1[:, :, cut:], anchor[0]))
     shift1 = [lax.ppermute(x, "tm", [(i, i + 1) for i in range(1, count - 1)]) for x in pieces[:2]]
     raw2 = project([(mixed2,), (inward2, first2), (middle2, second2)], info_raw, weights, after=(beside, q1), flops=10**10)

time: 213 us -> 214 us (level)
  local copies, waits for them, and re-layouts: 7.53 us -> 12 us
    ppermute x12, waiting for transfers between devices: 60.1 us -> 56.6 us  [send(): return lax.ppermute(x, 'head', pairs)]
    unnamed x24 -> x32, local copies, waits for them, and re-layouts: 2.22 us -> 5.3 us
  transfers between devices with their start and end apart: 24 -> 24, of which waited for: 13 -> 13; matrix products, arithmetic and copies ran while one was open for 6% -> 6% of each run, Pallas kernels for 24% -> 23%
where the time goes in v23:
time: 214 us; the launch traced here: 212 us
  waiting for transfers between devices  71.6 us (33%)
  starting transfers between devices  62.1 us (29%)
  Pallas kernels  55.5 us (26%)
  local copies, waits for them, and re-layouts  12 us (6%)
  other arithmetic  9.98 us (5%)
    ppermute x12, waiting for transfers between devices, send(): return lax.ppermute(x, 'head', pairs)  56.6 us
    ppermute x12, starting transfers between devices, send(): return lax.ppermute(x, 'head', pairs)  39.7 us
    pallas_call x3, Pallas kernels, project(): pl.pallas_call(functools.partial(project_body, pairs, len(after), wide, f...  32.2 us
    pallas_call x2, Pallas kernels, attend(): pl.pallas_call(functools.partial(attend_body, 256, len(queries), counts,...  13.7 us
    ppermute x1, waiting for transfers between devices, per_device(): following = lax.ppermute(frames[0], 'tm', downs)  11.8 us
    pallas_call x1, Pallas kernels, finish(): pl.pallas_call(finish_body, grid_spec=pltpu.PrefetchScalarGridSpec(num_sc...  9.58 us
    convert_element_type x3, other arithmetic, mix(): (centre + taps[0] * before + taps[1] * centre + taps[2] * after).astype(B...  7.14 us
    unnamed x32, local copies, waits for them, and re-layouts  5.3 us
  transfers between devices with their start and end apart: 24, of which 13 were waited for; matrix products, arithmetic and copies ran while one was open for 6% of the time, Pallas kernels for 23%

profile of v23, /device:TPU:10, one launch (start us, length us, event | category | flops | bytes accessed | tf_op | source)
XLA Modules:
  0.0 211.8 jit_solution(5219493409989281683)
XLA Ops:
  4.9 3.4 %collective-permute-start.1 = (bf16[512,1280]{1,0:T(8,128)(2,1)}, bf16[512,1280]{1,0:T(8,128)(2,1)}, u32[]{:S(2)}, u32[]{:S(2)}) collective-permute-start(bf16[512,1280]{1,0:T(8,128)(2,1)} %get-tuple-element.60), channel_id=1, source_target_pairs={{1,0},{2,3},{5,4},{6,7},{9,8},{10,11},{13,12},{14,15},{17,16},{18,... | collective-permute-start | bytes 3932168 | tf_op jit(solution)/shard_map/ppermute | solution.py:299
  8.5 11.8 %collective-permute-done = bf16[512,1280]{1,0:T(8,128)(2,1)S(1)} collective-permute-done((bf16[512,1280]{1,0:T(8,128)(2,1)}, bf16[512,1280]{1,0:T(8,128)(2,1)S(1)}, u32[]{:S(2)}, u32[]{:S(2)}) %collective-permute-start) | collective-permute-done | bytes 1310752 | tf_op jit(solution)/shard_map/ppermute | solution.py:318
  22.7 3.5 %collective-permute-start.9 = (bf16[512,1280]{1,0:T(8,128)(2,1)S(1)}, bf16[512,1280]{1,0:T(8,128)(2,1)}, u32[]{:S(2)}, u32[]{:S(2)}) collective-permute-start(bf16[512,1280]{1,0:T(8,128)(2,1)S(1)} %fusion.5.refs_2_.refs_1_), channel_id=1, source_target_pairs={{1,2},{2,1},{5,6},{6,5},{9,10},{10,9},{13,14},{14,13},{17,18},{18,... | collective-permute-start | bytes 3932168 | tf_op jit(solution)/shard_map/ppermute | solution.py:299
  26.2 4.0 %collective-permute-start.7 = (bf16[528,1280]{1,0:T(8,128)(2,1)S(1)}, bf16[528,1280]{1,0:T(8,128)(2,1)}, u32[]{:S(2)}, u32[]{:S(2)}) collective-permute-start(bf16[528,1280]{1,0:T(8,128)(2,1)S(1)} %pad_maximum_fusion), channel_id=1, source_target_pairs={{1,0},{2,3},{5,4},{6,7},{9,8},{10,11},{13,12},{14,15},{17,16},{18,... | collective-permute-start | bytes 4055048 | tf_op jit(solution)/shard_map/ppermute | solution.py:299
  30.3 6.3 %collective-permute-done.1 = bf16[512,1280]{1,0:T(8,128)(2,1)} collective-permute-done((bf16[512,1280]{1,0:T(8,128)(2,1)}, bf16[512,1280]{1,0:T(8,128)(2,1)}, u32[]{:S(2)}, u32[]{:S(2)}) %collective-permute-start.1) | collective-permute-done | bytes 1310752 | tf_op jit(solution)/shard_map/ppermute | solution.py:299
  38.5 3.6 %collective-permute-start.12 = (bf16[512,1280]{1,0:T(8,128)(2,1)}, bf16[512,1280]{1,0:T(8,128)(2,1)}, u32[]{:S(2)}, u32[]{:S(2)}) collective-permute-start(bf16[512,1280]{1,0:T(8,128)(2,1)} %collective-permute-done.1), channel_id=1, source_target_pairs={{4,0},{8,4},{12,8},{16,12},{20,16},{24,20},{28,24},{5,1},{9,5},{13... | collective-permute-start | bytes 3932168 | tf_op jit(solution)/shard_map/ppermute | solution.py:327
  42.2 11.1 %collective-permute-done.8.refs_3_.refs_2_ = bf16[512,1280]{1,0:T(8,128)(2,1)S(1)} collective-permute-done((bf16[512,1280]{1,0:T(8,128)(2,1)S(1)}, bf16[512,1280]{1,0:T(8,128)(2,1)S(1)}, u32[]{:S(2)}, u32[]{:S(2)}) %collective-permute-start.8) | collective-permute-done | bytes 1310752 | tf_op jit(solution)/shard_map/ppermute | solution.py:299
  54.7 3.5 %collective-permute-start.10 = (bf16[512,1280]{1,0:T(8,128)(2,1)S(1)}, bf16[512,1280]{1,0:T(8,128)(2,1)}, u32[]{:S(2)}, u32[]{:S(2)}) collective-permute-start(bf16[512,1280]{1,0:T(8,128)(2,1)S(1)} %collective-permute-done.8.refs_3_.refs_2_), channel_id=1, source_target_pairs={{1,2},{2,1},{5,6},{6,5},{9,10},{10,9},{13,14},{14,13},{17,18},{18,... | collective-permute-start | bytes 3932168 | tf_op jit(solution)/shard_map/ppermute | solution.py:299
  60.6 4.9 %collective-permute-done.7 = bf16[528,1280]{1,0:T(8,128)(2,1)} collective-permute-done((bf16[528,1280]{1,0:T(8,128)(2,1)S(1)}, bf16[528,1280]{1,0:T(8,128)(2,1)}, u32[]{:S(2)}, u32[]{:S(2)}) %collective-permute-start.7) | collective-permute-done | bytes 1351712 | tf_op jit(solution)/shard_map/ppermute | solution.py:299
  72.8 4.6 %collective-permute-start.6 = (bf16[512,1280]{1,0:T(8,128)(2,1)S(1)}, bf16[512,1280]{1,0:T(8,128)(2,1)}, u32[]{:S(2)}, u32[]{:S(2)}) collective-permute-start(bf16[512,1280]{1,0:T(8,128)(2,1)S(1)} %fusion.2.refs_2_), channel_id=1, source_target_pairs={{1,2},{2,1},{5,6},{6,5},{9,10},{10,9},{13,14},{14,13},{17,18},{18,... | collective-permute-start | bytes 3932168 | tf_op jit(solution)/shard_map/ppermute | solution.py:299
  77.4 10.5 %collective-permute-done.10.refs_7_.refs_6_ = bf16[512,1280]{1,0:T(8,128)(2,1)} collective-permute-done((bf16[512,1280]{1,0:T(8,128)(2,1)S(1)}, bf16[512,1280]{1,0:T(8,128)(2,1)}, u32[]{:S(2)}, u32[]{:S(2)}) %collective-permute-start.10) | collective-permute-done | bytes 1310752 | tf_op jit(solution)/shard_map/ppermute | solution.py:299
  87.9 5.4 %collective-permute-done.11.refs_6_.refs_5_ = bf16[512,1280]{1,0:T(8,128)(2,1)} collective-permute-done((bf16[512,1280]{1,0:T(8,128)(2,1)}, bf16[512,1280]{1,0:T(8,128)(2,1)}, u32[]{:S(2)}, u32[]{:S(2)}) %collective-permute-start.11) | collective-permute-done | bytes 1310752 | tf_op jit(solution)/shard_map/ppermute | solution.py:299
  93.3 4.5 %collective-permute-start.14 = (bf16[512,1280]{1,0:T(8,128)(2,1)}, bf16[512,1280]{1,0:T(8,128)(2,1)S(1)}, u32[]{:S(2)}, u32[]{:S(2)}) collective-permute-start(bf16[512,1280]{1,0:T(8,128)(2,1)} %collective-permute-done.10.refs_7_.refs_6_), channel_id=1, source_target_pairs={{1,0},{2,3},{5,4},{6,7},{9,8},{10,11},{13,12},{14,15},{17,16},{18,... | collective-permute-start | bytes 3932168 | tf_op jit(solution)/shard_map/ppermute | solution.py:299
  98.7 4.3 %collective-permute-done.3.refs_0_.refs_3_ = bf16[512,1280]{1,0:T(8,128)(2,1)} collective-permute-done((bf16[512,1280]{1,0:T(8,128)(2,1)S(1)}, bf16[512,1280]{1,0:T(8,128)(2,1)}, u32[]{:S(2)}, u32[]{:S(2)}) %collective-permute-start.3) | collective-permute-done | bytes 1310752 | tf_op jit(solution)/shard_map/ppermute | solution.py:299
  105.8 4.6 %collective-permute-start.4 = (bf16[512,1280]{1,0:T(8,128)(2,1)}, bf16[512,1280]{1,0:T(8,128)(2,1)}, u32[]{:S(2)}, u32[]{:S(2)}) collective-permute-start(bf16[512,1280]{1,0:T(8,128)(2,1)} %collective-permute-done.3.refs_0_.refs_3_), channel_id=1, source_target_pairs={{1,2},{2,1},{5,6},{6,5},{9,10},{10,9},{13,14},{14,13},{17,18},{18,... | collective-permute-start | bytes 3932168 | tf_op jit(solution)/shard_map/ppermute | solution.py:299
  110.5 4.9 %fusion.11 = (bf16[512,1280]{1,0:T(8,128)(2,1)}, bf16[512,1280]{1,0:T(8,128)(2,1)}) fusion(bf16[512,1280]{1,0:T(8,128)(2,1)} %collective-permute-done.12, bf16[512,1280]{1,0:T(8,128)(2,1)} %collective-permute-done.1, bf16[512,1280]{1,0:T(8,128)(2,1)} %collective-permute-done.13, f32[1280]{0:T(1024)S(1)} %get-tuple-element.52, ...), kind=kLoop, calls=%fused_computation.19 | loop fusion | flops 17039360 | bytes 7879681 | tf_op jit(solution)/shard_map/convert_element_type | solution.py:263
  118.5 8.7 %collective-permute-done.14.refs_8_.refs_7_ = bf16[512,1280]{1,0:T(8,128)(2,1)S(1)} collective-permute-done((bf16[512,1280]{1,0:T(8,128)(2,1)}, bf16[512,1280]{1,0:T(8,128)(2,1)S(1)}, u32[]{:S(2)}, u32[]{:S(2)}) %collective-permute-start.14) | collective-permute-done | bytes 1310752 | tf_op jit(solution)/shard_map/ppermute | solution.py:299
  128.2 10.7 %project_end.2.refs_0_.refs_3_ = bf16[2,5,512,128]{3,2,1,0:T(8,128)(2,1)S(1)} custom-call(s32[5]{0:T(128)S(1)} %stack.65.info, bf16[512,1280]{1,0:T(8,128)(2,1)} %collective-permute-done.3.refs_0_.refs_3_, bf16[512,1280]{1,0:T(8,128)(2,1)} %collective-permute-done.6.refs_1_.refs_5_, bf16[512,1280]{1,0:T(8,128)(2,1)S(1)} %copy-done.2, ...), custom_call_target="tpu_custom_call" | custom-call | flops 10000000000 | bytes 1 | tf_op jit(solution)/shard_map/project_end/pallas_call | solution.py:101
  144.1 4.2 %collective-permute-start.5 = (bf16[512,1280]{1,0:T(8,128)(2,1)}, bf16[512,1280]{1,0:T(8,128)(2,1)S(1)}, u32[]{:S(2)}, u32[]{:S(2)}) collective-permute-start(bf16[512,1280]{1,0:T(8,128)(2,1)} %collective-permute-done.4.inner), channel_id=1, source_target_pairs={{1,0},{2,3},{5,4},{6,7},{9,8},{10,11},{13,12},{14,15},{17,16},{18,... | collective-permute-start | bytes 3932168 | tf_op jit(solution)/shard_map/ppermute | solution.py:299
  150.9 7.8 %project_end.3.refs_1_.refs_0_ = bf16[5,512,128]{2,1,0:T(8,128)(2,1)S(1)} custom-call(s32[5]{0:T(128)S(1)} %stack.65.info, bf16[2,5,512,128]{3,2,1,0:T(8,128)(2,1)S(1)} %project_end.2.refs_0_.refs_3_, bf16[512,1280]{1,0:T(8,128)(2,1)S(1)} %copy-done.3, bf16[512,1280]{1,0:T(8,128)(2,1)S(1)} %copy-done.5, bf16[512,1280]{1,0:T(8,128)(2,1)S(1)} %copy-done, ...), custom_call_target="tpu_custom_call" | custom-call | flops 1000000000 | bytes 1 | tf_op jit(solution)/shard_map/project_end/pallas_call | solution.py:101
  160.4 13.7 %project_raw.1.raw = f32[3,5,512,128]{3,2,1,0:T(8,128)} custom-call(s32[4]{0:T(128)S(1)} %pad_add_fusion.2.info, bf16[16,1280]{1,0:T(8,128)(2,1)S(1)} %collective-permute-done.15.refs_0_, bf16[5,512,128]{2,1,0:T(8,128)(2,1)S(1)} %project_end.3.refs_1_.refs_0_, bf16[512,1280]{1,0:T(8,128)(2,1)S(1)} %copy-done.8, ...), custom_call_target="tpu_custom_call" | custom-call | flops 10000000000 | bytes 1 | tf_op jit(solution)/shard_map/project_raw/pallas_call | solution.py:101
  182.1 9.6 %finish.1 = (bf16[5,512,128]{2,1,0:T(8,128)(2,1)S(1)}, bf16[2,5,512,128]{3,2,1,0:T(8,128)(2,1)S(1)}) custom-call(s32[2]{0:T(128)S(1)} %pad_add_fusion.1.info, bf16[512,1280]{1,0:T(8,128)(2,1)} %collective-permute-done.4.inner, bf16[512,1280]{1,0:T(8,128)(2,1)S(1)} %collective-permute-done.5.outer, bf16[5120,640]{1,0:T(8,128)(2,1)} %wq.1, ...), custom_call_target="tpu_custom_call" | custom-call | flops 99999997952 | bytes 1 | tf_op jit(solution)/shard_map/finish/pallas_call | solution.py:139
  194.6 6.5 %attend.2.refs_7_ = bf16[2,512,640]{2,1,0:T(8,128)(2,1)} custom-call(s32[3]{0:T(128)S(1)} %get-tuple-element.67.info, bf16[5,512,128]{2,1,0:T(8,128)(2,1)S(1)} %project_end.3.refs_1_.refs_0_, bf16[2,5,512,128]{3,2,1,0:T(8,128)(2,1)S(1)} %select_select_fusion.refs_1_, bf16[2,5,512,128]{3,2,1,0:T(8,128)(2,1)S(1)} %collective-permute-done.20.refs_2_, ...), custom_call_target="tpu_custom_call" | custom-call | flops 13421772800 | bytes 3932160 | tf_op jit(solution)/shard_map/attend/pallas_call | solution.py:222
  204.4 7.3 %attend.3 = bf16[2,512,640]{2,1,0:T(8,128)(2,1)} custom-call(s32[3]{0:T(128)S(1)} %get-tuple-element.66.info, bf16[5,512,128]{2,1,0:T(8,128)(2,1)S(1)} %get-tuple-element.43.refs_0_, bf16[2,5,512,128]{3,2,1,0:T(8,128)(2,1)S(1)} %select_select_fusion.refs_1_, ...), custom_call_target="tpu_custom_call", output_to_operand_aliasing={{}: (8, {})} | custom-call | flops 13421772800 | bytes 3932160 | tf_op jit(solution)/shard_map/attend/pallas_call | solution.py:222
  (83 shorter events, 51.9 us)
Async XLA Ops:
  3.0 17.3 %collective-permute-start = (bf16[512,1280]{1,0:T(8,128)(2,1)}, bf16[512,1280]{1,0:T(8,128)(2,1)S(1)}, u32[]{:S(2)}, u32[]{:S(2)}) collective-permute-start(bf16[512,1280]{1,0:T(8,128)(2,1)} %get-tuple-element.60), channel_id=1, source_target_pairs={{4,0},{8,4},{12,8},{16,12},{20,16},{24,20},{28,24},{5,1},{9,5},{13... | collective-permute-start | bytes 3932168 | tf_op jit(solution)/shard_map/ppermute | solution.py:318
  4.9 31.8 %collective-permute-start.1 = (bf16[512,1280]{1,0:T(8,128)(2,1)}, bf16[512,1280]{1,0:T(8,128)(2,1)}, u32[]{:S(2)}, u32[]{:S(2)}) collective-permute-start(bf16[512,1280]{1,0:T(8,128)(2,1)} %get-tuple-element.60), channel_id=1, source_target_pairs={{1,0},{2,3},{5,4},{6,7},{9,8},{10,11},{13,12},{14,15},{17,16},{18,... | collective-permute-start | bytes 3932168 | tf_op jit(solution)/shard_map/ppermute | solution.py:299
  21.4 31.9 %collective-permute-start.8 = (bf16[512,1280]{1,0:T(8,128)(2,1)S(1)}, bf16[512,1280]{1,0:T(8,128)(2,1)S(1)}, u32[]{:S(2)}, u32[]{:S(2)}) collective-permute-start(bf16[512,1280]{1,0:T(8,128)(2,1)S(1)} %fusion.5.refs_2_.refs_1_), channel_id=1, source_target_pairs={{0,1},{3,2},{4,5},{7,6},{8,9},{11,10},{12,13},{15,14},{16,17},{19,... | collective-permute-start | bytes 3932168 | tf_op jit(solution)/shard_map/ppermute | solution.py:299
  22.7 32.0 %collective-permute-start.9 = (bf16[512,1280]{1,0:T(8,128)(2,1)S(1)}, bf16[512,1280]{1,0:T(8,128)(2,1)}, u32[]{:S(2)}, u32[]{:S(2)}) collective-permute-start(bf16[512,1280]{1,0:T(8,128)(2,1)S(1)} %fusion.5.refs_2_.refs_1_), channel_id=1, source_target_pairs={{1,2},{2,1},{5,6},{6,5},{9,10},{10,9},{13,14},{14,13},{17,18},{18,... | collective-permute-start | bytes 3932168 | tf_op jit(solution)/shard_map/ppermute | solution.py:299
  26.2 39.3 %collective-permute-start.7 = (bf16[528,1280]{1,0:T(8,128)(2,1)S(1)}, bf16[528,1280]{1,0:T(8,128)(2,1)}, u32[]{:S(2)}, u32[]{:S(2)}) collective-permute-start(bf16[528,1280]{1,0:T(8,128)(2,1)S(1)} %pad_maximum_fusion), channel_id=1, source_target_pairs={{1,0},{2,3},{5,4},{6,7},{9,8},{10,11},{13,12},{14,15},{17,16},{18,... | collective-permute-start | bytes 4055048 | tf_op jit(solution)/shard_map/ppermute | solution.py:299
  36.6 33.5 %collective-permute-start.2 = (bf16[512,1280]{1,0:T(8,128)(2,1)S(1)}, bf16[512,1280]{1,0:T(8,128)(2,1)S(1)}, u32[]{:S(2)}, u32[]{:S(2)}) collective-permute-start(bf16[512,1280]{1,0:T(8,128)(2,1)S(1)} %slice_bitcast_fusion), channel_id=1, source_target_pairs={{0,4},{4,8},{8,12},{12,16},{16,20},{20,24},{24,28},{1,5},{5,9},{9,... | collective-permute-start | bytes 3932168 | tf_op jit(solution)/shard_map/ppermute | solution.py:325
  38.5 34.3 %collective-permute-start.12 = (bf16[512,1280]{1,0:T(8,128)(2,1)}, bf16[512,1280]{1,0:T(8,128)(2,1)}, u32[]{:S(2)}, u32[]{:S(2)}) collective-permute-start(bf16[512,1280]{1,0:T(8,128)(2,1)} %collective-permute-done.1), channel_id=1, source_target_pairs={{4,0},{8,4},{12,8},{16,12},{20,16},{24,20},{28,24},{5,1},{9,5},{13... | collective-permute-start | bytes 3932168 | tf_op jit(solution)/shard_map/ppermute | solution.py:327
  54.7 33.2 %collective-permute-start.10 = (bf16[512,1280]{1,0:T(8,128)(2,1)S(1)}, bf16[512,1280]{1,0:T(8,128)(2,1)}, u32[]{:S(2)}, u32[]{:S(2)}) collective-permute-start(bf16[512,1280]{1,0:T(8,128)(2,1)S(1)} %collective-permute-done.8.refs_3_.refs_2_), channel_id=1, source_target_pairs={{1,2},{2,1},{5,6},{6,5},{9,10},{10,9},{13,14},{14,13},{17,18},{18,... | collective-permute-start | bytes 3932168 | tf_op jit(solution)/shard_map/ppermute | solution.py:299
  58.2 35.1 %collective-permute-start.11 = (bf16[512,1280]{1,0:T(8,128)(2,1)}, bf16[512,1280]{1,0:T(8,128)(2,1)}, u32[]{:S(2)}, u32[]{:S(2)}) collective-permute-start(bf16[512,1280]{1,0:T(8,128)(2,1)} %collective-permute-done.9.refs_5_.refs_4_), channel_id=1, source_target_pairs={{1,0},{2,3},{5,4},{6,7},{9,8},{10,11},{13,12},{14,15},{17,16},{18,... | collective-permute-start | bytes 3932168 | tf_op jit(solution)/shard_map/ppermute | solution.py:299
  68.1 25.2 %collective-permute-start.13 = (bf16[512,1280]{1,0:T(8,128)(2,1)}, bf16[512,1280]{1,0:T(8,128)(2,1)}, u32[]{:S(2)}, u32[]{:S(2)}) collective-permute-start(bf16[512,1280]{1,0:T(8,128)(2,1)} %slice.79), channel_id=1, source_target_pairs={{0,4},{4,8},{8,12},{12,16},{16,20},{20,24},{24,28},{1,5},{5,9},{9,... | collective-permute-start | bytes 3932168 | tf_op jit(solution)/shard_map/ppermute | solution.py:332
  71.3 31.7 %collective-permute-start.3 = (bf16[512,1280]{1,0:T(8,128)(2,1)S(1)}, bf16[512,1280]{1,0:T(8,128)(2,1)}, u32[]{:S(2)}, u32[]{:S(2)}) collective-permute-start(bf16[512,1280]{1,0:T(8,128)(2,1)S(1)} %fusion.2.refs_2_), channel_id=1, source_target_pairs={{0,1},{3,2},{4,5},{7,6},{8,9},{11,10},{12,13},{15,14},{16,17},{19,... | collective-permute-start | bytes 3932168 | tf_op jit(solution)/shard_map/ppermute | solution.py:299
  72.8 43.2 %collective-permute-start.6 = (bf16[512,1280]{1,0:T(8,128)(2,1)S(1)}, bf16[512,1280]{1,0:T(8,128)(2,1)}, u32[]{:S(2)}, u32[]{:S(2)}) collective-permute-start(bf16[512,1280]{1,0:T(8,128)(2,1)S(1)} %fusion.2.refs_2_), channel_id=1, source_target_pairs={{1,2},{2,1},{5,6},{6,5},{9,10},{10,9},{13,14},{14,13},{17,18},{18,... | collective-permute-start | bytes 3932168 | tf_op jit(solution)/shard_map/ppermute | solution.py:299
  93.3 33.9 %collective-permute-start.14 = (bf16[512,1280]{1,0:T(8,128)(2,1)}, bf16[512,1280]{1,0:T(8,128)(2,1)S(1)}, u32[]{:S(2)}, u32[]{:S(2)}) collective-permute-start(bf16[512,1280]{1,0:T(8,128)(2,1)} %collective-permute-done.10.refs_7_.refs_6_), channel_id=1, source_target_pairs={{1,0},{2,3},{5,4},{6,7},{9,8},{10,11},{13,12},{14,15},{17,16},{18,... | collective-permute-start | bytes 3932168 | tf_op jit(solution)/shard_map/ppermute | solution.py:299
  103.8 35.1 %collective-permute-start.15 = (bf16[16,1280]{1,0:T(8,128)(2,1)S(1)}, bf16[16,1280]{1,0:T(8,128)(2,1)S(1)}, u32[]{:S(2)}, u32[]{:S(2)}) collective-permute-start(bf16[16,1280]{1,0:T(8,128)(2,1)S(1)} %slice.86), channel_id=1, source_target_pairs={{0,4},{4,0},{8,12},{12,8},{16,20},{20,16},{24,28},{28,24},{1,5},{5... | collective-permute-start | bytes 122888 | tf_op jit(solution)/shard_map/ppermute | solution.py:345
  105.8 38.3 %collective-permute-start.4 = (bf16[512,1280]{1,0:T(8,128)(2,1)}, bf16[512,1280]{1,0:T(8,128)(2,1)}, u32[]{:S(2)}, u32[]{:S(2)}) collective-permute-start(bf16[512,1280]{1,0:T(8,128)(2,1)} %collective-permute-done.3.refs_0_.refs_3_), channel_id=1, source_target_pairs={{1,2},{2,1},{5,6},{6,5},{9,10},{10,9},{13,14},{14,13},{17,18},{18,... | collective-permute-start | bytes 3932168 | tf_op jit(solution)/shard_map/ppermute | solution.py:299
  116.0 42.8 %collective-permute-start.16 = (bf16[512,1280]{1,0:T(8,128)(2,1)}, bf16[512,1280]{1,0:T(8,128)(2,1)}, u32[]{:S(2)}, u32[]{:S(2)}) collective-permute-start(bf16[512,1280]{1,0:T(8,128)(2,1)} %collective-permute-done.6.refs_1_.refs_5_), channel_id=1, source_target_pairs={{1,0},{2,3},{5,4},{6,7},{9,8},{10,11},{13,12},{14,15},{17,16},{18,... | collective-permute-start | bytes 3932168 | tf_op jit(solution)/shard_map/ppermute | solution.py:299
  138.9 35.3 %collective-permute-start.17 = (bf16[2,5,512,128]{3,2,1,0:T(8,128)(2,1)S(1)}, bf16[2,5,512,128]{3,2,1,0:T(8,128)(2,1)}, u32[]{:S(2)}, u32[]{:S(2)}) collective-permute-start(bf16[2,5,512,128]{3,2,1,0:T(8,128)(2,1)S(1)} %project_end.2.refs_0_.refs_3_), channel_id=1, source_target_pairs={{0,8},{1,9},{2,10},{3,11}} | collective-permute-start | bytes 3932168 | tf_op jit(solution)/shard_map/ppermute | solution.py:252
  140.2 34.0 %collective-permute-start.18 = (bf16[2,5,512,128]{3,2,1,0:T(8,128)(2,1)S(1)}, bf16[2,5,512,128]{3,2,1,0:T(8,128)(2,1)}, u32[]{:S(2)}, u32[]{:S(2)}) collective-permute-start(bf16[2,5,512,128]{3,2,1,0:T(8,128)(2,1)S(1)} %project_end.2.refs_0_.refs_3_), channel_id=1, source_target_pairs={{0,16},{1,17},{2,18},{3,19}} | collective-permute-start | bytes 3932168 | tf_op jit(solution)/shard_map/ppermute | solution.py:252
  141.9 32.3 %collective-permute-start.19 = (bf16[2,5,512,128]{3,2,1,0:T(8,128)(2,1)S(1)}, bf16[2,5,512,128]{3,2,1,0:T(8,128)(2,1)}, u32[]{:S(2)}, u32[]{:S(2)}) collective-permute-start(bf16[2,5,512,128]{3,2,1,0:T(8,128)(2,1)S(1)} %project_end.2.refs_0_.refs_3_), channel_id=1, source_target_pairs={{0,24},{1,25},{2,26},{3,27}} | collective-permute-start | bytes 3932168 | tf_op jit(solution)/shard_map/ppermute | solution.py:252
  144.1 38.0 %collective-permute-start.5 = (bf16[512,1280]{1,0:T(8,128)(2,1)}, bf16[512,1280]{1,0:T(8,128)(2,1)S(1)}, u32[]{:S(2)}, u32[]{:S(2)}) collective-permute-start(bf16[512,1280]{1,0:T(8,128)(2,1)} %collective-permute-done.4.inner), channel_id=1, source_target_pairs={{1,0},{2,3},{5,4},{6,7},{9,8},{10,11},{13,12},{14,15},{17,16},{18,... | collective-permute-start | bytes 3932168 | tf_op jit(solution)/shard_map/ppermute | solution.py:299
  175.8 18.9 %collective-permute-start.20 = (bf16[2,5,512,128]{3,2,1,0:T(8,128)(2,1)S(1)}, bf16[2,5,512,128]{3,2,1,0:T(8,128)(2,1)S(1)}, u32[]{:S(2)}, u32[]{:S(2)}) collective-permute-start(bf16[2,5,512,128]{3,2,1,0:T(8,128)(2,1)S(1)} %select_select_fusion.refs_1_), channel_id=1, source_target_pairs={{0,4},{8,12},{16,20},{24,28},{1,5},{9,13},{17,21},{25,29},{2,6},{1... | collective-permute-start | bytes 3932168 | tf_op jit(solution)/shard_map/ppermute | solution.py:253
  177.1 17.5 %collective-permute-start.21 = (bf16[2,5,256,128]{3,2,1,0:T(8,128)(2,1)S(1)}, bf16[2,5,256,128]{3,2,1,0:T(8,128)(2,1)S(1)}, u32[]{:S(2)}, u32[]{:S(2)}) collective-permute-start(bf16[2,5,256,128]{3,2,1,0:T(8,128)(2,1)S(1)} %get-tuple-element.45), channel_id=1, source_target_pairs={{4,8},{8,12},{12,16},{16,20},{20,24},{24,28},{5,9},{9,13},{13,17},... | collective-permute-start | bytes 1966088 | tf_op jit(solution)/shard_map/ppermute | solution.py:351
  191.6 12.7 %collective-permute-start.23 = (bf16[2,5,512,128]{3,2,1,0:T(8,128)(2,1)S(1)}, bf16[2,5,512,128]{3,2,1,0:T(8,128)(2,1)S(1)}, u32[]{:S(2)}, u32[]{:S(2)}) collective-permute-start(bf16[2,5,512,128]{3,2,1,0:T(8,128)(2,1)S(1)} %get-tuple-element.50.refs_4_), channel_id=1, source_target_pairs={{0,4},{1,5},{2,6},{3,7}} | collective-permute-start | bytes 3932168 | tf_op jit(solution)/shard_map/ppermute | solution.py:354
  192.5 11.9 %collective-permute-start.22 = (bf16[2,5,256,128]{3,2,1,0:T(8,128)(2,1)S(1)}, bf16[2,5,256,128]{3,2,1,0:T(8,128)(2,1)S(1)}, u32[]{:S(2)}, u32[]{:S(2)}) collective-permute-start(bf16[2,5,256,128]{3,2,1,0:T(8,128)(2,1)S(1)} %get-tuple-element.49), channel_id=1, source_target_pairs={{4,8},{8,12},{12,16},{16,20},{20,24},{24,28},{5,9},{9,13},{13,17},... | collective-permute-start | bytes 1966088 | tf_op jit(solution)/shard_map/ppermute | solution.py:351
  (16 other events, 217.9 us)
